TPU v7x, 32 devices: a whole 2x2x4 slice. The times are simulated.
32 devices in a mesh: tm: 16 (over z, x, core), head: 2 (over y).
Axes of the slice: x: 2, y: 2, z: 4, core: 2. Of those that a mesh axis runs over, the one named last changes fastest.
Arguments:
- frames_in: bfloat16 [16, 1024, 1024], P('tm', 'head'), may hold values from -400 to 400
- in_weight: bfloat16 [1024, 5120], P('tm', 'head'), may hold values from -0.1875 to 0.1875
- out_weight: bfloat16 [1024, 1024], replicated, may hold values from -0.1875 to 0.1875
- block_ids: int32 [1024], replicated, may hold values from 0 to 15, as said below
- block_lists: int32 [16, 4], replicated, may hold values from 0 to 15, as said below
- decays: float32 [16, 16, 16], P('tm', 'head'), may hold values from 0.3 to 1
Outputs:
- layer_out: bfloat16 [16, 1024, 1024], P('tm', 'head')
Inputs may be any that keep to these rules, and one draw needn't show every extreme that they name: `block_ids`: each of the 16 block ids is held by exactly 64 tokens. `block_lists`: row g starts with g itself, followed by 4 - 1 further blocks, all different.
All inputs are finite; a program needn't handle non-finite values.
Results may differ from a plain program's by a relative error of at most 0.0069.
Values may be sent and summed in bfloat16 or wider, within the bound.
No kernel may reach another device: no remote copies, remote signals or barrier semaphores. Data moves between devices by JAX's collectives and lax.ppermute only.
A program may use at most 192 MiB of HBM per device.

v0:
```python
import math

import jax
import jax.numpy as jnp
from jax import lax
from jax.sharding import PartitionSpec as P

HD = 64
N = 64
TOKS = 1024
NB = 16


epsilon = 1e-06


def carried_in(shard, axis, combine, identity):
    peers, index = (lax.axis_size(axis), lax.axis_index(axis))
    everything = jax.tree.map(lambda part: lax.all_gather(part, axis), shard)
    start = jax.tree.map(
        lambda part, zero: jnp.broadcast_to(jnp.asarray(zero, part.dtype), part.shape),
        shard,
        identity,
    )

    def step(k, before):
        reached = k < index
        new = combine(before, jax.tree.map(lambda part: part[k], everything))
        return jax.tree.map(lambda a, b: jnp.where(reached, a, b), new, before)

    return lax.fori_loop(0, peers, step, start)


def head_norm(values):
    wide = values.astype(jnp.float32)
    return (wide * lax.rsqrt(jnp.mean(wide * wide, axis=-1, keepdims=True) + epsilon)).astype(
        jnp.bfloat16
    )


def combine(earlier, after_it):
    return (earlier[0] * after_it[0], after_it[0][:, :, None] * earlier[1] + after_it[1])


def body(frames_in, in_weight, out_weight, block_ids, block_lists, decays):
    frame_count, local_tokens, feature_width = frames_in.shape
    heads_here = decays.shape[1]
    groups = decays.shape[2]
    tokens = block_ids.shape[0]
    block_size = tokens // groups
    head_size = HD
    state_size = N
    selected_count = block_lists.shape[1]
    inputs_wide = frames_in.astype(jnp.float32)
    normed = (
        inputs_wide
        * lax.rsqrt(jnp.mean(inputs_wide * inputs_wide, axis=-1, keepdims=True) + epsilon)
    ).astype(jnp.bfloat16)
    full_rows = lax.all_gather(in_weight, "tm", axis=0, tiled=True)
    flat_rows = normed.reshape(frame_count * local_tokens, feature_width)
    local_flat = jnp.dot(
        flat_rows,
        lax.all_gather(full_rows, "head", axis=1, tiled=True),
        preferred_element_type=jnp.float32,
    ).astype(jnp.bfloat16)
    local_proj = local_flat.reshape(frame_count, local_tokens, local_flat.shape[1])
    projected = lax.all_to_all(local_proj, "head", split_axis=2, concat_axis=1, tiled=True)
    projected = projected.reshape(frame_count, tokens, heads_here, 5, head_size)
    sort_order = jnp.argsort(block_ids, stable=True)
    inverse_order = jnp.argsort(sort_order, stable=True)
    sorted_proj = jnp.take(projected, sort_order, axis=1).reshape(
        frame_count, groups, block_size, heads_here, 5, head_size
    )
    queries = head_norm(sorted_proj[:, :, :, :, 0])
    key_rows = head_norm(sorted_proj[:, :, :, :, 1])
    values_sorted = sorted_proj[:, :, :, :, 2]
    map_sorted = sorted_proj[:, :, :, :, 3, :state_size]
    readers_sorted = sorted_proj[:, :, :, :, 4, :state_size].astype(jnp.float32)
    chosen_keys = jnp.take(key_rows, block_lists, axis=1).reshape(
        frame_count, groups, selected_count * block_size, heads_here, head_size
    )
    chosen_values = jnp.take(values_sorted, block_lists, axis=1).reshape(
        frame_count, groups, selected_count * block_size, heads_here, head_size
    )
    updates = jnp.einsum(
        "fgshn,fgshd->fhgnd", map_sorted, values_sorted, preferred_element_type=jnp.float32
    )
    local_state = jnp.zeros((heads_here, groups, state_size, head_size), jnp.float32)
    running = jnp.ones((heads_here, groups), jnp.float32)
    frame_at = 0
    local_state = decays[frame_at][:, :, None, None] * local_state + updates[frame_at]
    running = decays[frame_at] * running
    states = [local_state]
    products = [running]
    identity = (
        jnp.ones((heads_here, groups), jnp.float32),
        jnp.zeros((heads_here, groups, state_size * head_size), jnp.float32),
    )
    carried = carried_in(
        (running, local_state.reshape(heads_here, groups, state_size * head_size)),
        "tm",
        combine,
        identity,
    )
    incoming = carried[1].reshape(heads_here, groups, state_size, head_size)
    ssm_scale = 1.0 / (N * math.sqrt(TOKS // NB))
    frame_at = 0
    full_state = states[frame_at] + products[frame_at][:, :, None, None] * incoming
    readout_sorted = (
        jnp.einsum(
            "gshn,hgnd->gshd", readers_sorted[frame_at], full_state, precision=lax.Precision.HIGHEST
        )
        * ssm_scale
    )
    scores = jnp.einsum(
        "gshd,guhd->hgsu",
        queries[frame_at],
        chosen_keys[frame_at],
        preferred_element_type=jnp.float32,
    ) / math.sqrt(head_size)
    exponent = jnp.exp(scores)
    weights = (exponent / jnp.sum(exponent, axis=-1, keepdims=True)).astype(jnp.bfloat16)
    attended = jnp.einsum(
        "hgsu,guhd->gshd", weights, chosen_values[frame_at], preferred_element_type=jnp.float32
    )
    mixed_sorted = (
        (attended + readout_sorted).astype(jnp.bfloat16).reshape(tokens, heads_here * head_size)
    )
    frames_mixed = [jnp.take(mixed_sorted, inverse_order, axis=0)]
    mixed = jnp.stack(frames_mixed, axis=0)
    token_mix = lax.all_to_all(mixed, "head", split_axis=1, concat_axis=2, tiled=True)
    result = jnp.dot(
        token_mix.reshape(frame_count * local_tokens, token_mix.shape[2]),
        out_weight,
        preferred_element_type=jnp.float32,
    )
    return result.astype(jnp.bfloat16).reshape(frame_count, local_tokens, feature_width)


def solution(mesh):
    return jax.shard_map(
        body,
        mesh=mesh,
        in_specs=(P("tm", "head", None), P("tm", "head"), P(), P(), P(), P("tm", "head", None)),
        out_specs=P("tm", "head", None),
        check_vma=False,
    )
```

profile of v0, /device:TPU:0, one launch (start us, length us, event | category | flops | bytes accessed | tf_op | source)
XLA Modules:
  0.0 758.7 jit_solution(5488556218809806266)
XLA Ops:
  7.3 61.1 %all-gather.4.cloned.1.call-done = bf16[1024,2560]{1,0:T(8,128)(2,1)} async-done(((bf16[64,2560]{1,0:T(8,128)(2,1)}), bf16[1024,2560]{1,0:T(8,128)(2,1)}) %all-gather.4.cloned.1.call-update) | async-done | bytes 5242896 | tf_op jit(solution)/shard_map/all_gather | solution.py:59
  68.7 129.3 %all-gather.6.cloned.1.call-done = bf16[1024,5120]{1,0:T(8,128)(2,1)} async-done(((bf16[1024,2560]{1,0:T(8,128)(2,1)}), bf16[1024,5120]{1,0:T(8,128)(2,1)}) %all-gather.6.cloned.1.call-update) | async-done | bytes 10485776 | tf_op jit(solution)/shard_map/all_gather | solution.py:63
  198.0 11.4 %fusion.2 = bf16[1,512,5120]{2,1,0:T(8,128)(2,1)} fusion(bf16[1024,5120]{1,0:T(8,128)(2,1)} %all-gather.6.cloned.1.call-done, bf16[1,512,1024]{2,1,0:T(8,128)(2,1)S(1)} %copy-done.3, f32[512]{0:T(512)S(1)} %add_rsqrt_fusion.2), kind=kOutput, calls=%fused_computation.14 | convolution fusion | flops 5372903424 | bytes 16779264 | tf_op jit(solution)/shard_map/dot_general | solution.py:61
  209.4 21.8 %copy.49 = bf16[1,512,5120]{1,0,2:T(2,128)(2,1)} copy(bf16[1,512,5120]{2,1,0:T(8,128)(2,1)} %fusion.2) | data formatting | bytes 10485760 | tf_op jit(solution)/shard_map/reshape | solution.py:66
  231.7 35.1 %reduce.4 = bf16[5120,512]{1,0:T(8,128)(2,1)} reduce(bf16[5120,1,512]{2,1,0:T(2,128)(2,1)} %bitcast.83, bf16[]{:T(256)} %broadcast.155), dimensions={1}, to_apply=%bitcast.66.reduce_sub_computation | reduce | bytes 10485762
  266.8 7.0 reshape.271
  273.9 6.1 all-to-all-start
  285.0 53.9 %all-to-all-done = bf16[2,2,655360]{2,1,0:T(2,128)(2,1)} async-done(((bf16[2,2,655360]{2,1,0:T(2,128)(2,1)}), bf16[2,2,655360]{2,1,0:T(2,128)(2,1)}, u32[]{:S(2)}, u32[]{:S(2)}) %all-to-all-start) | async-done | bytes 5242912 | tf_op jit(solution)/shard_map/all_to_all | solution.py:67
  338.9 12.5 %reshape.272 = bf16[5120,1,512]{2,1,0:T(2,128)(2,1)} reshape(bf16[2,2,655360]{2,1,0:T(2,128)(2,1)} %all-to-all-done) | data formatting | bytes 10485760
  351.4 5.5 copy.68
  356.9 23.7 %copy.50 = bf16[1,2,512,2560]{2,1,3,0:T(2,128)(2,1)} copy(bf16[1,2,512,2560]{2,3,1,0:T(8,128)(2,1)S(1)} %bitcast.88) | data formatting | bytes 10485760 | tf_op jit(solution)/shard_map/all_to_all | solution.py:67
  380.6 9.4 %reshape.233 = bf16[1024,8,5,64]{0,3,2,1:T(8,128)(2,1)} reshape(bf16[1,2,512,2560]{2,1,3,0:T(2,128)(2,1)} %copy.50) | data formatting | bytes 10485760 | tf_op jit(solution)/shard_map/reshape | solution.py:68
  390.0 12.2 %copy.51 = bf16[1024,8,5,64]{3,1,2,0:T(8,128)(2,1)} copy(bf16[1024,8,5,64]{0,3,2,1:T(8,128)(2,1)} %reshape.233) | data formatting | bytes 10485760 | tf_op jit(solution)/shard_map/reshape | solution.py:68
  402.2 15.0 %gather_fusion = bf16[1024,8,5,64]{3,1,2,0:T(8,128)(2,1)} fusion(bf16[1024,8,5,64]{3,1,2,0:T(8,128)(2,1)} %copy.51, s32[1024]{0:T(1024)S(1)} %fusion.31), kind=kCustom, calls=%fused_computation.2 | custom fusion | bytes 10489856 | tf_op jit(solution)/shard_map/jit(_take)/gather | solution.py:71
  417.2 10.4 %copy.52 = bf16[1024,8,5,64]{3,0,1,2:T(8,128)(2,1)} copy(bf16[1024,8,5,64]{3,1,2,0:T(8,128)(2,1)} %gather_fusion) | data formatting | bytes 10485760 | tf_op jit(solution)/shard_map/jit(_take)/gather | solution.py:71
  427.7 5.8 broadcast_select_fusion
  453.1 22.1 %all_gather.14 = f32[16,8,16]{2,1,0:T(8,128)S(1)} all-gather(f32[1,8,16]{2,1,0:T(8,128)S(1)} %copy-done.4), channel_id=1, replica_groups=mesh['tm'=16,'head'=2] {'tm'}, dimensions={0}, use_global_device_ids=true | all-gather | bytes 8704 | tf_op jit(solution)/shard_map/all_gather | solution.py:19
  475.2 5.7 slice_bitcast_fusion.4
  480.9 7.4 gather_fusion.2
  494.5 7.2 gather_fusion.3
  501.8 11.8 %broadcast_select_fusion.1 = (bf16[1,16,4,64,8,64]{5,3,4,2,1,0:T(8,128)(2,1)}, bf16[1,16,4,64,8,64]{5,3,4,2,1,0:T(8,128)(2,1)}) fusion(bf16[1,16,4,64,8,64]{5,3,4,2,1,0:T(8,128)(2,1)} %bitcast.87, pred[16,4]{1,0:T(8,128)(4,1)S(1)} %copy.48, bf16[1,16,4,64,8,64]{5,3,4,2,1,0:T(8,128)(2,1)} %bitcast.86), kind=kLoop, calls=%fused_computation.10 | loop fusion | flops 4194304 | bytes 16777280 | tf_op jit(solution)/shard_map/jit(_take)/select_n | solution.py:79
  513.6 13.8 %copy.57 = bf16[1,16,4,64,8,64]{3,2,5,1,4,0:T(4,128)(2,1)} copy(bf16[1,16,4,64,8,64]{5,3,4,2,1,0:T(8,128)(2,1)} %get-tuple-element.135) | data formatting | bytes 8388608 | tf_op jit(solution)/shard_map/jit(_take)/select_n | solution.py:79
  527.4 12.8 %squeeze_reshape.7 = bf16[16,256,8,64]{1,3,0,2:T(8,128)(2,1)} reshape(bf16[1,16,4,64,8,64]{3,2,5,1,4,0:T(4,128)(2,1)} %copy.57) | data formatting | bytes 8388608 | tf_op jit(solution)/shard_map/squeeze;reshape | solution.py:118
  540.2 13.7 %copy.54 = bf16[1,16,4,64,8,64]{3,2,5,4,1,0:T(4,128)(2,1)} copy(bf16[1,16,4,64,8,64]{5,3,4,2,1,0:T(8,128)(2,1)} %get-tuple-element.136) | data formatting | bytes 8388608 | tf_op jit(solution)/shard_map/jit(_take)/select_n | solution.py:82
  553.9 12.8 %squeeze_reshape.6 = bf16[16,256,8,64]{1,3,2,0:T(8,128)(2,1)} reshape(bf16[1,16,4,64,8,64]{3,2,5,4,1,0:T(4,128)(2,1)} %copy.54) | data formatting | bytes 8388608 | tf_op jit(solution)/shard_map/squeeze;reshape | solution.py:124
  569.6 8.2 %fusion.1 = (f32[8,16,64]{2,1,0:T(8,128)S(1)}, f32[8,16,64,256]{3,2,1,0:T(8,128)}) fusion(bf16[16,256,8,64]{1,3,0,2:T(8,128)(2,1)} %squeeze_reshape.7, f32[16,64,8]{1,0,2:T(8,128)S(1)} %add_rsqrt_fusion.1, bf16[1,16,64,8,5,64]{5,2,1,3,4,0:T(8,128)(2,1)} %copy-done.1), kind=kOutput, calls=%fused_computation.13 | convolution fusion | flops 274194432 | bytes 14745600 | tf_op jit(solution)/shard_map/gshd,guhd->hgsu/dot_general | solution.py:115
  577.8 39.1 %all-gather.8.cloned.1.call-done = f32[16,8,16,4096]{3,2,1,0:T(8,128)} async-done(((f32[1,8,16,4096]{3,2,1,0:T(8,128)}), f32[16,8,16,4096]{3,2,1,0:T(8,128)}) %all-gather.8.cloned.1.call-update) | async-done | bytes 33554448 | tf_op jit(solution)/shard_map/all_gather | solution.py:19
  616.9 62.7 %while.14 = (s32[]{:T(128)}, f32[8,16,4096]{2,1,0:T(8,128)}, s32[]{:T(128)}, f32[16,8,16]{2,1,0:T(8,128)S(1)}, f32[16,8,16,4096]{3,2,1,0:T(8,128)}, /*index=5*/s32[]{:T(128)}, s32[]{:T(128)}) while((s32[]{:T(128)}, f32[8,16,4096]{2,1,0:T(8,128)}, s32[]{:T(128)}, f32[16,8,16]{2,1,0:T(8,128)S(1)}, f32[16,8,16,4096]{3,2,1,0:T(8,128)}, ...), condition=%wide.region_7.9_spmd.clone, body=%wide.region_6.8_spmd.clone.sunk | while | flops 2097156 | bytes 6293105 | solution.py:31
  684.4 8.1 %fusion.8 = f32[16,8,64,64]{3,2,1,0:T(8,128)S(1)} fusion(bf16[16,64,8,64]{3,1,0,2:T(8,128)(2,1)} %get-tuple-element.134, f32[8,16,64,64]{3,2,1,0:T(8,128)} %reshape.207, f32[8,16,64,64]{3,2,1,0:T(8,128)} %fusion.19, f32[8,16]{1,0:T(8,128)S(1)} %bitcast.93, f32[8,16]{1,0:T(8,128)S(1)} %broadcast_multiply_fusion), kind=kOutput, calls=%fused_computation.24 | convolution fusion | flops 404226048 | bytes 7341056 | tf_op jit(solution)/shard_map/gshn,hgnd->gshd/dot_general | solution.py:110
  692.5 6.1 fusion.23
  715.6 8.0 %reduce.5 = bf16[1024,512]{1,0:T(8,128)(2,1)S(1)} reduce(bf16[1024,1,512]{2,1,0:T(2,128)(2,1)} %bitcast.90, bf16[]{:T(256)} %broadcast.155), dimensions={1}, to_apply=%bitcast.78.reduce_sub_computation | reduce | bytes 2097154
  725.3 17.9 %all_to_all.30 = bf16[2,2,131072]{2,1,0:T(2,128)(2,1)S(1)} all-to-all(bf16[2,2,131072]{2,1,0:T(2,128)(2,1)} %reshape.273), channel_id=1, replica_groups=mesh['tm'=16,'head'=2] {'head'}, dimensions={0} | all-to-all | bytes 2097152 | tf_op jit(solution)/shard_map/all_to_all | solution.py:131
  (91 shorter events, 129.9 us)
Async XLA Ops:
  6.5 741.7 %copy-start = (bf16[1024,1024]{1,0:T(8,128)(2,1)S(1)}, bf16[1024,1024]{1,0:T(8,128)(2,1)}, u32[]{:S(2)}) copy-start(bf16[1024,1024]{1,0:T(8,128)(2,1)} %param.12) | copy-start | bytes 6291460
  6.5 61.9 %copy-start.3 = (bf16[1,512,1024]{2,1,0:T(8,128)(2,1)S(1)}, bf16[1,512,1024]{2,1,0:T(8,128)(2,1)}, u32[]{:S(2)}) copy-start(bf16[1,512,1024]{2,1,0:T(8,128)(2,1)} %param.10) | copy-start | bytes 3145732
  6.5 61.8 %all-gather.4.cloned.1.call-start = ((), (), s32[]{:S(2)}) async-start(), calls=%async_computation.2 | async-start | bytes 5570560 | tf_op jit(solution)/shard_map/all_gather | solution.py:59
  7.3 190.8 %all-gather.6.cloned.1.call-start = ((), (), s32[]{:S(2)}) async-start(), calls=%async_computation.3 | async-start | bytes 15728640 | tf_op jit(solution)/shard_map/all_gather | solution.py:63
  273.9 6.6 copy-start.6
  273.9 11.1 %copy-start.4 = (f32[1,8,16]{2,1,0:T(8,128)S(1)}, f32[1,8,16]{2,1,0:T(8,128)}, u32[]{:S(2)}) copy-start(f32[1,8,16]{2,1,0:T(8,128)} %param.15) | copy-start | bytes 1540
  273.9 65.0 %all-to-all-start = ((bf16[2,2,655360]{2,1,0:T(2,128)(2,1)}), bf16[2,2,655360]{2,1,0:T(2,128)(2,1)}, u32[]{:S(2)}, u32[]{:S(2)}) async-start(bf16[2,2,655360]{2,1,0:T(2,128)(2,1)} %reshape.271), calls=%async_computation | async-start | bytes 10485760 | tf_op jit(solution)/shard_map/all_to_all | solution.py:67
  280.0 337.0 %all-gather.8.cloned.1.call-start = ((), (), s32[]{:S(2)}) async-start(), calls=%async_computation.4 | async-start | bytes 35651584 | tf_op jit(solution)/shard_map/all_gather | solution.py:19
  433.5 4.0 copy-start.1
  445.2 3.2 copy-start.5
  684.4 8.1 %copy-start.2 = (bf16[16,256,8,64]{1,3,2,0:T(8,128)(2,1)S(1)}, bf16[16,256,8,64]{1,3,2,0:T(8,128)(2,1)}, u32[]{:S(2)}) copy-start(bf16[16,256,8,64]{1,3,2,0:T(8,128)(2,1)} %squeeze_reshape.6) | copy-start | bytes 12582916
Sparse Core Ops, SparseCore 0:
  9.6 58.6 all-gather.3
  69.9 128.0 all-gather.5
  448.5 168.3 all-gather.7
where the time goes:
time: 768 us; the launch traced here: 759 us
  waiting for transfers between devices  284 us (37%)
  local copies, waits for them, and re-layouts  228 us (30%)
  other arithmetic  146 us (19%)
  matrix products  40.3 us (5%)
  blocking collectives  40 us (5%)
  between operations  13.7 us (2%)
    all_gather x1, waiting for transfers between devices, body(): lax.all_gather(full_rows, 'head', axis=1, tiled=True)  129 us
    select_n x16, other arithmetic, step(): return jax.tree.map(lambda a, b: jnp.where(reached, a, b), new, before)  62.6 us
    all_gather x1, waiting for transfers between devices, body(): full_rows = lax.all_gather(in_weight, 'tm', axis=0, tiled=True)  61.1 us
    all_to_all x1, waiting for transfers between devices, body(): lax.all_to_all(local_proj, 'head', split_axis=2, concat_axis=1, tiled=True)  53.9 us
    unnamed x3, other arithmetic  43.1 us
    all_gather x1, waiting for transfers between devices, carried_in(): everything = jax.tree.map(lambda part: lax.all_gather(part, axis), shard)  39.1 us
    unnamed x21, local copies, waits for them, and re-layouts  35 us
    gather x2, local copies, waits for them, and re-layouts, body(): jnp.take(projected, sort_order, axis=1)  25.4 us
  transfers between devices with their start and end apart: 4, of which 4 were waited for; matrix products, arithmetic and copies ran while one was open for 15% of the time, Pallas kernels for 0%

commit v1 on v0

v1 whole, which is shorter than its diff:
```python
import functools
import math

import jax
import jax.numpy as jnp
from jax import lax
from jax.experimental import pallas as pl
from jax.experimental.pallas import tpu as pltpu
from jax.sharding import PartitionSpec as P

HD = 64
N = 64
LANES = 2 * HD
PIECES = 5
EARLY = (2, 3)
LATE = (0, 1, 4)

epsilon = 1e-06

f32 = jnp.float32
bf16 = jnp.bfloat16


def params(mib=48):
    return pltpu.CompilerParams(vmem_limit_bytes=mib << 20)


def cost(flops, nbytes, transcendentals=0):
    return pl.CostEstimate(
        flops=int(flops), bytes_accessed=int(nbytes), transcendentals=int(transcendentals)
    )


def first_half(shape):
    return lax.broadcasted_iota(jnp.int32, shape, len(shape) - 1) < HD


def reorder_kernel(w_ref, early_ref, late_ref):
    pairs = w_ref.shape[1] // (2 * PIECES * HD)

    def piece(head, i):
        at = (head * PIECES + i) * HD
        return w_ref[:, at : at + HD]

    for p in range(pairs):
        for out_ref, kinds in ((early_ref, EARLY), (late_ref, LATE)):
            for j, i in enumerate(kinds):
                at = (p * len(kinds) + j) * LANES
                out_ref[:, at : at + LANES] = jnp.concatenate(
                    [piece(2 * p, i), piece(2 * p + 1, i)], axis=1
                )


def reorder(w):
    rows, cols = w.shape
    base = cols // PIECES
    return pl.pallas_call(
        reorder_kernel,
        out_shape=(
            jax.ShapeDtypeStruct((rows, base * len(EARLY)), bf16),
            jax.ShapeDtypeStruct((rows, base * len(LATE)), bf16),
        ),
        compiler_params=params(),
        cost_estimate=cost(0, 4 * rows * cols),
        name="reorder",
    )(w)


def sort_kernel(groups, ids_row_ref, ids_col_ref, *refs):
    part_refs = refs[:-3]
    sorted_ref, back_ref, normed = refs[-3:]
    local, width = part_refs[0].shape
    tokens = normed.shape[0]
    block = tokens // groups
    step = 128

    for k, part in enumerate(part_refs):

        def norm(c, _, part=part, k=k):
            at = pl.multiple_of(c * step, step)
            wide = part[pl.ds(at, step), :].astype(f32)
            scale = lax.rsqrt(jnp.mean(wide * wide, axis=-1, keepdims=True) + epsilon)
            normed[pl.ds(k * local + at, step), :] = (wide * scale).astype(bf16)
            return 0

        lax.fori_loop(0, local // step, norm, 0)

    ids_row = ids_row_ref[...]
    label = lax.broadcasted_iota(jnp.int32, (groups, tokens), 0)
    held = label == ids_row
    held_bf = jnp.where(held, 1.0, 0.0).astype(bf16)
    counts = []
    for c in range(tokens // 256):
        before = lax.broadcasted_iota(jnp.int32, (tokens, 256), 0) < (
            lax.broadcasted_iota(jnp.int32, (tokens, 256), 1) + c * 256
        )
        counts.append(
            jnp.dot(held_bf, jnp.where(before, 1.0, 0.0).astype(bf16), preferred_element_type=f32)
        )
    count = jnp.concatenate(counts, axis=1)
    rank_row = jnp.sum(
        jnp.where(held, count + (label * block).astype(f32), 0.0), axis=0, keepdims=True
    ).astype(jnp.int32)

    def place(c, _):
        at = pl.multiple_of(c * step, step)
        pick = (lax.broadcasted_iota(jnp.int32, (step, tokens), 0) + at) == rank_row
        pick = jnp.where(pick, 1.0, 0.0).astype(bf16)
        sorted_ref[pl.ds(at, step), :] = jnp.dot(
            pick, normed[...], preferred_element_type=f32
        ).astype(bf16)
        return 0

    lax.fori_loop(0, tokens // step, place, 0)

    lane = lax.broadcasted_iota(jnp.int32, (tokens, 128), 1)
    held_col = jnp.where(lane == ids_col_ref[...], 1.0, 0.0).astype(bf16)

    def place_back(c, _):
        at = pl.multiple_of(c * step, step)
        before = lax.broadcasted_iota(jnp.int32, (step, tokens), 1) < (
            lax.broadcasted_iota(jnp.int32, (step, tokens), 0) + at
        )
        count = jnp.dot(
            jnp.where(before, 1.0, 0.0).astype(bf16), held_col, preferred_element_type=f32
        )
        lane = lax.broadcasted_iota(jnp.int32, (step, 128), 1)
        mine = lane == ids_col_ref[pl.ds(at, step), :]
        rank = jnp.sum(
            jnp.where(mine, count + (lane * block).astype(f32), 0.0), axis=1, keepdims=True
        ).astype(jnp.int32)
        pick = lax.broadcasted_iota(jnp.int32, (step, tokens), 1) == rank
        back_ref[pl.ds(at, step), :] = jnp.where(pick, 1.0, 0.0).astype(bf16)
        return 0

    lax.fori_loop(0, tokens // step, place_back, 0)


def sort_tokens(ids, parts, groups):
    tokens = ids.shape[0]
    width = parts[0].shape[1]
    return pl.pallas_call(
        functools.partial(sort_kernel, groups),
        out_shape=(
            jax.ShapeDtypeStruct((tokens, width), bf16),
            jax.ShapeDtypeStruct((tokens, tokens), bf16),
        ),
        scratch_shapes=[pltpu.VMEM((tokens, width), bf16)],
        compiler_params=params(),
        cost_estimate=cost(2 * tokens * tokens * width, 6 * tokens * width),
        name="sort_tokens",
    )(ids.reshape(1, tokens), ids.reshape(tokens, 1), *parts)


def update_kernel(groups, x_ref, w_ref, v_ref, u_ref, b_ref):
    tokens = x_ref.shape[0]
    block = tokens // groups
    step = 256

    def project(c, _):
        at = pl.multiple_of(c * step, step)
        both = jnp.dot(
            x_ref[pl.ds(at, step), :], w_ref[...], preferred_element_type=f32
        ).astype(bf16)
        v_ref[pl.ds(at, step), :] = both[:, :LANES]
        b_ref[pl.ds(at, step), :] = both[:, LANES:]
        return 0

    lax.fori_loop(0, tokens // step, project, 0)
    for g in range(groups):
        rows = slice(g * block, (g + 1) * block)
        outer = lax.dot_general(
            b_ref[rows, :], v_ref[rows, :], (((0,), (0,)), ((), ())), preferred_element_type=f32
        )
        u_ref[g * N : (g + 1) * N, :] = jnp.where(
            first_half((N, LANES)), outer[:HD], outer[HD:]
        ).astype(bf16)


def project_updates(x, w, groups):
    tokens, width = x.shape
    pairs = w.shape[1] // (2 * LANES)
    return pl.pallas_call(
        functools.partial(update_kernel, groups),
        grid=(pairs,),
        in_specs=[
            pl.BlockSpec((tokens, width), lambda p: (0, 0)),
            pl.BlockSpec((width, 2 * LANES), lambda p: (0, p)),
        ],
        out_specs=(
            pl.BlockSpec((tokens, LANES), lambda p: (0, p)),
            pl.BlockSpec((groups * N, LANES), lambda p: (p, 0)),
        ),
        out_shape=(
            jax.ShapeDtypeStruct((tokens, pairs * LANES), bf16),
            jax.ShapeDtypeStruct((pairs * groups * N, LANES), bf16),
        ),
        scratch_shapes=[pltpu.VMEM((tokens, LANES), bf16)],
        compiler_params=params(),
        cost_estimate=cost(2 * tokens * width * w.shape[1], 2 * (tokens * width + w.size * 2)),
        name="project_updates",
    )(x, w)


def scan_kernel(d_ref, u_ref, s_ref):
    frames = u_ref.shape[0]
    state = jnp.zeros(u_ref.shape[1:], f32)
    for t in range(frames):
        state = d_ref[t] * state + u_ref[t].astype(f32)
        s_ref[t] = state.astype(bf16)


def scan_states(decay, update):
    return pl.pallas_call(
        scan_kernel,
        out_shape=jax.ShapeDtypeStruct(update.shape, bf16),
        compiler_params=params(),
        cost_estimate=cost(2 * update.size, 4 * update.size),
        name="scan_states",
    )(decay, update)


def attend_kernel(lists_ref, x_ref, w_ref, v_ref, a_ref, c_ref, q_ref, k_ref):
    tokens = x_ref.shape[0]
    groups, chosen = lists_ref.shape
    block = tokens // groups
    step = 256
    per = step // block

    def project(c, _):
        at = pl.multiple_of(c * step, step)
        three = jnp.dot(
            x_ref[pl.ds(at, step), :], w_ref[...], preferred_element_type=f32
        ).astype(bf16)
        c_ref[pl.ds(at, step), :] = three[:, 2 * LANES :]
        half = first_half((step, LANES))

        def head_norm(wide):
            square = wide * wide
            one = jnp.sum(jnp.where(half, square, 0.0), axis=-1, keepdims=True)
            two = jnp.sum(jnp.where(half, 0.0, square), axis=-1, keepdims=True)
            return wide * lax.rsqrt(jnp.where(half, one, two) * (1.0 / HD) + epsilon)

        q = head_norm(three[:, :LANES].astype(f32))
        k_ref[pl.ds(at, step), :] = head_norm(three[:, LANES : 2 * LANES].astype(f32)).astype(bf16)
        one = jnp.where(half, q, 0.0).astype(bf16)
        two = jnp.where(half, 0.0, q).astype(bf16)
        for i in range(per):
            rows = slice(i * block, (i + 1) * block)
            q_ref[c * per + i] = jnp.concatenate([one[rows], two[rows]], axis=0)
        return 0

    lax.fori_loop(0, tokens // step, project, 0)

    scale = math.log2(math.e) / math.sqrt(HD)
    for g in range(groups):
        starts = [pl.multiple_of(lists_ref[g, j] * block, block) for j in range(chosen)]
        keys = jnp.concatenate([k_ref[pl.ds(s, block), :] for s in starts], axis=0)
        values = jnp.concatenate([v_ref[pl.ds(s, block), :] for s in starts], axis=0)
        score = lax.dot_general(
            q_ref[g], keys, (((1,), (1,)), ((), ())), preferred_element_type=f32
        )
        e = jnp.exp2(score * scale)
        weight = (e * (1.0 / jnp.sum(e, axis=-1, keepdims=True))).astype(bf16)
        both = jnp.dot(weight, values, preferred_element_type=f32)
        a_ref[g * block : (g + 1) * block, :] = jnp.where(
            first_half((block, LANES)), both[:block], both[block:]
        )


def attend(lists, x, w, v):
    tokens, width = x.shape
    groups, chosen = lists.shape
    pairs = w.shape[1] // (3 * LANES)
    block = tokens // groups
    return pl.pallas_call(
        attend_kernel,
        grid_spec=pltpu.PrefetchScalarGridSpec(
            num_scalar_prefetch=1,
            grid=(pairs,),
            in_specs=[
                pl.BlockSpec((tokens, width), lambda p, _: (0, 0)),
                pl.BlockSpec((width, 3 * LANES), lambda p, _: (0, p)),
                pl.BlockSpec((tokens, LANES), lambda p, _: (0, p)),
            ],
            out_specs=(
                pl.BlockSpec((tokens, LANES), lambda p, _: (0, p)),
                pl.BlockSpec((tokens, LANES), lambda p, _: (0, p)),
            ),
            scratch_shapes=[
                pltpu.VMEM((groups, 2 * block, LANES), bf16),
                pltpu.VMEM((tokens, LANES), bf16),
            ],
        ),
        out_shape=(
            jax.ShapeDtypeStruct((tokens, pairs * LANES), f32),
            jax.ShapeDtypeStruct((tokens, pairs * LANES), bf16),
        ),
        compiler_params=params(),
        cost_estimate=cost(
            4 * tokens * width * w.shape[1],
            2 * (tokens * width + w.size + 4 * tokens * pairs * LANES),
            2 * pairs * tokens * chosen * block,
        ),
        name="attend",
    )(lists, x, w, v)


def mix_kernel(groups, a_ref, c_ref, s_ref, back_ref, out_ref, mixed):
    tokens = a_ref.shape[0]
    block = tokens // groups
    pairs = a_ref.shape[1] // LANES
    scale = 1.0 / (N * math.sqrt(block))
    for p in range(pairs):
        cols = slice(p * LANES, (p + 1) * LANES)
        for g in range(groups):
            rows = slice(g * block, (g + 1) * block)
            at = (p * groups + g) * N
            state = s_ref[at : at + N, :].astype(f32)
            half = first_half((N, LANES))
            wide = jnp.concatenate(
                [jnp.where(half, state, 0.0), jnp.where(half, 0.0, state)], axis=0
            ).astype(bf16)
            read = jnp.dot(c_ref[rows, cols], wide, preferred_element_type=f32)
            mixed[rows, cols] = (a_ref[rows, cols] + read * scale).astype(bf16)
    step = 256

    def place(c, _):
        at = pl.multiple_of(c * step, step)
        out_ref[pl.ds(at, step), :] = jnp.dot(
            back_ref[pl.ds(at, step), :], mixed[...], preferred_element_type=f32
        ).astype(bf16)
        return 0

    lax.fori_loop(0, tokens // step, place, 0)


def mix(attended, readers, state, back, groups):
    tokens, width = attended.shape
    return pl.pallas_call(
        functools.partial(mix_kernel, groups),
        out_shape=jax.ShapeDtypeStruct((tokens, width), bf16),
        scratch_shapes=[pltpu.VMEM((tokens, width), bf16)],
        compiler_params=params(),
        cost_estimate=cost(2 * tokens * tokens * width, 2 * tokens * tokens + 8 * tokens * width),
        name="mix",
    )(attended, readers, state, back)


def out_kernel(me_ref, w_ref, *refs):
    part_refs, out_ref = refs[:-1], refs[-1]
    peers = len(part_refs)
    depth = part_refs[0].shape[1]
    total = None
    for k, part in enumerate(part_refs):
        owner = lax.rem(me_ref[0] - k + peers, peers)
        rows = pl.ds(pl.multiple_of(owner * depth, depth), depth)
        term = jnp.dot(part[...], w_ref[rows, :], preferred_element_type=f32)
        total = term if total is None else total + term
    out_ref[...] = total.astype(bf16)


def project_out(me, w, parts):
    local = parts[0].shape[0]
    width = w.shape[1]
    vmem = pl.BlockSpec(memory_space=pltpu.VMEM)
    return pl.pallas_call(
        out_kernel,
        in_specs=[pl.BlockSpec(memory_space=pltpu.SMEM)] + [vmem] * (1 + len(parts)),
        out_specs=vmem,
        out_shape=jax.ShapeDtypeStruct((local, width), bf16),
        compiler_params=params(),
        cost_estimate=cost(2 * local * w.size, 2 * (w.size + 2 * local * width)),
        name="project_out",
    )(me.reshape(1), w, *parts)


def body(frames_in, in_weight, out_weight, block_ids, block_lists, decays):
    local_tokens = frames_in.shape[1]
    heads_here = decays.shape[1]
    groups = block_lists.shape[0]
    tokens = block_ids.shape[0]
    pairs = heads_here // 2
    frames, peers = lax.axis_size("tm"), lax.axis_size("head")
    frame, me = lax.axis_index("tm"), lax.axis_index("head")

    own = frames_in[0]
    parts = [own] + [
        lax.ppermute(own, "head", [(j, (j - k) % peers) for j in range(peers)])
        for k in range(1, peers)
    ]
    early, late = reorder(in_weight)
    w_early = lax.all_gather(early, "tm", axis=0, tiled=True)
    w_late = lax.all_gather(late, "tm", axis=0, tiled=True)

    ids = jnp.roll(block_ids, -me * local_tokens)
    x, back = sort_tokens(ids, parts, groups)
    v, update = project_updates(x, w_early, groups)

    rows = update.shape[0] // frames
    arrived = lax.all_to_all(
        update.reshape(frames, rows, LANES), "tm", split_axis=0, concat_axis=0, tiled=True
    )
    items = max(1, rows // N)
    per = rows // items
    all_decays = lax.all_gather(decays[0], "tm", axis=0)
    by_item = all_decays.reshape(frames, pairs, 2, groups).transpose(0, 1, 3, 2)
    by_item = by_item.reshape(frames, pairs * groups, 2)
    mine = lax.dynamic_slice_in_dim(by_item, frame * rows // N, items, axis=1)
    decay = jnp.repeat(mine, HD, axis=2).reshape(frames, items, 1, LANES)
    states = scan_states(decay, arrived.reshape(frames, items, per, LANES))
    state = lax.all_to_all(
        states.reshape(frames, rows, LANES), "tm", split_axis=0, concat_axis=0, tiled=True
    ).reshape(frames * rows, LANES)

    attended, readers = attend(block_lists, x, w_late, v)
    mixed = mix(attended, readers, state, back, groups)
    mixed = mixed.reshape(peers, local_tokens, heads_here * HD)
    features = [mixed[0]] + [
        lax.ppermute(mixed[k], "head", [(j, (j + k) % peers) for j in range(peers)])
        for k in range(1, peers)
    ]
    return project_out(me, out_weight, features)[None]


def solution(mesh):
    return jax.shard_map(
        body,
        mesh=mesh,
        in_specs=(P("tm", "head", None), P("tm", "head"), P(), P(), P(), P("tm", "head", None)),
        out_specs=P("tm", "head", None),
        check_vma=False,
    )
```

time: 768 us -> 178 us (0.23); the launches traced: 759 us -> 177 us
  waiting for transfers between devices: 284 us -> 45.7 us
  local copies, waits for them, and re-layouts: 228 us -> 10.6 us
  other arithmetic: 146 us -> 0.76 us
  Pallas kernels: 0 us -> 43 us
  matrix products: 40.3 us -> 0 us
  starting transfers between devices: 6.64 us -> 25.3 us
    all_gather x3 -> x2, waiting for transfers between devices: 230 us -> 6.19 us  [the longest x1 6.19 us: body(): w_early = lax.all_gather(early, 'tm', axis=0, tiled=True)]
    select_n x20 -> x0, other arithmetic: 81.7 us -> none  [the longest x16 62.6 us: step(): return jax.tree.map(lambda a, b: jnp.where(reached, a, b), new, before)]
    reshape x5 -> x3, local copies, waits for them, and re-layouts: 51.4 us -> 0.33 us  [the longest x1 0.22 us: sort_tokens(): ids.reshape(tokens, 1)]
    all_to_all x1 -> x2, waiting for transfers between devices: 53.9 us -> 3.45 us  [the longest x1 3.44 us: body(): lax.all_to_all(states.reshape(frames, rows, LANES), 'tm', split_axis=0, c...]
    gather x5 -> x0, local copies, waits for them, and re-layouts: 45.4 us -> none  [the longest x2 25.4 us: body(): jnp.take(projected, sort_order, axis=1)]
    unnamed x3 -> x0, other arithmetic: 43.1 us -> none
    pallas_call x0 -> x7, Pallas kernels: none -> 43 us  [the longest x1 17.2 us: attend(): pl.pallas_call(attend_kernel, grid_spec=pltpu.PrefetchScalarGridSpec(num_...]
    dot_general x6 -> x0, matrix products: 40.3 us -> none  [the longest x1 11.4 us: body(): jnp.dot(flat_rows, lax.all_gather(full_rows, 'head', axis=1, tiled=True),...]
  transfers between devices with their start and end apart: 4 -> 6, of which waited for: 4 -> 4; matrix products, arithmetic and copies ran while one was open for 15% -> 1% of each run, Pallas kernels for 0% -> 20%
where the time goes in v1:
time: 178 us; the launch traced here: 177 us
  waiting for transfers between devices  45.7 us (26%)
  Pallas kernels  43 us (24%)
  blocking collectives  37.6 us (21%)
  starting transfers between devices  25.3 us (14%)
  between operations  13.6 us (8%)
  local copies, waits for them, and re-layouts  10.6 us (6%)
    all_gather x1, blocking collectives, body(): all_decays = lax.all_gather(decays[0], 'tm', axis=0)  37.6 us
    ppermute x1, waiting for transfers between devices, body(): lax.ppermute(own, 'head', [(j, (j - k) % peers) for j in range(peers)])  22.4 us
    pallas_call x1, Pallas kernels, attend(): pl.pallas_call(attend_kernel, grid_spec=pltpu.PrefetchScalarGridSpec(num_...  17.2 us
    all_to_all x1, starting transfers between devices, body(): lax.all_to_all(states.reshape(frames, rows, LANES), 'tm', split_axis=0, c...  16.9 us
    ppermute x1, waiting for transfers between devices, body(): lax.ppermute(mixed[k], 'head', [(j, (j + k) % peers) for j in range(peers)])  13 us
    unnamed x23, local copies, waits for them, and re-layouts  9.69 us
    pallas_call x1, Pallas kernels, sort_tokens(): pl.pallas_call(functools.partial(sort_kernel, groups), out_shape=(jax.Sha...  9.25 us
    pallas_call x1, Pallas kernels, project_updates(): pl.pallas_call(functools.partial(update_kernel, groups), grid=(pairs,), i...  8.16 us
  transfers between devices with their start and end apart: 6, of which 4 were waited for; matrix products, arithmetic and copies ran while one was open for 1% of the time, Pallas kernels for 20%

profile of v1, /device:TPU:0, one launch (start us, length us, event | category | flops | bytes accessed | tf_op | source)
XLA Modules:
  0.0 176.5 jit_solution(3706153619541173562)
XLA Ops:
  6.5 1.0 copy-done.3
  7.5 0.8 reorder.1
  8.4 0.7 all-gather.3.cloned.1.call-update
  9.1 3.0 %collective-permute-start = (bf16[512,1024]{1,0:T(8,128)(2,1)}, bf16[512,1024]{1,0:T(8,128)(2,1)S(1)}, u32[]{:S(2)}, u32[]{:S(2)}) collective-permute-start(bf16[512,1024]{1,0:T(8,128)(2,1)} %bitcast.19), channel_id=1, source_target_pairs={{0,1},{1,0},{2,3},{3,2},{4,5},{5,4},{6,7},{7,6},{8,9},{9,8},{10,11... | collective-permute-start | bytes 3145736 | tf_op jit(solution)/shard_map/ppermute | solution.py:389
  12.2 0.8 fusion
  12.9 0.2 copy.12.ids_col_ref
  13.2 22.4 %collective-permute-done.refs_1_ = bf16[512,1024]{1,0:T(8,128)(2,1)S(1)} collective-permute-done((bf16[512,1024]{1,0:T(8,128)(2,1)}, bf16[512,1024]{1,0:T(8,128)(2,1)S(1)}, u32[]{:S(2)}, u32[]{:S(2)}) %collective-permute-start) | collective-permute-done | bytes 1048608 | tf_op jit(solution)/shard_map/ppermute | solution.py:389
  35.5 1.2 copy-done.4
  36.8 9.3 %sort_tokens.1 = (bf16[1024,1024]{1,0:T(8,128)(2,1)S(1)}, bf16[1024,1024]{1,0:T(8,128)(2,1)}) custom-call(s32[1,1024]{1,0:T(1,128)S(1)} %bitcast.18, s32[1024,1]{1,0:T(8,128)S(1)} %copy.12.ids_col_ref, bf16[512,1024]{1,0:T(8,128)(2,1)S(1)} %bitcast.20, bf16[512,1024]{1,0:T(8,128)(2,1)S(1)} %collective-permute-done.refs_1_), custom_call_target="tpu_custom_call" | custom-call | flops 2147483648 | bytes 6291456 | tf_op jit(solution)/shard_map/sort_tokens/pallas_call | solution.py:142
  46.0 1.3 copy-done.5
  47.3 6.2 %all-gather.5.cloned.1.call-done.w_ref = bf16[1024,1024]{1,0:T(8,128)(2,1)} async-done(((bf16[64,1024]{1,0:T(8,128)(2,1)}), bf16[1024,1024]{1,0:T(8,128)(2,1)}) %all-gather.5.cloned.1.call-update) | async-done | bytes 2097168 | tf_op jit(solution)/shard_map/all_gather | solution.py:393
  53.5 1.6 copy-done.6
  55.1 8.2 %project_updates.1 = (bf16[1024,512]{1,0:T(8,128)(2,1)S(1)}, bf16[4096,128]{1,0:T(8,128)(2,1)}) custom-call(bf16[1024,1024]{1,0:T(8,128)(2,1)S(1)} %copy-done.6, bf16[1024,1024]{1,0:T(8,128)(2,1)} %all-gather.5.cloned.1.call-done.w_ref), custom_call_target="tpu_custom_call" | custom-call | flops 2147483648 | bytes 6291456 | tf_op jit(solution)/shard_map/project_updates/pallas_call | solution.py:183
  63.3 1.1 copy-done.7
  64.4 3.8 %all-to-all-start = ((bf16[16,256,128]{2,1,0:T(8,128)(2,1)}), bf16[16,256,128]{2,1,0:T(8,128)(2,1)S(1)}, u32[]{:S(2)}, u32[]{:S(2)}) async-start(bf16[16,256,128]{2,1,0:T(8,128)(2,1)} %bitcast.6), calls=%async_computation | async-start | bytes 2097152 | tf_op jit(solution)/shard_map/all_to_all | solution.py:401
  68.2 37.6 %all_gather.11 = f32[16,8,16]{2,1,0:T(8,128)S(1)} all-gather(f32[1,8,16]{2,1,0:T(8,128)S(1)} %copy-done.9), channel_id=1, replica_groups=mesh['tm'=16,'head'=2] {'tm'}, dimensions={0}, use_global_device_ids=true | all-gather | bytes 8704 | tf_op jit(solution)/shard_map/all_gather | solution.py:406
  105.8 0.1 reshape.36
  106.0 0.2 copy.15
  106.2 0.1 broadcast_in_dim.6
  106.3 0.1 reshape_reshape.3.d_ref
  106.4 1.3 scan_states.1
  107.8 16.9 %all-to-all-start.1 = ((bf16[16,256,128]{2,1,0:T(8,128)(2,1)}), bf16[16,256,128]{2,1,0:T(8,128)(2,1)S(1)}, u32[]{:S(2)}, u32[]{:S(2)}) async-start(bf16[16,256,128]{2,1,0:T(8,128)(2,1)} %bitcast.8), calls=%async_computation.1 | async-start | bytes 2097152 | tf_op jit(solution)/shard_map/all_to_all | solution.py:412
  124.7 0.1 copy.13.lists_ref
  124.8 1.2 copy-done.8
  126.0 17.2 %attend.1 = (f32[1024,512]{1,0:T(8,128)S(1)}, bf16[1024,512]{1,0:T(8,128)(2,1)S(1)}) custom-call(s32[16,4]{1,0:T(8,128)S(1)} %copy.13.lists_ref, bf16[1024,1024]{1,0:T(8,128)(2,1)} %copy-done.5, bf16[1024,1536]{1,0:T(8,128)(2,1)} %all-gather.3.cloned.1.call-done.w_ref, bf16[1024,512]{1,0:T(8,128)(2,1)S(1)} %copy-done.8), custom_call_target="tpu_custom_call" | custom-call | flops 6442450944 | bytes 9437184 | tf_op jit(solution)/shard_map/attend/pallas_call | solution.py:276
  143.2 1.0 copy-done.1
  144.2 3.4 %all-to-all-done.1 = bf16[16,256,128]{2,1,0:T(8,128)(2,1)S(1)} async-done(((bf16[16,256,128]{2,1,0:T(8,128)(2,1)}), bf16[16,256,128]{2,1,0:T(8,128)(2,1)S(1)}, u32[]{:S(2)}, u32[]{:S(2)}) %all-to-all-start.1) | async-done | bytes 1048608 | tf_op jit(solution)/shard_map/all_to_all | solution.py:412
  147.6 1.2 copy-done.2
  148.8 4.0 %mix.1 = bf16[1024,512]{1,0:T(8,128)(2,1)S(1)} custom-call(f32[1024,512]{1,0:T(8,128)S(1)} %get-tuple-element.17.a_ref, bf16[1024,512]{1,0:T(8,128)(2,1)S(1)} %copy-done.2, bf16[4096,128]{1,0:T(8,128)(2,1)S(1)} %bitcast.15, bf16[1024,1024]{1,0:T(8,128)(2,1)} %get-tuple-element.20.back_ref), custom_call_target="tpu_custom_call" | custom-call | flops 1073741824 | bytes 6291456 | tf_op jit(solution)/shard_map/mix/pallas_call | solution.py:340
  153.0 1.5 collective-permute-start.1
  154.5 13.0 %collective-permute-done.1.refs_1_ = bf16[512,512]{1,0:T(8,128)(2,1)S(1)} collective-permute-done((bf16[512,512]{1,0:T(8,128)(2,1)S(1)}, bf16[512,512]{1,0:T(8,128)(2,1)S(1)}, u32[]{:S(2)}, u32[]{:S(2)}) %collective-permute-start.1) | collective-permute-done | bytes 524320 | tf_op jit(solution)/shard_map/ppermute | solution.py:420
  167.5 2.2 %project_out.1 = bf16[512,1024]{1,0:T(8,128)(2,1)} custom-call(s32[1]{0:T(128)} %bitcast.me_ref, bf16[1024,1024]{1,0:T(8,128)(2,1)S(1)} %copy-done, bf16[512,512]{1,0:T(8,128)(2,1)S(1)} %get-tuple-element.22.refs_0_, bf16[512,512]{1,0:T(8,128)(2,1)S(1)} %collective-permute-done.1.refs_1_), custom_call_target="tpu_custom_call" | custom-call | flops 1073741824 | bytes 4194304 | tf_op jit(solution)/shard_map/project_out/pallas_call | solution.py:367
  (22 shorter events, 0.3 us)
Async XLA Ops:
  6.5 47.0 %all-gather.5.cloned.1.call-start = ((), (), s32[]{:S(2)}) async-start(), calls=%async_computation.3 | async-start | bytes 2228224 | tf_op jit(solution)/shard_map/all_gather | solution.py:393
  6.5 1.0 copy-start.3
  8.4 116.4 %all-gather.3.cloned.1.call-start = ((), (), s32[]{:S(2)}) async-start(), calls=%async_computation.2 | async-start | bytes 3342336 | tf_op jit(solution)/shard_map/all_gather | solution.py:394
  9.1 26.4 %collective-permute-start = (bf16[512,1024]{1,0:T(8,128)(2,1)}, bf16[512,1024]{1,0:T(8,128)(2,1)S(1)}, u32[]{:S(2)}, u32[]{:S(2)}) collective-permute-start(bf16[512,1024]{1,0:T(8,128)(2,1)} %bitcast.19), channel_id=1, source_target_pairs={{0,1},{1,0},{2,3},{3,2},{4,5},{5,4},{6,7},{7,6},{8,9},{9,8},{10,11... | collective-permute-start | bytes 3145736 | tf_op jit(solution)/shard_map/ppermute | solution.py:389
  35.5 1.2 copy-start.4
  46.0 1.3 copy-start.5
  53.5 1.6 copy-start.6
  63.3 1.1 copy-start.7
  64.4 3.8 %copy-start.9 = (f32[1,8,16]{2,1,0:T(8,128)S(1)}, f32[1,8,16]{2,1,0:T(8,128)}, u32[]{:S(2)}) copy-start(f32[1,8,16]{2,1,0:T(8,128)} %param.11) | copy-start | bytes 1540
  64.4 42.1 %all-to-all-start = ((bf16[16,256,128]{2,1,0:T(8,128)(2,1)}), bf16[16,256,128]{2,1,0:T(8,128)(2,1)S(1)}, u32[]{:S(2)}, u32[]{:S(2)}) async-start(bf16[16,256,128]{2,1,0:T(8,128)(2,1)} %bitcast.6), calls=%async_computation | async-start | bytes 2097152 | tf_op jit(solution)/shard_map/all_to_all | solution.py:401
  106.4 18.3 %copy-start.10 = (s32[16,4]{0,1:T(4,128)S(1)}, s32[16,4]{0,1:T(4,128)}, u32[]{:S(2)}) copy-start(s32[16,4]{0,1:T(4,128)} %param.10) | copy-start | bytes 772
  107.8 39.9 %all-to-all-start.1 = ((bf16[16,256,128]{2,1,0:T(8,128)(2,1)}), bf16[16,256,128]{2,1,0:T(8,128)(2,1)S(1)}, u32[]{:S(2)}, u32[]{:S(2)}) async-start(bf16[16,256,128]{2,1,0:T(8,128)(2,1)} %bitcast.8), calls=%async_computation.1 | async-start | bytes 2097152 | tf_op jit(solution)/shard_map/all_to_all | solution.py:412
  124.8 1.2 copy-start.8
  143.2 1.0 copy-start.1
  147.6 1.2 copy-start.2
  152.9 14.6 %copy-start = (bf16[1024,1024]{1,0:T(8,128)(2,1)S(1)}, bf16[1024,1024]{1,0:T(8,128)(2,1)}, u32[]{:S(2)}) copy-start(bf16[1024,1024]{1,0:T(8,128)(2,1)} %w_ref.3) | copy-start | bytes 6291460
  153.0 14.5 %collective-permute-start.1 = (bf16[512,512]{1,0:T(8,128)(2,1)S(1)}, bf16[512,512]{1,0:T(8,128)(2,1)S(1)}, u32[]{:S(2)}, u32[]{:S(2)}) collective-permute-start(bf16[512,512]{1,0:T(8,128)(2,1)S(1)} %get-tuple-element.21), channel_id=1, source_target_pairs={{0,1},{1,0},{2,3},{3,2},{4,5},{5,4},{6,7},{7,6},{8,9},{9,8},{10,11... | collective-permute-start | bytes 1572872 | tf_op jit(solution)/shard_map/ppermute | solution.py:420
Sparse Core Ops, SparseCore 0:
  9.5 43.9 all-gather.4
  55.8 54.8 all-gather.2

commit v2 on v1

v2 whole, which is shorter than its diff:
```python
import functools
import math

import jax
import jax.numpy as jnp
from jax import lax
from jax.experimental import pallas as pl
from jax.experimental.pallas import tpu as pltpu
from jax.sharding import PartitionSpec as P

HD = 64
N = 64
LANES = 2 * HD
PIECES = 5
EARLY = (2, 3)
LATE = (0, 1, 4)

epsilon = 1e-06

f32 = jnp.float32
bf16 = jnp.bfloat16


def params(mib=32):
    return pltpu.CompilerParams(vmem_limit_bytes=mib << 20)


def cost(flops, nbytes, transcendentals=0):
    return pl.CostEstimate(
        flops=int(flops), bytes_accessed=int(nbytes), transcendentals=int(transcendentals)
    )


def first_half(shape):
    return lax.broadcasted_iota(jnp.int32, shape, len(shape) - 1) < HD


class Plan:
    def __init__(self, frames, peers, heads_here):
        self.merge = 2 if frames % 2 == 0 and heads_here % 4 == 0 else 1
        self.frames, self.peers = frames, peers
        self.heads = heads_here // self.merge
        self.pairs = self.heads // 2
        self.chips = frames // self.merge
        self.across = 2 if self.chips % 2 == 0 else 1
        self.along = self.chips // self.across
        self.chained = self.along <= 4
        if self.chained:
            moves = [0] + [s * k for k in range(1, self.along) for s in (-1, 1)]
            self.sources = [(m, f) for f in range(self.across) for m in moves]
        else:
            self.sources = [None]

    def core(self):
        return lax.rem(lax.axis_index("tm"), self.merge)

    def chip(self):
        return lax.div(lax.axis_index("tm"), self.merge)

    def at(self, a, b, c):
        return (a * self.across + b) * self.merge + c

    def move(self, block, step, valid):
        pairs = [
            (self.at(a, b, c), self.at(a + step, b, c))
            for a in valid
            if 0 <= a + step < self.along
            for b in range(self.across)
            for c in range(self.merge)
        ]
        return lax.ppermute(block, "tm", pairs)

    def cross(self, block, valid):
        pairs = [
            (self.at(a, b, c), self.at(a, 1 - b, c))
            for a in valid
            for b in range(2)
            for c in range(self.merge)
        ]
        return lax.ppermute(block, "tm", pairs)

    def swap(self, block):
        return lax.ppermute(block, "tm", [(t, t ^ 1) for t in range(self.frames)])

    def to_peer(self, block, k, other):
        if not other:
            pairs = [(j, (j + k) % self.peers) for j in range(self.peers)]
            return lax.ppermute(block, "head", pairs)
        if k == 0:
            return self.swap(block)
        pairs = [
            (t * self.peers + j, (t ^ 1) * self.peers + (j + k) % self.peers)
            for t in range(self.frames)
            for j in range(self.peers)
        ]
        return lax.ppermute(block, ("tm", "head"), pairs)

    def groups(self):
        if self.merge == 1:
            return None
        return [[j * self.merge + c for j in range(self.chips)] for c in range(self.merge)]

    def gather(self, block, gate=None):
        if not self.chained:
            whole = lax.all_gather(
                block, "tm", axis=0, tiled=True, axis_index_groups=self.groups()
            )
            return [whole], None
        n = self.along
        found = {(0, 0): block}
        for k in range(1, n):
            found[-k, 0] = self.move(found[1 - k, 0], 1, range(k - 1, n))
            found[k, 0] = self.move(found[k - 1, 0], -1, range(0, n - k + 1))
        if self.across == 2:
            for m in [0] + [s * k for k in range(1, n) for s in (-1, 1)]:
                valid = range(max(0, -m), min(n, n - m))
                found[m, 1] = self.cross(found[m, 0], valid)
        return [found[s] for s in self.sources], (found.get((-1, 0)), found.get((1, 0)))

    def assemble(self, refs, out):
        if not self.chained:
            out[...] = refs[0][...]
            return
        rows = refs[0].shape[0]
        chip = self.chip()
        a, b = lax.div(chip, self.across), lax.rem(chip, self.across)
        for ref, (m, flip) in zip(refs, self.sources):
            there = jnp.clip(a + m, 0, self.along - 1)
            side = 1 - b if flip else b
            at = pl.multiple_of((there * self.across + side) * rows, rows)

            @pl.when((a + m >= 0) & (a + m < self.along))
            def _(ref=ref, at=at):
                out[pl.ds(at, rows), :] = ref[...]


def halves(shape, one, two):
    return jnp.where(first_half(shape), one, two)


def reorder_kernel(plan, *refs):
    w_refs, (early_ref, late_ref) = refs[: plan.merge], refs[plan.merge :]
    rows = w_refs[0].shape[0]
    width = plan.heads * PIECES * HD
    first = plan.core() == 0

    def chosen(ref, at):
        one = ref[:, at : at + HD]
        return one if plan.merge == 1 else jnp.where(first, one, ref[:, width + at : width + at + HD])

    for p in range(plan.pairs):
        for out_ref, kinds in ((early_ref, EARLY), (late_ref, LATE)):
            for j, i in enumerate(kinds):
                to = (p * len(kinds) + j) * LANES
                blocks = []
                for ref in w_refs:
                    one, two = (
                        chosen(ref, ((2 * p + h) * PIECES + i) * HD) for h in range(2)
                    )
                    blocks.append(jnp.concatenate([one, two], axis=1))
                for s, block in enumerate(blocks):
                    if plan.merge == 2:
                        block = jnp.where(first, block, blocks[1 - s])
                    out_ref[s * rows : (s + 1) * rows, to : to + LANES] = block


def reorder(plan, weights):
    rows = weights[0].shape[0]
    base = plan.heads * HD
    return pl.pallas_call(
        functools.partial(reorder_kernel, plan),
        out_shape=(
            jax.ShapeDtypeStruct((plan.merge * rows, base * len(EARLY)), bf16),
            jax.ShapeDtypeStruct((plan.merge * rows, base * len(LATE)), bf16),
        ),
        compiler_params=params(),
        cost_estimate=cost(0, 4 * weights[0].size),
        name="reorder",
    )(*weights)


def normalise(part, out, at):
    step = min(128, part.shape[0])

    def norm(c, _):
        start = pl.multiple_of(c * step, step)
        wide = part[pl.ds(start, step), :].astype(f32)
        scale = lax.rsqrt(jnp.mean(wide * wide, axis=-1, keepdims=True) + epsilon)
        out[pl.ds(at + start, step), :] = (wide * scale).astype(bf16)
        return 0

    lax.fori_loop(0, part.shape[0] // step, norm, 0)


def order_kernel(plan, groups, ids_row_ref, ids_col_ref, *refs):
    own_refs = refs[: plan.merge]
    x_ref, rest_ref, back_ref, normed = refs[plan.merge :]
    local = own_refs[0].shape[0]
    tokens = back_ref.shape[0]
    block = tokens // groups
    step = 128
    for s, own in enumerate(own_refs):
        normalise(own, normed, s * local)

    label = lax.broadcasted_iota(jnp.int32, (groups, tokens), 0)
    held = label == ids_row_ref[...]
    held_bf = jnp.where(held, 1.0, 0.0).astype(bf16)
    counts = []
    for c in range(tokens // 256):
        before = lax.broadcasted_iota(jnp.int32, (tokens, 256), 0) < (
            lax.broadcasted_iota(jnp.int32, (tokens, 256), 1) + c * 256
        )
        counts.append(
            jnp.dot(held_bf, jnp.where(before, 1.0, 0.0).astype(bf16), preferred_element_type=f32)
        )
    count = jnp.concatenate(counts, axis=1)
    rank_row = jnp.sum(
        jnp.where(held, count + (label * block).astype(f32), 0.0), axis=0, keepdims=True
    ).astype(jnp.int32)

    def place(c, _):
        at = pl.multiple_of(c * step, step)
        pick = (lax.broadcasted_iota(jnp.int32, (step, tokens), 0) + at) == rank_row
        pick = jnp.where(pick, 1.0, 0.0).astype(bf16)
        rest_ref[pl.ds(at, step), :] = pick[:, local:]
        for s in range(plan.merge):
            x_ref[pl.ds(s * tokens + at, step), :] = jnp.dot(
                pick[:, :local], normed[s * local : (s + 1) * local], preferred_element_type=f32
            ).astype(bf16)
        return 0

    lax.fori_loop(0, tokens // step, place, 0)

    lane = lax.broadcasted_iota(jnp.int32, (tokens, 128), 1)
    held_col = jnp.where(lane == ids_col_ref[...], 1.0, 0.0).astype(bf16)

    def place_back(c, _):
        at = pl.multiple_of(c * step, step)
        before = lax.broadcasted_iota(jnp.int32, (step, tokens), 1) < (
            lax.broadcasted_iota(jnp.int32, (step, tokens), 0) + at
        )
        count = jnp.dot(
            jnp.where(before, 1.0, 0.0).astype(bf16), held_col, preferred_element_type=f32
        )
        lane = lax.broadcasted_iota(jnp.int32, (step, 128), 1)
        mine = lane == ids_col_ref[pl.ds(at, step), :]
        rank = jnp.sum(
            jnp.where(mine, count + (lane * block).astype(f32), 0.0), axis=1, keepdims=True
        ).astype(jnp.int32)
        pick = lax.broadcasted_iota(jnp.int32, (step, tokens), 1) == rank
        back_ref[pl.ds(at, step), :] = jnp.where(pick, 1.0, 0.0).astype(bf16)
        return 0

    lax.fori_loop(0, tokens // step, place_back, 0)


def order(plan, ids, owns, groups):
    tokens = ids.shape[0]
    local, width = owns[0].shape
    return pl.pallas_call(
        functools.partial(order_kernel, plan, groups),
        out_shape=(
            jax.ShapeDtypeStruct((plan.merge * tokens, width), bf16),
            jax.ShapeDtypeStruct((tokens, tokens - local), bf16),
            jax.ShapeDtypeStruct((tokens, tokens), bf16),
        ),
        scratch_shapes=[pltpu.VMEM((plan.merge * local, width), bf16)],
        compiler_params=params(),
        cost_estimate=cost(2 * tokens * tokens * width, 6 * tokens * width),
        name="order",
    )(ids.reshape(1, tokens), ids.reshape(tokens, 1), *owns)


def decay_row(plan, ref, frame, pair, g, groups):
    heads_here = plan.heads * plan.merge
    at = (frame * heads_here + plan.core() * plan.heads + 2 * pair) * groups + g
    return halves((1, LANES), ref[at], ref[at + groups])


def update_kernel(plan, groups, parts, decay_ref, part_ref, rest_ref, *refs):
    n = plan.merge * parts
    frame_refs, w_refs = refs[:n], refs[n : n + len(plan.sources)]
    x_ref, v_ref, u_ref, total_ref, normed, w_scr, b_scr = refs[n + len(plan.sources) :]
    tokens = rest_ref.shape[0]
    block = tokens // groups
    step = 256
    plan.assemble(w_refs, w_scr)

    for s in range(plan.merge):
        at = 0
        for ref in frame_refs[s * parts : (s + 1) * parts]:
            normalise(ref, normed, at)
            at += ref.shape[0]

        def place(c, _, s=s):
            at = pl.multiple_of(c * step, step)
            there = pl.ds(s * tokens + at, step)
            more = jnp.dot(rest_ref[pl.ds(at, step), :], normed[...], preferred_element_type=f32)
            x_ref[there, :] = part_ref[there, :] + more.astype(bf16)
            return 0

        lax.fori_loop(0, tokens // step, place, 0)

    def project(c, _):
        at = pl.ds(pl.multiple_of(c * step, step), step)
        both = jnp.dot(x_ref[at, :], w_scr[...], preferred_element_type=f32).astype(bf16)
        for p in range(plan.pairs):
            cols = slice(p * LANES, (p + 1) * LANES)
            v_ref[at, cols] = both[:, 2 * p * LANES : (2 * p + 1) * LANES]
            b_scr[at, cols] = both[:, (2 * p + 1) * LANES : (2 * p + 2) * LANES]
        return 0

    lax.fori_loop(0, plan.merge * tokens // step, project, 0)

    for s in range(plan.merge):
        for p in range(plan.pairs):
            cols = slice(p * LANES, (p + 1) * LANES)
            for g in range(0, groups, 2):
                rows = slice(s * tokens + g * block, s * tokens + (g + 2) * block)
                turned = b_scr[rows, cols].astype(f32).T
                half = lax.broadcasted_iota(jnp.int32, turned.shape, 1) < block
                wide = jnp.concatenate(
                    [jnp.where(half, turned, 0.0), jnp.where(half, 0.0, turned)], axis=0
                ).astype(bf16)
                outer = jnp.dot(wide, v_ref[rows, cols], preferred_element_type=f32)
                for i in range(2):
                    at = (p * groups + g + i) * N
                    m = outer[i * 2 * N : (i + 1) * 2 * N]
                    u_ref[s, at : at + N, :] = halves((N, LANES), m[:N], m[N:])

    core = plan.core()
    for p in range(plan.pairs):
        for g in range(groups):
            rows = slice((p * groups + g) * N, (p * groups + g + 1) * N)
            total = u_ref[core, rows, :]
            if plan.merge == 2:
                last = plan.chip() * plan.merge + 1
                decay = decay_row(plan, decay_ref, last, p, g, groups)
                total = decay * total + u_ref[1 - core, rows, :]
            total_ref[rows, :] = total.astype(bf16)


def project_updates(plan, decays, part, rest, frames, weights, groups):
    tokens, width = rest.shape[0], part.shape[1]
    cols = weights[0].shape[1]
    rows = plan.pairs * groups * N
    vmem = pl.BlockSpec(memory_space=pltpu.VMEM)
    every = plan.merge * tokens
    return pl.pallas_call(
        functools.partial(update_kernel, plan, groups, len(frames) // plan.merge),
        in_specs=[pl.BlockSpec(memory_space=pltpu.SMEM)]
        + [vmem] * (2 + len(frames) + len(weights)),
        out_shape=(
            jax.ShapeDtypeStruct((every, width), bf16),
            jax.ShapeDtypeStruct((every, plan.pairs * LANES), bf16),
            jax.ShapeDtypeStruct((plan.merge, rows, LANES), f32),
            jax.ShapeDtypeStruct((rows, LANES), bf16),
        ),
        scratch_shapes=[
            pltpu.VMEM((rest.shape[1], width), bf16),
            pltpu.VMEM((width, cols), bf16),
            pltpu.VMEM((every, plan.pairs * LANES), bf16),
        ],
        compiler_params=params(),
        cost_estimate=cost(2 * every * width * (cols + rest.shape[1]), 6 * every * width),
        name="project_updates",
    )(decays, part, rest, *frames, *weights)


def scan_kernel(plan, groups, decay_ref, u_ref, s_ref):
    rows = u_ref.shape[1]
    step = min(rows, N)
    for i in range(rows // step):
        at = slice(i * step, (i + 1) * step)
        item = lax.div(plan.chip() * rows + i * step, N)
        pair, g = lax.div(item, groups), lax.rem(item, groups)
        state = jnp.zeros((step, LANES), f32)
        for j in range(plan.chips):
            s_ref[j, at, :] = state.astype(bf16)
            decay = decay_row(plan, decay_ref, j * plan.merge, pair, g, groups)
            for t in range(1, plan.merge):
                decay = decay * decay_row(plan, decay_ref, j * plan.merge + t, pair, g, groups)
            state = decay * state + u_ref[j, at, :].astype(f32)


def scan_states(plan, decays, update, groups):
    return pl.pallas_call(
        functools.partial(scan_kernel, plan, groups),
        in_specs=[
            pl.BlockSpec(memory_space=pltpu.SMEM),
            pl.BlockSpec(memory_space=pltpu.VMEM),
        ],
        out_shape=jax.ShapeDtypeStruct(update.shape, bf16),
        compiler_params=params(),
        cost_estimate=cost(2 * update.size, 4 * update.size),
        name="scan_states",
    )(decays, update)


def attend_kernel(plan, lists_ref, x_ref, v_ref, *refs):
    w_refs = refs[: len(plan.sources)]
    a_ref, c_ref, w_scr, q_ref, k_ref = refs[len(plan.sources) :]
    tokens = x_ref.shape[0]
    groups, chosen = lists_ref.shape
    block = tokens // groups
    step = 256
    per = step // block

    @pl.when(pl.program_id(0) == 0)
    def _():
        plan.assemble(w_refs, w_scr)

    def project(c, _):
        at = pl.multiple_of(c * step, step)
        rows = pl.ds(at, step)
        every = jnp.dot(x_ref[rows, :], w_scr[...], preferred_element_type=f32).astype(bf16)
        half = first_half((step, LANES))

        def head_norm(wide):
            square = wide * wide
            one = jnp.sum(jnp.where(half, square, 0.0), axis=-1, keepdims=True)
            two = jnp.sum(jnp.where(half, 0.0, square), axis=-1, keepdims=True)
            return wide * lax.rsqrt(jnp.where(half, one, two) * (1.0 / HD) + epsilon)

        for p in range(plan.pairs):
            cols = slice(p * LANES, (p + 1) * LANES)
            q, k, reader = (
                every[:, (3 * p + i) * LANES : (3 * p + i + 1) * LANES] for i in range(3)
            )
            c_ref[rows, cols] = reader
            k_ref[rows, cols] = head_norm(k.astype(f32)).astype(bf16)
            q = head_norm(q.astype(f32))
            one = jnp.where(half, q, 0.0).astype(bf16)
            two = jnp.where(half, 0.0, q).astype(bf16)
            for i in range(per):
                part = slice(i * block, (i + 1) * block)
                q_ref[p, c * per + i] = jnp.concatenate([one[part], two[part]], axis=0)
        return 0

    lax.fori_loop(0, tokens // step, project, 0)

    scale = math.log2(math.e) / math.sqrt(HD)
    for p in range(plan.pairs):
        cols = slice(p * LANES, (p + 1) * LANES)
        for g in range(groups):
            starts = [pl.multiple_of(lists_ref[g, j] * block, block) for j in range(chosen)]
            keys = jnp.concatenate([k_ref[pl.ds(s, block), cols] for s in starts], axis=0)
            values = jnp.concatenate([v_ref[pl.ds(s, block), cols] for s in starts], axis=0)
            score = lax.dot_general(
                q_ref[p, g], keys, (((1,), (1,)), ((), ())), preferred_element_type=f32
            )
            e = jnp.exp2(score * scale)
            weight = (e * (1.0 / jnp.sum(e, axis=-1, keepdims=True))).astype(bf16)
            both = jnp.dot(weight, values, preferred_element_type=f32)
            a_ref[g * block : (g + 1) * block, cols] = halves(
                (block, LANES), both[:block], both[block:]
            )


def attend(plan, lists, x, v, weights):
    every, width = x.shape
    groups, chosen = lists.shape
    tokens = every // plan.merge
    block = tokens // groups
    cols = weights[0].shape[1]
    part = pl.BlockSpec((tokens, plan.pairs * LANES), lambda s, _: (s, 0))
    return pl.pallas_call(
        functools.partial(attend_kernel, plan),
        grid_spec=pltpu.PrefetchScalarGridSpec(
            num_scalar_prefetch=1,
            grid=(plan.merge,),
            in_specs=[pl.BlockSpec((tokens, width), lambda s, _: (s, 0)), part]
            + [pl.BlockSpec(w.shape, lambda s, _: (0, 0)) for w in weights],
            out_specs=(part, part),
            scratch_shapes=[
                pltpu.VMEM((width, cols), bf16),
                pltpu.VMEM((plan.pairs, groups, 2 * block, LANES), bf16),
                pltpu.VMEM((tokens, plan.pairs * LANES), bf16),
            ],
        ),
        out_shape=(
            jax.ShapeDtypeStruct((every, plan.pairs * LANES), f32),
            jax.ShapeDtypeStruct((every, plan.pairs * LANES), bf16),
        ),
        compiler_params=params(),
        cost_estimate=cost(
            4 * every * width * cols,
            2 * (every * width + width * cols + 4 * every * plan.pairs * LANES),
            2 * plan.pairs * every * chosen * block,
        ),
        name="attend",
    )(lists, x, v, *weights)


def mix_kernel(plan, groups, decay_ref, a_ref, c_ref, s_ref, u_ref, back_ref, *refs):
    out_refs, mixed = refs[:-1], refs[-1]
    tokens = back_ref.shape[0]
    block = tokens // groups
    width = plan.pairs * LANES
    scale = 1.0 / (N * math.sqrt(block))
    core = plan.core()
    for p in range(plan.pairs):
        cols = slice(p * LANES, (p + 1) * LANES)
        for g in range(groups):
            items = slice((p * groups + g) * N, (p * groups + g + 1) * N)
            state = s_ref[items, :].astype(f32)
            for t in range(plan.merge):
                slot = core if t == 0 else 1 - core
                decay = decay_row(plan, decay_ref, plan.chip() * plan.merge + t, p, g, groups)
                state = decay * state + u_ref[slot, items, :]
                half = first_half((N, LANES))
                wide = jnp.concatenate(
                    [jnp.where(half, state, 0.0), jnp.where(half, 0.0, state)], axis=0
                ).astype(bf16)
                rows = pl.ds(pl.multiple_of(slot * tokens + g * block, block), block)
                read = jnp.dot(c_ref[rows, cols], wide, preferred_element_type=f32)
                mixed[slot, g * block : (g + 1) * block, cols] = (
                    a_ref[rows, cols] + read * scale
                ).astype(bf16)
    local = out_refs[0].shape[0]
    for s in range(plan.merge):
        for k in range(plan.peers):
            out_refs[s * plan.peers + k][...] = jnp.dot(
                back_ref[k * local : (k + 1) * local, :], mixed[s], preferred_element_type=f32
            ).astype(bf16)


def mix(plan, decays, attended, readers, state, updates, back, groups):
    tokens = back.shape[0]
    width = attended.shape[1]
    out = jax.ShapeDtypeStruct((tokens // plan.peers, width), bf16)
    vmem = pl.BlockSpec(memory_space=pltpu.VMEM)
    return pl.pallas_call(
        functools.partial(mix_kernel, plan, groups),
        in_specs=[pl.BlockSpec(memory_space=pltpu.SMEM)] + [vmem] * 5,
        out_shape=(out,) * (plan.merge * plan.peers),
        scratch_shapes=[pltpu.VMEM((plan.merge, tokens, width), bf16)],
        compiler_params=params(),
        cost_estimate=cost(4 * tokens * tokens * width, 2 * tokens * tokens + 16 * tokens * width),
        name="mix",
    )(decays, attended, readers, state, updates, back)


def out_kernel(plan, w_ref, *refs):
    part_refs, out_ref = refs[:-1], refs[-1]
    depth = part_refs[0].shape[1]
    core, me = plan.core(), lax.axis_index("head")
    total = None
    for s in range(plan.merge):
        for k in range(plan.peers):
            owner = lax.rem(me - k + plan.peers, plan.peers) * plan.merge
            owner = owner + (core if s == 0 else 1 - core)
            rows = pl.ds(pl.multiple_of(owner * depth, depth), depth)
            term = jnp.dot(
                part_refs[s * plan.peers + k][...], w_ref[rows, :], preferred_element_type=f32
            )
            total = term if total is None else total + term
    out_ref[...] = total.astype(bf16)


def project_out(plan, w, parts):
    local = parts[0].shape[0]
    width = w.shape[1]
    return pl.pallas_call(
        functools.partial(out_kernel, plan),
        out_shape=jax.ShapeDtypeStruct((local, width), bf16),
        compiler_params=params(),
        cost_estimate=cost(2 * local * w.size, 2 * (w.size + 2 * local * width)),
        name="project_out",
    )(w, *parts)


def body(frames_in, in_weight, out_weight, block_ids, block_lists, decays):
    local_tokens = frames_in.shape[1]
    heads_here = decays.shape[1]
    groups = block_lists.shape[0]
    me = lax.axis_index("head")
    plan = Plan(lax.axis_size("tm"), lax.axis_size("head"), heads_here)

    weights = [in_weight] + [plan.swap(in_weight)] * (plan.merge - 1)
    early, late = reorder(plan, weights)

    own = frames_in[0]
    chunks = 2 if local_tokens >= 512 else 1
    arriving = [
        plan.to_peer(chunk, plan.peers - k, False)
        for k in range(1, plan.peers)
        for chunk in jnp.split(own, chunks)
    ]
    owns = [own]
    if plan.merge == 2:
        owns.append(plan.swap(own))
        arriving = arriving + [plan.swap(chunk) for chunk in arriving]

    w_early, gate = plan.gather(early)
    if gate is not None:
        late, _ = lax.optimization_barrier((late, gate))
    w_late, _ = plan.gather(late)

    ids = jnp.roll(block_ids, -me * local_tokens)
    all_decays = lax.all_gather(decays[0], "tm", axis=0).reshape(-1)
    ids, all_decays = lax.optimization_barrier((ids, all_decays))
    part, rest, back = order(plan, ids, owns, groups)
    x, v, updates, total = project_updates(
        plan, all_decays, part, rest, arriving, w_early, groups
    )

    def exchange(blocks):
        return lax.all_to_all(
            blocks, "tm", split_axis=0, concat_axis=0, tiled=True,
            axis_index_groups=plan.groups(),
        )

    rows = total.shape[0] // plan.chips
    arrived = exchange(total.reshape(plan.chips, rows, LANES))
    states = scan_states(plan, all_decays, arrived, groups)
    state = exchange(states).reshape(total.shape)

    attended, readers = attend(plan, block_lists, x, v, w_late)
    mixed = mix(plan, all_decays, attended, readers, state, updates, back, groups)
    features = [
        mixed[0] if s == 0 and k == 0 else plan.to_peer(mixed[s * plan.peers + k], k, s == 1)
        for s in range(plan.merge)
        for k in range(plan.peers)
    ]
    return project_out(plan, out_weight, features)[None]


def solution(mesh):
    return jax.shard_map(
        body,
        mesh=mesh,
        in_specs=(P("tm", "head", None), P("tm", "head"), P(), P(), P(), P("tm", "head", None)),
        out_specs=P("tm", "head", None),
        check_vma=False,
    )
```

time: 178 us -> 200 us (1.12)
  starting transfers between devices: 25.3 us -> 63.9 us
  blocking collectives: 37.6 us -> 23.2 us
  between operations: 13.6 us -> 0.57 us
  local copies, waits for them, and re-layouts: 10.6 us -> 21.5 us
  waiting for transfers between devices: 45.7 us -> 51.2 us
  Pallas kernels: 43 us -> 38 us
    ppermute x2 -> x35, starting transfers between devices: 4.57 us -> 54.2 us  [the longest x14 28.3 us: cross(): return lax.ppermute(block, 'tm', pairs)]
    ppermute x2 -> x35, waiting for transfers between devices: 35.3 us -> 51.2 us  [the longest x12 21 us: move(): return lax.ppermute(block, 'tm', pairs)]
    all_gather x1, blocking collectives: 37.6 us -> 23.2 us  [body(): all_decays = lax.all_gather(decays[0], 'tm', axis=0).reshape(-1)]
    all_to_all x2, starting transfers between devices: 20.7 us -> 9.7 us  [exchange(): lax.all_to_all(blocks, 'tm', split_axis=0, concat_axis=0, tiled=True, axi...]
    unnamed x23 -> x67, local copies, waits for them, and re-layouts: 9.69 us -> 19.1 us
    all_gather x2 -> x0, waiting for transfers between devices: 6.19 us -> none  [the longest x1 6.19 us: body(): w_early = lax.all_gather(early, 'tm', axis=0, tiled=True)]
    pallas_call x7, Pallas kernels: 43 us -> 38 us  [the longest x1 11.7 us: attend(): pl.pallas_call(functools.partial(attend_kernel, plan), grid_spec=pltpu.Pr...]
    all_to_all x2, waiting for transfers between devices: 3.45 us -> 0.01 us  [exchange(): lax.all_to_all(blocks, 'tm', split_axis=0, concat_axis=0, tiled=True, axi...]
  transfers between devices with their start and end apart: 6 -> 37, of which waited for: 4 -> 12; matrix products, arithmetic and copies ran while one was open for 1% -> 1% of each run, Pallas kernels for 20% -> 11%
where the time goes in v2:
time: 200 us; the launch traced here: 198 us
  starting transfers between devices  63.9 us (32%)
  waiting for transfers between devices  51.2 us (26%)
  Pallas kernels  38 us (19%)
  blocking collectives  23.2 us (12%)
  local copies, waits for them, and re-layouts  21.5 us (11%)
    ppermute x14, starting transfers between devices, cross(): return lax.ppermute(block, 'tm', pairs)  28.3 us
    all_gather x1, blocking collectives, body(): all_decays = lax.all_gather(decays[0], 'tm', axis=0).reshape(-1)  23.2 us
    ppermute x12, waiting for transfers between devices, move(): return lax.ppermute(block, 'tm', pairs)  21 us
    ppermute x12, starting transfers between devices, move(): return lax.ppermute(block, 'tm', pairs)  19.5 us
    unnamed x67, local copies, waits for them, and re-layouts  19.1 us
    ppermute x3, waiting for transfers between devices, to_peer(): return lax.ppermute(block, 'head', pairs)  16.9 us
    pallas_call x1, Pallas kernels, attend(): pl.pallas_call(functools.partial(attend_kernel, plan), grid_spec=pltpu.Pr...  11.7 us
    pallas_call x1, Pallas kernels, project_updates(): pl.pallas_call(functools.partial(update_kernel, plan, groups, len(frames)...  11.7 us
  transfers between devices with their start and end apart: 37, of which 12 were waited for; matrix products, arithmetic and copies ran while one was open for 1% of the time, Pallas kernels for 11%

profile of v2, /device:TPU:0, one launch (start us, length us, event | category | flops | bytes accessed | tf_op | source)
XLA Modules:
  0.0 198.4 jit_solution(9023850300891565741)
XLA Ops:
  1.9 3.0 %collective-permute-start.1 = (bf16[256,1024]{1,0:T(8,128)(2,1)S(1)}, bf16[256,1024]{1,0:T(8,128)(2,1)}, u32[]{:S(2)}, u32[]{:S(2)}) collective-permute-start(bf16[256,1024]{1,0:T(8,128)(2,1)S(1)} %get-tuple-element.42), channel_id=1, source_target_pairs={{0,1},{1,0},{2,3},{3,2},{4,5},{5,4},{6,7},{7,6},{8,9},{9,8},{10,11... | collective-permute-start | bytes 1572872 | tf_op jit(solution)/shard_map/ppermute | solution.py:88
  5.2 3.9 %collective-permute-start.6 = (bf16[128,512]{1,0:T(8,128)(2,1)S(1)}, bf16[128,512]{1,0:T(8,128)(2,1)S(1)}, u32[]{:S(2)}, u32[]{:S(2)}) collective-permute-start(bf16[128,512]{1,0:T(8,128)(2,1)S(1)} %get-tuple-element.27.refs_4_), channel_id=1, source_target_pairs={{0,8},{2,10},{4,12},{6,14},{8,16},{10,18},{12,20},{14,22},{16,24},... | collective-permute-start | bytes 393224 | tf_op jit(solution)/shard_map/ppermute | solution.py:71
  13.1 2.9 %collective-permute-done.7.refs_6_ = bf16[128,512]{1,0:T(8,128)(2,1)S(1)} collective-permute-done((bf16[128,512]{1,0:T(8,128)(2,1)S(1)}, bf16[128,512]{1,0:T(8,128)(2,1)S(1)}, u32[]{:S(2)}, u32[]{:S(2)}) %collective-permute-start.7) | collective-permute-done | bytes 131104 | tf_op jit(solution)/shard_map/ppermute | solution.py:71
  18.6 9.8 %collective-permute-done.2.refs_1_ = bf16[256,1024]{1,0:T(8,128)(2,1)} collective-permute-done((bf16[256,1024]{1,0:T(8,128)(2,1)S(1)}, bf16[256,1024]{1,0:T(8,128)(2,1)}, u32[]{:S(2)}, u32[]{:S(2)}) %collective-permute-start.2) | collective-permute-done | bytes 524320 | tf_op jit(solution)/shard_map/ppermute | solution.py:88
  28.9 3.6 %collective-permute-start.14 = (bf16[128,512]{1,0:T(8,128)(2,1)S(1)}, bf16[128,512]{1,0:T(8,128)(2,1)S(1)}, u32[]{:S(2)}, u32[]{:S(2)}) collective-permute-start(bf16[128,512]{1,0:T(8,128)(2,1)S(1)} %collective-permute-done.7.refs_6_), channel_id=1, source_target_pairs={{0,4},{2,6},{4,0},{6,2},{8,12},{10,14},{12,8},{14,10},{16,20},{18,... | collective-permute-start | bytes 393224 | tf_op jit(solution)/shard_map/ppermute | solution.py:80
  33.9 2.4 %collective-permute-done.14.refs_13_ = bf16[128,512]{1,0:T(8,128)(2,1)S(1)} collective-permute-done((bf16[128,512]{1,0:T(8,128)(2,1)S(1)}, bf16[128,512]{1,0:T(8,128)(2,1)S(1)}, u32[]{:S(2)}, u32[]{:S(2)}) %collective-permute-start.14) | collective-permute-done | bytes 131104 | tf_op jit(solution)/shard_map/ppermute | solution.py:80
  38.9 23.2 %all_gather.3 = f32[16,8,16]{2,1,0:T(8,128)S(1)} all-gather(f32[1,8,16]{2,1,0:T(8,128)S(1)} %copy-done.30), channel_id=1, replica_groups=mesh['tm'=16,'head'=2] {'tm'}, dimensions={0}, use_global_device_ids=true | all-gather | bytes 8704 | tf_op jit(solution)/shard_map/all_gather | solution.py:601
  63.4 1.9 collective-permute-start.16
  67.6 3.9 %collective-permute-start.18 = (bf16[128,512]{1,0:T(8,128)(2,1)}, bf16[128,512]{1,0:T(8,128)(2,1)S(1)}, u32[]{:S(2)}, u32[]{:S(2)}) collective-permute-start(bf16[128,512]{1,0:T(8,128)(2,1)} %collective-permute-done.11.refs_10_), channel_id=1, source_target_pairs={{0,4},{2,6},{4,0},{6,2},{1,5},{3,7},{5,1},{7,3}} | collective-permute-start | bytes 393224 | tf_op jit(solution)/shard_map/ppermute | solution.py:80
  73.9 7.9 %order.1 = (bf16[2048,1024]{1,0:T(8,128)(2,1)S(1)}, bf16[1024,512]{1,0:T(8,128)(2,1)S(1)}, bf16[1024,1024]{1,0:T(8,128)(2,1)S(1)}) custom-call(s32[1,1024]{1,0:T(1,128)S(1)} %bitcast.14, s32[1024,1]{1,0:T(8,128)S(1)} %copy-done.8, bf16[512,1024]{1,0:T(8,128)(2,1)S(1)} %bitcast.12, bf16[512,1024]{1,0:T(8,128)(2,1)S(1)} %copy-done.11), custom_call_target="tpu_custom_call" | custom-call | flops 2147483648 | bytes 6291456 | tf_op jit(solution)/shard_map/order/pallas_call | solution.py:260
  81.9 11.7 %project_updates.1 = (bf16[2048,1024]{1,0:T(8,128)(2,1)S(1)}, bf16[2048,256]{1,0:T(8,128)(2,1)S(1)}, f32[2,2048,128]{2,1,0:T(8,128)S(1)}, bf16[2048,128]{1,0:T(8,128)(2,1)}) custom-call(f32[2048]{0:T(1024)S(1)} %reshape.17.decay_ref, bf16[2048,1024]{1,0:T(8,128)(2,1)S(1)} %get-tuple-element.25.part_ref, bf16[1024,512]{1,0:T(8,128)(2,1)S(1)} %get-tuple-element.26.rest_ref, ...), custom_call_target="tpu_custom_call" | custom-call | flops 4294967296 | bytes 12582912 | tf_op jit(solution)/shard_map/project_updates/pallas_call | solution.py:349
  95.0 2.0 copy-done.26
  98.0 3.6 %all-to-all-start = ((bf16[8,256,128]{2,1,0:T(8,128)(2,1)}), bf16[8,256,128]{2,1,0:T(8,128)(2,1)S(1)}, u32[]{:S(2)}, u32[]{:S(2)}) async-start(bf16[8,256,128]{2,1,0:T(8,128)(2,1)} %bitcast.5), calls=%async_computation | async-start | bytes 1048576 | tf_op jit(solution)/shard_map/all_to_all | solution.py:609
  101.6 3.8 %collective-permute-start.19 = (bf16[128,768]{1,0:T(8,128)(2,1)S(1)}, bf16[128,768]{1,0:T(8,128)(2,1)S(1)}, u32[]{:S(2)}, u32[]{:S(2)}) collective-permute-start(bf16[128,768]{1,0:T(8,128)(2,1)S(1)} %get-tuple-element.31.refs_0_), channel_id=1, source_target_pairs={{0,8},{2,10},{4,12},{6,14},{8,16},{10,18},{12,20},{14,22},{16,24},... | collective-permute-start | bytes 589832 | tf_op jit(solution)/shard_map/ppermute | solution.py:71
  106.7 7.9 %collective-permute-done.19.refs_1_ = bf16[128,768]{1,0:T(8,128)(2,1)S(1)} collective-permute-done((bf16[128,768]{1,0:T(8,128)(2,1)S(1)}, bf16[128,768]{1,0:T(8,128)(2,1)S(1)}, u32[]{:S(2)}, u32[]{:S(2)}) %collective-permute-start.19) | collective-permute-done | bytes 196640 | tf_op jit(solution)/shard_map/ppermute | solution.py:71
  115.3 1.7 collective-permute-done.20.refs_2_
  122.4 7.3 %collective-permute-done.22.refs_4_ = bf16[128,768]{1,0:T(8,128)(2,1)} collective-permute-done((bf16[128,768]{1,0:T(8,128)(2,1)S(1)}, bf16[128,768]{1,0:T(8,128)(2,1)}, u32[]{:S(2)}, u32[]{:S(2)}) %collective-permute-start.22) | collective-permute-done | bytes 196640 | tf_op jit(solution)/shard_map/ppermute | solution.py:71
  131.1 1.6 scan_states.1
  132.7 6.1 %all-to-all-start.1 = ((bf16[8,256,128]{2,1,0:T(8,128)(2,1)}), bf16[8,256,128]{2,1,0:T(8,128)(2,1)S(1)}, u32[]{:S(2)}, u32[]{:S(2)}) async-start(bf16[8,256,128]{2,1,0:T(8,128)(2,1)} %scan_states.1), calls=%async_computation.1 | async-start | bytes 1048576 | tf_op jit(solution)/shard_map/all_to_all | solution.py:609
  138.8 3.9 %collective-permute-start.27 = (bf16[128,768]{1,0:T(8,128)(2,1)S(1)}, bf16[128,768]{1,0:T(8,128)(2,1)}, u32[]{:S(2)}, u32[]{:S(2)}) collective-permute-start(bf16[128,768]{1,0:T(8,128)(2,1)S(1)} %collective-permute-done.20.refs_2_), channel_id=1, source_target_pairs={{0,4},{2,6},{4,0},{6,2},{8,12},{10,14},{12,8},{14,10},{16,20},{18,... | collective-permute-start | bytes 589832 | tf_op jit(solution)/shard_map/ppermute | solution.py:80
  144.1 1.9 collective-permute-start.29
  147.3 4.1 %collective-permute-start.31 = (bf16[128,768]{1,0:T(8,128)(2,1)}, bf16[128,768]{1,0:T(8,128)(2,1)}, u32[]{:S(2)}, u32[]{:S(2)}) collective-permute-start(bf16[128,768]{1,0:T(8,128)(2,1)} %collective-permute-done.24.refs_6_), channel_id=1, source_target_pairs={{0,4},{2,6},{4,0},{6,2},{1,5},{3,7},{5,1},{7,3}} | collective-permute-start | bytes 589832 | tf_op jit(solution)/shard_map/ppermute | solution.py:80
  151.8 4.2 %collective-permute-done.29.refs_11_ = bf16[128,768]{1,0:T(8,128)(2,1)} collective-permute-done((bf16[128,768]{1,0:T(8,128)(2,1)}, bf16[128,768]{1,0:T(8,128)(2,1)}, u32[]{:S(2)}, u32[]{:S(2)}) %collective-permute-start.29) | collective-permute-done | bytes 196640 | tf_op jit(solution)/shard_map/ppermute | solution.py:80
  156.0 3.4 %collective-permute-done.31.refs_13_ = bf16[128,768]{1,0:T(8,128)(2,1)} collective-permute-done((bf16[128,768]{1,0:T(8,128)(2,1)}, bf16[128,768]{1,0:T(8,128)(2,1)}, u32[]{:S(2)}, u32[]{:S(2)}) %collective-permute-start.31) | collective-permute-done | bytes 196640 | tf_op jit(solution)/shard_map/ppermute | solution.py:80
  159.4 2.2 %copy-done.27 = bf16[2048,1024]{1,0:T(8,128)(2,1)S(1)} copy-done((bf16[2048,1024]{1,0:T(8,128)(2,1)S(1)}, bf16[2048,1024]{1,0:T(8,128)(2,1)}, u32[]{:S(2)}) %copy-start.27) | copy-done | bytes 4194328
  162.8 11.7 %attend.1 = (f32[2048,256]{1,0:T(8,128)S(1)}, bf16[2048,256]{1,0:T(8,128)(2,1)S(1)}) custom-call(s32[16,4]{1,0:T(8,128)S(1)} %copy.11.lists_ref, bf16[2048,1024]{1,0:T(8,128)(2,1)S(1)} %copy-done.27, bf16[2048,256]{1,0:T(8,128)(2,1)S(1)} %copy-done.29, bf16[128,768]{1,0:T(8,128)(2,1)S(1)} %get-tuple-element.31.refs_0_, ...), custom_call_target="tpu_custom_call" | custom-call | flops 6442450944 | bytes 9961472 | tf_op jit(solution)/shard_map/attend/pallas_call | solution.py:467
  176.9 1.6 copy-done.1
  178.5 1.6 copy-done.3
  181.3 2.6 %mix.1 = (bf16[512,256]{1,0:T(8,128)(2,1)S(1)}, bf16[512,256]{1,0:T(8,128)(2,1)S(1)}, bf16[512,256]{1,0:T(8,128)(2,1)S(1)}, bf16[512,256]{1,0:T(8,128)(2,1)S(1)}) custom-call(f32[2048]{0:T(1024)S(1)} %reshape.17.decay_ref, f32[2048,256]{1,0:T(8,128)S(1)} %copy-done.3, bf16[2048,256]{1,0:T(8,128)(2,1)S(1)} %copy-done.6, bf16[2048,128]{1,0:T(8,128)(2,1)S(1)} %bitcast.10, ...), custom_call_target="tpu_custom_call" | custom-call | flops 1073741824 | bytes 6291456 | tf_op jit(solution)/shard_map/mix/pallas_call | solution.py:533
  186.1 7.1 %collective-permute-done.32.refs_1_ = bf16[512,256]{1,0:T(8,128)(2,1)S(1)} collective-permute-done((bf16[512,256]{1,0:T(8,128)(2,1)S(1)}, bf16[512,256]{1,0:T(8,128)(2,1)S(1)}, u32[]{:S(2)}, u32[]{:S(2)}) %collective-permute-start.32) | collective-permute-done | bytes 262176 | tf_op jit(solution)/shard_map/ppermute | solution.py:88
  193.2 3.0 %collective-permute-done.34.refs_3_ = bf16[512,256]{1,0:T(8,128)(2,1)S(1)} collective-permute-done((bf16[512,256]{1,0:T(8,128)(2,1)S(1)}, bf16[512,256]{1,0:T(8,128)(2,1)S(1)}, u32[]{:S(2)}, u32[]{:S(2)}) %collective-permute-start.34) | collective-permute-done | bytes 262176 | tf_op jit(solution)/shard_map/ppermute | solution.py:96
  196.2 2.2 %project_out.1 = bf16[512,1024]{1,0:T(8,128)(2,1)} custom-call(bf16[1024,1024]{1,0:T(8,128)(2,1)S(1)} %copy-done.4, bf16[512,256]{1,0:T(8,128)(2,1)S(1)} %get-tuple-element.37.refs_0_, bf16[512,256]{1,0:T(8,128)(2,1)S(1)} %collective-permute-done.32.refs_1_, bf16[512,256]{1,0:T(8,128)(2,1)S(1)} %collective-permute-done.33.refs_2_, ...), custom_call_target="tpu_custom_call" | custom-call | flops 1073741824 | bytes 4194304 | tf_op jit(solution)/shard_map/project_out/pallas_call | solution.py:564
  (121 shorter events, 40.0 us)
Async XLA Ops:
  0.0 66.6 %collective-permute-start = (bf16[512,1024]{1,0:T(8,128)(2,1)}, bf16[512,1024]{1,0:T(8,128)(2,1)S(1)}, u32[]{:S(2)}, u32[]{:S(2)}) collective-permute-start(bf16[512,1024]{1,0:T(8,128)(2,1)} %bitcast.11), channel_id=1, source_target_pairs={{0,2},{2,0},{4,6},{6,4},{8,10},{10,8},{12,14},{14,12},{16,18},{18,... | collective-permute-start | bytes 3145736 | tf_op jit(solution)/shard_map/ppermute | solution.py:83
  1.9 16.0 %collective-permute-start.1 = (bf16[256,1024]{1,0:T(8,128)(2,1)S(1)}, bf16[256,1024]{1,0:T(8,128)(2,1)}, u32[]{:S(2)}, u32[]{:S(2)}) collective-permute-start(bf16[256,1024]{1,0:T(8,128)(2,1)S(1)} %get-tuple-element.42), channel_id=1, source_target_pairs={{0,1},{1,0},{2,3},{3,2},{4,5},{5,4},{6,7},{7,6},{8,9},{9,8},{10,11... | collective-permute-start | bytes 1572872 | tf_op jit(solution)/shard_map/ppermute | solution.py:88
  4.9 23.5 %collective-permute-start.2 = (bf16[256,1024]{1,0:T(8,128)(2,1)S(1)}, bf16[256,1024]{1,0:T(8,128)(2,1)}, u32[]{:S(2)}, u32[]{:S(2)}) collective-permute-start(bf16[256,1024]{1,0:T(8,128)(2,1)S(1)} %get-tuple-element.41), channel_id=1, source_target_pairs={{0,1},{1,0},{2,3},{3,2},{4,5},{5,4},{6,7},{7,6},{8,9},{9,8},{10,11... | collective-permute-start | bytes 1572872 | tf_op jit(solution)/shard_map/ppermute | solution.py:88
  9.1 6.9 %collective-permute-start.7 = (bf16[128,512]{1,0:T(8,128)(2,1)S(1)}, bf16[128,512]{1,0:T(8,128)(2,1)S(1)}, u32[]{:S(2)}, u32[]{:S(2)}) collective-permute-start(bf16[128,512]{1,0:T(8,128)(2,1)S(1)} %get-tuple-element.27.refs_4_), channel_id=1, source_target_pairs={{8,0},{10,2},{12,4},{14,6},{16,8},{18,10},{20,12},{22,14},{24,16},... | collective-permute-start | bytes 393224 | tf_op jit(solution)/shard_map/ppermute | solution.py:71
  15.9 12.5 %collective-permute-start.8 = (bf16[128,512]{1,0:T(8,128)(2,1)S(1)}, bf16[128,512]{1,0:T(8,128)(2,1)S(1)}, u32[]{:S(2)}, u32[]{:S(2)}) collective-permute-start(bf16[128,512]{1,0:T(8,128)(2,1)S(1)} %collective-permute-done.6.refs_5_), channel_id=1, source_target_pairs={{8,16},{10,18},{12,20},{14,22},{16,24},{18,26},{20,28},{22,30},{9,... | collective-permute-start | bytes 393224 | tf_op jit(solution)/shard_map/ppermute | solution.py:71
  16.6 12.3 %collective-permute-start.9 = (bf16[128,512]{1,0:T(8,128)(2,1)S(1)}, bf16[128,512]{1,0:T(8,128)(2,1)}, u32[]{:S(2)}, u32[]{:S(2)}) collective-permute-start(bf16[128,512]{1,0:T(8,128)(2,1)S(1)} %collective-permute-done.7.refs_6_), channel_id=1, source_target_pairs={{8,0},{10,2},{12,4},{14,6},{16,8},{18,10},{20,12},{22,14},{9,1},{1... | collective-permute-start | bytes 393224 | tf_op jit(solution)/shard_map/ppermute | solution.py:71
  17.9 14.6 %collective-permute-start.13 = (bf16[128,512]{1,0:T(8,128)(2,1)S(1)}, bf16[128,512]{1,0:T(8,128)(2,1)S(1)}, u32[]{:S(2)}, u32[]{:S(2)}) collective-permute-start(bf16[128,512]{1,0:T(8,128)(2,1)S(1)} %collective-permute-done.6.refs_5_), channel_id=1, source_target_pairs={{8,12},{10,14},{12,8},{14,10},{16,20},{18,22},{20,16},{22,18},{24,... | collective-permute-start | bytes 393224 | tf_op jit(solution)/shard_map/ppermute | solution.py:80
  28.4 53.4 %collective-permute-start.3 = (bf16[256,1024]{1,0:T(8,128)(2,1)}, bf16[256,1024]{1,0:T(8,128)(2,1)}, u32[]{:S(2)}, u32[]{:S(2)}) collective-permute-start(bf16[256,1024]{1,0:T(8,128)(2,1)} %collective-permute-done.1.refs_0_), channel_id=1, source_target_pairs={{0,2},{2,0},{4,6},{6,4},{8,10},{10,8},{12,14},{14,12},{16,18},{18,... | collective-permute-start | bytes 1572872 | tf_op jit(solution)/shard_map/ppermute | solution.py:83
  28.4 53.4 %collective-permute-start.4 = (bf16[256,1024]{1,0:T(8,128)(2,1)}, bf16[256,1024]{1,0:T(8,128)(2,1)}, u32[]{:S(2)}, u32[]{:S(2)}) collective-permute-start(bf16[256,1024]{1,0:T(8,128)(2,1)} %collective-permute-done.2.refs_1_), channel_id=1, source_target_pairs={{0,2},{2,0},{4,6},{6,4},{8,10},{10,8},{12,14},{14,12},{16,18},{18,... | collective-permute-start | bytes 1572872 | tf_op jit(solution)/shard_map/ppermute | solution.py:83
  28.9 7.4 %collective-permute-start.14 = (bf16[128,512]{1,0:T(8,128)(2,1)S(1)}, bf16[128,512]{1,0:T(8,128)(2,1)S(1)}, u32[]{:S(2)}, u32[]{:S(2)}) collective-permute-start(bf16[128,512]{1,0:T(8,128)(2,1)S(1)} %collective-permute-done.7.refs_6_), channel_id=1, source_target_pairs={{0,4},{2,6},{4,0},{6,2},{8,12},{10,14},{12,8},{14,10},{16,20},{18,... | collective-permute-start | bytes 393224 | tf_op jit(solution)/shard_map/ppermute | solution.py:80
  36.9 26.4 %collective-permute-start.11 = (bf16[128,512]{1,0:T(8,128)(2,1)}, bf16[128,512]{1,0:T(8,128)(2,1)}, u32[]{:S(2)}, u32[]{:S(2)}) collective-permute-start(bf16[128,512]{1,0:T(8,128)(2,1)} %collective-permute-done.9.refs_8_), channel_id=1, source_target_pairs={{8,0},{10,2},{12,4},{14,6},{9,1},{11,3},{13,5},{15,7}} | collective-permute-start | bytes 393224 | tf_op jit(solution)/shard_map/ppermute | solution.py:71
  38.2 27.1 %collective-permute-start.15 = (bf16[128,512]{1,0:T(8,128)(2,1)S(1)}, bf16[128,512]{1,0:T(8,128)(2,1)S(1)}, u32[]{:S(2)}, u32[]{:S(2)}) collective-permute-start(bf16[128,512]{1,0:T(8,128)(2,1)S(1)} %collective-permute-done.8.refs_7_), channel_id=1, source_target_pairs={{16,20},{18,22},{20,16},{22,18},{24,28},{26,30},{28,24},{30,26},{1... | collective-permute-start | bytes 393224 | tf_op jit(solution)/shard_map/ppermute | solution.py:80
  63.4 18.5 %collective-permute-start.16 = (bf16[128,512]{1,0:T(8,128)(2,1)}, bf16[128,512]{1,0:T(8,128)(2,1)S(1)}, u32[]{:S(2)}, u32[]{:S(2)}) collective-permute-start(bf16[128,512]{1,0:T(8,128)(2,1)} %collective-permute-done.9.refs_8_), channel_id=1, source_target_pairs={{0,4},{2,6},{4,0},{6,2},{8,12},{10,14},{12,8},{14,10},{1,5},{3,7},... | collective-permute-start | bytes 393224 | tf_op jit(solution)/shard_map/ppermute | solution.py:80
  65.9 15.9 %collective-permute-start.17 = (bf16[128,512]{1,0:T(8,128)(2,1)}, bf16[128,512]{1,0:T(8,128)(2,1)S(1)}, u32[]{:S(2)}, u32[]{:S(2)}) collective-permute-start(bf16[128,512]{1,0:T(8,128)(2,1)} %collective-permute-done.10.refs_9_), channel_id=1, source_target_pairs={{24,28},{26,30},{28,24},{30,26},{25,29},{27,31},{29,25},{31,27}} | collective-permute-start | bytes 393224 | tf_op jit(solution)/shard_map/ppermute | solution.py:80
  67.6 14.2 %collective-permute-start.18 = (bf16[128,512]{1,0:T(8,128)(2,1)}, bf16[128,512]{1,0:T(8,128)(2,1)S(1)}, u32[]{:S(2)}, u32[]{:S(2)}) collective-permute-start(bf16[128,512]{1,0:T(8,128)(2,1)} %collective-permute-done.11.refs_10_), channel_id=1, source_target_pairs={{0,4},{2,6},{4,0},{6,2},{1,5},{3,7},{5,1},{7,3}} | collective-permute-start | bytes 393224 | tf_op jit(solution)/shard_map/ppermute | solution.py:80
  98.0 33.1 %all-to-all-start = ((bf16[8,256,128]{2,1,0:T(8,128)(2,1)}), bf16[8,256,128]{2,1,0:T(8,128)(2,1)S(1)}, u32[]{:S(2)}, u32[]{:S(2)}) async-start(bf16[8,256,128]{2,1,0:T(8,128)(2,1)} %bitcast.5), calls=%async_computation | async-start | bytes 1048576 | tf_op jit(solution)/shard_map/all_to_all | solution.py:609
  101.6 13.0 %collective-permute-start.19 = (bf16[128,768]{1,0:T(8,128)(2,1)S(1)}, bf16[128,768]{1,0:T(8,128)(2,1)S(1)}, u32[]{:S(2)}, u32[]{:S(2)}) collective-permute-start(bf16[128,768]{1,0:T(8,128)(2,1)S(1)} %get-tuple-element.31.refs_0_), channel_id=1, source_target_pairs={{0,8},{2,10},{4,12},{6,14},{8,16},{10,18},{12,20},{14,22},{16,24},... | collective-permute-start | bytes 589832 | tf_op jit(solution)/shard_map/ppermute | solution.py:71
  105.4 11.6 %collective-permute-start.20 = (bf16[128,768]{1,0:T(8,128)(2,1)S(1)}, bf16[128,768]{1,0:T(8,128)(2,1)S(1)}, u32[]{:S(2)}, u32[]{:S(2)}) collective-permute-start(bf16[128,768]{1,0:T(8,128)(2,1)S(1)} %get-tuple-element.31.refs_0_), channel_id=1, source_target_pairs={{8,0},{10,2},{12,4},{14,6},{16,8},{18,10},{20,12},{22,14},{24,16},... | collective-permute-start | bytes 589832 | tf_op jit(solution)/shard_map/ppermute | solution.py:71
  117.0 12.8 %collective-permute-start.22 = (bf16[128,768]{1,0:T(8,128)(2,1)S(1)}, bf16[128,768]{1,0:T(8,128)(2,1)}, u32[]{:S(2)}, u32[]{:S(2)}) collective-permute-start(bf16[128,768]{1,0:T(8,128)(2,1)S(1)} %collective-permute-done.20.refs_2_), channel_id=1, source_target_pairs={{8,0},{10,2},{12,4},{14,6},{16,8},{18,10},{20,12},{22,14},{9,1},{1... | collective-permute-start | bytes 589832 | tf_op jit(solution)/shard_map/ppermute | solution.py:71
  118.3 24.4 %collective-permute-start.25 = (bf16[128,768]{1,0:T(8,128)(2,1)S(1)}, bf16[128,768]{1,0:T(8,128)(2,1)}, u32[]{:S(2)}, u32[]{:S(2)}) collective-permute-start(bf16[128,768]{1,0:T(8,128)(2,1)S(1)} %get-tuple-element.31.refs_0_), channel_id=1, source_target_pairs={{0,4},{2,6},{4,0},{6,2},{8,12},{10,14},{12,8},{14,10},{16,20},{18,... | collective-permute-start | bytes 589832 | tf_op jit(solution)/shard_map/ppermute | solution.py:80
  119.7 24.3 %collective-permute-start.26 = (bf16[128,768]{1,0:T(8,128)(2,1)S(1)}, bf16[128,768]{1,0:T(8,128)(2,1)}, u32[]{:S(2)}, u32[]{:S(2)}) collective-permute-start(bf16[128,768]{1,0:T(8,128)(2,1)S(1)} %collective-permute-done.19.refs_1_), channel_id=1, source_target_pairs={{8,12},{10,14},{12,8},{14,10},{16,20},{18,22},{20,16},{22,18},{24,... | collective-permute-start | bytes 589832 | tf_op jit(solution)/shard_map/ppermute | solution.py:80
  121.1 24.9 %collective-permute-start.23 = (bf16[128,768]{1,0:T(8,128)(2,1)S(1)}, bf16[128,768]{1,0:T(8,128)(2,1)}, u32[]{:S(2)}, u32[]{:S(2)}) collective-permute-start(bf16[128,768]{1,0:T(8,128)(2,1)S(1)} %collective-permute-done.21.refs_3_), channel_id=1, source_target_pairs={{16,24},{18,26},{20,28},{22,30},{17,25},{19,27},{21,29},{23,31}} | collective-permute-start | bytes 589832 | tf_op jit(solution)/shard_map/ppermute | solution.py:71
  129.8 17.6 %collective-permute-start.24 = (bf16[128,768]{1,0:T(8,128)(2,1)}, bf16[128,768]{1,0:T(8,128)(2,1)}, u32[]{:S(2)}, u32[]{:S(2)}) collective-permute-start(bf16[128,768]{1,0:T(8,128)(2,1)} %collective-permute-done.22.refs_4_), channel_id=1, source_target_pairs={{8,0},{10,2},{12,4},{14,6},{9,1},{11,3},{13,5},{15,7}} | collective-permute-start | bytes 589832 | tf_op jit(solution)/shard_map/ppermute | solution.py:71
  132.7 44.2 %all-to-all-start.1 = ((bf16[8,256,128]{2,1,0:T(8,128)(2,1)}), bf16[8,256,128]{2,1,0:T(8,128)(2,1)S(1)}, u32[]{:S(2)}, u32[]{:S(2)}) async-start(bf16[8,256,128]{2,1,0:T(8,128)(2,1)} %scan_states.1), calls=%async_computation.1 | async-start | bytes 1048576 | tf_op jit(solution)/shard_map/all_to_all | solution.py:609
  138.8 13.0 %collective-permute-start.27 = (bf16[128,768]{1,0:T(8,128)(2,1)S(1)}, bf16[128,768]{1,0:T(8,128)(2,1)}, u32[]{:S(2)}, u32[]{:S(2)}) collective-permute-start(bf16[128,768]{1,0:T(8,128)(2,1)S(1)} %collective-permute-done.20.refs_2_), channel_id=1, source_target_pairs={{0,4},{2,6},{4,0},{6,2},{8,12},{10,14},{12,8},{14,10},{16,20},{18,... | collective-permute-start | bytes 589832 | tf_op jit(solution)/shard_map/ppermute | solution.py:80
  142.7 9.1 %collective-permute-start.28 = (bf16[128,768]{1,0:T(8,128)(2,1)S(1)}, bf16[128,768]{1,0:T(8,128)(2,1)}, u32[]{:S(2)}, u32[]{:S(2)}) collective-permute-start(bf16[128,768]{1,0:T(8,128)(2,1)S(1)} %collective-permute-done.21.refs_3_), channel_id=1, source_target_pairs={{16,20},{18,22},{20,16},{22,18},{24,28},{26,30},{28,24},{30,26},{1... | collective-permute-start | bytes 589832 | tf_op jit(solution)/shard_map/ppermute | solution.py:80
  144.1 11.9 %collective-permute-start.29 = (bf16[128,768]{1,0:T(8,128)(2,1)}, bf16[128,768]{1,0:T(8,128)(2,1)}, u32[]{:S(2)}, u32[]{:S(2)}) collective-permute-start(bf16[128,768]{1,0:T(8,128)(2,1)} %collective-permute-done.22.refs_4_), channel_id=1, source_target_pairs={{0,4},{2,6},{4,0},{6,2},{8,12},{10,14},{12,8},{14,10},{1,5},{3,7},... | collective-permute-start | bytes 589832 | tf_op jit(solution)/shard_map/ppermute | solution.py:80
  146.0 10.0 %collective-permute-start.30 = (bf16[128,768]{1,0:T(8,128)(2,1)}, bf16[128,768]{1,0:T(8,128)(2,1)}, u32[]{:S(2)}, u32[]{:S(2)}) collective-permute-start(bf16[128,768]{1,0:T(8,128)(2,1)} %collective-permute-done.23.refs_5_), channel_id=1, source_target_pairs={{24,28},{26,30},{28,24},{30,26},{25,29},{27,31},{29,25},{31,27}} | collective-permute-start | bytes 589832 | tf_op jit(solution)/shard_map/ppermute | solution.py:80
  147.3 12.1 %collective-permute-start.31 = (bf16[128,768]{1,0:T(8,128)(2,1)}, bf16[128,768]{1,0:T(8,128)(2,1)}, u32[]{:S(2)}, u32[]{:S(2)}) collective-permute-start(bf16[128,768]{1,0:T(8,128)(2,1)} %collective-permute-done.24.refs_6_), channel_id=1, source_target_pairs={{0,4},{2,6},{4,0},{6,2},{1,5},{3,7},{5,1},{7,3}} | collective-permute-start | bytes 589832 | tf_op jit(solution)/shard_map/ppermute | solution.py:80
  183.9 9.3 %collective-permute-start.32 = (bf16[512,256]{1,0:T(8,128)(2,1)S(1)}, bf16[512,256]{1,0:T(8,128)(2,1)S(1)}, u32[]{:S(2)}, u32[]{:S(2)}) collective-permute-start(bf16[512,256]{1,0:T(8,128)(2,1)S(1)} %get-tuple-element.38), channel_id=1, source_target_pairs={{0,1},{1,0},{2,3},{3,2},{4,5},{5,4},{6,7},{7,6},{8,9},{9,8},{10,11... | collective-permute-start | bytes 786440 | tf_op jit(solution)/shard_map/ppermute | solution.py:88
  185.5 7.7 %collective-permute-start.33 = (bf16[512,256]{1,0:T(8,128)(2,1)S(1)}, bf16[512,256]{1,0:T(8,128)(2,1)S(1)}, u32[]{:S(2)}, u32[]{:S(2)}) collective-permute-start(bf16[512,256]{1,0:T(8,128)(2,1)S(1)} %get-tuple-element.39), channel_id=1, source_target_pairs={{0,2},{2,0},{4,6},{6,4},{8,10},{10,8},{12,14},{14,12},{16,18},{18,... | collective-permute-start | bytes 786440 | tf_op jit(solution)/shard_map/ppermute | solution.py:83
  185.5 10.7 %collective-permute-start.34 = (bf16[512,256]{1,0:T(8,128)(2,1)S(1)}, bf16[512,256]{1,0:T(8,128)(2,1)S(1)}, u32[]{:S(2)}, u32[]{:S(2)}) collective-permute-start(bf16[512,256]{1,0:T(8,128)(2,1)S(1)} %get-tuple-element.40), channel_id=1, source_target_pairs={{0,3},{1,2},{2,1},{3,0},{4,7},{5,6},{6,5},{7,4},{8,11},{9,10},{10,... | collective-permute-start | bytes 786440 | tf_op jit(solution)/shard_map/ppermute | solution.py:96
  (38 other events, 602.0 us)

commit v3 on v2

v3 whole, which is shorter than its diff:
```python
import functools
import math

import jax
import jax.numpy as jnp
from jax import lax
from jax.experimental import pallas as pl
from jax.experimental.pallas import tpu as pltpu
from jax.sharding import PartitionSpec as P

HD = 64
N = 64
LANES = 2 * HD
PIECES = 5
EARLY = (2, 3)
LATE = (0, 1, 4)

epsilon = 1e-06

f32 = jnp.float32
bf16 = jnp.bfloat16


def params(mib=60):
    return pltpu.CompilerParams(vmem_limit_bytes=mib << 20)


def cost(flops, nbytes, transcendentals=0):
    return pl.CostEstimate(
        flops=int(flops), bytes_accessed=int(nbytes), transcendentals=int(transcendentals)
    )


def first_half(shape):
    return lax.broadcasted_iota(jnp.int32, shape, len(shape) - 1) < HD


class Plan:
    def __init__(self, frames, peers, heads_here):
        self.merge = 2 if frames % 2 == 0 and heads_here % 4 == 0 else 1
        self.frames, self.peers = frames, peers
        self.heads = heads_here // self.merge
        self.pairs = self.heads // 2
        self.chips = frames // self.merge

    def core(self):
        return lax.rem(lax.axis_index("tm"), self.merge)

    def chip(self):
        return lax.div(lax.axis_index("tm"), self.merge)

    def swap(self, block):
        return lax.ppermute(block, "tm", [(t, t ^ 1) for t in range(self.frames)])

    def to_peer(self, block, k, other):
        if not other:
            pairs = [(j, (j + k) % self.peers) for j in range(self.peers)]
            return lax.ppermute(block, "head", pairs)
        if k == 0:
            return self.swap(block)
        pairs = [
            (t * self.peers + j, (t ^ 1) * self.peers + (j + k) % self.peers)
            for t in range(self.frames)
            for j in range(self.peers)
        ]
        return lax.ppermute(block, ("tm", "head"), pairs)

    def groups(self):
        if self.merge == 1:
            return None
        return [[j * self.merge + c for j in range(self.chips)] for c in range(self.merge)]

    def decay(self, refs, slot, pair, g):
        head = self.core() * self.heads + 2 * pair
        return halves((1, LANES), refs[slot][head, g], refs[slot][head + 1, g])

    def last_decay(self, refs, pair, g):
        if self.merge == 1:
            return self.decay(refs, 0, pair, g)
        one, two = (self.decay(refs, slot, pair, g) for slot in range(2))
        return jnp.where(self.core() == 0, two, one)


def halves(shape, one, two):
    return jnp.where(first_half(shape), one, two)


def reorder_kernel(plan, *refs):
    w_refs, out_ref = refs[:-1], refs[-1]
    rows = w_refs[0].shape[0]
    width = plan.heads * PIECES * HD
    first = plan.core() == 0

    def chosen(ref, at):
        one = ref[:, at : at + HD]
        if plan.merge == 1:
            return one
        return jnp.where(first, one, ref[:, width + at : width + at + HD])

    to = 0
    for kinds in (EARLY, LATE):
        for p in range(plan.pairs):
            for i in kinds:
                blocks = []
                for ref in w_refs:
                    one, two = (chosen(ref, ((2 * p + h) * PIECES + i) * HD) for h in range(2))
                    blocks.append(jnp.concatenate([one, two], axis=1))
                for s, block in enumerate(blocks):
                    if plan.merge == 2:
                        block = jnp.where(first, block, blocks[1 - s])
                    out_ref[s * rows : (s + 1) * rows, to : to + LANES] = block
                to += LANES


def reorder(plan, weights):
    rows = weights[0].shape[0]
    return pl.pallas_call(
        functools.partial(reorder_kernel, plan),
        out_shape=jax.ShapeDtypeStruct((plan.merge * rows, plan.heads * PIECES * HD), bf16),
        compiler_params=params(),
        cost_estimate=cost(0, 4 * weights[0].size),
        name="reorder",
    )(*weights)


def normalise(part, out, at):
    step = min(128, part.shape[0])

    def norm(c, _):
        start = pl.multiple_of(c * step, step)
        wide = part[pl.ds(start, step), :].astype(f32)
        scale = lax.rsqrt(jnp.mean(wide * wide, axis=-1, keepdims=True) + epsilon)
        out[pl.ds(at + start, step), :] = (wide * scale).astype(bf16)
        return 0

    lax.fori_loop(0, part.shape[0] // step, norm, 0)


def order_kernel(plan, groups, ids_row_ref, ids_col_ref, *refs):
    own_refs = refs[: plan.merge]
    x_ref, rest_ref, back_ref, normed = refs[plan.merge :]
    local = own_refs[0].shape[0]
    tokens = back_ref.shape[0]
    block = tokens // groups
    step = 128
    for s, own in enumerate(own_refs):
        normalise(own, normed, s * local)

    label = lax.broadcasted_iota(jnp.int32, (groups, tokens), 0)
    held = label == ids_row_ref[...]
    held_bf = jnp.where(held, 1.0, 0.0).astype(bf16)
    counts = []
    for c in range(tokens // 256):
        before = lax.broadcasted_iota(jnp.int32, (tokens, 256), 0) < (
            lax.broadcasted_iota(jnp.int32, (tokens, 256), 1) + c * 256
        )
        counts.append(
            jnp.dot(held_bf, jnp.where(before, 1.0, 0.0).astype(bf16), preferred_element_type=f32)
        )
    count = jnp.concatenate(counts, axis=1)
    rank_row = jnp.sum(
        jnp.where(held, count + (label * block).astype(f32), 0.0), axis=0, keepdims=True
    ).astype(jnp.int32)

    def place(c, _):
        at = pl.multiple_of(c * step, step)
        pick = (lax.broadcasted_iota(jnp.int32, (step, tokens), 0) + at) == rank_row
        pick = jnp.where(pick, 1.0, 0.0).astype(bf16)
        rest_ref[pl.ds(at, step), :] = pick[:, local:]
        for s in range(plan.merge):
            x_ref[pl.ds(s * tokens + at, step), :] = jnp.dot(
                pick[:, :local], normed[s * local : (s + 1) * local], preferred_element_type=f32
            ).astype(bf16)
        return 0

    lax.fori_loop(0, tokens // step, place, 0)

    lane = lax.broadcasted_iota(jnp.int32, (tokens, 128), 1)
    held_col = jnp.where(lane == ids_col_ref[...], 1.0, 0.0).astype(bf16)

    def place_back(c, _):
        at = pl.multiple_of(c * step, step)
        before = lax.broadcasted_iota(jnp.int32, (step, tokens), 1) < (
            lax.broadcasted_iota(jnp.int32, (step, tokens), 0) + at
        )
        count = jnp.dot(
            jnp.where(before, 1.0, 0.0).astype(bf16), held_col, preferred_element_type=f32
        )
        lane = lax.broadcasted_iota(jnp.int32, (step, 128), 1)
        mine = lane == ids_col_ref[pl.ds(at, step), :]
        rank = jnp.sum(
            jnp.where(mine, count + (lane * block).astype(f32), 0.0), axis=1, keepdims=True
        ).astype(jnp.int32)
        pick = lax.broadcasted_iota(jnp.int32, (step, tokens), 1) == rank
        back_ref[pl.ds(at, step), :] = jnp.where(pick, 1.0, 0.0).astype(bf16)
        return 0

    lax.fori_loop(0, tokens // step, place_back, 0)


def order(plan, ids, owns, groups):
    tokens = ids.shape[0]
    local, width = owns[0].shape
    return pl.pallas_call(
        functools.partial(order_kernel, plan, groups),
        out_shape=(
            jax.ShapeDtypeStruct((plan.merge * tokens, width), bf16),
            jax.ShapeDtypeStruct((tokens, tokens - local), bf16),
            jax.ShapeDtypeStruct((tokens, tokens), bf16),
        ),
        scratch_shapes=[pltpu.VMEM((plan.merge * local, width), bf16)],
        compiler_params=params(),
        cost_estimate=cost(2 * tokens * tokens * width, 6 * tokens * width),
        name="order",
    )(ids.reshape(1, tokens), ids.reshape(tokens, 1), *owns)


def update_kernel(plan, groups, parts, *refs):
    decay_refs, refs = refs[: plan.merge], refs[plan.merge :]
    part_ref, rest_ref, w_ref, refs = refs[0], refs[1], refs[2], refs[3:]
    frame_refs, refs = refs[: plan.merge * parts], refs[plan.merge * parts :]
    x_ref, v_ref, u_ref, total_ref, normed, kept = refs
    step = x_ref.shape[0]
    block = kept.shape[0] // (groups * plan.pairs)
    here = step // block
    slot, chunk = pl.program_id(0), pl.program_id(1)

    for s in range(plan.merge):

        @pl.when((slot == s) & (chunk == 0))
        def _(s=s):
            at = 0
            for ref in frame_refs[s * parts : (s + 1) * parts]:
                normalise(ref, normed, at)
                at += ref.shape[0]

    more = jnp.dot(rest_ref[...], normed[...], preferred_element_type=f32)
    x_ref[...] = part_ref[...] + more.astype(bf16)
    both = jnp.dot(
        x_ref[...], w_ref[:, : 2 * plan.pairs * LANES], preferred_element_type=f32
    ).astype(bf16)
    for p in range(plan.pairs):
        v = both[:, 2 * p * LANES : (2 * p + 1) * LANES]
        b = both[:, (2 * p + 1) * LANES : (2 * p + 2) * LANES]
        v_ref[:, p * LANES : (p + 1) * LANES] = v
        for i in range(0, here, 2):
            rows = slice(i * block, (i + 2) * block)
            turned = b[rows].astype(f32).T
            half = lax.broadcasted_iota(jnp.int32, turned.shape, 1) < block
            wide = jnp.concatenate(
                [jnp.where(half, turned, 0.0), jnp.where(half, 0.0, turned)], axis=0
            ).astype(bf16)
            outer = jnp.dot(wide, v[rows], preferred_element_type=f32)
            for n in range(2):
                m = outer[n * 2 * N : (n + 1) * 2 * N]
                at = ((i + n) * plan.pairs + p) * N
                u_ref[0, at : at + N, :] = halves((N, LANES), m[:N], m[N:])

    many = u_ref.shape[1]
    there = pl.ds(pl.multiple_of(chunk * many, many), many)
    if plan.merge == 2:

        @pl.when(slot == 0)
        def _():
            kept[there, :] = u_ref[0]

    @pl.when(slot == plan.merge - 1)
    def _():
        peers = total_ref.shape[0]
        share = many // peers
        items = max(1, share // N)
        first = plan.core() == 0
        for d in range(peers):
            for i in range(items):
                row = d * share + i * N
                size = min(N, share)
                item = row // N
                p, g = item % plan.pairs, chunk * here + item // plan.pairs
                last = plan.last_decay(decay_refs, p, g)
                total = u_ref[0, row : row + size, :]
                product = last
                if plan.merge == 2:
                    before = kept[pl.ds(chunk * many + row, size), :]
                    total = jnp.where(first, last, 1.0) * before + jnp.where(first, 1.0, last) * total
                    product = plan.decay(decay_refs, 0, p, g) * plan.decay(decay_refs, 1, p, g)
                total_ref[d, i * size : (i + 1) * size, :] = total.astype(bf16)
                for n in range(3):
                    piece = product.astype(bf16)
                    at = share + n * items + i
                    total_ref[d, at : at + 1, :] = piece
                    product = product - piece.astype(f32)


def share_rows(share):
    return share + 16 * -(-3 * max(1, share // N) // 16)


def project_updates(plan, decays, part, rest, frames, w, groups):
    tokens, width = rest.shape[0], part.shape[1]
    chunks = 4
    step = tokens // chunks
    rows = plan.pairs * groups * N
    every = plan.merge * tokens
    share = rows // plan.chips
    whole = lambda a: pl.BlockSpec(a.shape, lambda s, c: (0,) * a.ndim)
    last = plan.merge - 1
    return pl.pallas_call(
        functools.partial(update_kernel, plan, groups, len(frames) // plan.merge),
        grid=(plan.merge, chunks),
        in_specs=[pl.BlockSpec(memory_space=pltpu.SMEM)] * plan.merge
        + [
            pl.BlockSpec((step, width), lambda s, c: (s * chunks + c, 0)),
            pl.BlockSpec((step, rest.shape[1]), lambda s, c: (c, 0)),
            whole(w),
        ]
        + [whole(f) for f in frames],
        out_specs=(
            pl.BlockSpec((step, width), lambda s, c: (s * chunks + c, 0)),
            pl.BlockSpec((step, plan.pairs * LANES), lambda s, c: (s * chunks + c, 0)),
            pl.BlockSpec((1, rows // chunks, LANES), lambda s, c: (s, c, 0)),
            pl.BlockSpec(
                (plan.chips // chunks, share_rows(share), LANES),
                lambda s, c: (jnp.where(s == last, c, 0), 0, 0),
            ),
        ),
        out_shape=(
            jax.ShapeDtypeStruct((every, width), bf16),
            jax.ShapeDtypeStruct((every, plan.pairs * LANES), bf16),
            jax.ShapeDtypeStruct((plan.merge, rows, LANES), f32),
            jax.ShapeDtypeStruct((plan.chips, share_rows(share), LANES), bf16),
        ),
        scratch_shapes=[
            pltpu.VMEM((rest.shape[1], width), bf16),
            pltpu.VMEM((rows, LANES), f32),
        ],
        compiler_params=params(),
        cost_estimate=cost(
            2 * every * width * (2 * plan.pairs * LANES + rest.shape[1]), 6 * every * width
        ),
        name="project_updates",
    )(*decays, part, rest, w, *frames)


def scan_kernel(plan, u_ref, s_ref):
    share = s_ref.shape[1]
    size = min(share, N)
    items = share // size
    for i in range(items):
        at = slice(i * size, (i + 1) * size)
        state = jnp.zeros((size, LANES), f32)
        for j in range(plan.chips):
            s_ref[j, at, :] = state.astype(bf16)
            decay = jnp.zeros((1, LANES), f32)
            for n in range(3):
                row = share + n * items + i
                decay = decay + u_ref[j, row : row + 1, :].astype(f32)
            state = decay * state + u_ref[j, at, :].astype(f32)


def scan_states(plan, update, share):
    return pl.pallas_call(
        functools.partial(scan_kernel, plan),
        out_shape=jax.ShapeDtypeStruct((plan.chips, share, LANES), bf16),
        compiler_params=params(24),
        cost_estimate=cost(2 * update.size, 4 * update.size),
        name="scan_states",
    )(update)


def attend_kernel(plan, slot, *refs):
    lists_ref, refs = refs[0], refs[1:]
    decay_refs, refs = refs[: plan.merge], refs[plan.merge :]
    x_ref, v_ref, w_ref, u_ref, a_ref, c_ref, q_ref, k_ref = refs
    tokens = x_ref.shape[0]
    groups, chosen = lists_ref.shape
    block = tokens // groups
    step = 256
    per = step // block
    late = 2 * plan.pairs * LANES

    def project(c, _):
        at = pl.multiple_of(c * step, step)
        rows = pl.ds(at, step)
        every = jnp.dot(x_ref[rows, :], w_ref[:, late:], preferred_element_type=f32).astype(bf16)
        half = first_half((step, LANES))

        def head_norm(wide):
            square = wide * wide
            one = jnp.sum(jnp.where(half, square, 0.0), axis=-1, keepdims=True)
            two = jnp.sum(jnp.where(half, 0.0, square), axis=-1, keepdims=True)
            return wide * lax.rsqrt(jnp.where(half, one, two) * (1.0 / HD) + epsilon)

        for p in range(plan.pairs):
            cols = slice(p * LANES, (p + 1) * LANES)
            q, k, reader = (
                every[:, (3 * p + i) * LANES : (3 * p + i + 1) * LANES] for i in range(3)
            )
            c_ref[rows, cols] = reader
            k_ref[rows, cols] = head_norm(k.astype(f32)).astype(bf16)
            q = head_norm(q.astype(f32))
            one = jnp.where(half, q, 0.0).astype(bf16)
            two = jnp.where(half, 0.0, q).astype(bf16)
            for i in range(per):
                part = slice(i * block, (i + 1) * block)
                q_ref[p, c * per + i] = jnp.concatenate([one[part], two[part]], axis=0)
        return 0

    lax.fori_loop(0, tokens // step, project, 0)

    scale = math.log2(math.e) / math.sqrt(HD)
    for p in range(plan.pairs):
        cols = slice(p * LANES, (p + 1) * LANES)
        for g in range(groups):
            rows = slice(g * block, (g + 1) * block)
            starts = [pl.multiple_of(lists_ref[g, j] * block, block) for j in range(chosen)]
            keys = jnp.concatenate([k_ref[pl.ds(s, block), cols] for s in starts], axis=0)
            values = jnp.concatenate([v_ref[pl.ds(s, block), cols] for s in starts], axis=0)
            score = lax.dot_general(
                q_ref[p, g], keys, (((1,), (1,)), ((), ())), preferred_element_type=f32
            )
            e = jnp.exp2(score * scale)
            weight = (e * (1.0 / jnp.sum(e, axis=-1, keepdims=True))).astype(bf16)
            both = jnp.dot(weight, values, preferred_element_type=f32)
            attended = halves((block, LANES), both[:block], both[block:])
            items = slice((g * plan.pairs + p) * N, (g * plan.pairs + p + 1) * N)
            state = u_ref[slot, items, :]
            if plan.merge == 2:
                last = plan.last_decay(decay_refs, p, g)
                state = state + jnp.where(plan.core() == slot, 0.0, last) * u_ref[1 - slot, items, :]
            a_ref[rows, cols] = attended + read_out(c_ref[rows, cols], state, block)


def read_out(readers, state, block):
    half = first_half(state.shape)
    wide = jnp.concatenate([jnp.where(half, state, 0.0), jnp.where(half, 0.0, state)], axis=0)
    return jnp.dot(readers, wide.astype(bf16), preferred_element_type=f32) * (
        1.0 / (N * math.sqrt(block))
    )


def attend(plan, slot, lists, decays, x, v, w, updates):
    every, width = x.shape
    groups, chosen = lists.shape
    tokens = every // plan.merge
    block = tokens // groups
    cols = plan.pairs * LANES
    part = pl.BlockSpec((tokens, cols), lambda i: (0, 0))
    return pl.pallas_call(
        functools.partial(attend_kernel, plan, slot),
        grid=(1,),
        in_specs=[pl.BlockSpec(memory_space=pltpu.SMEM)] * (1 + plan.merge)
        + [
            pl.BlockSpec((tokens, width), lambda i: (slot, 0)),
            pl.BlockSpec((tokens, cols), lambda i: (slot, 0)),
            pl.BlockSpec(w.shape, lambda i: (0, 0)),
            pl.BlockSpec(updates.shape, lambda i: (0, 0, 0)),
        ],
        out_specs=(part, part),
        scratch_shapes=[
            pltpu.VMEM((plan.pairs, groups, 2 * block, LANES), bf16),
            pltpu.VMEM((tokens, cols), bf16),
        ],
        out_shape=(
            jax.ShapeDtypeStruct((tokens, cols), f32),
            jax.ShapeDtypeStruct((tokens, cols), bf16),
        ),
        compiler_params=params(),
        cost_estimate=cost(
            6 * tokens * width * 3 * cols,
            4 * (tokens * width + w.size + updates.size),
            2 * plan.pairs * tokens * chosen * block,
        ),
        name="attend",
    )(lists, *decays, x, v, w, updates)


def mix_kernel(plan, groups, *refs):
    decay_refs, refs = refs[: plan.merge], refs[plan.merge :]
    a_refs, refs = refs[: plan.merge], refs[plan.merge :]
    c_refs, refs = refs[: plan.merge], refs[plan.merge :]
    s_ref, back_ref, out_refs, mixed = refs[0], refs[1], refs[2:-1], refs[-1]
    tokens = back_ref.shape[0]
    block = tokens // groups
    first = plan.core() == 0
    for p in range(plan.pairs):
        cols = slice(p * LANES, (p + 1) * LANES)
        for g in range(groups):
            rows = slice(g * block, (g + 1) * block)
            at = (g * plan.pairs + p) * N
            readers = jnp.concatenate([c[rows, cols] for c in c_refs], axis=0)
            read = read_out(readers, s_ref[at : at + N, :].astype(f32), block)
            decays = [plan.decay(decay_refs, s, p, g) for s in range(plan.merge)]
            if plan.merge == 2:
                both = decays[0] * decays[1]
                decays = [jnp.where(first, decays[0], both), jnp.where(first, both, decays[1])]
            for s in range(plan.merge):
                mixed[s, rows, cols] = (
                    a_refs[s][rows, cols] + decays[s] * read[s * block : (s + 1) * block]
                ).astype(bf16)
    local = out_refs[0].shape[0]
    for s in range(plan.merge):
        for k in range(plan.peers):
            out_refs[s * plan.peers + k][...] = jnp.dot(
                back_ref[k * local : (k + 1) * local, :], mixed[s], preferred_element_type=f32
            ).astype(bf16)


def mix(plan, decays, attended, readers, state, back, groups):
    tokens = back.shape[0]
    width = attended[0].shape[1]
    out = jax.ShapeDtypeStruct((tokens // plan.peers, width), bf16)
    vmem = pl.BlockSpec(memory_space=pltpu.VMEM)
    return pl.pallas_call(
        functools.partial(mix_kernel, plan, groups),
        in_specs=[pl.BlockSpec(memory_space=pltpu.SMEM)] * plan.merge
        + [vmem] * (2 * plan.merge + 2),
        out_shape=(out,) * (plan.merge * plan.peers),
        scratch_shapes=[pltpu.VMEM((plan.merge, tokens, width), bf16)],
        compiler_params=params(24),
        cost_estimate=cost(4 * tokens * tokens * width, 2 * tokens * tokens + 16 * tokens * width),
        name="mix",
    )(*decays, *attended, *readers, state, back)


def out_kernel(plan, w_ref, *refs):
    part_refs, out_ref = refs[:-1], refs[-1]
    depth = part_refs[0].shape[1]
    core, me = plan.core(), lax.axis_index("head")
    total = None
    for s in range(plan.merge):
        for k in range(plan.peers):
            owner = lax.rem(me - k + plan.peers, plan.peers) * plan.merge
            owner = owner + (core if s == 0 else 1 - core)
            rows = pl.ds(pl.multiple_of(owner * depth, depth), depth)
            term = jnp.dot(
                part_refs[s * plan.peers + k][...], w_ref[rows, :], preferred_element_type=f32
            )
            total = term if total is None else total + term
    out_ref[...] = total.astype(bf16)


def project_out(plan, w, parts):
    local = parts[0].shape[0]
    width = w.shape[1]
    return pl.pallas_call(
        functools.partial(out_kernel, plan),
        out_shape=jax.ShapeDtypeStruct((local, width), bf16),
        compiler_params=params(24),
        cost_estimate=cost(2 * local * w.size, 2 * (w.size + 2 * local * width)),
        name="project_out",
    )(w, *parts)


def body(frames_in, in_weight, out_weight, block_ids, block_lists, decays):
    local_tokens = frames_in.shape[1]
    heads_here = decays.shape[1]
    groups = block_lists.shape[0]
    me = lax.axis_index("head")
    plan = Plan(lax.axis_size("tm"), lax.axis_size("head"), heads_here)

    weights = [in_weight] + [plan.swap(in_weight)] * (plan.merge - 1)
    w = lax.all_gather(
        reorder(plan, weights), "tm", axis=0, tiled=True, axis_index_groups=plan.groups()
    )
    rates = [decays[0]] + [plan.swap(decays[0])] * (plan.merge - 1)

    own = frames_in[0]
    chunks = 2 if local_tokens >= 512 else 1
    arriving = [
        plan.to_peer(chunk, plan.peers - k, False)
        for k in range(1, plan.peers)
        for chunk in jnp.split(own, chunks)
    ]
    owns = [own]
    if plan.merge == 2:
        owns.append(plan.swap(own))
        arriving = arriving + [plan.swap(chunk) for chunk in arriving]

    ids = jnp.roll(block_ids, -me * local_tokens)
    part, rest, back = order(plan, ids, owns, groups)
    x, v, updates, total = project_updates(plan, rates, part, rest, arriving, w, groups)

    def exchange(blocks):
        return lax.all_to_all(
            blocks, "tm", split_axis=0, concat_axis=0, tiled=True,
            axis_index_groups=plan.groups(),
        )

    share = updates.shape[1] // plan.chips
    arrived = exchange(total)
    attended = [attend(plan, 0, block_lists, rates, x, v, w, updates)]
    arrived, attended = lax.optimization_barrier((arrived, attended))
    states = scan_states(plan, arrived, share)
    if plan.merge == 2:
        x, states = lax.optimization_barrier((x, states))
        attended.append(attend(plan, 1, block_lists, rates, x, v, w, updates))
    state = exchange(states).reshape(-1, LANES)

    bases, readers = ([a[i] for a in attended] for i in range(2))
    mixed = mix(plan, rates, bases, readers, state, back, groups)
    features = [
        mixed[0] if s == 0 and k == 0 else plan.to_peer(mixed[s * plan.peers + k], k, s == 1)
        for s in range(plan.merge)
        for k in range(plan.peers)
    ]
    return project_out(plan, out_weight, features)[None]


def solution(mesh):
    return jax.shard_map(
        body,
        mesh=mesh,
        in_specs=(P("tm", "head", None), P("tm", "head"), P(), P(), P(), P("tm", "head", None)),
        out_specs=P("tm", "head", None),
        check_vma=False,
    )
```

time: 200 us -> 152 us (0.76)
  starting transfers between devices: 63.9 us -> 15.9 us
  Pallas kernels: 38 us -> 64.3 us
  blocking collectives: 23.2 us -> 0 us
  local copies, waits for them, and re-layouts: 21.5 us -> 8.22 us
  between operations: 0.57 us -> 13.6 us
  waiting for transfers between devices: 51.2 us -> 48.7 us
    ppermute x26 -> x0, starting transfers between devices: 47.8 us -> none  [the longest x14 28.3 us: cross(): return lax.ppermute(block, 'tm', pairs)]
    ppermute x26 -> x0, waiting for transfers between devices: 31.3 us -> none  [the longest x12 21 us: move(): return lax.ppermute(block, 'tm', pairs)]
    all_gather x1 -> x0, blocking collectives: 23.2 us -> none  [body(): all_decays = lax.all_gather(decays[0], 'tm', axis=0).reshape(-1)]
    pallas_call x3 -> x4, Pallas kernels: 13.5 us -> 32.9 us  [the longest x2 30 us: attend(): pl.pallas_call(functools.partial(attend_kernel, plan, slot), grid=(1,), i...]
    all_gather x0 -> x1, waiting for transfers between devices: none -> 14.3 us  [body(): lax.all_gather(reorder(plan, weights), 'tm', axis=0, tiled=True, axis_ind...]
    ppermute x3, waiting for transfers between devices: 16.9 us -> 30.7 us  [to_peer(): return lax.ppermute(block, 'head', pairs)]
    unnamed x67 -> x39, local copies, waits for them, and re-layouts: 19.1 us -> 5.9 us
    pallas_call x1, Pallas kernels: 7.93 us -> 12.4 us  [order(): pl.pallas_call(functools.partial(order_kernel, plan, groups), out_shape=(...]
  transfers between devices with their start and end apart: 37 -> 13, of which waited for: 12 -> 6; matrix products, arithmetic and copies ran while one was open for 1% -> 2% of each run, Pallas kernels for 11% -> 28%
where the time goes in v3:
time: 152 us; the launch traced here: 151 us
  Pallas kernels  64.3 us (42%)
  waiting for transfers between devices  48.7 us (32%)
  starting transfers between devices  15.9 us (10%)
  between operations  13.6 us (9%)
  local copies, waits for them, and re-layouts  8.22 us (5%)
    ppermute x3, waiting for transfers between devices, to_peer(): return lax.ppermute(block, 'head', pairs)  30.7 us
    pallas_call x2, Pallas kernels, attend(): pl.pallas_call(functools.partial(attend_kernel, plan, slot), grid=(1,), i...  30 us
    pallas_call x1, Pallas kernels, project_updates(): pl.pallas_call(functools.partial(update_kernel, plan, groups, len(frames)...  14.6 us
    all_gather x1, waiting for transfers between devices, body(): lax.all_gather(reorder(plan, weights), 'tm', axis=0, tiled=True, axis_ind...  14.3 us
    pallas_call x1, Pallas kernels, order(): pl.pallas_call(functools.partial(order_kernel, plan, groups), out_shape=(...  12.4 us
    all_to_all x2, starting transfers between devices, exchange(): lax.all_to_all(blocks, 'tm', split_axis=0, concat_axis=0, tiled=True, axi...  9.46 us
    unnamed x39, local copies, waits for them, and re-layouts  5.9 us
    ppermute x3, starting transfers between devices, to_peer(): return lax.ppermute(block, 'head', pairs)  4.34 us
  transfers between devices with their start and end apart: 13, of which 6 were waited for; matrix products, arithmetic and copies ran while one was open for 2% of the time, Pallas kernels for 28%

profile of v3, /device:TPU:0, one launch (start us, length us, event | category | flops | bytes accessed | tf_op | source)
XLA Modules:
  0.0 150.8 jit_solution(13215520192940443910)
XLA Ops:
  6.5 0.5 collective-permute-start.2
  7.0 1.5 collective-permute-done.2.refs_1_
  8.5 0.7 copy-done.10
  9.2 1.9 %reorder.1 = bf16[128,1280]{1,0:T(8,128)(2,1)} custom-call(bf16[64,2560]{1,0:T(8,128)(2,1)} %refs_0_.3, bf16[64,2560]{1,0:T(8,128)(2,1)} %copy-done.10), custom_call_target="tpu_custom_call" | custom-call | bytes 655360 | tf_op jit(solution)/shard_map/reorder/pallas_call | solution.py:117
  11.2 0.4 collective-permute-start.1
  11.6 1.3 slice_bitcast_fusion
  12.9 2.7 %collective-permute-start.3 = (bf16[256,1024]{1,0:T(8,128)(2,1)S(1)}, bf16[256,1024]{1,0:T(8,128)(2,1)S(1)}, u32[]{:S(2)}, u32[]{:S(2)}) collective-permute-start(bf16[256,1024]{1,0:T(8,128)(2,1)S(1)} %get-tuple-element.46), channel_id=1, source_target_pairs={{0,1},{1,0},{2,3},{3,2},{4,5},{5,4},{6,7},{7,6},{8,9},{9,8},{10,11... | collective-permute-start | bytes 1572872 | tf_op jit(solution)/shard_map/ppermute | solution.py:58
  15.6 0.1 collective-permute-start.4
  15.7 12.7 %collective-permute-done.3.refs_5_ = bf16[256,1024]{1,0:T(8,128)(2,1)S(1)} collective-permute-done((bf16[256,1024]{1,0:T(8,128)(2,1)S(1)}, bf16[256,1024]{1,0:T(8,128)(2,1)S(1)}, u32[]{:S(2)}, u32[]{:S(2)}) %collective-permute-start.3) | collective-permute-done | bytes 524320 | tf_op jit(solution)/shard_map/ppermute | solution.py:58
  28.4 10.9 %collective-permute-done.4.refs_6_ = bf16[256,1024]{1,0:T(8,128)(2,1)S(1)} collective-permute-done((bf16[256,1024]{1,0:T(8,128)(2,1)S(1)}, bf16[256,1024]{1,0:T(8,128)(2,1)S(1)}, u32[]{:S(2)}, u32[]{:S(2)}) %collective-permute-start.4) | collective-permute-done | bytes 524320 | tf_op jit(solution)/shard_map/ppermute | solution.py:58
  39.3 0.5 collective-permute-start
  39.8 0.1 fusion
  39.9 1.0 copy.9.ids_col_ref
  40.9 1.0 copy-done.14
  41.9 12.4 %order.1 = (bf16[2048,1024]{1,0:T(8,128)(2,1)}, bf16[1024,512]{1,0:T(8,128)(2,1)}, bf16[1024,1024]{1,0:T(8,128)(2,1)}) custom-call(s32[1,1024]{1,0:T(1,128)} %bitcast.19, s32[1024,1]{1,0:T(8,128)} %copy.9.ids_col_ref, bf16[512,1024]{1,0:T(8,128)(2,1)} %bitcast.17, bf16[512,1024]{1,0:T(8,128)(2,1)} %copy-done.14), custom_call_target="tpu_custom_call" | custom-call | flops 2147483648 | bytes 6291456 | tf_op jit(solution)/shard_map/order/pallas_call | solution.py:204
  54.3 14.3 %all-gather.2.cloned.1.call-done.refs_4_.refs_5_ = bf16[1024,1280]{1,0:T(8,128)(2,1)} async-done(((bf16[128,1280]{1,0:T(8,128)(2,1)}), bf16[1024,1280]{1,0:T(8,128)(2,1)}) %all-gather.2.cloned.1.call-update) | async-done | bytes 2621456 | tf_op jit(solution)/shard_map/all_gather | solution.py:562
  68.6 14.6 %project_updates.1 = (bf16[2048,1024]{1,0:T(8,128)(2,1)}, bf16[2048,256]{1,0:T(8,128)(2,1)}, f32[2,2048,128]{2,1,0:T(8,128)}, bf16[8,272,128]{2,1,0:T(8,128)(2,1)}) custom-call(f32[8,16]{1,0:T(8,128)} %bitcast.11, f32[8,16]{1,0:T(8,128)} %copy-done.8, bf16[2048,1024]{1,0:T(8,128)(2,1)} %get-tuple-element.25.refs_2_, ...), custom_call_target="tpu_custom_call" | custom-call | flops 4294967296 | bytes 12582912 | tf_op jit(solution)/shard_map/project_updates/pallas_call | solution.py:307
  83.2 3.5 %all-to-all-start = ((bf16[8,272,128]{2,1,0:T(8,128)(2,1)}), bf16[8,272,128]{2,1,0:T(8,128)(2,1)S(1)}, u32[]{:S(2)}, u32[]{:S(2)}) async-start(bf16[8,272,128]{2,1,0:T(8,128)(2,1)} %get-tuple-element.27), calls=%async_computation | async-start | bytes 1114112 | tf_op jit(solution)/shard_map/all_to_all | solution.py:584
  86.7 0.7 copy.10.refs_0_
  87.4 15.0 %attend.2 = (f32[1024,256]{1,0:T(8,128)}, bf16[1024,256]{1,0:T(8,128)(2,1)}) custom-call(s32[16,4]{1,0:T(8,128)} %copy.10.refs_0_, f32[8,16]{1,0:T(8,128)} %bitcast.12, f32[8,16]{1,0:T(8,128)} %copy-done.8, bf16[2048,1024]{1,0:T(8,128)(2,1)} %get-tuple-element.35.refs_3_, bf16[2048,256]{1,0:T(8,128)(2,1)} %get-tuple-element.29.refs_4_, ...), custom_call_target="tpu_custom_call" | custom-call | flops 4831838208 | bytes 11534336 | tf_op jit(solution)/shard_map/attend/pallas_call | solution.py:448
  102.4 0.9 scan_states.1
  103.3 5.9 %all-to-all-start.1 = ((bf16[8,256,128]{2,1,0:T(8,128)(2,1)}), bf16[8,256,128]{2,1,0:T(8,128)(2,1)S(1)}, u32[]{:S(2)}, u32[]{:S(2)}) async-start(bf16[8,256,128]{2,1,0:T(8,128)(2,1)} %scan_states.1), calls=%async_computation.1 | async-start | bytes 1048576 | tf_op jit(solution)/shard_map/all_to_all | solution.py:584
  109.2 15.1 %attend.3 = (f32[1024,256]{1,0:T(8,128)}, bf16[1024,256]{1,0:T(8,128)(2,1)}) custom-call(s32[16,4]{1,0:T(8,128)} %copy.10.refs_0_, f32[8,16]{1,0:T(8,128)} %bitcast.13, f32[8,16]{1,0:T(8,128)} %copy-done.8, bf16[2048,1024]{1,0:T(8,128)(2,1)} %get-tuple-element.35.refs_3_, bf16[2048,256]{1,0:T(8,128)(2,1)} %get-tuple-element.29.refs_4_, ...), custom_call_target="tpu_custom_call" | custom-call | flops 4831838208 | bytes 11534336 | tf_op jit(solution)/shard_map/attend/pallas_call | solution.py:448
  124.3 1.2 copy-done.2
  125.6 1.2 copy-done.3
  126.8 1.0 copy-done.5
  127.8 2.3 %mix.1 = (bf16[512,256]{1,0:T(8,128)(2,1)S(1)}, bf16[512,256]{1,0:T(8,128)(2,1)S(1)}, bf16[512,256]{1,0:T(8,128)(2,1)S(1)}, bf16[512,256]{1,0:T(8,128)(2,1)S(1)}) custom-call(f32[8,16]{1,0:T(8,128)S(1)} %bitcast.15, f32[8,16]{1,0:T(8,128)S(1)} %copy-done.9, f32[1024,256]{1,0:T(8,128)S(1)} %copy-done.2, f32[1024,256]{1,0:T(8,128)S(1)} %copy-done.3, ...), custom_call_target="tpu_custom_call" | custom-call | flops 1073741824 | bytes 6291456 | tf_op jit(solution)/shard_map/mix/pallas_call | solution.py:513
  130.1 1.5 %collective-permute-start.7 = (bf16[512,256]{1,0:T(8,128)(2,1)S(1)}, bf16[512,256]{1,0:T(8,128)(2,1)S(1)}, u32[]{:S(2)}, u32[]{:S(2)}) collective-permute-start(bf16[512,256]{1,0:T(8,128)(2,1)S(1)} %get-tuple-element.42), channel_id=1, source_target_pairs={{0,1},{1,0},{2,3},{3,2},{4,5},{5,4},{6,7},{7,6},{8,9},{9,8},{10,11... | collective-permute-start | bytes 786440 | tf_op jit(solution)/shard_map/ppermute | solution.py:58
  131.7 0.7 collective-permute-start.9
  132.4 7.1 %collective-permute-done.7.refs_1_ = bf16[512,256]{1,0:T(8,128)(2,1)S(1)} collective-permute-done((bf16[512,256]{1,0:T(8,128)(2,1)S(1)}, bf16[512,256]{1,0:T(8,128)(2,1)S(1)}, u32[]{:S(2)}, u32[]{:S(2)}) %collective-permute-start.7) | collective-permute-done | bytes 262176 | tf_op jit(solution)/shard_map/ppermute | solution.py:58
  139.5 2.2 %collective-permute-done.9.refs_3_ = bf16[512,256]{1,0:T(8,128)(2,1)S(1)} collective-permute-done((bf16[512,256]{1,0:T(8,128)(2,1)S(1)}, bf16[512,256]{1,0:T(8,128)(2,1)S(1)}, u32[]{:S(2)}, u32[]{:S(2)}) %collective-permute-start.9) | collective-permute-done | bytes 262176 | tf_op jit(solution)/shard_map/ppermute | solution.py:66
  141.7 2.2 %project_out.1 = bf16[512,1024]{1,0:T(8,128)(2,1)} custom-call(bf16[1024,1024]{1,0:T(8,128)(2,1)S(1)} %copy-done, bf16[512,256]{1,0:T(8,128)(2,1)S(1)} %get-tuple-element.41.refs_0_, bf16[512,256]{1,0:T(8,128)(2,1)S(1)} %collective-permute-done.7.refs_1_, bf16[512,256]{1,0:T(8,128)(2,1)S(1)} %collective-permute-done.8.refs_2_, ...), custom_call_target="tpu_custom_call" | custom-call | flops 1073741824 | bytes 4194304 | tf_op jit(solution)/shard_map/project_out/pallas_call | solution.py:545
  (45 shorter events, 0.1 us)
Async XLA Ops:
  6.5 32.8 %copy-start.6 = (f32[1,8,16]{2,1,0:T(8,128)S(1)}, f32[1,8,16]{2,1,0:T(8,128)}, u32[]{:S(2)}) copy-start(f32[1,8,16]{2,1,0:T(8,128)} %param.11) | copy-start | bytes 1540
  6.5 33.3 %copy-start.12 = (s32[1024]{0:T(1024)S(1)}, s32[1024]{0:T(1024)}, u32[]{:S(2)}) copy-start(s32[1024]{0:T(1024)} %param.9) | copy-start | bytes 12292
  6.5 62.0 %all-gather.2.cloned.1.call-start = ((), (), s32[]{:S(2)}) async-start(), calls=%async_computation.2 | async-start | bytes 2949120 | tf_op jit(solution)/shard_map/all_gather | solution.py:562
  6.5 1.9 %collective-permute-start.2 = (bf16[64,2560]{1,0:T(8,128)(2,1)}, bf16[64,2560]{1,0:T(8,128)(2,1)S(1)}, u32[]{:S(2)}, u32[]{:S(2)}) collective-permute-start(bf16[64,2560]{1,0:T(8,128)(2,1)} %refs_0_.3), channel_id=1, source_target_pairs={{0,2},{2,0},{4,6},{6,4},{8,10},{10,8},{12,14},{14,12},{16,18},{18,... | collective-permute-start | bytes 983048 | tf_op jit(solution)/shard_map/ppermute | solution.py:53
  8.5 0.7 copy-start.10
  11.2 29.8 %collective-permute-start.1 = (bf16[512,1024]{1,0:T(8,128)(2,1)}, bf16[512,1024]{1,0:T(8,128)(2,1)S(1)}, u32[]{:S(2)}, u32[]{:S(2)}) collective-permute-start(bf16[512,1024]{1,0:T(8,128)(2,1)} %bitcast.16), channel_id=1, source_target_pairs={{0,2},{2,0},{4,6},{6,4},{8,10},{10,8},{12,14},{14,12},{16,18},{18,... | collective-permute-start | bytes 3145736 | tf_op jit(solution)/shard_map/ppermute | solution.py:53
  12.9 15.5 %collective-permute-start.3 = (bf16[256,1024]{1,0:T(8,128)(2,1)S(1)}, bf16[256,1024]{1,0:T(8,128)(2,1)S(1)}, u32[]{:S(2)}, u32[]{:S(2)}) collective-permute-start(bf16[256,1024]{1,0:T(8,128)(2,1)S(1)} %get-tuple-element.46), channel_id=1, source_target_pairs={{0,1},{1,0},{2,3},{3,2},{4,5},{5,4},{6,7},{7,6},{8,9},{9,8},{10,11... | collective-permute-start | bytes 1572872 | tf_op jit(solution)/shard_map/ppermute | solution.py:58
  15.6 23.7 %collective-permute-start.4 = (bf16[256,1024]{1,0:T(8,128)(2,1)S(1)}, bf16[256,1024]{1,0:T(8,128)(2,1)S(1)}, u32[]{:S(2)}, u32[]{:S(2)}) collective-permute-start(bf16[256,1024]{1,0:T(8,128)(2,1)S(1)} %get-tuple-element.45), channel_id=1, source_target_pairs={{0,1},{1,0},{2,3},{3,2},{4,5},{5,4},{6,7},{7,6},{8,9},{9,8},{10,11... | collective-permute-start | bytes 1572872 | tf_op jit(solution)/shard_map/ppermute | solution.py:58
  28.4 25.9 %copy-start.15 = (bf16[256,1024]{1,0:T(8,128)(2,1)}, bf16[256,1024]{1,0:T(8,128)(2,1)S(1)}, u32[]{:S(2)}) copy-start(bf16[256,1024]{1,0:T(8,128)(2,1)S(1)} %collective-permute-done.3.refs_5_) | copy-start | bytes 1572868
  28.4 25.9 %collective-permute-start.5 = (bf16[256,1024]{1,0:T(8,128)(2,1)S(1)}, bf16[256,1024]{1,0:T(8,128)(2,1)S(1)}, u32[]{:S(2)}, u32[]{:S(2)}) collective-permute-start(bf16[256,1024]{1,0:T(8,128)(2,1)S(1)} %collective-permute-done.3.refs_5_), channel_id=1, source_target_pairs={{0,2},{2,0},{4,6},{6,4},{8,10},{10,8},{12,14},{14,12},{16,18},{18,... | collective-permute-start | bytes 1572872 | tf_op jit(solution)/shard_map/ppermute | solution.py:53
  39.3 29.3 %copy-start.16 = (bf16[256,1024]{1,0:T(8,128)(2,1)}, bf16[256,1024]{1,0:T(8,128)(2,1)S(1)}, u32[]{:S(2)}) copy-start(bf16[256,1024]{1,0:T(8,128)(2,1)S(1)} %collective-permute-done.4.refs_6_) | copy-start | bytes 1572868
  39.3 15.0 %collective-permute-start.6 = (bf16[256,1024]{1,0:T(8,128)(2,1)S(1)}, bf16[256,1024]{1,0:T(8,128)(2,1)S(1)}, u32[]{:S(2)}, u32[]{:S(2)}) collective-permute-start(bf16[256,1024]{1,0:T(8,128)(2,1)S(1)} %collective-permute-done.4.refs_6_), channel_id=1, source_target_pairs={{0,2},{2,0},{4,6},{6,4},{8,10},{10,8},{12,14},{14,12},{16,18},{18,... | collective-permute-start | bytes 1572872 | tf_op jit(solution)/shard_map/ppermute | solution.py:53
  39.3 15.0 %collective-permute-start = (f32[8,16]{1,0:T(8,128)S(1)}, f32[8,16]{1,0:T(8,128)S(1)}, u32[]{:S(2)}, u32[]{:S(2)}) collective-permute-start(f32[8,16]{1,0:T(8,128)S(1)} %bitcast.14), channel_id=1, source_target_pairs={{0,2},{2,0},{4,6},{6,4},{8,10},{10,8},{12,14},{14,12},{16,18},{18,... | collective-permute-start | bytes 1544 | tf_op jit(solution)/shard_map/ppermute | solution.py:53
  39.9 1.1 copy-start.11
  40.9 1.0 copy-start.14
  54.3 14.3 %copy-start.8 = (f32[8,16]{1,0:T(8,128)}, f32[8,16]{1,0:T(8,128)S(1)}, u32[]{:S(2)}) copy-start(f32[8,16]{1,0:T(8,128)S(1)} %collective-permute-done.refs_1_.refs_2_) | copy-start | bytes 1540
  54.3 14.3 %copy-start.17 = (bf16[256,1024]{1,0:T(8,128)(2,1)}, bf16[256,1024]{1,0:T(8,128)(2,1)S(1)}, u32[]{:S(2)}) copy-start(bf16[256,1024]{1,0:T(8,128)(2,1)S(1)} %collective-permute-done.5.refs_7_) | copy-start | bytes 1572868
  54.3 14.3 %copy-start.18 = (bf16[256,1024]{1,0:T(8,128)(2,1)}, bf16[256,1024]{1,0:T(8,128)(2,1)S(1)}, u32[]{:S(2)}) copy-start(bf16[256,1024]{1,0:T(8,128)(2,1)S(1)} %collective-permute-done.6.refs_8_) | copy-start | bytes 1572868
  68.6 18.1 %copy-start.13 = (s32[16,4]{0,1:T(4,128)S(1)}, s32[16,4]{0,1:T(4,128)}, u32[]{:S(2)}) copy-start(s32[16,4]{0,1:T(4,128)} %param.10) | copy-start | bytes 772
  83.2 19.2 %all-to-all-start = ((bf16[8,272,128]{2,1,0:T(8,128)(2,1)}), bf16[8,272,128]{2,1,0:T(8,128)(2,1)S(1)}, u32[]{:S(2)}, u32[]{:S(2)}) async-start(bf16[8,272,128]{2,1,0:T(8,128)(2,1)} %get-tuple-element.27), calls=%async_computation | async-start | bytes 1114112 | tf_op jit(solution)/shard_map/all_to_all | solution.py:584
  103.3 21.0 %all-to-all-start.1 = ((bf16[8,256,128]{2,1,0:T(8,128)(2,1)}), bf16[8,256,128]{2,1,0:T(8,128)(2,1)S(1)}, u32[]{:S(2)}, u32[]{:S(2)}) async-start(bf16[8,256,128]{2,1,0:T(8,128)(2,1)} %scan_states.1), calls=%async_computation.1 | async-start | bytes 1048576 | tf_op jit(solution)/shard_map/all_to_all | solution.py:584
  109.2 15.1 %copy-start.1 = (bf16[1024,1024]{1,0:T(8,128)(2,1)S(1)}, bf16[1024,1024]{1,0:T(8,128)(2,1)}, u32[]{:S(2)}) copy-start(bf16[1024,1024]{1,0:T(8,128)(2,1)} %get-tuple-element.40.refs_7_) | copy-start | bytes 6291460
  109.2 15.1 %copy-start.4 = (bf16[1024,256]{1,0:T(8,128)(2,1)S(1)}, bf16[1024,256]{1,0:T(8,128)(2,1)}, u32[]{:S(2)}) copy-start(bf16[1024,256]{1,0:T(8,128)(2,1)} %get-tuple-element.37.refs_4_) | copy-start | bytes 1572868
  109.2 15.1 %copy-start.7 = (f32[1,8,16]{2,1,0:T(8,128)S(1)}, f32[1,8,16]{2,1,0:T(8,128)}, u32[]{:S(2)}) copy-start(f32[1,8,16]{2,1,0:T(8,128)} %param.11) | copy-start | bytes 1540
  109.2 15.1 %copy-start.9 = (f32[8,16]{1,0:T(8,128)S(1)}, f32[8,16]{1,0:T(8,128)}, u32[]{:S(2)}) copy-start(f32[8,16]{1,0:T(8,128)} %copy-done.8) | copy-start | bytes 1540
  124.3 1.2 copy-start.2
  125.6 1.2 copy-start.3
  126.8 1.0 copy-start.5
  127.8 13.9 %copy-start = (bf16[1024,1024]{1,0:T(8,128)(2,1)S(1)}, bf16[1024,1024]{1,0:T(8,128)(2,1)}, u32[]{:S(2)}) copy-start(bf16[1024,1024]{1,0:T(8,128)(2,1)} %w_ref.1) | copy-start | bytes 6291460
  130.1 9.3 %collective-permute-start.7 = (bf16[512,256]{1,0:T(8,128)(2,1)S(1)}, bf16[512,256]{1,0:T(8,128)(2,1)S(1)}, u32[]{:S(2)}, u32[]{:S(2)}) collective-permute-start(bf16[512,256]{1,0:T(8,128)(2,1)S(1)} %get-tuple-element.42), channel_id=1, source_target_pairs={{0,1},{1,0},{2,3},{3,2},{4,5},{5,4},{6,7},{7,6},{8,9},{9,8},{10,11... | collective-permute-start | bytes 786440 | tf_op jit(solution)/shard_map/ppermute | solution.py:58
  131.7 7.8 %collective-permute-start.8 = (bf16[512,256]{1,0:T(8,128)(2,1)S(1)}, bf16[512,256]{1,0:T(8,128)(2,1)S(1)}, u32[]{:S(2)}, u32[]{:S(2)}) collective-permute-start(bf16[512,256]{1,0:T(8,128)(2,1)S(1)} %get-tuple-element.43), channel_id=1, source_target_pairs={{0,2},{2,0},{4,6},{6,4},{8,10},{10,8},{12,14},{14,12},{16,18},{18,... | collective-permute-start | bytes 786440 | tf_op jit(solution)/shard_map/ppermute | solution.py:53
  131.7 10.0 %collective-permute-start.9 = (bf16[512,256]{1,0:T(8,128)(2,1)S(1)}, bf16[512,256]{1,0:T(8,128)(2,1)S(1)}, u32[]{:S(2)}, u32[]{:S(2)}) collective-permute-start(bf16[512,256]{1,0:T(8,128)(2,1)S(1)} %get-tuple-element.44), channel_id=1, source_target_pairs={{0,3},{1,2},{2,1},{3,0},{4,7},{5,6},{6,5},{7,4},{8,11},{9,10},{10,... | collective-permute-start | bytes 786440 | tf_op jit(solution)/shard_map/ppermute | solution.py:66
Sparse Core Ops, SparseCore 0:
  11.3 57.2 all-gather.1

commit v4 on v3

v4 whole, which is shorter than its diff:
```python
import functools
import math

import jax
import jax.numpy as jnp
from jax import lax
from jax.experimental import pallas as pl
from jax.experimental.pallas import tpu as pltpu
from jax.sharding import PartitionSpec as P

HD = 64
N = 64
LANES = 2 * HD
PIECES = 5
EARLY = (2, 3)
LATE = (0, 1, 4)

epsilon = 1e-06

f32 = jnp.float32
bf16 = jnp.bfloat16


def params(mib=60):
    return pltpu.CompilerParams(vmem_limit_bytes=mib << 20)


def cost(flops, nbytes, transcendentals=0):
    return pl.CostEstimate(
        flops=int(flops), bytes_accessed=int(nbytes), transcendentals=int(transcendentals)
    )


def first_half(shape):
    return lax.broadcasted_iota(jnp.int32, shape, len(shape) - 1) < HD


class Plan:
    def __init__(self, frames, peers, heads_here):
        self.merge = 2 if frames % 2 == 0 and heads_here % 4 == 0 else 1
        self.frames, self.peers = frames, peers
        self.heads = heads_here // self.merge
        self.pairs = self.heads // 2
        self.chips = frames // self.merge
        self.across = 2 if self.chips % 2 == 0 else 1
        self.along = self.chips // self.across
        self.ringed = self.across == 2 and self.along <= 8

    def core(self):
        return lax.rem(lax.axis_index("tm"), self.merge)

    def chip(self):
        return lax.div(lax.axis_index("tm"), self.merge)

    def swap(self, block):
        return lax.ppermute(block, "tm", [(t, t ^ 1) for t in range(self.frames)])

    def round(self, block):
        a, b, c = self.along, self.across, self.merge
        pairs = [(t, (t + b * c) % (a * b * c)) for t in range(self.frames)]
        return lax.ppermute(block, "tm", pairs)

    def cross(self, block):
        c = self.merge
        pairs = [(t, (t // c ^ 1) * c + t % c) for t in range(self.frames)]
        return lax.ppermute(block, "tm", pairs)

    def assemble(self, refs, out, cols):
        rows = refs[0].shape[0]
        if len(refs) == 1:
            out[...] = refs[0][:, cols]
            return
        a, b = lax.div(self.chip(), self.across), lax.rem(self.chip(), self.across)
        for i, ref in enumerate(refs):
            k, flip = i // 2, i % 2
            there = lax.rem(a - k + self.along, self.along) * self.across
            at = (there + (1 - b if flip else b)) * rows
            out[pl.ds(pl.multiple_of(at, rows), rows), :] = ref[:, cols]

    def to_peer(self, block, k, other):
        if not other:
            pairs = [(j, (j + k) % self.peers) for j in range(self.peers)]
            return lax.ppermute(block, "head", pairs)
        if k == 0:
            return self.swap(block)
        pairs = [
            (t * self.peers + j, (t ^ 1) * self.peers + (j + k) % self.peers)
            for t in range(self.frames)
            for j in range(self.peers)
        ]
        return lax.ppermute(block, ("tm", "head"), pairs)

    def groups(self):
        if self.merge == 1:
            return None
        return [[j * self.merge + c for j in range(self.chips)] for c in range(self.merge)]

    def decay(self, refs, slot, pair, g):
        head = self.core() * self.heads + 2 * pair
        return halves((1, LANES), refs[slot][head, g], refs[slot][head + 1, g])

    def last_decay(self, refs, pair, g):
        if self.merge == 1:
            return self.decay(refs, 0, pair, g)
        one, two = (self.decay(refs, slot, pair, g) for slot in range(2))
        return jnp.where(self.core() == 0, two, one)


def halves(shape, one, two):
    return jnp.where(first_half(shape), one, two)


def reorder_kernel(plan, *refs):
    w_refs, out_ref = refs[:-1], refs[-1]
    rows = w_refs[0].shape[0]
    width = plan.heads * PIECES * HD
    first = plan.core() == 0

    def chosen(ref, at):
        one = ref[:, at : at + HD]
        if plan.merge == 1:
            return one
        return jnp.where(first, one, ref[:, width + at : width + at + HD])

    to = 0
    for kinds in (EARLY, LATE):
        for p in range(plan.pairs):
            for i in kinds:
                blocks = []
                for ref in w_refs:
                    one, two = (chosen(ref, ((2 * p + h) * PIECES + i) * HD) for h in range(2))
                    blocks.append(jnp.concatenate([one, two], axis=1))
                for s, block in enumerate(blocks):
                    if plan.merge == 2:
                        block = jnp.where(first, block, blocks[1 - s])
                    out_ref[s * rows : (s + 1) * rows, to : to + LANES] = block
                to += LANES


def reorder(plan, weights):
    rows = weights[0].shape[0]
    return pl.pallas_call(
        functools.partial(reorder_kernel, plan),
        out_shape=jax.ShapeDtypeStruct((plan.merge * rows, plan.heads * PIECES * HD), bf16),
        compiler_params=params(),
        cost_estimate=cost(0, 4 * weights[0].size),
        name="reorder",
    )(*weights)


def normalise(part, out, at):
    step = min(128, part.shape[0])

    def norm(c, _):
        start = pl.multiple_of(c * step, step)
        wide = part[pl.ds(start, step), :].astype(f32)
        scale = lax.rsqrt(jnp.mean(wide * wide, axis=-1, keepdims=True) + epsilon)
        out[pl.ds(at + start, step), :] = (wide * scale).astype(bf16)
        return 0

    lax.fori_loop(0, part.shape[0] // step, norm, 0)


def pick_kernel(groups, ids_ref, own_ref, rest_ref):
    tokens = ids_ref.shape[1]
    local = own_ref.shape[1]
    block = tokens // groups
    step = 128
    label = lax.broadcasted_iota(jnp.int32, (groups, tokens), 0)
    held = label == ids_ref[...]
    held_bf = jnp.where(held, 1.0, 0.0).astype(bf16)
    counts = []
    for c in range(tokens // 256):
        before = lax.broadcasted_iota(jnp.int32, (tokens, 256), 0) < (
            lax.broadcasted_iota(jnp.int32, (tokens, 256), 1) + c * 256
        )
        counts.append(
            jnp.dot(held_bf, jnp.where(before, 1.0, 0.0).astype(bf16), preferred_element_type=f32)
        )
    count = jnp.concatenate(counts, axis=1)
    rank = jnp.sum(
        jnp.where(held, count + (label * block).astype(f32), 0.0), axis=0, keepdims=True
    ).astype(jnp.int32)

    def place(c, _):
        at = pl.multiple_of(c * step, step)
        pick = (lax.broadcasted_iota(jnp.int32, (step, tokens), 0) + at) == rank
        pick = jnp.where(pick, 1.0, 0.0).astype(bf16)
        own_ref[pl.ds(at, step), :] = pick[:, :local]
        rest_ref[pl.ds(at, step), :] = pick[:, local:]
        return 0

    lax.fori_loop(0, tokens // step, place, 0)


def pick_tokens(ids, local, groups):
    tokens = ids.shape[0]
    return pl.pallas_call(
        functools.partial(pick_kernel, groups),
        out_shape=(
            jax.ShapeDtypeStruct((tokens, local), bf16),
            jax.ShapeDtypeStruct((tokens, tokens - local), bf16),
        ),
        compiler_params=params(),
        cost_estimate=cost(32 * tokens * tokens, 2 * tokens * tokens),
        name="pick_tokens",
    )(ids.reshape(1, tokens))


def back_kernel(groups, ids_ref, back_ref):
    tokens = back_ref.shape[0]
    block = tokens // groups
    step = 128
    lane = lax.broadcasted_iota(jnp.int32, (tokens, 128), 1)
    held = jnp.where(lane == ids_ref[...], 1.0, 0.0).astype(bf16)

    def place(c, _):
        at = pl.multiple_of(c * step, step)
        before = lax.broadcasted_iota(jnp.int32, (step, tokens), 1) < (
            lax.broadcasted_iota(jnp.int32, (step, tokens), 0) + at
        )
        count = jnp.dot(
            jnp.where(before, 1.0, 0.0).astype(bf16), held, preferred_element_type=f32
        )
        lane = lax.broadcasted_iota(jnp.int32, (step, 128), 1)
        mine = lane == ids_ref[pl.ds(at, step), :]
        rank = jnp.sum(
            jnp.where(mine, count + (lane * block).astype(f32), 0.0), axis=1, keepdims=True
        ).astype(jnp.int32)
        pick = lax.broadcasted_iota(jnp.int32, (step, tokens), 1) == rank
        back_ref[pl.ds(at, step), :] = jnp.where(pick, 1.0, 0.0).astype(bf16)
        return 0

    lax.fori_loop(0, tokens // step, place, 0)


def back_tokens(ids, groups):
    tokens = ids.shape[0]
    return pl.pallas_call(
        functools.partial(back_kernel, groups),
        out_shape=jax.ShapeDtypeStruct((tokens, tokens), bf16),
        compiler_params=params(),
        cost_estimate=cost(256 * tokens * tokens, 2 * tokens * tokens),
        name="back_tokens",
    )(ids.reshape(tokens, 1))


def place_kernel(merge, parts, *refs):
    pick_ref, refs = refs[0], refs[1:]
    frame_refs, refs = refs[: merge * parts], refs[merge * parts :]
    base_refs, (x_ref, normed) = refs[:-2], refs[-2:]
    slot, chunk = pl.program_id(0), pl.program_id(1)
    for s in range(merge):

        @pl.when((slot == s) & (chunk == 0))
        def _(s=s):
            at = 0
            for ref in frame_refs[s * parts : (s + 1) * parts]:
                normalise(ref, normed, at)
                at += ref.shape[0]

    placed = jnp.dot(pick_ref[...], normed[...], preferred_element_type=f32).astype(bf16)
    for base in base_refs:
        placed = base[...] + placed
    x_ref[...] = placed


def place_tokens(plan, pick, frames, base):
    tokens, count = pick.shape
    width = frames[0].shape[1]
    chunks = 4
    step = tokens // chunks
    rows = pl.BlockSpec((step, width), lambda s, c: (s * chunks + c, 0))
    return pl.pallas_call(
        functools.partial(place_kernel, plan.merge, len(frames) // plan.merge),
        grid=(plan.merge, chunks),
        in_specs=[pl.BlockSpec((step, count), lambda s, c: (c, 0))]
        + [pl.BlockSpec(f.shape, lambda s, c: (0, 0)) for f in frames]
        + [rows] * len(base),
        out_specs=rows,
        out_shape=jax.ShapeDtypeStruct((plan.merge * tokens, width), bf16),
        scratch_shapes=[pltpu.VMEM((count, width), bf16)],
        compiler_params=params(),
        cost_estimate=cost(4 * plan.merge * tokens * count * width, 6 * tokens * width),
        name="place_tokens",
    )(pick, *frames, *base)


def update_kernel(plan, groups, *refs):
    decay_refs, refs = refs[: plan.merge], refs[plan.merge :]
    x_ref, w_refs = refs[0], refs[1:-5]
    v_ref, u_ref, total_ref, w_scr, kept = refs[-5:]
    step = x_ref.shape[0]
    block = kept.shape[0] // (groups * plan.pairs)
    here = step // block
    slot, chunk = pl.program_id(0), pl.program_id(1)

    @pl.when((slot == 0) & (chunk == 0))
    def _():
        plan.assemble(w_refs, w_scr, slice(0, w_scr.shape[1]))

    both = jnp.dot(x_ref[...], w_scr[...], preferred_element_type=f32).astype(bf16)
    for p in range(plan.pairs):
        v = both[:, 2 * p * LANES : (2 * p + 1) * LANES]
        b = both[:, (2 * p + 1) * LANES : (2 * p + 2) * LANES]
        v_ref[:, p * LANES : (p + 1) * LANES] = v
        for i in range(0, here, 2):
            rows = slice(i * block, (i + 2) * block)
            turned = b[rows].astype(f32).T
            half = lax.broadcasted_iota(jnp.int32, turned.shape, 1) < block
            wide = jnp.concatenate(
                [jnp.where(half, turned, 0.0), jnp.where(half, 0.0, turned)], axis=0
            ).astype(bf16)
            outer = jnp.dot(wide, v[rows], preferred_element_type=f32)
            for n in range(2):
                m = outer[n * 2 * N : (n + 1) * 2 * N]
                at = ((i + n) * plan.pairs + p) * N
                u_ref[0, at : at + N, :] = halves((N, LANES), m[:N], m[N:])

    many = u_ref.shape[1]
    there = pl.ds(pl.multiple_of(chunk * many, many), many)
    if plan.merge == 2:

        @pl.when(slot == 0)
        def _():
            kept[there, :] = u_ref[0]

    @pl.when(slot == plan.merge - 1)
    def _():
        peers = total_ref.shape[0]
        share = many // peers
        items = max(1, share // N)
        first = plan.core() == 0
        for d in range(peers):
            for i in range(items):
                row = d * share + i * N
                size = min(N, share)
                item = row // N
                p, g = item % plan.pairs, chunk * here + item // plan.pairs
                last = plan.last_decay(decay_refs, p, g)
                total = u_ref[0, row : row + size, :]
                product = last
                if plan.merge == 2:
                    before = kept[pl.ds(chunk * many + row, size), :]
                    total = jnp.where(first, last, 1.0) * before + jnp.where(first, 1.0, last) * total
                    product = plan.decay(decay_refs, 0, p, g) * plan.decay(decay_refs, 1, p, g)
                total_ref[d, i * size : (i + 1) * size, :] = total.astype(bf16)
                for n in range(3):
                    piece = product.astype(bf16)
                    at = share + n * items + i
                    total_ref[d, at : at + 1, :] = piece
                    product = product - piece.astype(f32)


def share_rows(share):
    return share + 16 * -(-3 * max(1, share // N) // 16)


def project_updates(plan, decays, x, weights, groups):
    every, width = x.shape
    tokens = every // plan.merge
    chunks = 4
    step = tokens // chunks
    cols = plan.pairs * LANES
    rows = plan.pairs * groups * N
    share = rows // plan.chips
    last = plan.merge - 1
    return pl.pallas_call(
        functools.partial(update_kernel, plan, groups),
        grid=(plan.merge, chunks),
        in_specs=[pl.BlockSpec(memory_space=pltpu.SMEM)] * plan.merge
        + [pl.BlockSpec((step, width), lambda s, c: (s * chunks + c, 0))]
        + [pl.BlockSpec((w.shape[0], 2 * cols), lambda s, c: (0, 0)) for w in weights],
        out_specs=(
            pl.BlockSpec((step, cols), lambda s, c: (s * chunks + c, 0)),
            pl.BlockSpec((1, rows // chunks, LANES), lambda s, c: (s, c, 0)),
            pl.BlockSpec(
                (plan.chips // chunks, share_rows(share), LANES),
                lambda s, c: (jnp.where(s == last, c, 0), 0, 0),
            ),
        ),
        out_shape=(
            jax.ShapeDtypeStruct((every, cols), bf16),
            jax.ShapeDtypeStruct((plan.merge, rows, LANES), f32),
            jax.ShapeDtypeStruct((plan.chips, share_rows(share), LANES), bf16),
        ),
        scratch_shapes=[pltpu.VMEM((width, 2 * cols), bf16), pltpu.VMEM((rows, LANES), f32)],
        compiler_params=params(),
        cost_estimate=cost(4 * every * width * 2 * cols, 4 * every * width),
        name="project_updates",
    )(*decays, x, *weights)


def scan_kernel(plan, u_ref, s_ref):
    share = s_ref.shape[1]
    size = min(share, N)
    items = share // size
    for i in range(items):
        at = slice(i * size, (i + 1) * size)
        state = jnp.zeros((size, LANES), f32)
        for j in range(plan.chips):
            s_ref[j, at, :] = state.astype(bf16)
            decay = jnp.zeros((1, LANES), f32)
            for n in range(3):
                row = share + n * items + i
                decay = decay + u_ref[j, row : row + 1, :].astype(f32)
            state = decay * state + u_ref[j, at, :].astype(f32)


def scan_states(plan, update, share):
    return pl.pallas_call(
        functools.partial(scan_kernel, plan),
        out_shape=jax.ShapeDtypeStruct((plan.chips, share, LANES), bf16),
        compiler_params=params(24),
        cost_estimate=cost(2 * update.size, 4 * update.size),
        name="scan_states",
    )(update)


def attend_kernel(plan, slot, chunks, *refs):
    lists_ref, refs = refs[0], refs[1:]
    decay_refs, refs = refs[: plan.merge], refs[plan.merge :]
    x_ref, v_ref, u_ref, w_refs = refs[0], refs[1], refs[2], refs[3:-6]
    a_ref, c_out_ref, w_scr, q_ref, k_ref, c_ref = refs[-6:]
    tokens = v_ref.shape[0]
    groups, chosen = lists_ref.shape
    block = tokens // groups
    step = x_ref.shape[0]
    per = step // block
    early = 2 * plan.pairs * LANES
    i = pl.program_id(0)

    @pl.when(i == 0)
    def _():
        plan.assemble(w_refs, w_scr, slice(early, early + w_scr.shape[1]))

    @pl.when(i < chunks)
    def _():
        rows = pl.ds(pl.multiple_of(i * step, step), step)
        every = jnp.dot(x_ref[...], w_scr[...], preferred_element_type=f32).astype(bf16)
        half = first_half((step, LANES))

        def head_norm(wide):
            square = wide * wide
            one = jnp.sum(jnp.where(half, square, 0.0), axis=-1, keepdims=True)
            two = jnp.sum(jnp.where(half, 0.0, square), axis=-1, keepdims=True)
            return wide * lax.rsqrt(jnp.where(half, one, two) * (1.0 / HD) + epsilon)

        for p in range(plan.pairs):
            cols = slice(p * LANES, (p + 1) * LANES)
            q, k, reader = (
                every[:, (3 * p + j) * LANES : (3 * p + j + 1) * LANES] for j in range(3)
            )
            c_ref[rows, cols] = reader
            c_out_ref[:, cols] = reader
            k_ref[rows, cols] = head_norm(k.astype(f32)).astype(bf16)
            q = head_norm(q.astype(f32))
            one = jnp.where(half, q, 0.0).astype(bf16)
            two = jnp.where(half, 0.0, q).astype(bf16)
            for j in range(per):
                part = slice(j * block, (j + 1) * block)
                q_ref[p, i * per + j] = jnp.concatenate([one[part], two[part]], axis=0)

    scale = math.log2(math.e) / math.sqrt(HD)

    @pl.when(i >= chunks)
    def _():
        for n in range(per):
            g = (i - chunks) * per + n
            starts = [pl.multiple_of(lists_ref[g, j] * block, block) for j in range(chosen)]
            for p in range(plan.pairs):
                cols = slice(p * LANES, (p + 1) * LANES)
                keys = jnp.concatenate([k_ref[pl.ds(s, block), cols] for s in starts], axis=0)
                values = jnp.concatenate([v_ref[pl.ds(s, block), cols] for s in starts], axis=0)
                score = lax.dot_general(
                    q_ref[p, g], keys, (((1,), (1,)), ((), ())), preferred_element_type=f32
                )
                e = jnp.exp2(score * scale)
                weight = (e * (1.0 / jnp.sum(e, axis=-1, keepdims=True))).astype(bf16)
                both = jnp.dot(weight, values, preferred_element_type=f32)
                attended = halves((block, LANES), both[:block], both[block:])
                items = slice((n * plan.pairs + p) * N, (n * plan.pairs + p + 1) * N)
                state = u_ref[slot, items, :]
                if plan.merge == 2:
                    last = plan.last_decay(decay_refs, p, g)
                    last = jnp.where(plan.core() == slot, 0.0, last)
                    state = state + last * u_ref[1 - slot, items, :]
                readers = c_ref[pl.ds(pl.multiple_of(g * block, block), block), cols]
                a_ref[n * block : (n + 1) * block, cols] = attended + read_out(
                    readers, state, block
                )


def attend(plan, slot, lists, decays, x, v, weights, updates):
    every, width = x.shape
    groups, chosen = lists.shape
    tokens = every // plan.merge
    block = tokens // groups
    cols = plan.pairs * LANES
    chunks = 4
    step = tokens // chunks
    first = lambda i: jnp.minimum(i, chunks - 1)
    then = lambda i: jnp.maximum(i - chunks, 0)
    return pl.pallas_call(
        functools.partial(attend_kernel, plan, slot, chunks),
        grid=(2 * chunks,),
        in_specs=[pl.BlockSpec(memory_space=pltpu.SMEM)] * (1 + plan.merge)
        + [
            pl.BlockSpec((step, width), lambda i: (slot * chunks + first(i), 0)),
            pl.BlockSpec((tokens, cols), lambda i: (slot, 0)),
            pl.BlockSpec(
                (plan.merge, updates.shape[1] // chunks, LANES), lambda i: (0, then(i), 0)
            ),
        ]
        + [pl.BlockSpec(w.shape, lambda i: (0, 0)) for w in weights],
        out_specs=(
            pl.BlockSpec((step, cols), lambda i: (then(i), 0)),
            pl.BlockSpec((step, cols), lambda i: (first(i), 0)),
        ),
        scratch_shapes=[
            pltpu.VMEM((width, 3 * cols), bf16),
            pltpu.VMEM((plan.pairs, groups, 2 * block, LANES), bf16),
            pltpu.VMEM((tokens, cols), bf16),
            pltpu.VMEM((tokens, cols), bf16),
        ],
        out_shape=(
            jax.ShapeDtypeStruct((tokens, cols), f32),
            jax.ShapeDtypeStruct((tokens, cols), bf16),
        ),
        compiler_params=params(),
        cost_estimate=cost(
            6 * tokens * width * 3 * cols,
            4 * (tokens * width + 5 * width * cols + updates.size),
            2 * plan.pairs * tokens * chosen * block,
        ),
        name="attend",
    )(lists, *decays, x, v, updates, *weights)


def read_out(readers, state, block):
    half = first_half(state.shape)
    wide = jnp.concatenate([jnp.where(half, state, 0.0), jnp.where(half, 0.0, state)], axis=0)
    return jnp.dot(readers, wide.astype(bf16), preferred_element_type=f32) * (
        1.0 / (N * math.sqrt(block))
    )


def mix_kernel(plan, chunks, per, *refs):
    decay_refs, refs = refs[: plan.merge], refs[plan.merge :]
    a_refs, refs = refs[: plan.merge], refs[plan.merge :]
    c_refs, refs = refs[: plan.merge], refs[plan.merge :]
    s_ref, back_ref, out_refs, mixed = refs[0], refs[1], refs[2:-1], refs[-1]
    step, cols_here = a_refs[0].shape
    here = s_ref.shape[0] // (plan.pairs * N)
    block = step // here
    first = plan.core() == 0
    i = pl.program_id(0)

    @pl.when(i < chunks)
    def _():
        for n in range(here):
            g = i * here + n
            rows = slice(n * block, (n + 1) * block)
            to = pl.ds(pl.multiple_of(i * step + n * block, block), block)
            for p in range(plan.pairs):
                cols = slice(p * LANES, (p + 1) * LANES)
                at = (n * plan.pairs + p) * N
                readers = jnp.concatenate([c[rows, cols] for c in c_refs], axis=0)
                read = read_out(readers, s_ref[at : at + N, :].astype(f32), block)
                decays = [plan.decay(decay_refs, s, p, g) for s in range(plan.merge)]
                if plan.merge == 2:
                    both = decays[0] * decays[1]
                    decays = [jnp.where(first, decays[0], both), jnp.where(first, both, decays[1])]
                for s in range(plan.merge):
                    there = slice(s * cols_here + p * LANES, s * cols_here + (p + 1) * LANES)
                    mixed[to, there] = (
                        a_refs[s][rows, cols] + decays[s] * read[s * block : (s + 1) * block]
                    ).astype(bf16)

    @pl.when(i >= chunks)
    def _():
        placed = jnp.dot(back_ref[...], mixed[...], preferred_element_type=f32).astype(bf16)
        for k in range(plan.peers):

            @pl.when(lax.div(i - chunks, per) == k)
            def _(k=k):
                for s in range(plan.merge):
                    out_refs[s * plan.peers + k][...] = placed[
                        :, s * cols_here : (s + 1) * cols_here
                    ]


def mix(plan, decays, attended, readers, state, back):
    tokens = back.shape[0]
    width = attended[0].shape[1]
    local = tokens // plan.peers
    chunks = 4
    step = tokens // chunks
    size = min(256, local)
    per = local // size
    first = lambda i: (jnp.minimum(i, chunks - 1), 0)
    return pl.pallas_call(
        functools.partial(mix_kernel, plan, chunks, per),
        grid=(chunks + tokens // size,),
        in_specs=[pl.BlockSpec(memory_space=pltpu.SMEM)] * plan.merge
        + [pl.BlockSpec((step, width), first)] * (2 * plan.merge)
        + [
            pl.BlockSpec((state.shape[0] // chunks, LANES), first),
            pl.BlockSpec((size, tokens), lambda i: (jnp.maximum(i - chunks, 0), 0)),
        ],
        out_specs=tuple(
            pl.BlockSpec(
                (size, width), lambda i, k=k: (jnp.clip(i - chunks - k * per, 0, per - 1), 0)
            )
            for s in range(plan.merge)
            for k in range(plan.peers)
        ),
        out_shape=(jax.ShapeDtypeStruct((local, width), bf16),) * (plan.merge * plan.peers),
        scratch_shapes=[pltpu.VMEM((tokens, plan.merge * width), bf16)],
        compiler_params=params(),
        cost_estimate=cost(4 * tokens * tokens * width, 2 * tokens * tokens + 16 * tokens * width),
        name="mix",
    )(*decays, *attended, *readers, state, back)


def out_kernel(plan, w_ref, *refs):
    part_refs, out_ref = refs[:-1], refs[-1]
    depth = part_refs[0].shape[1]
    core, me = plan.core(), lax.axis_index("head")
    total = None
    for s in range(plan.merge):
        for k in range(plan.peers):
            owner = lax.rem(me - k + plan.peers, plan.peers) * plan.merge
            owner = owner + (core if s == 0 else 1 - core)
            rows = pl.ds(pl.multiple_of(owner * depth, depth), depth)
            term = jnp.dot(
                part_refs[s * plan.peers + k][...], w_ref[rows, :], preferred_element_type=f32
            )
            total = term if total is None else total + term
    out_ref[...] = total.astype(bf16)


def project_out(plan, w, parts):
    local = parts[0].shape[0]
    width = w.shape[1]
    return pl.pallas_call(
        functools.partial(out_kernel, plan),
        out_shape=jax.ShapeDtypeStruct((local, width), bf16),
        compiler_params=params(24),
        cost_estimate=cost(2 * local * w.size, 2 * (w.size + 2 * local * width)),
        name="project_out",
    )(w, *parts)


def body(frames_in, in_weight, out_weight, block_ids, block_lists, decays):
    local_tokens = frames_in.shape[1]
    heads_here = decays.shape[1]
    groups = block_lists.shape[0]
    me = lax.axis_index("head")
    plan = Plan(lax.axis_size("tm"), lax.axis_size("head"), heads_here)

    own = frames_in[0]
    chunks = 2 if local_tokens >= 512 else 1
    arriving = [
        plan.to_peer(chunk, plan.peers - k, False)
        for k in range(1, plan.peers)
        for chunk in jnp.split(own, chunks)
    ]
    owns = [own] + [plan.swap(own)] * (plan.merge - 1)
    rates = [decays[0]] + [plan.swap(decays[0])] * (plan.merge - 1)
    block = reorder(plan, [in_weight] + [plan.swap(in_weight)] * (plan.merge - 1))

    ids = jnp.roll(block_ids, -me * local_tokens)
    pick, rest = pick_tokens(ids, local_tokens, groups)
    part = place_tokens(plan, pick, owns, [])
    back = back_tokens(ids, groups)
    if plan.ringed:
        weights, beside = [], [pick, part, back]
        for k in range(plan.along):
            crossed = plan.cross(block)
            weights += [block, crossed]
            if k < plan.along - 1:
                block = plan.round(block)
                block, crossed, beside[:1] = lax.optimization_barrier((block, crossed, beside[:1]))
                weights[-1] = crossed
                beside = beside[1:]
                n = k - (plan.along - 1 - len(arriving))
                if 0 <= n < len(arriving):
                    arriving[n], block = lax.optimization_barrier((arriving[n], block))
    else:
        weights = [
            lax.all_gather(block, "tm", axis=0, tiled=True, axis_index_groups=plan.groups())
        ]
    if plan.merge == 2:
        arriving = arriving + [plan.swap(chunk) for chunk in arriving]
    x = place_tokens(plan, rest, arriving, [part])
    v, updates, total = project_updates(plan, rates, x, weights, groups)

    def exchange(blocks):
        return lax.all_to_all(
            blocks, "tm", split_axis=0, concat_axis=0, tiled=True,
            axis_index_groups=plan.groups(),
        )

    share = updates.shape[1] // plan.chips
    arrived = exchange(total)
    attended = [attend(plan, 0, block_lists, rates, x, v, weights, updates)]
    arrived, attended = lax.optimization_barrier((arrived, attended))
    states = scan_states(plan, arrived, share)
    if plan.merge == 2:
        x, states = lax.optimization_barrier((x, states))
        attended.append(attend(plan, 1, block_lists, rates, x, v, weights, updates))
    state = exchange(states).reshape(-1, LANES)

    bases, readers = ([a[i] for a in attended] for i in range(2))
    mixed = mix(plan, rates, bases, readers, state, back)
    features = [
        mixed[0] if s == 0 and k == 0 else plan.to_peer(mixed[s * plan.peers + k], k, s == 1)
        for s in range(plan.merge)
        for k in range(plan.peers)
    ]
    return project_out(plan, out_weight, features)[None]


def solution(mesh):
    return jax.shard_map(
        body,
        mesh=mesh,
        in_specs=(P("tm", "head", None), P("tm", "head"), P(), P(), P(), P("tm", "head", None)),
        out_specs=P("tm", "head", None),
        check_vma=False,
    )
```

time: 152 us -> 134 us (0.88)
  waiting for transfers between devices: 48.7 us -> 17.2 us
  Pallas kernels: 64.3 us -> 79.7 us
  between operations: 13.6 us -> 0.18 us
  starting transfers between devices: 15.9 us -> 25.5 us
    ppermute x3, waiting for transfers between devices: 30.7 us -> 7.32 us  [to_peer(): return lax.ppermute(block, 'head', pairs)]
    pallas_call x5 -> x8, Pallas kernels: 59.3 us -> 74.6 us  [the longest x2 29.6 us: attend(): pl.pallas_call(functools.partial(attend_kernel, plan, slot, chunks), grid...]
    all_gather x1 -> x0, waiting for transfers between devices: 14.3 us -> none  [body(): lax.all_gather(reorder(plan, weights), 'tm', axis=0, tiled=True, axis_ind...]
    ppermute x0 -> x7, starting transfers between devices: none -> 10.6 us  [the longest x3 5.64 us: round(): return lax.ppermute(block, 'tm', pairs)]
    ppermute x0 -> x7, waiting for transfers between devices: none -> 3.98 us  [the longest x3 3.97 us: round(): return lax.ppermute(block, 'tm', pairs)]
  transfers between devices with their start and end apart: 13 -> 19, of which waited for: 6 -> 5; matrix products, arithmetic and copies ran while one was open for 2% -> 3% of each run, Pallas kernels for 28% -> 44%
where the time goes in v4:
time: 134 us; the launch traced here: 133 us
  Pallas kernels  79.7 us (59%)
  starting transfers between devices  25.5 us (19%)
  waiting for transfers between devices  17.2 us (13%)
  local copies, waits for them, and re-layouts  9.51 us (7%)
    pallas_call x2, Pallas kernels, attend(): pl.pallas_call(functools.partial(attend_kernel, plan, slot, chunks), grid...  29.6 us
    pallas_call x2, Pallas kernels, place_tokens(): pl.pallas_call(functools.partial(place_kernel, plan.merge, len(frames) //...  19.6 us
    pallas_call x1, Pallas kernels, project_updates(): pl.pallas_call(functools.partial(update_kernel, plan, groups), grid=(plan...  9.85 us
    all_to_all x2, starting transfers between devices, exchange(): lax.all_to_all(blocks, 'tm', split_axis=0, concat_axis=0, tiled=True, axi...  9.46 us
    pallas_call x1, Pallas kernels, mix(): pl.pallas_call(functools.partial(mix_kernel, plan, chunks, per), grid=(ch...  7.67 us
    ppermute x3, waiting for transfers between devices, to_peer(): return lax.ppermute(block, 'head', pairs)  7.32 us
    unnamed x39, local copies, waits for them, and re-layouts  7.22 us
    ppermute x3, starting transfers between devices, round(): return lax.ppermute(block, 'tm', pairs)  5.64 us
  transfers between devices with their start and end apart: 19, of which 5 were waited for; matrix products, arithmetic and copies ran while one was open for 3% of the time, Pallas kernels for 44%

profile of v4, /device:TPU:0, one launch (start us, length us, event | category | flops | bytes accessed | tf_op | source)
XLA Modules:
  0.0 132.7 jit_solution(2793230764144331103)
XLA Ops:
  0.5 2.9 %collective-permute-done.2.refs_1_ = bf16[64,2560]{1,0:T(8,128)(2,1)S(1)} collective-permute-done((bf16[64,2560]{1,0:T(8,128)(2,1)}, bf16[64,2560]{1,0:T(8,128)(2,1)S(1)}, u32[]{:S(2)}, u32[]{:S(2)}) %collective-permute-start.2) | collective-permute-done | bytes 327712 | tf_op jit(solution)/shard_map/ppermute | solution.py:56
  4.1 1.9 %reorder.1.refs_3_.refs_6_ = bf16[128,1280]{1,0:T(8,128)(2,1)} custom-call(bf16[64,2560]{1,0:T(8,128)(2,1)} %refs_0_.3, bf16[64,2560]{1,0:T(8,128)(2,1)} %copy-done.3), custom_call_target="tpu_custom_call" | custom-call | bytes 655360 | tf_op jit(solution)/shard_map/reorder/pallas_call | solution.py:142
  6.1 2.9 %collective-permute-start.3 = (bf16[128,1280]{1,0:T(8,128)(2,1)}, bf16[128,1280]{1,0:T(8,128)(2,1)S(1)}, u32[]{:S(2)}, u32[]{:S(2)}) collective-permute-start(bf16[128,1280]{1,0:T(8,128)(2,1)} %reorder.1.refs_3_.refs_6_), channel_id=1, source_target_pairs={{0,8},{2,10},{4,12},{6,14},{8,16},{10,18},{12,20},{14,22},{16,24},... | collective-permute-start | bytes 983048 | tf_op jit(solution)/shard_map/ppermute | solution.py:61
  9.0 1.5 %collective-permute-start.4 = (bf16[128,1280]{1,0:T(8,128)(2,1)}, bf16[128,1280]{1,0:T(8,128)(2,1)}, u32[]{:S(2)}, u32[]{:S(2)}) collective-permute-start(bf16[128,1280]{1,0:T(8,128)(2,1)} %reorder.1.refs_3_.refs_6_), channel_id=1, source_target_pairs={{0,4},{2,6},{4,0},{6,2},{8,12},{10,14},{12,8},{14,10},{16,20},{18,... | collective-permute-start | bytes 983048 | tf_op jit(solution)/shard_map/ppermute | solution.py:66
  10.5 1.3 slice_bitcast_fusion
  11.8 1.6 %collective-permute-start.1 = (bf16[256,1024]{1,0:T(8,128)(2,1)S(1)}, bf16[256,1024]{1,0:T(8,128)(2,1)S(1)}, u32[]{:S(2)}, u32[]{:S(2)}) collective-permute-start(bf16[256,1024]{1,0:T(8,128)(2,1)S(1)} %get-tuple-element.62), channel_id=1, source_target_pairs={{0,1},{1,0},{2,3},{3,2},{4,5},{5,4},{6,7},{7,6},{8,9},{9,8},{10,11... | collective-permute-start | bytes 1572872 | tf_op jit(solution)/shard_map/ppermute | solution.py:83
  14.6 2.7 %pick_tokens.1 = (bf16[1024,512]{1,0:T(8,128)(2,1)}, bf16[1024,512]{1,0:T(8,128)(2,1)}) custom-call(s32[1,1024]{1,0:T(1,128)} %bitcast.13), custom_call_target="tpu_custom_call" | custom-call | flops 33554432 | bytes 2097152 | tf_op jit(solution)/shard_map/pick_tokens/pallas_call | solution.py:198
  17.2 2.0 %collective-permute-done.3.refs_5_.refs_8_ = bf16[128,1280]{1,0:T(8,128)(2,1)S(1)} collective-permute-done((bf16[128,1280]{1,0:T(8,128)(2,1)}, bf16[128,1280]{1,0:T(8,128)(2,1)S(1)}, u32[]{:S(2)}, u32[]{:S(2)}) %collective-permute-start.3) | collective-permute-done | bytes 327712 | tf_op jit(solution)/shard_map/ppermute | solution.py:61
  19.3 1.1 collective-permute-start.5
  20.4 1.5 %collective-permute-start.6 = (bf16[128,1280]{1,0:T(8,128)(2,1)S(1)}, bf16[128,1280]{1,0:T(8,128)(2,1)S(1)}, u32[]{:S(2)}, u32[]{:S(2)}) collective-permute-start(bf16[128,1280]{1,0:T(8,128)(2,1)S(1)} %collective-permute-done.3.refs_5_.refs_8_), channel_id=1, source_target_pairs={{0,4},{2,6},{4,0},{6,2},{8,12},{10,14},{12,8},{14,10},{16,20},{18,... | collective-permute-start | bytes 983048 | tf_op jit(solution)/shard_map/ppermute | solution.py:66
  21.9 1.0 copy-done.9
  22.9 9.4 %place_tokens.2.refs_5_ = bf16[2048,1024]{1,0:T(8,128)(2,1)} custom-call(bf16[1024,512]{1,0:T(8,128)(2,1)} %get-tuple-element.34.refs_0_, bf16[512,1024]{1,0:T(8,128)(2,1)} %bitcast.12, bf16[512,1024]{1,0:T(8,128)(2,1)} %copy-done.9), custom_call_target="tpu_custom_call" | custom-call | flops 4294967296 | bytes 6291456 | tf_op jit(solution)/shard_map/place_tokens/pallas_call | solution.py:274
  33.6 1.6 %collective-permute-start.9 = (bf16[128,1280]{1,0:T(8,128)(2,1)}, bf16[128,1280]{1,0:T(8,128)(2,1)S(1)}, u32[]{:S(2)}, u32[]{:S(2)}) collective-permute-start(bf16[128,1280]{1,0:T(8,128)(2,1)} %collective-permute-done.5.refs_7_.refs_10_), channel_id=1, source_target_pairs={{0,8},{2,10},{4,12},{6,14},{8,16},{10,18},{12,20},{14,22},{16,24},... | collective-permute-start | bytes 983048 | tf_op jit(solution)/shard_map/ppermute | solution.py:61
  35.2 1.0 copy.9.ids_ref
  36.2 5.2 %back_tokens.1.refs_7_ = bf16[1024,1024]{1,0:T(8,128)(2,1)} custom-call(s32[1024,1]{1,0:T(8,128)} %copy.9.ids_ref), custom_call_target="tpu_custom_call" | custom-call | flops 268435456 | bytes 2097152 | tf_op jit(solution)/shard_map/back_tokens/pallas_call | solution.py:239
  41.5 1.9 %collective-permute-done.9.refs_9_.refs_12_ = bf16[128,1280]{1,0:T(8,128)(2,1)S(1)} collective-permute-done((bf16[128,1280]{1,0:T(8,128)(2,1)}, bf16[128,1280]{1,0:T(8,128)(2,1)S(1)}, u32[]{:S(2)}, u32[]{:S(2)}) %collective-permute-start.9) | collective-permute-done | bytes 327712 | tf_op jit(solution)/shard_map/ppermute | solution.py:61
  44.0 1.5 %collective-permute-start.13 = (bf16[128,1280]{1,0:T(8,128)(2,1)S(1)}, bf16[128,1280]{1,0:T(8,128)(2,1)S(1)}, u32[]{:S(2)}, u32[]{:S(2)}) collective-permute-start(bf16[128,1280]{1,0:T(8,128)(2,1)S(1)} %collective-permute-done.9.refs_9_.refs_12_), channel_id=1, source_target_pairs={{0,4},{2,6},{4,0},{6,2},{8,12},{10,14},{12,8},{14,10},{16,20},{18,... | collective-permute-start | bytes 983048 | tf_op jit(solution)/shard_map/ppermute | solution.py:66
  45.5 0.8 copy-done.12
  46.5 10.1 %place_tokens.3.refs_2_.refs_3_ = bf16[2048,1024]{1,0:T(8,128)(2,1)} custom-call(bf16[1024,512]{1,0:T(8,128)(2,1)} %get-tuple-element.33.refs_0_, bf16[256,1024]{1,0:T(8,128)(2,1)} %copy-done.10, bf16[256,1024]{1,0:T(8,128)(2,1)} %copy-done.11, bf16[256,1024]{1,0:T(8,128)(2,1)} %copy-done.12, bf16[256,1024]{1,0:T(8,128)(2,1)} %copy-done.13, ...), custom_call_target="tpu_custom_call" | custom-call | flops 4294967296 | bytes 6291456 | tf_op jit(solution)/shard_map/place_tokens/pallas_call | solution.py:274
  58.0 9.8 %project_updates.1 = (bf16[2048,256]{1,0:T(8,128)(2,1)}, f32[2,2048,128]{2,1,0:T(8,128)}, bf16[8,272,128]{2,1,0:T(8,128)(2,1)}) custom-call(f32[8,16]{1,0:T(8,128)} %bitcast.15, f32[8,16]{1,0:T(8,128)} %copy-done.7, bf16[2048,1024]{1,0:T(8,128)(2,1)} %place_tokens.3.refs_2_.refs_3_, bf16[128,1280]{1,0:T(8,128)(2,1)} %reorder.1.refs_3_.refs_6_, ...), custom_call_target="tpu_custom_call" | custom-call | flops 4294967296 | bytes 8388608 | tf_op jit(solution)/shard_map/project_updates/pallas_call | solution.py:368
  67.9 3.5 %all-to-all-start = ((bf16[8,272,128]{2,1,0:T(8,128)(2,1)}), bf16[8,272,128]{2,1,0:T(8,128)(2,1)S(1)}, u32[]{:S(2)}, u32[]{:S(2)}) async-start(bf16[8,272,128]{2,1,0:T(8,128)(2,1)} %get-tuple-element.45), calls=%async_computation | async-start | bytes 1114112 | tf_op jit(solution)/shard_map/all_to_all | solution.py:700
  72.1 14.8 %attend.2 = (f32[1024,256]{1,0:T(8,128)}, bf16[1024,256]{1,0:T(8,128)(2,1)}) custom-call(s32[16,4]{1,0:T(8,128)} %copy.10.refs_0_, f32[8,16]{1,0:T(8,128)} %bitcast.16, f32[8,16]{1,0:T(8,128)} %copy-done.7, bf16[2048,1024]{1,0:T(8,128)(2,1)} %place_tokens.3.refs_2_.refs_3_, bf16[2048,256]{1,0:T(8,128)(2,1)} %get-tuple-element.46.refs_4_, ...), custom_call_target="tpu_custom_call" | custom-call | flops 4831838208 | bytes 11534336 | tf_op jit(solution)/shard_map/attend/pallas_call | solution.py:504
  86.9 0.9 scan_states.1
  87.8 5.9 %all-to-all-start.1 = ((bf16[8,256,128]{2,1,0:T(8,128)(2,1)}), bf16[8,256,128]{2,1,0:T(8,128)(2,1)S(1)}, u32[]{:S(2)}, u32[]{:S(2)}) async-start(bf16[8,256,128]{2,1,0:T(8,128)(2,1)} %scan_states.1), calls=%async_computation.1 | async-start | bytes 1048576 | tf_op jit(solution)/shard_map/all_to_all | solution.py:700
  93.8 14.8 %attend.3 = (f32[1024,256]{1,0:T(8,128)}, bf16[1024,256]{1,0:T(8,128)(2,1)}) custom-call(s32[16,4]{1,0:T(8,128)} %copy.10.refs_0_, f32[8,16]{1,0:T(8,128)} %bitcast.17, f32[8,16]{1,0:T(8,128)} %copy-done.7, bf16[2048,1024]{1,0:T(8,128)(2,1)} %place_tokens.3.refs_2_.refs_3_, bf16[2048,256]{1,0:T(8,128)(2,1)} %get-tuple-element.46.refs_4_, ...), custom_call_target="tpu_custom_call" | custom-call | flops 4831838208 | bytes 11534336 | tf_op jit(solution)/shard_map/attend/pallas_call | solution.py:504
  108.5 0.8 copy-done.2
  109.3 7.7 %mix.1 = (bf16[512,256]{1,0:T(8,128)(2,1)}, bf16[512,256]{1,0:T(8,128)(2,1)}, bf16[512,256]{1,0:T(8,128)(2,1)}, bf16[512,256]{1,0:T(8,128)(2,1)}) custom-call(f32[8,16]{1,0:T(8,128)} %bitcast.18, f32[8,16]{1,0:T(8,128)} %copy-done.7, f32[1024,256]{1,0:T(8,128)} %get-tuple-element.50.refs_2_, f32[1024,256]{1,0:T(8,128)} %get-tuple-element.53.refs_3_, ...), custom_call_target="tpu_custom_call" | custom-call | flops 1073741824 | bytes 6291456 | tf_op jit(solution)/shard_map/mix/pallas_call | solution.py:602
  117.0 1.6 %collective-permute-start.14 = (bf16[512,256]{1,0:T(8,128)(2,1)}, bf16[512,256]{1,0:T(8,128)(2,1)S(1)}, u32[]{:S(2)}, u32[]{:S(2)}) collective-permute-start(bf16[512,256]{1,0:T(8,128)(2,1)} %get-tuple-element.58), channel_id=1, source_target_pairs={{0,1},{1,0},{2,3},{3,2},{4,5},{5,4},{6,7},{7,6},{8,9},{9,8},{10,11... | collective-permute-start | bytes 786440 | tf_op jit(solution)/shard_map/ppermute | solution.py:83
  119.2 7.3 %collective-permute-done.14.refs_1_ = bf16[512,256]{1,0:T(8,128)(2,1)S(1)} collective-permute-done((bf16[512,256]{1,0:T(8,128)(2,1)}, bf16[512,256]{1,0:T(8,128)(2,1)S(1)}, u32[]{:S(2)}, u32[]{:S(2)}) %collective-permute-start.14) | collective-permute-done | bytes 262176 | tf_op jit(solution)/shard_map/ppermute | solution.py:83
  126.5 3.0 %collective-permute-done.16.refs_3_ = bf16[512,256]{1,0:T(8,128)(2,1)S(1)} collective-permute-done((bf16[512,256]{1,0:T(8,128)(2,1)}, bf16[512,256]{1,0:T(8,128)(2,1)S(1)}, u32[]{:S(2)}, u32[]{:S(2)}) %collective-permute-start.16) | collective-permute-done | bytes 262176 | tf_op jit(solution)/shard_map/ppermute | solution.py:91
  129.5 0.9 copy-done.1
  130.5 2.2 %project_out.1 = bf16[512,1024]{1,0:T(8,128)(2,1)} custom-call(bf16[1024,1024]{1,0:T(8,128)(2,1)S(1)} %copy-done, bf16[512,256]{1,0:T(8,128)(2,1)S(1)} %copy-done.1, bf16[512,256]{1,0:T(8,128)(2,1)S(1)} %collective-permute-done.14.refs_1_, bf16[512,256]{1,0:T(8,128)(2,1)S(1)} %collective-permute-done.15.refs_2_, ...), custom_call_target="tpu_custom_call" | custom-call | flops 1073741824 | bytes 4194304 | tf_op jit(solution)/shard_map/project_out/pallas_call | solution.py:646
  (59 shorter events, 7.2 us)
Async XLA Ops:
  0.0 13.9 %copy-start.5 = (s32[1024]{0:T(1024)S(1)}, s32[1024]{0:T(1024)}, u32[]{:S(2)}) copy-start(s32[1024]{0:T(1024)} %param.9) | copy-start | bytes 12292
  0.0 21.9 %collective-permute-start.7 = (bf16[512,1024]{1,0:T(8,128)(2,1)}, bf16[512,1024]{1,0:T(8,128)(2,1)S(1)}, u32[]{:S(2)}, u32[]{:S(2)}) collective-permute-start(bf16[512,1024]{1,0:T(8,128)(2,1)} %bitcast.11), channel_id=1, source_target_pairs={{0,2},{2,0},{4,6},{6,4},{8,10},{10,8},{12,14},{14,12},{16,18},{18,... | collective-permute-start | bytes 3145736 | tf_op jit(solution)/shard_map/ppermute | solution.py:56
  0.5 3.0 %collective-permute-start.2 = (bf16[64,2560]{1,0:T(8,128)(2,1)}, bf16[64,2560]{1,0:T(8,128)(2,1)S(1)}, u32[]{:S(2)}, u32[]{:S(2)}) collective-permute-start(bf16[64,2560]{1,0:T(8,128)(2,1)} %refs_0_.3), channel_id=1, source_target_pairs={{0,2},{2,0},{4,6},{6,4},{8,10},{10,8},{12,14},{14,12},{16,18},{18,... | collective-permute-start | bytes 983048 | tf_op jit(solution)/shard_map/ppermute | solution.py:56
  6.1 13.2 %collective-permute-start.3 = (bf16[128,1280]{1,0:T(8,128)(2,1)}, bf16[128,1280]{1,0:T(8,128)(2,1)S(1)}, u32[]{:S(2)}, u32[]{:S(2)}) collective-permute-start(bf16[128,1280]{1,0:T(8,128)(2,1)} %reorder.1.refs_3_.refs_6_), channel_id=1, source_target_pairs={{0,8},{2,10},{4,12},{6,14},{8,16},{10,18},{12,20},{14,22},{16,24},... | collective-permute-start | bytes 983048 | tf_op jit(solution)/shard_map/ppermute | solution.py:61
  9.0 10.2 %collective-permute-start.4 = (bf16[128,1280]{1,0:T(8,128)(2,1)}, bf16[128,1280]{1,0:T(8,128)(2,1)}, u32[]{:S(2)}, u32[]{:S(2)}) collective-permute-start(bf16[128,1280]{1,0:T(8,128)(2,1)} %reorder.1.refs_3_.refs_6_), channel_id=1, source_target_pairs={{0,4},{2,6},{4,0},{6,2},{8,12},{10,14},{12,8},{14,10},{16,20},{18,... | collective-permute-start | bytes 983048 | tf_op jit(solution)/shard_map/ppermute | solution.py:66
  11.8 20.6 %collective-permute-start.1 = (bf16[256,1024]{1,0:T(8,128)(2,1)S(1)}, bf16[256,1024]{1,0:T(8,128)(2,1)S(1)}, u32[]{:S(2)}, u32[]{:S(2)}) collective-permute-start(bf16[256,1024]{1,0:T(8,128)(2,1)S(1)} %get-tuple-element.62), channel_id=1, source_target_pairs={{0,1},{1,0},{2,3},{3,2},{4,5},{5,4},{6,7},{7,6},{8,9},{9,8},{10,11... | collective-permute-start | bytes 1572872 | tf_op jit(solution)/shard_map/ppermute | solution.py:83
  13.4 30.0 %collective-permute-start.8 = (bf16[256,1024]{1,0:T(8,128)(2,1)S(1)}, bf16[256,1024]{1,0:T(8,128)(2,1)S(1)}, u32[]{:S(2)}, u32[]{:S(2)}) collective-permute-start(bf16[256,1024]{1,0:T(8,128)(2,1)S(1)} %get-tuple-element.61), channel_id=1, source_target_pairs={{0,1},{1,0},{2,3},{3,2},{4,5},{5,4},{6,7},{7,6},{8,9},{9,8},{10,11... | collective-permute-start | bytes 1572872 | tf_op jit(solution)/shard_map/ppermute | solution.py:83
  19.3 13.0 %copy-start.14 = (bf16[128,1280]{1,0:T(8,128)(2,1)}, bf16[128,1280]{1,0:T(8,128)(2,1)S(1)}, u32[]{:S(2)}) copy-start(bf16[128,1280]{1,0:T(8,128)(2,1)S(1)} %collective-permute-done.3.refs_5_.refs_8_) | copy-start | bytes 983044
  19.3 15.9 %copy-start.4 = (s32[1024]{0:T(1024)S(1)}, s32[1024]{0:T(1024)}, u32[]{:S(2)}) copy-start(s32[1024]{0:T(1024)} %fusion) | copy-start | bytes 12292
  19.3 13.0 %collective-permute-start.5 = (bf16[128,1280]{1,0:T(8,128)(2,1)S(1)}, bf16[128,1280]{1,0:T(8,128)(2,1)}, u32[]{:S(2)}, u32[]{:S(2)}) collective-permute-start(bf16[128,1280]{1,0:T(8,128)(2,1)S(1)} %collective-permute-done.3.refs_5_.refs_8_), channel_id=1, source_target_pairs={{0,8},{2,10},{4,12},{6,14},{8,16},{10,18},{12,20},{14,22},{16,24},... | collective-permute-start | bytes 983048 | tf_op jit(solution)/shard_map/ppermute | solution.py:61
  20.4 11.9 %collective-permute-start.6 = (bf16[128,1280]{1,0:T(8,128)(2,1)S(1)}, bf16[128,1280]{1,0:T(8,128)(2,1)S(1)}, u32[]{:S(2)}, u32[]{:S(2)}) collective-permute-start(bf16[128,1280]{1,0:T(8,128)(2,1)S(1)} %collective-permute-done.3.refs_5_.refs_8_), channel_id=1, source_target_pairs={{0,4},{2,6},{4,0},{6,2},{8,12},{10,14},{12,8},{14,10},{16,20},{18,... | collective-permute-start | bytes 983048 | tf_op jit(solution)/shard_map/ppermute | solution.py:66
  21.9 1.0 copy-start.9
  32.3 11.2 %copy-start.6 = (f32[1,8,16]{2,1,0:T(8,128)S(1)}, f32[1,8,16]{2,1,0:T(8,128)}, u32[]{:S(2)}) copy-start(f32[1,8,16]{2,1,0:T(8,128)} %param.11) | copy-start | bytes 1540
  33.1 12.4 %copy-start.10 = (bf16[256,1024]{1,0:T(8,128)(2,1)}, bf16[256,1024]{1,0:T(8,128)(2,1)S(1)}, u32[]{:S(2)}) copy-start(bf16[256,1024]{1,0:T(8,128)(2,1)S(1)} %collective-permute-done.1.refs_1_) | copy-start | bytes 1572868
  33.1 8.4 %collective-permute-start.10 = (bf16[128,1280]{1,0:T(8,128)(2,1)}, bf16[128,1280]{1,0:T(8,128)(2,1)S(1)}, u32[]{:S(2)}, u32[]{:S(2)}) collective-permute-start(bf16[128,1280]{1,0:T(8,128)(2,1)} %collective-permute-done.5.refs_7_.refs_10_), channel_id=1, source_target_pairs={{0,4},{2,6},{4,0},{6,2},{8,12},{10,14},{12,8},{14,10},{16,20},{18,... | collective-permute-start | bytes 983048 | tf_op jit(solution)/shard_map/ppermute | solution.py:66
  33.6 9.8 %collective-permute-start.9 = (bf16[128,1280]{1,0:T(8,128)(2,1)}, bf16[128,1280]{1,0:T(8,128)(2,1)S(1)}, u32[]{:S(2)}, u32[]{:S(2)}) collective-permute-start(bf16[128,1280]{1,0:T(8,128)(2,1)} %collective-permute-done.5.refs_7_.refs_10_), channel_id=1, source_target_pairs={{0,8},{2,10},{4,12},{6,14},{8,16},{10,18},{12,20},{14,22},{16,24},... | collective-permute-start | bytes 983048 | tf_op jit(solution)/shard_map/ppermute | solution.py:61
  41.5 4.0 %collective-permute-start.11 = (bf16[256,1024]{1,0:T(8,128)(2,1)S(1)}, bf16[256,1024]{1,0:T(8,128)(2,1)S(1)}, u32[]{:S(2)}, u32[]{:S(2)}) collective-permute-start(bf16[256,1024]{1,0:T(8,128)(2,1)S(1)} %collective-permute-done.1.refs_1_), channel_id=1, source_target_pairs={{0,2},{2,0},{4,6},{6,4},{8,10},{10,8},{12,14},{14,12},{16,18},{18,... | collective-permute-start | bytes 1572872 | tf_op jit(solution)/shard_map/ppermute | solution.py:56
  41.5 15.2 %copy-start.16 = (bf16[128,1280]{1,0:T(8,128)(2,1)}, bf16[128,1280]{1,0:T(8,128)(2,1)S(1)}, u32[]{:S(2)}) copy-start(bf16[128,1280]{1,0:T(8,128)(2,1)S(1)} %collective-permute-done.10.refs_8_.refs_11_) | copy-start | bytes 983044
  43.4 13.3 %copy-start.17 = (bf16[128,1280]{1,0:T(8,128)(2,1)}, bf16[128,1280]{1,0:T(8,128)(2,1)S(1)}, u32[]{:S(2)}) copy-start(bf16[128,1280]{1,0:T(8,128)(2,1)S(1)} %collective-permute-done.9.refs_9_.refs_12_) | copy-start | bytes 983044
  43.4 2.1 %copy-start.11 = (bf16[256,1024]{1,0:T(8,128)(2,1)}, bf16[256,1024]{1,0:T(8,128)(2,1)S(1)}, u32[]{:S(2)}) copy-start(bf16[256,1024]{1,0:T(8,128)(2,1)S(1)} %collective-permute-done.8.refs_2_) | copy-start | bytes 1572868
  43.4 2.1 %collective-permute-start.12 = (bf16[256,1024]{1,0:T(8,128)(2,1)S(1)}, bf16[256,1024]{1,0:T(8,128)(2,1)S(1)}, u32[]{:S(2)}, u32[]{:S(2)}) collective-permute-start(bf16[256,1024]{1,0:T(8,128)(2,1)S(1)} %collective-permute-done.8.refs_2_), channel_id=1, source_target_pairs={{0,2},{2,0},{4,6},{6,4},{8,10},{10,8},{12,14},{14,12},{16,18},{18,... | collective-permute-start | bytes 1572872 | tf_op jit(solution)/shard_map/ppermute | solution.py:56
  43.5 13.2 %collective-permute-start = (f32[8,16]{1,0:T(8,128)S(1)}, f32[8,16]{1,0:T(8,128)S(1)}, u32[]{:S(2)}, u32[]{:S(2)}) collective-permute-start(f32[8,16]{1,0:T(8,128)S(1)} %bitcast.19), channel_id=1, source_target_pairs={{0,2},{2,0},{4,6},{6,4},{8,10},{10,8},{12,14},{14,12},{16,18},{18,... | collective-permute-start | bytes 1544 | tf_op jit(solution)/shard_map/ppermute | solution.py:56
  44.0 12.7 %collective-permute-start.13 = (bf16[128,1280]{1,0:T(8,128)(2,1)S(1)}, bf16[128,1280]{1,0:T(8,128)(2,1)S(1)}, u32[]{:S(2)}, u32[]{:S(2)}) collective-permute-start(bf16[128,1280]{1,0:T(8,128)(2,1)S(1)} %collective-permute-done.9.refs_9_.refs_12_), channel_id=1, source_target_pairs={{0,4},{2,6},{4,0},{6,2},{8,12},{10,14},{12,8},{14,10},{16,20},{18,... | collective-permute-start | bytes 983048 | tf_op jit(solution)/shard_map/ppermute | solution.py:66
  45.5 1.1 copy-start.13
  56.7 14.8 %copy-start.8 = (s32[16,4]{0,1:T(4,128)S(1)}, s32[16,4]{0,1:T(4,128)}, u32[]{:S(2)}) copy-start(s32[16,4]{0,1:T(4,128)} %param.10) | copy-start | bytes 772
  67.9 19.0 %all-to-all-start = ((bf16[8,272,128]{2,1,0:T(8,128)(2,1)}), bf16[8,272,128]{2,1,0:T(8,128)(2,1)S(1)}, u32[]{:S(2)}, u32[]{:S(2)}) async-start(bf16[8,272,128]{2,1,0:T(8,128)(2,1)} %get-tuple-element.45), calls=%async_computation | async-start | bytes 1114112 | tf_op jit(solution)/shard_map/all_to_all | solution.py:700
  87.8 20.7 %all-to-all-start.1 = ((bf16[8,256,128]{2,1,0:T(8,128)(2,1)}), bf16[8,256,128]{2,1,0:T(8,128)(2,1)S(1)}, u32[]{:S(2)}, u32[]{:S(2)}) async-start(bf16[8,256,128]{2,1,0:T(8,128)(2,1)} %scan_states.1), calls=%async_computation.1 | async-start | bytes 1048576 | tf_op jit(solution)/shard_map/all_to_all | solution.py:700
  109.3 20.2 %copy-start = (bf16[1024,1024]{1,0:T(8,128)(2,1)S(1)}, bf16[1024,1024]{1,0:T(8,128)(2,1)}, u32[]{:S(2)}) copy-start(bf16[1024,1024]{1,0:T(8,128)(2,1)} %w_ref.1) | copy-start | bytes 6291460
  117.0 9.5 %collective-permute-start.14 = (bf16[512,256]{1,0:T(8,128)(2,1)}, bf16[512,256]{1,0:T(8,128)(2,1)S(1)}, u32[]{:S(2)}, u32[]{:S(2)}) collective-permute-start(bf16[512,256]{1,0:T(8,128)(2,1)} %get-tuple-element.58), channel_id=1, source_target_pairs={{0,1},{1,0},{2,3},{3,2},{4,5},{5,4},{6,7},{7,6},{8,9},{9,8},{10,11... | collective-permute-start | bytes 786440 | tf_op jit(solution)/shard_map/ppermute | solution.py:83
  118.6 7.9 %collective-permute-start.15 = (bf16[512,256]{1,0:T(8,128)(2,1)}, bf16[512,256]{1,0:T(8,128)(2,1)S(1)}, u32[]{:S(2)}, u32[]{:S(2)}) collective-permute-start(bf16[512,256]{1,0:T(8,128)(2,1)} %get-tuple-element.59), channel_id=1, source_target_pairs={{0,2},{2,0},{4,6},{6,4},{8,10},{10,8},{12,14},{14,12},{16,18},{18,... | collective-permute-start | bytes 786440 | tf_op jit(solution)/shard_map/ppermute | solution.py:56
  118.6 10.9 %collective-permute-start.16 = (bf16[512,256]{1,0:T(8,128)(2,1)}, bf16[512,256]{1,0:T(8,128)(2,1)S(1)}, u32[]{:S(2)}, u32[]{:S(2)}) collective-permute-start(bf16[512,256]{1,0:T(8,128)(2,1)} %get-tuple-element.60), channel_id=1, source_target_pairs={{0,3},{1,2},{2,1},{3,0},{4,7},{5,6},{6,5},{7,4},{8,11},{9,10},{10,... | collective-permute-start | bytes 786440 | tf_op jit(solution)/shard_map/ppermute | solution.py:91
  129.5 1.0 copy-start.1
  (6 other events, 4.4 us)

commit v5 on v4

v5 whole, which is shorter than its diff:
```python
import functools
import math

import jax
import jax.numpy as jnp
from jax import lax
from jax.experimental import pallas as pl
from jax.experimental.pallas import tpu as pltpu
from jax.sharding import PartitionSpec as P

HD = 64
N = 64
LANES = 2 * HD
PIECES = 5
EARLY = (2, 3)
LATE = (0, 1, 4)

epsilon = 1e-06

f32 = jnp.float32
bf16 = jnp.bfloat16


def params(mib=60):
    return pltpu.CompilerParams(vmem_limit_bytes=mib << 20)


def cost(flops, nbytes, transcendentals=0):
    return pl.CostEstimate(
        flops=int(flops), bytes_accessed=int(nbytes), transcendentals=int(transcendentals)
    )


def first_half(shape):
    return lax.broadcasted_iota(jnp.int32, shape, len(shape) - 1) < HD


class Plan:
    def __init__(self, frames, peers, heads_here):
        self.merge = 2 if frames % 2 == 0 and heads_here % 4 == 0 else 1
        self.frames, self.peers = frames, peers
        self.heads = heads_here // self.merge
        self.pairs = self.heads // 2
        self.chips = frames // self.merge
        self.across = 2 if self.chips % 2 == 0 else 1
        self.along = self.chips // self.across
        self.ringed = self.across == 2 and self.along <= 8

    def core(self):
        return lax.rem(lax.axis_index("tm"), self.merge)

    def chip(self):
        return lax.div(lax.axis_index("tm"), self.merge)

    def swap(self, block):
        return lax.ppermute(block, "tm", [(t, t ^ 1) for t in range(self.frames)])

    def round(self, block):
        a, b, c = self.along, self.across, self.merge
        pairs = [(t, (t + b * c) % (a * b * c)) for t in range(self.frames)]
        return lax.ppermute(block, "tm", pairs)

    def cross(self, block):
        c = self.merge
        pairs = [(t, (t // c ^ 1) * c + t % c) for t in range(self.frames)]
        return lax.ppermute(block, "tm", pairs)

    def gather(self, copies, refs, out, cols):
        if len(refs) == 1:
            return [copies.start(refs[0].at[:, cols], out)]
        rows = refs[0].shape[0]
        a, b = lax.div(self.chip(), self.across), lax.rem(self.chip(), self.across)
        made = []
        for i, ref in enumerate(refs):
            k, flip = i // 2, i % 2
            there = lax.rem(a - k + self.along, self.along) * self.across
            at = pl.multiple_of((there + (1 - b if flip else b)) * rows, rows)
            made.append(copies.start(ref.at[:, cols], out.at[pl.ds(at, rows), :]))
        return made

    def to_peer(self, block, k, other):
        if not other:
            pairs = [(j, (j + k) % self.peers) for j in range(self.peers)]
            return lax.ppermute(block, "head", pairs)
        if k == 0:
            return self.swap(block)
        pairs = [
            (t * self.peers + j, (t ^ 1) * self.peers + (j + k) % self.peers)
            for t in range(self.frames)
            for j in range(self.peers)
        ]
        return lax.ppermute(block, ("tm", "head"), pairs)

    def groups(self):
        if self.merge == 1:
            return None
        return [[j * self.merge + c for j in range(self.chips)] for c in range(self.merge)]

    def decay(self, refs, slot, pair, g):
        head = self.core() * self.heads + 2 * pair
        return halves((1, LANES), refs[slot][head, g], refs[slot][head + 1, g])

    def last_decay(self, refs, pair, g):
        if self.merge == 1:
            return self.decay(refs, 0, pair, g)
        one, two = (self.decay(refs, slot, pair, g) for slot in range(2))
        return jnp.where(self.core() == 0, two, one)


class Copies:
    room = 48

    def __init__(self, sems):
        self.sems, self.made = sems, []

    def start(self, src, dst):
        copy = pltpu.make_async_copy(src, dst, self.sems.at[len(self.made)])
        copy.start()
        self.made.append(copy)
        return copy

    @staticmethod
    def scratch():
        return pltpu.SemaphoreType.DMA((Copies.room,))


def finish(copies):
    for copy in copies:
        copy.wait()


def halves(shape, one, two):
    return jnp.where(first_half(shape), one, two)


def reorder_kernel(plan, *refs):
    w_refs, out_ref = refs[:-1], refs[-1]
    rows = w_refs[0].shape[0]
    width = plan.heads * PIECES * HD
    first = plan.core() == 0

    def chosen(ref, at):
        one = ref[:, at : at + HD]
        if plan.merge == 1:
            return one
        return jnp.where(first, one, ref[:, width + at : width + at + HD])

    to = 0
    for kinds in (EARLY, LATE):
        for p in range(plan.pairs):
            for i in kinds:
                blocks = []
                for ref in w_refs:
                    one, two = (chosen(ref, ((2 * p + h) * PIECES + i) * HD) for h in range(2))
                    blocks.append(jnp.concatenate([one, two], axis=1))
                for s, block in enumerate(blocks):
                    if plan.merge == 2:
                        block = jnp.where(first, block, blocks[1 - s])
                    out_ref[s * rows : (s + 1) * rows, to : to + LANES] = block
                to += LANES


def reorder(plan, weights):
    rows = weights[0].shape[0]
    return pl.pallas_call(
        functools.partial(reorder_kernel, plan),
        out_shape=jax.ShapeDtypeStruct((plan.merge * rows, plan.heads * PIECES * HD), bf16),
        compiler_params=params(),
        cost_estimate=cost(0, 4 * weights[0].size),
        name="reorder",
    )(*weights)


def normalise(part, out, at):
    step = min(128, part.shape[0])

    def norm(c, _):
        start = pl.multiple_of(c * step, step)
        wide = part[pl.ds(start, step), :].astype(f32)
        scale = lax.rsqrt(jnp.mean(wide * wide, axis=-1, keepdims=True) + epsilon)
        out[pl.ds(at + start, step), :] = (wide * scale).astype(bf16)
        return 0

    lax.fori_loop(0, part.shape[0] // step, norm, 0)


def pick_kernel(groups, ids_ref, own_ref, rest_ref):
    tokens = ids_ref.shape[1]
    local = own_ref.shape[1]
    block = tokens // groups
    step = 128
    label = lax.broadcasted_iota(jnp.int32, (groups, tokens), 0)
    held = label == ids_ref[...]
    held_bf = jnp.where(held, 1.0, 0.0).astype(bf16)
    counts = []
    for c in range(tokens // 256):
        before = lax.broadcasted_iota(jnp.int32, (tokens, 256), 0) < (
            lax.broadcasted_iota(jnp.int32, (tokens, 256), 1) + c * 256
        )
        counts.append(
            jnp.dot(held_bf, jnp.where(before, 1.0, 0.0).astype(bf16), preferred_element_type=f32)
        )
    count = jnp.concatenate(counts, axis=1)
    rank = jnp.sum(
        jnp.where(held, count + (label * block).astype(f32), 0.0), axis=0, keepdims=True
    ).astype(jnp.int32)

    def place(c, _):
        at = pl.multiple_of(c * step, step)
        pick = (lax.broadcasted_iota(jnp.int32, (step, tokens), 0) + at) == rank
        pick = jnp.where(pick, 1.0, 0.0).astype(bf16)
        own_ref[pl.ds(at, step), :] = pick[:, :local]
        rest_ref[pl.ds(at, step), :] = pick[:, local:]
        return 0

    lax.fori_loop(0, tokens // step, place, 0)


def pick_tokens(ids, local, groups):
    tokens = ids.shape[0]
    return pl.pallas_call(
        functools.partial(pick_kernel, groups),
        out_shape=(
            jax.ShapeDtypeStruct((tokens, local), bf16),
            jax.ShapeDtypeStruct((tokens, tokens - local), bf16),
        ),
        compiler_params=params(),
        cost_estimate=cost(32 * tokens * tokens, 2 * tokens * tokens),
        name="pick_tokens",
    )(ids.reshape(1, tokens))


def back_kernel(groups, ids_ref, back_ref):
    tokens = back_ref.shape[0]
    block = tokens // groups
    step = 128
    lane = lax.broadcasted_iota(jnp.int32, (tokens, 128), 1)
    held = jnp.where(lane == ids_ref[...], 1.0, 0.0).astype(bf16)

    def place(c, _):
        at = pl.multiple_of(c * step, step)
        before = lax.broadcasted_iota(jnp.int32, (step, tokens), 1) < (
            lax.broadcasted_iota(jnp.int32, (step, tokens), 0) + at
        )
        count = jnp.dot(
            jnp.where(before, 1.0, 0.0).astype(bf16), held, preferred_element_type=f32
        )
        lane = lax.broadcasted_iota(jnp.int32, (step, 128), 1)
        mine = lane == ids_ref[pl.ds(at, step), :]
        rank = jnp.sum(
            jnp.where(mine, count + (lane * block).astype(f32), 0.0), axis=1, keepdims=True
        ).astype(jnp.int32)
        pick = lax.broadcasted_iota(jnp.int32, (step, tokens), 1) == rank
        back_ref[pl.ds(at, step), :] = jnp.where(pick, 1.0, 0.0).astype(bf16)
        return 0

    lax.fori_loop(0, tokens // step, place, 0)


def back_tokens(ids, groups):
    tokens = ids.shape[0]
    return pl.pallas_call(
        functools.partial(back_kernel, groups),
        out_shape=jax.ShapeDtypeStruct((tokens, tokens), bf16),
        compiler_params=params(),
        cost_estimate=cost(256 * tokens * tokens, 2 * tokens * tokens),
        name="back_tokens",
    )(ids.reshape(tokens, 1))


def place_kernel(merge, *refs):
    pick_ref, frame_refs = refs[0], refs[1 : 1 + merge]
    x_ref, pick, raw, normed, x, sems = refs[1 + merge :]
    copies = Copies(sems)
    local = raw.shape[1]
    tokens = pick.shape[0]
    step = 256
    arriving = [copies.start(ref, raw.at[s]) for s, ref in enumerate(frame_refs)]
    picking = copies.start(pick_ref, pick)
    leaving = []
    for s in range(merge):
        arriving[s].wait()
        normalise(raw.at[s], normed, 0)
        if s == 0:
            picking.wait()
        for at in range(0, tokens, step):
            there = slice(s * tokens + at, s * tokens + at + step)
            x[there, :] = jnp.dot(
                pick[at : at + step, :], normed[...], preferred_element_type=f32
            ).astype(bf16)
            leaving.append(copies.start(x.at[there], x_ref.at[there]))
    finish(leaving)


def place_tokens(plan, pick, frames):
    tokens, count = pick.shape
    width = frames[0].shape[1]
    every = plan.merge * tokens
    any_space = pl.BlockSpec(memory_space=pl.ANY)
    return pl.pallas_call(
        functools.partial(place_kernel, plan.merge),
        in_specs=[any_space] * (1 + len(frames)),
        out_specs=any_space,
        out_shape=jax.ShapeDtypeStruct((every, width), bf16),
        scratch_shapes=[
            pltpu.VMEM((tokens, count), bf16),
            pltpu.VMEM((plan.merge, count, width), bf16),
            pltpu.VMEM((count, width), bf16),
            pltpu.VMEM((every, width), bf16),
            Copies.scratch(),
        ],
        compiler_params=params(),
        cost_estimate=cost(4 * every * count * width, 6 * tokens * width),
        name="place_tokens",
    )(pick, *frames)


def update_kernel(plan, groups, parts, *refs):
    decay_refs, refs = refs[: plan.merge], refs[plan.merge :]
    part_ref, rest_ref, refs = refs[0], refs[1], refs[2:]
    frame_refs, refs = refs[: plan.merge * parts], refs[plan.merge * parts :]
    w_refs, refs = refs[:-13], refs[-13:]
    x_out, v_out, u_out, total_ref, rest, raw, normed, w, x, v, b, u, sems = refs
    copies = Copies(sems)
    tokens = rest.shape[0]
    block = tokens // groups
    step = 256
    here = step // block
    many = here * plan.pairs * N

    arriving = []
    for s in range(plan.merge):
        at = 0
        for ref in frame_refs[s * parts : (s + 1) * parts]:
            size = ref.shape[0]
            arriving.append(copies.start(ref, raw.at[s, at : at + size, :]))
            at += size
    picking = [copies.start(rest_ref, rest), copies.start(part_ref, x)]
    weights = plan.gather(copies, w_refs, w, slice(0, w.shape[1]))

    leaving = []
    for s in range(plan.merge):
        finish(arriving[s * parts : (s + 1) * parts])
        normalise(raw.at[s], normed, 0)
        if s == 0:
            finish(picking)
        for at in range(0, tokens, step):
            there = slice(s * tokens + at, s * tokens + at + step)
            more = jnp.dot(rest[at : at + step, :], normed[...], preferred_element_type=f32)
            x[there, :] = x[there, :] + more.astype(bf16)
            leaving.append(copies.start(x.at[there], x_out.at[there]))
    finish(weights)

    def project(c, _):
        at = pl.ds(pl.multiple_of(c * step, step), step)
        both = jnp.dot(x[at, :], w[...], preferred_element_type=f32).astype(bf16)
        for p in range(plan.pairs):
            cols = slice(p * LANES, (p + 1) * LANES)
            v[at, cols] = both[:, 2 * p * LANES : (2 * p + 1) * LANES]
            b[at, cols] = both[:, (2 * p + 1) * LANES : (2 * p + 2) * LANES]
        return 0

    lax.fori_loop(0, plan.merge * tokens // step, project, 0)
    leaving.append(copies.start(v, v_out))

    for s in range(plan.merge):
        for p in range(plan.pairs):
            cols = slice(p * LANES, (p + 1) * LANES)
            for g in range(0, groups, 2):
                rows = slice(s * tokens + g * block, s * tokens + (g + 2) * block)
                turned = b[rows, cols].astype(f32).T
                half = lax.broadcasted_iota(jnp.int32, turned.shape, 1) < block
                wide = jnp.concatenate(
                    [jnp.where(half, turned, 0.0), jnp.where(half, 0.0, turned)], axis=0
                ).astype(bf16)
                outer = jnp.dot(wide, v[rows, cols], preferred_element_type=f32)
                for n in range(2):
                    m = outer[n * 2 * N : (n + 1) * 2 * N]
                    at = ((g + n) * plan.pairs + p) * N
                    u[s, at : at + N, :] = halves((N, LANES), m[:N], m[N:])
        leaving.append(copies.start(u.at[s], u_out.at[s]))

    peers = total_ref.shape[0]
    share = u.shape[1] // peers
    items = max(1, share // N)
    size = min(N, share)
    first = plan.core() == 0
    for d in range(peers):
        for i in range(items):
            row = d * share + i * N
            p, g = row // N % plan.pairs, row // N // plan.pairs
            last = plan.last_decay(decay_refs, p, g)
            total = u[plan.merge - 1, row : row + size, :]
            product = last
            if plan.merge == 2:
                before = u[0, row : row + size, :]
                total = jnp.where(first, last, 1.0) * before + jnp.where(first, 1.0, last) * total
                product = plan.decay(decay_refs, 0, p, g) * plan.decay(decay_refs, 1, p, g)
            total_ref[d, i * size : (i + 1) * size, :] = total.astype(bf16)
            for n in range(3):
                piece = product.astype(bf16)
                at = share + n * items + i
                total_ref[d, at : at + 1, :] = piece
                product = product - piece.astype(f32)
    finish(leaving)


def share_rows(share):
    return share + 16 * -(-3 * max(1, share // N) // 16)


def project_updates(plan, decays, part, rest, frames, weights, groups):
    every, width = part.shape
    tokens, count = rest.shape
    cols = plan.pairs * LANES
    rows = plan.pairs * groups * N
    share = rows // plan.chips
    any_space = pl.BlockSpec(memory_space=pl.ANY)
    return pl.pallas_call(
        functools.partial(update_kernel, plan, groups, len(frames) // plan.merge),
        in_specs=[pl.BlockSpec(memory_space=pltpu.SMEM)] * plan.merge
        + [any_space] * (2 + len(frames) + len(weights)),
        out_specs=(any_space,) * 3 + (pl.BlockSpec(memory_space=pltpu.VMEM),),
        out_shape=(
            jax.ShapeDtypeStruct((every, width), bf16),
            jax.ShapeDtypeStruct((every, cols), bf16),
            jax.ShapeDtypeStruct((plan.merge, rows, LANES), f32),
            jax.ShapeDtypeStruct((plan.chips, share_rows(share), LANES), bf16),
        ),
        scratch_shapes=[
            pltpu.VMEM((tokens, count), bf16),
            pltpu.VMEM((plan.merge, count, width), bf16),
            pltpu.VMEM((count, width), bf16),
            pltpu.VMEM((width, 2 * cols), bf16),
            pltpu.VMEM((every, width), bf16),
            pltpu.VMEM((every, cols), bf16),
            pltpu.VMEM((every, cols), bf16),
            pltpu.VMEM((plan.merge, rows, LANES), f32),
            Copies.scratch(),
        ],
        compiler_params=params(),
        cost_estimate=cost(4 * every * width * (2 * cols + count), 6 * every * width),
        name="project_updates",
    )(*decays, part, rest, *frames, *weights)


def scan_kernel(plan, u_ref, s_ref):
    share = s_ref.shape[1]
    size = min(share, N)
    items = share // size
    for i in range(items):
        at = slice(i * size, (i + 1) * size)
        state = jnp.zeros((size, LANES), f32)
        for j in range(plan.chips):
            s_ref[j, at, :] = state.astype(bf16)
            decay = jnp.zeros((1, LANES), f32)
            for n in range(3):
                row = share + n * items + i
                decay = decay + u_ref[j, row : row + 1, :].astype(f32)
            state = decay * state + u_ref[j, at, :].astype(f32)


def scan_states(plan, update, share):
    return pl.pallas_call(
        functools.partial(scan_kernel, plan),
        out_shape=jax.ShapeDtypeStruct((plan.chips, share, LANES), bf16),
        compiler_params=params(24),
        cost_estimate=cost(2 * update.size, 4 * update.size),
        name="scan_states",
    )(update)


def attend_kernel(plan, slot, *refs):
    lists_ref, refs = refs[0], refs[1:]
    decay_refs, refs = refs[: plan.merge], refs[plan.merge :]
    x_in, v_in, u_in, w_refs, refs = refs[0], refs[1], refs[2], refs[3:-11], refs[-11:]
    a_out, c_out, x, v, u, w, q_ref, k_ref, a, c_ref, sems = refs
    copies = Copies(sems)
    tokens = x.shape[0]
    groups, chosen = lists_ref.shape
    block = tokens // groups
    step = 256
    per = step // block
    early = 2 * plan.pairs * LANES
    mine = slice(slot * tokens, (slot + 1) * tokens)

    weights = plan.gather(copies, w_refs, w, slice(early, early + w.shape[1]))
    arriving = []
    for at in range(0, tokens, step):
        from_ = slice(slot * tokens + at, slot * tokens + at + step)
        arriving.append(copies.start(x_in.at[from_], x.at[at : at + step]))
    later = [copies.start(v_in.at[mine], v), copies.start(u_in, u)]

    half = first_half((step, LANES))

    def head_norm(wide):
        square = wide * wide
        one = jnp.sum(jnp.where(half, square, 0.0), axis=-1, keepdims=True)
        two = jnp.sum(jnp.where(half, 0.0, square), axis=-1, keepdims=True)
        return wide * lax.rsqrt(jnp.where(half, one, two) * (1.0 / HD) + epsilon)

    finish(weights)
    for at in range(0, tokens, step):
        arriving[at // step].wait()
        rows = slice(at, at + step)
        every = jnp.dot(x[rows, :], w[...], preferred_element_type=f32).astype(bf16)
        for p in range(plan.pairs):
            cols = slice(p * LANES, (p + 1) * LANES)
            q, k, reader = (
                every[:, (3 * p + i) * LANES : (3 * p + i + 1) * LANES] for i in range(3)
            )
            c_ref[rows, cols] = reader
            k_ref[rows, cols] = head_norm(k.astype(f32)).astype(bf16)
            q = head_norm(q.astype(f32))
            one = jnp.where(half, q, 0.0).astype(bf16)
            two = jnp.where(half, 0.0, q).astype(bf16)
            for i in range(per):
                part = slice(i * block, (i + 1) * block)
                q_ref[p, at // block + i] = jnp.concatenate([one[part], two[part]], axis=0)
    leaving = [copies.start(c_ref, c_out)]
    finish(later)

    scale = math.log2(math.e) / math.sqrt(HD)
    for g in range(groups):
        rows = slice(g * block, (g + 1) * block)
        starts = [pl.multiple_of(lists_ref[g, j] * block, block) for j in range(chosen)]
        for p in range(plan.pairs):
            cols = slice(p * LANES, (p + 1) * LANES)
            keys = jnp.concatenate([k_ref[pl.ds(s, block), cols] for s in starts], axis=0)
            values = jnp.concatenate([v[pl.ds(s, block), cols] for s in starts], axis=0)
            score = lax.dot_general(
                q_ref[p, g], keys, (((1,), (1,)), ((), ())), preferred_element_type=f32
            )
            e = jnp.exp2(score * scale)
            weight = (e * (1.0 / jnp.sum(e, axis=-1, keepdims=True))).astype(bf16)
            both = jnp.dot(weight, values, preferred_element_type=f32)
            attended = halves((block, LANES), both[:block], both[block:])
            items = slice((g * plan.pairs + p) * N, (g * plan.pairs + p + 1) * N)
            state = u[slot, items, :]
            if plan.merge == 2:
                last = plan.last_decay(decay_refs, p, g)
                last = jnp.where(plan.core() == slot, 0.0, last)
                state = state + last * u[1 - slot, items, :]
            a[rows, cols] = attended + read_out(c_ref[rows, cols], state, block)
        if (g + 1) % per == 0:
            done = slice((g + 1 - per) * block, (g + 1) * block)
            leaving.append(copies.start(a.at[done], a_out.at[done]))
    finish(leaving)


def attend(plan, slot, lists, decays, x, v, weights, updates):
    every, width = x.shape
    groups, chosen = lists.shape
    tokens = every // plan.merge
    block = tokens // groups
    cols = plan.pairs * LANES
    any_space = pl.BlockSpec(memory_space=pl.ANY)
    return pl.pallas_call(
        functools.partial(attend_kernel, plan, slot),
        in_specs=[pl.BlockSpec(memory_space=pltpu.SMEM)] * (1 + plan.merge)
        + [any_space] * (3 + len(weights)),
        out_specs=(any_space,) * 2,
        scratch_shapes=[
            pltpu.VMEM((tokens, width), bf16),
            pltpu.VMEM((tokens, cols), bf16),
            pltpu.VMEM(updates.shape, f32),
            pltpu.VMEM((width, 3 * cols), bf16),
            pltpu.VMEM((plan.pairs, groups, 2 * block, LANES), bf16),
            pltpu.VMEM((tokens, cols), bf16),
            pltpu.VMEM((tokens, cols), f32),
            pltpu.VMEM((tokens, cols), bf16),
            Copies.scratch(),
        ],
        out_shape=(
            jax.ShapeDtypeStruct((tokens, cols), f32),
            jax.ShapeDtypeStruct((tokens, cols), bf16),
        ),
        compiler_params=params(),
        cost_estimate=cost(
            6 * tokens * width * 3 * cols,
            4 * (tokens * width + 5 * width * cols + updates.size),
            2 * plan.pairs * tokens * chosen * block,
        ),
        name="attend",
    )(lists, *decays, x, v, updates, *weights)


def read_out(readers, state, block):
    half = first_half(state.shape)
    wide = jnp.concatenate([jnp.where(half, state, 0.0), jnp.where(half, 0.0, state)], axis=0)
    return jnp.dot(readers, wide.astype(bf16), preferred_element_type=f32) * (
        1.0 / (N * math.sqrt(block))
    )


def mix_kernel(plan, groups, *refs):
    decay_refs, refs = refs[: plan.merge], refs[plan.merge :]
    a_ins, refs = refs[: plan.merge], refs[plan.merge :]
    c_ins, refs = refs[: plan.merge], refs[plan.merge :]
    s_in, back_in, refs = refs[0], refs[1], refs[2:]
    out_refs, (a, c, state, back, mixed, sems) = refs[:-6], refs[-6:]
    copies = Copies(sems)
    tokens = back.shape[0]
    block = tokens // groups
    width = a.shape[2]
    here = groups // 4
    step = here * block
    many = here * plan.pairs * N
    first = plan.core() == 0

    arriving = []
    for i in range(4):
        rows = slice(i * step, (i + 1) * step)
        items = slice(i * many, (i + 1) * many)
        arriving.append([copies.start(s_in.at[items], state.at[items])])
        for s in range(plan.merge):
            arriving[-1] += [
                copies.start(a_ins[s].at[rows], a.at[s, rows, :]),
                copies.start(c_ins[s].at[rows], c.at[s, rows, :]),
            ]
    local = tokens // plan.peers
    turning = [
        copies.start(back_in.at[k * local : (k + 1) * local], back.at[k * local : (k + 1) * local])
        for k in range(plan.peers)
    ]

    for g in range(groups):
        if g % here == 0:
            finish(arriving[g // here])
        rows = slice(g * block, (g + 1) * block)
        for p in range(plan.pairs):
            cols = slice(p * LANES, (p + 1) * LANES)
            at = (g * plan.pairs + p) * N
            readers = jnp.concatenate([c[s, rows, cols] for s in range(plan.merge)], axis=0)
            read = read_out(readers, state[at : at + N, :].astype(f32), block)
            decays = [plan.decay(decay_refs, s, p, g) for s in range(plan.merge)]
            if plan.merge == 2:
                both = decays[0] * decays[1]
                decays = [jnp.where(first, decays[0], both), jnp.where(first, both, decays[1])]
            for s in range(plan.merge):
                there = slice(s * width + p * LANES, s * width + (p + 1) * LANES)
                mixed[rows, there] = (
                    a[s, rows, cols] + decays[s] * read[s * block : (s + 1) * block]
                ).astype(bf16)

    for k in range(plan.peers):
        turning[k].wait()
        placed = jnp.dot(
            back[k * local : (k + 1) * local, :], mixed[...], preferred_element_type=f32
        ).astype(bf16)
        for s in range(plan.merge):
            out_refs[s * plan.peers + k][...] = placed[:, s * width : (s + 1) * width]


def mix(plan, decays, attended, readers, state, back, groups):
    tokens = back.shape[0]
    width = attended[0].shape[1]
    local = tokens // plan.peers
    count = plan.merge * plan.peers
    any_space = pl.BlockSpec(memory_space=pl.ANY)
    return pl.pallas_call(
        functools.partial(mix_kernel, plan, groups),
        in_specs=[pl.BlockSpec(memory_space=pltpu.SMEM)] * plan.merge
        + [any_space] * (2 * plan.merge + 2),
        out_specs=(pl.BlockSpec(memory_space=pltpu.VMEM),) * count,
        out_shape=(jax.ShapeDtypeStruct((local, width), bf16),) * count,
        scratch_shapes=[
            pltpu.VMEM((plan.merge, tokens, width), f32),
            pltpu.VMEM((plan.merge, tokens, width), bf16),
            pltpu.VMEM(state.shape, bf16),
            pltpu.VMEM((tokens, tokens), bf16),
            pltpu.VMEM((tokens, plan.merge * width), bf16),
            Copies.scratch(),
        ],
        compiler_params=params(),
        cost_estimate=cost(4 * tokens * tokens * width, 2 * tokens * tokens + 16 * tokens * width),
        name="mix",
    )(*decays, *attended, *readers, state, back)


def out_kernel(plan, w_ref, *refs):
    part_refs, out_ref = refs[:-1], refs[-1]
    depth = part_refs[0].shape[1]
    core, me = plan.core(), lax.axis_index("head")
    total = None
    for s in range(plan.merge):
        for k in range(plan.peers):
            owner = lax.rem(me - k + plan.peers, plan.peers) * plan.merge
            owner = owner + (core if s == 0 else 1 - core)
            rows = pl.ds(pl.multiple_of(owner * depth, depth), depth)
            term = jnp.dot(
                part_refs[s * plan.peers + k][...], w_ref[rows, :], preferred_element_type=f32
            )
            total = term if total is None else total + term
    out_ref[...] = total.astype(bf16)


def project_out(plan, w, parts):
    local = parts[0].shape[0]
    width = w.shape[1]
    return pl.pallas_call(
        functools.partial(out_kernel, plan),
        out_shape=jax.ShapeDtypeStruct((local, width), bf16),
        compiler_params=params(24),
        cost_estimate=cost(2 * local * w.size, 2 * (w.size + 2 * local * width)),
        name="project_out",
    )(w, *parts)


def body(frames_in, in_weight, out_weight, block_ids, block_lists, decays):
    local_tokens = frames_in.shape[1]
    heads_here = decays.shape[1]
    groups = block_lists.shape[0]
    me = lax.axis_index("head")
    plan = Plan(lax.axis_size("tm"), lax.axis_size("head"), heads_here)

    own = frames_in[0]
    arriving = [plan.to_peer(own, plan.peers - k, False) for k in range(1, plan.peers)]
    owns = [own] + [plan.swap(own)] * (plan.merge - 1)
    rates = [decays[0]] + [plan.swap(decays[0])] * (plan.merge - 1)
    block = reorder(plan, [in_weight] + [plan.swap(in_weight)] * (plan.merge - 1))

    ids = jnp.roll(block_ids, -me * local_tokens)
    pick, rest = pick_tokens(ids, local_tokens, groups)
    part = place_tokens(plan, pick, owns)
    if plan.ringed:
        weights, beside = [], [pick, part]
        for k in range(plan.along):
            crossed = plan.cross(block)
            weights += [block, crossed]
            if k < plan.along - 1:
                block = plan.round(block)
                block, crossed, beside[:1] = lax.optimization_barrier((block, crossed, beside[:1]))
                weights[-1] = crossed
                beside = beside[1:]
                n = k - (plan.along - 1 - len(arriving))
                if 0 <= n < len(arriving):
                    arriving[n], block = lax.optimization_barrier((arriving[n], block))
    else:
        weights = [
            lax.all_gather(block, "tm", axis=0, tiled=True, axis_index_groups=plan.groups())
        ]
    if plan.merge == 2:
        arriving = arriving + [plan.swap(chunk) for chunk in arriving]
    x, v, updates, total = project_updates(plan, rates, part, rest, arriving, weights, groups)

    def exchange(blocks):
        return lax.all_to_all(
            blocks, "tm", split_axis=0, concat_axis=0, tiled=True,
            axis_index_groups=plan.groups(),
        )

    share = updates.shape[1] // plan.chips
    arrived = exchange(total)
    attended = [attend(plan, 0, block_lists, rates, x, v, weights, updates)]
    arrived, attended = lax.optimization_barrier((arrived, attended))
    states = scan_states(plan, arrived, share)
    x, states = lax.optimization_barrier((x, states))
    if plan.merge == 2:
        attended.append(attend(plan, 1, block_lists, rates, x, v, weights, updates))
    state = exchange(states).reshape(-1, LANES)
    ids, attended = lax.optimization_barrier((ids, attended))
    back = back_tokens(ids, groups)

    bases, readers = ([a[i] for a in attended] for i in range(2))
    mixed = mix(plan, rates, bases, readers, state, back, groups)
    features = [
        mixed[0] if s == 0 and k == 0 else plan.to_peer(mixed[s * plan.peers + k], k, s == 1)
        for s in range(plan.merge)
        for k in range(plan.peers)
    ]
    return project_out(plan, out_weight, features)[None]


def solution(mesh):
    return jax.shard_map(
        body,
        mesh=mesh,
        in_specs=(P("tm", "head", None), P("tm", "head"), P(), P(), P(), P("tm", "head", None)),
        out_specs=P("tm", "head", None),
        check_vma=False,
    )
```

time: 134 us -> 136 us (1.015)
  waiting for transfers between devices: 17.2 us -> 35 us
  Pallas kernels: 79.7 us -> 69.1 us
  local copies, waits for them, and re-layouts: 9.51 us -> 6.23 us
  starting transfers between devices: 25.5 us -> 23.3 us
    pallas_call x6 -> x5, Pallas kernels: 66.7 us -> 56 us  [the longest x2 29.7 us: attend(): pl.pallas_call(functools.partial(attend_kernel, plan, slot), in_specs=[pl...]
    ppermute x3, waiting for transfers between devices: 3.97 us -> 13.4 us  [round(): return lax.ppermute(block, 'tm', pairs)]
    ppermute x4, waiting for transfers between devices: 0.01 us -> 7.48 us  [cross(): return lax.ppermute(block, 'tm', pairs)]
    unnamed x39 -> x37, local copies, waits for them, and re-layouts: 7.22 us -> 5.2 us
    ppermute x6 -> x5, waiting for transfers between devices: 2.92 us -> 4.37 us  [swap(): return lax.ppermute(block, 'tm', [(t, t ^ 1) for t in range(self.frames)])]
    ppermute x3, starting transfers between devices: 5.64 us -> 4.23 us  [round(): return lax.ppermute(block, 'tm', pairs)]
    ppermute x3 -> x2, starting transfers between devices: 3.68 us -> 3.02 us  [to_peer(): return lax.ppermute(block, 'head', pairs)]
    ppermute x3 -> x2, waiting for transfers between devices: 7.32 us -> 7.31 us  [to_peer(): return lax.ppermute(block, 'head', pairs)]
  transfers between devices with their start and end apart: 19 -> 17, of which waited for: 5 -> 8; matrix products, arithmetic and copies ran while one was open for 3% -> 2% of each run, Pallas kernels for 44% -> 34%
where the time goes in v5:
time: 136 us; the launch traced here: 135 us
  Pallas kernels  69.1 us (51%)
  waiting for transfers between devices  35 us (26%)
  starting transfers between devices  23.3 us (17%)
  local copies, waits for them, and re-layouts  6.23 us (5%)
    pallas_call x2, Pallas kernels, attend(): pl.pallas_call(functools.partial(attend_kernel, plan, slot), in_specs=[pl...  29.7 us
    pallas_call x1, Pallas kernels, project_updates(): pl.pallas_call(functools.partial(update_kernel, plan, groups, len(frames)...  14 us
    ppermute x3, waiting for transfers between devices, round(): return lax.ppermute(block, 'tm', pairs)  13.4 us
    all_to_all x2, starting transfers between devices, exchange(): lax.all_to_all(blocks, 'tm', split_axis=0, concat_axis=0, tiled=True, axi...  9.48 us
    ppermute x4, waiting for transfers between devices, cross(): return lax.ppermute(block, 'tm', pairs)  7.48 us
    ppermute x2, waiting for transfers between devices, to_peer(): return lax.ppermute(block, 'head', pairs)  7.31 us
    pallas_call x1, Pallas kernels, place_tokens(): pl.pallas_call(functools.partial(place_kernel, plan.merge), in_specs=[any...  6.21 us
    pallas_call x1, Pallas kernels, mix(): pl.pallas_call(functools.partial(mix_kernel, plan, groups), in_specs=[pl....  6.04 us
  transfers between devices with their start and end apart: 17, of which 8 were waited for; matrix products, arithmetic and copies ran while one was open for 2% of the time, Pallas kernels for 34%

profile of v5, /device:TPU:0, one launch (start us, length us, event | category | flops | bytes accessed | tf_op | source)
XLA Modules:
  0.0 135.2 jit_solution(16527644238927457104)
XLA Ops:
  0.5 2.9 %collective-permute-done.3.refs_1_ = bf16[64,2560]{1,0:T(8,128)(2,1)S(1)} collective-permute-done((bf16[64,2560]{1,0:T(8,128)(2,1)}, bf16[64,2560]{1,0:T(8,128)(2,1)S(1)}, u32[]{:S(2)}, u32[]{:S(2)}) %collective-permute-start.3) | collective-permute-done | bytes 327712 | tf_op jit(solution)/shard_map/ppermute | solution.py:56
  4.1 2.0 %reorder.1.refs_6_ = bf16[128,1280]{1,0:T(8,128)(2,1)} custom-call(bf16[64,2560]{1,0:T(8,128)(2,1)} %refs_0_.3, bf16[64,2560]{1,0:T(8,128)(2,1)} %copy-done.3), custom_call_target="tpu_custom_call" | custom-call | bytes 655360 | tf_op jit(solution)/shard_map/reorder/pallas_call | solution.py:165
  6.1 2.9 %collective-permute-start.4 = (bf16[128,1280]{1,0:T(8,128)(2,1)}, bf16[128,1280]{1,0:T(8,128)(2,1)S(1)}, u32[]{:S(2)}, u32[]{:S(2)}) collective-permute-start(bf16[128,1280]{1,0:T(8,128)(2,1)} %reorder.1.refs_6_), channel_id=1, source_target_pairs={{0,8},{2,10},{4,12},{6,14},{8,16},{10,18},{12,20},{14,22},{16,24},... | collective-permute-start | bytes 983048 | tf_op jit(solution)/shard_map/ppermute | solution.py:61
  9.1 1.5 %collective-permute-start.5 = (bf16[128,1280]{1,0:T(8,128)(2,1)}, bf16[128,1280]{1,0:T(8,128)(2,1)S(1)}, u32[]{:S(2)}, u32[]{:S(2)}) collective-permute-start(bf16[128,1280]{1,0:T(8,128)(2,1)} %reorder.1.refs_6_), channel_id=1, source_target_pairs={{0,4},{2,6},{4,0},{6,2},{8,12},{10,14},{12,8},{14,10},{16,20},{18,... | collective-permute-start | bytes 983048 | tf_op jit(solution)/shard_map/ppermute | solution.py:66
  10.6 1.5 %collective-permute-start.2 = (bf16[512,1024]{1,0:T(8,128)(2,1)}, bf16[512,1024]{1,0:T(8,128)(2,1)S(1)}, u32[]{:S(2)}, u32[]{:S(2)}) collective-permute-start(bf16[512,1024]{1,0:T(8,128)(2,1)} %bitcast.15), channel_id=1, source_target_pairs={{0,1},{1,0},{2,3},{3,2},{4,5},{5,4},{6,7},{7,6},{8,9},{9,8},{10,11... | collective-permute-start | bytes 3145736 | tf_op jit(solution)/shard_map/ppermute | solution.py:84
  12.1 1.4 fusion
  13.4 2.7 %pick_tokens.1 = (bf16[1024,512]{1,0:T(8,128)(2,1)}, bf16[1024,512]{1,0:T(8,128)(2,1)}) custom-call(s32[1,1024]{1,0:T(1,128)} %bitcast.7), custom_call_target="tpu_custom_call" | custom-call | flops 33554432 | bytes 2097152 | tf_op jit(solution)/shard_map/pick_tokens/pallas_call | solution.py:221
  16.1 3.2 %collective-permute-done.4.refs_8_ = bf16[128,1280]{1,0:T(8,128)(2,1)S(1)} collective-permute-done((bf16[128,1280]{1,0:T(8,128)(2,1)}, bf16[128,1280]{1,0:T(8,128)(2,1)S(1)}, u32[]{:S(2)}, u32[]{:S(2)}) %collective-permute-start.4) | collective-permute-done | bytes 327712 | tf_op jit(solution)/shard_map/ppermute | solution.py:61
  19.3 1.0 collective-permute-start.6
  20.3 1.5 %collective-permute-start.7 = (bf16[128,1280]{1,0:T(8,128)(2,1)S(1)}, bf16[128,1280]{1,0:T(8,128)(2,1)S(1)}, u32[]{:S(2)}, u32[]{:S(2)}) collective-permute-start(bf16[128,1280]{1,0:T(8,128)(2,1)S(1)} %collective-permute-done.4.refs_8_), channel_id=1, source_target_pairs={{0,4},{2,6},{4,0},{6,2},{8,12},{10,14},{12,8},{14,10},{16,20},{18,... | collective-permute-start | bytes 983048 | tf_op jit(solution)/shard_map/ppermute | solution.py:66
  21.8 1.0 copy-done.9
  22.8 6.2 %place_tokens.1.refs_2_ = bf16[2048,1024]{1,0:T(8,128)(2,1)} custom-call(bf16[1024,512]{1,0:T(8,128)(2,1)} %get-tuple-element.37.refs_0_, bf16[512,1024]{1,0:T(8,128)(2,1)} %bitcast.16, bf16[512,1024]{1,0:T(8,128)(2,1)} %copy-done.9), custom_call_target="tpu_custom_call" | custom-call | flops 4294967296 | bytes 6291456 | tf_op jit(solution)/shard_map/place_tokens/pallas_call | solution.py:300
  29.0 1.4 %collective-permute-done.6.refs_10_ = bf16[128,1280]{1,0:T(8,128)(2,1)S(1)} collective-permute-done((bf16[128,1280]{1,0:T(8,128)(2,1)S(1)}, bf16[128,1280]{1,0:T(8,128)(2,1)S(1)}, u32[]{:S(2)}, u32[]{:S(2)}) %collective-permute-start.6) | collective-permute-done | bytes 327712 | tf_op jit(solution)/shard_map/ppermute | solution.py:61
  30.7 1.1 collective-permute-start.9
  31.8 8.8 %collective-permute-done.8.refs_12_ = bf16[128,1280]{1,0:T(8,128)(2,1)S(1)} collective-permute-done((bf16[128,1280]{1,0:T(8,128)(2,1)S(1)}, bf16[128,1280]{1,0:T(8,128)(2,1)S(1)}, u32[]{:S(2)}, u32[]{:S(2)}) %collective-permute-start.8) | collective-permute-done | bytes 327712 | tf_op jit(solution)/shard_map/ppermute | solution.py:61
  40.7 1.0 collective-permute-start.11
  41.9 1.5 %collective-permute-done.refs_1_.refs_2_ = f32[8,16]{1,0:T(8,128)S(1)} collective-permute-done((f32[8,16]{1,0:T(8,128)S(1)}, f32[8,16]{1,0:T(8,128)S(1)}, u32[]{:S(2)}, u32[]{:S(2)}) %collective-permute-start) | collective-permute-done | bytes 544 | tf_op jit(solution)/shard_map/ppermute | solution.py:56
  43.4 7.5 %collective-permute-done.11.refs_13_ = bf16[128,1280]{1,0:T(8,128)(2,1)S(1)} collective-permute-done((bf16[128,1280]{1,0:T(8,128)(2,1)S(1)}, bf16[128,1280]{1,0:T(8,128)(2,1)S(1)}, u32[]{:S(2)}, u32[]{:S(2)}) %collective-permute-start.11) | collective-permute-done | bytes 327712 | tf_op jit(solution)/shard_map/ppermute | solution.py:66
  51.9 14.0 %project_updates.1 = (bf16[2048,1024]{1,0:T(8,128)(2,1)}, bf16[2048,256]{1,0:T(8,128)(2,1)}, f32[2,2048,128]{2,1,0:T(8,128)}, bf16[8,272,128]{2,1,0:T(8,128)(2,1)}) custom-call(f32[8,16]{1,0:T(8,128)} %bitcast.9, f32[8,16]{1,0:T(8,128)} %copy-done.6, bf16[2048,1024]{1,0:T(8,128)(2,1)} %place_tokens.1.refs_2_, bf16[1024,512]{1,0:T(8,128)(2,1)} %get-tuple-element.38.refs_3_, ...), custom_call_target="tpu_custom_call" | custom-call | flops 8589934592 | bytes 12582912 | tf_op jit(solution)/shard_map/project_updates/pallas_call | solution.py:419
  66.0 3.7 %all-to-all-start = ((bf16[8,272,128]{2,1,0:T(8,128)(2,1)}), bf16[8,272,128]{2,1,0:T(8,128)(2,1)S(1)}, u32[]{:S(2)}, u32[]{:S(2)}) async-start(bf16[8,272,128]{2,1,0:T(8,128)(2,1)} %get-tuple-element.47), calls=%async_computation | async-start | bytes 1114112 | tf_op jit(solution)/shard_map/all_to_all | solution.py:748
  70.4 14.9 %attend.2 = (f32[1024,256]{1,0:T(8,128)}, bf16[1024,256]{1,0:T(8,128)(2,1)}) custom-call(s32[16,4]{1,0:T(8,128)} %copy.9.refs_0_, f32[8,16]{1,0:T(8,128)} %bitcast.10, f32[8,16]{1,0:T(8,128)} %copy-done.6, bf16[2048,1024]{1,0:T(8,128)(2,1)} %get-tuple-element.56.refs_3_, bf16[2048,256]{1,0:T(8,128)(2,1)} %get-tuple-element.49.refs_4_, ...), custom_call_target="tpu_custom_call" | custom-call | flops 4831838208 | bytes 11534336 | tf_op jit(solution)/shard_map/attend/pallas_call | solution.py:558
  85.3 0.9 scan_states.1
  86.2 5.7 %all-to-all-start.1 = ((bf16[8,256,128]{2,1,0:T(8,128)(2,1)}), bf16[8,256,128]{2,1,0:T(8,128)(2,1)S(1)}, u32[]{:S(2)}, u32[]{:S(2)}) async-start(bf16[8,256,128]{2,1,0:T(8,128)(2,1)} %scan_states.1), calls=%async_computation.1 | async-start | bytes 1048576 | tf_op jit(solution)/shard_map/all_to_all | solution.py:748
  92.0 14.9 %attend.3 = (f32[1024,256]{1,0:T(8,128)}, bf16[1024,256]{1,0:T(8,128)(2,1)}) custom-call(s32[16,4]{1,0:T(8,128)} %copy.9.refs_0_, f32[8,16]{1,0:T(8,128)} %bitcast.11, f32[8,16]{1,0:T(8,128)} %copy-done.6, bf16[2048,1024]{1,0:T(8,128)(2,1)} %get-tuple-element.56.refs_3_, bf16[2048,256]{1,0:T(8,128)(2,1)} %get-tuple-element.49.refs_4_, ...), custom_call_target="tpu_custom_call" | custom-call | flops 4831838208 | bytes 11534336 | tf_op jit(solution)/shard_map/attend/pallas_call | solution.py:558
  106.9 1.0 copy.11.ids_ref
  107.9 5.3 %back_tokens.1.refs_7_ = bf16[1024,1024]{1,0:T(8,128)(2,1)} custom-call(s32[1024,1]{1,0:T(8,128)} %copy.11.ids_ref), custom_call_target="tpu_custom_call" | custom-call | flops 268435456 | bytes 2097152 | tf_op jit(solution)/shard_map/back_tokens/pallas_call | solution.py:262
  114.0 6.0 %mix.1 = (bf16[512,256]{1,0:T(8,128)(2,1)}, bf16[512,256]{1,0:T(8,128)(2,1)}, bf16[512,256]{1,0:T(8,128)(2,1)}, bf16[512,256]{1,0:T(8,128)(2,1)}) custom-call(f32[8,16]{1,0:T(8,128)} %bitcast.12, f32[8,16]{1,0:T(8,128)} %copy-done.6, f32[1024,256]{1,0:T(8,128)} %get-tuple-element.59.refs_2_, f32[1024,256]{1,0:T(8,128)} %get-tuple-element.60.refs_3_, ...), custom_call_target="tpu_custom_call" | custom-call | flops 1073741824 | bytes 6291456 | tf_op jit(solution)/shard_map/mix/pallas_call | solution.py:661
  120.0 1.5 %collective-permute-start.12 = (bf16[512,256]{1,0:T(8,128)(2,1)}, bf16[512,256]{1,0:T(8,128)(2,1)S(1)}, u32[]{:S(2)}, u32[]{:S(2)}) collective-permute-start(bf16[512,256]{1,0:T(8,128)(2,1)} %get-tuple-element.66), channel_id=1, source_target_pairs={{0,1},{1,0},{2,3},{3,2},{4,5},{5,4},{6,7},{7,6},{8,9},{9,8},{10,11... | collective-permute-start | bytes 786440 | tf_op jit(solution)/shard_map/ppermute | solution.py:84
  122.2 7.3 %collective-permute-done.12.refs_1_ = bf16[512,256]{1,0:T(8,128)(2,1)S(1)} collective-permute-done((bf16[512,256]{1,0:T(8,128)(2,1)}, bf16[512,256]{1,0:T(8,128)(2,1)S(1)}, u32[]{:S(2)}, u32[]{:S(2)}) %collective-permute-start.12) | collective-permute-done | bytes 262176 | tf_op jit(solution)/shard_map/ppermute | solution.py:84
  129.5 2.5 %collective-permute-done.14.refs_3_ = bf16[512,256]{1,0:T(8,128)(2,1)S(1)} collective-permute-done((bf16[512,256]{1,0:T(8,128)(2,1)}, bf16[512,256]{1,0:T(8,128)(2,1)S(1)}, u32[]{:S(2)}, u32[]{:S(2)}) %collective-permute-start.14) | collective-permute-done | bytes 262176 | tf_op jit(solution)/shard_map/ppermute | solution.py:92
  132.0 0.9 copy-done.1
  133.0 2.2 %project_out.1 = bf16[512,1024]{1,0:T(8,128)(2,1)} custom-call(bf16[1024,1024]{1,0:T(8,128)(2,1)S(1)} %copy-done, bf16[512,256]{1,0:T(8,128)(2,1)S(1)} %copy-done.1, bf16[512,256]{1,0:T(8,128)(2,1)S(1)} %collective-permute-done.12.refs_1_, bf16[512,256]{1,0:T(8,128)(2,1)S(1)} %collective-permute-done.13.refs_2_, ...), custom_call_target="tpu_custom_call" | custom-call | flops 1073741824 | bytes 4194304 | tf_op jit(solution)/shard_map/project_out/pallas_call | solution.py:701
  (51 shorter events, 5.0 us)
Async XLA Ops:
  0.0 21.8 %collective-permute-start.1 = (bf16[512,1024]{1,0:T(8,128)(2,1)}, bf16[512,1024]{1,0:T(8,128)(2,1)S(1)}, u32[]{:S(2)}, u32[]{:S(2)}) collective-permute-start(bf16[512,1024]{1,0:T(8,128)(2,1)} %bitcast.14), channel_id=1, source_target_pairs={{0,2},{2,0},{4,6},{6,4},{8,10},{10,8},{12,14},{14,12},{16,18},{18,... | collective-permute-start | bytes 3145736 | tf_op jit(solution)/shard_map/ppermute | solution.py:56
  0.5 3.0 %collective-permute-start.3 = (bf16[64,2560]{1,0:T(8,128)(2,1)}, bf16[64,2560]{1,0:T(8,128)(2,1)S(1)}, u32[]{:S(2)}, u32[]{:S(2)}) collective-permute-start(bf16[64,2560]{1,0:T(8,128)(2,1)} %refs_0_.3), channel_id=1, source_target_pairs={{0,2},{2,0},{4,6},{6,4},{8,10},{10,8},{12,14},{14,12},{16,18},{18,... | collective-permute-start | bytes 983048 | tf_op jit(solution)/shard_map/ppermute | solution.py:56
  6.1 13.2 %collective-permute-start.4 = (bf16[128,1280]{1,0:T(8,128)(2,1)}, bf16[128,1280]{1,0:T(8,128)(2,1)S(1)}, u32[]{:S(2)}, u32[]{:S(2)}) collective-permute-start(bf16[128,1280]{1,0:T(8,128)(2,1)} %reorder.1.refs_6_), channel_id=1, source_target_pairs={{0,8},{2,10},{4,12},{6,14},{8,16},{10,18},{12,20},{14,22},{16,24},... | collective-permute-start | bytes 983048 | tf_op jit(solution)/shard_map/ppermute | solution.py:61
  9.1 10.2 %collective-permute-start.5 = (bf16[128,1280]{1,0:T(8,128)(2,1)}, bf16[128,1280]{1,0:T(8,128)(2,1)S(1)}, u32[]{:S(2)}, u32[]{:S(2)}) collective-permute-start(bf16[128,1280]{1,0:T(8,128)(2,1)} %reorder.1.refs_6_), channel_id=1, source_target_pairs={{0,4},{2,6},{4,0},{6,2},{8,12},{10,14},{12,8},{14,10},{16,20},{18,... | collective-permute-start | bytes 983048 | tf_op jit(solution)/shard_map/ppermute | solution.py:66
  10.6 30.1 %collective-permute-start.2 = (bf16[512,1024]{1,0:T(8,128)(2,1)}, bf16[512,1024]{1,0:T(8,128)(2,1)S(1)}, u32[]{:S(2)}, u32[]{:S(2)}) collective-permute-start(bf16[512,1024]{1,0:T(8,128)(2,1)} %bitcast.15), channel_id=1, source_target_pairs={{0,1},{1,0},{2,3},{3,2},{4,5},{5,4},{6,7},{7,6},{8,9},{9,8},{10,11... | collective-permute-start | bytes 3145736 | tf_op jit(solution)/shard_map/ppermute | solution.py:84
  19.3 9.7 %copy-start.11 = (bf16[128,1280]{1,0:T(8,128)(2,1)}, bf16[128,1280]{1,0:T(8,128)(2,1)S(1)}, u32[]{:S(2)}) copy-start(bf16[128,1280]{1,0:T(8,128)(2,1)S(1)} %collective-permute-done.4.refs_8_) | copy-start | bytes 983044
  19.3 9.7 %copy-start.12 = (bf16[128,1280]{1,0:T(8,128)(2,1)}, bf16[128,1280]{1,0:T(8,128)(2,1)S(1)}, u32[]{:S(2)}) copy-start(bf16[128,1280]{1,0:T(8,128)(2,1)S(1)} %collective-permute-done.5.refs_7_) | copy-start | bytes 983044
  19.3 22.5 %copy-start.5 = (f32[1,8,16]{2,1,0:T(8,128)S(1)}, f32[1,8,16]{2,1,0:T(8,128)}, u32[]{:S(2)}) copy-start(f32[1,8,16]{2,1,0:T(8,128)} %param.11) | copy-start | bytes 1540
  19.3 11.1 %collective-permute-start.6 = (bf16[128,1280]{1,0:T(8,128)(2,1)S(1)}, bf16[128,1280]{1,0:T(8,128)(2,1)S(1)}, u32[]{:S(2)}, u32[]{:S(2)}) collective-permute-start(bf16[128,1280]{1,0:T(8,128)(2,1)S(1)} %collective-permute-done.4.refs_8_), channel_id=1, source_target_pairs={{0,8},{2,10},{4,12},{6,14},{8,16},{10,18},{12,20},{14,22},{16,24},... | collective-permute-start | bytes 983048 | tf_op jit(solution)/shard_map/ppermute | solution.py:61
  20.3 10.1 %collective-permute-start.7 = (bf16[128,1280]{1,0:T(8,128)(2,1)S(1)}, bf16[128,1280]{1,0:T(8,128)(2,1)S(1)}, u32[]{:S(2)}, u32[]{:S(2)}) collective-permute-start(bf16[128,1280]{1,0:T(8,128)(2,1)S(1)} %collective-permute-done.4.refs_8_), channel_id=1, source_target_pairs={{0,4},{2,6},{4,0},{6,2},{8,12},{10,14},{12,8},{14,10},{16,20},{18,... | collective-permute-start | bytes 983048 | tf_op jit(solution)/shard_map/ppermute | solution.py:66
  21.8 1.0 copy-start.9
  30.4 10.2 %copy-start.13 = (bf16[128,1280]{1,0:T(8,128)(2,1)}, bf16[128,1280]{1,0:T(8,128)(2,1)S(1)}, u32[]{:S(2)}) copy-start(bf16[128,1280]{1,0:T(8,128)(2,1)S(1)} %collective-permute-done.6.refs_10_) | copy-start | bytes 983044
  30.4 10.2 %copy-start.14 = (bf16[128,1280]{1,0:T(8,128)(2,1)}, bf16[128,1280]{1,0:T(8,128)(2,1)S(1)}, u32[]{:S(2)}) copy-start(bf16[128,1280]{1,0:T(8,128)(2,1)S(1)} %collective-permute-done.7.refs_9_) | copy-start | bytes 983044
  30.4 10.2 %collective-permute-start.8 = (bf16[128,1280]{1,0:T(8,128)(2,1)S(1)}, bf16[128,1280]{1,0:T(8,128)(2,1)S(1)}, u32[]{:S(2)}, u32[]{:S(2)}) collective-permute-start(bf16[128,1280]{1,0:T(8,128)(2,1)S(1)} %collective-permute-done.6.refs_10_), channel_id=1, source_target_pairs={{0,8},{2,10},{4,12},{6,14},{8,16},{10,18},{12,20},{14,22},{16,24},... | collective-permute-start | bytes 983048 | tf_op jit(solution)/shard_map/ppermute | solution.py:61
  30.7 9.9 %collective-permute-start.9 = (bf16[128,1280]{1,0:T(8,128)(2,1)S(1)}, bf16[128,1280]{1,0:T(8,128)(2,1)S(1)}, u32[]{:S(2)}, u32[]{:S(2)}) collective-permute-start(bf16[128,1280]{1,0:T(8,128)(2,1)S(1)} %collective-permute-done.6.refs_10_), channel_id=1, source_target_pairs={{0,4},{2,6},{4,0},{6,2},{8,12},{10,14},{12,8},{14,10},{16,20},{18,... | collective-permute-start | bytes 983048 | tf_op jit(solution)/shard_map/ppermute | solution.py:66
  40.6 10.3 %copy-start.15 = (bf16[128,1280]{1,0:T(8,128)(2,1)}, bf16[128,1280]{1,0:T(8,128)(2,1)S(1)}, u32[]{:S(2)}) copy-start(bf16[128,1280]{1,0:T(8,128)(2,1)S(1)} %collective-permute-done.8.refs_12_) | copy-start | bytes 983044
  40.6 10.3 %copy-start.16 = (bf16[128,1280]{1,0:T(8,128)(2,1)}, bf16[128,1280]{1,0:T(8,128)(2,1)S(1)}, u32[]{:S(2)}) copy-start(bf16[128,1280]{1,0:T(8,128)(2,1)S(1)} %collective-permute-done.9.refs_11_) | copy-start | bytes 983044
  40.7 10.2 %copy-start.8 = (bf16[512,1024]{1,0:T(8,128)(2,1)}, bf16[512,1024]{1,0:T(8,128)(2,1)S(1)}, u32[]{:S(2)}) copy-start(bf16[512,1024]{1,0:T(8,128)(2,1)S(1)} %collective-permute-done.2.refs_4_) | copy-start | bytes 3145732
  40.7 10.2 %collective-permute-start.10 = (bf16[512,1024]{1,0:T(8,128)(2,1)S(1)}, bf16[512,1024]{1,0:T(8,128)(2,1)S(1)}, u32[]{:S(2)}, u32[]{:S(2)}) collective-permute-start(bf16[512,1024]{1,0:T(8,128)(2,1)S(1)} %collective-permute-done.2.refs_4_), channel_id=1, source_target_pairs={{0,2},{2,0},{4,6},{6,4},{8,10},{10,8},{12,14},{14,12},{16,18},{18,... | collective-permute-start | bytes 3145736 | tf_op jit(solution)/shard_map/ppermute | solution.py:56
  40.7 10.1 %collective-permute-start.11 = (bf16[128,1280]{1,0:T(8,128)(2,1)S(1)}, bf16[128,1280]{1,0:T(8,128)(2,1)S(1)}, u32[]{:S(2)}, u32[]{:S(2)}) collective-permute-start(bf16[128,1280]{1,0:T(8,128)(2,1)S(1)} %collective-permute-done.8.refs_12_), channel_id=1, source_target_pairs={{0,4},{2,6},{4,0},{6,2},{8,12},{10,14},{12,8},{14,10},{16,20},{18,... | collective-permute-start | bytes 983048 | tf_op jit(solution)/shard_map/ppermute | solution.py:66
  41.8 1.6 %collective-permute-start = (f32[8,16]{1,0:T(8,128)S(1)}, f32[8,16]{1,0:T(8,128)S(1)}, u32[]{:S(2)}, u32[]{:S(2)}) collective-permute-start(f32[8,16]{1,0:T(8,128)S(1)} %bitcast.13), channel_id=1, source_target_pairs={{0,2},{2,0},{4,6},{6,4},{8,10},{10,8},{12,14},{14,12},{16,18},{18,... | collective-permute-start | bytes 1544 | tf_op jit(solution)/shard_map/ppermute | solution.py:56
  43.4 7.5 %copy-start.6 = (f32[8,16]{1,0:T(8,128)}, f32[8,16]{1,0:T(8,128)S(1)}, u32[]{:S(2)}) copy-start(f32[8,16]{1,0:T(8,128)S(1)} %collective-permute-done.refs_1_.refs_2_) | copy-start | bytes 1540
  50.9 1.1 copy-start.10
  51.9 17.8 %copy-start.7 = (s32[16,4]{0,1:T(4,128)S(1)}, s32[16,4]{0,1:T(4,128)}, u32[]{:S(2)}) copy-start(s32[16,4]{0,1:T(4,128)} %param.10) | copy-start | bytes 772
  66.0 19.3 %all-to-all-start = ((bf16[8,272,128]{2,1,0:T(8,128)(2,1)}), bf16[8,272,128]{2,1,0:T(8,128)(2,1)S(1)}, u32[]{:S(2)}, u32[]{:S(2)}) async-start(bf16[8,272,128]{2,1,0:T(8,128)(2,1)} %get-tuple-element.47), calls=%async_computation | async-start | bytes 1114112 | tf_op jit(solution)/shard_map/all_to_all | solution.py:748
  86.2 26.9 %all-to-all-start.1 = ((bf16[8,256,128]{2,1,0:T(8,128)(2,1)}), bf16[8,256,128]{2,1,0:T(8,128)(2,1)S(1)}, u32[]{:S(2)}, u32[]{:S(2)}) async-start(bf16[8,256,128]{2,1,0:T(8,128)(2,1)} %scan_states.1), calls=%async_computation.1 | async-start | bytes 1048576 | tf_op jit(solution)/shard_map/all_to_all | solution.py:748
  92.0 14.9 %copy-start.4 = (s32[1024]{0:T(1024)S(1)}, s32[1024]{0:T(1024)}, u32[]{:S(2)}) copy-start(s32[1024]{0:T(1024)} %fusion) | copy-start | bytes 12292
  114.0 18.0 %copy-start = (bf16[1024,1024]{1,0:T(8,128)(2,1)S(1)}, bf16[1024,1024]{1,0:T(8,128)(2,1)}, u32[]{:S(2)}) copy-start(bf16[1024,1024]{1,0:T(8,128)(2,1)} %w_ref.1) | copy-start | bytes 6291460
  120.0 9.5 %collective-permute-start.12 = (bf16[512,256]{1,0:T(8,128)(2,1)}, bf16[512,256]{1,0:T(8,128)(2,1)S(1)}, u32[]{:S(2)}, u32[]{:S(2)}) collective-permute-start(bf16[512,256]{1,0:T(8,128)(2,1)} %get-tuple-element.66), channel_id=1, source_target_pairs={{0,1},{1,0},{2,3},{3,2},{4,5},{5,4},{6,7},{7,6},{8,9},{9,8},{10,11... | collective-permute-start | bytes 786440 | tf_op jit(solution)/shard_map/ppermute | solution.py:84
  121.5 8.0 %collective-permute-start.13 = (bf16[512,256]{1,0:T(8,128)(2,1)}, bf16[512,256]{1,0:T(8,128)(2,1)S(1)}, u32[]{:S(2)}, u32[]{:S(2)}) collective-permute-start(bf16[512,256]{1,0:T(8,128)(2,1)} %get-tuple-element.67), channel_id=1, source_target_pairs={{0,2},{2,0},{4,6},{6,4},{8,10},{10,8},{12,14},{14,12},{16,18},{18,... | collective-permute-start | bytes 786440 | tf_op jit(solution)/shard_map/ppermute | solution.py:56
  121.5 10.5 %collective-permute-start.14 = (bf16[512,256]{1,0:T(8,128)(2,1)}, bf16[512,256]{1,0:T(8,128)(2,1)S(1)}, u32[]{:S(2)}, u32[]{:S(2)}) collective-permute-start(bf16[512,256]{1,0:T(8,128)(2,1)} %get-tuple-element.68), channel_id=1, source_target_pairs={{0,3},{1,2},{2,1},{3,0},{4,7},{5,6},{6,5},{7,4},{8,11},{9,10},{10,... | collective-permute-start | bytes 786440 | tf_op jit(solution)/shard_map/ppermute | solution.py:92
  132.0 1.0 copy-start.1
  (3 other events, 2.2 us)

commit v6 on v5

--- a/solution.py
+++ b/solution.py
@@ -17,11 +17,15 @@
 
 epsilon = 1e-06
 
+vmem = pl.BlockSpec(memory_space=pltpu.VMEM)
+smem = pl.BlockSpec(memory_space=pltpu.SMEM)
+hbm = pl.BlockSpec(memory_space=pltpu.HBM)
+
 f32 = jnp.float32
 bf16 = jnp.bfloat16
 
 
-def params(mib=60):
+def params(mib=28):
     return pltpu.CompilerParams(vmem_limit_bytes=mib << 20)
 
 
@@ -65,9 +69,9 @@
         pairs = [(t, (t // c ^ 1) * c + t % c) for t in range(self.frames)]
         return lax.ppermute(block, "tm", pairs)
 
-    def gather(self, copies, refs, out, cols):
+    def places(self, refs):
         if len(refs) == 1:
-            return [copies.start(refs[0].at[:, cols], out)]
+            return [(refs[0], slice(None))]
         rows = refs[0].shape[0]
         a, b = lax.div(self.chip(), self.across), lax.rem(self.chip(), self.across)
         made = []
@@ -75,7 +79,7 @@
             k, flip = i // 2, i % 2
             there = lax.rem(a - k + self.along, self.along) * self.across
             at = pl.multiple_of((there + (1 - b if flip else b)) * rows, rows)
-            made.append(copies.start(ref.at[:, cols], out.at[pl.ds(at, rows), :]))
+            made.append((ref, pl.ds(at, rows)))
         return made
 
     def to_peer(self, block, k, other):
@@ -134,7 +138,7 @@
 
 
 def reorder_kernel(plan, *refs):
-    w_refs, out_ref = refs[:-1], refs[-1]
+    w_refs, out_refs = refs[:-2], refs[-2:]
     rows = w_refs[0].shape[0]
     width = plan.heads * PIECES * HD
     first = plan.core() == 0
@@ -145,26 +149,28 @@
             return one
         return jnp.where(first, one, ref[:, width + at : width + at + HD])
 
-    to = 0
-    for kinds in (EARLY, LATE):
-        for p in range(plan.pairs):
-            for i in kinds:
-                blocks = []
-                for ref in w_refs:
-                    one, two = (chosen(ref, ((2 * p + h) * PIECES + i) * HD) for h in range(2))
-                    blocks.append(jnp.concatenate([one, two], axis=1))
-                for s, block in enumerate(blocks):
-                    if plan.merge == 2:
-                        block = jnp.where(first, block, blocks[1 - s])
-                    out_ref[s * rows : (s + 1) * rows, to : to + LANES] = block
-                to += LANES
+    early = [(p, i) for i in EARLY for p in range(plan.pairs)]
+    late = [(p, i) for p in range(plan.pairs) for i in LATE]
+    for out_ref, order in zip(out_refs, (early, late)):
+        for n, (p, i) in enumerate(order):
+            blocks = []
+            for ref in w_refs:
+                one, two = (chosen(ref, ((2 * p + h) * PIECES + i) * HD) for h in range(2))
+                blocks.append(jnp.concatenate([one, two], axis=1))
+            for s, block in enumerate(blocks):
+                if plan.merge == 2:
+                    block = jnp.where(first, block, blocks[1 - s])
+                out_ref[s * rows : (s + 1) * rows, n * LANES : (n + 1) * LANES] = block
 
 
 def reorder(plan, weights):
     rows = weights[0].shape[0]
     return pl.pallas_call(
         functools.partial(reorder_kernel, plan),
-        out_shape=jax.ShapeDtypeStruct((plan.merge * rows, plan.heads * PIECES * HD), bf16),
+        out_shape=tuple(
+            jax.ShapeDtypeStruct((plan.merge * rows, plan.heads * len(kinds) * HD), bf16)
+            for kinds in (EARLY, LATE)
+        ),
         compiler_params=params(),
         cost_estimate=cost(0, 4 * weights[0].size),
         name="reorder",
@@ -268,47 +274,26 @@
     )(ids.reshape(tokens, 1))
 
 
-def place_kernel(merge, *refs):
-    pick_ref, frame_refs = refs[0], refs[1 : 1 + merge]
-    x_ref, pick, raw, normed, x, sems = refs[1 + merge :]
-    copies = Copies(sems)
-    local = raw.shape[1]
-    tokens = pick.shape[0]
+def place_kernel(merge, pick_ref, *refs):
+    frame_refs, x_ref, normed = refs[:merge], refs[-2], refs[-1]
+    tokens = pick_ref.shape[0]
     step = 256
-    arriving = [copies.start(ref, raw.at[s]) for s, ref in enumerate(frame_refs)]
-    picking = copies.start(pick_ref, pick)
-    leaving = []
     for s in range(merge):
-        arriving[s].wait()
-        normalise(raw.at[s], normed, 0)
-        if s == 0:
-            picking.wait()
+        normalise(frame_refs[s], normed.at[s], 0)
         for at in range(0, tokens, step):
-            there = slice(s * tokens + at, s * tokens + at + step)
-            x[there, :] = jnp.dot(
-                pick[at : at + step, :], normed[...], preferred_element_type=f32
+            x_ref[s * tokens + at : s * tokens + at + step, :] = jnp.dot(
+                pick_ref[at : at + step, :], normed[s], preferred_element_type=f32
             ).astype(bf16)
-            leaving.append(copies.start(x.at[there], x_ref.at[there]))
-    finish(leaving)
 
 
 def place_tokens(plan, pick, frames):
     tokens, count = pick.shape
     width = frames[0].shape[1]
     every = plan.merge * tokens
-    any_space = pl.BlockSpec(memory_space=pl.ANY)
     return pl.pallas_call(
         functools.partial(place_kernel, plan.merge),
-        in_specs=[any_space] * (1 + len(frames)),
-        out_specs=any_space,
         out_shape=jax.ShapeDtypeStruct((every, width), bf16),
-        scratch_shapes=[
-            pltpu.VMEM((tokens, count), bf16),
-            pltpu.VMEM((plan.merge, count, width), bf16),
-            pltpu.VMEM((count, width), bf16),
-            pltpu.VMEM((every, width), bf16),
-            Copies.scratch(),
-        ],
+        scratch_shapes=[pltpu.VMEM((plan.merge, count, width), bf16)],
         compiler_params=params(),
         cost_estimate=cost(4 * every * count * width, 6 * tokens * width),
         name="place_tokens",
@@ -320,23 +305,37 @@
     part_ref, rest_ref, refs = refs[0], refs[1], refs[2:]
     frame_refs, refs = refs[: plan.merge * parts], refs[plan.merge * parts :]
     w_refs, refs = refs[:-13], refs[-13:]
-    x_out, v_out, u_out, total_ref, rest, raw, normed, w, x, v, b, u, sems = refs
+    x_out, v_out, u_out, total_ref, rest, raw, normed, w, turned, x, v, u, sems = refs
     copies = Copies(sems)
     tokens = rest.shape[0]
     block = tokens // groups
     step = 256
     here = step // block
-    many = here * plan.pairs * N
-
-    arriving = []
+    cols = plan.pairs * LANES
+
+    weights = []
+    for ref, rows in plan.places(w_refs):
+        weights.append(copies.start(ref.at[:, cols:], turned.at[rows]))
+        weights.append(copies.start(ref.at[:, :cols], w.at[rows]))
+    arriving, picking = [], [copies.start(rest_ref, rest)]
     for s in range(plan.merge):
         at = 0
         for ref in frame_refs[s * parts : (s + 1) * parts]:
             size = ref.shape[0]
             arriving.append(copies.start(ref, raw.at[s, at : at + size, :]))
             at += size
-    picking = [copies.start(rest_ref, rest), copies.start(part_ref, x)]
-    weights = plan.gather(copies, w_refs, w, slice(0, w.shape[1]))
+        mine = slice(s * tokens, (s + 1) * tokens)
+        picking.append(copies.start(part_ref.at[mine], x.at[mine]))
+
+    finish(weights)
+    maps = jnp.concatenate(
+        [
+            turned[at : at + LANES, :].astype(f32).T.astype(bf16)
+            for at in range(0, turned.shape[0], LANES)
+        ],
+        axis=1,
+    )
+    lane = lax.div(lax.broadcasted_iota(jnp.int32, (LANES, step), 1), block)
 
     leaving = []
     for s in range(plan.merge):
@@ -347,37 +346,28 @@
         for at in range(0, tokens, step):
             there = slice(s * tokens + at, s * tokens + at + step)
             more = jnp.dot(rest[at : at + step, :], normed[...], preferred_element_type=f32)
-            x[there, :] = x[there, :] + more.astype(bf16)
+            placed = x[there, :] + more.astype(bf16)
+            x[there, :] = placed
             leaving.append(copies.start(x.at[there], x_out.at[there]))
-    finish(weights)
-
-    def project(c, _):
-        at = pl.ds(pl.multiple_of(c * step, step), step)
-        both = jnp.dot(x[at, :], w[...], preferred_element_type=f32).astype(bf16)
-        for p in range(plan.pairs):
-            cols = slice(p * LANES, (p + 1) * LANES)
-            v[at, cols] = both[:, 2 * p * LANES : (2 * p + 1) * LANES]
-            b[at, cols] = both[:, (2 * p + 1) * LANES : (2 * p + 2) * LANES]
-        return 0
-
-    lax.fori_loop(0, plan.merge * tokens // step, project, 0)
-    leaving.append(copies.start(v, v_out))
-
-    for s in range(plan.merge):
-        for p in range(plan.pairs):
-            cols = slice(p * LANES, (p + 1) * LANES)
-            for g in range(0, groups, 2):
-                rows = slice(s * tokens + g * block, s * tokens + (g + 2) * block)
-                turned = b[rows, cols].astype(f32).T
-                half = lax.broadcasted_iota(jnp.int32, turned.shape, 1) < block
+            values = jnp.dot(placed, w[...], preferred_element_type=f32).astype(bf16)
+            v[there, :] = values
+            b = lax.dot_general(
+                maps, placed, (((1,), (1,)), ((), ())), preferred_element_type=f32
+            )
+            for p in range(plan.pairs):
+                mine = b[p * LANES : (p + 1) * LANES]
                 wide = jnp.concatenate(
-                    [jnp.where(half, turned, 0.0), jnp.where(half, 0.0, turned)], axis=0
-                ).astype(bf16)
-                outer = jnp.dot(wide, v[rows, cols], preferred_element_type=f32)
-                for n in range(2):
-                    m = outer[n * 2 * N : (n + 1) * 2 * N]
-                    at = ((g + n) * plan.pairs + p) * N
-                    u[s, at : at + N, :] = halves((N, LANES), m[:N], m[N:])
+                    [jnp.where(lane == i, mine, 0.0).astype(bf16) for i in range(here)], axis=0
+                )
+                outer = jnp.dot(
+                    wide, values[:, p * LANES : (p + 1) * LANES], preferred_element_type=f32
+                )
+                for i in range(here):
+                    m = outer[i * 2 * N : (i + 1) * 2 * N]
+                    row = ((at // block + i) * plan.pairs + p) * N
+                    u[s, row : row + N, :] = halves((N, LANES), m[:N], m[N:])
+        mine = slice(s * tokens, (s + 1) * tokens)
+        leaving.append(copies.start(v.at[mine], v_out.at[mine]))
         leaving.append(copies.start(u.at[s], u_out.at[s]))
 
     peers = total_ref.shape[0]
@@ -415,12 +405,10 @@
     cols = plan.pairs * LANES
     rows = plan.pairs * groups * N
     share = rows // plan.chips
-    any_space = pl.BlockSpec(memory_space=pl.ANY)
     return pl.pallas_call(
         functools.partial(update_kernel, plan, groups, len(frames) // plan.merge),
-        in_specs=[pl.BlockSpec(memory_space=pltpu.SMEM)] * plan.merge
-        + [any_space] * (2 + len(frames) + len(weights)),
-        out_specs=(any_space,) * 3 + (pl.BlockSpec(memory_space=pltpu.VMEM),),
+        in_specs=[smem] * plan.merge + [hbm] * (2 + len(frames) + len(weights)),
+        out_specs=(hbm,) * 3 + (vmem,),
         out_shape=(
             jax.ShapeDtypeStruct((every, width), bf16),
             jax.ShapeDtypeStruct((every, cols), bf16),
@@ -431,14 +419,14 @@
             pltpu.VMEM((tokens, count), bf16),
             pltpu.VMEM((plan.merge, count, width), bf16),
             pltpu.VMEM((count, width), bf16),
-            pltpu.VMEM((width, 2 * cols), bf16),
+            pltpu.VMEM((width, cols), bf16),
+            pltpu.VMEM((width, cols), bf16),
             pltpu.VMEM((every, width), bf16),
-            pltpu.VMEM((every, cols), bf16),
             pltpu.VMEM((every, cols), bf16),
             pltpu.VMEM((plan.merge, rows, LANES), f32),
             Copies.scratch(),
         ],
-        compiler_params=params(),
+        compiler_params=params(60),
         cost_estimate=cost(4 * every * width * (2 * cols + count), 6 * every * width),
         name="project_updates",
     )(*decays, part, rest, *frames, *weights)
@@ -473,32 +461,37 @@
 def attend_kernel(plan, slot, *refs):
     lists_ref, refs = refs[0], refs[1:]
     decay_refs, refs = refs[: plan.merge], refs[plan.merge :]
-    x_in, v_in, u_in, w_refs, refs = refs[0], refs[1], refs[2], refs[3:-11], refs[-11:]
-    a_out, c_out, x, v, u, w, q_ref, k_ref, a, c_ref, sems = refs
+    x_in, v_in, u_in, w_refs, refs = refs[0], refs[1], refs[2], refs[3:-13], refs[-13:]
+    a_out, c_out, x, v, u, w, q_ref, k_ref, wide_v, e_ref, a, c_ref, sems = refs
     copies = Copies(sems)
     tokens = x.shape[0]
     groups, chosen = lists_ref.shape
     block = tokens // groups
     step = 256
     per = step // block
-    early = 2 * plan.pairs * LANES
     mine = slice(slot * tokens, (slot + 1) * tokens)
 
-    weights = plan.gather(copies, w_refs, w, slice(early, early + w.shape[1]))
+    weights = [copies.start(ref, w.at[rows]) for ref, rows in plan.places(w_refs)]
     arriving = []
     for at in range(0, tokens, step):
         from_ = slice(slot * tokens + at, slot * tokens + at + step)
         arriving.append(copies.start(x_in.at[from_], x.at[at : at + step]))
     later = [copies.start(v_in.at[mine], v), copies.start(u_in, u)]
 
+    same = lax.div(lax.broadcasted_iota(jnp.int32, (2 * LANES, 2 * LANES), 0), HD) == lax.div(
+        lax.broadcasted_iota(jnp.int32, (2 * LANES, 2 * LANES), 1), HD
+    )
+    same = jnp.where(same, 1.0, 0.0).astype(bf16)
+
+    def head_norm(values):
+        square = values * values
+        high = square.astype(bf16)
+        low = (square - high.astype(f32)).astype(bf16)
+        total = jnp.dot(high, same, preferred_element_type=f32)
+        total = total + jnp.dot(low, same, preferred_element_type=f32)
+        return values * lax.rsqrt(total * (1.0 / HD) + epsilon)
+
     half = first_half((step, LANES))
-
-    def head_norm(wide):
-        square = wide * wide
-        one = jnp.sum(jnp.where(half, square, 0.0), axis=-1, keepdims=True)
-        two = jnp.sum(jnp.where(half, 0.0, square), axis=-1, keepdims=True)
-        return wide * lax.rsqrt(jnp.where(half, one, two) * (1.0 / HD) + epsilon)
-
     finish(weights)
     for at in range(0, tokens, step):
         arriving[at // step].wait()
@@ -506,12 +499,11 @@
         every = jnp.dot(x[rows, :], w[...], preferred_element_type=f32).astype(bf16)
         for p in range(plan.pairs):
             cols = slice(p * LANES, (p + 1) * LANES)
-            q, k, reader = (
-                every[:, (3 * p + i) * LANES : (3 * p + i + 1) * LANES] for i in range(3)
-            )
-            c_ref[rows, cols] = reader
-            k_ref[rows, cols] = head_norm(k.astype(f32)).astype(bf16)
-            q = head_norm(q.astype(f32))
+            first = 3 * p * LANES
+            c_ref[rows, cols] = every[:, first + 2 * LANES : first + 3 * LANES]
+            both = head_norm(every[:, first : first + 2 * LANES].astype(f32))
+            k_ref[p, rows, :] = both[:, LANES:].astype(bf16)
+            q = both[:, :LANES]
             one = jnp.where(half, q, 0.0).astype(bf16)
             two = jnp.where(half, 0.0, q).astype(bf16)
             for i in range(per):
@@ -519,29 +511,41 @@
                 q_ref[p, at // block + i] = jnp.concatenate([one[part], two[part]], axis=0)
     leaving = [copies.start(c_ref, c_out)]
     finish(later)
+    for p in range(plan.pairs):
+        wide_v[p, :, :LANES] = v[:, p * LANES : (p + 1) * LANES]
+        wide_v[p, :, LANES:] = jnp.ones((tokens, LANES), bf16)
 
     scale = math.log2(math.e) / math.sqrt(HD)
+    starts = [
+        [pl.multiple_of(lists_ref[g, j] * block, block) for j in range(chosen)]
+        for g in range(groups)
+    ]
     for g in range(groups):
-        rows = slice(g * block, (g + 1) * block)
-        starts = [pl.multiple_of(lists_ref[g, j] * block, block) for j in range(chosen)]
         for p in range(plan.pairs):
-            cols = slice(p * LANES, (p + 1) * LANES)
-            keys = jnp.concatenate([k_ref[pl.ds(s, block), cols] for s in starts], axis=0)
-            values = jnp.concatenate([v[pl.ds(s, block), cols] for s in starts], axis=0)
+            keys = jnp.concatenate([k_ref[p, pl.ds(s, block), :] for s in starts[g]], axis=0)
             score = lax.dot_general(
                 q_ref[p, g], keys, (((1,), (1,)), ((), ())), preferred_element_type=f32
             )
-            e = jnp.exp2(score * scale)
-            weight = (e * (1.0 / jnp.sum(e, axis=-1, keepdims=True))).astype(bf16)
-            both = jnp.dot(weight, values, preferred_element_type=f32)
-            attended = halves((block, LANES), both[:block], both[block:])
+            e_ref[p, g] = jnp.exp2(score * scale).astype(bf16)
+    for g in range(groups):
+        rows = slice(g * block, (g + 1) * block)
+        for p in range(plan.pairs):
+            cols = slice(p * LANES, (p + 1) * LANES)
+            values = jnp.concatenate([wide_v[p, pl.ds(s, block), :] for s in starts[g]], axis=0)
+            both = jnp.dot(e_ref[p, g], values, preferred_element_type=f32)
+            both = both[:, :LANES] / both[:, LANES:]
+            a[rows, cols] = halves((block, LANES), both[:block], both[block:])
+    for g in range(groups):
+        rows = slice(g * block, (g + 1) * block)
+        for p in range(plan.pairs):
+            cols = slice(p * LANES, (p + 1) * LANES)
             items = slice((g * plan.pairs + p) * N, (g * plan.pairs + p + 1) * N)
             state = u[slot, items, :]
             if plan.merge == 2:
                 last = plan.last_decay(decay_refs, p, g)
                 last = jnp.where(plan.core() == slot, 0.0, last)
                 state = state + last * u[1 - slot, items, :]
-            a[rows, cols] = attended + read_out(c_ref[rows, cols], state, block)
+            a[rows, cols] = a[rows, cols] + read_out(c_ref[rows, cols], state, block)
         if (g + 1) % per == 0:
             done = slice((g + 1 - per) * block, (g + 1) * block)
             leaving.append(copies.start(a.at[done], a_out.at[done]))
@@ -554,19 +558,19 @@
     tokens = every // plan.merge
     block = tokens // groups
     cols = plan.pairs * LANES
-    any_space = pl.BlockSpec(memory_space=pl.ANY)
     return pl.pallas_call(
         functools.partial(attend_kernel, plan, slot),
-        in_specs=[pl.BlockSpec(memory_space=pltpu.SMEM)] * (1 + plan.merge)
-        + [any_space] * (3 + len(weights)),
-        out_specs=(any_space,) * 2,
+        in_specs=[smem] * (1 + plan.merge) + [hbm] * (3 + len(weights)),
+        out_specs=(hbm,) * 2,
         scratch_shapes=[
             pltpu.VMEM((tokens, width), bf16),
             pltpu.VMEM((tokens, cols), bf16),
             pltpu.VMEM(updates.shape, f32),
             pltpu.VMEM((width, 3 * cols), bf16),
             pltpu.VMEM((plan.pairs, groups, 2 * block, LANES), bf16),
-            pltpu.VMEM((tokens, cols), bf16),
+            pltpu.VMEM((plan.pairs, tokens, LANES), bf16),
+            pltpu.VMEM((plan.pairs, tokens, 2 * LANES), bf16),
+            pltpu.VMEM((plan.pairs, groups, 2 * block, chosen * block), bf16),
             pltpu.VMEM((tokens, cols), f32),
             pltpu.VMEM((tokens, cols), bf16),
             Copies.scratch(),
@@ -575,7 +579,7 @@
             jax.ShapeDtypeStruct((tokens, cols), f32),
             jax.ShapeDtypeStruct((tokens, cols), bf16),
         ),
-        compiler_params=params(),
+        compiler_params=params(60),
         cost_estimate=cost(
             6 * tokens * width * 3 * cols,
             4 * (tokens * width + 5 * width * cols + updates.size),
@@ -595,44 +599,20 @@
 
 def mix_kernel(plan, groups, *refs):
     decay_refs, refs = refs[: plan.merge], refs[plan.merge :]
-    a_ins, refs = refs[: plan.merge], refs[plan.merge :]
-    c_ins, refs = refs[: plan.merge], refs[plan.merge :]
-    s_in, back_in, refs = refs[0], refs[1], refs[2:]
-    out_refs, (a, c, state, back, mixed, sems) = refs[:-6], refs[-6:]
-    copies = Copies(sems)
-    tokens = back.shape[0]
+    a_refs, refs = refs[: plan.merge], refs[plan.merge :]
+    c_refs, refs = refs[: plan.merge], refs[plan.merge :]
+    s_ref, back_ref, out_refs, mixed = refs[0], refs[1], refs[2:-1], refs[-1]
+    tokens = back_ref.shape[0]
     block = tokens // groups
-    width = a.shape[2]
-    here = groups // 4
-    step = here * block
-    many = here * plan.pairs * N
+    width = a_refs[0].shape[1]
     first = plan.core() == 0
-
-    arriving = []
-    for i in range(4):
-        rows = slice(i * step, (i + 1) * step)
-        items = slice(i * many, (i + 1) * many)
-        arriving.append([copies.start(s_in.at[items], state.at[items])])
-        for s in range(plan.merge):
-            arriving[-1] += [
-                copies.start(a_ins[s].at[rows], a.at[s, rows, :]),
-                copies.start(c_ins[s].at[rows], c.at[s, rows, :]),
-            ]
-    local = tokens // plan.peers
-    turning = [
-        copies.start(back_in.at[k * local : (k + 1) * local], back.at[k * local : (k + 1) * local])
-        for k in range(plan.peers)
-    ]
-
     for g in range(groups):
-        if g % here == 0:
-            finish(arriving[g // here])
         rows = slice(g * block, (g + 1) * block)
         for p in range(plan.pairs):
             cols = slice(p * LANES, (p + 1) * LANES)
             at = (g * plan.pairs + p) * N
-            readers = jnp.concatenate([c[s, rows, cols] for s in range(plan.merge)], axis=0)
-            read = read_out(readers, state[at : at + N, :].astype(f32), block)
+            readers = jnp.concatenate([c[rows, cols] for c in c_refs], axis=0)
+            read = read_out(readers, s_ref[at : at + N, :].astype(f32), block)
             decays = [plan.decay(decay_refs, s, p, g) for s in range(plan.merge)]
             if plan.merge == 2:
                 both = decays[0] * decays[1]
@@ -640,13 +620,12 @@
             for s in range(plan.merge):
                 there = slice(s * width + p * LANES, s * width + (p + 1) * LANES)
                 mixed[rows, there] = (
-                    a[s, rows, cols] + decays[s] * read[s * block : (s + 1) * block]
+                    a_refs[s][rows, cols] + decays[s] * read[s * block : (s + 1) * block]
                 ).astype(bf16)
-
+    local = tokens // plan.peers
     for k in range(plan.peers):
-        turning[k].wait()
         placed = jnp.dot(
-            back[k * local : (k + 1) * local, :], mixed[...], preferred_element_type=f32
+            back_ref[k * local : (k + 1) * local, :], mixed[...], preferred_element_type=f32
         ).astype(bf16)
         for s in range(plan.merge):
             out_refs[s * plan.peers + k][...] = placed[:, s * width : (s + 1) * width]
@@ -655,24 +634,13 @@
 def mix(plan, decays, attended, readers, state, back, groups):
     tokens = back.shape[0]
     width = attended[0].shape[1]
-    local = tokens // plan.peers
     count = plan.merge * plan.peers
-    any_space = pl.BlockSpec(memory_space=pl.ANY)
     return pl.pallas_call(
         functools.partial(mix_kernel, plan, groups),
-        in_specs=[pl.BlockSpec(memory_space=pltpu.SMEM)] * plan.merge
-        + [any_space] * (2 * plan.merge + 2),
-        out_specs=(pl.BlockSpec(memory_space=pltpu.VMEM),) * count,
-        out_shape=(jax.ShapeDtypeStruct((local, width), bf16),) * count,
-        scratch_shapes=[
-            pltpu.VMEM((plan.merge, tokens, width), f32),
-            pltpu.VMEM((plan.merge, tokens, width), bf16),
-            pltpu.VMEM(state.shape, bf16),
-            pltpu.VMEM((tokens, tokens), bf16),
-            pltpu.VMEM((tokens, plan.merge * width), bf16),
-            Copies.scratch(),
-        ],
-        compiler_params=params(),
+        in_specs=[smem] * plan.merge + [vmem] * (2 * plan.merge + 2),
+        out_shape=(jax.ShapeDtypeStruct((tokens // plan.peers, width), bf16),) * count,
+        scratch_shapes=[pltpu.VMEM((tokens, plan.merge * width), bf16)],
+        compiler_params=params(24),
         cost_estimate=cost(4 * tokens * tokens * width, 2 * tokens * tokens + 16 * tokens * width),
         name="mix",
     )(*decays, *attended, *readers, state, back)
@@ -718,31 +686,49 @@
     arriving = [plan.to_peer(own, plan.peers - k, False) for k in range(1, plan.peers)]
     owns = [own] + [plan.swap(own)] * (plan.merge - 1)
     rates = [decays[0]] + [plan.swap(decays[0])] * (plan.merge - 1)
-    block = reorder(plan, [in_weight] + [plan.swap(in_weight)] * (plan.merge - 1))
+    blocks = reorder(plan, [in_weight] + [plan.swap(in_weight)] * (plan.merge - 1))
 
     ids = jnp.roll(block_ids, -me * local_tokens)
+    ids, rates = lax.optimization_barrier((ids, rates))
     pick, rest = pick_tokens(ids, local_tokens, groups)
     part = place_tokens(plan, pick, owns)
     if plan.ringed:
-        weights, beside = [], [pick, part]
-        for k in range(plan.along):
-            crossed = plan.cross(block)
-            weights += [block, crossed]
-            if k < plan.along - 1:
-                block = plan.round(block)
-                block, crossed, beside[:1] = lax.optimization_barrier((block, crossed, beside[:1]))
-                weights[-1] = crossed
-                beside = beside[1:]
-                n = k - (plan.along - 1 - len(arriving))
-                if 0 <= n < len(arriving):
-                    arriving[n], block = lax.optimization_barrier((arriving[n], block))
+        def step(block, with_):
+            return lax.optimization_barrier((plan.round(block), plan.cross(block), with_))[:2]
+
+        def late_step(tie):
+            late[-1], _ = lax.optimization_barrier((late[-1], tie))
+            if len(late) < plan.along:
+                passed, crossed = step(late[-1], [])
+                late.append(passed)
+            else:
+                crossed = plan.cross(late[-1])
+            late_crossed.append(crossed)
+
+        early, early_crossed, late, late_crossed = [blocks[0]], [], [blocks[1]], []
+        beside = [pick, part]
+        for k in range(plan.along - 1):
+            passed, crossed = step(early[-1], beside[k : k + 1])
+            early.append(passed)
+            early_crossed.append(crossed)
+        early_crossed.append(plan.cross(early[-1]))
+        late_step(early[min(1, plan.along - 1)])
+        arriving, _ = lax.optimization_barrier((arriving, (early_crossed[-1], late[-1])))
+        if plan.along > 1:
+            late_step(early[min(2, plan.along - 1)])
+        early = [b for pair in zip(early, early_crossed) for b in pair]
     else:
-        weights = [
-            lax.all_gather(block, "tm", axis=0, tiled=True, axis_index_groups=plan.groups())
-        ]
+        early, late = (
+            [lax.all_gather(b, "tm", axis=0, tiled=True, axis_index_groups=plan.groups())]
+            for b in blocks
+        )
     if plan.merge == 2:
         arriving = arriving + [plan.swap(chunk) for chunk in arriving]
-    x, v, updates, total = project_updates(plan, rates, part, rest, arriving, weights, groups)
+    x, v, updates, total = project_updates(plan, rates, part, rest, arriving, early, groups)
+    if plan.ringed:
+        while len(late_crossed) < plan.along:
+            late_step(total)
+        late = [b for pair in zip(late, late_crossed) for b in pair]
 
     def exchange(blocks):
         return lax.all_to_all(
@@ -752,12 +738,12 @@
 
     share = updates.shape[1] // plan.chips
     arrived = exchange(total)
-    attended = [attend(plan, 0, block_lists, rates, x, v, weights, updates)]
+    attended = [attend(plan, 0, block_lists, rates, x, v, late, updates)]
     arrived, attended = lax.optimization_barrier((arrived, attended))
     states = scan_states(plan, arrived, share)
     x, states = lax.optimization_barrier((x, states))
     if plan.merge == 2:
-        attended.append(attend(plan, 1, block_lists, rates, x, v, weights, updates))
+        attended.append(attend(plan, 1, block_lists, rates, x, v, late, updates))
     state = exchange(states).reshape(-1, LANES)
     ids, attended = lax.optimization_barrier((ids, attended))
     back = back_tokens(ids, groups)

time: 136 us -> 133 us (0.978)
  Pallas kernels: 69.1 us -> 45.9 us
  starting transfers between devices: 23.3 us -> 34.2 us
  local copies, waits for them, and re-layouts: 6.23 us -> 11.3 us
  waiting for transfers between devices: 35 us -> 39.9 us
    pallas_call x5, Pallas kernels: 44 us -> 24.8 us  [the longest x2 18.7 us: attend(): pl.pallas_call(functools.partial(attend_kernel, plan, slot), in_specs=[sm...]
    ppermute x3 -> x6, waiting for transfers between devices: 13.4 us -> 21.2 us  [round(): return lax.ppermute(block, 'tm', pairs)]
    unnamed x37 -> x63, local copies, waits for them, and re-layouts: 5.2 us -> 11.1 us
    ppermute x3 -> x6, starting transfers between devices: 4.23 us -> 9.05 us  [round(): return lax.ppermute(block, 'tm', pairs)]
    ppermute x4 -> x8, starting transfers between devices: 5.09 us -> 9.55 us  [cross(): return lax.ppermute(block, 'tm', pairs)]
    ppermute x5, waiting for transfers between devices: 4.37 us -> 1.72 us  [swap(): return lax.ppermute(block, 'tm', [(t, t ^ 1) for t in range(self.frames)])]
    pallas_call x1, Pallas kernels: 5.25 us -> 2.86 us  [back_tokens(): pl.pallas_call(functools.partial(back_kernel, groups), out_shape=jax.Shap...]
    pallas_call x1, Pallas kernels: 2.71 us -> 0.7 us  [pick_tokens(): pl.pallas_call(functools.partial(pick_kernel, groups), out_shape=(jax.Sha...]
  transfers between devices with their start and end apart: 17 -> 24, of which waited for: 8 -> 12; matrix products, arithmetic and copies ran while one was open for 2% -> 1% of each run, Pallas kernels for 34% -> 31%
where the time goes in v6:
time: 133 us; the launch traced here: 132 us
  Pallas kernels  45.9 us (35%)
  waiting for transfers between devices  39.9 us (30%)
  starting transfers between devices  34.2 us (26%)
  local copies, waits for them, and re-layouts  11.3 us (8%)
    ppermute x6, waiting for transfers between devices, round(): return lax.ppermute(block, 'tm', pairs)  21.2 us
    pallas_call x2, Pallas kernels, attend(): pl.pallas_call(functools.partial(attend_kernel, plan, slot), in_specs=[sm...  18.7 us
    pallas_call x1, Pallas kernels, project_updates(): pl.pallas_call(functools.partial(update_kernel, plan, groups, len(frames)...  14.4 us
    unnamed x63, local copies, waits for them, and re-layouts  11.1 us
    all_to_all x2, starting transfers between devices, exchange(): lax.all_to_all(blocks, 'tm', split_axis=0, concat_axis=0, tiled=True, axi...  9.89 us
    ppermute x8, starting transfers between devices, cross(): return lax.ppermute(block, 'tm', pairs)  9.55 us
    ppermute x6, starting transfers between devices, round(): return lax.ppermute(block, 'tm', pairs)  9.05 us
    ppermute x8, waiting for transfers between devices, cross(): return lax.ppermute(block, 'tm', pairs)  6.49 us
  transfers between devices with their start and end apart: 24, of which 12 were waited for; matrix products, arithmetic and copies ran while one was open for 1% of the time, Pallas kernels for 31%

profile of v6, /device:TPU:0, one launch (start us, length us, event | category | flops | bytes accessed | tf_op | source)
XLA Modules:
  0.0 132.3 jit_solution(1064896345498889244)
XLA Ops:
  0.5 3.0 %collective-permute-start.2 = (bf16[512,1024]{1,0:T(8,128)(2,1)}, bf16[512,1024]{1,0:T(8,128)(2,1)S(1)}, u32[]{:S(2)}, u32[]{:S(2)}) collective-permute-start(bf16[512,1024]{1,0:T(8,128)(2,1)} %bitcast.15), channel_id=1, source_target_pairs={{0,1},{1,0},{2,3},{3,2},{4,5},{5,4},{6,7},{7,6},{8,9},{9,8},{10,11... | collective-permute-start | bytes 3145736 | tf_op jit(solution)/shard_map/ppermute | solution.py:88
  4.6 2.9 %collective-permute-start.4 = (bf16[128,512]{1,0:T(8,128)(2,1)S(1)}, bf16[128,512]{1,0:T(8,128)(2,1)S(1)}, u32[]{:S(2)}, u32[]{:S(2)}) collective-permute-start(bf16[128,512]{1,0:T(8,128)(2,1)S(1)} %get-tuple-element.56.refs_6_), channel_id=1, source_target_pairs={{0,8},{2,10},{4,12},{6,14},{8,16},{10,18},{12,20},{14,22},{16,24},... | collective-permute-start | bytes 393224 | tf_op jit(solution)/shard_map/ppermute | solution.py:65
  7.6 1.5 %collective-permute-start.5 = (bf16[128,512]{1,0:T(8,128)(2,1)S(1)}, bf16[128,512]{1,0:T(8,128)(2,1)S(1)}, u32[]{:S(2)}, u32[]{:S(2)}) collective-permute-start(bf16[128,512]{1,0:T(8,128)(2,1)S(1)} %get-tuple-element.56.refs_6_), channel_id=1, source_target_pairs={{0,4},{2,6},{4,0},{6,2},{8,12},{10,14},{12,8},{14,10},{16,20},{18,... | collective-permute-start | bytes 393224 | tf_op jit(solution)/shard_map/ppermute | solution.py:70
  11.2 2.2 %collective-permute-done.4.refs_8_ = bf16[128,512]{1,0:T(8,128)(2,1)S(1)} collective-permute-done((bf16[128,512]{1,0:T(8,128)(2,1)S(1)}, bf16[128,512]{1,0:T(8,128)(2,1)S(1)}, u32[]{:S(2)}, u32[]{:S(2)}) %collective-permute-start.4) | collective-permute-done | bytes 131104 | tf_op jit(solution)/shard_map/ppermute | solution.py:65
  14.4 1.5 %collective-permute-start.7 = (bf16[128,512]{1,0:T(8,128)(2,1)S(1)}, bf16[128,512]{1,0:T(8,128)(2,1)S(1)}, u32[]{:S(2)}, u32[]{:S(2)}) collective-permute-start(bf16[128,512]{1,0:T(8,128)(2,1)S(1)} %collective-permute-done.4.refs_8_), channel_id=1, source_target_pairs={{0,4},{2,6},{4,0},{6,2},{8,12},{10,14},{12,8},{14,10},{16,20},{18,... | collective-permute-start | bytes 393224 | tf_op jit(solution)/shard_map/ppermute | solution.py:70
  15.9 1.2 copy-done.9
  17.1 3.7 %place_tokens.1.refs_2_ = bf16[2048,1024]{1,0:T(8,128)(2,1)S(1)} custom-call(bf16[1024,512]{1,0:T(8,128)(2,1)S(1)} %get-tuple-element.54.pick_ref, bf16[512,1024]{1,0:T(8,128)(2,1)S(1)} %bitcast.16, bf16[512,1024]{1,0:T(8,128)(2,1)S(1)} %collective-permute-done.1.refs_1_), custom_call_target="tpu_custom_call" | custom-call | flops 4294967296 | bytes 6291456 | tf_op jit(solution)/shard_map/place_tokens/pallas_call | solution.py:293
  20.9 2.0 %copy-done.13 = bf16[2048,1024]{1,0:T(8,128)(2,1)} copy-done((bf16[2048,1024]{1,0:T(8,128)(2,1)}, bf16[2048,1024]{1,0:T(8,128)(2,1)S(1)}, u32[]{:S(2)}) %copy-start.13) | copy-done | bytes 4194328
  22.9 1.6 %collective-permute-start.8 = (bf16[128,512]{1,0:T(8,128)(2,1)S(1)}, bf16[128,512]{1,0:T(8,128)(2,1)S(1)}, u32[]{:S(2)}, u32[]{:S(2)}) collective-permute-start(bf16[128,512]{1,0:T(8,128)(2,1)S(1)} %collective-permute-done.6.refs_10_), channel_id=1, source_target_pairs={{0,8},{2,10},{4,12},{6,14},{8,16},{10,18},{12,20},{14,22},{16,24},... | collective-permute-start | bytes 393224 | tf_op jit(solution)/shard_map/ppermute | solution.py:65
  25.5 1.5 %collective-permute-start.12 = (bf16[128,768]{1,0:T(8,128)(2,1)S(1)}, bf16[128,768]{1,0:T(8,128)(2,1)S(1)}, u32[]{:S(2)}, u32[]{:S(2)}) collective-permute-start(bf16[128,768]{1,0:T(8,128)(2,1)S(1)} %get-tuple-element.61.refs_6_), channel_id=1, source_target_pairs={{0,4},{2,6},{4,0},{6,2},{8,12},{10,14},{12,8},{14,10},{16,20},{18,... | collective-permute-start | bytes 589832 | tf_op jit(solution)/shard_map/ppermute | solution.py:70
  27.0 3.9 %collective-permute-done.8.refs_12_ = bf16[128,512]{1,0:T(8,128)(2,1)S(1)} collective-permute-done((bf16[128,512]{1,0:T(8,128)(2,1)S(1)}, bf16[128,512]{1,0:T(8,128)(2,1)S(1)}, u32[]{:S(2)}, u32[]{:S(2)}) %collective-permute-start.8) | collective-permute-done | bytes 131104 | tf_op jit(solution)/shard_map/ppermute | solution.py:65
  31.8 1.2 collective-permute-done.11.refs_8_
  33.7 2.2 %collective-permute-done.10.refs_13_ = bf16[128,512]{1,0:T(8,128)(2,1)S(1)} collective-permute-done((bf16[128,512]{1,0:T(8,128)(2,1)S(1)}, bf16[128,512]{1,0:T(8,128)(2,1)S(1)}, u32[]{:S(2)}, u32[]{:S(2)}) %collective-permute-start.10) | collective-permute-done | bytes 131104 | tf_op jit(solution)/shard_map/ppermute | solution.py:70
  39.5 14.4 %project_updates.1 = (bf16[2048,1024]{1,0:T(8,128)(2,1)}, bf16[2048,256]{1,0:T(8,128)(2,1)}, f32[2,2048,128]{2,1,0:T(8,128)}, bf16[8,272,128]{2,1,0:T(8,128)(2,1)}) custom-call(f32[8,16]{1,0:T(8,128)} %bitcast.10, f32[8,16]{1,0:T(8,128)} %copy-done.7, bf16[2048,1024]{1,0:T(8,128)(2,1)} %copy-done.13, bf16[1024,512]{1,0:T(8,128)(2,1)} %copy-done.12, ...), custom_call_target="tpu_custom_call" | custom-call | flops 8589934592 | bytes 12582912 | tf_op jit(solution)/shard_map/project_updates/pallas_call | solution.py:408
  53.9 3.9 %all-to-all-start = ((bf16[8,272,128]{2,1,0:T(8,128)(2,1)}), bf16[8,272,128]{2,1,0:T(8,128)(2,1)S(1)}, u32[]{:S(2)}, u32[]{:S(2)}) async-start(bf16[8,272,128]{2,1,0:T(8,128)(2,1)} %get-tuple-element.67), calls=%async_computation | async-start | bytes 1114112 | tf_op jit(solution)/shard_map/all_to_all | solution.py:734
  57.9 2.2 %collective-permute-start.16 = (bf16[128,768]{1,0:T(8,128)(2,1)S(1)}, bf16[128,768]{1,0:T(8,128)(2,1)S(1)}, u32[]{:S(2)}, u32[]{:S(2)}) collective-permute-start(bf16[128,768]{1,0:T(8,128)(2,1)S(1)} %collective-permute-done.14.refs_10_), channel_id=1, source_target_pairs={{0,8},{2,10},{4,12},{6,14},{8,16},{10,18},{12,20},{14,22},{16,24},... | collective-permute-start | bytes 589832 | tf_op jit(solution)/shard_map/ppermute | solution.py:65
  60.1 1.5 %collective-permute-start.17 = (bf16[128,768]{1,0:T(8,128)(2,1)S(1)}, bf16[128,768]{1,0:T(8,128)(2,1)S(1)}, u32[]{:S(2)}, u32[]{:S(2)}) collective-permute-start(bf16[128,768]{1,0:T(8,128)(2,1)S(1)} %collective-permute-done.14.refs_10_), channel_id=1, source_target_pairs={{0,4},{2,6},{4,0},{6,2},{8,12},{10,14},{12,8},{14,10},{16,20},{18,... | collective-permute-start | bytes 589832 | tf_op jit(solution)/shard_map/ppermute | solution.py:70
  61.6 13.8 %collective-permute-done.16.refs_12_ = bf16[128,768]{1,0:T(8,128)(2,1)S(1)} collective-permute-done((bf16[128,768]{1,0:T(8,128)(2,1)S(1)}, bf16[128,768]{1,0:T(8,128)(2,1)S(1)}, u32[]{:S(2)}, u32[]{:S(2)}) %collective-permute-start.16) | collective-permute-done | bytes 196640 | tf_op jit(solution)/shard_map/ppermute | solution.py:65
  75.4 1.5 %collective-permute-start.18 = (bf16[128,768]{1,0:T(8,128)(2,1)S(1)}, bf16[128,768]{1,0:T(8,128)(2,1)S(1)}, u32[]{:S(2)}, u32[]{:S(2)}) collective-permute-start(bf16[128,768]{1,0:T(8,128)(2,1)S(1)} %collective-permute-done.16.refs_12_), channel_id=1, source_target_pairs={{0,4},{2,6},{4,0},{6,2},{8,12},{10,14},{12,8},{14,10},{16,20},{18,... | collective-permute-start | bytes 589832 | tf_op jit(solution)/shard_map/ppermute | solution.py:70
  77.6 3.6 %collective-permute-done.18.refs_13_ = bf16[128,768]{1,0:T(8,128)(2,1)S(1)} collective-permute-done((bf16[128,768]{1,0:T(8,128)(2,1)S(1)}, bf16[128,768]{1,0:T(8,128)(2,1)S(1)}, u32[]{:S(2)}, u32[]{:S(2)}) %collective-permute-start.18) | collective-permute-done | bytes 196640 | tf_op jit(solution)/shard_map/ppermute | solution.py:70
  81.9 9.3 %attend.2 = (f32[1024,256]{1,0:T(8,128)}, bf16[1024,256]{1,0:T(8,128)(2,1)}) custom-call(s32[16,4]{1,0:T(8,128)} %copy.9.refs_0_, f32[8,16]{1,0:T(8,128)} %bitcast.11, f32[8,16]{1,0:T(8,128)} %copy-done.7, bf16[2048,1024]{1,0:T(8,128)(2,1)} %get-tuple-element.84.refs_3_, bf16[2048,256]{1,0:T(8,128)(2,1)} %get-tuple-element.69.refs_4_, ...), custom_call_target="tpu_custom_call" | custom-call | flops 4831838208 | bytes 11534336 | tf_op jit(solution)/shard_map/attend/pallas_call | solution.py:561
  92.1 6.0 %all-to-all-start.1 = ((bf16[8,256,128]{2,1,0:T(8,128)(2,1)}), bf16[8,256,128]{2,1,0:T(8,128)(2,1)S(1)}, u32[]{:S(2)}, u32[]{:S(2)}) async-start(bf16[8,256,128]{2,1,0:T(8,128)(2,1)} %scan_states.1), calls=%async_computation.1 | async-start | bytes 1048576 | tf_op jit(solution)/shard_map/all_to_all | solution.py:734
  98.1 9.4 %attend.3 = (f32[1024,256]{1,0:T(8,128)}, bf16[1024,256]{1,0:T(8,128)(2,1)}) custom-call(s32[16,4]{1,0:T(8,128)} %copy.9.refs_0_, f32[8,16]{1,0:T(8,128)} %bitcast.12, f32[8,16]{1,0:T(8,128)} %copy-done.7, bf16[2048,1024]{1,0:T(8,128)(2,1)} %get-tuple-element.84.refs_3_, bf16[2048,256]{1,0:T(8,128)(2,1)} %get-tuple-element.69.refs_4_, ...), custom_call_target="tpu_custom_call" | custom-call | flops 4831838208 | bytes 11534336 | tf_op jit(solution)/shard_map/attend/pallas_call | solution.py:561
  107.7 2.9 %back_tokens.1.refs_7_ = bf16[1024,1024]{1,0:T(8,128)(2,1)S(1)} custom-call(s32[1024,1]{1,0:T(8,128)S(1)} %copy.11.ids_ref), custom_call_target="tpu_custom_call" | custom-call | flops 268435456 | bytes 2097152 | tf_op jit(solution)/shard_map/back_tokens/pallas_call | solution.py:268
  110.6 1.4 %all-to-all-done.1 = bf16[8,256,128]{2,1,0:T(8,128)(2,1)S(1)} async-done(((bf16[8,256,128]{2,1,0:T(8,128)(2,1)}), bf16[8,256,128]{2,1,0:T(8,128)(2,1)S(1)}, u32[]{:S(2)}, u32[]{:S(2)}) %all-to-all-start.1) | async-done | bytes 524320 | tf_op jit(solution)/shard_map/all_to_all | solution.py:734
  112.0 1.2 copy-done.1
  113.2 1.2 copy-done.2
  116.5 2.3 %mix.1 = (bf16[512,256]{1,0:T(8,128)(2,1)S(1)}, bf16[512,256]{1,0:T(8,128)(2,1)S(1)}, bf16[512,256]{1,0:T(8,128)(2,1)S(1)}, bf16[512,256]{1,0:T(8,128)(2,1)S(1)}) custom-call(f32[8,16]{1,0:T(8,128)S(1)} %bitcast.13, f32[8,16]{1,0:T(8,128)S(1)} %copy-done.8, f32[1024,256]{1,0:T(8,128)S(1)} %copy-done.1, f32[1024,256]{1,0:T(8,128)S(1)} %copy-done.2, ...), custom_call_target="tpu_custom_call" | custom-call | flops 1073741824 | bytes 6291456 | tf_op jit(solution)/shard_map/mix/pallas_call | solution.py:638
  118.8 1.6 %collective-permute-start.19 = (bf16[512,256]{1,0:T(8,128)(2,1)S(1)}, bf16[512,256]{1,0:T(8,128)(2,1)S(1)}, u32[]{:S(2)}, u32[]{:S(2)}) collective-permute-start(bf16[512,256]{1,0:T(8,128)(2,1)S(1)} %get-tuple-element.94), channel_id=1, source_target_pairs={{0,1},{1,0},{2,3},{3,2},{4,5},{5,4},{6,7},{7,6},{8,9},{9,8},{10,11... | collective-permute-start | bytes 786440 | tf_op jit(solution)/shard_map/ppermute | solution.py:88
  121.0 6.5 %collective-permute-done.19.refs_1_ = bf16[512,256]{1,0:T(8,128)(2,1)S(1)} collective-permute-done((bf16[512,256]{1,0:T(8,128)(2,1)S(1)}, bf16[512,256]{1,0:T(8,128)(2,1)S(1)}, u32[]{:S(2)}, u32[]{:S(2)}) %collective-permute-start.19) | collective-permute-done | bytes 262176 | tf_op jit(solution)/shard_map/ppermute | solution.py:88
  127.5 2.6 %collective-permute-done.21.refs_3_ = bf16[512,256]{1,0:T(8,128)(2,1)S(1)} collective-permute-done((bf16[512,256]{1,0:T(8,128)(2,1)S(1)}, bf16[512,256]{1,0:T(8,128)(2,1)S(1)}, u32[]{:S(2)}, u32[]{:S(2)}) %collective-permute-start.21) | collective-permute-done | bytes 262176 | tf_op jit(solution)/shard_map/ppermute | solution.py:96
  130.1 2.2 %project_out.1 = bf16[512,1024]{1,0:T(8,128)(2,1)} custom-call(bf16[1024,1024]{1,0:T(8,128)(2,1)S(1)} %copy-done, bf16[512,256]{1,0:T(8,128)(2,1)S(1)} %get-tuple-element.93.refs_0_, bf16[512,256]{1,0:T(8,128)(2,1)S(1)} %collective-permute-done.19.refs_1_, bf16[512,256]{1,0:T(8,128)(2,1)S(1)} %collective-permute-done.20.refs_2_, ...), custom_call_target="tpu_custom_call" | custom-call | flops 1073741824 | bytes 4194304 | tf_op jit(solution)/shard_map/project_out/pallas_call | solution.py:669
  (91 shorter events, 16.1 us)
Async XLA Ops:
  0.0 15.9 %collective-permute-start.1 = (bf16[512,1024]{1,0:T(8,128)(2,1)}, bf16[512,1024]{1,0:T(8,128)(2,1)S(1)}, u32[]{:S(2)}, u32[]{:S(2)}) collective-permute-start(bf16[512,1024]{1,0:T(8,128)(2,1)} %bitcast.14), channel_id=1, source_target_pairs={{0,2},{2,0},{4,6},{6,4},{8,10},{10,8},{12,14},{14,12},{16,18},{18,... | collective-permute-start | bytes 3145736 | tf_op jit(solution)/shard_map/ppermute | solution.py:60
  0.5 3.0 %collective-permute-start.3 = (bf16[64,2560]{1,0:T(8,128)(2,1)}, bf16[64,2560]{1,0:T(8,128)(2,1)S(1)}, u32[]{:S(2)}, u32[]{:S(2)}) collective-permute-start(bf16[64,2560]{1,0:T(8,128)(2,1)} %refs_0_.3), channel_id=1, source_target_pairs={{0,2},{2,0},{4,6},{6,4},{8,10},{10,8},{12,14},{14,12},{16,18},{18,... | collective-permute-start | bytes 983048 | tf_op jit(solution)/shard_map/ppermute | solution.py:60
  0.5 33.2 %collective-permute-start.2 = (bf16[512,1024]{1,0:T(8,128)(2,1)}, bf16[512,1024]{1,0:T(8,128)(2,1)S(1)}, u32[]{:S(2)}, u32[]{:S(2)}) collective-permute-start(bf16[512,1024]{1,0:T(8,128)(2,1)} %bitcast.15), channel_id=1, source_target_pairs={{0,1},{1,0},{2,3},{3,2},{4,5},{5,4},{6,7},{7,6},{8,9},{9,8},{10,11... | collective-permute-start | bytes 3145736 | tf_op jit(solution)/shard_map/ppermute | solution.py:88
  4.6 16.2 %copy-start.11 = (bf16[128,512]{1,0:T(8,128)(2,1)}, bf16[128,512]{1,0:T(8,128)(2,1)S(1)}, u32[]{:S(2)}) copy-start(bf16[128,512]{1,0:T(8,128)(2,1)S(1)} %get-tuple-element.56.refs_6_) | copy-start | bytes 393220
  4.6 20.8 %copy-start.10 = (bf16[128,768]{1,0:T(8,128)(2,1)}, bf16[128,768]{1,0:T(8,128)(2,1)S(1)}, u32[]{:S(2)}) copy-start(bf16[128,768]{1,0:T(8,128)(2,1)S(1)} %get-tuple-element.61.refs_6_) | copy-start | bytes 589828
  4.6 8.8 %collective-permute-start.4 = (bf16[128,512]{1,0:T(8,128)(2,1)S(1)}, bf16[128,512]{1,0:T(8,128)(2,1)S(1)}, u32[]{:S(2)}, u32[]{:S(2)}) collective-permute-start(bf16[128,512]{1,0:T(8,128)(2,1)S(1)} %get-tuple-element.56.refs_6_), channel_id=1, source_target_pairs={{0,8},{2,10},{4,12},{6,14},{8,16},{10,18},{12,20},{14,22},{16,24},... | collective-permute-start | bytes 393224 | tf_op jit(solution)/shard_map/ppermute | solution.py:65
  7.6 5.8 %collective-permute-start.5 = (bf16[128,512]{1,0:T(8,128)(2,1)S(1)}, bf16[128,512]{1,0:T(8,128)(2,1)S(1)}, u32[]{:S(2)}, u32[]{:S(2)}) collective-permute-start(bf16[128,512]{1,0:T(8,128)(2,1)S(1)} %get-tuple-element.56.refs_6_), channel_id=1, source_target_pairs={{0,4},{2,6},{4,0},{6,2},{8,12},{10,14},{12,8},{14,10},{16,20},{18,... | collective-permute-start | bytes 393224 | tf_op jit(solution)/shard_map/ppermute | solution.py:70
  9.1 1.4 %collective-permute-start = (f32[8,16]{1,0:T(8,128)}, f32[8,16]{1,0:T(8,128)S(1)}, u32[]{:S(2)}, u32[]{:S(2)}) collective-permute-start(f32[8,16]{1,0:T(8,128)} %bitcast.9), channel_id=1, source_target_pairs={{0,2},{2,0},{4,6},{6,4},{8,10},{10,8},{12,14},{14,12},{16,18},{18,... | collective-permute-start | bytes 1544 | tf_op jit(solution)/shard_map/ppermute | solution.py:60
  13.4 9.5 %collective-permute-start.6 = (bf16[128,512]{1,0:T(8,128)(2,1)S(1)}, bf16[128,512]{1,0:T(8,128)(2,1)S(1)}, u32[]{:S(2)}, u32[]{:S(2)}) collective-permute-start(bf16[128,512]{1,0:T(8,128)(2,1)S(1)} %collective-permute-done.4.refs_8_), channel_id=1, source_target_pairs={{0,8},{2,10},{4,12},{6,14},{8,16},{10,18},{12,20},{14,22},{16,24},... | collective-permute-start | bytes 393224 | tf_op jit(solution)/shard_map/ppermute | solution.py:65
  14.4 8.5 %collective-permute-start.7 = (bf16[128,512]{1,0:T(8,128)(2,1)S(1)}, bf16[128,512]{1,0:T(8,128)(2,1)S(1)}, u32[]{:S(2)}, u32[]{:S(2)}) collective-permute-start(bf16[128,512]{1,0:T(8,128)(2,1)S(1)} %collective-permute-done.4.refs_8_), channel_id=1, source_target_pairs={{0,4},{2,6},{4,0},{6,2},{8,12},{10,14},{12,8},{14,10},{16,20},{18,... | collective-permute-start | bytes 393224 | tf_op jit(solution)/shard_map/ppermute | solution.py:70
  22.9 15.7 %copy-start.26 = (bf16[128,512]{1,0:T(8,128)(2,1)}, bf16[128,512]{1,0:T(8,128)(2,1)S(1)}, u32[]{:S(2)}) copy-start(bf16[128,512]{1,0:T(8,128)(2,1)S(1)} %collective-permute-done.6.refs_10_) | copy-start | bytes 393220
  22.9 7.9 %collective-permute-start.8 = (bf16[128,512]{1,0:T(8,128)(2,1)S(1)}, bf16[128,512]{1,0:T(8,128)(2,1)S(1)}, u32[]{:S(2)}, u32[]{:S(2)}) collective-permute-start(bf16[128,512]{1,0:T(8,128)(2,1)S(1)} %collective-permute-done.6.refs_10_), channel_id=1, source_target_pairs={{0,8},{2,10},{4,12},{6,14},{8,16},{10,18},{12,20},{14,22},{16,24},... | collective-permute-start | bytes 393224 | tf_op jit(solution)/shard_map/ppermute | solution.py:65
  24.6 6.3 %collective-permute-start.9 = (bf16[128,512]{1,0:T(8,128)(2,1)S(1)}, bf16[128,512]{1,0:T(8,128)(2,1)S(1)}, u32[]{:S(2)}, u32[]{:S(2)}) collective-permute-start(bf16[128,512]{1,0:T(8,128)(2,1)S(1)} %collective-permute-done.6.refs_10_), channel_id=1, source_target_pairs={{0,4},{2,6},{4,0},{6,2},{8,12},{10,14},{12,8},{14,10},{16,20},{18,... | collective-permute-start | bytes 393224 | tf_op jit(solution)/shard_map/ppermute | solution.py:70
  25.1 7.9 %collective-permute-start.11 = (bf16[128,768]{1,0:T(8,128)(2,1)S(1)}, bf16[128,768]{1,0:T(8,128)(2,1)S(1)}, u32[]{:S(2)}, u32[]{:S(2)}) collective-permute-start(bf16[128,768]{1,0:T(8,128)(2,1)S(1)} %get-tuple-element.61.refs_6_), channel_id=1, source_target_pairs={{0,8},{2,10},{4,12},{6,14},{8,16},{10,18},{12,20},{14,22},{16,24},... | collective-permute-start | bytes 589832 | tf_op jit(solution)/shard_map/ppermute | solution.py:65
  25.5 8.3 %collective-permute-start.12 = (bf16[128,768]{1,0:T(8,128)(2,1)S(1)}, bf16[128,768]{1,0:T(8,128)(2,1)S(1)}, u32[]{:S(2)}, u32[]{:S(2)}) collective-permute-start(bf16[128,768]{1,0:T(8,128)(2,1)S(1)} %get-tuple-element.61.refs_6_), channel_id=1, source_target_pairs={{0,4},{2,6},{4,0},{6,2},{8,12},{10,14},{12,8},{14,10},{16,20},{18,... | collective-permute-start | bytes 589832 | tf_op jit(solution)/shard_map/ppermute | solution.py:70
  30.9 5.0 %collective-permute-start.10 = (bf16[128,512]{1,0:T(8,128)(2,1)S(1)}, bf16[128,512]{1,0:T(8,128)(2,1)S(1)}, u32[]{:S(2)}, u32[]{:S(2)}) collective-permute-start(bf16[128,512]{1,0:T(8,128)(2,1)S(1)} %collective-permute-done.8.refs_12_), channel_id=1, source_target_pairs={{0,4},{2,6},{4,0},{6,2},{8,12},{10,14},{12,8},{14,10},{16,20},{18,... | collective-permute-start | bytes 393224 | tf_op jit(solution)/shard_map/ppermute | solution.py:70
  33.0 20.9 %copy-start.17 = (bf16[128,768]{1,0:T(8,128)(2,1)}, bf16[128,768]{1,0:T(8,128)(2,1)S(1)}, u32[]{:S(2)}) copy-start(bf16[128,768]{1,0:T(8,128)(2,1)S(1)} %collective-permute-done.11.refs_8_) | copy-start | bytes 589828
  33.7 20.2 %copy-start.18 = (bf16[128,768]{1,0:T(8,128)(2,1)}, bf16[128,768]{1,0:T(8,128)(2,1)S(1)}, u32[]{:S(2)}) copy-start(bf16[128,768]{1,0:T(8,128)(2,1)S(1)} %collective-permute-done.12.refs_7_) | copy-start | bytes 589828
  35.9 2.7 %collective-permute-start.13 = (bf16[512,1024]{1,0:T(8,128)(2,1)S(1)}, bf16[512,1024]{1,0:T(8,128)(2,1)S(1)}, u32[]{:S(2)}, u32[]{:S(2)}) collective-permute-start(bf16[512,1024]{1,0:T(8,128)(2,1)S(1)} %collective-permute-done.2.refs_4_), channel_id=1, source_target_pairs={{0,2},{2,0},{4,6},{6,4},{8,10},{10,8},{12,14},{14,12},{16,18},{18,... | collective-permute-start | bytes 3145736 | tf_op jit(solution)/shard_map/ppermute | solution.py:60
  35.9 21.9 %collective-permute-start.14 = (bf16[128,768]{1,0:T(8,128)(2,1)S(1)}, bf16[128,768]{1,0:T(8,128)(2,1)S(1)}, u32[]{:S(2)}, u32[]{:S(2)}) collective-permute-start(bf16[128,768]{1,0:T(8,128)(2,1)S(1)} %collective-permute-done.11.refs_8_), channel_id=1, source_target_pairs={{0,8},{2,10},{4,12},{6,14},{8,16},{10,18},{12,20},{14,22},{16,24},... | collective-permute-start | bytes 589832 | tf_op jit(solution)/shard_map/ppermute | solution.py:65
  36.8 21.1 %collective-permute-start.15 = (bf16[128,768]{1,0:T(8,128)(2,1)S(1)}, bf16[128,768]{1,0:T(8,128)(2,1)S(1)}, u32[]{:S(2)}, u32[]{:S(2)}) collective-permute-start(bf16[128,768]{1,0:T(8,128)(2,1)S(1)} %collective-permute-done.11.refs_8_), channel_id=1, source_target_pairs={{0,4},{2,6},{4,0},{6,2},{8,12},{10,14},{12,8},{14,10},{16,20},{18,... | collective-permute-start | bytes 589832 | tf_op jit(solution)/shard_map/ppermute | solution.py:70
  39.5 37.4 %copy-start.14 = (s32[16,4]{0,1:T(4,128)S(1)}, s32[16,4]{0,1:T(4,128)}, u32[]{:S(2)}) copy-start(s32[16,4]{0,1:T(4,128)} %param.10) | copy-start | bytes 772
  53.9 37.3 %all-to-all-start = ((bf16[8,272,128]{2,1,0:T(8,128)(2,1)}), bf16[8,272,128]{2,1,0:T(8,128)(2,1)S(1)}, u32[]{:S(2)}, u32[]{:S(2)}) async-start(bf16[8,272,128]{2,1,0:T(8,128)(2,1)} %get-tuple-element.67), calls=%async_computation | async-start | bytes 1114112 | tf_op jit(solution)/shard_map/all_to_all | solution.py:734
  57.9 23.3 %copy-start.19 = (bf16[128,768]{1,0:T(8,128)(2,1)}, bf16[128,768]{1,0:T(8,128)(2,1)S(1)}, u32[]{:S(2)}) copy-start(bf16[128,768]{1,0:T(8,128)(2,1)S(1)} %collective-permute-done.14.refs_10_) | copy-start | bytes 589828
  57.9 23.3 %copy-start.20 = (bf16[128,768]{1,0:T(8,128)(2,1)}, bf16[128,768]{1,0:T(8,128)(2,1)S(1)}, u32[]{:S(2)}) copy-start(bf16[128,768]{1,0:T(8,128)(2,1)S(1)} %collective-permute-done.15.refs_9_) | copy-start | bytes 589828
  57.9 17.5 %collective-permute-start.16 = (bf16[128,768]{1,0:T(8,128)(2,1)S(1)}, bf16[128,768]{1,0:T(8,128)(2,1)S(1)}, u32[]{:S(2)}, u32[]{:S(2)}) collective-permute-start(bf16[128,768]{1,0:T(8,128)(2,1)S(1)} %collective-permute-done.14.refs_10_), channel_id=1, source_target_pairs={{0,8},{2,10},{4,12},{6,14},{8,16},{10,18},{12,20},{14,22},{16,24},... | collective-permute-start | bytes 589832 | tf_op jit(solution)/shard_map/ppermute | solution.py:65
  60.1 15.3 %collective-permute-start.17 = (bf16[128,768]{1,0:T(8,128)(2,1)S(1)}, bf16[128,768]{1,0:T(8,128)(2,1)S(1)}, u32[]{:S(2)}, u32[]{:S(2)}) collective-permute-start(bf16[128,768]{1,0:T(8,128)(2,1)S(1)} %collective-permute-done.14.refs_10_), channel_id=1, source_target_pairs={{0,4},{2,6},{4,0},{6,2},{8,12},{10,14},{12,8},{14,10},{16,20},{18,... | collective-permute-start | bytes 589832 | tf_op jit(solution)/shard_map/ppermute | solution.py:70
  75.4 5.8 %collective-permute-start.18 = (bf16[128,768]{1,0:T(8,128)(2,1)S(1)}, bf16[128,768]{1,0:T(8,128)(2,1)S(1)}, u32[]{:S(2)}, u32[]{:S(2)}) collective-permute-start(bf16[128,768]{1,0:T(8,128)(2,1)S(1)} %collective-permute-done.16.refs_12_), channel_id=1, source_target_pairs={{0,4},{2,6},{4,0},{6,2},{8,12},{10,14},{12,8},{14,10},{16,20},{18,... | collective-permute-start | bytes 589832 | tf_op jit(solution)/shard_map/ppermute | solution.py:70
  92.1 19.8 %all-to-all-start.1 = ((bf16[8,256,128]{2,1,0:T(8,128)(2,1)}), bf16[8,256,128]{2,1,0:T(8,128)(2,1)S(1)}, u32[]{:S(2)}, u32[]{:S(2)}) async-start(bf16[8,256,128]{2,1,0:T(8,128)(2,1)} %scan_states.1), calls=%async_computation.1 | async-start | bytes 1048576 | tf_op jit(solution)/shard_map/all_to_all | solution.py:734
  118.8 8.7 %collective-permute-start.19 = (bf16[512,256]{1,0:T(8,128)(2,1)S(1)}, bf16[512,256]{1,0:T(8,128)(2,1)S(1)}, u32[]{:S(2)}, u32[]{:S(2)}) collective-permute-start(bf16[512,256]{1,0:T(8,128)(2,1)S(1)} %get-tuple-element.94), channel_id=1, source_target_pairs={{0,1},{1,0},{2,3},{3,2},{4,5},{5,4},{6,7},{7,6},{8,9},{9,8},{10,11... | collective-permute-start | bytes 786440 | tf_op jit(solution)/shard_map/ppermute | solution.py:88
  120.4 7.1 %collective-permute-start.20 = (bf16[512,256]{1,0:T(8,128)(2,1)S(1)}, bf16[512,256]{1,0:T(8,128)(2,1)S(1)}, u32[]{:S(2)}, u32[]{:S(2)}) collective-permute-start(bf16[512,256]{1,0:T(8,128)(2,1)S(1)} %get-tuple-element.95), channel_id=1, source_target_pairs={{0,2},{2,0},{4,6},{6,4},{8,10},{10,8},{12,14},{14,12},{16,18},{18,... | collective-permute-start | bytes 786440 | tf_op jit(solution)/shard_map/ppermute | solution.py:60
  120.4 9.7 %collective-permute-start.21 = (bf16[512,256]{1,0:T(8,128)(2,1)S(1)}, bf16[512,256]{1,0:T(8,128)(2,1)S(1)}, u32[]{:S(2)}, u32[]{:S(2)}) collective-permute-start(bf16[512,256]{1,0:T(8,128)(2,1)S(1)} %get-tuple-element.96), channel_id=1, source_target_pairs={{0,3},{1,2},{2,1},{3,0},{4,7},{5,6},{6,5},{7,4},{8,11},{9,10},{10,... | collective-permute-start | bytes 786440 | tf_op jit(solution)/shard_map/ppermute | solution.py:96
  (23 other events, 118.3 us)

commit v7 on v6

--- a/solution.py
+++ b/solution.py
@@ -19,13 +19,12 @@
 
 vmem = pl.BlockSpec(memory_space=pltpu.VMEM)
 smem = pl.BlockSpec(memory_space=pltpu.SMEM)
-hbm = pl.BlockSpec(memory_space=pltpu.HBM)
 
 f32 = jnp.float32
 bf16 = jnp.bfloat16
 
 
-def params(mib=28):
+def params(mib=16):
     return pltpu.CompilerParams(vmem_limit_bytes=mib << 20)
 
 
@@ -109,28 +108,6 @@
             return self.decay(refs, 0, pair, g)
         one, two = (self.decay(refs, slot, pair, g) for slot in range(2))
         return jnp.where(self.core() == 0, two, one)
-
-
-class Copies:
-    room = 48
-
-    def __init__(self, sems):
-        self.sems, self.made = sems, []
-
-    def start(self, src, dst):
-        copy = pltpu.make_async_copy(src, dst, self.sems.at[len(self.made)])
-        copy.start()
-        self.made.append(copy)
-        return copy
-
-    @staticmethod
-    def scratch():
-        return pltpu.SemaphoreType.DMA((Copies.room,))
-
-
-def finish(copies):
-    for copy in copies:
-        copy.wait()
 
 
 def halves(shape, one, two):
@@ -304,30 +281,17 @@
     decay_refs, refs = refs[: plan.merge], refs[plan.merge :]
     part_ref, rest_ref, refs = refs[0], refs[1], refs[2:]
     frame_refs, refs = refs[: plan.merge * parts], refs[plan.merge * parts :]
-    w_refs, refs = refs[:-13], refs[-13:]
-    x_out, v_out, u_out, total_ref, rest, raw, normed, w, turned, x, v, u, sems = refs
-    copies = Copies(sems)
-    tokens = rest.shape[0]
+    w_refs, refs = refs[:-7], refs[-7:]
+    x_ref, v_ref, u_ref, total_ref, normed, w, turned = refs
+    tokens = rest_ref.shape[0]
     block = tokens // groups
     step = 256
     here = step // block
     cols = plan.pairs * LANES
 
-    weights = []
     for ref, rows in plan.places(w_refs):
-        weights.append(copies.start(ref.at[:, cols:], turned.at[rows]))
-        weights.append(copies.start(ref.at[:, :cols], w.at[rows]))
-    arriving, picking = [], [copies.start(rest_ref, rest)]
-    for s in range(plan.merge):
-        at = 0
-        for ref in frame_refs[s * parts : (s + 1) * parts]:
-            size = ref.shape[0]
-            arriving.append(copies.start(ref, raw.at[s, at : at + size, :]))
-            at += size
-        mine = slice(s * tokens, (s + 1) * tokens)
-        picking.append(copies.start(part_ref.at[mine], x.at[mine]))
-
-    finish(weights)
+        w[rows, :] = ref[:, :cols]
+        turned[rows, :] = ref[:, cols:]
     maps = jnp.concatenate(
         [
             turned[at : at + LANES, :].astype(f32).T.astype(bf16)
@@ -337,20 +301,18 @@
     )
     lane = lax.div(lax.broadcasted_iota(jnp.int32, (LANES, step), 1), block)
 
-    leaving = []
     for s in range(plan.merge):
-        finish(arriving[s * parts : (s + 1) * parts])
-        normalise(raw.at[s], normed, 0)
-        if s == 0:
-            finish(picking)
+        at = 0
+        for ref in frame_refs[s * parts : (s + 1) * parts]:
+            normalise(ref, normed.at[s], at)
+            at += ref.shape[0]
         for at in range(0, tokens, step):
             there = slice(s * tokens + at, s * tokens + at + step)
-            more = jnp.dot(rest[at : at + step, :], normed[...], preferred_element_type=f32)
-            placed = x[there, :] + more.astype(bf16)
-            x[there, :] = placed
-            leaving.append(copies.start(x.at[there], x_out.at[there]))
+            more = jnp.dot(rest_ref[at : at + step, :], normed[s], preferred_element_type=f32)
+            placed = part_ref[there, :] + more.astype(bf16)
+            x_ref[there, :] = placed
             values = jnp.dot(placed, w[...], preferred_element_type=f32).astype(bf16)
-            v[there, :] = values
+            v_ref[there, :] = values
             b = lax.dot_general(
                 maps, placed, (((1,), (1,)), ((), ())), preferred_element_type=f32
             )
@@ -365,13 +327,10 @@
                 for i in range(here):
                     m = outer[i * 2 * N : (i + 1) * 2 * N]
                     row = ((at // block + i) * plan.pairs + p) * N
-                    u[s, row : row + N, :] = halves((N, LANES), m[:N], m[N:])
-        mine = slice(s * tokens, (s + 1) * tokens)
-        leaving.append(copies.start(v.at[mine], v_out.at[mine]))
-        leaving.append(copies.start(u.at[s], u_out.at[s]))
+                    u_ref[s, row : row + N, :] = halves((N, LANES), m[:N], m[N:])
 
     peers = total_ref.shape[0]
-    share = u.shape[1] // peers
+    share = u_ref.shape[1] // peers
     items = max(1, share // N)
     size = min(N, share)
     first = plan.core() == 0
@@ -380,10 +339,10 @@
             row = d * share + i * N
             p, g = row // N % plan.pairs, row // N // plan.pairs
             last = plan.last_decay(decay_refs, p, g)
-            total = u[plan.merge - 1, row : row + size, :]
+            total = u_ref[plan.merge - 1, row : row + size, :]
             product = last
             if plan.merge == 2:
-                before = u[0, row : row + size, :]
+                before = u_ref[0, row : row + size, :]
                 total = jnp.where(first, last, 1.0) * before + jnp.where(first, 1.0, last) * total
                 product = plan.decay(decay_refs, 0, p, g) * plan.decay(decay_refs, 1, p, g)
             total_ref[d, i * size : (i + 1) * size, :] = total.astype(bf16)
@@ -392,7 +351,6 @@
                 at = share + n * items + i
                 total_ref[d, at : at + 1, :] = piece
                 product = product - piece.astype(f32)
-    finish(leaving)
 
 
 def share_rows(share):
@@ -407,8 +365,7 @@
     share = rows // plan.chips
     return pl.pallas_call(
         functools.partial(update_kernel, plan, groups, len(frames) // plan.merge),
-        in_specs=[smem] * plan.merge + [hbm] * (2 + len(frames) + len(weights)),
-        out_specs=(hbm,) * 3 + (vmem,),
+        in_specs=[smem] * plan.merge + [vmem] * (2 + len(frames) + len(weights)),
         out_shape=(
             jax.ShapeDtypeStruct((every, width), bf16),
             jax.ShapeDtypeStruct((every, cols), bf16),
@@ -416,17 +373,11 @@
             jax.ShapeDtypeStruct((plan.chips, share_rows(share), LANES), bf16),
         ),
         scratch_shapes=[
-            pltpu.VMEM((tokens, count), bf16),
             pltpu.VMEM((plan.merge, count, width), bf16),
-            pltpu.VMEM((count, width), bf16),
             pltpu.VMEM((width, cols), bf16),
             pltpu.VMEM((width, cols), bf16),
-            pltpu.VMEM((every, width), bf16),
-            pltpu.VMEM((every, cols), bf16),
-            pltpu.VMEM((plan.merge, rows, LANES), f32),
-            Copies.scratch(),
         ],
-        compiler_params=params(60),
+        compiler_params=params(),
         cost_estimate=cost(4 * every * width * (2 * cols + count), 6 * every * width),
         name="project_updates",
     )(*decays, part, rest, *frames, *weights)
@@ -452,7 +403,7 @@
     return pl.pallas_call(
         functools.partial(scan_kernel, plan),
         out_shape=jax.ShapeDtypeStruct((plan.chips, share, LANES), bf16),
-        compiler_params=params(24),
+        compiler_params=params(),
         cost_estimate=cost(2 * update.size, 4 * update.size),
         name="scan_states",
     )(update)
@@ -461,22 +412,16 @@
 def attend_kernel(plan, slot, *refs):
     lists_ref, refs = refs[0], refs[1:]
     decay_refs, refs = refs[: plan.merge], refs[plan.merge :]
-    x_in, v_in, u_in, w_refs, refs = refs[0], refs[1], refs[2], refs[3:-13], refs[-13:]
-    a_out, c_out, x, v, u, w, q_ref, k_ref, wide_v, e_ref, a, c_ref, sems = refs
-    copies = Copies(sems)
-    tokens = x.shape[0]
+    x_ref, v_ref, u_ref, w_refs, refs = refs[0], refs[1], refs[2], refs[3:-7], refs[-7:]
+    a, c_ref, w, q_ref, k_ref, wide_v, e_ref = refs
+    tokens = a.shape[0]
     groups, chosen = lists_ref.shape
     block = tokens // groups
     step = 256
     per = step // block
-    mine = slice(slot * tokens, (slot + 1) * tokens)
-
-    weights = [copies.start(ref, w.at[rows]) for ref, rows in plan.places(w_refs)]
-    arriving = []
-    for at in range(0, tokens, step):
-        from_ = slice(slot * tokens + at, slot * tokens + at + step)
-        arriving.append(copies.start(x_in.at[from_], x.at[at : at + step]))
-    later = [copies.start(v_in.at[mine], v), copies.start(u_in, u)]
+    first_row = slot * tokens
+    for ref, rows in plan.places(w_refs):
+        w[rows, :] = ref[...]
 
     same = lax.div(lax.broadcasted_iota(jnp.int32, (2 * LANES, 2 * LANES), 0), HD) == lax.div(
         lax.broadcasted_iota(jnp.int32, (2 * LANES, 2 * LANES), 1), HD
@@ -492,11 +437,10 @@
         return values * lax.rsqrt(total * (1.0 / HD) + epsilon)
 
     half = first_half((step, LANES))
-    finish(weights)
     for at in range(0, tokens, step):
-        arriving[at // step].wait()
         rows = slice(at, at + step)
-        every = jnp.dot(x[rows, :], w[...], preferred_element_type=f32).astype(bf16)
+        mine = slice(first_row + at, first_row + at + step)
+        every = jnp.dot(x_ref[mine, :], w[...], preferred_element_type=f32).astype(bf16)
         for p in range(plan.pairs):
             cols = slice(p * LANES, (p + 1) * LANES)
             first = 3 * p * LANES
@@ -509,10 +453,8 @@
             for i in range(per):
                 part = slice(i * block, (i + 1) * block)
                 q_ref[p, at // block + i] = jnp.concatenate([one[part], two[part]], axis=0)
-    leaving = [copies.start(c_ref, c_out)]
-    finish(later)
     for p in range(plan.pairs):
-        wide_v[p, :, :LANES] = v[:, p * LANES : (p + 1) * LANES]
+        wide_v[p, :, :LANES] = v_ref[first_row : first_row + tokens, p * LANES : (p + 1) * LANES]
         wide_v[p, :, LANES:] = jnp.ones((tokens, LANES), bf16)
 
     scale = math.log2(math.e) / math.sqrt(HD)
@@ -540,16 +482,12 @@
         for p in range(plan.pairs):
             cols = slice(p * LANES, (p + 1) * LANES)
             items = slice((g * plan.pairs + p) * N, (g * plan.pairs + p + 1) * N)
-            state = u[slot, items, :]
+            state = u_ref[slot, items, :]
             if plan.merge == 2:
                 last = plan.last_decay(decay_refs, p, g)
                 last = jnp.where(plan.core() == slot, 0.0, last)
-                state = state + last * u[1 - slot, items, :]
+                state = state + last * u_ref[1 - slot, items, :]
             a[rows, cols] = a[rows, cols] + read_out(c_ref[rows, cols], state, block)
-        if (g + 1) % per == 0:
-            done = slice((g + 1 - per) * block, (g + 1) * block)
-            leaving.append(copies.start(a.at[done], a_out.at[done]))
-    finish(leaving)
 
 
 def attend(plan, slot, lists, decays, x, v, weights, updates):
@@ -560,26 +498,19 @@
     cols = plan.pairs * LANES
     return pl.pallas_call(
         functools.partial(attend_kernel, plan, slot),
-        in_specs=[smem] * (1 + plan.merge) + [hbm] * (3 + len(weights)),
-        out_specs=(hbm,) * 2,
+        in_specs=[smem] * (1 + plan.merge) + [vmem] * (3 + len(weights)),
         scratch_shapes=[
-            pltpu.VMEM((tokens, width), bf16),
-            pltpu.VMEM((tokens, cols), bf16),
-            pltpu.VMEM(updates.shape, f32),
             pltpu.VMEM((width, 3 * cols), bf16),
             pltpu.VMEM((plan.pairs, groups, 2 * block, LANES), bf16),
             pltpu.VMEM((plan.pairs, tokens, LANES), bf16),
             pltpu.VMEM((plan.pairs, tokens, 2 * LANES), bf16),
             pltpu.VMEM((plan.pairs, groups, 2 * block, chosen * block), bf16),
-            pltpu.VMEM((tokens, cols), f32),
-            pltpu.VMEM((tokens, cols), bf16),
-            Copies.scratch(),
         ],
         out_shape=(
             jax.ShapeDtypeStruct((tokens, cols), f32),
             jax.ShapeDtypeStruct((tokens, cols), bf16),
         ),
-        compiler_params=params(60),
+        compiler_params=params(),
         cost_estimate=cost(
             6 * tokens * width * 3 * cols,
             4 * (tokens * width + 5 * width * cols + updates.size),
@@ -640,7 +571,7 @@
         in_specs=[smem] * plan.merge + [vmem] * (2 * plan.merge + 2),
         out_shape=(jax.ShapeDtypeStruct((tokens // plan.peers, width), bf16),) * count,
         scratch_shapes=[pltpu.VMEM((tokens, plan.merge * width), bf16)],
-        compiler_params=params(24),
+        compiler_params=params(),
         cost_estimate=cost(4 * tokens * tokens * width, 2 * tokens * tokens + 16 * tokens * width),
         name="mix",
     )(*decays, *attended, *readers, state, back)
@@ -669,7 +600,7 @@
     return pl.pallas_call(
         functools.partial(out_kernel, plan),
         out_shape=jax.ShapeDtypeStruct((local, width), bf16),
-        compiler_params=params(24),
+        compiler_params=params(),
         cost_estimate=cost(2 * local * w.size, 2 * (w.size + 2 * local * width)),
         name="project_out",
     )(w, *parts)
@@ -691,33 +622,35 @@
     ids = jnp.roll(block_ids, -me * local_tokens)
     ids, rates = lax.optimization_barrier((ids, rates))
     pick, rest = pick_tokens(ids, local_tokens, groups)
-    part = place_tokens(plan, pick, owns)
     if plan.ringed:
         def step(block, with_):
             return lax.optimization_barrier((plan.round(block), plan.cross(block), with_))[:2]
 
-        def late_step(tie):
-            late[-1], _ = lax.optimization_barrier((late[-1], tie))
-            if len(late) < plan.along:
-                passed, crossed = step(late[-1], [])
-                late.append(passed)
-            else:
-                crossed = plan.cross(late[-1])
-            late_crossed.append(crossed)
-
-        early, early_crossed, late, late_crossed = [blocks[0]], [], [blocks[1]], []
-        beside = [pick, part]
+        early, late, crossed = [blocks[0]], [blocks[1]], [[], []]
+        part = None
         for k in range(plan.along - 1):
-            passed, crossed = step(early[-1], beside[k : k + 1])
+            passed, across = step(late[-1], [])
+            late.append(passed)
+            crossed[1].append(across)
+            if part is None:
+                pick, _ = lax.optimization_barrier((pick, passed))
+                part = place_tokens(plan, pick, owns)
+            beside = [[pick], [part], [late[-1]]][min(k, 2)]
+            passed, across = step(early[-1], beside)
             early.append(passed)
-            early_crossed.append(crossed)
-        early_crossed.append(plan.cross(early[-1]))
-        late_step(early[min(1, plan.along - 1)])
-        arriving, _ = lax.optimization_barrier((arriving, (early_crossed[-1], late[-1])))
-        if plan.along > 1:
-            late_step(early[min(2, plan.along - 1)])
-        early = [b for pair in zip(early, early_crossed) for b in pair]
+            crossed[0].append(across)
+        crossed[0].append(plan.cross(early[-1]))
+        crossed[1].append(plan.cross(late[-1]))
+        arriving, _ = lax.optimization_barrier((arriving, crossed[0][-1]))
+        rest, _ = lax.optimization_barrier((rest, late[-1]))
+        early, late = (
+            [b for pair in zip(blocks, across) for b in pair]
+            for blocks, across in zip((early, late), crossed)
+        )
+        if part is None:
+            part = place_tokens(plan, pick, owns)
     else:
+        part = place_tokens(plan, pick, owns)
         early, late = (
             [lax.all_gather(b, "tm", axis=0, tiled=True, axis_index_groups=plan.groups())]
             for b in blocks
@@ -725,11 +658,6 @@
     if plan.merge == 2:
         arriving = arriving + [plan.swap(chunk) for chunk in arriving]
     x, v, updates, total = project_updates(plan, rates, part, rest, arriving, early, groups)
-    if plan.ringed:
-        while len(late_crossed) < plan.along:
-            late_step(total)
-        late = [b for pair in zip(late, late_crossed) for b in pair]
-
     def exchange(blocks):
         return lax.all_to_all(
             blocks, "tm", split_axis=0, concat_axis=0, tiled=True,

time: 133 us -> 139 us (1.045)
  local copies, waits for them, and re-layouts: 11.3 us -> 27.3 us
  Pallas kernels: 45.9 us -> 34.1 us
    unnamed x63 -> x71, local copies, waits for them, and re-layouts: 11.1 us -> 27 us
    ppermute x6, waiting for transfers between devices: 21.2 us -> 5.65 us  [round(): return lax.ppermute(block, 'tm', pairs)]
    ppermute x8, waiting for transfers between devices: 6.49 us -> 18.9 us  [cross(): return lax.ppermute(block, 'tm', pairs)]
    pallas_call x2, Pallas kernels: 18.7 us -> 11.1 us  [attend(): pl.pallas_call(functools.partial(attend_kernel, plan, slot), in_specs=[sm...]
    ppermute x5, waiting for transfers between devices: 1.72 us -> 6.41 us  [swap(): return lax.ppermute(block, 'tm', [(t, t ^ 1) for t in range(self.frames)])]
    pallas_call x1, Pallas kernels: 14.4 us -> 10.1 us  [project_updates(): pl.pallas_call(functools.partial(update_kernel, plan, groups, len(frames)...]
    ppermute x8, starting transfers between devices: 9.55 us -> 12.1 us  [cross(): return lax.ppermute(block, 'tm', pairs)]
    ppermute x2, starting transfers between devices: 4.56 us -> 3.1 us  [to_peer(): return lax.ppermute(block, 'head', pairs)]
  transfers between devices with their start and end apart: 24 -> 24, of which waited for: 12 -> 11; matrix products, arithmetic and copies ran while one was open for 1% -> 1% of each run, Pallas kernels for 31% -> 13%
where the time goes in v7:
time: 139 us; the launch traced here: 138 us
  waiting for transfers between devices  40.6 us (29%)
  starting transfers between devices  34.8 us (25%)
  Pallas kernels  34.1 us (25%)
  local copies, waits for them, and re-layouts  27.3 us (20%)
    unnamed x71, local copies, waits for them, and re-layouts  27 us
    ppermute x8, waiting for transfers between devices, cross(): return lax.ppermute(block, 'tm', pairs)  18.9 us
    ppermute x8, starting transfers between devices, cross(): return lax.ppermute(block, 'tm', pairs)  12.1 us
    pallas_call x2, Pallas kernels, attend(): pl.pallas_call(functools.partial(attend_kernel, plan, slot), in_specs=[sm...  11.1 us
    pallas_call x1, Pallas kernels, project_updates(): pl.pallas_call(functools.partial(update_kernel, plan, groups, len(frames)...  10.1 us
    all_to_all x2, starting transfers between devices, exchange(): lax.all_to_all(blocks, 'tm', split_axis=0, concat_axis=0, tiled=True, axi...  9.9 us
    ppermute x6, starting transfers between devices, round(): return lax.ppermute(block, 'tm', pairs)  8.52 us
    ppermute x2, waiting for transfers between devices, to_peer(): return lax.ppermute(block, 'head', pairs)  7.11 us
  transfers between devices with their start and end apart: 24, of which 11 were waited for; matrix products, arithmetic and copies ran while one was open for 1% of the time, Pallas kernels for 13%

profile of v7, /device:TPU:0, one launch (start us, length us, event | category | flops | bytes accessed | tf_op | source)
XLA Modules:
  0.0 137.7 jit_solution(4313146059231635282)
XLA Ops:
  0.5 2.9 %collective-permute-done.1.refs_1_ = bf16[64,2560]{1,0:T(8,128)(2,1)S(1)} collective-permute-done((bf16[64,2560]{1,0:T(8,128)(2,1)}, bf16[64,2560]{1,0:T(8,128)(2,1)S(1)}, u32[]{:S(2)}, u32[]{:S(2)}) %collective-permute-start.1) | collective-permute-done | bytes 327712 | tf_op jit(solution)/shard_map/ppermute | solution.py:59
  4.6 3.0 %collective-permute-start.2 = (bf16[128,768]{1,0:T(8,128)(2,1)S(1)}, bf16[128,768]{1,0:T(8,128)(2,1)S(1)}, u32[]{:S(2)}, u32[]{:S(2)}) collective-permute-start(bf16[128,768]{1,0:T(8,128)(2,1)S(1)} %get-tuple-element.53.refs_6_), channel_id=1, source_target_pairs={{0,8},{2,10},{4,12},{6,14},{8,16},{10,18},{12,20},{14,22},{16,24},... | collective-permute-start | bytes 589832 | tf_op jit(solution)/shard_map/ppermute | solution.py:64
  10.6 1.6 %collective-permute-start.10 = (bf16[128,512]{1,0:T(8,128)(2,1)S(1)}, bf16[128,512]{1,0:T(8,128)(2,1)}, u32[]{:S(2)}, u32[]{:S(2)}) collective-permute-start(bf16[128,512]{1,0:T(8,128)(2,1)S(1)} %get-tuple-element.60.refs_6_), channel_id=1, source_target_pairs={{0,8},{2,10},{4,12},{6,14},{8,16},{10,18},{12,20},{14,22},{16,24},... | collective-permute-start | bytes 393224 | tf_op jit(solution)/shard_map/ppermute | solution.py:64
  12.1 3.1 %collective-permute-done.2.refs_8_ = bf16[128,768]{1,0:T(8,128)(2,1)S(1)} collective-permute-done((bf16[128,768]{1,0:T(8,128)(2,1)S(1)}, bf16[128,768]{1,0:T(8,128)(2,1)S(1)}, u32[]{:S(2)}, u32[]{:S(2)}) %collective-permute-start.2) | collective-permute-done | bytes 196640 | tf_op jit(solution)/shard_map/ppermute | solution.py:64
  16.6 1.7 %collective-permute-start.6 = (bf16[128,768]{1,0:T(8,128)(2,1)S(1)}, bf16[128,768]{1,0:T(8,128)(2,1)S(1)}, u32[]{:S(2)}, u32[]{:S(2)}) collective-permute-start(bf16[128,768]{1,0:T(8,128)(2,1)S(1)} %collective-permute-done.2.refs_8_), channel_id=1, source_target_pairs={{0,4},{2,6},{4,0},{6,2},{8,12},{10,14},{12,8},{14,10},{16,20},{18,... | collective-permute-start | bytes 589832 | tf_op jit(solution)/shard_map/ppermute | solution.py:69
  20.7 5.7 %collective-permute-done.11.refs_7_ = bf16[128,512]{1,0:T(8,128)(2,1)S(1)} collective-permute-done((bf16[128,512]{1,0:T(8,128)(2,1)S(1)}, bf16[128,512]{1,0:T(8,128)(2,1)S(1)}, u32[]{:S(2)}, u32[]{:S(2)}) %collective-permute-start.11) | collective-permute-done | bytes 131104 | tf_op jit(solution)/shard_map/ppermute | solution.py:69
  27.1 1.8 %collective-permute-start.13 = (bf16[128,512]{1,0:T(8,128)(2,1)}, bf16[128,512]{1,0:T(8,128)(2,1)S(1)}, u32[]{:S(2)}, u32[]{:S(2)}) collective-permute-start(bf16[128,512]{1,0:T(8,128)(2,1)} %collective-permute-done.10.refs_8_), channel_id=1, source_target_pairs={{0,4},{2,6},{4,0},{6,2},{8,12},{10,14},{12,8},{14,10},{16,20},{18,... | collective-permute-start | bytes 393224 | tf_op jit(solution)/shard_map/ppermute | solution.py:69
  32.2 3.6 %place_tokens.1.refs_2_ = bf16[2048,1024]{1,0:T(8,128)(2,1)S(1)} custom-call(bf16[1024,512]{1,0:T(8,128)(2,1)S(1)} %get-tuple-element.55.pick_ref, bf16[512,1024]{1,0:T(8,128)(2,1)S(1)} %bitcast.16, bf16[512,1024]{1,0:T(8,128)(2,1)S(1)} %collective-permute-done.4.refs_1_), custom_call_target="tpu_custom_call" | custom-call | flops 4294967296 | bytes 6291456 | tf_op jit(solution)/shard_map/place_tokens/pallas_call | solution.py:270
  35.9 1.8 %collective-permute-start.14 = (bf16[128,512]{1,0:T(8,128)(2,1)S(1)}, bf16[128,512]{1,0:T(8,128)(2,1)S(1)}, u32[]{:S(2)}, u32[]{:S(2)}) collective-permute-start(bf16[128,512]{1,0:T(8,128)(2,1)S(1)} %collective-permute-done.12.refs_10_), channel_id=1, source_target_pairs={{0,8},{2,10},{4,12},{6,14},{8,16},{10,18},{12,20},{14,22},{16,24},... | collective-permute-start | bytes 393224 | tf_op jit(solution)/shard_map/ppermute | solution.py:64
  37.7 1.7 %collective-permute-start.15 = (bf16[128,512]{1,0:T(8,128)(2,1)S(1)}, bf16[128,512]{1,0:T(8,128)(2,1)S(1)}, u32[]{:S(2)}, u32[]{:S(2)}) collective-permute-start(bf16[128,512]{1,0:T(8,128)(2,1)S(1)} %collective-permute-done.12.refs_10_), channel_id=1, source_target_pairs={{0,4},{2,6},{4,0},{6,2},{8,12},{10,14},{12,8},{14,10},{16,20},{18,... | collective-permute-start | bytes 393224 | tf_op jit(solution)/shard_map/ppermute | solution.py:69
  40.2 2.5 %collective-permute-done.14.refs_12_ = bf16[128,512]{1,0:T(8,128)(2,1)S(1)} collective-permute-done((bf16[128,512]{1,0:T(8,128)(2,1)S(1)}, bf16[128,512]{1,0:T(8,128)(2,1)S(1)}, u32[]{:S(2)}, u32[]{:S(2)}) %collective-permute-start.14) | collective-permute-done | bytes 131104 | tf_op jit(solution)/shard_map/ppermute | solution.py:64
  43.0 2.0 %collective-permute-start.16 = (bf16[128,512]{1,0:T(8,128)(2,1)S(1)}, bf16[128,512]{1,0:T(8,128)(2,1)S(1)}, u32[]{:S(2)}, u32[]{:S(2)}) collective-permute-start(bf16[128,512]{1,0:T(8,128)(2,1)S(1)} %collective-permute-done.14.refs_12_), channel_id=1, source_target_pairs={{0,4},{2,6},{4,0},{6,2},{8,12},{10,14},{12,8},{14,10},{16,20},{18,... | collective-permute-start | bytes 393224 | tf_op jit(solution)/shard_map/ppermute | solution.py:69
  45.0 2.9 %collective-permute-done.16.refs_13_ = bf16[128,512]{1,0:T(8,128)(2,1)S(1)} collective-permute-done((bf16[128,512]{1,0:T(8,128)(2,1)S(1)}, bf16[128,512]{1,0:T(8,128)(2,1)S(1)}, u32[]{:S(2)}, u32[]{:S(2)}) %collective-permute-start.16) | collective-permute-done | bytes 131104 | tf_op jit(solution)/shard_map/ppermute | solution.py:69
  48.0 2.6 %collective-permute-done.17.refs_5_ = bf16[512,1024]{1,0:T(8,128)(2,1)S(1)} collective-permute-done((bf16[512,1024]{1,0:T(8,128)(2,1)S(1)}, bf16[512,1024]{1,0:T(8,128)(2,1)S(1)}, u32[]{:S(2)}, u32[]{:S(2)}) %collective-permute-start.17) | collective-permute-done | bytes 1048608 | tf_op jit(solution)/shard_map/ppermute | solution.py:59
  50.6 10.1 %project_updates.1 = (bf16[2048,1024]{1,0:T(8,128)(2,1)S(1)}, bf16[2048,256]{1,0:T(8,128)(2,1)S(1)}, f32[2,2048,128]{2,1,0:T(8,128)S(1)}, bf16[8,272,128]{2,1,0:T(8,128)(2,1)}) custom-call(f32[8,16]{1,0:T(8,128)S(1)} %bitcast.10, f32[8,16]{1,0:T(8,128)S(1)} %collective-permute-done.refs_1_.refs_2_, bf16[2048,1024]{1,0:T(8,128)(2,1)S(1)} %place_tokens.1.refs_2_, ...), custom_call_target="tpu_custom_call" | custom-call | flops 8589934592 | bytes 12582912 | tf_op jit(solution)/shard_map/project_updates/pallas_call | solution.py:366
  60.7 2.0 %copy-done.25 = bf16[2048,1024]{1,0:T(8,128)(2,1)} copy-done((bf16[2048,1024]{1,0:T(8,128)(2,1)}, bf16[2048,1024]{1,0:T(8,128)(2,1)S(1)}, u32[]{:S(2)}) %copy-start.25) | copy-done | bytes 4194328
  65.1 4.6 %all-to-all-start = ((bf16[8,272,128]{2,1,0:T(8,128)(2,1)}), bf16[8,272,128]{2,1,0:T(8,128)(2,1)S(1)}, u32[]{:S(2)}, u32[]{:S(2)}) async-start(bf16[8,272,128]{2,1,0:T(8,128)(2,1)} %get-tuple-element.68), calls=%async_computation | async-start | bytes 1114112 | tf_op jit(solution)/shard_map/all_to_all | solution.py:662
  69.7 2.0 %collective-permute-start.18 = (bf16[128,768]{1,0:T(8,128)(2,1)}, bf16[128,768]{1,0:T(8,128)(2,1)S(1)}, u32[]{:S(2)}, u32[]{:S(2)}) collective-permute-start(bf16[128,768]{1,0:T(8,128)(2,1)} %copy-done.18), channel_id=1, source_target_pairs={{0,4},{2,6},{4,0},{6,2},{8,12},{10,14},{12,8},{14,10},{16,20},{18,... | collective-permute-start | bytes 589832 | tf_op jit(solution)/shard_map/ppermute | solution.py:69
  71.8 10.0 %collective-permute-done.18.refs_13_ = bf16[128,768]{1,0:T(8,128)(2,1)S(1)} collective-permute-done((bf16[128,768]{1,0:T(8,128)(2,1)}, bf16[128,768]{1,0:T(8,128)(2,1)S(1)}, u32[]{:S(2)}, u32[]{:S(2)}) %collective-permute-start.18) | collective-permute-done | bytes 196640 | tf_op jit(solution)/shard_map/ppermute | solution.py:69
  82.7 2.2 %copy-done.26 = bf16[2048,1024]{1,0:T(8,128)(2,1)S(1)} copy-done((bf16[2048,1024]{1,0:T(8,128)(2,1)S(1)}, bf16[2048,1024]{1,0:T(8,128)(2,1)}, u32[]{:S(2)}) %copy-start.26) | copy-done | bytes 4194328
  84.9 1.6 %copy-done.29 = f32[2,2048,128]{2,1,0:T(8,128)S(1)} copy-done((f32[2,2048,128]{2,1,0:T(8,128)S(1)}, f32[2,2048,128]{2,1,0:T(8,128)}, u32[]{:S(2)}) %copy-start.29) | copy-done | bytes 2097176
  87.7 5.5 %attend.2 = (f32[1024,256]{1,0:T(8,128)S(1)}, bf16[1024,256]{1,0:T(8,128)(2,1)S(1)}) custom-call(s32[16,4]{1,0:T(8,128)S(1)} %copy.9.refs_0_, f32[8,16]{1,0:T(8,128)S(1)} %bitcast.11, f32[8,16]{1,0:T(8,128)S(1)} %collective-permute-done.refs_1_.refs_2_, bf16[2048,1024]{1,0:T(8,128)(2,1)S(1)} %copy-done.26, bf16[2048,256]{1,0:T(8,128)(2,1)S(1)} %copy-done.32, ...), custom_call_target="tpu_custom_call" | custom-call | flops 4831838208 | bytes 11534336 | tf_op jit(solution)/shard_map/attend/pallas_call | solution.py:499
  96.1 5.3 %all-to-all-start.1 = ((bf16[8,256,128]{2,1,0:T(8,128)(2,1)}), bf16[8,256,128]{2,1,0:T(8,128)(2,1)S(1)}, u32[]{:S(2)}, u32[]{:S(2)}) async-start(bf16[8,256,128]{2,1,0:T(8,128)(2,1)} %scan_states.1), calls=%async_computation.1 | async-start | bytes 1048576 | tf_op jit(solution)/shard_map/all_to_all | solution.py:662
  101.4 2.2 %copy-done.27 = bf16[2048,1024]{1,0:T(8,128)(2,1)S(1)} copy-done((bf16[2048,1024]{1,0:T(8,128)(2,1)S(1)}, bf16[2048,1024]{1,0:T(8,128)(2,1)}, u32[]{:S(2)}) %copy-start.27) | copy-done | bytes 4194328
  103.6 1.6 %copy-done.30 = f32[2,2048,128]{2,1,0:T(8,128)S(1)} copy-done((f32[2,2048,128]{2,1,0:T(8,128)S(1)}, f32[2,2048,128]{2,1,0:T(8,128)}, u32[]{:S(2)}) %copy-start.30) | copy-done | bytes 2097176
  106.4 5.5 %attend.3 = (f32[1024,256]{1,0:T(8,128)S(1)}, bf16[1024,256]{1,0:T(8,128)(2,1)S(1)}) custom-call(s32[16,4]{1,0:T(8,128)S(1)} %copy.9.refs_0_, f32[8,16]{1,0:T(8,128)S(1)} %bitcast.12, f32[8,16]{1,0:T(8,128)S(1)} %collective-permute-done.refs_1_.refs_2_, bf16[2048,1024]{1,0:T(8,128)(2,1)S(1)} %copy-done.27, bf16[2048,256]{1,0:T(8,128)(2,1)S(1)} %copy-done.33, ...), custom_call_target="tpu_custom_call" | custom-call | flops 4831838208 | bytes 11534336 | tf_op jit(solution)/shard_map/attend/pallas_call | solution.py:499
  113.9 2.9 %back_tokens.1.refs_7_ = bf16[1024,1024]{1,0:T(8,128)(2,1)S(1)} custom-call(s32[1024,1]{1,0:T(8,128)S(1)} %copy.11.ids_ref), custom_call_target="tpu_custom_call" | custom-call | flops 268435456 | bytes 2097152 | tf_op jit(solution)/shard_map/back_tokens/pallas_call | solution.py:245
  121.4 2.3 %mix.1 = (bf16[512,256]{1,0:T(8,128)(2,1)S(1)}, bf16[512,256]{1,0:T(8,128)(2,1)S(1)}, bf16[512,256]{1,0:T(8,128)(2,1)S(1)}, bf16[512,256]{1,0:T(8,128)(2,1)S(1)}) custom-call(f32[8,16]{1,0:T(8,128)S(1)} %bitcast.13, f32[8,16]{1,0:T(8,128)S(1)} %collective-permute-done.refs_1_.refs_2_, f32[1024,256]{1,0:T(8,128)S(1)} %copy-done.2, f32[1024,256]{1,0:T(8,128)S(1)} %copy-done.4, ...), custom_call_target="tpu_custom_call" | custom-call | flops 1073741824 | bytes 6291456 | tf_op jit(solution)/shard_map/mix/pallas_call | solution.py:569
  123.7 1.6 %collective-permute-start.19 = (bf16[512,256]{1,0:T(8,128)(2,1)S(1)}, bf16[512,256]{1,0:T(8,128)(2,1)S(1)}, u32[]{:S(2)}, u32[]{:S(2)}) collective-permute-start(bf16[512,256]{1,0:T(8,128)(2,1)S(1)} %get-tuple-element.90), channel_id=1, source_target_pairs={{0,1},{1,0},{2,3},{3,2},{4,5},{5,4},{6,7},{7,6},{8,9},{9,8},{10,11... | collective-permute-start | bytes 786440 | tf_op jit(solution)/shard_map/ppermute | solution.py:87
  125.9 7.1 %collective-permute-done.19.refs_1_ = bf16[512,256]{1,0:T(8,128)(2,1)S(1)} collective-permute-done((bf16[512,256]{1,0:T(8,128)(2,1)S(1)}, bf16[512,256]{1,0:T(8,128)(2,1)S(1)}, u32[]{:S(2)}, u32[]{:S(2)}) %collective-permute-start.19) | collective-permute-done | bytes 262176 | tf_op jit(solution)/shard_map/ppermute | solution.py:87
  133.0 2.5 %collective-permute-done.21.refs_3_ = bf16[512,256]{1,0:T(8,128)(2,1)S(1)} collective-permute-done((bf16[512,256]{1,0:T(8,128)(2,1)S(1)}, bf16[512,256]{1,0:T(8,128)(2,1)S(1)}, u32[]{:S(2)}, u32[]{:S(2)}) %collective-permute-start.21) | collective-permute-done | bytes 262176 | tf_op jit(solution)/shard_map/ppermute | solution.py:95
  135.5 2.2 %project_out.1 = bf16[512,1024]{1,0:T(8,128)(2,1)} custom-call(bf16[1024,1024]{1,0:T(8,128)(2,1)S(1)} %copy-done, bf16[512,256]{1,0:T(8,128)(2,1)S(1)} %get-tuple-element.89.refs_0_, bf16[512,256]{1,0:T(8,128)(2,1)S(1)} %collective-permute-done.19.refs_1_, bf16[512,256]{1,0:T(8,128)(2,1)S(1)} %collective-permute-done.20.refs_2_, ...), custom_call_target="tpu_custom_call" | custom-call | flops 1073741824 | bytes 4194304 | tf_op jit(solution)/shard_map/project_out/pallas_call | solution.py:600
  (99 shorter events, 29.1 us)
Async XLA Ops:
  0.0 30.5 %collective-permute-start.4 = (bf16[512,1024]{1,0:T(8,128)(2,1)}, bf16[512,1024]{1,0:T(8,128)(2,1)S(1)}, u32[]{:S(2)}, u32[]{:S(2)}) collective-permute-start(bf16[512,1024]{1,0:T(8,128)(2,1)} %bitcast.14), channel_id=1, source_target_pairs={{0,2},{2,0},{4,6},{6,4},{8,10},{10,8},{12,14},{14,12},{16,18},{18,... | collective-permute-start | bytes 3145736 | tf_op jit(solution)/shard_map/ppermute | solution.py:59
  0.5 3.0 %collective-permute-start.1 = (bf16[64,2560]{1,0:T(8,128)(2,1)}, bf16[64,2560]{1,0:T(8,128)(2,1)S(1)}, u32[]{:S(2)}, u32[]{:S(2)}) collective-permute-start(bf16[64,2560]{1,0:T(8,128)(2,1)} %refs_0_.3), channel_id=1, source_target_pairs={{0,2},{2,0},{4,6},{6,4},{8,10},{10,8},{12,14},{14,12},{16,18},{18,... | collective-permute-start | bytes 983048 | tf_op jit(solution)/shard_map/ppermute | solution.py:59
  4.6 10.7 %collective-permute-start.2 = (bf16[128,768]{1,0:T(8,128)(2,1)S(1)}, bf16[128,768]{1,0:T(8,128)(2,1)S(1)}, u32[]{:S(2)}, u32[]{:S(2)}) collective-permute-start(bf16[128,768]{1,0:T(8,128)(2,1)S(1)} %get-tuple-element.53.refs_6_), channel_id=1, source_target_pairs={{0,8},{2,10},{4,12},{6,14},{8,16},{10,18},{12,20},{14,22},{16,24},... | collective-permute-start | bytes 589832 | tf_op jit(solution)/shard_map/ppermute | solution.py:64
  7.6 7.7 %collective-permute-start.3 = (bf16[128,768]{1,0:T(8,128)(2,1)S(1)}, bf16[128,768]{1,0:T(8,128)(2,1)S(1)}, u32[]{:S(2)}, u32[]{:S(2)}) collective-permute-start(bf16[128,768]{1,0:T(8,128)(2,1)S(1)} %get-tuple-element.53.refs_6_), channel_id=1, source_target_pairs={{0,4},{2,6},{4,0},{6,2},{8,12},{10,14},{12,8},{14,10},{16,20},{18,... | collective-permute-start | bytes 589832 | tf_op jit(solution)/shard_map/ppermute | solution.py:69
  9.0 36.0 %collective-permute-start.9 = (bf16[512,1024]{1,0:T(8,128)(2,1)}, bf16[512,1024]{1,0:T(8,128)(2,1)S(1)}, u32[]{:S(2)}, u32[]{:S(2)}) collective-permute-start(bf16[512,1024]{1,0:T(8,128)(2,1)} %bitcast.15), channel_id=1, source_target_pairs={{0,1},{1,0},{2,3},{3,2},{4,5},{5,4},{6,7},{7,6},{8,9},{9,8},{10,11... | collective-permute-start | bytes 3145736 | tf_op jit(solution)/shard_map/ppermute | solution.py:87
  10.6 7.8 %collective-permute-start.10 = (bf16[128,512]{1,0:T(8,128)(2,1)S(1)}, bf16[128,512]{1,0:T(8,128)(2,1)}, u32[]{:S(2)}, u32[]{:S(2)}) collective-permute-start(bf16[128,512]{1,0:T(8,128)(2,1)S(1)} %get-tuple-element.60.refs_6_), channel_id=1, source_target_pairs={{0,8},{2,10},{4,12},{6,14},{8,16},{10,18},{12,20},{14,22},{16,24},... | collective-permute-start | bytes 393224 | tf_op jit(solution)/shard_map/ppermute | solution.py:64
  15.3 1.4 collective-permute-start
  15.3 66.5 %copy-start.12 = (bf16[128,768]{1,0:T(8,128)(2,1)}, bf16[128,768]{1,0:T(8,128)(2,1)S(1)}, u32[]{:S(2)}) copy-start(bf16[128,768]{1,0:T(8,128)(2,1)S(1)} %collective-permute-done.3.refs_7_) | copy-start | bytes 589828
  15.3 11.9 %collective-permute-start.5 = (bf16[128,768]{1,0:T(8,128)(2,1)S(1)}, bf16[128,768]{1,0:T(8,128)(2,1)S(1)}, u32[]{:S(2)}, u32[]{:S(2)}) collective-permute-start(bf16[128,768]{1,0:T(8,128)(2,1)S(1)} %collective-permute-done.2.refs_8_), channel_id=1, source_target_pairs={{0,8},{2,10},{4,12},{6,14},{8,16},{10,18},{12,20},{14,22},{16,24},... | collective-permute-start | bytes 589832 | tf_op jit(solution)/shard_map/ppermute | solution.py:64
  16.6 12.3 %collective-permute-start.6 = (bf16[128,768]{1,0:T(8,128)(2,1)S(1)}, bf16[128,768]{1,0:T(8,128)(2,1)S(1)}, u32[]{:S(2)}, u32[]{:S(2)}) collective-permute-start(bf16[128,768]{1,0:T(8,128)(2,1)S(1)} %collective-permute-done.2.refs_8_), channel_id=1, source_target_pairs={{0,4},{2,6},{4,0},{6,2},{8,12},{10,14},{12,8},{14,10},{16,20},{18,... | collective-permute-start | bytes 589832 | tf_op jit(solution)/shard_map/ppermute | solution.py:69
  18.4 8.0 %collective-permute-start.11 = (bf16[128,512]{1,0:T(8,128)(2,1)S(1)}, bf16[128,512]{1,0:T(8,128)(2,1)S(1)}, u32[]{:S(2)}, u32[]{:S(2)}) collective-permute-start(bf16[128,512]{1,0:T(8,128)(2,1)S(1)} %get-tuple-element.60.refs_6_), channel_id=1, source_target_pairs={{0,4},{2,6},{4,0},{6,2},{8,12},{10,14},{12,8},{14,10},{16,20},{18,... | collective-permute-start | bytes 393224 | tf_op jit(solution)/shard_map/ppermute | solution.py:69
  20.7 29.9 %copy-start.10 = (f32[1,8,16]{2,1,0:T(8,128)S(1)}, f32[1,8,16]{2,1,0:T(8,128)}, u32[]{:S(2)}) copy-start(f32[1,8,16]{2,1,0:T(8,128)} %param.11) | copy-start | bytes 1540
  27.1 8.8 %collective-permute-start.12 = (bf16[128,512]{1,0:T(8,128)(2,1)}, bf16[128,512]{1,0:T(8,128)(2,1)S(1)}, u32[]{:S(2)}, u32[]{:S(2)}) collective-permute-start(bf16[128,512]{1,0:T(8,128)(2,1)} %collective-permute-done.10.refs_8_), channel_id=1, source_target_pairs={{0,8},{2,10},{4,12},{6,14},{8,16},{10,18},{12,20},{14,22},{16,24},... | collective-permute-start | bytes 393224 | tf_op jit(solution)/shard_map/ppermute | solution.py:64
  27.1 54.6 %copy-start.14 = (bf16[128,768]{1,0:T(8,128)(2,1)}, bf16[128,768]{1,0:T(8,128)(2,1)S(1)}, u32[]{:S(2)}) copy-start(bf16[128,768]{1,0:T(8,128)(2,1)S(1)} %collective-permute-done.5.refs_10_) | copy-start | bytes 589828
  27.1 8.8 %collective-permute-start.13 = (bf16[128,512]{1,0:T(8,128)(2,1)}, bf16[128,512]{1,0:T(8,128)(2,1)S(1)}, u32[]{:S(2)}, u32[]{:S(2)}) collective-permute-start(bf16[128,512]{1,0:T(8,128)(2,1)} %collective-permute-done.10.refs_8_), channel_id=1, source_target_pairs={{0,4},{2,6},{4,0},{6,2},{8,12},{10,14},{12,8},{14,10},{16,20},{18,... | collective-permute-start | bytes 393224 | tf_op jit(solution)/shard_map/ppermute | solution.py:69
  28.9 10.6 %collective-permute-start.7 = (bf16[128,768]{1,0:T(8,128)(2,1)S(1)}, bf16[128,768]{1,0:T(8,128)(2,1)S(1)}, u32[]{:S(2)}, u32[]{:S(2)}) collective-permute-start(bf16[128,768]{1,0:T(8,128)(2,1)S(1)} %collective-permute-done.5.refs_10_), channel_id=1, source_target_pairs={{0,8},{2,10},{4,12},{6,14},{8,16},{10,18},{12,20},{14,22},{16,24},... | collective-permute-start | bytes 589832 | tf_op jit(solution)/shard_map/ppermute | solution.py:64
  30.5 9.0 %collective-permute-start.8 = (bf16[128,768]{1,0:T(8,128)(2,1)S(1)}, bf16[128,768]{1,0:T(8,128)(2,1)S(1)}, u32[]{:S(2)}, u32[]{:S(2)}) collective-permute-start(bf16[128,768]{1,0:T(8,128)(2,1)S(1)} %collective-permute-done.5.refs_10_), channel_id=1, source_target_pairs={{0,4},{2,6},{4,0},{6,2},{8,12},{10,14},{12,8},{14,10},{16,20},{18,... | collective-permute-start | bytes 589832 | tf_op jit(solution)/shard_map/ppermute | solution.py:69
  32.2 18.4 %copy-start.24 = (bf16[128,512]{1,0:T(8,128)(2,1)S(1)}, bf16[128,512]{1,0:T(8,128)(2,1)}, u32[]{:S(2)}) copy-start(bf16[128,512]{1,0:T(8,128)(2,1)} %copy-done.23) | copy-start | bytes 393220
  35.9 6.8 %collective-permute-start.14 = (bf16[128,512]{1,0:T(8,128)(2,1)S(1)}, bf16[128,512]{1,0:T(8,128)(2,1)S(1)}, u32[]{:S(2)}, u32[]{:S(2)}) collective-permute-start(bf16[128,512]{1,0:T(8,128)(2,1)S(1)} %collective-permute-done.12.refs_10_), channel_id=1, source_target_pairs={{0,8},{2,10},{4,12},{6,14},{8,16},{10,18},{12,20},{14,22},{16,24},... | collective-permute-start | bytes 393224 | tf_op jit(solution)/shard_map/ppermute | solution.py:64
  37.7 5.2 %collective-permute-start.15 = (bf16[128,512]{1,0:T(8,128)(2,1)S(1)}, bf16[128,512]{1,0:T(8,128)(2,1)S(1)}, u32[]{:S(2)}, u32[]{:S(2)}) collective-permute-start(bf16[128,512]{1,0:T(8,128)(2,1)S(1)} %collective-permute-done.12.refs_10_), channel_id=1, source_target_pairs={{0,4},{2,6},{4,0},{6,2},{8,12},{10,14},{12,8},{14,10},{16,20},{18,... | collective-permute-start | bytes 393224 | tf_op jit(solution)/shard_map/ppermute | solution.py:69
  39.5 21.3 %copy-start.18 = (bf16[128,768]{1,0:T(8,128)(2,1)}, bf16[128,768]{1,0:T(8,128)(2,1)S(1)}, u32[]{:S(2)}) copy-start(bf16[128,768]{1,0:T(8,128)(2,1)S(1)} %collective-permute-done.7.refs_12_) | copy-start | bytes 589828
  43.0 5.0 %collective-permute-start.16 = (bf16[128,512]{1,0:T(8,128)(2,1)S(1)}, bf16[128,512]{1,0:T(8,128)(2,1)S(1)}, u32[]{:S(2)}, u32[]{:S(2)}) collective-permute-start(bf16[128,512]{1,0:T(8,128)(2,1)S(1)} %collective-permute-done.14.refs_12_), channel_id=1, source_target_pairs={{0,4},{2,6},{4,0},{6,2},{8,12},{10,14},{12,8},{14,10},{16,20},{18,... | collective-permute-start | bytes 393224 | tf_op jit(solution)/shard_map/ppermute | solution.py:69
  47.9 2.7 %collective-permute-start.17 = (bf16[512,1024]{1,0:T(8,128)(2,1)S(1)}, bf16[512,1024]{1,0:T(8,128)(2,1)S(1)}, u32[]{:S(2)}, u32[]{:S(2)}) collective-permute-start(bf16[512,1024]{1,0:T(8,128)(2,1)S(1)} %collective-permute-done.9.refs_4_), channel_id=1, source_target_pairs={{0,2},{2,0},{4,6},{6,4},{8,10},{10,8},{12,14},{14,12},{16,18},{18,... | collective-permute-start | bytes 3145736 | tf_op jit(solution)/shard_map/ppermute | solution.py:59
  48.0 23.7 %copy-start.34 = (s32[16,4]{0,1:T(4,128)S(1)}, s32[16,4]{0,1:T(4,128)}, u32[]{:S(2)}) copy-start(s32[16,4]{0,1:T(4,128)} %param.10) | copy-start | bytes 772
  48.0 33.8 %copy-start.17 = (bf16[128,768]{1,0:T(8,128)(2,1)S(1)}, bf16[128,768]{1,0:T(8,128)(2,1)}, u32[]{:S(2)}) copy-start(bf16[128,768]{1,0:T(8,128)(2,1)} %copy-done.16) | copy-start | bytes 589828
  48.0 33.8 %copy-start.22 = (bf16[128,768]{1,0:T(8,128)(2,1)S(1)}, bf16[128,768]{1,0:T(8,128)(2,1)}, u32[]{:S(2)}) copy-start(bf16[128,768]{1,0:T(8,128)(2,1)} %copy-done.21) | copy-start | bytes 589828
  65.1 30.0 %all-to-all-start = ((bf16[8,272,128]{2,1,0:T(8,128)(2,1)}), bf16[8,272,128]{2,1,0:T(8,128)(2,1)S(1)}, u32[]{:S(2)}, u32[]{:S(2)}) async-start(bf16[8,272,128]{2,1,0:T(8,128)(2,1)} %get-tuple-element.68), calls=%async_computation | async-start | bytes 1114112 | tf_op jit(solution)/shard_map/all_to_all | solution.py:662
  69.7 12.1 %collective-permute-start.18 = (bf16[128,768]{1,0:T(8,128)(2,1)}, bf16[128,768]{1,0:T(8,128)(2,1)S(1)}, u32[]{:S(2)}, u32[]{:S(2)}) collective-permute-start(bf16[128,768]{1,0:T(8,128)(2,1)} %copy-done.18), channel_id=1, source_target_pairs={{0,4},{2,6},{4,0},{6,2},{8,12},{10,14},{12,8},{14,10},{16,20},{18,... | collective-permute-start | bytes 589832 | tf_op jit(solution)/shard_map/ppermute | solution.py:69
  96.1 20.7 %all-to-all-start.1 = ((bf16[8,256,128]{2,1,0:T(8,128)(2,1)}), bf16[8,256,128]{2,1,0:T(8,128)(2,1)S(1)}, u32[]{:S(2)}, u32[]{:S(2)}) async-start(bf16[8,256,128]{2,1,0:T(8,128)(2,1)} %scan_states.1), calls=%async_computation.1 | async-start | bytes 1048576 | tf_op jit(solution)/shard_map/all_to_all | solution.py:662
  123.7 9.3 %collective-permute-start.19 = (bf16[512,256]{1,0:T(8,128)(2,1)S(1)}, bf16[512,256]{1,0:T(8,128)(2,1)S(1)}, u32[]{:S(2)}, u32[]{:S(2)}) collective-permute-start(bf16[512,256]{1,0:T(8,128)(2,1)S(1)} %get-tuple-element.90), channel_id=1, source_target_pairs={{0,1},{1,0},{2,3},{3,2},{4,5},{5,4},{6,7},{7,6},{8,9},{9,8},{10,11... | collective-permute-start | bytes 786440 | tf_op jit(solution)/shard_map/ppermute | solution.py:87
  125.3 7.7 %collective-permute-start.20 = (bf16[512,256]{1,0:T(8,128)(2,1)S(1)}, bf16[512,256]{1,0:T(8,128)(2,1)S(1)}, u32[]{:S(2)}, u32[]{:S(2)}) collective-permute-start(bf16[512,256]{1,0:T(8,128)(2,1)S(1)} %get-tuple-element.91), channel_id=1, source_target_pairs={{0,2},{2,0},{4,6},{6,4},{8,10},{10,8},{12,14},{14,12},{16,18},{18,... | collective-permute-start | bytes 786440 | tf_op jit(solution)/shard_map/ppermute | solution.py:59
  125.3 10.2 %collective-permute-start.21 = (bf16[512,256]{1,0:T(8,128)(2,1)S(1)}, bf16[512,256]{1,0:T(8,128)(2,1)S(1)}, u32[]{:S(2)}, u32[]{:S(2)}) collective-permute-start(bf16[512,256]{1,0:T(8,128)(2,1)S(1)} %get-tuple-element.92), channel_id=1, source_target_pairs={{0,3},{1,2},{2,1},{3,0},{4,7},{5,6},{6,5},{7,4},{8,11},{9,10},{10,... | collective-permute-start | bytes 786440 | tf_op jit(solution)/shard_map/ppermute | solution.py:95
  (27 other events, 66.9 us)

commit v8 on v6

--- a/solution.py
+++ b/solution.py
@@ -19,13 +19,14 @@
 
 vmem = pl.BlockSpec(memory_space=pltpu.VMEM)
 smem = pl.BlockSpec(memory_space=pltpu.SMEM)
+
 hbm = pl.BlockSpec(memory_space=pltpu.HBM)
 
 f32 = jnp.float32
 bf16 = jnp.bfloat16
 
 
-def params(mib=28):
+def params(mib=16):
     return pltpu.CompilerParams(vmem_limit_bytes=mib << 20)
 
 
@@ -115,12 +116,12 @@
     room = 48
 
     def __init__(self, sems):
-        self.sems, self.made = sems, []
+        self.sems, self.count = sems, 0
 
     def start(self, src, dst):
-        copy = pltpu.make_async_copy(src, dst, self.sems.at[len(self.made)])
+        copy = pltpu.make_async_copy(src, dst, self.sems.at[self.count])
         copy.start()
-        self.made.append(copy)
+        self.count += 1
         return copy
 
     @staticmethod
@@ -190,11 +191,9 @@
     lax.fori_loop(0, part.shape[0] // step, norm, 0)
 
 
-def pick_kernel(groups, ids_ref, own_ref, rest_ref):
+def rank_kernel(groups, ids_ref, row_ref, col_ref):
     tokens = ids_ref.shape[1]
-    local = own_ref.shape[1]
     block = tokens // groups
-    step = 128
     label = lax.broadcasted_iota(jnp.int32, (groups, tokens), 0)
     held = label == ids_ref[...]
     held_bf = jnp.where(held, 1.0, 0.0).astype(bf16)
@@ -209,143 +208,108 @@
     count = jnp.concatenate(counts, axis=1)
     rank = jnp.sum(
         jnp.where(held, count + (label * block).astype(f32), 0.0), axis=0, keepdims=True
-    ).astype(jnp.int32)
-
-    def place(c, _):
-        at = pl.multiple_of(c * step, step)
-        pick = (lax.broadcasted_iota(jnp.int32, (step, tokens), 0) + at) == rank
-        pick = jnp.where(pick, 1.0, 0.0).astype(bf16)
-        own_ref[pl.ds(at, step), :] = pick[:, :local]
-        rest_ref[pl.ds(at, step), :] = pick[:, local:]
-        return 0
-
-    lax.fori_loop(0, tokens // step, place, 0)
-
-
-def pick_tokens(ids, local, groups):
+    )
+    row_ref[...] = rank
+    for at in range(0, tokens, LANES):
+        wide = jnp.broadcast_to(rank[:, at : at + LANES], (LANES, LANES))
+        col_ref[at : at + LANES, :] = wide.T
+
+
+def rank_tokens(ids, groups):
     tokens = ids.shape[0]
     return pl.pallas_call(
-        functools.partial(pick_kernel, groups),
+        functools.partial(rank_kernel, groups),
         out_shape=(
-            jax.ShapeDtypeStruct((tokens, local), bf16),
-            jax.ShapeDtypeStruct((tokens, tokens - local), bf16),
+            jax.ShapeDtypeStruct((1, tokens), f32),
+            jax.ShapeDtypeStruct((tokens, LANES), f32),
         ),
         compiler_params=params(),
-        cost_estimate=cost(32 * tokens * tokens, 2 * tokens * tokens),
-        name="pick_tokens",
+        cost_estimate=cost(0, 4 * tokens),
+        name="rank_tokens",
     )(ids.reshape(1, tokens))
 
 
-def back_kernel(groups, ids_ref, back_ref):
-    tokens = back_ref.shape[0]
-    block = tokens // groups
-    step = 128
-    lane = lax.broadcasted_iota(jnp.int32, (tokens, 128), 1)
-    held = jnp.where(lane == ids_ref[...], 1.0, 0.0).astype(bf16)
-
-    def place(c, _):
-        at = pl.multiple_of(c * step, step)
-        before = lax.broadcasted_iota(jnp.int32, (step, tokens), 1) < (
-            lax.broadcasted_iota(jnp.int32, (step, tokens), 0) + at
-        )
-        count = jnp.dot(
-            jnp.where(before, 1.0, 0.0).astype(bf16), held, preferred_element_type=f32
-        )
-        lane = lax.broadcasted_iota(jnp.int32, (step, 128), 1)
-        mine = lane == ids_ref[pl.ds(at, step), :]
-        rank = jnp.sum(
-            jnp.where(mine, count + (lane * block).astype(f32), 0.0), axis=1, keepdims=True
-        ).astype(jnp.int32)
-        pick = lax.broadcasted_iota(jnp.int32, (step, tokens), 1) == rank
-        back_ref[pl.ds(at, step), :] = jnp.where(pick, 1.0, 0.0).astype(bf16)
-        return 0
-
-    lax.fori_loop(0, tokens // step, place, 0)
-
-
-def back_tokens(ids, groups):
-    tokens = ids.shape[0]
-    return pl.pallas_call(
-        functools.partial(back_kernel, groups),
-        out_shape=jax.ShapeDtypeStruct((tokens, tokens), bf16),
-        compiler_params=params(),
-        cost_estimate=cost(256 * tokens * tokens, 2 * tokens * tokens),
-        name="back_tokens",
-    )(ids.reshape(tokens, 1))
-
-
-def place_kernel(merge, pick_ref, *refs):
+def picks(rank, at, rows):
+    places = lax.broadcasted_iota(jnp.int32, (rows, rank.shape[1]), 0) + at
+    return jnp.where(places.astype(f32) == rank, 1.0, 0.0).astype(bf16)
+
+
+def place_kernel(merge, rank_ref, *refs):
     frame_refs, x_ref, normed = refs[:merge], refs[-2], refs[-1]
-    tokens = pick_ref.shape[0]
+    tokens = rank_ref.shape[1]
+    local = frame_refs[0].shape[0]
     step = 256
     for s in range(merge):
         normalise(frame_refs[s], normed.at[s], 0)
-        for at in range(0, tokens, step):
+    for at in range(0, tokens, step):
+        pick = picks(rank_ref[:, :local], at, step)
+        for s in range(merge):
             x_ref[s * tokens + at : s * tokens + at + step, :] = jnp.dot(
-                pick_ref[at : at + step, :], normed[s], preferred_element_type=f32
+                pick, normed[s], preferred_element_type=f32
             ).astype(bf16)
 
 
-def place_tokens(plan, pick, frames):
-    tokens, count = pick.shape
-    width = frames[0].shape[1]
-    every = plan.merge * tokens
+def place_tokens(plan, rank, frames):
+    tokens = rank.shape[1]
+    local, width = frames[0].shape
     return pl.pallas_call(
         functools.partial(place_kernel, plan.merge),
-        out_shape=jax.ShapeDtypeStruct((every, width), bf16),
-        scratch_shapes=[pltpu.VMEM((plan.merge, count, width), bf16)],
+        out_shape=jax.ShapeDtypeStruct((plan.merge * tokens, width), bf16),
+        scratch_shapes=[pltpu.VMEM((plan.merge, local, width), bf16)],
         compiler_params=params(),
-        cost_estimate=cost(4 * every * count * width, 6 * tokens * width),
+        cost_estimate=cost(0, 4 * tokens),
         name="place_tokens",
-    )(pick, *frames)
+    )(rank, *frames)
 
 
 def update_kernel(plan, groups, parts, *refs):
     decay_refs, refs = refs[: plan.merge], refs[plan.merge :]
-    part_ref, rest_ref, refs = refs[0], refs[1], refs[2:]
+    rank_ref, part_ref, refs = refs[0], refs[1], refs[2:]
     frame_refs, refs = refs[: plan.merge * parts], refs[plan.merge * parts :]
     w_refs, refs = refs[:-13], refs[-13:]
-    x_out, v_out, u_out, total_ref, rest, raw, normed, w, turned, x, v, u, sems = refs
+    x_out, v_out, local_out, total_ref, raw, normed, w, turned, x, v, u, left, sems = refs
     copies = Copies(sems)
-    tokens = rest.shape[0]
+    tokens = rank_ref.shape[1]
+    count = raw.shape[1]
     block = tokens // groups
     step = 256
     here = step // block
     cols = plan.pairs * LANES
 
-    weights = []
-    for ref, rows in plan.places(w_refs):
-        weights.append(copies.start(ref.at[:, cols:], turned.at[rows]))
-        weights.append(copies.start(ref.at[:, :cols], w.at[rows]))
-    arriving, picking = [], [copies.start(rest_ref, rest)]
+    arriving, partly, weights = [], [], []
     for s in range(plan.merge):
         at = 0
         for ref in frame_refs[s * parts : (s + 1) * parts]:
             size = ref.shape[0]
             arriving.append(copies.start(ref, raw.at[s, at : at + size, :]))
             at += size
-        mine = slice(s * tokens, (s + 1) * tokens)
-        picking.append(copies.start(part_ref.at[mine], x.at[mine]))
-
-    finish(weights)
-    maps = jnp.concatenate(
-        [
-            turned[at : at + LANES, :].astype(f32).T.astype(bf16)
-            for at in range(0, turned.shape[0], LANES)
-        ],
-        axis=1,
-    )
+        if s == 0:
+            for ref, rows in plan.places(w_refs):
+                weights.append(copies.start(ref.at[:, cols:], turned.at[rows]))
+                weights.append(copies.start(ref.at[:, :cols], w.at[rows]))
+        for at in range(s * tokens, (s + 1) * tokens, step):
+            there = slice(at, at + step)
+            partly.append(copies.start(part_ref.at[there], x.at[there]))
+
     lane = lax.div(lax.broadcasted_iota(jnp.int32, (LANES, step), 1), block)
-
     leaving = []
     for s in range(plan.merge):
         finish(arriving[s * parts : (s + 1) * parts])
         normalise(raw.at[s], normed, 0)
         if s == 0:
-            finish(picking)
+            finish(weights)
+            maps = jnp.concatenate(
+                [
+                    turned[at : at + LANES, :].astype(f32).T.astype(bf16)
+                    for at in range(0, turned.shape[0], LANES)
+                ],
+                axis=1,
+            )
         for at in range(0, tokens, step):
             there = slice(s * tokens + at, s * tokens + at + step)
-            more = jnp.dot(rest[at : at + step, :], normed[...], preferred_element_type=f32)
+            pick = picks(rank_ref[:, tokens - count :], at, step)
+            more = jnp.dot(pick, normed[...], preferred_element_type=f32)
+            partly[there.start // step].wait()
             placed = x[there, :] + more.astype(bf16)
             x[there, :] = placed
             leaving.append(copies.start(x.at[there], x_out.at[there]))
@@ -368,7 +332,6 @@
                     u[s, row : row + N, :] = halves((N, LANES), m[:N], m[N:])
         mine = slice(s * tokens, (s + 1) * tokens)
         leaving.append(copies.start(v.at[mine], v_out.at[mine]))
-        leaving.append(copies.start(u.at[s], u_out.at[s]))
 
     peers = total_ref.shape[0]
     share = u.shape[1] // peers
@@ -378,20 +341,29 @@
     for d in range(peers):
         for i in range(items):
             row = d * share + i * N
+            rows = slice(row, row + size)
             p, g = row // N % plan.pairs, row // N // plan.pairs
-            last = plan.last_decay(decay_refs, p, g)
-            total = u[plan.merge - 1, row : row + size, :]
-            product = last
+            product = last = plan.last_decay(decay_refs, p, g)
             if plan.merge == 2:
-                before = u[0, row : row + size, :]
-                total = jnp.where(first, last, 1.0) * before + jnp.where(first, 1.0, last) * total
+                one, two = u[0, rows, :], u[1, rows, :]
+                one, two = (
+                    one + jnp.where(first, 0.0, last) * two,
+                    two + jnp.where(first, last, 0.0) * one,
+                )
+                left[0, rows, :] = one.astype(bf16)
+                left[1, rows, :] = two.astype(bf16)
+                total = jnp.where(first, two, one)
                 product = plan.decay(decay_refs, 0, p, g) * plan.decay(decay_refs, 1, p, g)
+            else:
+                total = u[0, rows, :]
+                left[0, rows, :] = total.astype(bf16)
             total_ref[d, i * size : (i + 1) * size, :] = total.astype(bf16)
             for n in range(3):
                 piece = product.astype(bf16)
                 at = share + n * items + i
                 total_ref[d, at : at + 1, :] = piece
                 product = product - piece.astype(f32)
+    leaving.append(copies.start(left, local_out))
     finish(leaving)
 
 
@@ -399,24 +371,24 @@
     return share + 16 * -(-3 * max(1, share // N) // 16)
 
 
-def project_updates(plan, decays, part, rest, frames, weights, groups):
+def project_updates(plan, decays, rank, part, frames, weights, groups):
     every, width = part.shape
-    tokens, count = rest.shape
+    tokens = rank.shape[1]
+    count = frames[0].shape[0] * len(frames) // plan.merge
     cols = plan.pairs * LANES
     rows = plan.pairs * groups * N
     share = rows // plan.chips
     return pl.pallas_call(
         functools.partial(update_kernel, plan, groups, len(frames) // plan.merge),
-        in_specs=[smem] * plan.merge + [hbm] * (2 + len(frames) + len(weights)),
+        in_specs=[smem] * plan.merge + [vmem] + [hbm] * (1 + len(frames) + len(weights)),
         out_specs=(hbm,) * 3 + (vmem,),
         out_shape=(
             jax.ShapeDtypeStruct((every, width), bf16),
             jax.ShapeDtypeStruct((every, cols), bf16),
-            jax.ShapeDtypeStruct((plan.merge, rows, LANES), f32),
+            jax.ShapeDtypeStruct((plan.merge, rows, LANES), bf16),
             jax.ShapeDtypeStruct((plan.chips, share_rows(share), LANES), bf16),
         ),
         scratch_shapes=[
-            pltpu.VMEM((tokens, count), bf16),
             pltpu.VMEM((plan.merge, count, width), bf16),
             pltpu.VMEM((count, width), bf16),
             pltpu.VMEM((width, cols), bf16),
@@ -424,12 +396,13 @@
             pltpu.VMEM((every, width), bf16),
             pltpu.VMEM((every, cols), bf16),
             pltpu.VMEM((plan.merge, rows, LANES), f32),
+            pltpu.VMEM((plan.merge, rows, LANES), bf16),
             Copies.scratch(),
         ],
         compiler_params=params(60),
         cost_estimate=cost(4 * every * width * (2 * cols + count), 6 * every * width),
         name="project_updates",
-    )(*decays, part, rest, *frames, *weights)
+    )(*decays, rank, part, *frames, *weights)
 
 
 def scan_kernel(plan, u_ref, s_ref):
@@ -452,31 +425,30 @@
     return pl.pallas_call(
         functools.partial(scan_kernel, plan),
         out_shape=jax.ShapeDtypeStruct((plan.chips, share, LANES), bf16),
-        compiler_params=params(24),
+        compiler_params=params(),
         cost_estimate=cost(2 * update.size, 4 * update.size),
         name="scan_states",
     )(update)
 
 
 def attend_kernel(plan, slot, *refs):
-    lists_ref, refs = refs[0], refs[1:]
-    decay_refs, refs = refs[: plan.merge], refs[plan.merge :]
-    x_in, v_in, u_in, w_refs, refs = refs[0], refs[1], refs[2], refs[3:-13], refs[-13:]
-    a_out, c_out, x, v, u, w, q_ref, k_ref, wide_v, e_ref, a, c_ref, sems = refs
+    lists_ref, x_in, v_in, local_in, refs = refs[0], refs[1], refs[2], refs[3], refs[4:]
+    w_refs, refs = refs[:-13], refs[-13:]
+    a_out, c_out, x, v, local, w, q_ref, k_ref, wide_v, e_ref, a, c_ref, sems = refs
     copies = Copies(sems)
     tokens = x.shape[0]
     groups, chosen = lists_ref.shape
     block = tokens // groups
     step = 256
     per = step // block
-    mine = slice(slot * tokens, (slot + 1) * tokens)
 
     weights = [copies.start(ref, w.at[rows]) for ref, rows in plan.places(w_refs)]
     arriving = []
     for at in range(0, tokens, step):
         from_ = slice(slot * tokens + at, slot * tokens + at + step)
         arriving.append(copies.start(x_in.at[from_], x.at[at : at + step]))
-    later = [copies.start(v_in.at[mine], v), copies.start(u_in, u)]
+    mine = slice(slot * tokens, (slot + 1) * tokens)
+    later = [copies.start(v_in.at[mine], v), copies.start(local_in.at[slot], local)]
 
     same = lax.div(lax.broadcasted_iota(jnp.int32, (2 * LANES, 2 * LANES), 0), HD) == lax.div(
         lax.broadcasted_iota(jnp.int32, (2 * LANES, 2 * LANES), 1), HD
@@ -494,8 +466,8 @@
     half = first_half((step, LANES))
     finish(weights)
     for at in range(0, tokens, step):
+        rows = slice(at, at + step)
         arriving[at // step].wait()
-        rows = slice(at, at + step)
         every = jnp.dot(x[rows, :], w[...], preferred_element_type=f32).astype(bf16)
         for p in range(plan.pairs):
             cols = slice(p * LANES, (p + 1) * LANES)
@@ -540,19 +512,16 @@
         for p in range(plan.pairs):
             cols = slice(p * LANES, (p + 1) * LANES)
             items = slice((g * plan.pairs + p) * N, (g * plan.pairs + p + 1) * N)
-            state = u[slot, items, :]
-            if plan.merge == 2:
-                last = plan.last_decay(decay_refs, p, g)
-                last = jnp.where(plan.core() == slot, 0.0, last)
-                state = state + last * u[1 - slot, items, :]
-            a[rows, cols] = a[rows, cols] + read_out(c_ref[rows, cols], state, block)
+            a[rows, cols] = a[rows, cols] + read_out(
+                c_ref[rows, cols], local[items, :].astype(f32), block
+            )
         if (g + 1) % per == 0:
             done = slice((g + 1 - per) * block, (g + 1) * block)
             leaving.append(copies.start(a.at[done], a_out.at[done]))
     finish(leaving)
 
 
-def attend(plan, slot, lists, decays, x, v, weights, updates):
+def attend(plan, slot, lists, x, v, weights, local):
     every, width = x.shape
     groups, chosen = lists.shape
     tokens = every // plan.merge
@@ -560,12 +529,12 @@
     cols = plan.pairs * LANES
     return pl.pallas_call(
         functools.partial(attend_kernel, plan, slot),
-        in_specs=[smem] * (1 + plan.merge) + [hbm] * (3 + len(weights)),
+        in_specs=[smem] + [hbm] * (3 + len(weights)),
         out_specs=(hbm,) * 2,
         scratch_shapes=[
             pltpu.VMEM((tokens, width), bf16),
             pltpu.VMEM((tokens, cols), bf16),
-            pltpu.VMEM(updates.shape, f32),
+            pltpu.VMEM(local.shape[1:], bf16),
             pltpu.VMEM((width, 3 * cols), bf16),
             pltpu.VMEM((plan.pairs, groups, 2 * block, LANES), bf16),
             pltpu.VMEM((plan.pairs, tokens, LANES), bf16),
@@ -582,11 +551,11 @@
         compiler_params=params(60),
         cost_estimate=cost(
             6 * tokens * width * 3 * cols,
-            4 * (tokens * width + 5 * width * cols + updates.size),
+            4 * (tokens * width + 5 * width * cols + local.size),
             2 * plan.pairs * tokens * chosen * block,
         ),
         name="attend",
-    )(lists, *decays, x, v, updates, *weights)
+    )(lists, x, v, local, *weights)
 
 
 def read_out(readers, state, block):
@@ -599,20 +568,39 @@
 
 def mix_kernel(plan, groups, *refs):
     decay_refs, refs = refs[: plan.merge], refs[plan.merge :]
-    a_refs, refs = refs[: plan.merge], refs[plan.merge :]
-    c_refs, refs = refs[: plan.merge], refs[plan.merge :]
-    s_ref, back_ref, out_refs, mixed = refs[0], refs[1], refs[2:-1], refs[-1]
-    tokens = back_ref.shape[0]
+    a_ins, refs = refs[: plan.merge], refs[plan.merge :]
+    c_ins, refs = refs[: plan.merge], refs[plan.merge :]
+    s_in, rank_in, refs = refs[0], refs[1], refs[2:]
+    out_refs, (a, c, state, rank, mixed, sems) = refs[:-6], refs[-6:]
+    copies = Copies(sems)
+    tokens = rank.shape[0]
     block = tokens // groups
-    width = a_refs[0].shape[1]
+    width = a.shape[2]
+    here = groups // 4
+    many = here * plan.pairs * N
     first = plan.core() == 0
+
+    arriving = []
+    for i in range(4):
+        rows = slice(i * here * block, (i + 1) * here * block)
+        items = slice(i * many, (i + 1) * many)
+        arriving.append([copies.start(s_in.at[items], state.at[items])])
+        for s in range(plan.merge):
+            arriving[-1] += [
+                copies.start(c_ins[s].at[rows], c.at[s, rows, :]),
+                copies.start(a_ins[s].at[rows], a.at[s, rows, :]),
+            ]
+    ranking = copies.start(rank_in, rank)
+
     for g in range(groups):
+        if g % here == 0:
+            finish(arriving[g // here])
         rows = slice(g * block, (g + 1) * block)
         for p in range(plan.pairs):
             cols = slice(p * LANES, (p + 1) * LANES)
             at = (g * plan.pairs + p) * N
-            readers = jnp.concatenate([c[rows, cols] for c in c_refs], axis=0)
-            read = read_out(readers, s_ref[at : at + N, :].astype(f32), block)
+            readers = jnp.concatenate([c[s, rows, cols] for s in range(plan.merge)], axis=0)
+            read = read_out(readers, state[at : at + N, :].astype(f32), block)
             decays = [plan.decay(decay_refs, s, p, g) for s in range(plan.merge)]
             if plan.merge == 2:
                 both = decays[0] * decays[1]
@@ -620,30 +608,54 @@
             for s in range(plan.merge):
                 there = slice(s * width + p * LANES, s * width + (p + 1) * LANES)
                 mixed[rows, there] = (
-                    a_refs[s][rows, cols] + decays[s] * read[s * block : (s + 1) * block]
+                    a[s, rows, cols] + decays[s] * read[s * block : (s + 1) * block]
                 ).astype(bf16)
+
+    ranking.wait()
     local = tokens // plan.peers
-    for k in range(plan.peers):
-        placed = jnp.dot(
-            back_ref[k * local : (k + 1) * local, :], mixed[...], preferred_element_type=f32
-        ).astype(bf16)
+    step = min(256, local)
+    for at in range(0, tokens, step):
+        place = rank[at : at + step, :]
+        pick = jnp.concatenate(
+            [
+                jnp.where(
+                    (lax.broadcasted_iota(jnp.int32, place.shape, 1) + t).astype(f32) == place,
+                    1.0,
+                    0.0,
+                ).astype(bf16)
+                for t in range(0, tokens, LANES)
+            ],
+            axis=1,
+        )
+        placed = jnp.dot(pick, mixed[...], preferred_element_type=f32).astype(bf16)
+        k, to = at // local, at % local
         for s in range(plan.merge):
-            out_refs[s * plan.peers + k][...] = placed[:, s * width : (s + 1) * width]
-
-
-def mix(plan, decays, attended, readers, state, back, groups):
-    tokens = back.shape[0]
+            out_refs[s * plan.peers + k][to : to + step, :] = placed[
+                :, s * width : (s + 1) * width
+            ]
+
+
+def mix(plan, decays, attended, readers, state, rank, groups):
+    tokens = rank.shape[0]
     width = attended[0].shape[1]
     count = plan.merge * plan.peers
     return pl.pallas_call(
         functools.partial(mix_kernel, plan, groups),
-        in_specs=[smem] * plan.merge + [vmem] * (2 * plan.merge + 2),
+        in_specs=[smem] * plan.merge + [hbm] * (2 * plan.merge + 2),
+        out_specs=(vmem,) * count,
         out_shape=(jax.ShapeDtypeStruct((tokens // plan.peers, width), bf16),) * count,
-        scratch_shapes=[pltpu.VMEM((tokens, plan.merge * width), bf16)],
-        compiler_params=params(24),
+        scratch_shapes=[
+            pltpu.VMEM((plan.merge, tokens, width), f32),
+            pltpu.VMEM((plan.merge, tokens, width), bf16),
+            pltpu.VMEM(state.shape, bf16),
+            pltpu.VMEM(rank.shape, f32),
+            pltpu.VMEM((tokens, plan.merge * width), bf16),
+            Copies.scratch(),
+        ],
+        compiler_params=params(56),
         cost_estimate=cost(4 * tokens * tokens * width, 2 * tokens * tokens + 16 * tokens * width),
         name="mix",
-    )(*decays, *attended, *readers, state, back)
+    )(*decays, *attended, *readers, state, rank)
 
 
 def out_kernel(plan, w_ref, *refs):
@@ -669,7 +681,7 @@
     return pl.pallas_call(
         functools.partial(out_kernel, plan),
         out_shape=jax.ShapeDtypeStruct((local, width), bf16),
-        compiler_params=params(24),
+        compiler_params=params(),
         cost_estimate=cost(2 * local * w.size, 2 * (w.size + 2 * local * width)),
         name="project_out",
     )(w, *parts)
@@ -689,46 +701,44 @@
     blocks = reorder(plan, [in_weight] + [plan.swap(in_weight)] * (plan.merge - 1))
 
     ids = jnp.roll(block_ids, -me * local_tokens)
-    ids, rates = lax.optimization_barrier((ids, rates))
-    pick, rest = pick_tokens(ids, local_tokens, groups)
-    part = place_tokens(plan, pick, owns)
     if plan.ringed:
         def step(block, with_):
             return lax.optimization_barrier((plan.round(block), plan.cross(block), with_))[:2]
 
-        def late_step(tie):
-            late[-1], _ = lax.optimization_barrier((late[-1], tie))
-            if len(late) < plan.along:
-                passed, crossed = step(late[-1], [])
-                late.append(passed)
-            else:
-                crossed = plan.cross(late[-1])
-            late_crossed.append(crossed)
-
-        early, early_crossed, late, late_crossed = [blocks[0]], [], [blocks[1]], []
-        beside = [pick, part]
+        early, late, crossed = [blocks[0]], [blocks[1]], [[], []]
+        rank = part = None
         for k in range(plan.along - 1):
-            passed, crossed = step(early[-1], beside[k : k + 1])
+            passed, across = step(early[-1], [[], [], late[-1:]][min(k, 2)] + [part] * (k == 1))
             early.append(passed)
-            early_crossed.append(crossed)
-        early_crossed.append(plan.cross(early[-1]))
-        late_step(early[min(1, plan.along - 1)])
-        arriving, _ = lax.optimization_barrier((arriving, (early_crossed[-1], late[-1])))
-        if plan.along > 1:
-            late_step(early[min(2, plan.along - 1)])
-        early = [b for pair in zip(early, early_crossed) for b in pair]
+            crossed[0].append(across)
+            if k == 0:
+                ids, rates, _ = lax.optimization_barrier((ids, rates, early[-1]))
+                rank, places = rank_tokens(ids, groups)
+            passed, across = step(late[-1], [])
+            late.append(passed)
+            crossed[1].append(across)
+            if k == 0:
+                rank, _ = lax.optimization_barrier((rank, late[-1]))
+                part = place_tokens(plan, rank, owns)
+        crossed[0].append(plan.cross(early[-1]))
+        arriving, _ = lax.optimization_barrier((arriving, crossed[0][-1]))
+        early = [b for pair in zip(early, crossed[0]) for b in pair]
     else:
+        rank = part = None
         early, late = (
             [lax.all_gather(b, "tm", axis=0, tiled=True, axis_index_groups=plan.groups())]
             for b in blocks
         )
+    if part is None:
+        rank, places = rank_tokens(ids, groups)
+        part = place_tokens(plan, rank, owns)
     if plan.merge == 2:
         arriving = arriving + [plan.swap(chunk) for chunk in arriving]
-    x, v, updates, total = project_updates(plan, rates, part, rest, arriving, early, groups)
+    x, v, local, total = project_updates(plan, rates, rank, part, arriving, early, groups)
     if plan.ringed:
-        while len(late_crossed) < plan.along:
-            late_step(total)
-        late = [b for pair in zip(late, late_crossed) for b in pair]
+        late[-1], _ = lax.optimization_barrier((late[-1], total))
+        crossed[1].append(plan.cross(late[-1]))
+        late = [b for pair in zip(late, crossed[1]) for b in pair]
 
     def exchange(blocks):
         return lax.all_to_all(
@@ -736,20 +746,18 @@
             axis_index_groups=plan.groups(),
         )
 
-    share = updates.shape[1] // plan.chips
+    share = local.shape[1] // plan.chips
     arrived = exchange(total)
-    attended = [attend(plan, 0, block_lists, rates, x, v, late, updates)]
+    attended = [attend(plan, 0, block_lists, x, v, late, local)]
     arrived, attended = lax.optimization_barrier((arrived, attended))
     states = scan_states(plan, arrived, share)
     x, states = lax.optimization_barrier((x, states))
     if plan.merge == 2:
-        attended.append(attend(plan, 1, block_lists, rates, x, v, late, updates))
+        attended.append(attend(plan, 1, block_lists, x, v, late, local))
     state = exchange(states).reshape(-1, LANES)
-    ids, attended = lax.optimization_barrier((ids, attended))
-    back = back_tokens(ids, groups)
 
     bases, readers = ([a[i] for a in attended] for i in range(2))
-    mixed = mix(plan, rates, bases, readers, state, back, groups)
+    mixed = mix(plan, rates, bases, readers, state, places, groups)
     features = [
         mixed[0] if s == 0 and k == 0 else plan.to_peer(mixed[s * plan.peers + k], k, s == 1)
         for s in range(plan.merge)

time: 133 us -> 143 us (1.075)
  waiting for transfers between devices: 39.9 us -> 51.9 us
  local copies, waits for them, and re-layouts: 11.3 us -> 9.17 us
    ppermute x8, waiting for transfers between devices: 6.49 us -> 10.6 us  [cross(): return lax.ppermute(block, 'tm', pairs)]
    ppermute x5, waiting for transfers between devices: 1.72 us -> 5.64 us  [swap(): return lax.ppermute(block, 'tm', [(t, t ^ 1) for t in range(self.frames)])]
    all_to_all x2, waiting for transfers between devices: 1.39 us -> 4.75 us  [exchange(): lax.all_to_all(blocks, 'tm', split_axis=0, concat_axis=0, tiled=True, axi...]
    pallas_call x1, Pallas kernels: 2.31 us -> 5.65 us  [mix(): pl.pallas_call(functools.partial(mix_kernel, plan, groups), in_specs=[sme...]
    pallas_call x2 -> x1, Pallas kernels: 3.57 us -> 0.45 us  [rank_tokens(): pl.pallas_call(functools.partial(rank_kernel, groups), out_shape=(jax.Sha...]
    unnamed x63 -> x53, local copies, waits for them, and re-layouts: 11.1 us -> 9.17 us
    ppermute x8, starting transfers between devices: 9.55 us -> 11 us  [cross(): return lax.ppermute(block, 'tm', pairs)]
  transfers between devices with their start and end apart: 24 -> 24, of which waited for: 12 -> 12; matrix products, arithmetic and copies ran while one was open for 1% -> 1% of each run, Pallas kernels for 31% -> 16%
where the time goes in v8:
time: 143 us; the launch traced here: 142 us
  waiting for transfers between devices  51.9 us (36%)
  Pallas kernels  45.2 us (32%)
  starting transfers between devices  34.8 us (24%)
  local copies, waits for them, and re-layouts  9.17 us (6%)
    ppermute x6, waiting for transfers between devices, round(): return lax.ppermute(block, 'tm', pairs)  21.6 us
    pallas_call x2, Pallas kernels, attend(): pl.pallas_call(functools.partial(attend_kernel, plan, slot), in_specs=[sm...  18.1 us
    pallas_call x1, Pallas kernels, project_updates(): pl.pallas_call(functools.partial(update_kernel, plan, groups, len(frames)...  14.1 us
    ppermute x8, starting transfers between devices, cross(): return lax.ppermute(block, 'tm', pairs)  11 us
    ppermute x8, waiting for transfers between devices, cross(): return lax.ppermute(block, 'tm', pairs)  10.6 us
    all_to_all x2, starting transfers between devices, exchange(): lax.all_to_all(blocks, 'tm', split_axis=0, concat_axis=0, tiled=True, axi...  10.1 us
    unnamed x53, local copies, waits for them, and re-layouts  9.17 us
    ppermute x6, starting transfers between devices, round(): return lax.ppermute(block, 'tm', pairs)  8.23 us
  transfers between devices with their start and end apart: 24, of which 12 were waited for; matrix products, arithmetic and copies ran while one was open for 1% of the time, Pallas kernels for 16%

profile of v8, /device:TPU:0, one launch (start us, length us, event | category | flops | bytes accessed | tf_op | source)
XLA Modules:
  0.0 142.1 jit_solution(9746228679256322837)
XLA Ops:
  0.5 2.5 %collective-permute-start.7 = (bf16[512,1024]{1,0:T(8,128)(2,1)}, bf16[512,1024]{1,0:T(8,128)(2,1)S(1)}, u32[]{:S(2)}, u32[]{:S(2)}) collective-permute-start(bf16[512,1024]{1,0:T(8,128)(2,1)} %bitcast.6), channel_id=1, source_target_pairs={{0,1},{1,0},{2,3},{3,2},{4,5},{5,4},{6,7},{7,6},{8,9},{9,8},{10,11... | collective-permute-start | bytes 3145736 | tf_op jit(solution)/shard_map/ppermute | solution.py:89
  3.2 1.6 %collective-permute-done.1.refs_1_ = bf16[64,2560]{1,0:T(8,128)(2,1)S(1)} collective-permute-done((bf16[64,2560]{1,0:T(8,128)(2,1)}, bf16[64,2560]{1,0:T(8,128)(2,1)S(1)}, u32[]{:S(2)}, u32[]{:S(2)}) %collective-permute-start.1) | collective-permute-done | bytes 327712 | tf_op jit(solution)/shard_map/ppermute | solution.py:61
  6.0 1.6 %collective-permute-start.2 = (bf16[128,512]{1,0:T(8,128)(2,1)S(1)}, bf16[128,512]{1,0:T(8,128)(2,1)S(1)}, u32[]{:S(2)}, u32[]{:S(2)}) collective-permute-start(bf16[128,512]{1,0:T(8,128)(2,1)S(1)} %get-tuple-element.44.refs_6_), channel_id=1, source_target_pairs={{0,8},{2,10},{4,12},{6,14},{8,16},{10,18},{12,20},{14,22},{16,24},... | collective-permute-start | bytes 393224 | tf_op jit(solution)/shard_map/ppermute | solution.py:66
  7.6 1.6 %collective-permute-start.4 = (bf16[128,768]{1,0:T(8,128)(2,1)S(1)}, bf16[128,768]{1,0:T(8,128)(2,1)S(1)}, u32[]{:S(2)}, u32[]{:S(2)}) collective-permute-start(bf16[128,768]{1,0:T(8,128)(2,1)S(1)} %get-tuple-element.50.refs_4_), channel_id=1, source_target_pairs={{0,8},{2,10},{4,12},{6,14},{8,16},{10,18},{12,20},{14,22},{16,24},... | collective-permute-start | bytes 589832 | tf_op jit(solution)/shard_map/ppermute | solution.py:66
  9.2 1.5 %collective-permute-start.5 = (bf16[128,768]{1,0:T(8,128)(2,1)S(1)}, bf16[128,768]{1,0:T(8,128)(2,1)S(1)}, u32[]{:S(2)}, u32[]{:S(2)}) collective-permute-start(bf16[128,768]{1,0:T(8,128)(2,1)S(1)} %get-tuple-element.50.refs_4_), channel_id=1, source_target_pairs={{0,4},{2,6},{4,0},{6,2},{8,12},{10,14},{12,8},{14,10},{16,20},{18,... | collective-permute-start | bytes 589832 | tf_op jit(solution)/shard_map/ppermute | solution.py:71
  10.7 3.5 %collective-permute-done.2.refs_8_ = bf16[128,512]{1,0:T(8,128)(2,1)S(1)} collective-permute-done((bf16[128,512]{1,0:T(8,128)(2,1)S(1)}, bf16[128,512]{1,0:T(8,128)(2,1)S(1)}, u32[]{:S(2)}, u32[]{:S(2)}) %collective-permute-start.2) | collective-permute-done | bytes 131104 | tf_op jit(solution)/shard_map/ppermute | solution.py:66
  14.1 1.5 %collective-permute-start.3 = (bf16[128,512]{1,0:T(8,128)(2,1)S(1)}, bf16[128,512]{1,0:T(8,128)(2,1)S(1)}, u32[]{:S(2)}, u32[]{:S(2)}) collective-permute-start(bf16[128,512]{1,0:T(8,128)(2,1)S(1)} %get-tuple-element.44.refs_6_), channel_id=1, source_target_pairs={{0,4},{2,6},{4,0},{6,2},{8,12},{10,14},{12,8},{14,10},{16,20},{18,... | collective-permute-start | bytes 393224 | tf_op jit(solution)/shard_map/ppermute | solution.py:71
  15.6 3.5 %collective-permute-done.3.refs_7_ = bf16[128,512]{1,0:T(8,128)(2,1)S(1)} collective-permute-done((bf16[128,512]{1,0:T(8,128)(2,1)S(1)}, bf16[128,512]{1,0:T(8,128)(2,1)S(1)}, u32[]{:S(2)}, u32[]{:S(2)}) %collective-permute-start.3) | collective-permute-done | bytes 131104 | tf_op jit(solution)/shard_map/ppermute | solution.py:71
  20.0 1.5 %collective-permute-start.9 = (bf16[128,512]{1,0:T(8,128)(2,1)S(1)}, bf16[128,512]{1,0:T(8,128)(2,1)}, u32[]{:S(2)}, u32[]{:S(2)}) collective-permute-start(bf16[128,512]{1,0:T(8,128)(2,1)S(1)} %collective-permute-done.2.refs_8_), channel_id=1, source_target_pairs={{0,4},{2,6},{4,0},{6,2},{8,12},{10,14},{12,8},{14,10},{16,20},{18,... | collective-permute-start | bytes 393224 | tf_op jit(solution)/shard_map/ppermute | solution.py:71
  27.2 3.5 %place_tokens.1.refs_3_ = bf16[2048,1024]{1,0:T(8,128)(2,1)S(1)} custom-call(f32[1,1024]{1,0:T(1,128)S(1)} %get-tuple-element.52.rank_ref.refs_2_, bf16[512,1024]{1,0:T(8,128)(2,1)S(1)} %bitcast.7, bf16[512,1024]{1,0:T(8,128)(2,1)S(1)} %collective-permute-done.6.refs_1_), custom_call_target="tpu_custom_call" | custom-call | bytes 4096 | tf_op jit(solution)/shard_map/place_tokens/pallas_call | solution.py:255
  30.7 2.0 %copy-done = bf16[2048,1024]{1,0:T(8,128)(2,1)} copy-done((bf16[2048,1024]{1,0:T(8,128)(2,1)}, bf16[2048,1024]{1,0:T(8,128)(2,1)S(1)}, u32[]{:S(2)}) %copy-start) | copy-done | bytes 4194328
  32.7 1.6 %collective-permute-start.10 = (bf16[128,512]{1,0:T(8,128)(2,1)}, bf16[128,512]{1,0:T(8,128)(2,1)S(1)}, u32[]{:S(2)}, u32[]{:S(2)}) collective-permute-start(bf16[128,512]{1,0:T(8,128)(2,1)} %collective-permute-done.8.refs_10_), channel_id=1, source_target_pairs={{0,8},{2,10},{4,12},{6,14},{8,16},{10,18},{12,20},{14,22},{16,24},... | collective-permute-start | bytes 393224 | tf_op jit(solution)/shard_map/ppermute | solution.py:66
  34.3 1.5 %collective-permute-start.11 = (bf16[128,512]{1,0:T(8,128)(2,1)}, bf16[128,512]{1,0:T(8,128)(2,1)S(1)}, u32[]{:S(2)}, u32[]{:S(2)}) collective-permute-start(bf16[128,512]{1,0:T(8,128)(2,1)} %collective-permute-done.8.refs_10_), channel_id=1, source_target_pairs={{0,4},{2,6},{4,0},{6,2},{8,12},{10,14},{12,8},{14,10},{16,20},{18,... | collective-permute-start | bytes 393224 | tf_op jit(solution)/shard_map/ppermute | solution.py:71
  35.8 3.9 %collective-permute-done.10.refs_12_ = bf16[128,512]{1,0:T(8,128)(2,1)S(1)} collective-permute-done((bf16[128,512]{1,0:T(8,128)(2,1)}, bf16[128,512]{1,0:T(8,128)(2,1)S(1)}, u32[]{:S(2)}, u32[]{:S(2)}) %collective-permute-start.10) | collective-permute-done | bytes 131104 | tf_op jit(solution)/shard_map/ppermute | solution.py:66
  39.8 1.5 %collective-permute-start.14 = (bf16[128,512]{1,0:T(8,128)(2,1)S(1)}, bf16[128,512]{1,0:T(8,128)(2,1)S(1)}, u32[]{:S(2)}, u32[]{:S(2)}) collective-permute-start(bf16[128,512]{1,0:T(8,128)(2,1)S(1)} %collective-permute-done.10.refs_12_), channel_id=1, source_target_pairs={{0,4},{2,6},{4,0},{6,2},{8,12},{10,14},{12,8},{14,10},{16,20},{18,... | collective-permute-start | bytes 393224 | tf_op jit(solution)/shard_map/ppermute | solution.py:71
  41.3 3.5 %collective-permute-done.14.refs_13_ = bf16[128,512]{1,0:T(8,128)(2,1)S(1)} collective-permute-done((bf16[128,512]{1,0:T(8,128)(2,1)S(1)}, bf16[128,512]{1,0:T(8,128)(2,1)S(1)}, u32[]{:S(2)}, u32[]{:S(2)}) %collective-permute-start.14) | collective-permute-done | bytes 131104 | tf_op jit(solution)/shard_map/ppermute | solution.py:71
  44.8 2.7 %collective-permute-done.15.refs_5_ = bf16[512,1024]{1,0:T(8,128)(2,1)S(1)} collective-permute-done((bf16[512,1024]{1,0:T(8,128)(2,1)S(1)}, bf16[512,1024]{1,0:T(8,128)(2,1)S(1)}, u32[]{:S(2)}, u32[]{:S(2)}) %collective-permute-start.15) | collective-permute-done | bytes 1048608 | tf_op jit(solution)/shard_map/ppermute | solution.py:61
  48.5 14.1 %project_updates.1 = (bf16[2048,1024]{1,0:T(8,128)(2,1)}, bf16[2048,256]{1,0:T(8,128)(2,1)}, bf16[2,2048,128]{2,1,0:T(8,128)(2,1)}, bf16[8,272,128]{2,1,0:T(8,128)(2,1)}) custom-call(f32[8,16]{1,0:T(8,128)} %bitcast.11, f32[8,16]{1,0:T(8,128)} %copy-done.10, f32[1,1024]{1,0:T(1,128)} %copy-done.6, bf16[2048,1024]{1,0:T(8,128)(2,1)} %copy-done, ...), custom_call_target="tpu_custom_call" | custom-call | flops 8589934592 | bytes 12582912 | tf_op jit(solution)/shard_map/project_updates/pallas_call | solution.py:381
  62.7 4.2 %all-to-all-start = ((bf16[8,272,128]{2,1,0:T(8,128)(2,1)}), bf16[8,272,128]{2,1,0:T(8,128)(2,1)S(1)}, u32[]{:S(2)}, u32[]{:S(2)}) async-start(bf16[8,272,128]{2,1,0:T(8,128)(2,1)} %get-tuple-element.60), calls=%async_computation | async-start | bytes 1114112 | tf_op jit(solution)/shard_map/all_to_all | solution.py:744
  66.9 2.0 %collective-permute-start.16 = (bf16[128,768]{1,0:T(8,128)(2,1)S(1)}, bf16[128,768]{1,0:T(8,128)(2,1)S(1)}, u32[]{:S(2)}, u32[]{:S(2)}) collective-permute-start(bf16[128,768]{1,0:T(8,128)(2,1)S(1)} %collective-permute-done.12.refs_8_), channel_id=1, source_target_pairs={{0,8},{2,10},{4,12},{6,14},{8,16},{10,18},{12,20},{14,22},{16,24},... | collective-permute-start | bytes 589832 | tf_op jit(solution)/shard_map/ppermute | solution.py:66
  70.4 14.1 %collective-permute-done.16.refs_10_ = bf16[128,768]{1,0:T(8,128)(2,1)S(1)} collective-permute-done((bf16[128,768]{1,0:T(8,128)(2,1)S(1)}, bf16[128,768]{1,0:T(8,128)(2,1)S(1)}, u32[]{:S(2)}, u32[]{:S(2)}) %collective-permute-start.16) | collective-permute-done | bytes 196640 | tf_op jit(solution)/shard_map/ppermute | solution.py:66
  84.6 1.5 %collective-permute-start.18 = (bf16[128,768]{1,0:T(8,128)(2,1)S(1)}, bf16[128,768]{1,0:T(8,128)(2,1)S(1)}, u32[]{:S(2)}, u32[]{:S(2)}) collective-permute-start(bf16[128,768]{1,0:T(8,128)(2,1)S(1)} %collective-permute-done.16.refs_10_), channel_id=1, source_target_pairs={{0,4},{2,6},{4,0},{6,2},{8,12},{10,14},{12,8},{14,10},{16,20},{18,... | collective-permute-start | bytes 589832 | tf_op jit(solution)/shard_map/ppermute | solution.py:71
  86.8 3.6 %collective-permute-done.18.refs_11_ = bf16[128,768]{1,0:T(8,128)(2,1)S(1)} collective-permute-done((bf16[128,768]{1,0:T(8,128)(2,1)S(1)}, bf16[128,768]{1,0:T(8,128)(2,1)S(1)}, u32[]{:S(2)}, u32[]{:S(2)}) %collective-permute-start.18) | collective-permute-done | bytes 196640 | tf_op jit(solution)/shard_map/ppermute | solution.py:71
  91.1 9.1 %attend.2 = (f32[1024,256]{1,0:T(8,128)}, bf16[1024,256]{1,0:T(8,128)(2,1)}) custom-call(s32[16,4]{1,0:T(8,128)} %copy.7.refs_0_, bf16[2048,1024]{1,0:T(8,128)(2,1)} %get-tuple-element.73.refs_1_, bf16[2048,256]{1,0:T(8,128)(2,1)} %get-tuple-element.62.refs_2_, bf16[2,2048,128]{2,1,0:T(8,128)(2,1)} %get-tuple-element.63.refs_3_, bf16[128,768]{1,0:T(8,128)(2,1)} %copy-done.7, ...), custom_call_target="tpu_custom_call" | custom-call | flops 4831838208 | bytes 11534336 | tf_op jit(solution)/shard_map/attend/pallas_call | solution.py:530
  101.1 5.9 %all-to-all-start.1 = ((bf16[8,256,128]{2,1,0:T(8,128)(2,1)}), bf16[8,256,128]{2,1,0:T(8,128)(2,1)S(1)}, u32[]{:S(2)}, u32[]{:S(2)}) async-start(bf16[8,256,128]{2,1,0:T(8,128)(2,1)} %scan_states.1), calls=%async_computation.1 | async-start | bytes 1048576 | tf_op jit(solution)/shard_map/all_to_all | solution.py:744
  107.0 9.1 %attend.3 = (f32[1024,256]{1,0:T(8,128)}, bf16[1024,256]{1,0:T(8,128)(2,1)}) custom-call(s32[16,4]{1,0:T(8,128)} %copy.7.refs_0_, bf16[2048,1024]{1,0:T(8,128)(2,1)} %get-tuple-element.73.refs_1_, bf16[2048,256]{1,0:T(8,128)(2,1)} %get-tuple-element.62.refs_2_, bf16[2,2048,128]{2,1,0:T(8,128)(2,1)} %get-tuple-element.63.refs_3_, bf16[128,768]{1,0:T(8,128)(2,1)} %copy-done.7, ...), custom_call_target="tpu_custom_call" | custom-call | flops 4831838208 | bytes 11534336 | tf_op jit(solution)/shard_map/attend/pallas_call | solution.py:530
  116.1 4.7 %all-to-all-done.1 = bf16[8,256,128]{2,1,0:T(8,128)(2,1)S(1)} async-done(((bf16[8,256,128]{2,1,0:T(8,128)(2,1)}), bf16[8,256,128]{2,1,0:T(8,128)(2,1)S(1)}, u32[]{:S(2)}, u32[]{:S(2)}) %all-to-all-start.1) | async-done | bytes 524320 | tf_op jit(solution)/shard_map/all_to_all | solution.py:744
  121.7 5.7 %mix.1 = (bf16[512,256]{1,0:T(8,128)(2,1)}, bf16[512,256]{1,0:T(8,128)(2,1)}, bf16[512,256]{1,0:T(8,128)(2,1)}, bf16[512,256]{1,0:T(8,128)(2,1)}) custom-call(f32[8,16]{1,0:T(8,128)} %bitcast.12, f32[8,16]{1,0:T(8,128)} %copy-done.10, f32[1024,256]{1,0:T(8,128)} %get-tuple-element.71.refs_2_, f32[1024,256]{1,0:T(8,128)} %get-tuple-element.74.refs_3_, ...), custom_call_target="tpu_custom_call" | custom-call | flops 1073741824 | bytes 6291456 | tf_op jit(solution)/shard_map/mix/pallas_call | solution.py:642
  127.3 1.5 %collective-permute-start.19 = (bf16[512,256]{1,0:T(8,128)(2,1)}, bf16[512,256]{1,0:T(8,128)(2,1)S(1)}, u32[]{:S(2)}, u32[]{:S(2)}) collective-permute-start(bf16[512,256]{1,0:T(8,128)(2,1)} %get-tuple-element.80), channel_id=1, source_target_pairs={{0,1},{1,0},{2,3},{3,2},{4,5},{5,4},{6,7},{7,6},{8,9},{9,8},{10,11... | collective-permute-start | bytes 786440 | tf_op jit(solution)/shard_map/ppermute | solution.py:89
  129.5 6.7 %collective-permute-done.19.refs_1_ = bf16[512,256]{1,0:T(8,128)(2,1)S(1)} collective-permute-done((bf16[512,256]{1,0:T(8,128)(2,1)}, bf16[512,256]{1,0:T(8,128)(2,1)S(1)}, u32[]{:S(2)}, u32[]{:S(2)}) %collective-permute-start.19) | collective-permute-done | bytes 262176 | tf_op jit(solution)/shard_map/ppermute | solution.py:89
  136.3 2.6 %collective-permute-done.21.refs_3_ = bf16[512,256]{1,0:T(8,128)(2,1)S(1)} collective-permute-done((bf16[512,256]{1,0:T(8,128)(2,1)}, bf16[512,256]{1,0:T(8,128)(2,1)S(1)}, u32[]{:S(2)}, u32[]{:S(2)}) %collective-permute-start.21) | collective-permute-done | bytes 262176 | tf_op jit(solution)/shard_map/ppermute | solution.py:97
  139.8 2.2 %project_out.1 = bf16[512,1024]{1,0:T(8,128)(2,1)} custom-call(bf16[1024,1024]{1,0:T(8,128)(2,1)S(1)} %copy-done.1, bf16[512,256]{1,0:T(8,128)(2,1)S(1)} %copy-done.5, bf16[512,256]{1,0:T(8,128)(2,1)S(1)} %collective-permute-done.19.refs_1_, bf16[512,256]{1,0:T(8,128)(2,1)S(1)} %collective-permute-done.20.refs_2_, ...), custom_call_target="tpu_custom_call" | custom-call | flops 1073741824 | bytes 4194304 | tf_op jit(solution)/shard_map/project_out/pallas_call | solution.py:681
  (79 shorter events, 15.6 us)
Async XLA Ops:
  0.0 23.4 %collective-permute-start.6 = (bf16[512,1024]{1,0:T(8,128)(2,1)}, bf16[512,1024]{1,0:T(8,128)(2,1)S(1)}, u32[]{:S(2)}, u32[]{:S(2)}) collective-permute-start(bf16[512,1024]{1,0:T(8,128)(2,1)} %bitcast.5), channel_id=1, source_target_pairs={{0,2},{2,0},{4,6},{6,4},{8,10},{10,8},{12,14},{14,12},{16,18},{18,... | collective-permute-start | bytes 3145736 | tf_op jit(solution)/shard_map/ppermute | solution.py:61
  0.5 40.9 %collective-permute-start.7 = (bf16[512,1024]{1,0:T(8,128)(2,1)}, bf16[512,1024]{1,0:T(8,128)(2,1)S(1)}, u32[]{:S(2)}, u32[]{:S(2)}) collective-permute-start(bf16[512,1024]{1,0:T(8,128)(2,1)} %bitcast.6), channel_id=1, source_target_pairs={{0,1},{1,0},{2,3},{3,2},{4,5},{5,4},{6,7},{7,6},{8,9},{9,8},{10,11... | collective-permute-start | bytes 3145736 | tf_op jit(solution)/shard_map/ppermute | solution.py:89
  3.0 1.8 %collective-permute-start.1 = (bf16[64,2560]{1,0:T(8,128)(2,1)}, bf16[64,2560]{1,0:T(8,128)(2,1)S(1)}, u32[]{:S(2)}, u32[]{:S(2)}) collective-permute-start(bf16[64,2560]{1,0:T(8,128)(2,1)} %refs_0_.3), channel_id=1, source_target_pairs={{0,2},{2,0},{4,6},{6,4},{8,10},{10,8},{12,14},{14,12},{16,18},{18,... | collective-permute-start | bytes 983048 | tf_op jit(solution)/shard_map/ppermute | solution.py:61
  5.9 41.5 %copy-start.8 = (bf16[128,512]{1,0:T(8,128)(2,1)}, bf16[128,512]{1,0:T(8,128)(2,1)S(1)}, u32[]{:S(2)}) copy-start(bf16[128,512]{1,0:T(8,128)(2,1)S(1)} %get-tuple-element.44.refs_6_) | copy-start | bytes 393220
  6.0 56.7 %copy-start.7 = (bf16[128,768]{1,0:T(8,128)(2,1)}, bf16[128,768]{1,0:T(8,128)(2,1)S(1)}, u32[]{:S(2)}) copy-start(bf16[128,768]{1,0:T(8,128)(2,1)S(1)} %get-tuple-element.50.refs_4_) | copy-start | bytes 589828
  6.0 8.2 %collective-permute-start.2 = (bf16[128,512]{1,0:T(8,128)(2,1)S(1)}, bf16[128,512]{1,0:T(8,128)(2,1)S(1)}, u32[]{:S(2)}, u32[]{:S(2)}) collective-permute-start(bf16[128,512]{1,0:T(8,128)(2,1)S(1)} %get-tuple-element.44.refs_6_), channel_id=1, source_target_pairs={{0,8},{2,10},{4,12},{6,14},{8,16},{10,18},{12,20},{14,22},{16,24},... | collective-permute-start | bytes 393224 | tf_op jit(solution)/shard_map/ppermute | solution.py:66
  7.6 12.4 %collective-permute-start.4 = (bf16[128,768]{1,0:T(8,128)(2,1)S(1)}, bf16[128,768]{1,0:T(8,128)(2,1)S(1)}, u32[]{:S(2)}, u32[]{:S(2)}) collective-permute-start(bf16[128,768]{1,0:T(8,128)(2,1)S(1)} %get-tuple-element.50.refs_4_), channel_id=1, source_target_pairs={{0,8},{2,10},{4,12},{6,14},{8,16},{10,18},{12,20},{14,22},{16,24},... | collective-permute-start | bytes 589832 | tf_op jit(solution)/shard_map/ppermute | solution.py:66
  9.2 12.4 %collective-permute-start.5 = (bf16[128,768]{1,0:T(8,128)(2,1)S(1)}, bf16[128,768]{1,0:T(8,128)(2,1)S(1)}, u32[]{:S(2)}, u32[]{:S(2)}) collective-permute-start(bf16[128,768]{1,0:T(8,128)(2,1)S(1)} %get-tuple-element.50.refs_4_), channel_id=1, source_target_pairs={{0,4},{2,6},{4,0},{6,2},{8,12},{10,14},{12,8},{14,10},{16,20},{18,... | collective-permute-start | bytes 589832 | tf_op jit(solution)/shard_map/ppermute | solution.py:71
  14.1 33.3 %copy-start.21 = (bf16[128,512]{1,0:T(8,128)(2,1)}, bf16[128,512]{1,0:T(8,128)(2,1)S(1)}, u32[]{:S(2)}) copy-start(bf16[128,512]{1,0:T(8,128)(2,1)S(1)} %collective-permute-done.2.refs_8_) | copy-start | bytes 393220
  14.1 5.0 %collective-permute-start.3 = (bf16[128,512]{1,0:T(8,128)(2,1)S(1)}, bf16[128,512]{1,0:T(8,128)(2,1)S(1)}, u32[]{:S(2)}, u32[]{:S(2)}) collective-permute-start(bf16[128,512]{1,0:T(8,128)(2,1)S(1)} %get-tuple-element.44.refs_6_), channel_id=1, source_target_pairs={{0,4},{2,6},{4,0},{6,2},{8,12},{10,14},{12,8},{14,10},{16,20},{18,... | collective-permute-start | bytes 393224 | tf_op jit(solution)/shard_map/ppermute | solution.py:71
  19.1 28.4 %copy-start.22 = (bf16[128,512]{1,0:T(8,128)(2,1)}, bf16[128,512]{1,0:T(8,128)(2,1)S(1)}, u32[]{:S(2)}) copy-start(bf16[128,512]{1,0:T(8,128)(2,1)S(1)} %collective-permute-done.3.refs_7_) | copy-start | bytes 393220
  19.1 13.6 %collective-permute-start.8 = (bf16[128,512]{1,0:T(8,128)(2,1)S(1)}, bf16[128,512]{1,0:T(8,128)(2,1)}, u32[]{:S(2)}, u32[]{:S(2)}) collective-permute-start(bf16[128,512]{1,0:T(8,128)(2,1)S(1)} %collective-permute-done.2.refs_8_), channel_id=1, source_target_pairs={{0,8},{2,10},{4,12},{6,14},{8,16},{10,18},{12,20},{14,22},{16,24},... | collective-permute-start | bytes 393224 | tf_op jit(solution)/shard_map/ppermute | solution.py:66
  20.0 42.6 %copy-start.14 = (bf16[128,768]{1,0:T(8,128)(2,1)}, bf16[128,768]{1,0:T(8,128)(2,1)S(1)}, u32[]{:S(2)}) copy-start(bf16[128,768]{1,0:T(8,128)(2,1)S(1)} %collective-permute-done.4.refs_6_) | copy-start | bytes 589828
  20.0 12.7 %collective-permute-start.9 = (bf16[128,512]{1,0:T(8,128)(2,1)S(1)}, bf16[128,512]{1,0:T(8,128)(2,1)}, u32[]{:S(2)}, u32[]{:S(2)}) collective-permute-start(bf16[128,512]{1,0:T(8,128)(2,1)S(1)} %collective-permute-done.2.refs_8_), channel_id=1, source_target_pairs={{0,4},{2,6},{4,0},{6,2},{8,12},{10,14},{12,8},{14,10},{16,20},{18,... | collective-permute-start | bytes 393224 | tf_op jit(solution)/shard_map/ppermute | solution.py:71
  21.5 41.1 %copy-start.15 = (bf16[128,768]{1,0:T(8,128)(2,1)}, bf16[128,768]{1,0:T(8,128)(2,1)S(1)}, u32[]{:S(2)}) copy-start(bf16[128,768]{1,0:T(8,128)(2,1)S(1)} %collective-permute-done.5.refs_5_) | copy-start | bytes 589828
  21.5 1.4 collective-permute-start
  22.9 12.9 %collective-permute-start.12 = (bf16[128,768]{1,0:T(8,128)(2,1)S(1)}, bf16[128,768]{1,0:T(8,128)(2,1)S(1)}, u32[]{:S(2)}, u32[]{:S(2)}) collective-permute-start(bf16[128,768]{1,0:T(8,128)(2,1)S(1)} %collective-permute-done.4.refs_6_), channel_id=1, source_target_pairs={{0,8},{2,10},{4,12},{6,14},{8,16},{10,18},{12,20},{14,22},{16,24},... | collective-permute-start | bytes 589832 | tf_op jit(solution)/shard_map/ppermute | solution.py:66
  23.4 12.5 %collective-permute-start.13 = (bf16[128,768]{1,0:T(8,128)(2,1)S(1)}, bf16[128,768]{1,0:T(8,128)(2,1)S(1)}, u32[]{:S(2)}, u32[]{:S(2)}) collective-permute-start(bf16[128,768]{1,0:T(8,128)(2,1)S(1)} %collective-permute-done.4.refs_6_), channel_id=1, source_target_pairs={{0,4},{2,6},{4,0},{6,2},{8,12},{10,14},{12,8},{14,10},{16,20},{18,... | collective-permute-start | bytes 589832 | tf_op jit(solution)/shard_map/ppermute | solution.py:71
  32.7 53.4 %copy-start.11 = (s32[16,4]{0,1:T(4,128)S(1)}, s32[16,4]{0,1:T(4,128)}, u32[]{:S(2)}) copy-start(s32[16,4]{0,1:T(4,128)} %param.10) | copy-start | bytes 772
  32.7 7.1 %collective-permute-start.10 = (bf16[128,512]{1,0:T(8,128)(2,1)}, bf16[128,512]{1,0:T(8,128)(2,1)S(1)}, u32[]{:S(2)}, u32[]{:S(2)}) collective-permute-start(bf16[128,512]{1,0:T(8,128)(2,1)} %collective-permute-done.8.refs_10_), channel_id=1, source_target_pairs={{0,8},{2,10},{4,12},{6,14},{8,16},{10,18},{12,20},{14,22},{16,24},... | collective-permute-start | bytes 393224 | tf_op jit(solution)/shard_map/ppermute | solution.py:66
  34.3 5.4 %collective-permute-start.11 = (bf16[128,512]{1,0:T(8,128)(2,1)}, bf16[128,512]{1,0:T(8,128)(2,1)S(1)}, u32[]{:S(2)}, u32[]{:S(2)}) collective-permute-start(bf16[128,512]{1,0:T(8,128)(2,1)} %collective-permute-done.8.refs_10_), channel_id=1, source_target_pairs={{0,4},{2,6},{4,0},{6,2},{8,12},{10,14},{12,8},{14,10},{16,20},{18,... | collective-permute-start | bytes 393224 | tf_op jit(solution)/shard_map/ppermute | solution.py:71
  35.8 33.1 %copy-start.16 = (bf16[128,768]{1,0:T(8,128)(2,1)}, bf16[128,768]{1,0:T(8,128)(2,1)S(1)}, u32[]{:S(2)}) copy-start(bf16[128,768]{1,0:T(8,128)(2,1)S(1)} %collective-permute-done.12.refs_8_) | copy-start | bytes 589828
  39.8 5.0 %collective-permute-start.14 = (bf16[128,512]{1,0:T(8,128)(2,1)S(1)}, bf16[128,512]{1,0:T(8,128)(2,1)S(1)}, u32[]{:S(2)}, u32[]{:S(2)}) collective-permute-start(bf16[128,512]{1,0:T(8,128)(2,1)S(1)} %collective-permute-done.10.refs_12_), channel_id=1, source_target_pairs={{0,4},{2,6},{4,0},{6,2},{8,12},{10,14},{12,8},{14,10},{16,20},{18,... | collective-permute-start | bytes 393224 | tf_op jit(solution)/shard_map/ppermute | solution.py:71
  44.8 2.7 %collective-permute-start.15 = (bf16[512,1024]{1,0:T(8,128)(2,1)S(1)}, bf16[512,1024]{1,0:T(8,128)(2,1)S(1)}, u32[]{:S(2)}, u32[]{:S(2)}) collective-permute-start(bf16[512,1024]{1,0:T(8,128)(2,1)S(1)} %collective-permute-done.7.refs_4_), channel_id=1, source_target_pairs={{0,2},{2,0},{4,6},{6,4},{8,10},{10,8},{12,14},{14,12},{16,18},{18,... | collective-permute-start | bytes 3145736 | tf_op jit(solution)/shard_map/ppermute | solution.py:61
  62.7 37.5 %all-to-all-start = ((bf16[8,272,128]{2,1,0:T(8,128)(2,1)}), bf16[8,272,128]{2,1,0:T(8,128)(2,1)S(1)}, u32[]{:S(2)}, u32[]{:S(2)}) async-start(bf16[8,272,128]{2,1,0:T(8,128)(2,1)} %get-tuple-element.60), calls=%async_computation | async-start | bytes 1114112 | tf_op jit(solution)/shard_map/all_to_all | solution.py:744
  66.9 17.6 %collective-permute-start.16 = (bf16[128,768]{1,0:T(8,128)(2,1)S(1)}, bf16[128,768]{1,0:T(8,128)(2,1)S(1)}, u32[]{:S(2)}, u32[]{:S(2)}) collective-permute-start(bf16[128,768]{1,0:T(8,128)(2,1)S(1)} %collective-permute-done.12.refs_8_), channel_id=1, source_target_pairs={{0,8},{2,10},{4,12},{6,14},{8,16},{10,18},{12,20},{14,22},{16,24},... | collective-permute-start | bytes 589832 | tf_op jit(solution)/shard_map/ppermute | solution.py:66
  69.0 15.6 %collective-permute-start.17 = (bf16[128,768]{1,0:T(8,128)(2,1)S(1)}, bf16[128,768]{1,0:T(8,128)(2,1)S(1)}, u32[]{:S(2)}, u32[]{:S(2)}) collective-permute-start(bf16[128,768]{1,0:T(8,128)(2,1)S(1)} %collective-permute-done.12.refs_8_), channel_id=1, source_target_pairs={{0,4},{2,6},{4,0},{6,2},{8,12},{10,14},{12,8},{14,10},{16,20},{18,... | collective-permute-start | bytes 589832 | tf_op jit(solution)/shard_map/ppermute | solution.py:71
  84.6 5.9 %collective-permute-start.18 = (bf16[128,768]{1,0:T(8,128)(2,1)S(1)}, bf16[128,768]{1,0:T(8,128)(2,1)S(1)}, u32[]{:S(2)}, u32[]{:S(2)}) collective-permute-start(bf16[128,768]{1,0:T(8,128)(2,1)S(1)} %collective-permute-done.16.refs_10_), channel_id=1, source_target_pairs={{0,4},{2,6},{4,0},{6,2},{8,12},{10,14},{12,8},{14,10},{16,20},{18,... | collective-permute-start | bytes 589832 | tf_op jit(solution)/shard_map/ppermute | solution.py:71
  101.1 19.8 %all-to-all-start.1 = ((bf16[8,256,128]{2,1,0:T(8,128)(2,1)}), bf16[8,256,128]{2,1,0:T(8,128)(2,1)S(1)}, u32[]{:S(2)}, u32[]{:S(2)}) async-start(bf16[8,256,128]{2,1,0:T(8,128)(2,1)} %scan_states.1), calls=%async_computation.1 | async-start | bytes 1048576 | tf_op jit(solution)/shard_map/all_to_all | solution.py:744
  127.3 8.9 %collective-permute-start.19 = (bf16[512,256]{1,0:T(8,128)(2,1)}, bf16[512,256]{1,0:T(8,128)(2,1)S(1)}, u32[]{:S(2)}, u32[]{:S(2)}) collective-permute-start(bf16[512,256]{1,0:T(8,128)(2,1)} %get-tuple-element.80), channel_id=1, source_target_pairs={{0,1},{1,0},{2,3},{3,2},{4,5},{5,4},{6,7},{7,6},{8,9},{9,8},{10,11... | collective-permute-start | bytes 786440 | tf_op jit(solution)/shard_map/ppermute | solution.py:89
  128.9 7.4 %collective-permute-start.20 = (bf16[512,256]{1,0:T(8,128)(2,1)}, bf16[512,256]{1,0:T(8,128)(2,1)S(1)}, u32[]{:S(2)}, u32[]{:S(2)}) collective-permute-start(bf16[512,256]{1,0:T(8,128)(2,1)} %get-tuple-element.81), channel_id=1, source_target_pairs={{0,2},{2,0},{4,6},{6,4},{8,10},{10,8},{12,14},{14,12},{16,18},{18,... | collective-permute-start | bytes 786440 | tf_op jit(solution)/shard_map/ppermute | solution.py:61
  128.9 10.0 %collective-permute-start.21 = (bf16[512,256]{1,0:T(8,128)(2,1)}, bf16[512,256]{1,0:T(8,128)(2,1)S(1)}, u32[]{:S(2)}, u32[]{:S(2)}) collective-permute-start(bf16[512,256]{1,0:T(8,128)(2,1)} %get-tuple-element.82), channel_id=1, source_target_pairs={{0,3},{1,2},{2,1},{3,0},{4,7},{5,6},{6,5},{7,4},{8,11},{9,10},{10,... | collective-permute-start | bytes 786440 | tf_op jit(solution)/shard_map/ppermute | solution.py:97
  (18 other events, 140.3 us)

commit v9 on v8

--- a/solution.py
+++ b/solution.py
@@ -49,7 +49,7 @@
         self.chips = frames // self.merge
         self.across = 2 if self.chips % 2 == 0 else 1
         self.along = self.chips // self.across
-        self.ringed = self.across == 2 and self.along <= 8
+        self.ringed = self.across == 2 and 2 <= self.along <= 8
 
     def core(self):
         return lax.rem(lax.axis_index("tm"), self.merge)
@@ -75,12 +75,14 @@
             return [(refs[0], slice(None))]
         rows = refs[0].shape[0]
         a, b = lax.div(self.chip(), self.across), lax.rem(self.chip(), self.across)
+        n = self.along
         made = []
         for i, ref in enumerate(refs):
-            k, flip = i // 2, i % 2
-            there = lax.rem(a - k + self.along, self.along) * self.across
-            at = pl.multiple_of((there + (1 - b if flip else b)) * rows, rows)
-            made.append((ref, pl.ds(at, rows)))
+            k, flip = (i, 0) if i < n else (min(i - n, n - 1), 1)
+            there = lax.rem(a - k + n, n) * self.across
+            at = (there + (1 - b if flip else b)) * rows
+            at = at + (rows // 2 if i == 2 * n else 0)
+            made.append((ref, pl.ds(pl.multiple_of(at, rows // 2), ref.shape[0])))
         return made
 
     def to_peer(self, block, k, other):
@@ -139,7 +141,7 @@
 
 
 def reorder_kernel(plan, *refs):
-    w_refs, out_refs = refs[:-2], refs[-2:]
+    w_refs, out_ref = refs[:-1], refs[-1]
     rows = w_refs[0].shape[0]
     width = plan.heads * PIECES * HD
     first = plan.core() == 0
@@ -150,28 +152,24 @@
             return one
         return jnp.where(first, one, ref[:, width + at : width + at + HD])
 
-    early = [(p, i) for i in EARLY for p in range(plan.pairs)]
-    late = [(p, i) for p in range(plan.pairs) for i in LATE]
-    for out_ref, order in zip(out_refs, (early, late)):
-        for n, (p, i) in enumerate(order):
-            blocks = []
-            for ref in w_refs:
-                one, two = (chosen(ref, ((2 * p + h) * PIECES + i) * HD) for h in range(2))
-                blocks.append(jnp.concatenate([one, two], axis=1))
-            for s, block in enumerate(blocks):
-                if plan.merge == 2:
-                    block = jnp.where(first, block, blocks[1 - s])
-                out_ref[s * rows : (s + 1) * rows, n * LANES : (n + 1) * LANES] = block
+    order = [(p, i) for i in EARLY for p in range(plan.pairs)]
+    order += [(p, i) for p in range(plan.pairs) for i in LATE]
+    for n, (p, i) in enumerate(order):
+        blocks = []
+        for ref in w_refs:
+            one, two = (chosen(ref, ((2 * p + h) * PIECES + i) * HD) for h in range(2))
+            blocks.append(jnp.concatenate([one, two], axis=1))
+        for s, block in enumerate(blocks):
+            if plan.merge == 2:
+                block = jnp.where(first, block, blocks[1 - s])
+            out_ref[s * rows : (s + 1) * rows, n * LANES : (n + 1) * LANES] = block
 
 
 def reorder(plan, weights):
     rows = weights[0].shape[0]
     return pl.pallas_call(
         functools.partial(reorder_kernel, plan),
-        out_shape=tuple(
-            jax.ShapeDtypeStruct((plan.merge * rows, plan.heads * len(kinds) * HD), bf16)
-            for kinds in (EARLY, LATE)
-        ),
+        out_shape=jax.ShapeDtypeStruct((plan.merge * rows, plan.heads * PIECES * HD), bf16),
         compiler_params=params(),
         cost_estimate=cost(0, 4 * weights[0].size),
         name="reorder",
@@ -234,104 +232,92 @@
     return jnp.where(places.astype(f32) == rank, 1.0, 0.0).astype(bf16)
 
 
-def place_kernel(merge, rank_ref, *refs):
-    frame_refs, x_ref, normed = refs[:merge], refs[-2], refs[-1]
+def place_kernel(merge, parts, start, rank_ref, *refs):
+    frame_refs, refs = refs[: merge * parts], refs[merge * parts :]
+    base_refs, (x_ref, normed) = refs[:-2], refs[-2:]
     tokens = rank_ref.shape[1]
-    local = frame_refs[0].shape[0]
+    count = normed.shape[1]
     step = 256
     for s in range(merge):
-        normalise(frame_refs[s], normed.at[s], 0)
+        at = 0
+        for ref in frame_refs[s * parts : (s + 1) * parts]:
+            normalise(ref, normed.at[s], at)
+            at += ref.shape[0]
     for at in range(0, tokens, step):
-        pick = picks(rank_ref[:, :local], at, step)
+        pick = picks(rank_ref[:, start : start + count], at, step)
         for s in range(merge):
-            x_ref[s * tokens + at : s * tokens + at + step, :] = jnp.dot(
-                pick, normed[s], preferred_element_type=f32
-            ).astype(bf16)
-
-
-def place_tokens(plan, rank, frames):
+            there = slice(s * tokens + at, s * tokens + at + step)
+            placed = jnp.dot(pick, normed[s], preferred_element_type=f32).astype(bf16)
+            for base in base_refs:
+                placed = base[there, :] + placed
+            x_ref[there, :] = placed
+
+
+def place_tokens(plan, rank, start, frames, base):
     tokens = rank.shape[1]
-    local, width = frames[0].shape
+    width = frames[0].shape[1]
+    parts = len(frames) // plan.merge
+    count = parts * frames[0].shape[0]
     return pl.pallas_call(
-        functools.partial(place_kernel, plan.merge),
+        functools.partial(place_kernel, plan.merge, parts, start),
         out_shape=jax.ShapeDtypeStruct((plan.merge * tokens, width), bf16),
-        scratch_shapes=[pltpu.VMEM((plan.merge, local, width), bf16)],
+        scratch_shapes=[pltpu.VMEM((plan.merge, count, width), bf16)],
         compiler_params=params(),
         cost_estimate=cost(0, 4 * tokens),
         name="place_tokens",
-    )(rank, *frames)
-
-
-def update_kernel(plan, groups, parts, *refs):
-    decay_refs, refs = refs[: plan.merge], refs[plan.merge :]
-    rank_ref, part_ref, refs = refs[0], refs[1], refs[2:]
-    frame_refs, refs = refs[: plan.merge * parts], refs[plan.merge * parts :]
-    w_refs, refs = refs[:-13], refs[-13:]
-    x_out, v_out, local_out, total_ref, raw, normed, w, turned, x, v, u, left, sems = refs
+    )(rank, *frames, *base)
+
+
+def update_kernel(plan, groups, *refs):
+    decay_refs, x_in, refs = refs[: plan.merge], refs[plan.merge], refs[plan.merge + 1 :]
+    w_refs, refs = refs[:-10], refs[-10:]
+    v_out, local_out, total_ref, w, turned, x, v, u, left, sems = refs
     copies = Copies(sems)
-    tokens = rank_ref.shape[1]
-    count = raw.shape[1]
+    every = x.shape[0]
+    tokens = every // plan.merge
     block = tokens // groups
     step = 256
     here = step // block
     cols = plan.pairs * LANES
 
-    arriving, partly, weights = [], [], []
-    for s in range(plan.merge):
-        at = 0
-        for ref in frame_refs[s * parts : (s + 1) * parts]:
-            size = ref.shape[0]
-            arriving.append(copies.start(ref, raw.at[s, at : at + size, :]))
-            at += size
-        if s == 0:
-            for ref, rows in plan.places(w_refs):
-                weights.append(copies.start(ref.at[:, cols:], turned.at[rows]))
-                weights.append(copies.start(ref.at[:, :cols], w.at[rows]))
-        for at in range(s * tokens, (s + 1) * tokens, step):
-            there = slice(at, at + step)
-            partly.append(copies.start(part_ref.at[there], x.at[there]))
-
+    weights, arriving = [], []
+    for ref, rows in plan.places(w_refs):
+        weights.append(copies.start(ref.at[:, cols : 2 * cols], turned.at[rows]))
+        weights.append(copies.start(ref.at[:, :cols], w.at[rows]))
+    for at in range(0, every, step):
+        arriving.append(copies.start(x_in.at[at : at + step], x.at[at : at + step]))
+
+    finish(weights)
+    maps = jnp.concatenate(
+        [
+            turned[at : at + LANES, :].astype(f32).T.astype(bf16)
+            for at in range(0, turned.shape[0], LANES)
+        ],
+        axis=1,
+    )
     lane = lax.div(lax.broadcasted_iota(jnp.int32, (LANES, step), 1), block)
     leaving = []
-    for s in range(plan.merge):
-        finish(arriving[s * parts : (s + 1) * parts])
-        normalise(raw.at[s], normed, 0)
-        if s == 0:
-            finish(weights)
-            maps = jnp.concatenate(
-                [
-                    turned[at : at + LANES, :].astype(f32).T.astype(bf16)
-                    for at in range(0, turned.shape[0], LANES)
-                ],
-                axis=1,
+    for at in range(0, every, step):
+        there = slice(at, at + step)
+        arriving[at // step].wait()
+        values = jnp.dot(x[there, :], w[...], preferred_element_type=f32).astype(bf16)
+        v[there, :] = values
+        leaving.append(copies.start(v.at[there], v_out.at[there]))
+        b = lax.dot_general(
+            maps, x[there, :], (((1,), (1,)), ((), ())), preferred_element_type=f32
+        )
+        for p in range(plan.pairs):
+            mine = b[p * LANES : (p + 1) * LANES]
+            wide = jnp.concatenate(
+                [jnp.where(lane == i, mine, 0.0).astype(bf16) for i in range(here)], axis=0
             )
-        for at in range(0, tokens, step):
-            there = slice(s * tokens + at, s * tokens + at + step)
-            pick = picks(rank_ref[:, tokens - count :], at, step)
-            more = jnp.dot(pick, normed[...], preferred_element_type=f32)
-            partly[there.start // step].wait()
-            placed = x[there, :] + more.astype(bf16)
-            x[there, :] = placed
-            leaving.append(copies.start(x.at[there], x_out.at[there]))
-            values = jnp.dot(placed, w[...], preferred_element_type=f32).astype(bf16)
-            v[there, :] = values
-            b = lax.dot_general(
-                maps, placed, (((1,), (1,)), ((), ())), preferred_element_type=f32
+            outer = jnp.dot(
+                wide, values[:, p * LANES : (p + 1) * LANES], preferred_element_type=f32
             )
-            for p in range(plan.pairs):
-                mine = b[p * LANES : (p + 1) * LANES]
-                wide = jnp.concatenate(
-                    [jnp.where(lane == i, mine, 0.0).astype(bf16) for i in range(here)], axis=0
-                )
-                outer = jnp.dot(
-                    wide, values[:, p * LANES : (p + 1) * LANES], preferred_element_type=f32
-                )
-                for i in range(here):
-                    m = outer[i * 2 * N : (i + 1) * 2 * N]
-                    row = ((at // block + i) * plan.pairs + p) * N
-                    u[s, row : row + N, :] = halves((N, LANES), m[:N], m[N:])
-        mine = slice(s * tokens, (s + 1) * tokens)
-        leaving.append(copies.start(v.at[mine], v_out.at[mine]))
+            for i in range(here):
+                m = outer[i * 2 * N : (i + 1) * 2 * N]
+                row = ((at % tokens // block + i) * plan.pairs + p) * N
+                u[at // tokens, row : row + N, :] = halves((N, LANES), m[:N], m[N:])
 
     peers = total_ref.shape[0]
     share = u.shape[1] // peers
@@ -371,26 +357,21 @@
     return share + 16 * -(-3 * max(1, share // N) // 16)
 
 
-def project_updates(plan, decays, rank, part, frames, weights, groups):
-    every, width = part.shape
-    tokens = rank.shape[1]
-    count = frames[0].shape[0] * len(frames) // plan.merge
+def project_updates(plan, decays, x, weights, groups):
+    every, width = x.shape
     cols = plan.pairs * LANES
     rows = plan.pairs * groups * N
     share = rows // plan.chips
     return pl.pallas_call(
-        functools.partial(update_kernel, plan, groups, len(frames) // plan.merge),
-        in_specs=[smem] * plan.merge + [vmem] + [hbm] * (1 + len(frames) + len(weights)),
-        out_specs=(hbm,) * 3 + (vmem,),
+        functools.partial(update_kernel, plan, groups),
+        in_specs=[smem] * plan.merge + [hbm] * (1 + len(weights)),
+        out_specs=(hbm,) * 2 + (vmem,),
         out_shape=(
-            jax.ShapeDtypeStruct((every, width), bf16),
             jax.ShapeDtypeStruct((every, cols), bf16),
             jax.ShapeDtypeStruct((plan.merge, rows, LANES), bf16),
             jax.ShapeDtypeStruct((plan.chips, share_rows(share), LANES), bf16),
         ),
         scratch_shapes=[
-            pltpu.VMEM((plan.merge, count, width), bf16),
-            pltpu.VMEM((count, width), bf16),
             pltpu.VMEM((width, cols), bf16),
             pltpu.VMEM((width, cols), bf16),
             pltpu.VMEM((every, width), bf16),
@@ -400,9 +381,9 @@
             Copies.scratch(),
         ],
         compiler_params=params(60),
-        cost_estimate=cost(4 * every * width * (2 * cols + count), 6 * every * width),
+        cost_estimate=cost(4 * every * width * 2 * cols, 6 * every * width),
         name="project_updates",
-    )(*decays, rank, part, *frames, *weights)
+    )(*decays, x, *weights)
 
 
 def scan_kernel(plan, u_ref, s_ref):
@@ -442,7 +423,11 @@
     step = 256
     per = step // block
 
-    weights = [copies.start(ref, w.at[rows]) for ref, rows in plan.places(w_refs)]
+    early = 2 * plan.pairs * LANES
+    weights = [
+        copies.start(ref.at[:, early : early + w.shape[1]], w.at[rows])
+        for ref, rows in plan.places(w_refs)
+    ]
     arriving = []
     for at in range(0, tokens, step):
         from_ = slice(slot * tokens + at, slot * tokens + at + step)
@@ -698,47 +683,38 @@
     arriving = [plan.to_peer(own, plan.peers - k, False) for k in range(1, plan.peers)]
     owns = [own] + [plan.swap(own)] * (plan.merge - 1)
     rates = [decays[0]] + [plan.swap(decays[0])] * (plan.merge - 1)
-    blocks = reorder(plan, [in_weight] + [plan.swap(in_weight)] * (plan.merge - 1))
-
+    block = reorder(plan, [in_weight] + [plan.swap(in_weight)] * (plan.merge - 1))
     ids = jnp.roll(block_ids, -me * local_tokens)
+    ids, rates = lax.optimization_barrier((ids, rates))
+    rank, places = rank_tokens(ids, groups)
+    part = place_tokens(plan, rank, 0, owns, [])
+
+    def fill(arriving):
+        if plan.merge == 2:
+            arriving = arriving + [plan.swap(tokens) for tokens in arriving]
+        return place_tokens(plan, rank, local_tokens, arriving, [part])
+
     if plan.ringed:
-        def step(block, with_):
-            return lax.optimization_barrier((plan.round(block), plan.cross(block), with_))[:2]
-
-        early, late, crossed = [blocks[0]], [blocks[1]], [[], []]
-        rank = part = None
+        blocks, crossed = [block], []
+        half = block.shape[0] // 2
         for k in range(plan.along - 1):
-            passed, across = step(early[-1], [[], [], late[-1:]][min(k, 2)] + [part] * (k == 1))
-            early.append(passed)
-            crossed[0].append(across)
-            if k == 0:
-                ids, rates, _ = lax.optimization_barrier((ids, rates, early[-1]))
-                rank, places = rank_tokens(ids, groups)
-            passed, across = step(late[-1], [])
-            late.append(passed)
-            crossed[1].append(across)
-            if k == 0:
-                rank, _ = lax.optimization_barrier((rank, late[-1]))
-                part = place_tokens(plan, rank, owns)
-        crossed[0].append(plan.cross(early[-1]))
-        arriving, _ = lax.optimization_barrier((arriving, crossed[0][-1]))
-        early = [b for pair in zip(early, crossed[0]) for b in pair]
+            with_ = part if k == 0 else ()
+            if k == plan.along - 2:
+                arriving, _ = lax.optimization_barrier((arriving, blocks[-1]))
+                x = with_ = fill(arriving)
+            passed, across, with_ = lax.optimization_barrier(
+                (plan.round(blocks[-1]), plan.cross(blocks[-1]), with_)
+            )
+            blocks.append(passed)
+            crossed.append(across)
+        last = [plan.cross(blocks[-1][:half]), plan.round(crossed[-1][half:])]
+        weights = blocks + crossed + last
     else:
-        rank = part = None
-        early, late = (
-            [lax.all_gather(b, "tm", axis=0, tiled=True, axis_index_groups=plan.groups())]
-            for b in blocks
-        )
-    if part is None:
-        rank, places = rank_tokens(ids, groups)
-        part = place_tokens(plan, rank, owns)
-    if plan.merge == 2:
-        arriving = arriving + [plan.swap(chunk) for chunk in arriving]
-    x, v, local, total = project_updates(plan, rates, rank, part, arriving, early, groups)
-    if plan.ringed:
-        late[-1], _ = lax.optimization_barrier((late[-1], total))
-        crossed[1].append(plan.cross(late[-1]))
-        late = [b for pair in zip(late, crossed[1]) for b in pair]
+        weights = [
+            lax.all_gather(block, "tm", axis=0, tiled=True, axis_index_groups=plan.groups())
+        ]
+        x = fill(arriving)
+    v, local, total = project_updates(plan, rates, x, weights, groups)
 
     def exchange(blocks):
         return lax.all_to_all(
@@ -748,12 +724,12 @@
 
     share = local.shape[1] // plan.chips
     arrived = exchange(total)
-    attended = [attend(plan, 0, block_lists, x, v, late, local)]
+    attended = [attend(plan, 0, block_lists, x, v, weights, local)]
     arrived, attended = lax.optimization_barrier((arrived, attended))
     states = scan_states(plan, arrived, share)
     x, states = lax.optimization_barrier((x, states))
     if plan.merge == 2:
-        attended.append(attend(plan, 1, block_lists, x, v, late, local))
+        attended.append(attend(plan, 1, block_lists, x, v, weights, local))
     state = exchange(states).reshape(-1, LANES)
 
     bases, readers = ([a[i] for a in attended] for i in range(2))

time: 143 us -> 118 us (0.83)
  starting transfers between devices: 34.8 us -> 20.7 us
  waiting for transfers between devices: 51.9 us -> 42.5 us
    ppermute x6 -> x4, waiting for transfers between devices: 21.6 us -> 15 us  [round(): return lax.ppermute(block, 'tm', pairs)]
    ppermute x8 -> x4, starting transfers between devices: 11 us -> 5.14 us  [cross(): return lax.ppermute(block, 'tm', pairs)]
    ppermute x6 -> x4, starting transfers between devices: 8.23 us -> 2.7 us  [round(): return lax.ppermute(block, 'tm', pairs)]
    ppermute x8 -> x4, waiting for transfers between devices: 10.6 us -> 6.69 us  [cross(): return lax.ppermute(block, 'tm', pairs)]
    all_to_all x2, waiting for transfers between devices: 4.75 us -> 8.32 us  [exchange(): lax.all_to_all(blocks, 'tm', split_axis=0, concat_axis=0, tiled=True, axi...]
    all_to_all x2, starting transfers between devices: 10.1 us -> 7.38 us  [exchange(): lax.all_to_all(blocks, 'tm', split_axis=0, concat_axis=0, tiled=True, axi...]
    ppermute x5, waiting for transfers between devices: 5.64 us -> 3.31 us  [swap(): return lax.ppermute(block, 'tm', [(t, t ^ 1) for t in range(self.frames)])]
    unnamed x53 -> x37, local copies, waits for them, and re-layouts: 9.17 us -> 8.16 us
  transfers between devices with their start and end apart: 24 -> 18, of which waited for: 12 -> 13; matrix products, arithmetic and copies ran while one was open for 1% -> 1% of each run, Pallas kernels for 16% -> 22%
where the time goes in v9:
time: 118 us; the launch traced here: 117 us
  Pallas kernels  44.8 us (38%)
  waiting for transfers between devices  42.5 us (36%)
  starting transfers between devices  20.7 us (18%)
  local copies, waits for them, and re-layouts  8.18 us (7%)
    pallas_call x2, Pallas kernels, attend(): pl.pallas_call(functools.partial(attend_kernel, plan, slot), in_specs=[sm...  18.2 us
    ppermute x4, waiting for transfers between devices, round(): return lax.ppermute(block, 'tm', pairs)  15 us
    pallas_call x1, Pallas kernels, project_updates(): pl.pallas_call(functools.partial(update_kernel, plan, groups), in_specs=[...  10.2 us
    all_to_all x2, waiting for transfers between devices, exchange(): lax.all_to_all(blocks, 'tm', split_axis=0, concat_axis=0, tiled=True, axi...  8.32 us
    unnamed x37, local copies, waits for them, and re-layouts  8.16 us
    all_to_all x2, starting transfers between devices, exchange(): lax.all_to_all(blocks, 'tm', split_axis=0, concat_axis=0, tiled=True, axi...  7.38 us
    pallas_call x2, Pallas kernels, place_tokens(): pl.pallas_call(functools.partial(place_kernel, plan.merge, parts, start),...  7.02 us
    ppermute x2, waiting for transfers between devices, to_peer(): return lax.ppermute(block, 'head', pairs)  6.93 us
  transfers between devices with their start and end apart: 18, of which 13 were waited for; matrix products, arithmetic and copies ran while one was open for 1% of the time, Pallas kernels for 22%

profile of v9, /device:TPU:0, one launch (start us, length us, event | category | flops | bytes accessed | tf_op | source)
XLA Modules:
  0.0 117.2 jit_solution(5691642342662567229)
XLA Ops:
  0.5 2.5 %collective-permute-start.1 = (bf16[512,1024]{1,0:T(8,128)(2,1)}, bf16[512,1024]{1,0:T(8,128)(2,1)S(1)}, u32[]{:S(2)}, u32[]{:S(2)}) collective-permute-start(bf16[512,1024]{1,0:T(8,128)(2,1)} %bitcast.6), channel_id=1, source_target_pairs={{0,1},{1,0},{2,3},{3,2},{4,5},{5,4},{6,7},{7,6},{8,9},{9,8},{10,11... | collective-permute-start | bytes 3145736 | tf_op jit(solution)/shard_map/ppermute | solution.py:91
  3.2 1.6 %collective-permute-done.2.refs_1_ = bf16[64,2560]{1,0:T(8,128)(2,1)S(1)} collective-permute-done((bf16[64,2560]{1,0:T(8,128)(2,1)}, bf16[64,2560]{1,0:T(8,128)(2,1)S(1)}, u32[]{:S(2)}, u32[]{:S(2)}) %collective-permute-start.2) | collective-permute-done | bytes 327712 | tf_op jit(solution)/shard_map/ppermute | solution.py:61
  4.8 1.0 copy-done.4
  6.0 1.6 %collective-permute-start.3 = (bf16[128,1280]{1,0:T(8,128)(2,1)S(1)}, bf16[128,1280]{1,0:T(8,128)(2,1)S(1)}, u32[]{:S(2)}, u32[]{:S(2)}) collective-permute-start(bf16[128,1280]{1,0:T(8,128)(2,1)S(1)} %reorder.1.refs_3_.refs_4_), channel_id=1, source_target_pairs={{0,8},{2,10},{4,12},{6,14},{8,16},{10,18},{12,20},{14,22},{16,24},... | collective-permute-start | bytes 983048 | tf_op jit(solution)/shard_map/ppermute | solution.py:66
  7.6 1.5 %collective-permute-start.4 = (bf16[128,1280]{1,0:T(8,128)(2,1)S(1)}, bf16[128,1280]{1,0:T(8,128)(2,1)S(1)}, u32[]{:S(2)}, u32[]{:S(2)}) collective-permute-start(bf16[128,1280]{1,0:T(8,128)(2,1)S(1)} %reorder.1.refs_3_.refs_4_), channel_id=1, source_target_pairs={{0,4},{2,6},{4,0},{6,2},{8,12},{10,14},{12,8},{14,10},{16,20},{18,... | collective-permute-start | bytes 983048 | tf_op jit(solution)/shard_map/ppermute | solution.py:71
  11.8 1.2 %copy-done.2 = bf16[1,512,1024]{2,1,0:T(8,128)(2,1)S(1)} copy-done((bf16[1,512,1024]{2,1,0:T(8,128)(2,1)S(1)}, bf16[1,512,1024]{2,1,0:T(8,128)(2,1)}, u32[]{:S(2)}) %copy-start.2) | copy-done | bytes 1048600
  13.0 3.5 %place_tokens.2.refs_2_ = bf16[2048,1024]{1,0:T(8,128)(2,1)S(1)} custom-call(f32[1,1024]{1,0:T(1,128)S(1)} %get-tuple-element.36.rank_ref, bf16[512,1024]{1,0:T(8,128)(2,1)S(1)} %bitcast.7, bf16[512,1024]{1,0:T(8,128)(2,1)S(1)} %collective-permute-done.5.refs_1_), custom_call_target="tpu_custom_call" | custom-call | bytes 4096 | tf_op jit(solution)/shard_map/place_tokens/pallas_call | solution.py:261
  16.5 1.2 %collective-permute-done.3.refs_4_.refs_5_ = bf16[128,1280]{1,0:T(8,128)(2,1)S(1)} collective-permute-done((bf16[128,1280]{1,0:T(8,128)(2,1)S(1)}, bf16[128,1280]{1,0:T(8,128)(2,1)S(1)}, u32[]{:S(2)}, u32[]{:S(2)}) %collective-permute-start.3) | collective-permute-done | bytes 327712 | tf_op jit(solution)/shard_map/ppermute | solution.py:66
  17.7 1.0 collective-permute-start.6
  18.7 1.5 %collective-permute-start.7 = (bf16[128,1280]{1,0:T(8,128)(2,1)S(1)}, bf16[128,1280]{1,0:T(8,128)(2,1)S(1)}, u32[]{:S(2)}, u32[]{:S(2)}) collective-permute-start(bf16[128,1280]{1,0:T(8,128)(2,1)S(1)} %collective-permute-done.3.refs_4_.refs_5_), channel_id=1, source_target_pairs={{0,4},{2,6},{4,0},{6,2},{8,12},{10,14},{12,8},{14,10},{16,20},{18,... | collective-permute-start | bytes 983048 | tf_op jit(solution)/shard_map/ppermute | solution.py:71
  20.2 8.4 %collective-permute-done.6.refs_5_.refs_6_ = bf16[128,1280]{1,0:T(8,128)(2,1)S(1)} collective-permute-done((bf16[128,1280]{1,0:T(8,128)(2,1)S(1)}, bf16[128,1280]{1,0:T(8,128)(2,1)S(1)}, u32[]{:S(2)}, u32[]{:S(2)}) %collective-permute-start.6) | collective-permute-done | bytes 327712 | tf_op jit(solution)/shard_map/ppermute | solution.py:66
  28.8 1.6 %collective-permute-start.10 = (bf16[128,1280]{1,0:T(8,128)(2,1)S(1)}, bf16[128,1280]{1,0:T(8,128)(2,1)S(1)}, u32[]{:S(2)}, u32[]{:S(2)}) collective-permute-start(bf16[128,1280]{1,0:T(8,128)(2,1)S(1)} %collective-permute-done.6.refs_5_.refs_6_), channel_id=1, source_target_pairs={{0,4},{2,6},{4,0},{6,2},{8,12},{10,14},{12,8},{14,10},{16,20},{18,... | collective-permute-start | bytes 983048 | tf_op jit(solution)/shard_map/ppermute | solution.py:71
  30.3 1.1 collective-permute-done.8.refs_1_
  31.4 3.6 %place_tokens.3.refs_2_.refs_1_ = bf16[2048,1024]{1,0:T(8,128)(2,1)S(1)} custom-call(f32[1,1024]{1,0:T(1,128)S(1)} %get-tuple-element.36.rank_ref, bf16[512,1024]{1,0:T(8,128)(2,1)S(1)} %collective-permute-done.1.refs_0_, bf16[512,1024]{1,0:T(8,128)(2,1)S(1)} %collective-permute-done.8.refs_1_, bf16[2048,1024]{1,0:T(8,128)(2,1)S(1)} %place_tokens.2.refs_2_), custom_call_target="tpu_custom_call" | custom-call | bytes 4096 | tf_op jit(solution)/shard_map/place_tokens/pallas_call | solution.py:261
  35.0 2.0 %copy-done = bf16[2048,1024]{1,0:T(8,128)(2,1)} copy-done((bf16[2048,1024]{1,0:T(8,128)(2,1)}, bf16[2048,1024]{1,0:T(8,128)(2,1)S(1)}, u32[]{:S(2)}) %copy-start) | copy-done | bytes 4194328
  37.0 1.9 %collective-permute-done.10.refs_9_.refs_10_ = bf16[128,1280]{1,0:T(8,128)(2,1)S(1)} collective-permute-done((bf16[128,1280]{1,0:T(8,128)(2,1)S(1)}, bf16[128,1280]{1,0:T(8,128)(2,1)S(1)}, u32[]{:S(2)}, u32[]{:S(2)}) %collective-permute-start.10) | collective-permute-done | bytes 327712 | tf_op jit(solution)/shard_map/ppermute | solution.py:71
  38.9 3.0 %collective-permute-done.9.refs_6_.refs_7_ = bf16[128,1280]{1,0:T(8,128)(2,1)S(1)} collective-permute-done((bf16[128,1280]{1,0:T(8,128)(2,1)S(1)}, bf16[128,1280]{1,0:T(8,128)(2,1)S(1)}, u32[]{:S(2)}, u32[]{:S(2)}) %collective-permute-start.9) | collective-permute-done | bytes 327712 | tf_op jit(solution)/shard_map/ppermute | solution.py:66
  42.6 4.8 %collective-permute-done.11.refs_10_.refs_11_ = bf16[64,1280]{1,0:T(8,128)(2,1)S(1)} collective-permute-done((bf16[64,1280]{1,0:T(8,128)(2,1)S(1)}, bf16[64,1280]{1,0:T(8,128)(2,1)S(1)}, u32[]{:S(2)}, u32[]{:S(2)}) %collective-permute-start.11) | collective-permute-done | bytes 163872 | tf_op jit(solution)/shard_map/ppermute | solution.py:71
  47.4 2.3 %collective-permute-done.12.refs_11_.refs_12_ = bf16[64,1280]{1,0:T(8,128)(2,1)S(1)} collective-permute-done((bf16[64,1280]{1,0:T(8,128)(2,1)S(1)}, bf16[64,1280]{1,0:T(8,128)(2,1)S(1)}, u32[]{:S(2)}, u32[]{:S(2)}) %collective-permute-start.12) | collective-permute-done | bytes 163872 | tf_op jit(solution)/shard_map/ppermute | solution.py:66
  50.4 10.2 %project_updates.1 = (bf16[2048,256]{1,0:T(8,128)(2,1)}, bf16[2,2048,128]{2,1,0:T(8,128)(2,1)}, bf16[8,272,128]{2,1,0:T(8,128)(2,1)}) custom-call(f32[8,16]{1,0:T(8,128)} %bitcast.11, f32[8,16]{1,0:T(8,128)} %copy-done.10, bf16[2048,1024]{1,0:T(8,128)(2,1)} %copy-done, bf16[128,1280]{1,0:T(8,128)(2,1)} %copy-done.5, bf16[128,1280]{1,0:T(8,128)(2,1)} %copy-done.12, ...), custom_call_target="tpu_custom_call" | custom-call | flops 4294967296 | bytes 12582912 | tf_op jit(solution)/shard_map/project_updates/pallas_call | solution.py:365
  60.6 3.7 %all-to-all-start = ((bf16[8,272,128]{2,1,0:T(8,128)(2,1)}), bf16[8,272,128]{2,1,0:T(8,128)(2,1)S(1)}, u32[]{:S(2)}, u32[]{:S(2)}) async-start(bf16[8,272,128]{2,1,0:T(8,128)(2,1)} %get-tuple-element.44), calls=%async_computation | async-start | bytes 1114112 | tf_op jit(solution)/shard_map/all_to_all | solution.py:720
  65.1 9.1 %attend.2 = (f32[1024,256]{1,0:T(8,128)}, bf16[1024,256]{1,0:T(8,128)(2,1)}) custom-call(s32[16,4]{1,0:T(8,128)} %copy.7.refs_0_, bf16[2048,1024]{1,0:T(8,128)(2,1)} %copy-done, bf16[2048,256]{1,0:T(8,128)(2,1)} %get-tuple-element.45.refs_2_, bf16[2,2048,128]{2,1,0:T(8,128)(2,1)} %get-tuple-element.46.refs_3_, bf16[128,1280]{1,0:T(8,128)(2,1)} %copy-done.5, ...), custom_call_target="tpu_custom_call" | custom-call | flops 4831838208 | bytes 11534336 | tf_op jit(solution)/shard_map/attend/pallas_call | solution.py:515
  74.2 3.5 %all-to-all-done.u_ref = bf16[8,272,128]{2,1,0:T(8,128)(2,1)S(1)} async-done(((bf16[8,272,128]{2,1,0:T(8,128)(2,1)}), bf16[8,272,128]{2,1,0:T(8,128)(2,1)S(1)}, u32[]{:S(2)}, u32[]{:S(2)}) %all-to-all-start) | async-done | bytes 557088 | tf_op jit(solution)/shard_map/all_to_all | solution.py:720
  78.6 3.6 %all-to-all-start.1 = ((bf16[8,256,128]{2,1,0:T(8,128)(2,1)}), bf16[8,256,128]{2,1,0:T(8,128)(2,1)S(1)}, u32[]{:S(2)}, u32[]{:S(2)}) async-start(bf16[8,256,128]{2,1,0:T(8,128)(2,1)} %scan_states.1), calls=%async_computation.1 | async-start | bytes 1048576 | tf_op jit(solution)/shard_map/all_to_all | solution.py:720
  82.3 9.1 %attend.3 = (f32[1024,256]{1,0:T(8,128)}, bf16[1024,256]{1,0:T(8,128)(2,1)}) custom-call(s32[16,4]{1,0:T(8,128)} %copy.7.refs_0_, bf16[2048,1024]{1,0:T(8,128)(2,1)} %copy-done, bf16[2048,256]{1,0:T(8,128)(2,1)} %get-tuple-element.45.refs_2_, bf16[2,2048,128]{2,1,0:T(8,128)(2,1)} %get-tuple-element.46.refs_3_, bf16[128,1280]{1,0:T(8,128)(2,1)} %copy-done.5, ...), custom_call_target="tpu_custom_call" | custom-call | flops 4831838208 | bytes 11534336 | tf_op jit(solution)/shard_map/attend/pallas_call | solution.py:515
  91.4 4.8 %all-to-all-done.1 = bf16[8,256,128]{2,1,0:T(8,128)(2,1)S(1)} async-done(((bf16[8,256,128]{2,1,0:T(8,128)(2,1)}), bf16[8,256,128]{2,1,0:T(8,128)(2,1)S(1)}, u32[]{:S(2)}, u32[]{:S(2)}) %all-to-all-start.1) | async-done | bytes 524320 | tf_op jit(solution)/shard_map/all_to_all | solution.py:720
  97.0 5.6 %mix.1 = (bf16[512,256]{1,0:T(8,128)(2,1)}, bf16[512,256]{1,0:T(8,128)(2,1)}, bf16[512,256]{1,0:T(8,128)(2,1)}, bf16[512,256]{1,0:T(8,128)(2,1)}) custom-call(f32[8,16]{1,0:T(8,128)} %bitcast.12, f32[8,16]{1,0:T(8,128)} %copy-done.10, f32[1024,256]{1,0:T(8,128)} %get-tuple-element.49.refs_2_, f32[1024,256]{1,0:T(8,128)} %get-tuple-element.52.refs_3_, ...), custom_call_target="tpu_custom_call" | custom-call | flops 1073741824 | bytes 6291456 | tf_op jit(solution)/shard_map/mix/pallas_call | solution.py:627
  102.6 1.4 %collective-permute-start.13 = (bf16[512,256]{1,0:T(8,128)(2,1)}, bf16[512,256]{1,0:T(8,128)(2,1)S(1)}, u32[]{:S(2)}, u32[]{:S(2)}) collective-permute-start(bf16[512,256]{1,0:T(8,128)(2,1)} %get-tuple-element.58), channel_id=1, source_target_pairs={{0,1},{1,0},{2,3},{3,2},{4,5},{5,4},{6,7},{7,6},{8,9},{9,8},{10,11... | collective-permute-start | bytes 786440 | tf_op jit(solution)/shard_map/ppermute | solution.py:91
  104.8 6.9 %collective-permute-done.13.refs_1_ = bf16[512,256]{1,0:T(8,128)(2,1)S(1)} collective-permute-done((bf16[512,256]{1,0:T(8,128)(2,1)}, bf16[512,256]{1,0:T(8,128)(2,1)S(1)}, u32[]{:S(2)}, u32[]{:S(2)}) %collective-permute-start.13) | collective-permute-done | bytes 262176 | tf_op jit(solution)/shard_map/ppermute | solution.py:91
  111.8 2.2 %collective-permute-done.15.refs_3_ = bf16[512,256]{1,0:T(8,128)(2,1)S(1)} collective-permute-done((bf16[512,256]{1,0:T(8,128)(2,1)}, bf16[512,256]{1,0:T(8,128)(2,1)S(1)}, u32[]{:S(2)}, u32[]{:S(2)}) %collective-permute-start.15) | collective-permute-done | bytes 262176 | tf_op jit(solution)/shard_map/ppermute | solution.py:99
  114.0 0.9 copy-done.6
  114.9 2.2 %project_out.1 = bf16[512,1024]{1,0:T(8,128)(2,1)} custom-call(bf16[1024,1024]{1,0:T(8,128)(2,1)S(1)} %copy-done.1, bf16[512,256]{1,0:T(8,128)(2,1)S(1)} %copy-done.6, bf16[512,256]{1,0:T(8,128)(2,1)S(1)} %collective-permute-done.13.refs_1_, bf16[512,256]{1,0:T(8,128)(2,1)S(1)} %collective-permute-done.14.refs_2_, ...), custom_call_target="tpu_custom_call" | custom-call | flops 1073741824 | bytes 4194304 | tf_op jit(solution)/shard_map/project_out/pallas_call | solution.py:666
  (54 shorter events, 8.2 us)
Async XLA Ops:
  0.0 11.8 %collective-permute-start.5 = (bf16[512,1024]{1,0:T(8,128)(2,1)}, bf16[512,1024]{1,0:T(8,128)(2,1)S(1)}, u32[]{:S(2)}, u32[]{:S(2)}) collective-permute-start(bf16[512,1024]{1,0:T(8,128)(2,1)} %bitcast.5), channel_id=1, source_target_pairs={{0,2},{2,0},{4,6},{6,4},{8,10},{10,8},{12,14},{14,12},{16,18},{18,... | collective-permute-start | bytes 3145736 | tf_op jit(solution)/shard_map/ppermute | solution.py:61
  0.5 28.2 %collective-permute-start.1 = (bf16[512,1024]{1,0:T(8,128)(2,1)}, bf16[512,1024]{1,0:T(8,128)(2,1)S(1)}, u32[]{:S(2)}, u32[]{:S(2)}) collective-permute-start(bf16[512,1024]{1,0:T(8,128)(2,1)} %bitcast.6), channel_id=1, source_target_pairs={{0,1},{1,0},{2,3},{3,2},{4,5},{5,4},{6,7},{7,6},{8,9},{9,8},{10,11... | collective-permute-start | bytes 3145736 | tf_op jit(solution)/shard_map/ppermute | solution.py:91
  3.0 1.8 %collective-permute-start.2 = (bf16[64,2560]{1,0:T(8,128)(2,1)}, bf16[64,2560]{1,0:T(8,128)(2,1)S(1)}, u32[]{:S(2)}, u32[]{:S(2)}) collective-permute-start(bf16[64,2560]{1,0:T(8,128)(2,1)} %refs_0_.3), channel_id=1, source_target_pairs={{0,2},{2,0},{4,6},{6,4},{8,10},{10,8},{12,14},{14,12},{16,18},{18,... | collective-permute-start | bytes 983048 | tf_op jit(solution)/shard_map/ppermute | solution.py:61
  4.8 1.0 copy-start.4
  5.9 43.8 %copy-start.5 = (bf16[128,1280]{1,0:T(8,128)(2,1)}, bf16[128,1280]{1,0:T(8,128)(2,1)S(1)}, u32[]{:S(2)}) copy-start(bf16[128,1280]{1,0:T(8,128)(2,1)S(1)} %reorder.1.refs_3_.refs_4_) | copy-start | bytes 983044
  6.0 11.8 %collective-permute-start.3 = (bf16[128,1280]{1,0:T(8,128)(2,1)S(1)}, bf16[128,1280]{1,0:T(8,128)(2,1)S(1)}, u32[]{:S(2)}, u32[]{:S(2)}) collective-permute-start(bf16[128,1280]{1,0:T(8,128)(2,1)S(1)} %reorder.1.refs_3_.refs_4_), channel_id=1, source_target_pairs={{0,8},{2,10},{4,12},{6,14},{8,16},{10,18},{12,20},{14,22},{16,24},... | collective-permute-start | bytes 983048 | tf_op jit(solution)/shard_map/ppermute | solution.py:66
  7.6 10.1 %collective-permute-start.4 = (bf16[128,1280]{1,0:T(8,128)(2,1)S(1)}, bf16[128,1280]{1,0:T(8,128)(2,1)S(1)}, u32[]{:S(2)}, u32[]{:S(2)}) collective-permute-start(bf16[128,1280]{1,0:T(8,128)(2,1)S(1)} %reorder.1.refs_3_.refs_4_), channel_id=1, source_target_pairs={{0,4},{2,6},{4,0},{6,2},{8,12},{10,14},{12,8},{14,10},{16,20},{18,... | collective-permute-start | bytes 983048 | tf_op jit(solution)/shard_map/ppermute | solution.py:71
  9.1 1.4 %collective-permute-start = (f32[8,16]{1,0:T(8,128)}, f32[8,16]{1,0:T(8,128)S(1)}, u32[]{:S(2)}, u32[]{:S(2)}) collective-permute-start(f32[8,16]{1,0:T(8,128)} %bitcast.10), channel_id=1, source_target_pairs={{0,2},{2,0},{4,6},{6,4},{8,10},{10,8},{12,14},{14,12},{16,18},{18,... | collective-permute-start | bytes 1544 | tf_op jit(solution)/shard_map/ppermute | solution.py:61
  10.5 24.5 %copy-start.10 = (f32[8,16]{1,0:T(8,128)}, f32[8,16]{1,0:T(8,128)S(1)}, u32[]{:S(2)}) copy-start(f32[8,16]{1,0:T(8,128)S(1)} %collective-permute-done.refs_1_) | copy-start | bytes 1540
  11.8 1.2 %copy-start.2 = (bf16[1,512,1024]{2,1,0:T(8,128)(2,1)S(1)}, bf16[1,512,1024]{2,1,0:T(8,128)(2,1)}, u32[]{:S(2)}) copy-start(bf16[1,512,1024]{2,1,0:T(8,128)(2,1)} %param.6) | copy-start | bytes 3145732
  17.7 17.3 %copy-start.12 = (bf16[128,1280]{1,0:T(8,128)(2,1)}, bf16[128,1280]{1,0:T(8,128)(2,1)S(1)}, u32[]{:S(2)}) copy-start(bf16[128,1280]{1,0:T(8,128)(2,1)S(1)} %collective-permute-done.3.refs_4_.refs_5_) | copy-start | bytes 983044
  17.7 17.3 %copy-start.13 = (bf16[128,1280]{1,0:T(8,128)(2,1)}, bf16[128,1280]{1,0:T(8,128)(2,1)S(1)}, u32[]{:S(2)}) copy-start(bf16[128,1280]{1,0:T(8,128)(2,1)S(1)} %collective-permute-done.4.refs_7_.refs_8_) | copy-start | bytes 983044
  17.7 10.9 %collective-permute-start.6 = (bf16[128,1280]{1,0:T(8,128)(2,1)S(1)}, bf16[128,1280]{1,0:T(8,128)(2,1)S(1)}, u32[]{:S(2)}, u32[]{:S(2)}) collective-permute-start(bf16[128,1280]{1,0:T(8,128)(2,1)S(1)} %collective-permute-done.3.refs_4_.refs_5_), channel_id=1, source_target_pairs={{0,8},{2,10},{4,12},{6,14},{8,16},{10,18},{12,20},{14,22},{16,24},... | collective-permute-start | bytes 983048 | tf_op jit(solution)/shard_map/ppermute | solution.py:66
  18.7 9.9 %collective-permute-start.7 = (bf16[128,1280]{1,0:T(8,128)(2,1)S(1)}, bf16[128,1280]{1,0:T(8,128)(2,1)S(1)}, u32[]{:S(2)}, u32[]{:S(2)}) collective-permute-start(bf16[128,1280]{1,0:T(8,128)(2,1)S(1)} %collective-permute-done.3.refs_4_.refs_5_), channel_id=1, source_target_pairs={{0,4},{2,6},{4,0},{6,2},{8,12},{10,14},{12,8},{14,10},{16,20},{18,... | collective-permute-start | bytes 983048 | tf_op jit(solution)/shard_map/ppermute | solution.py:71
  28.7 6.3 %copy-start.14 = (bf16[128,1280]{1,0:T(8,128)(2,1)}, bf16[128,1280]{1,0:T(8,128)(2,1)S(1)}, u32[]{:S(2)}) copy-start(bf16[128,1280]{1,0:T(8,128)(2,1)S(1)} %collective-permute-done.6.refs_5_.refs_6_) | copy-start | bytes 983044
  28.7 6.3 %copy-start.15 = (bf16[128,1280]{1,0:T(8,128)(2,1)}, bf16[128,1280]{1,0:T(8,128)(2,1)S(1)}, u32[]{:S(2)}) copy-start(bf16[128,1280]{1,0:T(8,128)(2,1)S(1)} %collective-permute-done.7.refs_8_.refs_9_) | copy-start | bytes 983044
  28.7 2.7 %collective-permute-start.8 = (bf16[512,1024]{1,0:T(8,128)(2,1)S(1)}, bf16[512,1024]{1,0:T(8,128)(2,1)S(1)}, u32[]{:S(2)}, u32[]{:S(2)}) collective-permute-start(bf16[512,1024]{1,0:T(8,128)(2,1)S(1)} %collective-permute-done.1.refs_0_), channel_id=1, source_target_pairs={{0,2},{2,0},{4,6},{6,4},{8,10},{10,8},{12,14},{14,12},{16,18},{18,... | collective-permute-start | bytes 3145736 | tf_op jit(solution)/shard_map/ppermute | solution.py:61
  28.8 10.1 %collective-permute-start.10 = (bf16[128,1280]{1,0:T(8,128)(2,1)S(1)}, bf16[128,1280]{1,0:T(8,128)(2,1)S(1)}, u32[]{:S(2)}, u32[]{:S(2)}) collective-permute-start(bf16[128,1280]{1,0:T(8,128)(2,1)S(1)} %collective-permute-done.6.refs_5_.refs_6_), channel_id=1, source_target_pairs={{0,4},{2,6},{4,0},{6,2},{8,12},{10,14},{12,8},{14,10},{16,20},{18,... | collective-permute-start | bytes 983048 | tf_op jit(solution)/shard_map/ppermute | solution.py:71
  30.3 11.6 %collective-permute-start.9 = (bf16[128,1280]{1,0:T(8,128)(2,1)S(1)}, bf16[128,1280]{1,0:T(8,128)(2,1)S(1)}, u32[]{:S(2)}, u32[]{:S(2)}) collective-permute-start(bf16[128,1280]{1,0:T(8,128)(2,1)S(1)} %collective-permute-done.6.refs_5_.refs_6_), channel_id=1, source_target_pairs={{0,8},{2,10},{4,12},{6,14},{8,16},{10,18},{12,20},{14,22},{16,24},... | collective-permute-start | bytes 983048 | tf_op jit(solution)/shard_map/ppermute | solution.py:66
  35.0 2.0 %copy-start = (bf16[2048,1024]{1,0:T(8,128)(2,1)}, bf16[2048,1024]{1,0:T(8,128)(2,1)S(1)}, u32[]{:S(2)}) copy-start(bf16[2048,1024]{1,0:T(8,128)(2,1)S(1)} %place_tokens.3.refs_2_.refs_1_) | copy-start | bytes 12582916
  38.9 10.8 %copy-start.8 = (bf16[128,1280]{1,0:T(8,128)(2,1)}, bf16[128,1280]{1,0:T(8,128)(2,1)S(1)}, u32[]{:S(2)}) copy-start(bf16[128,1280]{1,0:T(8,128)(2,1)S(1)} %collective-permute-done.10.refs_9_.refs_10_) | copy-start | bytes 983044
  41.9 7.8 %copy-start.9 = (bf16[128,1280]{1,0:T(8,128)(2,1)}, bf16[128,1280]{1,0:T(8,128)(2,1)S(1)}, u32[]{:S(2)}) copy-start(bf16[128,1280]{1,0:T(8,128)(2,1)S(1)} %collective-permute-done.9.refs_6_.refs_7_) | copy-start | bytes 983044
  41.9 5.5 %collective-permute-start.11 = (bf16[64,1280]{1,0:T(8,128)(2,1)S(1)}, bf16[64,1280]{1,0:T(8,128)(2,1)S(1)}, u32[]{:S(2)}, u32[]{:S(2)}) collective-permute-start(bf16[64,1280]{1,0:T(8,128)(2,1)S(1)} %slice.6), channel_id=1, source_target_pairs={{0,4},{2,6},{4,0},{6,2},{8,12},{10,14},{12,8},{14,10},{16,20},{18,... | collective-permute-start | bytes 491528 | tf_op jit(solution)/shard_map/ppermute | solution.py:71
  42.5 21.9 %copy-start.11 = (s32[16,4]{0,1:T(4,128)S(1)}, s32[16,4]{0,1:T(4,128)}, u32[]{:S(2)}) copy-start(s32[16,4]{0,1:T(4,128)} %param.10) | copy-start | bytes 772
  42.5 7.2 %collective-permute-start.12 = (bf16[64,1280]{1,0:T(8,128)(2,1)S(1)}, bf16[64,1280]{1,0:T(8,128)(2,1)S(1)}, u32[]{:S(2)}, u32[]{:S(2)}) collective-permute-start(bf16[64,1280]{1,0:T(8,128)(2,1)S(1)} %slice.7), channel_id=1, source_target_pairs={{0,8},{2,10},{4,12},{6,14},{8,16},{10,18},{12,20},{14,22},{16,24},... | collective-permute-start | bytes 491528 | tf_op jit(solution)/shard_map/ppermute | solution.py:66
  47.4 2.3 %copy-start.16 = (bf16[64,1280]{1,0:T(8,128)(2,1)}, bf16[64,1280]{1,0:T(8,128)(2,1)S(1)}, u32[]{:S(2)}) copy-start(bf16[64,1280]{1,0:T(8,128)(2,1)S(1)} %collective-permute-done.11.refs_10_.refs_11_) | copy-start | bytes 491524
  60.6 17.0 %all-to-all-start = ((bf16[8,272,128]{2,1,0:T(8,128)(2,1)}), bf16[8,272,128]{2,1,0:T(8,128)(2,1)S(1)}, u32[]{:S(2)}, u32[]{:S(2)}) async-start(bf16[8,272,128]{2,1,0:T(8,128)(2,1)} %get-tuple-element.44), calls=%async_computation | async-start | bytes 1114112 | tf_op jit(solution)/shard_map/all_to_all | solution.py:720
  78.6 17.6 %all-to-all-start.1 = ((bf16[8,256,128]{2,1,0:T(8,128)(2,1)}), bf16[8,256,128]{2,1,0:T(8,128)(2,1)S(1)}, u32[]{:S(2)}, u32[]{:S(2)}) async-start(bf16[8,256,128]{2,1,0:T(8,128)(2,1)} %scan_states.1), calls=%async_computation.1 | async-start | bytes 1048576 | tf_op jit(solution)/shard_map/all_to_all | solution.py:720
  91.4 22.6 %copy-start.1 = (bf16[1024,1024]{1,0:T(8,128)(2,1)S(1)}, bf16[1024,1024]{1,0:T(8,128)(2,1)}, u32[]{:S(2)}) copy-start(bf16[1024,1024]{1,0:T(8,128)(2,1)} %w_ref.1) | copy-start | bytes 6291460
  102.6 9.1 %collective-permute-start.13 = (bf16[512,256]{1,0:T(8,128)(2,1)}, bf16[512,256]{1,0:T(8,128)(2,1)S(1)}, u32[]{:S(2)}, u32[]{:S(2)}) collective-permute-start(bf16[512,256]{1,0:T(8,128)(2,1)} %get-tuple-element.58), channel_id=1, source_target_pairs={{0,1},{1,0},{2,3},{3,2},{4,5},{5,4},{6,7},{7,6},{8,9},{9,8},{10,11... | collective-permute-start | bytes 786440 | tf_op jit(solution)/shard_map/ppermute | solution.py:91
  104.0 7.8 %collective-permute-start.14 = (bf16[512,256]{1,0:T(8,128)(2,1)}, bf16[512,256]{1,0:T(8,128)(2,1)S(1)}, u32[]{:S(2)}, u32[]{:S(2)}) collective-permute-start(bf16[512,256]{1,0:T(8,128)(2,1)} %get-tuple-element.59), channel_id=1, source_target_pairs={{0,2},{2,0},{4,6},{6,4},{8,10},{10,8},{12,14},{14,12},{16,18},{18,... | collective-permute-start | bytes 786440 | tf_op jit(solution)/shard_map/ppermute | solution.py:61
  104.0 10.0 %collective-permute-start.15 = (bf16[512,256]{1,0:T(8,128)(2,1)}, bf16[512,256]{1,0:T(8,128)(2,1)S(1)}, u32[]{:S(2)}, u32[]{:S(2)}) collective-permute-start(bf16[512,256]{1,0:T(8,128)(2,1)} %get-tuple-element.60), channel_id=1, source_target_pairs={{0,3},{1,2},{2,1},{3,0},{4,7},{5,6},{6,5},{7,4},{8,11},{9,10},{10,... | collective-permute-start | bytes 786440 | tf_op jit(solution)/shard_map/ppermute | solution.py:99
  (4 other events, 3.3 us)

commit v10 on v9

--- a/solution.py
+++ b/solution.py
@@ -41,7 +41,7 @@
 
 
 class Plan:
-    def __init__(self, frames, peers, heads_here):
+    def __init__(self, frames, peers, heads_here, width):
         self.merge = 2 if frames % 2 == 0 and heads_here % 4 == 0 else 1
         self.frames, self.peers = frames, peers
         self.heads = heads_here // self.merge
@@ -49,7 +49,7 @@
         self.chips = frames // self.merge
         self.across = 2 if self.chips % 2 == 0 else 1
         self.along = self.chips // self.across
-        self.ringed = self.across == 2 and 2 <= self.along <= 8
+        self.ringed = self.across == 2 and 2 <= self.along <= 8 and width % (self.chips * LANES) == 0
 
     def core(self):
         return lax.rem(lax.axis_index("tm"), self.merge)
@@ -69,6 +69,10 @@
         c = self.merge
         pairs = [(t, (t // c ^ 1) * c + t % c) for t in range(self.frames)]
         return lax.ppermute(block, "tm", pairs)
+
+    def last_chip(self):
+        a, b = lax.div(self.chip(), self.across), lax.rem(self.chip(), self.across)
+        return lax.rem(a + 1, self.along) * self.across + (self.across - 1 - b)
 
     def places(self, refs):
         if len(refs) == 1:
@@ -268,26 +272,17 @@
     )(rank, *frames, *base)
 
 
-def update_kernel(plan, groups, *refs):
-    decay_refs, x_in, refs = refs[: plan.merge], refs[plan.merge], refs[plan.merge + 1 :]
-    w_refs, refs = refs[:-10], refs[-10:]
-    v_out, local_out, total_ref, w, turned, x, v, u, left, sems = refs
-    copies = Copies(sems)
-    every = x.shape[0]
-    tokens = every // plan.merge
-    block = tokens // groups
+def project_kernel(plan, x_ref, *refs):
+    w_refs, (v_ref, b_ref, rest_ref, w, turned) = refs[:-5], refs[-5:]
+    every = x_ref.shape[0]
     step = 256
-    here = step // block
     cols = plan.pairs * LANES
-
-    weights, arriving = [], []
+    if len(w_refs) > 1:
+        w[...] = jnp.zeros_like(w)
+        turned[...] = jnp.zeros_like(turned)
     for ref, rows in plan.places(w_refs):
-        weights.append(copies.start(ref.at[:, cols : 2 * cols], turned.at[rows]))
-        weights.append(copies.start(ref.at[:, :cols], w.at[rows]))
-    for at in range(0, every, step):
-        arriving.append(copies.start(x_in.at[at : at + step], x.at[at : at + step]))
-
-    finish(weights)
+        w[rows, :] = ref[:, :cols]
+        turned[rows, :] = ref[:, cols : 2 * cols]
     maps = jnp.concatenate(
         [
             turned[at : at + LANES, :].astype(f32).T.astype(bf16)
@@ -295,17 +290,66 @@
         ],
         axis=1,
     )
+    for at in range(0, every, step):
+        x = x_ref[at : at + step, :]
+        v_ref[at : at + step, :] = jnp.dot(x, w[...], preferred_element_type=f32)
+        b_ref[:, at : at + step] = lax.dot_general(
+            maps, x, (((1,), (1,)), ((), ())), preferred_element_type=f32
+        )
+    count = rest_ref.shape[1]
+    there = plan.last_chip() * count
+    for at in range(0, every, step):
+        rest = x_ref[at : at + step, :count]
+        for c in range(count, x_ref.shape[1], count):
+            rest = jnp.where(there == c, x_ref[at : at + step, c : c + count], rest)
+        rest_ref[at : at + step, :] = rest
+
+
+def project(plan, x, weights):
+    every, width = x.shape
+    cols = plan.pairs * LANES
+    count = max(LANES, width // plan.chips)
+    return pl.pallas_call(
+        functools.partial(project_kernel, plan),
+        out_shape=(
+            jax.ShapeDtypeStruct((every, cols), f32),
+            jax.ShapeDtypeStruct((cols, every), f32),
+            jax.ShapeDtypeStruct((every, count), bf16),
+        ),
+        scratch_shapes=[pltpu.VMEM((width, cols), bf16), pltpu.VMEM((width, cols), bf16)],
+        compiler_params=params(),
+        cost_estimate=cost(0, 4 * width),
+        name="project",
+    )(x, *weights)
+
+
+def update_kernel(plan, groups, *refs):
+    decay_refs, refs = refs[: plan.merge], refs[plan.merge :]
+    v_ref, b_ref, x_ref, last_refs, (left, total_ref, u) = (
+        refs[0], refs[1], refs[2], refs[3:-3], refs[-3:]
+    )
+    every = v_ref.shape[0]
+    tokens = every // plan.merge
+    block = tokens // groups
+    step = 256
+    here = step // block
+    cols = plan.pairs * LANES
+    if last_refs:
+        w = jnp.concatenate([ref[:, : 2 * cols] for ref in last_refs], axis=0)
+        maps = w[:, cols:].astype(f32).T.astype(bf16)
+        w = w[:, :cols]
+
     lane = lax.div(lax.broadcasted_iota(jnp.int32, (LANES, step), 1), block)
-    leaving = []
     for at in range(0, every, step):
         there = slice(at, at + step)
-        arriving[at // step].wait()
-        values = jnp.dot(x[there, :], w[...], preferred_element_type=f32).astype(bf16)
-        v[there, :] = values
-        leaving.append(copies.start(v.at[there], v_out.at[there]))
-        b = lax.dot_general(
-            maps, x[there, :], (((1,), (1,)), ((), ())), preferred_element_type=f32
-        )
+        values, b = v_ref[there, :], b_ref[:, there]
+        if last_refs:
+            x = x_ref[there, :]
+            values = values + jnp.dot(x, w, preferred_element_type=f32)
+            b = b + lax.dot_general(
+                maps, x, (((1,), (1,)), ((), ())), preferred_element_type=f32
+            )
+        values = values.astype(bf16)
         for p in range(plan.pairs):
             mine = b[p * LANES : (p + 1) * LANES]
             wide = jnp.concatenate(
@@ -349,41 +393,28 @@
                 at = share + n * items + i
                 total_ref[d, at : at + 1, :] = piece
                 product = product - piece.astype(f32)
-    leaving.append(copies.start(left, local_out))
-    finish(leaving)
 
 
 def share_rows(share):
     return share + 16 * -(-3 * max(1, share // N) // 16)
 
 
-def project_updates(plan, decays, x, weights, groups):
-    every, width = x.shape
-    cols = plan.pairs * LANES
+def block_updates(plan, decays, v, b, x, last, groups):
+    every, cols = v.shape
     rows = plan.pairs * groups * N
     share = rows // plan.chips
     return pl.pallas_call(
         functools.partial(update_kernel, plan, groups),
-        in_specs=[smem] * plan.merge + [hbm] * (1 + len(weights)),
-        out_specs=(hbm,) * 2 + (vmem,),
+        in_specs=[smem] * plan.merge + [vmem] * (3 + len(last)),
         out_shape=(
-            jax.ShapeDtypeStruct((every, cols), bf16),
             jax.ShapeDtypeStruct((plan.merge, rows, LANES), bf16),
             jax.ShapeDtypeStruct((plan.chips, share_rows(share), LANES), bf16),
         ),
-        scratch_shapes=[
-            pltpu.VMEM((width, cols), bf16),
-            pltpu.VMEM((width, cols), bf16),
-            pltpu.VMEM((every, width), bf16),
-            pltpu.VMEM((every, cols), bf16),
-            pltpu.VMEM((plan.merge, rows, LANES), f32),
-            pltpu.VMEM((plan.merge, rows, LANES), bf16),
-            Copies.scratch(),
-        ],
-        compiler_params=params(60),
-        cost_estimate=cost(4 * every * width * 2 * cols, 6 * every * width),
-        name="project_updates",
-    )(*decays, x, *weights)
+        scratch_shapes=[pltpu.VMEM((plan.merge, rows, LANES), f32)],
+        compiler_params=params(),
+        cost_estimate=cost(4 * every * 256 * 2 * cols, 6 * every * cols),
+        name="block_updates",
+    )(*decays, v, b, x, *last)
 
 
 def scan_kernel(plan, u_ref, s_ref):
@@ -413,27 +444,26 @@
 
 
 def attend_kernel(plan, slot, *refs):
-    lists_ref, x_in, v_in, local_in, refs = refs[0], refs[1], refs[2], refs[3], refs[4:]
-    w_refs, refs = refs[:-13], refs[-13:]
-    a_out, c_out, x, v, local, w, q_ref, k_ref, wide_v, e_ref, a, c_ref, sems = refs
+    lists_ref, x_in, local_in, refs = refs[0], refs[1], refs[2], refs[3:]
+    w_refs, refs = refs[:-12], refs[-12:]
+    a_out, c_out, x, local, w, q_ref, k_ref, wide_v, e_ref, a, c_ref, sems = refs
     copies = Copies(sems)
     tokens = x.shape[0]
     groups, chosen = lists_ref.shape
     block = tokens // groups
     step = 256
     per = step // block
-
-    early = 2 * plan.pairs * LANES
-    weights = [
-        copies.start(ref.at[:, early : early + w.shape[1]], w.at[rows])
-        for ref, rows in plan.places(w_refs)
-    ]
+    wide = plan.pairs * LANES
+
+    weights = []
+    for ref, rows in plan.places(w_refs):
+        weights.append(copies.start(ref.at[:, :wide], w.at[rows, :wide]))
+        weights.append(copies.start(ref.at[:, 2 * wide :], w.at[rows, wide:]))
     arriving = []
     for at in range(0, tokens, step):
         from_ = slice(slot * tokens + at, slot * tokens + at + step)
         arriving.append(copies.start(x_in.at[from_], x.at[at : at + step]))
-    mine = slice(slot * tokens, (slot + 1) * tokens)
-    later = [copies.start(v_in.at[mine], v), copies.start(local_in.at[slot], local)]
+    later = copies.start(local_in.at[slot], local)
 
     same = lax.div(lax.broadcasted_iota(jnp.int32, (2 * LANES, 2 * LANES), 0), HD) == lax.div(
         lax.broadcasted_iota(jnp.int32, (2 * LANES, 2 * LANES), 1), HD
@@ -456,7 +486,8 @@
         every = jnp.dot(x[rows, :], w[...], preferred_element_type=f32).astype(bf16)
         for p in range(plan.pairs):
             cols = slice(p * LANES, (p + 1) * LANES)
-            first = 3 * p * LANES
+            wide_v[p, rows, :LANES] = every[:, cols]
+            first = wide + 3 * p * LANES
             c_ref[rows, cols] = every[:, first + 2 * LANES : first + 3 * LANES]
             both = head_norm(every[:, first : first + 2 * LANES].astype(f32))
             k_ref[p, rows, :] = both[:, LANES:].astype(bf16)
@@ -467,9 +498,8 @@
                 part = slice(i * block, (i + 1) * block)
                 q_ref[p, at // block + i] = jnp.concatenate([one[part], two[part]], axis=0)
     leaving = [copies.start(c_ref, c_out)]
-    finish(later)
+    later.wait()
     for p in range(plan.pairs):
-        wide_v[p, :, :LANES] = v[:, p * LANES : (p + 1) * LANES]
         wide_v[p, :, LANES:] = jnp.ones((tokens, LANES), bf16)
 
     scale = math.log2(math.e) / math.sqrt(HD)
@@ -506,7 +536,7 @@
     finish(leaving)
 
 
-def attend(plan, slot, lists, x, v, weights, local):
+def attend(plan, slot, lists, x, weights, local):
     every, width = x.shape
     groups, chosen = lists.shape
     tokens = every // plan.merge
@@ -514,13 +544,12 @@
     cols = plan.pairs * LANES
     return pl.pallas_call(
         functools.partial(attend_kernel, plan, slot),
-        in_specs=[smem] + [hbm] * (3 + len(weights)),
+        in_specs=[smem] + [hbm] * (2 + len(weights)),
         out_specs=(hbm,) * 2,
         scratch_shapes=[
             pltpu.VMEM((tokens, width), bf16),
-            pltpu.VMEM((tokens, cols), bf16),
             pltpu.VMEM(local.shape[1:], bf16),
-            pltpu.VMEM((width, 3 * cols), bf16),
+            pltpu.VMEM((width, 4 * cols), bf16),
             pltpu.VMEM((plan.pairs, groups, 2 * block, LANES), bf16),
             pltpu.VMEM((plan.pairs, tokens, LANES), bf16),
             pltpu.VMEM((plan.pairs, tokens, 2 * LANES), bf16),
@@ -540,7 +569,7 @@
             2 * plan.pairs * tokens * chosen * block,
         ),
         name="attend",
-    )(lists, x, v, local, *weights)
+    )(lists, x, local, *weights)
 
 
 def read_out(readers, state, block):
@@ -598,26 +627,28 @@
 
     ranking.wait()
     local = tokens // plan.peers
-    step = min(256, local)
-    for at in range(0, tokens, step):
+    for k in list(range(1, plan.peers)) + [0]:
+        placed = back_rows(rank, k * local, mixed, local)
+        for s in range(plan.merge):
+            out_refs[s * plan.peers + k][...] = placed[:, s * width : (s + 1) * width]
+
+
+def back_rows(rank, start, mixed, rows):
+    tokens = rank.shape[0]
+    step = min(256, rows)
+    placed = []
+    for at in range(start, start + rows, step):
         place = rank[at : at + step, :]
+        lane = lax.broadcasted_iota(jnp.int32, place.shape, 1)
         pick = jnp.concatenate(
             [
-                jnp.where(
-                    (lax.broadcasted_iota(jnp.int32, place.shape, 1) + t).astype(f32) == place,
-                    1.0,
-                    0.0,
-                ).astype(bf16)
+                jnp.where((lane + t).astype(f32) == place, 1.0, 0.0).astype(bf16)
                 for t in range(0, tokens, LANES)
             ],
             axis=1,
         )
-        placed = jnp.dot(pick, mixed[...], preferred_element_type=f32).astype(bf16)
-        k, to = at // local, at % local
-        for s in range(plan.merge):
-            out_refs[s * plan.peers + k][to : to + step, :] = placed[
-                :, s * width : (s + 1) * width
-            ]
+        placed.append(jnp.dot(pick, mixed[...], preferred_element_type=f32).astype(bf16))
+    return jnp.concatenate(placed, axis=0)
 
 
 def mix(plan, decays, attended, readers, state, rank, groups):
@@ -643,33 +674,28 @@
     )(*decays, *attended, *readers, state, rank)
 
 
-def out_kernel(plan, w_ref, *refs):
-    part_refs, out_ref = refs[:-1], refs[-1]
+def out_kernel(plan, sources, w_ref, *refs):
+    part_refs, base_refs, out_ref = refs[: len(sources)], refs[len(sources) : -1], refs[-1]
     depth = part_refs[0].shape[1]
     core, me = plan.core(), lax.axis_index("head")
-    total = None
-    for s in range(plan.merge):
-        for k in range(plan.peers):
-            owner = lax.rem(me - k + plan.peers, plan.peers) * plan.merge
-            owner = owner + (core if s == 0 else 1 - core)
-            rows = pl.ds(pl.multiple_of(owner * depth, depth), depth)
-            term = jnp.dot(
-                part_refs[s * plan.peers + k][...], w_ref[rows, :], preferred_element_type=f32
-            )
-            total = term if total is None else total + term
-    out_ref[...] = total.astype(bf16)
-
-
-def project_out(plan, w, parts):
-    local = parts[0].shape[0]
-    width = w.shape[1]
-    return pl.pallas_call(
-        functools.partial(out_kernel, plan),
-        out_shape=jax.ShapeDtypeStruct((local, width), bf16),
+    total = base_refs[0][...] if base_refs else 0.0
+    for (s, k), part in zip(sources, part_refs):
+        owner = lax.rem(me - k + plan.peers, plan.peers) * plan.merge
+        owner = owner + (core if s == 0 else 1 - core)
+        rows = pl.ds(pl.multiple_of(owner * depth, depth), depth)
+        total = total + jnp.dot(part[...], w_ref[rows, :], preferred_element_type=f32)
+    out_ref[...] = total.astype(out_ref.dtype)
+
+
+def project_out(plan, w, parts, base, kind):
+    local, width = next(iter(parts.values())).shape[0], w.shape[1]
+    return pl.pallas_call(
+        functools.partial(out_kernel, plan, list(parts)),
+        out_shape=jax.ShapeDtypeStruct((local, width), kind),
         compiler_params=params(),
-        cost_estimate=cost(2 * local * w.size, 2 * (w.size + 2 * local * width)),
+        cost_estimate=cost(0, 4 * local),
         name="project_out",
-    )(w, *parts)
+    )(w, *parts.values(), *base)
 
 
 def body(frames_in, in_weight, out_weight, block_ids, block_lists, decays):
@@ -677,7 +703,7 @@
     heads_here = decays.shape[1]
     groups = block_lists.shape[0]
     me = lax.axis_index("head")
-    plan = Plan(lax.axis_size("tm"), lax.axis_size("head"), heads_here)
+    plan = Plan(lax.axis_size("tm"), lax.axis_size("head"), heads_here, frames_in.shape[2])
 
     own = frames_in[0]
     arriving = [plan.to_peer(own, plan.peers - k, False) for k in range(1, plan.peers)]
@@ -714,7 +740,12 @@
             lax.all_gather(block, "tm", axis=0, tiled=True, axis_index_groups=plan.groups())
         ]
         x = fill(arriving)
-    v, local, total = project_updates(plan, rates, x, weights, groups)
+    if plan.ringed:
+        v, b, x_last = project(plan, x, weights[:-2])
+        local, total = block_updates(plan, rates, v, b, x_last, last, groups)
+    else:
+        v, b, x_last = project(plan, x, weights)
+        local, total = block_updates(plan, rates, v, b, x_last, [], groups)
 
     def exchange(blocks):
         return lax.all_to_all(
@@ -724,22 +755,26 @@
 
     share = local.shape[1] // plan.chips
     arrived = exchange(total)
-    attended = [attend(plan, 0, block_lists, x, v, weights, local)]
+    attended = [attend(plan, 0, block_lists, x, weights, local)]
     arrived, attended = lax.optimization_barrier((arrived, attended))
     states = scan_states(plan, arrived, share)
     x, states = lax.optimization_barrier((x, states))
     if plan.merge == 2:
-        attended.append(attend(plan, 1, block_lists, x, v, weights, local))
+        attended.append(attend(plan, 1, block_lists, x, weights, local))
     state = exchange(states).reshape(-1, LANES)
 
     bases, readers = ([a[i] for a in attended] for i in range(2))
     mixed = mix(plan, rates, bases, readers, state, places, groups)
-    features = [
-        mixed[0] if s == 0 and k == 0 else plan.to_peer(mixed[s * plan.peers + k], k, s == 1)
+    moved = {
+        (s, k): plan.to_peer(mixed[s * plan.peers + k], k, s == 1)
         for s in range(plan.merge)
-        for k in range(plan.peers)
-    ]
-    return project_out(plan, out_weight, features)[None]
+        for k in range(1, plan.peers)
+    }
+    near = {(0, 0): mixed[0]}
+    if plan.merge == 2:
+        near[1, 0] = plan.swap(mixed[plan.peers])
+    result = project_out(plan, out_weight, near, [], f32)
+    return project_out(plan, out_weight, moved, [result], bf16)[None]
 
 
 def solution(mesh):

time: 118 us -> 113 us (0.958)
  Pallas kernels: 44.8 us -> 42.4 us
  local copies, waits for them, and re-layouts: 8.18 us -> 6.06 us
    pallas_call x2 -> x4, Pallas kernels: 12.5 us -> 9.84 us  [the longest x1 4.33 us: block_updates(): pl.pallas_call(functools.partial(update_kernel, plan, groups), in_specs=[...]
    ppermute x1, waiting for transfers between devices: 2.24 us -> 4.71 us  [to_peer(): return lax.ppermute(block, ('tm', 'head'), pairs)]
    unnamed x37 -> x41, local copies, waits for them, and re-layouts: 8.16 us -> 6.04 us
  transfers between devices with their start and end apart: 18 -> 18, of which waited for: 13 -> 13; matrix products, arithmetic and copies ran while one was open for 1% -> 1% of each run, Pallas kernels for 22% -> 26%
where the time goes in v10:
time: 113 us
  waiting for transfers between devices  42.7 us (38%)
  Pallas kernels  42.4 us (38%)
  starting transfers between devices  20.4 us (18%)
  local copies, waits for them, and re-layouts  6.06 us (5%)
    pallas_call x2, Pallas kernels, attend(): pl.pallas_call(functools.partial(attend_kernel, plan, slot), in_specs=[sm...  18.3 us
    ppermute x4, waiting for transfers between devices, round(): return lax.ppermute(block, 'tm', pairs)  15 us
    all_to_all x2, waiting for transfers between devices, exchange(): lax.all_to_all(blocks, 'tm', split_axis=0, concat_axis=0, tiled=True, axi...  8.26 us
    all_to_all x2, starting transfers between devices, exchange(): lax.all_to_all(blocks, 'tm', split_axis=0, concat_axis=0, tiled=True, axi...  7.36 us
    pallas_call x2, Pallas kernels, place_tokens(): pl.pallas_call(functools.partial(place_kernel, plan.merge, parts, start),...  7.04 us
    unnamed x41, local copies, waits for them, and re-layouts  6.04 us
    ppermute x2, waiting for transfers between devices, to_peer(): return lax.ppermute(block, 'head', pairs)  5.86 us
    pallas_call x1, Pallas kernels, mix(): pl.pallas_call(functools.partial(mix_kernel, plan, groups), in_specs=[sme...  5.67 us
  transfers between devices with their start and end apart: 18, of which 13 were waited for; matrix products, arithmetic and copies ran while one was open for 1% of the time, Pallas kernels for 26%

profile of v10, /device:TPU:0, one launch (start us, length us, event | category | flops | bytes accessed | tf_op | source)
XLA Modules:
  0.0 112.6 jit_solution(746628209246262708)
XLA Ops:
  0.5 2.5 %collective-permute-start.1 = (bf16[512,1024]{1,0:T(8,128)(2,1)}, bf16[512,1024]{1,0:T(8,128)(2,1)S(1)}, u32[]{:S(2)}, u32[]{:S(2)}) collective-permute-start(bf16[512,1024]{1,0:T(8,128)(2,1)} %bitcast.6), channel_id=1, source_target_pairs={{0,1},{1,0},{2,3},{3,2},{4,5},{5,4},{6,7},{7,6},{8,9},{9,8},{10,11... | collective-permute-start | bytes 3145736 | tf_op jit(solution)/shard_map/ppermute | solution.py:95
  3.2 1.6 %collective-permute-done.2.refs_1_ = bf16[64,2560]{1,0:T(8,128)(2,1)S(1)} collective-permute-done((bf16[64,2560]{1,0:T(8,128)(2,1)}, bf16[64,2560]{1,0:T(8,128)(2,1)S(1)}, u32[]{:S(2)}, u32[]{:S(2)}) %collective-permute-start.2) | collective-permute-done | bytes 327712 | tf_op jit(solution)/shard_map/ppermute | solution.py:61
  4.8 1.0 copy-done.11
  6.0 1.6 %collective-permute-start.3 = (bf16[128,1280]{1,0:T(8,128)(2,1)S(1)}, bf16[128,1280]{1,0:T(8,128)(2,1)S(1)}, u32[]{:S(2)}, u32[]{:S(2)}) collective-permute-start(bf16[128,1280]{1,0:T(8,128)(2,1)S(1)} %reorder.1.refs_0_.refs_3_), channel_id=1, source_target_pairs={{0,8},{2,10},{4,12},{6,14},{8,16},{10,18},{12,20},{14,22},{16,24},... | collective-permute-start | bytes 983048 | tf_op jit(solution)/shard_map/ppermute | solution.py:66
  7.6 1.5 %collective-permute-start.4 = (bf16[128,1280]{1,0:T(8,128)(2,1)S(1)}, bf16[128,1280]{1,0:T(8,128)(2,1)S(1)}, u32[]{:S(2)}, u32[]{:S(2)}) collective-permute-start(bf16[128,1280]{1,0:T(8,128)(2,1)S(1)} %reorder.1.refs_0_.refs_3_), channel_id=1, source_target_pairs={{0,4},{2,6},{4,0},{6,2},{8,12},{10,14},{12,8},{14,10},{16,20},{18,... | collective-permute-start | bytes 983048 | tf_op jit(solution)/shard_map/ppermute | solution.py:71
  11.7 1.2 %copy-done.3 = bf16[1,512,1024]{2,1,0:T(8,128)(2,1)S(1)} copy-done((bf16[1,512,1024]{2,1,0:T(8,128)(2,1)S(1)}, bf16[1,512,1024]{2,1,0:T(8,128)(2,1)}, u32[]{:S(2)}) %copy-start.3) | copy-done | bytes 1048600
  12.9 3.5 %place_tokens.2.refs_2_ = bf16[2048,1024]{1,0:T(8,128)(2,1)S(1)} custom-call(f32[1,1024]{1,0:T(1,128)S(1)} %get-tuple-element.38.rank_ref, bf16[512,1024]{1,0:T(8,128)(2,1)S(1)} %bitcast.7, bf16[512,1024]{1,0:T(8,128)(2,1)S(1)} %collective-permute-done.5.refs_1_), custom_call_target="tpu_custom_call" | custom-call | bytes 4096 | tf_op jit(solution)/shard_map/place_tokens/pallas_call | solution.py:265
  16.4 1.3 %collective-permute-done.3.refs_1_.refs_4_ = bf16[128,1280]{1,0:T(8,128)(2,1)S(1)} collective-permute-done((bf16[128,1280]{1,0:T(8,128)(2,1)S(1)}, bf16[128,1280]{1,0:T(8,128)(2,1)S(1)}, u32[]{:S(2)}, u32[]{:S(2)}) %collective-permute-start.3) | collective-permute-done | bytes 327712 | tf_op jit(solution)/shard_map/ppermute | solution.py:66
  17.7 1.0 collective-permute-start.6
  18.7 1.5 %collective-permute-start.7 = (bf16[128,1280]{1,0:T(8,128)(2,1)S(1)}, bf16[128,1280]{1,0:T(8,128)(2,1)S(1)}, u32[]{:S(2)}, u32[]{:S(2)}) collective-permute-start(bf16[128,1280]{1,0:T(8,128)(2,1)S(1)} %collective-permute-done.3.refs_1_.refs_4_), channel_id=1, source_target_pairs={{0,4},{2,6},{4,0},{6,2},{8,12},{10,14},{12,8},{14,10},{16,20},{18,... | collective-permute-start | bytes 983048 | tf_op jit(solution)/shard_map/ppermute | solution.py:71
  20.2 8.4 %collective-permute-done.6.refs_2_.refs_5_ = bf16[128,1280]{1,0:T(8,128)(2,1)S(1)} collective-permute-done((bf16[128,1280]{1,0:T(8,128)(2,1)S(1)}, bf16[128,1280]{1,0:T(8,128)(2,1)S(1)}, u32[]{:S(2)}, u32[]{:S(2)}) %collective-permute-start.6) | collective-permute-done | bytes 327712 | tf_op jit(solution)/shard_map/ppermute | solution.py:66
  28.8 1.6 %collective-permute-start.10 = (bf16[128,1280]{1,0:T(8,128)(2,1)S(1)}, bf16[128,1280]{1,0:T(8,128)(2,1)S(1)}, u32[]{:S(2)}, u32[]{:S(2)}) collective-permute-start(bf16[128,1280]{1,0:T(8,128)(2,1)S(1)} %collective-permute-done.6.refs_2_.refs_5_), channel_id=1, source_target_pairs={{0,4},{2,6},{4,0},{6,2},{8,12},{10,14},{12,8},{14,10},{16,20},{18,... | collective-permute-start | bytes 983048 | tf_op jit(solution)/shard_map/ppermute | solution.py:71
  30.3 1.1 collective-permute-done.8.refs_1_
  31.4 3.6 %place_tokens.3.x_ref.refs_1_ = bf16[2048,1024]{1,0:T(8,128)(2,1)S(1)} custom-call(f32[1,1024]{1,0:T(1,128)S(1)} %get-tuple-element.38.rank_ref, bf16[512,1024]{1,0:T(8,128)(2,1)S(1)} %collective-permute-done.1.refs_0_, bf16[512,1024]{1,0:T(8,128)(2,1)S(1)} %collective-permute-done.8.refs_1_, bf16[2048,1024]{1,0:T(8,128)(2,1)S(1)} %place_tokens.2.refs_2_), custom_call_target="tpu_custom_call" | custom-call | bytes 4096 | tf_op jit(solution)/shard_map/place_tokens/pallas_call | solution.py:265
  35.0 3.9 %collective-permute-done.10.refs_6_.refs_9_ = bf16[128,1280]{1,0:T(8,128)(2,1)S(1)} collective-permute-done((bf16[128,1280]{1,0:T(8,128)(2,1)S(1)}, bf16[128,1280]{1,0:T(8,128)(2,1)S(1)}, u32[]{:S(2)}, u32[]{:S(2)}) %collective-permute-start.10) | collective-permute-done | bytes 327712 | tf_op jit(solution)/shard_map/ppermute | solution.py:71
  38.9 3.0 %collective-permute-done.9.refs_3_.refs_6_ = bf16[128,1280]{1,0:T(8,128)(2,1)S(1)} collective-permute-done((bf16[128,1280]{1,0:T(8,128)(2,1)S(1)}, bf16[128,1280]{1,0:T(8,128)(2,1)S(1)}, u32[]{:S(2)}, u32[]{:S(2)}) %collective-permute-start.9) | collective-permute-done | bytes 327712 | tf_op jit(solution)/shard_map/ppermute | solution.py:66
  42.7 3.1 %project.1 = (f32[2048,256]{1,0:T(8,128)S(1)}, f32[256,2048]{1,0:T(8,128)S(1)}, bf16[2048,128]{1,0:T(8,128)(2,1)S(1)}) custom-call(bf16[2048,1024]{1,0:T(8,128)(2,1)S(1)} %place_tokens.3.x_ref.refs_1_, bf16[128,1280]{1,0:T(8,128)(2,1)S(1)} %reorder.1.refs_0_.refs_3_, bf16[128,1280]{1,0:T(8,128)(2,1)S(1)} %collective-permute-done.3.refs_1_.refs_4_, ...), custom_call_target="tpu_custom_call" | custom-call | bytes 4096 | tf_op jit(solution)/shard_map/project/pallas_call | solution.py:312
  45.8 1.6 %collective-permute-done.11.refs_5_.refs_10_ = bf16[64,1280]{1,0:T(8,128)(2,1)S(1)} collective-permute-done((bf16[64,1280]{1,0:T(8,128)(2,1)S(1)}, bf16[64,1280]{1,0:T(8,128)(2,1)S(1)}, u32[]{:S(2)}, u32[]{:S(2)}) %collective-permute-start.11) | collective-permute-done | bytes 163872 | tf_op jit(solution)/shard_map/ppermute | solution.py:71
  47.4 2.3 %collective-permute-done.12.refs_6_.refs_11_ = bf16[64,1280]{1,0:T(8,128)(2,1)S(1)} collective-permute-done((bf16[64,1280]{1,0:T(8,128)(2,1)S(1)}, bf16[64,1280]{1,0:T(8,128)(2,1)S(1)}, u32[]{:S(2)}, u32[]{:S(2)}) %collective-permute-start.12) | collective-permute-done | bytes 163872 | tf_op jit(solution)/shard_map/ppermute | solution.py:66
  49.7 4.3 %block_updates.1 = (bf16[2,2048,128]{2,1,0:T(8,128)(2,1)S(1)}, bf16[8,272,128]{2,1,0:T(8,128)(2,1)}) custom-call(f32[8,16]{1,0:T(8,128)S(1)} %bitcast.11, f32[8,16]{1,0:T(8,128)S(1)} %collective-permute-done.refs_1_, f32[2048,256]{1,0:T(8,128)S(1)} %get-tuple-element.46.refs_2_, f32[256,2048]{1,0:T(8,128)S(1)} %get-tuple-element.47.refs_3_, ...), custom_call_target="tpu_custom_call" | custom-call | flops 1073741824 | bytes 3145728 | tf_op jit(solution)/shard_map/block_updates/pallas_call | solution.py:406
  54.6 3.7 %all-to-all-start = ((bf16[8,272,128]{2,1,0:T(8,128)(2,1)}), bf16[8,272,128]{2,1,0:T(8,128)(2,1)S(1)}, u32[]{:S(2)}, u32[]{:S(2)}) async-start(bf16[8,272,128]{2,1,0:T(8,128)(2,1)} %get-tuple-element.49), calls=%async_computation | async-start | bytes 1114112 | tf_op jit(solution)/shard_map/all_to_all | solution.py:751
  59.1 9.1 %attend.2 = (f32[1024,256]{1,0:T(8,128)}, bf16[1024,256]{1,0:T(8,128)(2,1)}) custom-call(s32[16,4]{1,0:T(8,128)} %copy.7.refs_0_, bf16[2048,1024]{1,0:T(8,128)(2,1)} %copy-done, bf16[2,2048,128]{2,1,0:T(8,128)(2,1)} %copy-done.17, bf16[128,1280]{1,0:T(8,128)(2,1)} %copy-done.2, bf16[128,1280]{1,0:T(8,128)(2,1)} %copy-done.7, bf16[128,1280]{1,0:T(8,128)(2,1)} %copy-done.9, ...), custom_call_target="tpu_custom_call" | custom-call | flops 4831838208 | bytes 11534336 | tf_op jit(solution)/shard_map/attend/pallas_call | solution.py:545
  68.2 3.5 %all-to-all-done.u_ref = bf16[8,272,128]{2,1,0:T(8,128)(2,1)S(1)} async-done(((bf16[8,272,128]{2,1,0:T(8,128)(2,1)}), bf16[8,272,128]{2,1,0:T(8,128)(2,1)S(1)}, u32[]{:S(2)}, u32[]{:S(2)}) %all-to-all-start) | async-done | bytes 557088 | tf_op jit(solution)/shard_map/all_to_all | solution.py:751
  71.7 1.0 scan_states.1
  72.6 3.6 %all-to-all-start.1 = ((bf16[8,256,128]{2,1,0:T(8,128)(2,1)}), bf16[8,256,128]{2,1,0:T(8,128)(2,1)S(1)}, u32[]{:S(2)}, u32[]{:S(2)}) async-start(bf16[8,256,128]{2,1,0:T(8,128)(2,1)} %scan_states.1), calls=%async_computation.1 | async-start | bytes 1048576 | tf_op jit(solution)/shard_map/all_to_all | solution.py:751
  76.3 9.1 %attend.3 = (f32[1024,256]{1,0:T(8,128)}, bf16[1024,256]{1,0:T(8,128)(2,1)}) custom-call(s32[16,4]{1,0:T(8,128)} %copy.7.refs_0_, bf16[2048,1024]{1,0:T(8,128)(2,1)} %copy-done, bf16[2,2048,128]{2,1,0:T(8,128)(2,1)} %copy-done.17, bf16[128,1280]{1,0:T(8,128)(2,1)} %copy-done.2, bf16[128,1280]{1,0:T(8,128)(2,1)} %copy-done.7, bf16[128,1280]{1,0:T(8,128)(2,1)} %copy-done.9, ...), custom_call_target="tpu_custom_call" | custom-call | flops 4831838208 | bytes 11534336 | tf_op jit(solution)/shard_map/attend/pallas_call | solution.py:545
  85.4 4.8 %all-to-all-done.1 = bf16[8,256,128]{2,1,0:T(8,128)(2,1)S(1)} async-done(((bf16[8,256,128]{2,1,0:T(8,128)(2,1)}), bf16[8,256,128]{2,1,0:T(8,128)(2,1)S(1)}, u32[]{:S(2)}, u32[]{:S(2)}) %all-to-all-start.1) | async-done | bytes 524320 | tf_op jit(solution)/shard_map/all_to_all | solution.py:751
  91.0 5.7 %mix.1 = (bf16[512,256]{1,0:T(8,128)(2,1)}, bf16[512,256]{1,0:T(8,128)(2,1)}, bf16[512,256]{1,0:T(8,128)(2,1)}, bf16[512,256]{1,0:T(8,128)(2,1)}) custom-call(f32[8,16]{1,0:T(8,128)} %bitcast.10, f32[8,16]{1,0:T(8,128)} %copy-done.16, f32[1024,256]{1,0:T(8,128)} %get-tuple-element.53.refs_2_, f32[1024,256]{1,0:T(8,128)} %get-tuple-element.56.refs_3_, ...), custom_call_target="tpu_custom_call" | custom-call | flops 1073741824 | bytes 6291456 | tf_op jit(solution)/shard_map/mix/pallas_call | solution.py:658
  96.8 1.4 %collective-permute-start.13 = (bf16[512,256]{1,0:T(8,128)(2,1)}, bf16[512,256]{1,0:T(8,128)(2,1)S(1)}, u32[]{:S(2)}, u32[]{:S(2)}) collective-permute-start(bf16[512,256]{1,0:T(8,128)(2,1)} %get-tuple-element.61), channel_id=1, source_target_pairs={{0,1},{1,0},{2,3},{3,2},{4,5},{5,4},{6,7},{7,6},{8,9},{9,8},{10,11... | collective-permute-start | bytes 786440 | tf_op jit(solution)/shard_map/ppermute | solution.py:95
  100.3 5.9 %collective-permute-done.13.refs_0_ = bf16[512,256]{1,0:T(8,128)(2,1)S(1)} collective-permute-done((bf16[512,256]{1,0:T(8,128)(2,1)}, bf16[512,256]{1,0:T(8,128)(2,1)S(1)}, u32[]{:S(2)}, u32[]{:S(2)}) %collective-permute-start.13) | collective-permute-done | bytes 262176 | tf_op jit(solution)/shard_map/ppermute | solution.py:95
  106.2 4.7 %collective-permute-done.14.refs_1_ = bf16[512,256]{1,0:T(8,128)(2,1)S(1)} collective-permute-done((bf16[512,256]{1,0:T(8,128)(2,1)}, bf16[512,256]{1,0:T(8,128)(2,1)S(1)}, u32[]{:S(2)}, u32[]{:S(2)}) %collective-permute-start.14) | collective-permute-done | bytes 262176 | tf_op jit(solution)/shard_map/ppermute | solution.py:103
  110.9 1.7 %project_out.3 = bf16[512,1024]{1,0:T(8,128)(2,1)} custom-call(bf16[1024,1024]{1,0:T(8,128)(2,1)S(1)} %copy-done.1, bf16[512,256]{1,0:T(8,128)(2,1)S(1)} %collective-permute-done.13.refs_0_, bf16[512,256]{1,0:T(8,128)(2,1)S(1)} %collective-permute-done.14.refs_1_, f32[512,1024]{1,0:T(8,128)S(1)} %project_out.2.refs_2_), custom_call_target="tpu_custom_call" | custom-call | bytes 2048 | tf_op jit(solution)/shard_map/project_out/pallas_call | solution.py:692
  (60 shorter events, 8.5 us)
Async XLA Ops:
  0.0 11.7 %collective-permute-start.5 = (bf16[512,1024]{1,0:T(8,128)(2,1)}, bf16[512,1024]{1,0:T(8,128)(2,1)S(1)}, u32[]{:S(2)}, u32[]{:S(2)}) collective-permute-start(bf16[512,1024]{1,0:T(8,128)(2,1)} %bitcast.5), channel_id=1, source_target_pairs={{0,2},{2,0},{4,6},{6,4},{8,10},{10,8},{12,14},{14,12},{16,18},{18,... | collective-permute-start | bytes 3145736 | tf_op jit(solution)/shard_map/ppermute | solution.py:61
  0.5 28.2 %collective-permute-start.1 = (bf16[512,1024]{1,0:T(8,128)(2,1)}, bf16[512,1024]{1,0:T(8,128)(2,1)S(1)}, u32[]{:S(2)}, u32[]{:S(2)}) collective-permute-start(bf16[512,1024]{1,0:T(8,128)(2,1)} %bitcast.6), channel_id=1, source_target_pairs={{0,1},{1,0},{2,3},{3,2},{4,5},{5,4},{6,7},{7,6},{8,9},{9,8},{10,11... | collective-permute-start | bytes 3145736 | tf_op jit(solution)/shard_map/ppermute | solution.py:95
  3.0 1.8 %collective-permute-start.2 = (bf16[64,2560]{1,0:T(8,128)(2,1)}, bf16[64,2560]{1,0:T(8,128)(2,1)S(1)}, u32[]{:S(2)}, u32[]{:S(2)}) collective-permute-start(bf16[64,2560]{1,0:T(8,128)(2,1)} %refs_0_.3), channel_id=1, source_target_pairs={{0,2},{2,0},{4,6},{6,4},{8,10},{10,8},{12,14},{14,12},{16,18},{18,... | collective-permute-start | bytes 983048 | tf_op jit(solution)/shard_map/ppermute | solution.py:61
  5.9 36.7 %copy-start.2 = (bf16[128,1280]{1,0:T(8,128)(2,1)}, bf16[128,1280]{1,0:T(8,128)(2,1)S(1)}, u32[]{:S(2)}) copy-start(bf16[128,1280]{1,0:T(8,128)(2,1)S(1)} %reorder.1.refs_0_.refs_3_) | copy-start | bytes 983044
  6.0 11.8 %collective-permute-start.3 = (bf16[128,1280]{1,0:T(8,128)(2,1)S(1)}, bf16[128,1280]{1,0:T(8,128)(2,1)S(1)}, u32[]{:S(2)}, u32[]{:S(2)}) collective-permute-start(bf16[128,1280]{1,0:T(8,128)(2,1)S(1)} %reorder.1.refs_0_.refs_3_), channel_id=1, source_target_pairs={{0,8},{2,10},{4,12},{6,14},{8,16},{10,18},{12,20},{14,22},{16,24},... | collective-permute-start | bytes 983048 | tf_op jit(solution)/shard_map/ppermute | solution.py:66
  7.6 10.1 %collective-permute-start.4 = (bf16[128,1280]{1,0:T(8,128)(2,1)S(1)}, bf16[128,1280]{1,0:T(8,128)(2,1)S(1)}, u32[]{:S(2)}, u32[]{:S(2)}) collective-permute-start(bf16[128,1280]{1,0:T(8,128)(2,1)S(1)} %reorder.1.refs_0_.refs_3_), channel_id=1, source_target_pairs={{0,4},{2,6},{4,0},{6,2},{8,12},{10,14},{12,8},{14,10},{16,20},{18,... | collective-permute-start | bytes 983048 | tf_op jit(solution)/shard_map/ppermute | solution.py:71
  9.1 1.4 %collective-permute-start = (f32[8,16]{1,0:T(8,128)}, f32[8,16]{1,0:T(8,128)S(1)}, u32[]{:S(2)}, u32[]{:S(2)}) collective-permute-start(f32[8,16]{1,0:T(8,128)} %bitcast.9), channel_id=1, source_target_pairs={{0,2},{2,0},{4,6},{6,4},{8,10},{10,8},{12,14},{14,12},{16,18},{18,... | collective-permute-start | bytes 1544 | tf_op jit(solution)/shard_map/ppermute | solution.py:61
  17.7 24.9 %copy-start.7 = (bf16[128,1280]{1,0:T(8,128)(2,1)}, bf16[128,1280]{1,0:T(8,128)(2,1)S(1)}, u32[]{:S(2)}) copy-start(bf16[128,1280]{1,0:T(8,128)(2,1)S(1)} %collective-permute-done.3.refs_1_.refs_4_) | copy-start | bytes 983044
  17.7 24.9 %copy-start.8 = (bf16[128,1280]{1,0:T(8,128)(2,1)}, bf16[128,1280]{1,0:T(8,128)(2,1)S(1)}, u32[]{:S(2)}) copy-start(bf16[128,1280]{1,0:T(8,128)(2,1)S(1)} %collective-permute-done.4.refs_4_.refs_7_) | copy-start | bytes 983044
  17.7 10.9 %collective-permute-start.6 = (bf16[128,1280]{1,0:T(8,128)(2,1)S(1)}, bf16[128,1280]{1,0:T(8,128)(2,1)S(1)}, u32[]{:S(2)}, u32[]{:S(2)}) collective-permute-start(bf16[128,1280]{1,0:T(8,128)(2,1)S(1)} %collective-permute-done.3.refs_1_.refs_4_), channel_id=1, source_target_pairs={{0,8},{2,10},{4,12},{6,14},{8,16},{10,18},{12,20},{14,22},{16,24},... | collective-permute-start | bytes 983048 | tf_op jit(solution)/shard_map/ppermute | solution.py:66
  18.7 9.9 %collective-permute-start.7 = (bf16[128,1280]{1,0:T(8,128)(2,1)S(1)}, bf16[128,1280]{1,0:T(8,128)(2,1)S(1)}, u32[]{:S(2)}, u32[]{:S(2)}) collective-permute-start(bf16[128,1280]{1,0:T(8,128)(2,1)S(1)} %collective-permute-done.3.refs_1_.refs_4_), channel_id=1, source_target_pairs={{0,4},{2,6},{4,0},{6,2},{8,12},{10,14},{12,8},{14,10},{16,20},{18,... | collective-permute-start | bytes 983048 | tf_op jit(solution)/shard_map/ppermute | solution.py:71
  28.7 14.0 %copy-start.9 = (bf16[128,1280]{1,0:T(8,128)(2,1)}, bf16[128,1280]{1,0:T(8,128)(2,1)S(1)}, u32[]{:S(2)}) copy-start(bf16[128,1280]{1,0:T(8,128)(2,1)S(1)} %collective-permute-done.6.refs_2_.refs_5_) | copy-start | bytes 983044
  28.7 14.0 %copy-start.10 = (bf16[128,1280]{1,0:T(8,128)(2,1)}, bf16[128,1280]{1,0:T(8,128)(2,1)S(1)}, u32[]{:S(2)}) copy-start(bf16[128,1280]{1,0:T(8,128)(2,1)S(1)} %collective-permute-done.7.refs_5_.refs_8_) | copy-start | bytes 983044
  28.7 2.7 %collective-permute-start.8 = (bf16[512,1024]{1,0:T(8,128)(2,1)S(1)}, bf16[512,1024]{1,0:T(8,128)(2,1)S(1)}, u32[]{:S(2)}, u32[]{:S(2)}) collective-permute-start(bf16[512,1024]{1,0:T(8,128)(2,1)S(1)} %collective-permute-done.1.refs_0_), channel_id=1, source_target_pairs={{0,2},{2,0},{4,6},{6,4},{8,10},{10,8},{12,14},{14,12},{16,18},{18,... | collective-permute-start | bytes 3145736 | tf_op jit(solution)/shard_map/ppermute | solution.py:61
  28.8 10.1 %collective-permute-start.10 = (bf16[128,1280]{1,0:T(8,128)(2,1)S(1)}, bf16[128,1280]{1,0:T(8,128)(2,1)S(1)}, u32[]{:S(2)}, u32[]{:S(2)}) collective-permute-start(bf16[128,1280]{1,0:T(8,128)(2,1)S(1)} %collective-permute-done.6.refs_2_.refs_5_), channel_id=1, source_target_pairs={{0,4},{2,6},{4,0},{6,2},{8,12},{10,14},{12,8},{14,10},{16,20},{18,... | collective-permute-start | bytes 983048 | tf_op jit(solution)/shard_map/ppermute | solution.py:71
  30.3 11.6 %collective-permute-start.9 = (bf16[128,1280]{1,0:T(8,128)(2,1)S(1)}, bf16[128,1280]{1,0:T(8,128)(2,1)S(1)}, u32[]{:S(2)}, u32[]{:S(2)}) collective-permute-start(bf16[128,1280]{1,0:T(8,128)(2,1)S(1)} %collective-permute-done.6.refs_2_.refs_5_), channel_id=1, source_target_pairs={{0,8},{2,10},{4,12},{6,14},{8,16},{10,18},{12,20},{14,22},{16,24},... | collective-permute-start | bytes 983048 | tf_op jit(solution)/shard_map/ppermute | solution.py:66
  35.0 10.8 %copy-start = (bf16[2048,1024]{1,0:T(8,128)(2,1)}, bf16[2048,1024]{1,0:T(8,128)(2,1)S(1)}, u32[]{:S(2)}) copy-start(bf16[2048,1024]{1,0:T(8,128)(2,1)S(1)} %place_tokens.3.x_ref.refs_1_) | copy-start | bytes 12582916
  38.9 6.9 %copy-start.4 = (bf16[128,1280]{1,0:T(8,128)(2,1)}, bf16[128,1280]{1,0:T(8,128)(2,1)S(1)}, u32[]{:S(2)}) copy-start(bf16[128,1280]{1,0:T(8,128)(2,1)S(1)} %collective-permute-done.10.refs_6_.refs_9_) | copy-start | bytes 983044
  41.9 3.9 %copy-start.5 = (bf16[128,1280]{1,0:T(8,128)(2,1)}, bf16[128,1280]{1,0:T(8,128)(2,1)S(1)}, u32[]{:S(2)}) copy-start(bf16[128,1280]{1,0:T(8,128)(2,1)S(1)} %collective-permute-done.9.refs_3_.refs_6_) | copy-start | bytes 983044
  41.9 5.5 %collective-permute-start.11 = (bf16[64,1280]{1,0:T(8,128)(2,1)S(1)}, bf16[64,1280]{1,0:T(8,128)(2,1)S(1)}, u32[]{:S(2)}, u32[]{:S(2)}) collective-permute-start(bf16[64,1280]{1,0:T(8,128)(2,1)S(1)} %slice.6), channel_id=1, source_target_pairs={{0,4},{2,6},{4,0},{6,2},{8,12},{10,14},{12,8},{14,10},{16,20},{18,... | collective-permute-start | bytes 491528 | tf_op jit(solution)/shard_map/ppermute | solution.py:71
  42.5 7.2 %copy-start.15 = (f32[1,8,16]{2,1,0:T(8,128)S(1)}, f32[1,8,16]{2,1,0:T(8,128)}, u32[]{:S(2)}) copy-start(f32[1,8,16]{2,1,0:T(8,128)} %param.11) | copy-start | bytes 1540
  42.5 7.2 %collective-permute-start.12 = (bf16[64,1280]{1,0:T(8,128)(2,1)S(1)}, bf16[64,1280]{1,0:T(8,128)(2,1)S(1)}, u32[]{:S(2)}, u32[]{:S(2)}) collective-permute-start(bf16[64,1280]{1,0:T(8,128)(2,1)S(1)} %slice.7), channel_id=1, source_target_pairs={{0,8},{2,10},{4,12},{6,14},{8,16},{10,18},{12,20},{14,22},{16,24},... | collective-permute-start | bytes 491528 | tf_op jit(solution)/shard_map/ppermute | solution.py:66
  47.4 6.6 %copy-start.13 = (bf16[64,1280]{1,0:T(8,128)(2,1)}, bf16[64,1280]{1,0:T(8,128)(2,1)S(1)}, u32[]{:S(2)}) copy-start(bf16[64,1280]{1,0:T(8,128)(2,1)S(1)} %collective-permute-done.11.refs_5_.refs_10_) | copy-start | bytes 491524
  49.7 4.3 %copy-start.14 = (bf16[64,1280]{1,0:T(8,128)(2,1)}, bf16[64,1280]{1,0:T(8,128)(2,1)S(1)}, u32[]{:S(2)}) copy-start(bf16[64,1280]{1,0:T(8,128)(2,1)S(1)} %collective-permute-done.12.refs_6_.refs_11_) | copy-start | bytes 491524
  49.7 8.7 %copy-start.19 = (s32[16,4]{0,1:T(4,128)S(1)}, s32[16,4]{0,1:T(4,128)}, u32[]{:S(2)}) copy-start(s32[16,4]{0,1:T(4,128)} %param.10) | copy-start | bytes 772
  54.6 4.4 %copy-start.17 = (bf16[2,2048,128]{2,1,0:T(8,128)(2,1)}, bf16[2,2048,128]{2,1,0:T(8,128)(2,1)S(1)}, u32[]{:S(2)}) copy-start(bf16[2,2048,128]{2,1,0:T(8,128)(2,1)S(1)} %get-tuple-element.50.refs_2_) | copy-start | bytes 3145732
  54.6 17.0 %all-to-all-start = ((bf16[8,272,128]{2,1,0:T(8,128)(2,1)}), bf16[8,272,128]{2,1,0:T(8,128)(2,1)S(1)}, u32[]{:S(2)}, u32[]{:S(2)}) async-start(bf16[8,272,128]{2,1,0:T(8,128)(2,1)} %get-tuple-element.49), calls=%async_computation | async-start | bytes 1114112 | tf_op jit(solution)/shard_map/all_to_all | solution.py:751
  72.6 17.6 %all-to-all-start.1 = ((bf16[8,256,128]{2,1,0:T(8,128)(2,1)}), bf16[8,256,128]{2,1,0:T(8,128)(2,1)S(1)}, u32[]{:S(2)}, u32[]{:S(2)}) async-start(bf16[8,256,128]{2,1,0:T(8,128)(2,1)} %scan_states.1), calls=%async_computation.1 | async-start | bytes 1048576 | tf_op jit(solution)/shard_map/all_to_all | solution.py:751
  91.0 7.6 %copy-start.1 = (bf16[1024,1024]{1,0:T(8,128)(2,1)S(1)}, bf16[1024,1024]{1,0:T(8,128)(2,1)}, u32[]{:S(2)}) copy-start(bf16[1024,1024]{1,0:T(8,128)(2,1)} %w_ref.3) | copy-start | bytes 6291460
  96.7 1.9 %collective-permute-start.15 = (bf16[512,256]{1,0:T(8,128)(2,1)}, bf16[512,256]{1,0:T(8,128)(2,1)S(1)}, u32[]{:S(2)}, u32[]{:S(2)}) collective-permute-start(bf16[512,256]{1,0:T(8,128)(2,1)} %get-tuple-element.64), channel_id=1, source_target_pairs={{0,2},{2,0},{4,6},{6,4},{8,10},{10,8},{12,14},{14,12},{16,18},{18,... | collective-permute-start | bytes 786440 | tf_op jit(solution)/shard_map/ppermute | solution.py:61
  96.8 9.4 %collective-permute-start.13 = (bf16[512,256]{1,0:T(8,128)(2,1)}, bf16[512,256]{1,0:T(8,128)(2,1)S(1)}, u32[]{:S(2)}, u32[]{:S(2)}) collective-permute-start(bf16[512,256]{1,0:T(8,128)(2,1)} %get-tuple-element.61), channel_id=1, source_target_pairs={{0,1},{1,0},{2,3},{3,2},{4,5},{5,4},{6,7},{7,6},{8,9},{9,8},{10,11... | collective-permute-start | bytes 786440 | tf_op jit(solution)/shard_map/ppermute | solution.py:95
  98.1 12.7 %collective-permute-start.14 = (bf16[512,256]{1,0:T(8,128)(2,1)}, bf16[512,256]{1,0:T(8,128)(2,1)S(1)}, u32[]{:S(2)}, u32[]{:S(2)}) collective-permute-start(bf16[512,256]{1,0:T(8,128)(2,1)} %get-tuple-element.62), channel_id=1, source_target_pairs={{0,3},{1,2},{2,1},{3,0},{4,7},{5,6},{6,5},{7,4},{8,11},{9,10},{10,... | collective-permute-start | bytes 786440 | tf_op jit(solution)/shard_map/ppermute | solution.py:103
  (6 other events, 5.3 us)

commit v11 on v10

--- a/solution.py
+++ b/solution.py
@@ -417,53 +417,55 @@
     )(*decays, v, b, x, *last)
 
 
-def scan_kernel(plan, u_ref, s_ref):
-    share = s_ref.shape[1]
+def scan_kernel(plan, u_ref, *s_refs):
+    splits = len(s_refs)
+    share = s_refs[0].shape[1] * splits
     size = min(share, N)
     items = share // size
     for i in range(items):
-        at = slice(i * size, (i + 1) * size)
+        out_ref, to = s_refs[i % splits], i // splits * size
         state = jnp.zeros((size, LANES), f32)
         for j in range(plan.chips):
-            s_ref[j, at, :] = state.astype(bf16)
+            out_ref[j, to : to + size, :] = state.astype(bf16)
             decay = jnp.zeros((1, LANES), f32)
             for n in range(3):
                 row = share + n * items + i
                 decay = decay + u_ref[j, row : row + 1, :].astype(f32)
-            state = decay * state + u_ref[j, at, :].astype(f32)
-
-
-def scan_states(plan, update, share):
+            state = decay * state + u_ref[j, i * size : (i + 1) * size, :].astype(f32)
+
+
+def scan_states(plan, update, share, splits):
     return pl.pallas_call(
         functools.partial(scan_kernel, plan),
-        out_shape=jax.ShapeDtypeStruct((plan.chips, share, LANES), bf16),
+        out_shape=(jax.ShapeDtypeStruct((plan.chips, share // splits, LANES), bf16),) * splits,
         compiler_params=params(),
         cost_estimate=cost(2 * update.size, 4 * update.size),
         name="scan_states",
     )(update)
 
 
-def attend_kernel(plan, slot, *refs):
+def attend_kernel(plan, groups, *refs):
     lists_ref, x_in, local_in, refs = refs[0], refs[1], refs[2], refs[3:]
-    w_refs, refs = refs[:-12], refs[-12:]
-    a_out, c_out, x, local, w, q_ref, k_ref, wide_v, e_ref, a, c_ref, sems = refs
+    ends = 2 * plan.merge + 10
+    w_refs, refs = refs[:-ends], refs[-ends:]
+    a_outs, refs = refs[: plan.merge], refs[plan.merge :]
+    c_outs, refs = refs[: plan.merge], refs[plan.merge :]
+    x, local, w, q_ref, k_ref, wide_v, e_ref, a, c_ref, sems = refs
     copies = Copies(sems)
-    tokens = x.shape[0]
-    groups, chosen = lists_ref.shape
+    tokens = a.shape[1]
+    chosen = lists_ref.shape[0] // groups
     block = tokens // groups
     step = 256
     per = step // block
     wide = plan.pairs * LANES
 
-    weights = []
+    weights, arriving = [], []
     for ref, rows in plan.places(w_refs):
         weights.append(copies.start(ref.at[:, :wide], w.at[rows, :wide]))
         weights.append(copies.start(ref.at[:, 2 * wide :], w.at[rows, wide:]))
-    arriving = []
-    for at in range(0, tokens, step):
-        from_ = slice(slot * tokens + at, slot * tokens + at + step)
-        arriving.append(copies.start(x_in.at[from_], x.at[at : at + step]))
-    later = copies.start(local_in.at[slot], local)
+    for at in range(0, plan.merge * tokens, step):
+        arriving.append(copies.start(x_in.at[at : at + step], x.at[at : at + step]))
+    later = [copies.start(local_in.at[s], local.at[s]) for s in range(plan.merge)]
 
     same = lax.div(lax.broadcasted_iota(jnp.int32, (2 * LANES, 2 * LANES), 0), HD) == lax.div(
         lax.broadcasted_iota(jnp.int32, (2 * LANES, 2 * LANES), 1), HD
@@ -479,94 +481,96 @@
         return values * lax.rsqrt(total * (1.0 / HD) + epsilon)
 
     half = first_half((step, LANES))
-    finish(weights)
-    for at in range(0, tokens, step):
-        rows = slice(at, at + step)
-        arriving[at // step].wait()
-        every = jnp.dot(x[rows, :], w[...], preferred_element_type=f32).astype(bf16)
-        for p in range(plan.pairs):
-            cols = slice(p * LANES, (p + 1) * LANES)
-            wide_v[p, rows, :LANES] = every[:, cols]
-            first = wide + 3 * p * LANES
-            c_ref[rows, cols] = every[:, first + 2 * LANES : first + 3 * LANES]
-            both = head_norm(every[:, first : first + 2 * LANES].astype(f32))
-            k_ref[p, rows, :] = both[:, LANES:].astype(bf16)
-            q = both[:, :LANES]
-            one = jnp.where(half, q, 0.0).astype(bf16)
-            two = jnp.where(half, 0.0, q).astype(bf16)
-            for i in range(per):
-                part = slice(i * block, (i + 1) * block)
-                q_ref[p, at // block + i] = jnp.concatenate([one[part], two[part]], axis=0)
-    leaving = [copies.start(c_ref, c_out)]
-    later.wait()
+    scale = math.log2(math.e) / math.sqrt(HD)
+    starts = [
+        [pl.multiple_of(lists_ref[g * chosen + j] * block, block) for j in range(chosen)]
+        for g in range(groups)
+    ]
     for p in range(plan.pairs):
         wide_v[p, :, LANES:] = jnp.ones((tokens, LANES), bf16)
-
-    scale = math.log2(math.e) / math.sqrt(HD)
-    starts = [
-        [pl.multiple_of(lists_ref[g, j] * block, block) for j in range(chosen)]
-        for g in range(groups)
-    ]
-    for g in range(groups):
-        for p in range(plan.pairs):
-            keys = jnp.concatenate([k_ref[p, pl.ds(s, block), :] for s in starts[g]], axis=0)
-            score = lax.dot_general(
-                q_ref[p, g], keys, (((1,), (1,)), ((), ())), preferred_element_type=f32
-            )
-            e_ref[p, g] = jnp.exp2(score * scale).astype(bf16)
-    for g in range(groups):
-        rows = slice(g * block, (g + 1) * block)
-        for p in range(plan.pairs):
-            cols = slice(p * LANES, (p + 1) * LANES)
-            values = jnp.concatenate([wide_v[p, pl.ds(s, block), :] for s in starts[g]], axis=0)
-            both = jnp.dot(e_ref[p, g], values, preferred_element_type=f32)
-            both = both[:, :LANES] / both[:, LANES:]
-            a[rows, cols] = halves((block, LANES), both[:block], both[block:])
-    for g in range(groups):
-        rows = slice(g * block, (g + 1) * block)
-        for p in range(plan.pairs):
-            cols = slice(p * LANES, (p + 1) * LANES)
-            items = slice((g * plan.pairs + p) * N, (g * plan.pairs + p + 1) * N)
-            a[rows, cols] = a[rows, cols] + read_out(
-                c_ref[rows, cols], local[items, :].astype(f32), block
-            )
-        if (g + 1) % per == 0:
-            done = slice((g + 1 - per) * block, (g + 1) * block)
-            leaving.append(copies.start(a.at[done], a_out.at[done]))
+    finish(weights)
+    leaving = []
+    for slot in range(plan.merge):
+        for at in range(0, tokens, step):
+            rows = slice(at, at + step)
+            there = slot * tokens + at
+            arriving[there // step].wait()
+            every = jnp.dot(
+                x[there : there + step, :], w[...], preferred_element_type=f32
+            ).astype(bf16)
+            for p in range(plan.pairs):
+                cols = slice(p * LANES, (p + 1) * LANES)
+                wide_v[p, rows, :LANES] = every[:, cols]
+                first = wide + 3 * p * LANES
+                c_ref[slot, rows, cols] = every[:, first + 2 * LANES : first + 3 * LANES]
+                both = head_norm(every[:, first : first + 2 * LANES].astype(f32))
+                k_ref[p, rows, :] = both[:, LANES:].astype(bf16)
+                q = both[:, :LANES]
+                one = jnp.where(half, q, 0.0).astype(bf16)
+                two = jnp.where(half, 0.0, q).astype(bf16)
+                for i in range(per):
+                    part = slice(i * block, (i + 1) * block)
+                    q_ref[p, at // block + i] = jnp.concatenate([one[part], two[part]], axis=0)
+        leaving.append(copies.start(c_ref.at[slot], c_outs[slot]))
+        for g in range(groups):
+            for p in range(plan.pairs):
+                keys = jnp.concatenate([k_ref[p, pl.ds(s, block), :] for s in starts[g]], axis=0)
+                score = lax.dot_general(
+                    q_ref[p, g], keys, (((1,), (1,)), ((), ())), preferred_element_type=f32
+                )
+                e_ref[p, g] = jnp.exp2(score * scale).astype(bf16)
+        for g in range(groups):
+            rows = slice(g * block, (g + 1) * block)
+            for p in range(plan.pairs):
+                cols = slice(p * LANES, (p + 1) * LANES)
+                values = jnp.concatenate(
+                    [wide_v[p, pl.ds(s, block), :] for s in starts[g]], axis=0
+                )
+                both = jnp.dot(e_ref[p, g], values, preferred_element_type=f32)
+                both = both[:, :LANES] / both[:, LANES:]
+                a[slot, rows, cols] = halves((block, LANES), both[:block], both[block:])
+        later[slot].wait()
+        for g in range(groups):
+            rows = slice(g * block, (g + 1) * block)
+            for p in range(plan.pairs):
+                cols = slice(p * LANES, (p + 1) * LANES)
+                items = slice((g * plan.pairs + p) * N, (g * plan.pairs + p + 1) * N)
+                a[slot, rows, cols] = a[slot, rows, cols] + read_out(
+                    c_ref[slot, rows, cols], local[slot, items, :].astype(f32), block
+                )
+        leaving.append(copies.start(a.at[slot], a_outs[slot]))
     finish(leaving)
 
 
-def attend(plan, slot, lists, x, weights, local):
+def attend(plan, groups, lists, x, weights, local):
     every, width = x.shape
-    groups, chosen = lists.shape
+    chosen = lists.shape[0] // groups
     tokens = every // plan.merge
     block = tokens // groups
     cols = plan.pairs * LANES
     return pl.pallas_call(
-        functools.partial(attend_kernel, plan, slot),
+        functools.partial(attend_kernel, plan, groups),
         in_specs=[smem] + [hbm] * (2 + len(weights)),
-        out_specs=(hbm,) * 2,
+        out_specs=(hbm,) * (2 * plan.merge),
         scratch_shapes=[
-            pltpu.VMEM((tokens, width), bf16),
-            pltpu.VMEM(local.shape[1:], bf16),
+            pltpu.VMEM((every, width), bf16),
+            pltpu.VMEM(local.shape, bf16),
             pltpu.VMEM((width, 4 * cols), bf16),
             pltpu.VMEM((plan.pairs, groups, 2 * block, LANES), bf16),
             pltpu.VMEM((plan.pairs, tokens, LANES), bf16),
             pltpu.VMEM((plan.pairs, tokens, 2 * LANES), bf16),
             pltpu.VMEM((plan.pairs, groups, 2 * block, chosen * block), bf16),
-            pltpu.VMEM((tokens, cols), f32),
-            pltpu.VMEM((tokens, cols), bf16),
+            pltpu.VMEM((plan.merge, tokens, cols), f32),
+            pltpu.VMEM((plan.merge, tokens, cols), bf16),
             Copies.scratch(),
         ],
-        out_shape=(
-            jax.ShapeDtypeStruct((tokens, cols), f32),
-            jax.ShapeDtypeStruct((tokens, cols), bf16),
-        ),
+        out_shape=(jax.ShapeDtypeStruct((tokens, cols), f32),) * plan.merge
+        + (jax.ShapeDtypeStruct((tokens, cols), bf16),) * plan.merge,
         compiler_params=params(60),
         cost_estimate=cost(
-            6 * tokens * width * 3 * cols,
-            4 * (tokens * width + 5 * width * cols + local.size),
-            2 * plan.pairs * tokens * chosen * block,
+            6 * every * width * 3 * cols,
+            4 * (every * width + 5 * width * cols + local.size),
+            2 * plan.pairs * every * chosen * block,
         ),
         name="attend",
     )(lists, x, local, *weights)
@@ -580,7 +584,7 @@
     )
 
 
-def mix_kernel(plan, groups, *refs):
+def mix_kernel(plan, groups, pairs, *refs):
     decay_refs, refs = refs[: plan.merge], refs[plan.merge :]
     a_ins, refs = refs[: plan.merge], refs[plan.merge :]
     c_ins, refs = refs[: plan.merge], refs[plan.merge :]
@@ -590,19 +594,20 @@
     tokens = rank.shape[0]
     block = tokens // groups
     width = a.shape[2]
-    here = groups // 4
-    many = here * plan.pairs * N
+    here = groups // 2
+    many = here * len(pairs) * N
     first = plan.core() == 0
+    cols_in = slice(pairs[0] * LANES, (pairs[-1] + 1) * LANES)
 
     arriving = []
-    for i in range(4):
+    for i in range(2):
         rows = slice(i * here * block, (i + 1) * here * block)
         items = slice(i * many, (i + 1) * many)
         arriving.append([copies.start(s_in.at[items], state.at[items])])
         for s in range(plan.merge):
             arriving[-1] += [
-                copies.start(c_ins[s].at[rows], c.at[s, rows, :]),
-                copies.start(a_ins[s].at[rows], a.at[s, rows, :]),
+                copies.start(c_ins[s].at[rows, cols_in], c.at[s, rows, :]),
+                copies.start(a_ins[s].at[rows, cols_in], a.at[s, rows, :]),
             ]
     ranking = copies.start(rank_in, rank)
 
@@ -610,9 +615,9 @@
         if g % here == 0:
             finish(arriving[g // here])
         rows = slice(g * block, (g + 1) * block)
-        for p in range(plan.pairs):
-            cols = slice(p * LANES, (p + 1) * LANES)
-            at = (g * plan.pairs + p) * N
+        for i, p in enumerate(pairs):
+            cols = slice(i * LANES, (i + 1) * LANES)
+            at = (g * len(pairs) + i) * N
             readers = jnp.concatenate([c[s, rows, cols] for s in range(plan.merge)], axis=0)
             read = read_out(readers, state[at : at + N, :].astype(f32), block)
             decays = [plan.decay(decay_refs, s, p, g) for s in range(plan.merge)]
@@ -620,7 +625,7 @@
                 both = decays[0] * decays[1]
                 decays = [jnp.where(first, decays[0], both), jnp.where(first, both, decays[1])]
             for s in range(plan.merge):
-                there = slice(s * width + p * LANES, s * width + (p + 1) * LANES)
+                there = slice(s * width + i * LANES, s * width + (i + 1) * LANES)
                 mixed[rows, there] = (
                     a[s, rows, cols] + decays[s] * read[s * block : (s + 1) * block]
                 ).astype(bf16)
@@ -651,12 +656,12 @@
     return jnp.concatenate(placed, axis=0)
 
 
-def mix(plan, decays, attended, readers, state, rank, groups):
+def mix(plan, pairs, decays, attended, readers, state, rank, groups):
     tokens = rank.shape[0]
-    width = attended[0].shape[1]
+    width = len(pairs) * LANES
     count = plan.merge * plan.peers
     return pl.pallas_call(
-        functools.partial(mix_kernel, plan, groups),
+        functools.partial(mix_kernel, plan, groups, pairs),
         in_specs=[smem] * plan.merge + [hbm] * (2 * plan.merge + 2),
         out_specs=(vmem,) * count,
         out_shape=(jax.ShapeDtypeStruct((tokens // plan.peers, width), bf16),) * count,
@@ -668,7 +673,7 @@
             pltpu.VMEM((tokens, plan.merge * width), bf16),
             Copies.scratch(),
         ],
-        compiler_params=params(56),
+        compiler_params=params(60),
         cost_estimate=cost(4 * tokens * tokens * width, 2 * tokens * tokens + 16 * tokens * width),
         name="mix",
     )(*decays, *attended, *readers, state, rank)
@@ -676,13 +681,13 @@
 
 def out_kernel(plan, sources, w_ref, *refs):
     part_refs, base_refs, out_ref = refs[: len(sources)], refs[len(sources) : -1], refs[-1]
-    depth = part_refs[0].shape[1]
+    depth = plan.pairs * LANES
     core, me = plan.core(), lax.axis_index("head")
     total = base_refs[0][...] if base_refs else 0.0
-    for (s, k), part in zip(sources, part_refs):
+    for (s, k, at), part in zip(sources, part_refs):
         owner = lax.rem(me - k + plan.peers, plan.peers) * plan.merge
         owner = owner + (core if s == 0 else 1 - core)
-        rows = pl.ds(pl.multiple_of(owner * depth, depth), depth)
+        rows = pl.ds(pl.multiple_of(owner * depth + at, LANES), part.shape[1])
         total = total + jnp.dot(part[...], w_ref[rows, :], preferred_element_type=f32)
     out_ref[...] = total.astype(out_ref.dtype)
 
@@ -711,7 +716,7 @@
     rates = [decays[0]] + [plan.swap(decays[0])] * (plan.merge - 1)
     block = reorder(plan, [in_weight] + [plan.swap(in_weight)] * (plan.merge - 1))
     ids = jnp.roll(block_ids, -me * local_tokens)
-    ids, rates = lax.optimization_barrier((ids, rates))
+    ids, rates, lists = lax.optimization_barrier((ids, rates, block_lists.reshape(-1)))
     rank, places = rank_tokens(ids, groups)
     part = place_tokens(plan, rank, 0, owns, [])
 
@@ -754,27 +759,34 @@
         )
 
     share = local.shape[1] // plan.chips
+    splits = plan.pairs if share % (plan.pairs * N) == 0 else 1
     arrived = exchange(total)
-    attended = [attend(plan, 0, block_lists, x, weights, local)]
+    attended = attend(plan, groups, lists, x, weights, local)
     arrived, attended = lax.optimization_barrier((arrived, attended))
-    states = scan_states(plan, arrived, share)
-    x, states = lax.optimization_barrier((x, states))
-    if plan.merge == 2:
-        attended.append(attend(plan, 1, block_lists, x, weights, local))
-    state = exchange(states).reshape(-1, LANES)
-
-    bases, readers = ([a[i] for a in attended] for i in range(2))
-    mixed = mix(plan, rates, bases, readers, state, places, groups)
-    moved = {
-        (s, k): plan.to_peer(mixed[s * plan.peers + k], k, s == 1)
-        for s in range(plan.merge)
-        for k in range(1, plan.peers)
-    }
-    near = {(0, 0): mixed[0]}
-    if plan.merge == 2:
-        near[1, 0] = plan.swap(mixed[plan.peers])
+    bases, readers = attended[: plan.merge], attended[plan.merge :]
+    states = [exchange(s) for s in scan_states(plan, arrived, share, splits)]
+
+    near, moved = {}, []
+    for i, state in enumerate(states):
+        pairs = list(range(plan.pairs)) if splits == 1 else [i]
+        mixed = mix(
+            plan, pairs, rates, bases, readers, state.reshape(-1, LANES), places, groups
+        )
+        at = pairs[0] * LANES
+        moved.append(
+            {
+                (s, k, at): plan.to_peer(mixed[s * plan.peers + k], k, s == 1)
+                for s in range(plan.merge)
+                for k in range(1, plan.peers)
+            }
+        )
+        near[0, 0, at] = mixed[0]
+        if plan.merge == 2:
+            near[1, 0, at] = plan.swap(mixed[plan.peers])
+    for parts in moved[:-1]:
+        near |= parts
     result = project_out(plan, out_weight, near, [], f32)
-    return project_out(plan, out_weight, moved, [result], bf16)[None]
+    return project_out(plan, out_weight, moved[-1], [result], bf16)[None]
 
 
 def solution(mesh):

time: 113 us -> 118 us (1.044)
  blocking collectives: 0 us -> 13.8 us
  waiting for transfers between devices: 42.7 us -> 32.2 us
    all_to_all x0 -> x1, blocking collectives: none -> 13.8 us  [exchange(): lax.all_to_all(blocks, 'tm', split_axis=0, concat_axis=0, tiled=True, axi...]
    ppermute x4, waiting for transfers between devices: 5.53 us -> 12.1 us  [cross(): return lax.ppermute(block, 'tm', pairs)]
    all_to_all x2, waiting for transfers between devices: 8.26 us -> 2.11 us  [exchange(): lax.all_to_all(blocks, 'tm', split_axis=0, concat_axis=0, tiled=True, axi...]
    ppermute x2 -> x3, waiting for transfers between devices: 5.86 us -> 0.01 us  [to_peer(): return lax.ppermute(block, 'head', pairs)]
    ppermute x4, waiting for transfers between devices: 15 us -> 9.46 us  [round(): return lax.ppermute(block, 'tm', pairs)]
    ppermute x5 -> x6, starting transfers between devices: 0.82 us -> 2.17 us  [swap(): return lax.ppermute(block, 'tm', [(t, t ^ 1) for t in range(self.frames)])]
    ppermute x1 -> x2, waiting for transfers between devices: 4.71 us -> 5.8 us  [to_peer(): return lax.ppermute(block, ('tm', 'head'), pairs)]
    ppermute x2 -> x3, starting transfers between devices: 3.88 us -> 4.61 us  [to_peer(): return lax.ppermute(block, 'head', pairs)]
  transfers between devices with their start and end apart: 18 -> 21, of which waited for: 13 -> 11; matrix products, arithmetic and copies ran while one was open for 1% -> 2% of each run, Pallas kernels for 26% -> 31%
where the time goes in v11:
time: 118 us; the launch traced here: 117 us
  Pallas kernels  42.7 us (36%)
  waiting for transfers between devices  32.2 us (27%)
  starting transfers between devices  20.7 us (18%)
  blocking collectives  13.8 us (12%)
  local copies, waits for them, and re-layouts  6.81 us (6%)
    pallas_call x1, Pallas kernels, attend(): pl.pallas_call(functools.partial(attend_kernel, plan, groups), in_specs=[...  14.8 us
    all_to_all x1, blocking collectives, exchange(): lax.all_to_all(blocks, 'tm', split_axis=0, concat_axis=0, tiled=True, axi...  13.8 us
    ppermute x4, waiting for transfers between devices, cross(): return lax.ppermute(block, 'tm', pairs)  12.1 us
    ppermute x4, waiting for transfers between devices, round(): return lax.ppermute(block, 'tm', pairs)  9.46 us
    pallas_call x2, Pallas kernels, mix(): pl.pallas_call(functools.partial(mix_kernel, plan, groups, pairs), in_spe...  8.69 us
    all_to_all x2, starting transfers between devices, exchange(): lax.all_to_all(blocks, 'tm', split_axis=0, concat_axis=0, tiled=True, axi...  7.36 us
    pallas_call x2, Pallas kernels, place_tokens(): pl.pallas_call(functools.partial(place_kernel, plan.merge, parts, start),...  7.02 us
    unnamed x43, local copies, waits for them, and re-layouts  6.16 us
  transfers between devices with their start and end apart: 21, of which 11 were waited for; matrix products, arithmetic and copies ran while one was open for 2% of the time, Pallas kernels for 31%

profile of v11, /device:TPU:0, one launch (start us, length us, event | category | flops | bytes accessed | tf_op | source)
XLA Modules:
  0.0 117.4 jit_solution(14989033467809434277)
XLA Ops:
  0.5 2.5 %collective-permute-start.1 = (bf16[512,1024]{1,0:T(8,128)(2,1)}, bf16[512,1024]{1,0:T(8,128)(2,1)S(1)}, u32[]{:S(2)}, u32[]{:S(2)}) collective-permute-start(bf16[512,1024]{1,0:T(8,128)(2,1)} %bitcast.7), channel_id=1, source_target_pairs={{0,1},{1,0},{2,3},{3,2},{4,5},{5,4},{6,7},{7,6},{8,9},{9,8},{10,11... | collective-permute-start | bytes 3145736 | tf_op jit(solution)/shard_map/ppermute | solution.py:95
  3.2 1.6 %collective-permute-done.2.refs_1_ = bf16[64,2560]{1,0:T(8,128)(2,1)S(1)} collective-permute-done((bf16[64,2560]{1,0:T(8,128)(2,1)}, bf16[64,2560]{1,0:T(8,128)(2,1)S(1)}, u32[]{:S(2)}, u32[]{:S(2)}) %collective-permute-start.2) | collective-permute-done | bytes 327712 | tf_op jit(solution)/shard_map/ppermute | solution.py:61
  4.8 1.0 copy-done.11
  5.9 1.6 %collective-permute-start.4 = (bf16[128,1280]{1,0:T(8,128)(2,1)S(1)}, bf16[128,1280]{1,0:T(8,128)(2,1)S(1)}, u32[]{:S(2)}, u32[]{:S(2)}) collective-permute-start(bf16[128,1280]{1,0:T(8,128)(2,1)S(1)} %reorder.1.refs_0_.refs_3_), channel_id=1, source_target_pairs={{0,4},{2,6},{4,0},{6,2},{8,12},{10,14},{12,8},{14,10},{16,20},{18,... | collective-permute-start | bytes 983048 | tf_op jit(solution)/shard_map/ppermute | solution.py:71
  7.5 1.6 %collective-permute-start.3 = (bf16[128,1280]{1,0:T(8,128)(2,1)S(1)}, bf16[128,1280]{1,0:T(8,128)(2,1)S(1)}, u32[]{:S(2)}, u32[]{:S(2)}) collective-permute-start(bf16[128,1280]{1,0:T(8,128)(2,1)S(1)} %reorder.1.refs_0_.refs_3_), channel_id=1, source_target_pairs={{0,8},{2,10},{4,12},{6,14},{8,16},{10,18},{12,20},{14,22},{16,24},... | collective-permute-start | bytes 983048 | tf_op jit(solution)/shard_map/ppermute | solution.py:66
  12.5 1.2 %copy-done.4 = bf16[1,512,1024]{2,1,0:T(8,128)(2,1)S(1)} copy-done((bf16[1,512,1024]{2,1,0:T(8,128)(2,1)S(1)}, bf16[1,512,1024]{2,1,0:T(8,128)(2,1)}, u32[]{:S(2)}) %copy-start.4) | copy-done | bytes 1048600
  13.7 3.5 %place_tokens.2.refs_2_ = bf16[2048,1024]{1,0:T(8,128)(2,1)S(1)} custom-call(f32[1,1024]{1,0:T(1,128)S(1)} %get-tuple-element.45.rank_ref, bf16[512,1024]{1,0:T(8,128)(2,1)S(1)} %bitcast.8, bf16[512,1024]{1,0:T(8,128)(2,1)S(1)} %collective-permute-done.5.refs_1_), custom_call_target="tpu_custom_call" | custom-call | bytes 4096 | tf_op jit(solution)/shard_map/place_tokens/pallas_call | solution.py:265
  17.2 1.7 %collective-permute-done.3.refs_1_.refs_4_ = bf16[128,1280]{1,0:T(8,128)(2,1)S(1)} collective-permute-done((bf16[128,1280]{1,0:T(8,128)(2,1)S(1)}, bf16[128,1280]{1,0:T(8,128)(2,1)S(1)}, u32[]{:S(2)}, u32[]{:S(2)}) %collective-permute-start.3) | collective-permute-done | bytes 327712 | tf_op jit(solution)/shard_map/ppermute | solution.py:66
  19.5 8.2 %collective-permute-done.7.refs_5_.refs_8_ = bf16[128,1280]{1,0:T(8,128)(2,1)S(1)} collective-permute-done((bf16[128,1280]{1,0:T(8,128)(2,1)S(1)}, bf16[128,1280]{1,0:T(8,128)(2,1)S(1)}, u32[]{:S(2)}, u32[]{:S(2)}) %collective-permute-start.7) | collective-permute-done | bytes 327712 | tf_op jit(solution)/shard_map/ppermute | solution.py:71
  27.7 2.1 %collective-permute-done.6.refs_2_.refs_5_ = bf16[128,1280]{1,0:T(8,128)(2,1)S(1)} collective-permute-done((bf16[128,1280]{1,0:T(8,128)(2,1)S(1)}, bf16[128,1280]{1,0:T(8,128)(2,1)S(1)}, u32[]{:S(2)}, u32[]{:S(2)}) %collective-permute-start.6) | collective-permute-done | bytes 327712 | tf_op jit(solution)/shard_map/ppermute | solution.py:66
  29.8 1.6 %collective-permute-start.10 = (bf16[128,1280]{1,0:T(8,128)(2,1)S(1)}, bf16[128,1280]{1,0:T(8,128)(2,1)S(1)}, u32[]{:S(2)}, u32[]{:S(2)}) collective-permute-start(bf16[128,1280]{1,0:T(8,128)(2,1)S(1)} %collective-permute-done.6.refs_2_.refs_5_), channel_id=1, source_target_pairs={{0,4},{2,6},{4,0},{6,2},{8,12},{10,14},{12,8},{14,10},{16,20},{18,... | collective-permute-start | bytes 983048 | tf_op jit(solution)/shard_map/ppermute | solution.py:71
  31.3 1.1 collective-permute-done.8.refs_1_
  32.4 3.6 %place_tokens.3.x_ref.refs_1_ = bf16[2048,1024]{1,0:T(8,128)(2,1)S(1)} custom-call(f32[1,1024]{1,0:T(1,128)S(1)} %get-tuple-element.45.rank_ref, bf16[512,1024]{1,0:T(8,128)(2,1)S(1)} %collective-permute-done.1.refs_0_, bf16[512,1024]{1,0:T(8,128)(2,1)S(1)} %collective-permute-done.8.refs_1_, bf16[2048,1024]{1,0:T(8,128)(2,1)S(1)} %place_tokens.2.refs_2_), custom_call_target="tpu_custom_call" | custom-call | bytes 4096 | tf_op jit(solution)/shard_map/place_tokens/pallas_call | solution.py:265
  36.0 3.9 %collective-permute-done.10.refs_6_.refs_9_ = bf16[128,1280]{1,0:T(8,128)(2,1)S(1)} collective-permute-done((bf16[128,1280]{1,0:T(8,128)(2,1)S(1)}, bf16[128,1280]{1,0:T(8,128)(2,1)S(1)}, u32[]{:S(2)}, u32[]{:S(2)}) %collective-permute-start.10) | collective-permute-done | bytes 327712 | tf_op jit(solution)/shard_map/ppermute | solution.py:71
  39.9 3.0 %collective-permute-done.9.refs_3_.refs_6_ = bf16[128,1280]{1,0:T(8,128)(2,1)S(1)} collective-permute-done((bf16[128,1280]{1,0:T(8,128)(2,1)S(1)}, bf16[128,1280]{1,0:T(8,128)(2,1)S(1)}, u32[]{:S(2)}, u32[]{:S(2)}) %collective-permute-start.9) | collective-permute-done | bytes 327712 | tf_op jit(solution)/shard_map/ppermute | solution.py:66
  43.6 3.1 %project.1 = (f32[2048,256]{1,0:T(8,128)S(1)}, f32[256,2048]{1,0:T(8,128)S(1)}, bf16[2048,128]{1,0:T(8,128)(2,1)S(1)}) custom-call(bf16[2048,1024]{1,0:T(8,128)(2,1)S(1)} %place_tokens.3.x_ref.refs_1_, bf16[128,1280]{1,0:T(8,128)(2,1)S(1)} %reorder.1.refs_0_.refs_3_, bf16[128,1280]{1,0:T(8,128)(2,1)S(1)} %collective-permute-done.3.refs_1_.refs_4_, ...), custom_call_target="tpu_custom_call" | custom-call | bytes 4096 | tf_op jit(solution)/shard_map/project/pallas_call | solution.py:312
  47.5 2.7 %collective-permute-done.12.refs_6_.refs_11_ = bf16[64,1280]{1,0:T(8,128)(2,1)S(1)} collective-permute-done((bf16[64,1280]{1,0:T(8,128)(2,1)S(1)}, bf16[64,1280]{1,0:T(8,128)(2,1)S(1)}, u32[]{:S(2)}, u32[]{:S(2)}) %collective-permute-start.12) | collective-permute-done | bytes 163872 | tf_op jit(solution)/shard_map/ppermute | solution.py:66
  50.3 4.3 %block_updates.1 = (bf16[2,2048,128]{2,1,0:T(8,128)(2,1)S(1)}, bf16[8,272,128]{2,1,0:T(8,128)(2,1)}) custom-call(f32[8,16]{1,0:T(8,128)S(1)} %bitcast.12, f32[8,16]{1,0:T(8,128)S(1)} %collective-permute-done.refs_1_, f32[2048,256]{1,0:T(8,128)S(1)} %get-tuple-element.53.refs_2_, f32[256,2048]{1,0:T(8,128)S(1)} %get-tuple-element.54.refs_3_, ...), custom_call_target="tpu_custom_call" | custom-call | flops 1073741824 | bytes 3145728 | tf_op jit(solution)/shard_map/block_updates/pallas_call | solution.py:406
  54.6 3.7 %all-to-all-start = ((bf16[8,272,128]{2,1,0:T(8,128)(2,1)}), bf16[8,272,128]{2,1,0:T(8,128)(2,1)S(1)}, u32[]{:S(2)}, u32[]{:S(2)}) async-start(bf16[8,272,128]{2,1,0:T(8,128)(2,1)} %get-tuple-element.56), calls=%async_computation | async-start | bytes 1114112 | tf_op jit(solution)/shard_map/all_to_all | solution.py:756
  58.4 14.8 %attend.1 = (f32[1024,256]{1,0:T(8,128)}, f32[1024,256]{1,0:T(8,128)}, bf16[1024,256]{1,0:T(8,128)(2,1)}, bf16[1024,256]{1,0:T(8,128)(2,1)}) custom-call(s32[64]{0:T(128)} %reshape.12.refs_0_, bf16[2048,1024]{1,0:T(8,128)(2,1)} %copy-done, bf16[2,2048,128]{2,1,0:T(8,128)(2,1)} %copy-done.18, bf16[128,1280]{1,0:T(8,128)(2,1)} %copy-done.3, ...), custom_call_target="tpu_custom_call" | custom-call | flops 9663676416 | bytes 15728640 | tf_op jit(solution)/shard_map/attend/pallas_call | solution.py:551
  73.9 13.8 %all_to_all.15 = bf16[8,128,128]{2,1,0:T(8,128)(2,1)} all-to-all(bf16[8,128,128]{2,1,0:T(8,128)(2,1)S(1)} %get-tuple-element.72), channel_id=1, replica_groups={{0,4,8,12,16,20,24,28},{2,6,10,14,18,22,26,30},{1,5,9,13,17,21,25,29},{..., dimensions={0} | all-to-all | bytes 524288 | tf_op jit(solution)/shard_map/all_to_all | solution.py:756
  87.8 3.6 %all-to-all-start.1 = ((bf16[8,128,128]{2,1,0:T(8,128)(2,1)}), bf16[8,128,128]{2,1,0:T(8,128)(2,1)S(1)}, u32[]{:S(2)}, u32[]{:S(2)}) async-start(bf16[8,128,128]{2,1,0:T(8,128)(2,1)} %get-tuple-element.68), calls=%async_computation.1 | async-start | bytes 524288 | tf_op jit(solution)/shard_map/all_to_all | solution.py:756
  91.4 4.3 %mix.3 = (bf16[512,128]{1,0:T(8,128)(2,1)}, bf16[512,128]{1,0:T(8,128)(2,1)}, bf16[512,128]{1,0:T(8,128)(2,1)}, bf16[512,128]{1,0:T(8,128)(2,1)}) custom-call(f32[8,16]{1,0:T(8,128)} %bitcast.10, f32[8,16]{1,0:T(8,128)} %copy-done.17, f32[1024,256]{1,0:T(8,128)} %get-tuple-element.63.refs_2_, f32[1024,256]{1,0:T(8,128)} %get-tuple-element.64.refs_3_, ...), custom_call_target="tpu_custom_call" | custom-call | flops 536870912 | bytes 4194304 | tf_op jit(solution)/shard_map/mix/pallas_call | solution.py:663
  95.9 1.4 %collective-permute-start.17 = (bf16[512,128]{1,0:T(8,128)(2,1)}, bf16[512,128]{1,0:T(8,128)(2,1)S(1)}, u32[]{:S(2)}, u32[]{:S(2)}) collective-permute-start(bf16[512,128]{1,0:T(8,128)(2,1)} %get-tuple-element.77), channel_id=1, source_target_pairs={{0,1},{1,0},{2,3},{3,2},{4,5},{5,4},{6,7},{7,6},{8,9},{9,8},{10,11... | collective-permute-start | bytes 393224 | tf_op jit(solution)/shard_map/ppermute | solution.py:95
  97.2 2.1 %all-to-all-done.1 = bf16[8,128,128]{2,1,0:T(8,128)(2,1)S(1)} async-done(((bf16[8,128,128]{2,1,0:T(8,128)(2,1)}), bf16[8,128,128]{2,1,0:T(8,128)(2,1)S(1)}, u32[]{:S(2)}, u32[]{:S(2)}) %all-to-all-start.1) | async-done | bytes 262176 | tf_op jit(solution)/shard_map/all_to_all | solution.py:756
  100.0 4.3 %mix.2 = (bf16[512,128]{1,0:T(8,128)(2,1)}, bf16[512,128]{1,0:T(8,128)(2,1)}, bf16[512,128]{1,0:T(8,128)(2,1)}, bf16[512,128]{1,0:T(8,128)(2,1)}) custom-call(f32[8,16]{1,0:T(8,128)} %bitcast.11, f32[8,16]{1,0:T(8,128)} %copy-done.17, f32[1024,256]{1,0:T(8,128)} %get-tuple-element.63.refs_2_, f32[1024,256]{1,0:T(8,128)} %get-tuple-element.64.refs_3_, ...), custom_call_target="tpu_custom_call" | custom-call | flops 536870912 | bytes 4194304 | tf_op jit(solution)/shard_map/mix/pallas_call | solution.py:663
  104.5 1.4 %collective-permute-start.16 = (bf16[512,128]{1,0:T(8,128)(2,1)}, bf16[512,128]{1,0:T(8,128)(2,1)S(1)}, u32[]{:S(2)}, u32[]{:S(2)}) collective-permute-start(bf16[512,128]{1,0:T(8,128)(2,1)} %get-tuple-element.76), channel_id=1, source_target_pairs={{0,2},{2,0},{4,6},{6,4},{8,10},{10,8},{12,14},{14,12},{16,18},{18,... | collective-permute-start | bytes 393224 | tf_op jit(solution)/shard_map/ppermute | solution.py:61
  107.3 3.0 %collective-permute-done.18.refs_5_ = bf16[512,128]{1,0:T(8,128)(2,1)S(1)} collective-permute-done((bf16[512,128]{1,0:T(8,128)(2,1)S(1)}, bf16[512,128]{1,0:T(8,128)(2,1)S(1)}, u32[]{:S(2)}, u32[]{:S(2)}) %collective-permute-start.18) | collective-permute-done | bytes 131104 | tf_op jit(solution)/shard_map/ppermute | solution.py:103
  110.3 0.9 copy-done.15
  111.2 1.8 %project_out.2.refs_2_ = f32[512,1024]{1,0:T(8,128)S(1)} custom-call(bf16[1024,1024]{1,0:T(8,128)(2,1)S(1)} %copy-done.1, bf16[512,128]{1,0:T(8,128)(2,1)S(1)} %copy-done.14, bf16[512,128]{1,0:T(8,128)(2,1)S(1)} %collective-permute-done.15.refs_1_, bf16[512,128]{1,0:T(8,128)(2,1)S(1)} %copy-done.15, bf16[512,128]{1,0:T(8,128)(2,1)S(1)} %collective-permute-done.16.refs_3_, ...), custom_call_target="tpu_custom_call" | custom-call | bytes 2048 | tf_op jit(solution)/shard_map/project_out/pallas_call | solution.py:697
  113.0 2.8 %collective-permute-done.14.refs_1_ = bf16[512,128]{1,0:T(8,128)(2,1)S(1)} collective-permute-done((bf16[512,128]{1,0:T(8,128)(2,1)}, bf16[512,128]{1,0:T(8,128)(2,1)S(1)}, u32[]{:S(2)}, u32[]{:S(2)}) %collective-permute-start.14) | collective-permute-done | bytes 131104 | tf_op jit(solution)/shard_map/ppermute | solution.py:103
  115.7 1.7 %project_out.3 = bf16[512,1024]{1,0:T(8,128)(2,1)} custom-call(bf16[1024,1024]{1,0:T(8,128)(2,1)S(1)} %copy-done.1, bf16[512,128]{1,0:T(8,128)(2,1)S(1)} %collective-permute-done.13.refs_0_, bf16[512,128]{1,0:T(8,128)(2,1)S(1)} %collective-permute-done.14.refs_1_, f32[512,1024]{1,0:T(8,128)S(1)} %project_out.2.refs_2_), custom_call_target="tpu_custom_call" | custom-call | bytes 2048 | tf_op jit(solution)/shard_map/project_out/pallas_call | solution.py:697
  (70 shorter events, 9.3 us)
Async XLA Ops:
  0.0 12.5 %collective-permute-start.5 = (bf16[512,1024]{1,0:T(8,128)(2,1)}, bf16[512,1024]{1,0:T(8,128)(2,1)S(1)}, u32[]{:S(2)}, u32[]{:S(2)}) collective-permute-start(bf16[512,1024]{1,0:T(8,128)(2,1)} %bitcast.6), channel_id=1, source_target_pairs={{0,2},{2,0},{4,6},{6,4},{8,10},{10,8},{12,14},{14,12},{16,18},{18,... | collective-permute-start | bytes 3145736 | tf_op jit(solution)/shard_map/ppermute | solution.py:61
  0.5 29.3 %collective-permute-start.1 = (bf16[512,1024]{1,0:T(8,128)(2,1)}, bf16[512,1024]{1,0:T(8,128)(2,1)S(1)}, u32[]{:S(2)}, u32[]{:S(2)}) collective-permute-start(bf16[512,1024]{1,0:T(8,128)(2,1)} %bitcast.7), channel_id=1, source_target_pairs={{0,1},{1,0},{2,3},{3,2},{4,5},{5,4},{6,7},{7,6},{8,9},{9,8},{10,11... | collective-permute-start | bytes 3145736 | tf_op jit(solution)/shard_map/ppermute | solution.py:95
  3.0 1.8 %collective-permute-start.2 = (bf16[64,2560]{1,0:T(8,128)(2,1)}, bf16[64,2560]{1,0:T(8,128)(2,1)S(1)}, u32[]{:S(2)}, u32[]{:S(2)}) collective-permute-start(bf16[64,2560]{1,0:T(8,128)(2,1)} %refs_0_.1), channel_id=1, source_target_pairs={{0,2},{2,0},{4,6},{6,4},{8,10},{10,8},{12,14},{14,12},{16,18},{18,... | collective-permute-start | bytes 983048 | tf_op jit(solution)/shard_map/ppermute | solution.py:61
  5.9 11.3 %collective-permute-start.4 = (bf16[128,1280]{1,0:T(8,128)(2,1)S(1)}, bf16[128,1280]{1,0:T(8,128)(2,1)S(1)}, u32[]{:S(2)}, u32[]{:S(2)}) collective-permute-start(bf16[128,1280]{1,0:T(8,128)(2,1)S(1)} %reorder.1.refs_0_.refs_3_), channel_id=1, source_target_pairs={{0,4},{2,6},{4,0},{6,2},{8,12},{10,14},{12,8},{14,10},{16,20},{18,... | collective-permute-start | bytes 983048 | tf_op jit(solution)/shard_map/ppermute | solution.py:71
  7.5 11.4 %collective-permute-start.3 = (bf16[128,1280]{1,0:T(8,128)(2,1)S(1)}, bf16[128,1280]{1,0:T(8,128)(2,1)S(1)}, u32[]{:S(2)}, u32[]{:S(2)}) collective-permute-start(bf16[128,1280]{1,0:T(8,128)(2,1)S(1)} %reorder.1.refs_0_.refs_3_), channel_id=1, source_target_pairs={{0,8},{2,10},{4,12},{6,14},{8,16},{10,18},{12,20},{14,22},{16,24},... | collective-permute-start | bytes 983048 | tf_op jit(solution)/shard_map/ppermute | solution.py:66
  9.1 2.2 %collective-permute-start = (f32[8,16]{1,0:T(8,128)}, f32[8,16]{1,0:T(8,128)S(1)}, u32[]{:S(2)}, u32[]{:S(2)}) collective-permute-start(f32[8,16]{1,0:T(8,128)} %bitcast.9), channel_id=1, source_target_pairs={{0,2},{2,0},{4,6},{6,4},{8,10},{10,8},{12,14},{14,12},{16,18},{18,... | collective-permute-start | bytes 1544 | tf_op jit(solution)/shard_map/ppermute | solution.py:61
  11.2 39.0 %copy-start.17 = (f32[8,16]{1,0:T(8,128)}, f32[8,16]{1,0:T(8,128)S(1)}, u32[]{:S(2)}) copy-start(f32[8,16]{1,0:T(8,128)S(1)} %collective-permute-done.refs_1_) | copy-start | bytes 1540
  17.2 26.4 %copy-start.7 = (bf16[128,1280]{1,0:T(8,128)(2,1)}, bf16[128,1280]{1,0:T(8,128)(2,1)S(1)}, u32[]{:S(2)}) copy-start(bf16[128,1280]{1,0:T(8,128)(2,1)S(1)} %collective-permute-done.4.refs_4_.refs_7_) | copy-start | bytes 983044
  18.9 24.7 %copy-start.8 = (bf16[128,1280]{1,0:T(8,128)(2,1)}, bf16[128,1280]{1,0:T(8,128)(2,1)S(1)}, u32[]{:S(2)}) copy-start(bf16[128,1280]{1,0:T(8,128)(2,1)S(1)} %collective-permute-done.3.refs_1_.refs_4_) | copy-start | bytes 983044
  18.9 8.8 %collective-permute-start.7 = (bf16[128,1280]{1,0:T(8,128)(2,1)S(1)}, bf16[128,1280]{1,0:T(8,128)(2,1)S(1)}, u32[]{:S(2)}, u32[]{:S(2)}) collective-permute-start(bf16[128,1280]{1,0:T(8,128)(2,1)S(1)} %collective-permute-done.3.refs_1_.refs_4_), channel_id=1, source_target_pairs={{0,4},{2,6},{4,0},{6,2},{8,12},{10,14},{12,8},{14,10},{16,20},{18,... | collective-permute-start | bytes 983048 | tf_op jit(solution)/shard_map/ppermute | solution.py:71
  19.5 10.3 %collective-permute-start.6 = (bf16[128,1280]{1,0:T(8,128)(2,1)S(1)}, bf16[128,1280]{1,0:T(8,128)(2,1)S(1)}, u32[]{:S(2)}, u32[]{:S(2)}) collective-permute-start(bf16[128,1280]{1,0:T(8,128)(2,1)S(1)} %collective-permute-done.3.refs_1_.refs_4_), channel_id=1, source_target_pairs={{0,8},{2,10},{4,12},{6,14},{8,16},{10,18},{12,20},{14,22},{16,24},... | collective-permute-start | bytes 983048 | tf_op jit(solution)/shard_map/ppermute | solution.py:66
  27.7 15.9 %copy-start.9 = (bf16[128,1280]{1,0:T(8,128)(2,1)}, bf16[128,1280]{1,0:T(8,128)(2,1)S(1)}, u32[]{:S(2)}) copy-start(bf16[128,1280]{1,0:T(8,128)(2,1)S(1)} %collective-permute-done.7.refs_5_.refs_8_) | copy-start | bytes 983044
  29.8 13.9 %copy-start.10 = (bf16[128,1280]{1,0:T(8,128)(2,1)}, bf16[128,1280]{1,0:T(8,128)(2,1)S(1)}, u32[]{:S(2)}) copy-start(bf16[128,1280]{1,0:T(8,128)(2,1)S(1)} %collective-permute-done.6.refs_2_.refs_5_) | copy-start | bytes 983044
  29.8 2.7 %collective-permute-start.8 = (bf16[512,1024]{1,0:T(8,128)(2,1)S(1)}, bf16[512,1024]{1,0:T(8,128)(2,1)S(1)}, u32[]{:S(2)}, u32[]{:S(2)}) collective-permute-start(bf16[512,1024]{1,0:T(8,128)(2,1)S(1)} %collective-permute-done.1.refs_0_), channel_id=1, source_target_pairs={{0,2},{2,0},{4,6},{6,4},{8,10},{10,8},{12,14},{14,12},{16,18},{18,... | collective-permute-start | bytes 3145736 | tf_op jit(solution)/shard_map/ppermute | solution.py:61
  29.8 10.1 %collective-permute-start.10 = (bf16[128,1280]{1,0:T(8,128)(2,1)S(1)}, bf16[128,1280]{1,0:T(8,128)(2,1)S(1)}, u32[]{:S(2)}, u32[]{:S(2)}) collective-permute-start(bf16[128,1280]{1,0:T(8,128)(2,1)S(1)} %collective-permute-done.6.refs_2_.refs_5_), channel_id=1, source_target_pairs={{0,4},{2,6},{4,0},{6,2},{8,12},{10,14},{12,8},{14,10},{16,20},{18,... | collective-permute-start | bytes 983048 | tf_op jit(solution)/shard_map/ppermute | solution.py:71
  31.3 11.6 %collective-permute-start.9 = (bf16[128,1280]{1,0:T(8,128)(2,1)S(1)}, bf16[128,1280]{1,0:T(8,128)(2,1)S(1)}, u32[]{:S(2)}, u32[]{:S(2)}) collective-permute-start(bf16[128,1280]{1,0:T(8,128)(2,1)S(1)} %collective-permute-done.6.refs_2_.refs_5_), channel_id=1, source_target_pairs={{0,8},{2,10},{4,12},{6,14},{8,16},{10,18},{12,20},{14,22},{16,24},... | collective-permute-start | bytes 983048 | tf_op jit(solution)/shard_map/ppermute | solution.py:66
  36.0 10.8 %copy-start = (bf16[2048,1024]{1,0:T(8,128)(2,1)}, bf16[2048,1024]{1,0:T(8,128)(2,1)S(1)}, u32[]{:S(2)}) copy-start(bf16[2048,1024]{1,0:T(8,128)(2,1)S(1)} %place_tokens.3.x_ref.refs_1_) | copy-start | bytes 12582916
  39.9 6.9 %copy-start.5 = (bf16[128,1280]{1,0:T(8,128)(2,1)}, bf16[128,1280]{1,0:T(8,128)(2,1)S(1)}, u32[]{:S(2)}) copy-start(bf16[128,1280]{1,0:T(8,128)(2,1)S(1)} %collective-permute-done.10.refs_6_.refs_9_) | copy-start | bytes 983044
  42.9 7.3 %copy-start.16 = (f32[1,8,16]{2,1,0:T(8,128)S(1)}, f32[1,8,16]{2,1,0:T(8,128)}, u32[]{:S(2)}) copy-start(f32[1,8,16]{2,1,0:T(8,128)} %param.11) | copy-start | bytes 1540
  42.9 7.3 %collective-permute-start.12 = (bf16[64,1280]{1,0:T(8,128)(2,1)S(1)}, bf16[64,1280]{1,0:T(8,128)(2,1)S(1)}, u32[]{:S(2)}, u32[]{:S(2)}) collective-permute-start(bf16[64,1280]{1,0:T(8,128)(2,1)S(1)} %slice.7), channel_id=1, source_target_pairs={{0,8},{2,10},{4,12},{6,14},{8,16},{10,18},{12,20},{14,22},{16,24},... | collective-permute-start | bytes 491528 | tf_op jit(solution)/shard_map/ppermute | solution.py:66
  43.0 7.2 %collective-permute-start.11 = (bf16[64,1280]{1,0:T(8,128)(2,1)S(1)}, bf16[64,1280]{1,0:T(8,128)(2,1)S(1)}, u32[]{:S(2)}, u32[]{:S(2)}) collective-permute-start(bf16[64,1280]{1,0:T(8,128)(2,1)S(1)} %slice.6), channel_id=1, source_target_pairs={{0,4},{2,6},{4,0},{6,2},{8,12},{10,14},{12,8},{14,10},{16,20},{18,... | collective-permute-start | bytes 491528 | tf_op jit(solution)/shard_map/ppermute | solution.py:71
  54.6 18.5 %all-to-all-start = ((bf16[8,272,128]{2,1,0:T(8,128)(2,1)}), bf16[8,272,128]{2,1,0:T(8,128)(2,1)S(1)}, u32[]{:S(2)}, u32[]{:S(2)}) async-start(bf16[8,272,128]{2,1,0:T(8,128)(2,1)} %get-tuple-element.56), calls=%async_computation | async-start | bytes 1114112 | tf_op jit(solution)/shard_map/all_to_all | solution.py:756
  87.8 11.6 %all-to-all-start.1 = ((bf16[8,128,128]{2,1,0:T(8,128)(2,1)}), bf16[8,128,128]{2,1,0:T(8,128)(2,1)S(1)}, u32[]{:S(2)}, u32[]{:S(2)}) async-start(bf16[8,128,128]{2,1,0:T(8,128)(2,1)} %get-tuple-element.68), calls=%async_computation.1 | async-start | bytes 524288 | tf_op jit(solution)/shard_map/all_to_all | solution.py:756
  95.7 8.7 %copy-start.20 = (bf16[512,128]{1,0:T(8,128)(2,1)S(1)}, bf16[512,128]{1,0:T(8,128)(2,1)}, u32[]{:S(2)}) copy-start(bf16[512,128]{1,0:T(8,128)(2,1)} %get-tuple-element.78) | copy-start | bytes 393220
  95.8 14.5 %copy-start.1 = (bf16[1024,1024]{1,0:T(8,128)(2,1)S(1)}, bf16[1024,1024]{1,0:T(8,128)(2,1)}, u32[]{:S(2)}) copy-start(bf16[1024,1024]{1,0:T(8,128)(2,1)} %w_ref.3) | copy-start | bytes 6291460
  95.8 14.5 %copy-start.14 = (bf16[512,128]{1,0:T(8,128)(2,1)S(1)}, bf16[512,128]{1,0:T(8,128)(2,1)}, u32[]{:S(2)}) copy-start(bf16[512,128]{1,0:T(8,128)(2,1)} %get-tuple-element.73.refs_0_) | copy-start | bytes 393220
  95.8 10.8 %collective-permute-start.15 = (bf16[512,128]{1,0:T(8,128)(2,1)}, bf16[512,128]{1,0:T(8,128)(2,1)S(1)}, u32[]{:S(2)}, u32[]{:S(2)}) collective-permute-start(bf16[512,128]{1,0:T(8,128)(2,1)} %get-tuple-element.74), channel_id=1, source_target_pairs={{0,2},{2,0},{4,6},{6,4},{8,10},{10,8},{12,14},{14,12},{16,18},{18,... | collective-permute-start | bytes 393224 | tf_op jit(solution)/shard_map/ppermute | solution.py:61
  95.9 11.4 %collective-permute-start.17 = (bf16[512,128]{1,0:T(8,128)(2,1)}, bf16[512,128]{1,0:T(8,128)(2,1)S(1)}, u32[]{:S(2)}, u32[]{:S(2)}) collective-permute-start(bf16[512,128]{1,0:T(8,128)(2,1)} %get-tuple-element.77), channel_id=1, source_target_pairs={{0,1},{1,0},{2,3},{3,2},{4,5},{5,4},{6,7},{7,6},{8,9},{9,8},{10,11... | collective-permute-start | bytes 393224 | tf_op jit(solution)/shard_map/ppermute | solution.py:95
  104.4 5.9 %collective-permute-start.18 = (bf16[512,128]{1,0:T(8,128)(2,1)S(1)}, bf16[512,128]{1,0:T(8,128)(2,1)S(1)}, u32[]{:S(2)}, u32[]{:S(2)}) collective-permute-start(bf16[512,128]{1,0:T(8,128)(2,1)S(1)} %copy-done.20), channel_id=1, source_target_pairs={{0,3},{1,2},{2,1},{3,0},{4,7},{5,6},{6,5},{7,4},{8,11},{9,10},{10,... | collective-permute-start | bytes 393224 | tf_op jit(solution)/shard_map/ppermute | solution.py:103
  104.5 5.8 %collective-permute-start.16 = (bf16[512,128]{1,0:T(8,128)(2,1)}, bf16[512,128]{1,0:T(8,128)(2,1)S(1)}, u32[]{:S(2)}, u32[]{:S(2)}) collective-permute-start(bf16[512,128]{1,0:T(8,128)(2,1)} %get-tuple-element.76), channel_id=1, source_target_pairs={{0,2},{2,0},{4,6},{6,4},{8,10},{10,8},{12,14},{14,12},{16,18},{18,... | collective-permute-start | bytes 393224 | tf_op jit(solution)/shard_map/ppermute | solution.py:61
  105.9 7.1 %collective-permute-start.13 = (bf16[512,128]{1,0:T(8,128)(2,1)}, bf16[512,128]{1,0:T(8,128)(2,1)S(1)}, u32[]{:S(2)}, u32[]{:S(2)}) collective-permute-start(bf16[512,128]{1,0:T(8,128)(2,1)} %get-tuple-element.70), channel_id=1, source_target_pairs={{0,1},{1,0},{2,3},{3,2},{4,5},{5,4},{6,7},{7,6},{8,9},{9,8},{10,11... | collective-permute-start | bytes 393224 | tf_op jit(solution)/shard_map/ppermute | solution.py:95
  106.6 9.1 %collective-permute-start.14 = (bf16[512,128]{1,0:T(8,128)(2,1)}, bf16[512,128]{1,0:T(8,128)(2,1)S(1)}, u32[]{:S(2)}, u32[]{:S(2)}) collective-permute-start(bf16[512,128]{1,0:T(8,128)(2,1)} %get-tuple-element.71), channel_id=1, source_target_pairs={{0,3},{1,2},{2,1},{3,0},{4,7},{5,6},{6,5},{7,4},{8,11},{9,10},{10,... | collective-permute-start | bytes 393224 | tf_op jit(solution)/shard_map/ppermute | solution.py:103
  (10 other events, 21.7 us)

commit v12 on v10

--- a/solution.py
+++ b/solution.py
@@ -193,7 +193,7 @@
     lax.fori_loop(0, part.shape[0] // step, norm, 0)
 
 
-def rank_kernel(groups, ids_ref, row_ref, col_ref):
+def rank_kernel(groups, ids_ref, row_ref):
     tokens = ids_ref.shape[1]
     block = tokens // groups
     label = lax.broadcasted_iota(jnp.int32, (groups, tokens), 0)
@@ -208,27 +208,37 @@
             jnp.dot(held_bf, jnp.where(before, 1.0, 0.0).astype(bf16), preferred_element_type=f32)
         )
     count = jnp.concatenate(counts, axis=1)
-    rank = jnp.sum(
+    row_ref[...] = jnp.sum(
         jnp.where(held, count + (label * block).astype(f32), 0.0), axis=0, keepdims=True
     )
-    row_ref[...] = rank
-    for at in range(0, tokens, LANES):
-        wide = jnp.broadcast_to(rank[:, at : at + LANES], (LANES, LANES))
-        col_ref[at : at + LANES, :] = wide.T
 
 
 def rank_tokens(ids, groups):
     tokens = ids.shape[0]
     return pl.pallas_call(
         functools.partial(rank_kernel, groups),
-        out_shape=(
-            jax.ShapeDtypeStruct((1, tokens), f32),
-            jax.ShapeDtypeStruct((tokens, LANES), f32),
-        ),
+        out_shape=jax.ShapeDtypeStruct((1, tokens), f32),
         compiler_params=params(),
         cost_estimate=cost(0, 4 * tokens),
         name="rank_tokens",
     )(ids.reshape(1, tokens))
+
+
+def turn_kernel(row_ref, col_ref):
+    for at in range(0, col_ref.shape[0], LANES):
+        col_ref[at : at + LANES, :] = jnp.broadcast_to(
+            row_ref[:, at : at + LANES], (LANES, LANES)
+        ).T
+
+
+def turn_places(rank):
+    return pl.pallas_call(
+        turn_kernel,
+        out_shape=jax.ShapeDtypeStruct((rank.shape[1], LANES), f32),
+        compiler_params=params(),
+        cost_estimate=cost(0, 4 * LANES),
+        name="turn_places",
+    )(rank)
 
 
 def picks(rank, at, rows):
@@ -325,9 +335,11 @@
 
 def update_kernel(plan, groups, *refs):
     decay_refs, refs = refs[: plan.merge], refs[plan.merge :]
-    v_ref, b_ref, x_ref, last_refs, (left, total_ref, u) = (
-        refs[0], refs[1], refs[2], refs[3:-3], refs[-3:]
+    v_ref, b_ref, x_ref, last_refs, (left, total_out, total_ref, u, sems) = (
+        refs[0], refs[1], refs[2], refs[3:-5], refs[-5:]
     )
+    copies = Copies(sems)
+    leaving = []
     every = v_ref.shape[0]
     tokens = every // plan.merge
     block = tokens // groups
@@ -393,6 +405,10 @@
                 at = share + n * items + i
                 total_ref[d, at : at + 1, :] = piece
                 product = product - piece.astype(f32)
+        if (d + 1) % (peers // 4) == 0:
+            done = slice(d + 1 - peers // 4, d + 1)
+            leaving.append(copies.start(total_ref.at[done], total_out.at[done]))
+    finish(leaving)
 
 
 def share_rows(share):
@@ -406,11 +422,16 @@
     return pl.pallas_call(
         functools.partial(update_kernel, plan, groups),
         in_specs=[smem] * plan.merge + [vmem] * (3 + len(last)),
+        out_specs=(vmem, hbm),
         out_shape=(
             jax.ShapeDtypeStruct((plan.merge, rows, LANES), bf16),
             jax.ShapeDtypeStruct((plan.chips, share_rows(share), LANES), bf16),
         ),
-        scratch_shapes=[pltpu.VMEM((plan.merge, rows, LANES), f32)],
+        scratch_shapes=[
+            pltpu.VMEM((plan.chips, share_rows(share), LANES), bf16),
+            pltpu.VMEM((plan.merge, rows, LANES), f32),
+            Copies.scratch(),
+        ],
         compiler_params=params(),
         cost_estimate=cost(4 * every * 256 * 2 * cols, 6 * every * cols),
         name="block_updates",
@@ -585,7 +606,7 @@
     a_ins, refs = refs[: plan.merge], refs[plan.merge :]
     c_ins, refs = refs[: plan.merge], refs[plan.merge :]
     s_in, rank_in, refs = refs[0], refs[1], refs[2:]
-    out_refs, (a, c, state, rank, mixed, sems) = refs[:-6], refs[-6:]
+    out_refs, (a, c, state, rank, mixed, out, sems) = refs[:-7], refs[-7:]
     copies = Copies(sems)
     tokens = rank.shape[0]
     block = tokens // groups
@@ -627,10 +648,14 @@
 
     ranking.wait()
     local = tokens // plan.peers
+    leaving = []
     for k in list(range(1, plan.peers)) + [0]:
         placed = back_rows(rank, k * local, mixed, local)
         for s in range(plan.merge):
-            out_refs[s * plan.peers + k][...] = placed[:, s * width : (s + 1) * width]
+            i = s * plan.peers + k
+            out[i] = placed[:, s * width : (s + 1) * width]
+            leaving.append(copies.start(out.at[i], out_refs[i]))
+    finish(leaving)
 
 
 def back_rows(rank, start, mixed, rows):
@@ -658,7 +683,7 @@
     return pl.pallas_call(
         functools.partial(mix_kernel, plan, groups),
         in_specs=[smem] * plan.merge + [hbm] * (2 * plan.merge + 2),
-        out_specs=(vmem,) * count,
+        out_specs=(hbm,) * count,
         out_shape=(jax.ShapeDtypeStruct((tokens // plan.peers, width), bf16),) * count,
         scratch_shapes=[
             pltpu.VMEM((plan.merge, tokens, width), f32),
@@ -666,32 +691,49 @@
             pltpu.VMEM(state.shape, bf16),
             pltpu.VMEM(rank.shape, f32),
             pltpu.VMEM((tokens, plan.merge * width), bf16),
+            pltpu.VMEM((count, tokens // plan.peers, width), bf16),
             Copies.scratch(),
         ],
-        compiler_params=params(56),
+        compiler_params=params(60),
         cost_estimate=cost(4 * tokens * tokens * width, 2 * tokens * tokens + 16 * tokens * width),
         name="mix",
     )(*decays, *attended, *readers, state, rank)
 
 
 def out_kernel(plan, sources, w_ref, *refs):
-    part_refs, base_refs, out_ref = refs[: len(sources)], refs[len(sources) : -1], refs[-1]
+    part_refs, base_refs, out_ref = refs[: len(sources)], refs[len(sources) : -3], refs[-3]
+    kept, sems = refs[-2:]
+    copies = Copies(sems)
     depth = part_refs[0].shape[1]
     core, me = plan.core(), lax.axis_index("head")
-    total = base_refs[0][...] if base_refs else 0.0
-    for (s, k), part in zip(sources, part_refs):
+    owners = []
+    for s, k in sources:
         owner = lax.rem(me - k + plan.peers, plan.peers) * plan.merge
-        owner = owner + (core if s == 0 else 1 - core)
-        rows = pl.ds(pl.multiple_of(owner * depth, depth), depth)
-        total = total + jnp.dot(part[...], w_ref[rows, :], preferred_element_type=f32)
-    out_ref[...] = total.astype(out_ref.dtype)
+        owners.append(owner + (core if s == 0 else 1 - core))
+    leaving = []
+    step = min(128, out_ref.shape[0])
+    for at in range(0, out_ref.shape[0], step):
+        there = slice(at, at + step)
+        total = base_refs[0][there, :] if base_refs else 0.0
+        for owner, part in zip(owners, part_refs):
+            rows = pl.ds(pl.multiple_of(owner * depth, depth), depth)
+            total = total + jnp.dot(part[there, :], w_ref[rows, :], preferred_element_type=f32)
+        if base_refs:
+            kept[there, :] = total.astype(out_ref.dtype)
+            leaving.append(copies.start(kept.at[there], out_ref.at[there]))
+        else:
+            out_ref[there, :] = total.astype(out_ref.dtype)
+    finish(leaving)
 
 
 def project_out(plan, w, parts, base, kind):
     local, width = next(iter(parts.values())).shape[0], w.shape[1]
     return pl.pallas_call(
         functools.partial(out_kernel, plan, list(parts)),
+        in_specs=[vmem] * (1 + len(parts) + len(base)),
+        out_specs=hbm if base else vmem,
         out_shape=jax.ShapeDtypeStruct((local, width), kind),
+        scratch_shapes=[pltpu.VMEM((local, width), kind), Copies.scratch()],
         compiler_params=params(),
         cost_estimate=cost(0, 4 * local),
         name="project_out",
@@ -712,10 +754,9 @@
     block = reorder(plan, [in_weight] + [plan.swap(in_weight)] * (plan.merge - 1))
     ids = jnp.roll(block_ids, -me * local_tokens)
     ids, rates = lax.optimization_barrier((ids, rates))
-    rank, places = rank_tokens(ids, groups)
-    part = place_tokens(plan, rank, 0, owns, [])
-
-    def fill(arriving):
+    rank = rank_tokens(ids, groups)
+
+    def fill(arriving, part):
         if plan.merge == 2:
             arriving = arriving + [plan.swap(tokens) for tokens in arriving]
         return place_tokens(plan, rank, local_tokens, arriving, [part])
@@ -724,10 +765,14 @@
         blocks, crossed = [block], []
         half = block.shape[0] // 2
         for k in range(plan.along - 1):
-            with_ = part if k == 0 else ()
+            with_ = rank if k == 0 else ()
+            if k == min(1, plan.along - 2):
+                rank, owns, _ = lax.optimization_barrier((rank, owns, blocks[-1]))
+                part = with_ = place_tokens(plan, rank, 0, owns, [])
+                places = turn_places(rank)
             if k == plan.along - 2:
                 arriving, _ = lax.optimization_barrier((arriving, blocks[-1]))
-                x = with_ = fill(arriving)
+                x = with_ = fill(arriving, part)
             passed, across, with_ = lax.optimization_barrier(
                 (plan.round(blocks[-1]), plan.cross(blocks[-1]), with_)
             )
@@ -739,7 +784,8 @@
         weights = [
             lax.all_gather(block, "tm", axis=0, tiled=True, axis_index_groups=plan.groups())
         ]
-        x = fill(arriving)
+        places = turn_places(rank)
+        x = fill(arriving, place_tokens(plan, rank, 0, owns, []))
     if plan.ringed:
         v, b, x_last = project(plan, x, weights[:-2])
         local, total = block_updates(plan, rates, v, b, x_last, last, groups)

time: 113 us -> 113 us (level)
    pallas_call x3 -> x4, Pallas kernels: 2.84 us -> 3.54 us  [the longest x2 3.03 us: project_out(): pl.pallas_call(functools.partial(out_kernel, plan, list(parts)), in_specs...]
  transfers between devices with their start and end apart: 18 -> 18, of which waited for: 13 -> 13; matrix products, arithmetic and copies ran while one was open for 1% -> 1% of each run, Pallas kernels for 26% -> 27%
where the time goes in v12:
time: 113 us
  Pallas kernels  43.4 us (38%)
  waiting for transfers between devices  42.1 us (37%)
  starting transfers between devices  20.4 us (18%)
  local copies, waits for them, and re-layouts  5.54 us (5%)
    pallas_call x2, Pallas kernels, attend(): pl.pallas_call(functools.partial(attend_kernel, plan, slot), in_specs=[sm...  18.3 us
    ppermute x4, waiting for transfers between devices, round(): return lax.ppermute(block, 'tm', pairs)  16 us
    all_to_all x2, starting transfers between devices, exchange(): lax.all_to_all(blocks, 'tm', split_axis=0, concat_axis=0, tiled=True, axi...  7.38 us
    all_to_all x2, waiting for transfers between devices, exchange(): lax.all_to_all(blocks, 'tm', split_axis=0, concat_axis=0, tiled=True, axi...  7.2 us
    pallas_call x2, Pallas kernels, place_tokens(): pl.pallas_call(functools.partial(place_kernel, plan.merge, parts, start),...  7.02 us
    pallas_call x1, Pallas kernels, mix(): pl.pallas_call(functools.partial(mix_kernel, plan, groups), in_specs=[sme...  5.7 us
    ppermute x4, waiting for transfers between devices, cross(): return lax.ppermute(block, 'tm', pairs)  5.53 us
    unnamed x41, local copies, waits for them, and re-layouts  5.51 us
  transfers between devices with their start and end apart: 18, of which 13 were waited for; matrix products, arithmetic and copies ran while one was open for 1% of the time, Pallas kernels for 27%

profile of v12, /device:TPU:0, one launch (start us, length us, event | category | flops | bytes accessed | tf_op | source)
XLA Modules:
  0.0 112.7 jit_solution(18169410584386297170)
XLA Ops:
  0.5 2.5 %collective-permute-start.5 = (bf16[512,1024]{1,0:T(8,128)(2,1)}, bf16[512,1024]{1,0:T(8,128)(2,1)S(1)}, u32[]{:S(2)}, u32[]{:S(2)}) collective-permute-start(bf16[512,1024]{1,0:T(8,128)(2,1)} %bitcast.6), channel_id=1, source_target_pairs={{0,1},{1,0},{2,3},{3,2},{4,5},{5,4},{6,7},{7,6},{8,9},{9,8},{10,11... | collective-permute-start | bytes 3145736 | tf_op jit(solution)/shard_map/ppermute | solution.py:95
  3.2 1.6 %collective-permute-done.2.refs_1_ = bf16[64,2560]{1,0:T(8,128)(2,1)S(1)} collective-permute-done((bf16[64,2560]{1,0:T(8,128)(2,1)}, bf16[64,2560]{1,0:T(8,128)(2,1)S(1)}, u32[]{:S(2)}, u32[]{:S(2)}) %collective-permute-start.2) | collective-permute-done | bytes 327712 | tf_op jit(solution)/shard_map/ppermute | solution.py:61
  4.8 1.0 copy-done.11
  6.0 1.6 %collective-permute-start.3 = (bf16[128,1280]{1,0:T(8,128)(2,1)S(1)}, bf16[128,1280]{1,0:T(8,128)(2,1)S(1)}, u32[]{:S(2)}, u32[]{:S(2)}) collective-permute-start(bf16[128,1280]{1,0:T(8,128)(2,1)S(1)} %reorder.1.refs_0_.refs_3_), channel_id=1, source_target_pairs={{0,8},{2,10},{4,12},{6,14},{8,16},{10,18},{12,20},{14,22},{16,24},... | collective-permute-start | bytes 983048 | tf_op jit(solution)/shard_map/ppermute | solution.py:66
  7.6 1.5 %collective-permute-start.4 = (bf16[128,1280]{1,0:T(8,128)(2,1)S(1)}, bf16[128,1280]{1,0:T(8,128)(2,1)S(1)}, u32[]{:S(2)}, u32[]{:S(2)}) collective-permute-start(bf16[128,1280]{1,0:T(8,128)(2,1)S(1)} %reorder.1.refs_0_.refs_3_), channel_id=1, source_target_pairs={{0,4},{2,6},{4,0},{6,2},{8,12},{10,14},{12,8},{14,10},{16,20},{18,... | collective-permute-start | bytes 983048 | tf_op jit(solution)/shard_map/ppermute | solution.py:71
  10.8 6.9 %collective-permute-done.3.refs_1_.refs_4_ = bf16[128,1280]{1,0:T(8,128)(2,1)S(1)} collective-permute-done((bf16[128,1280]{1,0:T(8,128)(2,1)S(1)}, bf16[128,1280]{1,0:T(8,128)(2,1)S(1)}, u32[]{:S(2)}, u32[]{:S(2)}) %collective-permute-start.3) | collective-permute-done | bytes 327712 | tf_op jit(solution)/shard_map/ppermute | solution.py:66
  17.7 1.0 collective-permute-start.6
  18.7 1.5 %collective-permute-start.7 = (bf16[128,1280]{1,0:T(8,128)(2,1)S(1)}, bf16[128,1280]{1,0:T(8,128)(2,1)S(1)}, u32[]{:S(2)}, u32[]{:S(2)}) collective-permute-start(bf16[128,1280]{1,0:T(8,128)(2,1)S(1)} %collective-permute-done.3.refs_1_.refs_4_), channel_id=1, source_target_pairs={{0,4},{2,6},{4,0},{6,2},{8,12},{10,14},{12,8},{14,10},{16,20},{18,... | collective-permute-start | bytes 983048 | tf_op jit(solution)/shard_map/ppermute | solution.py:71
  20.2 1.2 %copy-done.4 = bf16[1,512,1024]{2,1,0:T(8,128)(2,1)S(1)} copy-done((bf16[1,512,1024]{2,1,0:T(8,128)(2,1)S(1)}, bf16[1,512,1024]{2,1,0:T(8,128)(2,1)}, u32[]{:S(2)}) %copy-start.4) | copy-done | bytes 1048600
  21.5 3.5 %place_tokens.2.refs_2_ = bf16[2048,1024]{1,0:T(8,128)(2,1)S(1)} custom-call(f32[1,1024]{1,0:T(1,128)S(1)} %rank_tokens.1.rank_ref.row_ref, bf16[512,1024]{1,0:T(8,128)(2,1)S(1)} %bitcast.7, bf16[512,1024]{1,0:T(8,128)(2,1)S(1)} %collective-permute-done.1.refs_1_), custom_call_target="tpu_custom_call" | custom-call | bytes 4096 | tf_op jit(solution)/shard_map/place_tokens/pallas_call | solution.py:275
  24.9 3.7 %collective-permute-done.6.refs_2_.refs_5_ = bf16[128,1280]{1,0:T(8,128)(2,1)S(1)} collective-permute-done((bf16[128,1280]{1,0:T(8,128)(2,1)S(1)}, bf16[128,1280]{1,0:T(8,128)(2,1)S(1)}, u32[]{:S(2)}, u32[]{:S(2)}) %collective-permute-start.6) | collective-permute-done | bytes 327712 | tf_op jit(solution)/shard_map/ppermute | solution.py:66
  28.8 1.6 %collective-permute-start.10 = (bf16[128,1280]{1,0:T(8,128)(2,1)S(1)}, bf16[128,1280]{1,0:T(8,128)(2,1)S(1)}, u32[]{:S(2)}, u32[]{:S(2)}) collective-permute-start(bf16[128,1280]{1,0:T(8,128)(2,1)S(1)} %collective-permute-done.6.refs_2_.refs_5_), channel_id=1, source_target_pairs={{0,4},{2,6},{4,0},{6,2},{8,12},{10,14},{12,8},{14,10},{16,20},{18,... | collective-permute-start | bytes 983048 | tf_op jit(solution)/shard_map/ppermute | solution.py:71
  30.3 1.1 collective-permute-done.8.refs_1_
  31.4 3.6 %place_tokens.3.x_ref.refs_1_ = bf16[2048,1024]{1,0:T(8,128)(2,1)S(1)} custom-call(f32[1,1024]{1,0:T(1,128)S(1)} %rank_tokens.1.rank_ref.row_ref, bf16[512,1024]{1,0:T(8,128)(2,1)S(1)} %collective-permute-done.5.refs_0_, bf16[512,1024]{1,0:T(8,128)(2,1)S(1)} %collective-permute-done.8.refs_1_, bf16[2048,1024]{1,0:T(8,128)(2,1)S(1)} %place_tokens.2.refs_2_), custom_call_target="tpu_custom_call" | custom-call | bytes 4096 | tf_op jit(solution)/shard_map/place_tokens/pallas_call | solution.py:275
  35.0 3.9 %collective-permute-done.10.refs_6_.refs_9_ = bf16[128,1280]{1,0:T(8,128)(2,1)S(1)} collective-permute-done((bf16[128,1280]{1,0:T(8,128)(2,1)S(1)}, bf16[128,1280]{1,0:T(8,128)(2,1)S(1)}, u32[]{:S(2)}, u32[]{:S(2)}) %collective-permute-start.10) | collective-permute-done | bytes 327712 | tf_op jit(solution)/shard_map/ppermute | solution.py:71
  38.9 3.0 %collective-permute-done.9.refs_3_.refs_6_ = bf16[128,1280]{1,0:T(8,128)(2,1)S(1)} collective-permute-done((bf16[128,1280]{1,0:T(8,128)(2,1)S(1)}, bf16[128,1280]{1,0:T(8,128)(2,1)S(1)}, u32[]{:S(2)}, u32[]{:S(2)}) %collective-permute-start.9) | collective-permute-done | bytes 327712 | tf_op jit(solution)/shard_map/ppermute | solution.py:66
  42.7 3.1 %project.1 = (f32[2048,256]{1,0:T(8,128)S(1)}, f32[256,2048]{1,0:T(8,128)S(1)}, bf16[2048,128]{1,0:T(8,128)(2,1)S(1)}) custom-call(bf16[2048,1024]{1,0:T(8,128)(2,1)S(1)} %place_tokens.3.x_ref.refs_1_, bf16[128,1280]{1,0:T(8,128)(2,1)S(1)} %reorder.1.refs_0_.refs_3_, bf16[128,1280]{1,0:T(8,128)(2,1)S(1)} %collective-permute-done.3.refs_1_.refs_4_, ...), custom_call_target="tpu_custom_call" | custom-call | bytes 4096 | tf_op jit(solution)/shard_map/project/pallas_call | solution.py:322
  45.8 1.6 %collective-permute-done.11.refs_5_.refs_10_ = bf16[64,1280]{1,0:T(8,128)(2,1)S(1)} collective-permute-done((bf16[64,1280]{1,0:T(8,128)(2,1)S(1)}, bf16[64,1280]{1,0:T(8,128)(2,1)S(1)}, u32[]{:S(2)}, u32[]{:S(2)}) %collective-permute-start.11) | collective-permute-done | bytes 163872 | tf_op jit(solution)/shard_map/ppermute | solution.py:71
  47.4 2.3 %collective-permute-done.12.refs_6_.refs_11_ = bf16[64,1280]{1,0:T(8,128)(2,1)S(1)} collective-permute-done((bf16[64,1280]{1,0:T(8,128)(2,1)S(1)}, bf16[64,1280]{1,0:T(8,128)(2,1)S(1)}, u32[]{:S(2)}, u32[]{:S(2)}) %collective-permute-start.12) | collective-permute-done | bytes 163872 | tf_op jit(solution)/shard_map/ppermute | solution.py:66
  49.7 4.6 %block_updates.1 = (bf16[2,2048,128]{2,1,0:T(8,128)(2,1)S(1)}, bf16[8,272,128]{2,1,0:T(8,128)(2,1)}) custom-call(f32[8,16]{1,0:T(8,128)S(1)} %bitcast.11, f32[8,16]{1,0:T(8,128)S(1)} %collective-permute-done.refs_1_, f32[2048,256]{1,0:T(8,128)S(1)} %get-tuple-element.49.refs_2_, f32[256,2048]{1,0:T(8,128)S(1)} %get-tuple-element.50.refs_3_, ...), custom_call_target="tpu_custom_call" | custom-call | flops 1073741824 | bytes 3145728 | tf_op jit(solution)/shard_map/block_updates/pallas_call | solution.py:422
  54.4 3.7 %all-to-all-start = ((bf16[8,272,128]{2,1,0:T(8,128)(2,1)}), bf16[8,272,128]{2,1,0:T(8,128)(2,1)S(1)}, u32[]{:S(2)}, u32[]{:S(2)}) async-start(bf16[8,272,128]{2,1,0:T(8,128)(2,1)} %get-tuple-element.52), calls=%async_computation | async-start | bytes 1114112 | tf_op jit(solution)/shard_map/all_to_all | solution.py:797
  58.8 9.2 %attend.2 = (f32[1024,256]{1,0:T(8,128)}, bf16[1024,256]{1,0:T(8,128)(2,1)}) custom-call(s32[16,4]{1,0:T(8,128)} %copy.7.refs_0_, bf16[2048,1024]{1,0:T(8,128)(2,1)} %copy-done, bf16[2,2048,128]{2,1,0:T(8,128)(2,1)} %copy-done.17, bf16[128,1280]{1,0:T(8,128)(2,1)} %copy-done.3, bf16[128,1280]{1,0:T(8,128)(2,1)} %copy-done.7, bf16[128,1280]{1,0:T(8,128)(2,1)} %copy-done.9, ...), custom_call_target="tpu_custom_call" | custom-call | flops 4831838208 | bytes 11534336 | tf_op jit(solution)/shard_map/attend/pallas_call | solution.py:566
  68.0 3.5 %all-to-all-done.u_ref = bf16[8,272,128]{2,1,0:T(8,128)(2,1)S(1)} async-done(((bf16[8,272,128]{2,1,0:T(8,128)(2,1)}), bf16[8,272,128]{2,1,0:T(8,128)(2,1)S(1)}, u32[]{:S(2)}, u32[]{:S(2)}) %all-to-all-start) | async-done | bytes 557088 | tf_op jit(solution)/shard_map/all_to_all | solution.py:797
  72.4 3.6 %all-to-all-start.1 = ((bf16[8,256,128]{2,1,0:T(8,128)(2,1)}), bf16[8,256,128]{2,1,0:T(8,128)(2,1)S(1)}, u32[]{:S(2)}, u32[]{:S(2)}) async-start(bf16[8,256,128]{2,1,0:T(8,128)(2,1)} %scan_states.1), calls=%async_computation.1 | async-start | bytes 1048576 | tf_op jit(solution)/shard_map/all_to_all | solution.py:797
  77.1 9.1 %attend.3 = (f32[1024,256]{1,0:T(8,128)}, bf16[1024,256]{1,0:T(8,128)(2,1)}) custom-call(s32[16,4]{1,0:T(8,128)} %copy.7.refs_0_, bf16[2048,1024]{1,0:T(8,128)(2,1)} %copy-done, bf16[2,2048,128]{2,1,0:T(8,128)(2,1)} %copy-done.17, bf16[128,1280]{1,0:T(8,128)(2,1)} %copy-done.3, bf16[128,1280]{1,0:T(8,128)(2,1)} %copy-done.7, bf16[128,1280]{1,0:T(8,128)(2,1)} %copy-done.9, ...), custom_call_target="tpu_custom_call" | custom-call | flops 4831838208 | bytes 11534336 | tf_op jit(solution)/shard_map/attend/pallas_call | solution.py:566
  86.2 3.7 %all-to-all-done.1 = bf16[8,256,128]{2,1,0:T(8,128)(2,1)S(1)} async-done(((bf16[8,256,128]{2,1,0:T(8,128)(2,1)}), bf16[8,256,128]{2,1,0:T(8,128)(2,1)S(1)}, u32[]{:S(2)}, u32[]{:S(2)}) %all-to-all-start.1) | async-done | bytes 524320 | tf_op jit(solution)/shard_map/all_to_all | solution.py:797
  90.7 5.7 %mix.1 = (bf16[512,256]{1,0:T(8,128)(2,1)}, bf16[512,256]{1,0:T(8,128)(2,1)}, bf16[512,256]{1,0:T(8,128)(2,1)}, bf16[512,256]{1,0:T(8,128)(2,1)}) custom-call(f32[8,16]{1,0:T(8,128)} %bitcast.10, f32[8,16]{1,0:T(8,128)} %copy-done.16, f32[1024,256]{1,0:T(8,128)} %get-tuple-element.56.refs_2_, f32[1024,256]{1,0:T(8,128)} %get-tuple-element.59.refs_3_, ...), custom_call_target="tpu_custom_call" | custom-call | flops 1073741824 | bytes 6291456 | tf_op jit(solution)/shard_map/mix/pallas_call | solution.py:683
  96.5 1.4 %collective-permute-start.13 = (bf16[512,256]{1,0:T(8,128)(2,1)}, bf16[512,256]{1,0:T(8,128)(2,1)S(1)}, u32[]{:S(2)}, u32[]{:S(2)}) collective-permute-start(bf16[512,256]{1,0:T(8,128)(2,1)} %get-tuple-element.63), channel_id=1, source_target_pairs={{0,1},{1,0},{2,3},{3,2},{4,5},{5,4},{6,7},{7,6},{8,9},{9,8},{10,11... | collective-permute-start | bytes 786440 | tf_op jit(solution)/shard_map/ppermute | solution.py:95
  99.4 1.2 %project_out.2.refs_2_ = f32[512,1024]{1,0:T(8,128)S(1)} custom-call(bf16[1024,1024]{1,0:T(8,128)(2,1)S(1)} %copy-done.1, bf16[512,256]{1,0:T(8,128)(2,1)S(1)} %copy-done.12, bf16[512,256]{1,0:T(8,128)(2,1)S(1)} %collective-permute-done.15.refs_1_), custom_call_target="tpu_custom_call" | custom-call | bytes 2048 | tf_op jit(solution)/shard_map/project_out/pallas_call | solution.py:731
  100.5 5.4 %collective-permute-done.13.refs_0_ = bf16[512,256]{1,0:T(8,128)(2,1)S(1)} collective-permute-done((bf16[512,256]{1,0:T(8,128)(2,1)}, bf16[512,256]{1,0:T(8,128)(2,1)S(1)}, u32[]{:S(2)}, u32[]{:S(2)}) %collective-permute-start.13) | collective-permute-done | bytes 262176 | tf_op jit(solution)/shard_map/ppermute | solution.py:95
  105.9 4.7 %collective-permute-done.14.refs_1_ = bf16[512,256]{1,0:T(8,128)(2,1)S(1)} collective-permute-done((bf16[512,256]{1,0:T(8,128)(2,1)}, bf16[512,256]{1,0:T(8,128)(2,1)S(1)}, u32[]{:S(2)}, u32[]{:S(2)}) %collective-permute-start.14) | collective-permute-done | bytes 262176 | tf_op jit(solution)/shard_map/ppermute | solution.py:103
  110.6 1.9 %project_out.3 = bf16[512,1024]{1,0:T(8,128)(2,1)} custom-call(bf16[1024,1024]{1,0:T(8,128)(2,1)S(1)} %copy-done.1, bf16[512,256]{1,0:T(8,128)(2,1)S(1)} %collective-permute-done.13.refs_0_, bf16[512,256]{1,0:T(8,128)(2,1)S(1)} %collective-permute-done.14.refs_1_, f32[512,1024]{1,0:T(8,128)S(1)} %project_out.2.refs_2_), custom_call_target="tpu_custom_call" | custom-call | bytes 2048 | tf_op jit(solution)/shard_map/project_out/pallas_call | solution.py:731
  (61 shorter events, 8.3 us)
Async XLA Ops:
  0.0 20.2 %collective-permute-start.1 = (bf16[512,1024]{1,0:T(8,128)(2,1)}, bf16[512,1024]{1,0:T(8,128)(2,1)S(1)}, u32[]{:S(2)}, u32[]{:S(2)}) collective-permute-start(bf16[512,1024]{1,0:T(8,128)(2,1)} %bitcast.5), channel_id=1, source_target_pairs={{0,2},{2,0},{4,6},{6,4},{8,10},{10,8},{12,14},{14,12},{16,18},{18,... | collective-permute-start | bytes 3145736 | tf_op jit(solution)/shard_map/ppermute | solution.py:61
  0.5 28.2 %collective-permute-start.5 = (bf16[512,1024]{1,0:T(8,128)(2,1)}, bf16[512,1024]{1,0:T(8,128)(2,1)S(1)}, u32[]{:S(2)}, u32[]{:S(2)}) collective-permute-start(bf16[512,1024]{1,0:T(8,128)(2,1)} %bitcast.6), channel_id=1, source_target_pairs={{0,1},{1,0},{2,3},{3,2},{4,5},{5,4},{6,7},{7,6},{8,9},{9,8},{10,11... | collective-permute-start | bytes 3145736 | tf_op jit(solution)/shard_map/ppermute | solution.py:95
  3.0 1.8 %collective-permute-start.2 = (bf16[64,2560]{1,0:T(8,128)(2,1)}, bf16[64,2560]{1,0:T(8,128)(2,1)S(1)}, u32[]{:S(2)}, u32[]{:S(2)}) collective-permute-start(bf16[64,2560]{1,0:T(8,128)(2,1)} %refs_0_.3), channel_id=1, source_target_pairs={{0,2},{2,0},{4,6},{6,4},{8,10},{10,8},{12,14},{14,12},{16,18},{18,... | collective-permute-start | bytes 983048 | tf_op jit(solution)/shard_map/ppermute | solution.py:61
  5.9 36.7 %copy-start.3 = (bf16[128,1280]{1,0:T(8,128)(2,1)}, bf16[128,1280]{1,0:T(8,128)(2,1)S(1)}, u32[]{:S(2)}) copy-start(bf16[128,1280]{1,0:T(8,128)(2,1)S(1)} %reorder.1.refs_0_.refs_3_) | copy-start | bytes 983044
  6.0 11.8 %collective-permute-start.3 = (bf16[128,1280]{1,0:T(8,128)(2,1)S(1)}, bf16[128,1280]{1,0:T(8,128)(2,1)S(1)}, u32[]{:S(2)}, u32[]{:S(2)}) collective-permute-start(bf16[128,1280]{1,0:T(8,128)(2,1)S(1)} %reorder.1.refs_0_.refs_3_), channel_id=1, source_target_pairs={{0,8},{2,10},{4,12},{6,14},{8,16},{10,18},{12,20},{14,22},{16,24},... | collective-permute-start | bytes 983048 | tf_op jit(solution)/shard_map/ppermute | solution.py:66
  7.6 10.1 %collective-permute-start.4 = (bf16[128,1280]{1,0:T(8,128)(2,1)S(1)}, bf16[128,1280]{1,0:T(8,128)(2,1)S(1)}, u32[]{:S(2)}, u32[]{:S(2)}) collective-permute-start(bf16[128,1280]{1,0:T(8,128)(2,1)S(1)} %reorder.1.refs_0_.refs_3_), channel_id=1, source_target_pairs={{0,4},{2,6},{4,0},{6,2},{8,12},{10,14},{12,8},{14,10},{16,20},{18,... | collective-permute-start | bytes 983048 | tf_op jit(solution)/shard_map/ppermute | solution.py:71
  9.1 1.4 %collective-permute-start = (f32[8,16]{1,0:T(8,128)}, f32[8,16]{1,0:T(8,128)S(1)}, u32[]{:S(2)}, u32[]{:S(2)}) collective-permute-start(f32[8,16]{1,0:T(8,128)} %bitcast.9), channel_id=1, source_target_pairs={{0,2},{2,0},{4,6},{6,4},{8,10},{10,8},{12,14},{14,12},{16,18},{18,... | collective-permute-start | bytes 1544 | tf_op jit(solution)/shard_map/ppermute | solution.py:61
  10.5 39.3 %copy-start.16 = (f32[8,16]{1,0:T(8,128)}, f32[8,16]{1,0:T(8,128)S(1)}, u32[]{:S(2)}) copy-start(f32[8,16]{1,0:T(8,128)S(1)} %collective-permute-done.refs_1_) | copy-start | bytes 1540
  17.7 24.9 %copy-start.7 = (bf16[128,1280]{1,0:T(8,128)(2,1)}, bf16[128,1280]{1,0:T(8,128)(2,1)S(1)}, u32[]{:S(2)}) copy-start(bf16[128,1280]{1,0:T(8,128)(2,1)S(1)} %collective-permute-done.3.refs_1_.refs_4_) | copy-start | bytes 983044
  17.7 24.9 %copy-start.8 = (bf16[128,1280]{1,0:T(8,128)(2,1)}, bf16[128,1280]{1,0:T(8,128)(2,1)S(1)}, u32[]{:S(2)}) copy-start(bf16[128,1280]{1,0:T(8,128)(2,1)S(1)} %collective-permute-done.4.refs_4_.refs_7_) | copy-start | bytes 983044
  17.7 10.9 %collective-permute-start.6 = (bf16[128,1280]{1,0:T(8,128)(2,1)S(1)}, bf16[128,1280]{1,0:T(8,128)(2,1)S(1)}, u32[]{:S(2)}, u32[]{:S(2)}) collective-permute-start(bf16[128,1280]{1,0:T(8,128)(2,1)S(1)} %collective-permute-done.3.refs_1_.refs_4_), channel_id=1, source_target_pairs={{0,8},{2,10},{4,12},{6,14},{8,16},{10,18},{12,20},{14,22},{16,24},... | collective-permute-start | bytes 983048 | tf_op jit(solution)/shard_map/ppermute | solution.py:66
  18.7 9.9 %collective-permute-start.7 = (bf16[128,1280]{1,0:T(8,128)(2,1)S(1)}, bf16[128,1280]{1,0:T(8,128)(2,1)S(1)}, u32[]{:S(2)}, u32[]{:S(2)}) collective-permute-start(bf16[128,1280]{1,0:T(8,128)(2,1)S(1)} %collective-permute-done.3.refs_1_.refs_4_), channel_id=1, source_target_pairs={{0,4},{2,6},{4,0},{6,2},{8,12},{10,14},{12,8},{14,10},{16,20},{18,... | collective-permute-start | bytes 983048 | tf_op jit(solution)/shard_map/ppermute | solution.py:71
  28.7 14.0 %copy-start.9 = (bf16[128,1280]{1,0:T(8,128)(2,1)}, bf16[128,1280]{1,0:T(8,128)(2,1)S(1)}, u32[]{:S(2)}) copy-start(bf16[128,1280]{1,0:T(8,128)(2,1)S(1)} %collective-permute-done.6.refs_2_.refs_5_) | copy-start | bytes 983044
  28.7 14.0 %copy-start.10 = (bf16[128,1280]{1,0:T(8,128)(2,1)}, bf16[128,1280]{1,0:T(8,128)(2,1)S(1)}, u32[]{:S(2)}) copy-start(bf16[128,1280]{1,0:T(8,128)(2,1)S(1)} %collective-permute-done.7.refs_5_.refs_8_) | copy-start | bytes 983044
  28.7 2.7 %collective-permute-start.8 = (bf16[512,1024]{1,0:T(8,128)(2,1)S(1)}, bf16[512,1024]{1,0:T(8,128)(2,1)S(1)}, u32[]{:S(2)}, u32[]{:S(2)}) collective-permute-start(bf16[512,1024]{1,0:T(8,128)(2,1)S(1)} %collective-permute-done.5.refs_0_), channel_id=1, source_target_pairs={{0,2},{2,0},{4,6},{6,4},{8,10},{10,8},{12,14},{14,12},{16,18},{18,... | collective-permute-start | bytes 3145736 | tf_op jit(solution)/shard_map/ppermute | solution.py:61
  28.8 10.1 %collective-permute-start.10 = (bf16[128,1280]{1,0:T(8,128)(2,1)S(1)}, bf16[128,1280]{1,0:T(8,128)(2,1)S(1)}, u32[]{:S(2)}, u32[]{:S(2)}) collective-permute-start(bf16[128,1280]{1,0:T(8,128)(2,1)S(1)} %collective-permute-done.6.refs_2_.refs_5_), channel_id=1, source_target_pairs={{0,4},{2,6},{4,0},{6,2},{8,12},{10,14},{12,8},{14,10},{16,20},{18,... | collective-permute-start | bytes 983048 | tf_op jit(solution)/shard_map/ppermute | solution.py:71
  30.3 11.6 %collective-permute-start.9 = (bf16[128,1280]{1,0:T(8,128)(2,1)S(1)}, bf16[128,1280]{1,0:T(8,128)(2,1)S(1)}, u32[]{:S(2)}, u32[]{:S(2)}) collective-permute-start(bf16[128,1280]{1,0:T(8,128)(2,1)S(1)} %collective-permute-done.6.refs_2_.refs_5_), channel_id=1, source_target_pairs={{0,8},{2,10},{4,12},{6,14},{8,16},{10,18},{12,20},{14,22},{16,24},... | collective-permute-start | bytes 983048 | tf_op jit(solution)/shard_map/ppermute | solution.py:66
  35.0 10.8 %copy-start = (bf16[2048,1024]{1,0:T(8,128)(2,1)}, bf16[2048,1024]{1,0:T(8,128)(2,1)S(1)}, u32[]{:S(2)}) copy-start(bf16[2048,1024]{1,0:T(8,128)(2,1)S(1)} %place_tokens.3.x_ref.refs_1_) | copy-start | bytes 12582916
  38.9 6.9 %copy-start.5 = (bf16[128,1280]{1,0:T(8,128)(2,1)}, bf16[128,1280]{1,0:T(8,128)(2,1)S(1)}, u32[]{:S(2)}) copy-start(bf16[128,1280]{1,0:T(8,128)(2,1)S(1)} %collective-permute-done.10.refs_6_.refs_9_) | copy-start | bytes 983044
  41.9 5.5 %collective-permute-start.11 = (bf16[64,1280]{1,0:T(8,128)(2,1)S(1)}, bf16[64,1280]{1,0:T(8,128)(2,1)S(1)}, u32[]{:S(2)}, u32[]{:S(2)}) collective-permute-start(bf16[64,1280]{1,0:T(8,128)(2,1)S(1)} %slice.6), channel_id=1, source_target_pairs={{0,4},{2,6},{4,0},{6,2},{8,12},{10,14},{12,8},{14,10},{16,20},{18,... | collective-permute-start | bytes 491528 | tf_op jit(solution)/shard_map/ppermute | solution.py:71
  42.5 7.2 %copy-start.15 = (f32[1,8,16]{2,1,0:T(8,128)S(1)}, f32[1,8,16]{2,1,0:T(8,128)}, u32[]{:S(2)}) copy-start(f32[1,8,16]{2,1,0:T(8,128)} %param.11) | copy-start | bytes 1540
  42.5 7.2 %collective-permute-start.12 = (bf16[64,1280]{1,0:T(8,128)(2,1)S(1)}, bf16[64,1280]{1,0:T(8,128)(2,1)S(1)}, u32[]{:S(2)}, u32[]{:S(2)}) collective-permute-start(bf16[64,1280]{1,0:T(8,128)(2,1)S(1)} %slice.7), channel_id=1, source_target_pairs={{0,8},{2,10},{4,12},{6,14},{8,16},{10,18},{12,20},{14,22},{16,24},... | collective-permute-start | bytes 491528 | tf_op jit(solution)/shard_map/ppermute | solution.py:66
  47.4 6.9 %copy-start.13 = (bf16[64,1280]{1,0:T(8,128)(2,1)}, bf16[64,1280]{1,0:T(8,128)(2,1)S(1)}, u32[]{:S(2)}) copy-start(bf16[64,1280]{1,0:T(8,128)(2,1)S(1)} %collective-permute-done.11.refs_5_.refs_10_) | copy-start | bytes 491524
  49.7 4.6 %copy-start.14 = (bf16[64,1280]{1,0:T(8,128)(2,1)}, bf16[64,1280]{1,0:T(8,128)(2,1)S(1)}, u32[]{:S(2)}) copy-start(bf16[64,1280]{1,0:T(8,128)(2,1)S(1)} %collective-permute-done.12.refs_6_.refs_11_) | copy-start | bytes 491524
  49.7 8.4 %copy-start.19 = (s32[16,4]{0,1:T(4,128)S(1)}, s32[16,4]{0,1:T(4,128)}, u32[]{:S(2)}) copy-start(s32[16,4]{0,1:T(4,128)} %param.10) | copy-start | bytes 772
  54.4 4.4 %copy-start.17 = (bf16[2,2048,128]{2,1,0:T(8,128)(2,1)}, bf16[2,2048,128]{2,1,0:T(8,128)(2,1)S(1)}, u32[]{:S(2)}) copy-start(bf16[2,2048,128]{2,1,0:T(8,128)(2,1)S(1)} %get-tuple-element.53.refs_2_) | copy-start | bytes 3145732
  54.4 17.0 %all-to-all-start = ((bf16[8,272,128]{2,1,0:T(8,128)(2,1)}), bf16[8,272,128]{2,1,0:T(8,128)(2,1)S(1)}, u32[]{:S(2)}, u32[]{:S(2)}) async-start(bf16[8,272,128]{2,1,0:T(8,128)(2,1)} %get-tuple-element.52), calls=%async_computation | async-start | bytes 1114112 | tf_op jit(solution)/shard_map/all_to_all | solution.py:797
  72.4 17.6 %all-to-all-start.1 = ((bf16[8,256,128]{2,1,0:T(8,128)(2,1)}), bf16[8,256,128]{2,1,0:T(8,128)(2,1)S(1)}, u32[]{:S(2)}, u32[]{:S(2)}) async-start(bf16[8,256,128]{2,1,0:T(8,128)(2,1)} %scan_states.1), calls=%async_computation.1 | async-start | bytes 1048576 | tf_op jit(solution)/shard_map/all_to_all | solution.py:797
  90.7 7.7 %copy-start.1 = (bf16[1024,1024]{1,0:T(8,128)(2,1)S(1)}, bf16[1024,1024]{1,0:T(8,128)(2,1)}, u32[]{:S(2)}) copy-start(bf16[1024,1024]{1,0:T(8,128)(2,1)} %w_ref.3) | copy-start | bytes 6291460
  96.5 1.9 %collective-permute-start.15 = (bf16[512,256]{1,0:T(8,128)(2,1)}, bf16[512,256]{1,0:T(8,128)(2,1)S(1)}, u32[]{:S(2)}, u32[]{:S(2)}) collective-permute-start(bf16[512,256]{1,0:T(8,128)(2,1)} %get-tuple-element.66), channel_id=1, source_target_pairs={{0,2},{2,0},{4,6},{6,4},{8,10},{10,8},{12,14},{14,12},{16,18},{18,... | collective-permute-start | bytes 786440 | tf_op jit(solution)/shard_map/ppermute | solution.py:61
  96.5 9.4 %collective-permute-start.13 = (bf16[512,256]{1,0:T(8,128)(2,1)}, bf16[512,256]{1,0:T(8,128)(2,1)S(1)}, u32[]{:S(2)}, u32[]{:S(2)}) collective-permute-start(bf16[512,256]{1,0:T(8,128)(2,1)} %get-tuple-element.63), channel_id=1, source_target_pairs={{0,1},{1,0},{2,3},{3,2},{4,5},{5,4},{6,7},{7,6},{8,9},{9,8},{10,11... | collective-permute-start | bytes 786440 | tf_op jit(solution)/shard_map/ppermute | solution.py:95
  97.9 12.7 %collective-permute-start.14 = (bf16[512,256]{1,0:T(8,128)(2,1)}, bf16[512,256]{1,0:T(8,128)(2,1)S(1)}, u32[]{:S(2)}, u32[]{:S(2)}) collective-permute-start(bf16[512,256]{1,0:T(8,128)(2,1)} %get-tuple-element.64), channel_id=1, source_target_pairs={{0,3},{1,2},{2,1},{3,0},{4,7},{5,6},{6,5},{7,4},{8,11},{9,10},{10,... | collective-permute-start | bytes 786440 | tf_op jit(solution)/shard_map/ppermute | solution.py:103
  (6 other events, 8.7 us)

commit v13 on v12

--- a/solution.py
+++ b/solution.py
@@ -145,39 +145,41 @@
 
 
 def reorder_kernel(plan, *refs):
-    w_refs, out_ref = refs[:-1], refs[-1]
-    rows = w_refs[0].shape[0]
+    w_ref, out_ref = refs[0], refs[-1]
+    rows = w_ref.shape[0]
     width = plan.heads * PIECES * HD
     first = plan.core() == 0
 
-    def chosen(ref, at):
-        one = ref[:, at : at + HD]
+    def chosen(at):
+        one = w_ref[:, at : at + HD]
         if plan.merge == 1:
             return one
-        return jnp.where(first, one, ref[:, width + at : width + at + HD])
+        return jnp.where(first, one, w_ref[:, width + at : width + at + HD])
 
     order = [(p, i) for i in EARLY for p in range(plan.pairs)]
     order += [(p, i) for p in range(plan.pairs) for i in LATE]
     for n, (p, i) in enumerate(order):
-        blocks = []
-        for ref in w_refs:
-            one, two = (chosen(ref, ((2 * p + h) * PIECES + i) * HD) for h in range(2))
-            blocks.append(jnp.concatenate([one, two], axis=1))
-        for s, block in enumerate(blocks):
-            if plan.merge == 2:
-                block = jnp.where(first, block, blocks[1 - s])
-            out_ref[s * rows : (s + 1) * rows, n * LANES : (n + 1) * LANES] = block
-
-
-def reorder(plan, weights):
-    rows = weights[0].shape[0]
+        block = jnp.concatenate(
+            [chosen(((2 * p + h) * PIECES + i) * HD) for h in range(2)], axis=1
+        )
+        cols = slice(n * LANES, (n + 1) * LANES)
+        if len(refs) == 2:
+            out_ref[:, cols] = block
+        else:
+            mine = refs[1][:, cols]
+            out_ref[:rows, cols] = jnp.where(first, mine, block)
+            out_ref[rows:, cols] = jnp.where(first, block, mine)
+
+
+def reorder(plan, w, mine=()):
+    rows = w.shape[0] * (1 + len(mine))
     return pl.pallas_call(
         functools.partial(reorder_kernel, plan),
-        out_shape=jax.ShapeDtypeStruct((plan.merge * rows, plan.heads * PIECES * HD), bf16),
+        out_shape=jax.ShapeDtypeStruct((rows, plan.heads * PIECES * HD), bf16),
         compiler_params=params(),
-        cost_estimate=cost(0, 4 * weights[0].size),
+        cost_estimate=cost(0, 4 * rows),
         name="reorder",
-    )(*weights)
+    )(w, *mine)
 
 
 def normalise(part, out, at):
@@ -236,7 +238,7 @@
         turn_kernel,
         out_shape=jax.ShapeDtypeStruct((rank.shape[1], LANES), f32),
         compiler_params=params(),
-        cost_estimate=cost(0, 4 * LANES),
+        cost_estimate=cost(2e10, 4 * LANES),
         name="turn_places",
     )(rank)
 
@@ -247,16 +249,15 @@
 
 
 def place_kernel(merge, parts, start, rank_ref, *refs):
-    frame_refs, refs = refs[: merge * parts], refs[merge * parts :]
+    frame_refs, refs = refs[:parts], refs[parts:]
     base_refs, (x_ref, normed) = refs[:-2], refs[-2:]
     tokens = rank_ref.shape[1]
     count = normed.shape[1]
     step = 256
-    for s in range(merge):
-        at = 0
-        for ref in frame_refs[s * parts : (s + 1) * parts]:
-            normalise(ref, normed.at[s], at)
-            at += ref.shape[0]
+    at = 0
+    for ref in frame_refs:
+        normalise(ref, normed.at[at // count], at % count)
+        at += ref.shape[0]
     for at in range(0, tokens, step):
         pick = picks(rank_ref[:, start : start + count], at, step)
         for s in range(merge):
@@ -270,10 +271,9 @@
 def place_tokens(plan, rank, start, frames, base):
     tokens = rank.shape[1]
     width = frames[0].shape[1]
-    parts = len(frames) // plan.merge
-    count = parts * frames[0].shape[0]
-    return pl.pallas_call(
-        functools.partial(place_kernel, plan.merge, parts, start),
+    count = sum(f.shape[0] for f in frames) // plan.merge
+    return pl.pallas_call(
+        functools.partial(place_kernel, plan.merge, len(frames), start),
         out_shape=jax.ShapeDtypeStruct((plan.merge * tokens, width), bf16),
         scratch_shapes=[pltpu.VMEM((plan.merge, count, width), bf16)],
         compiler_params=params(),
@@ -583,7 +583,7 @@
             jax.ShapeDtypeStruct((tokens, cols), f32),
             jax.ShapeDtypeStruct((tokens, cols), bf16),
         ),
-        compiler_params=params(60),
+        compiler_params=params(60 + 3 * slot),
         cost_estimate=cost(
             6 * tokens * width * 3 * cols,
             4 * (tokens * width + 5 * width * cols + local.size),
@@ -751,7 +751,9 @@
     arriving = [plan.to_peer(own, plan.peers - k, False) for k in range(1, plan.peers)]
     owns = [own] + [plan.swap(own)] * (plan.merge - 1)
     rates = [decays[0]] + [plan.swap(decays[0])] * (plan.merge - 1)
-    block = reorder(plan, [in_weight] + [plan.swap(in_weight)] * (plan.merge - 1))
+    block = reorder(plan, in_weight)
+    if plan.merge == 2:
+        block = reorder(plan, plan.swap(in_weight), [block])
     ids = jnp.roll(block_ids, -me * local_tokens)
     ids, rates = lax.optimization_barrier((ids, rates))
     rank = rank_tokens(ids, groups)
@@ -769,13 +771,17 @@
             if k == min(1, plan.along - 2):
                 rank, owns, _ = lax.optimization_barrier((rank, owns, blocks[-1]))
                 part = with_ = place_tokens(plan, rank, 0, owns, [])
-                places = turn_places(rank)
             if k == plan.along - 2:
                 arriving, _ = lax.optimization_barrier((arriving, blocks[-1]))
-                x = with_ = fill(arriving, part)
+                x = fill(arriving, part)
             passed, across, with_ = lax.optimization_barrier(
                 (plan.round(blocks[-1]), plan.cross(blocks[-1]), with_)
             )
+            if k == plan.along - 2:
+                rank, passed, across = lax.optimization_barrier((rank, passed, across))
+                places, passed, across = lax.optimization_barrier(
+                    (turn_places(rank), passed, across)
+                )
             blocks.append(passed)
             crossed.append(across)
         last = [plan.cross(blocks[-1][:half]), plan.round(crossed[-1][half:])]

time: 113 us -> 111 us (0.982)
  waiting for transfers between devices: 42.1 us -> 37.4 us
  starting transfers between devices: 20.4 us -> 22.8 us
    ppermute x5, waiting for transfers between devices: 3.31 us -> 0.62 us  [swap(): return lax.ppermute(block, 'tm', [(t, t ^ 1) for t in range(self.frames)])]
    ppermute x4, waiting for transfers between devices: 16 us -> 13.5 us  [round(): return lax.ppermute(block, 'tm', pairs)]
    all_to_all x2, starting transfers between devices: 7.38 us -> 9.06 us  [exchange(): lax.all_to_all(blocks, 'tm', split_axis=0, concat_axis=0, tiled=True, axi...]
    ppermute x4, waiting for transfers between devices: 5.53 us -> 7.05 us  [cross(): return lax.ppermute(block, 'tm', pairs)]
    unnamed x41 -> x43, local copies, waits for them, and re-layouts: 5.51 us -> 5.65 us
  transfers between devices with their start and end apart: 18 -> 18, of which waited for: 13 -> 10; matrix products, arithmetic and copies ran while one was open for 1% -> 1% of each run, Pallas kernels for 27% -> 27%
where the time goes in v13:
time: 111 us
  Pallas kernels  43.4 us (39%)
  waiting for transfers between devices  37.4 us (34%)
  starting transfers between devices  22.8 us (21%)
  local copies, waits for them, and re-layouts  5.67 us (5%)
    pallas_call x2, Pallas kernels, attend(): pl.pallas_call(functools.partial(attend_kernel, plan, slot), in_specs=[sm...  18.3 us
    ppermute x4, waiting for transfers between devices, round(): return lax.ppermute(block, 'tm', pairs)  13.5 us
    all_to_all x2, starting transfers between devices, exchange(): lax.all_to_all(blocks, 'tm', split_axis=0, concat_axis=0, tiled=True, axi...  9.06 us
    ppermute x4, waiting for transfers between devices, cross(): return lax.ppermute(block, 'tm', pairs)  7.05 us
    pallas_call x2, Pallas kernels, place_tokens(): pl.pallas_call(functools.partial(place_kernel, plan.merge, len(frames), s...  7.03 us
    all_to_all x2, waiting for transfers between devices, exchange(): lax.all_to_all(blocks, 'tm', split_axis=0, concat_axis=0, tiled=True, axi...  6.14 us
    pallas_call x1, Pallas kernels, mix(): pl.pallas_call(functools.partial(mix_kernel, plan, groups), in_specs=[sme...  5.69 us
    unnamed x43, local copies, waits for them, and re-layouts  5.65 us
  transfers between devices with their start and end apart: 18, of which 10 were waited for; matrix products, arithmetic and copies ran while one was open for 1% of the time, Pallas kernels for 27%

profile of v13, /device:TPU:0, one launch (start us, length us, event | category | flops | bytes accessed | tf_op | source)
XLA Modules:
  0.0 110.5 jit_solution(4670826069210762951)
XLA Ops:
  0.5 3.0 %collective-permute-start.5 = (bf16[512,1024]{1,0:T(8,128)(2,1)}, bf16[512,1024]{1,0:T(8,128)(2,1)S(1)}, u32[]{:S(2)}, u32[]{:S(2)}) collective-permute-start(bf16[512,1024]{1,0:T(8,128)(2,1)} %bitcast.6), channel_id=1, source_target_pairs={{0,1},{1,0},{2,3},{3,2},{4,5},{5,4},{6,7},{7,6},{8,9},{9,8},{10,11... | collective-permute-start | bytes 3145736 | tf_op jit(solution)/shard_map/ppermute | solution.py:95
  3.5 1.0 copy-done.12
  4.7 1.8 %collective-permute-start.3 = (bf16[128,1280]{1,0:T(8,128)(2,1)S(1)}, bf16[128,1280]{1,0:T(8,128)(2,1)S(1)}, u32[]{:S(2)}, u32[]{:S(2)}) collective-permute-start(bf16[128,1280]{1,0:T(8,128)(2,1)S(1)} %reorder.3.refs_0_.refs_3_), channel_id=1, source_target_pairs={{0,8},{2,10},{4,12},{6,14},{8,16},{10,18},{12,20},{14,22},{16,24},... | collective-permute-start | bytes 983048 | tf_op jit(solution)/shard_map/ppermute | solution.py:66
  6.5 1.5 %collective-permute-start.4 = (bf16[128,1280]{1,0:T(8,128)(2,1)S(1)}, bf16[128,1280]{1,0:T(8,128)(2,1)S(1)}, u32[]{:S(2)}, u32[]{:S(2)}) collective-permute-start(bf16[128,1280]{1,0:T(8,128)(2,1)S(1)} %reorder.3.refs_0_.refs_3_), channel_id=1, source_target_pairs={{0,4},{2,6},{4,0},{6,2},{8,12},{10,14},{12,8},{14,10},{16,20},{18,... | collective-permute-start | bytes 983048 | tf_op jit(solution)/shard_map/ppermute | solution.py:71
  9.7 6.8 %collective-permute-done.3.refs_1_.refs_4_ = bf16[128,1280]{1,0:T(8,128)(2,1)S(1)} collective-permute-done((bf16[128,1280]{1,0:T(8,128)(2,1)S(1)}, bf16[128,1280]{1,0:T(8,128)(2,1)S(1)}, u32[]{:S(2)}, u32[]{:S(2)}) %collective-permute-start.3) | collective-permute-done | bytes 327712 | tf_op jit(solution)/shard_map/ppermute | solution.py:66
  16.6 1.0 collective-permute-start.6
  17.6 1.5 %collective-permute-start.7 = (bf16[128,1280]{1,0:T(8,128)(2,1)S(1)}, bf16[128,1280]{1,0:T(8,128)(2,1)S(1)}, u32[]{:S(2)}, u32[]{:S(2)}) collective-permute-start(bf16[128,1280]{1,0:T(8,128)(2,1)S(1)} %collective-permute-done.3.refs_1_.refs_4_), channel_id=1, source_target_pairs={{0,4},{2,6},{4,0},{6,2},{8,12},{10,14},{12,8},{14,10},{16,20},{18,... | collective-permute-start | bytes 983048 | tf_op jit(solution)/shard_map/ppermute | solution.py:71
  19.1 1.2 %copy-done.3 = bf16[1,512,1024]{2,1,0:T(8,128)(2,1)S(1)} copy-done((bf16[1,512,1024]{2,1,0:T(8,128)(2,1)S(1)}, bf16[1,512,1024]{2,1,0:T(8,128)(2,1)}, u32[]{:S(2)}) %copy-start.3) | copy-done | bytes 1048600
  20.3 3.5 %place_tokens.2.refs_2_ = bf16[2048,1024]{1,0:T(8,128)(2,1)S(1)} custom-call(f32[1,1024]{1,0:T(1,128)S(1)} %rank_tokens.1.rank_ref.row_ref, bf16[512,1024]{1,0:T(8,128)(2,1)S(1)} %bitcast.7, bf16[512,1024]{1,0:T(8,128)(2,1)S(1)} %collective-permute-done.1.refs_1_), custom_call_target="tpu_custom_call" | custom-call | bytes 4096 | tf_op jit(solution)/shard_map/place_tokens/pallas_call | solution.py:275
  23.8 3.8 %collective-permute-done.6.refs_2_.refs_5_ = bf16[128,1280]{1,0:T(8,128)(2,1)S(1)} collective-permute-done((bf16[128,1280]{1,0:T(8,128)(2,1)S(1)}, bf16[128,1280]{1,0:T(8,128)(2,1)S(1)}, u32[]{:S(2)}, u32[]{:S(2)}) %collective-permute-start.6) | collective-permute-done | bytes 327712 | tf_op jit(solution)/shard_map/ppermute | solution.py:66
  27.7 1.3 %collective-permute-start.10 = (bf16[128,1280]{1,0:T(8,128)(2,1)S(1)}, bf16[128,1280]{1,0:T(8,128)(2,1)S(1)}, u32[]{:S(2)}, u32[]{:S(2)}) collective-permute-start(bf16[128,1280]{1,0:T(8,128)(2,1)S(1)} %collective-permute-done.6.refs_2_.refs_5_), channel_id=1, source_target_pairs={{0,4},{2,6},{4,0},{6,2},{8,12},{10,14},{12,8},{14,10},{16,20},{18,... | collective-permute-start | bytes 983048 | tf_op jit(solution)/shard_map/ppermute | solution.py:71
  29.0 7.0 %collective-permute-done.10.refs_6_.refs_9_ = bf16[128,1280]{1,0:T(8,128)(2,1)S(1)} collective-permute-done((bf16[128,1280]{1,0:T(8,128)(2,1)S(1)}, bf16[128,1280]{1,0:T(8,128)(2,1)S(1)}, u32[]{:S(2)}, u32[]{:S(2)}) %collective-permute-start.10) | collective-permute-done | bytes 327712 | tf_op jit(solution)/shard_map/ppermute | solution.py:71
  36.0 2.5 %collective-permute-done.9.refs_3_.refs_6_ = bf16[128,1280]{1,0:T(8,128)(2,1)S(1)} collective-permute-done((bf16[128,1280]{1,0:T(8,128)(2,1)S(1)}, bf16[128,1280]{1,0:T(8,128)(2,1)S(1)}, u32[]{:S(2)}, u32[]{:S(2)}) %collective-permute-start.9) | collective-permute-done | bytes 327712 | tf_op jit(solution)/shard_map/ppermute | solution.py:66
  38.8 1.1 collective-permute-start.11
  40.0 3.6 %place_tokens.3.x_ref.refs_1_ = bf16[2048,1024]{1,0:T(8,128)(2,1)S(1)} custom-call(f32[1,1024]{1,0:T(1,128)S(1)} %rank_tokens.1.rank_ref.row_ref, bf16[512,1024]{1,0:T(8,128)(2,1)S(1)} %collective-permute-done.5.refs_0_, bf16[512,1024]{1,0:T(8,128)(2,1)S(1)} %collective-permute-done.8.refs_1_, bf16[2048,1024]{1,0:T(8,128)(2,1)S(1)} %place_tokens.2.refs_2_), custom_call_target="tpu_custom_call" | custom-call | bytes 4096 | tf_op jit(solution)/shard_map/place_tokens/pallas_call | solution.py:275
  43.7 3.1 %project.1 = (f32[2048,256]{1,0:T(8,128)S(1)}, f32[256,2048]{1,0:T(8,128)S(1)}, bf16[2048,128]{1,0:T(8,128)(2,1)S(1)}) custom-call(bf16[2048,1024]{1,0:T(8,128)(2,1)S(1)} %place_tokens.3.x_ref.refs_1_, bf16[128,1280]{1,0:T(8,128)(2,1)S(1)} %reorder.3.refs_0_.refs_3_, bf16[128,1280]{1,0:T(8,128)(2,1)S(1)} %collective-permute-done.3.refs_1_.refs_4_, ...), custom_call_target="tpu_custom_call" | custom-call | bytes 4096 | tf_op jit(solution)/shard_map/project/pallas_call | solution.py:322
  47.1 4.6 %block_updates.1 = (bf16[2,2048,128]{2,1,0:T(8,128)(2,1)S(1)}, bf16[8,272,128]{2,1,0:T(8,128)(2,1)}) custom-call(f32[8,16]{1,0:T(8,128)S(1)} %bitcast.11, f32[8,16]{1,0:T(8,128)S(1)} %collective-permute-done.refs_1_, f32[2048,256]{1,0:T(8,128)S(1)} %get-tuple-element.60.refs_2_, f32[256,2048]{1,0:T(8,128)S(1)} %get-tuple-element.61.refs_3_, ...), custom_call_target="tpu_custom_call" | custom-call | flops 1073741824 | bytes 3145728 | tf_op jit(solution)/shard_map/block_updates/pallas_call | solution.py:422
  51.7 1.0 copy-done.18
  52.7 5.3 %all-to-all-start = ((bf16[8,272,128]{2,1,0:T(8,128)(2,1)}), bf16[8,272,128]{2,1,0:T(8,128)(2,1)S(1)}, u32[]{:S(2)}, u32[]{:S(2)}) async-start(bf16[8,272,128]{2,1,0:T(8,128)(2,1)} %get-tuple-element.63), calls=%async_computation | async-start | bytes 1114112 | tf_op jit(solution)/shard_map/all_to_all | solution.py:803
  58.7 9.1 %attend.2 = (f32[1024,256]{1,0:T(8,128)}, bf16[1024,256]{1,0:T(8,128)(2,1)}) custom-call(s32[16,4]{1,0:T(8,128)} %copy.7.refs_0_, bf16[2048,1024]{1,0:T(8,128)(2,1)} %copy-done, bf16[2,2048,128]{2,1,0:T(8,128)(2,1)} %copy-done.18, bf16[128,1280]{1,0:T(8,128)(2,1)} %copy-done.2, bf16[128,1280]{1,0:T(8,128)(2,1)} %copy-done.7, bf16[128,1280]{1,0:T(8,128)(2,1)} %copy-done.10, ...), custom_call_target="tpu_custom_call" | custom-call | flops 4831838208 | bytes 11534336 | tf_op jit(solution)/shard_map/attend/pallas_call | solution.py:566
  67.8 2.2 %all-to-all-done.u_ref = bf16[8,272,128]{2,1,0:T(8,128)(2,1)S(1)} async-done(((bf16[8,272,128]{2,1,0:T(8,128)(2,1)}), bf16[8,272,128]{2,1,0:T(8,128)(2,1)S(1)}, u32[]{:S(2)}, u32[]{:S(2)}) %all-to-all-start) | async-done | bytes 557088 | tf_op jit(solution)/shard_map/all_to_all | solution.py:803
  70.0 1.0 scan_states.1
  71.0 3.8 %all-to-all-start.1 = ((bf16[8,256,128]{2,1,0:T(8,128)(2,1)}), bf16[8,256,128]{2,1,0:T(8,128)(2,1)S(1)}, u32[]{:S(2)}, u32[]{:S(2)}) async-start(bf16[8,256,128]{2,1,0:T(8,128)(2,1)} %scan_states.1), calls=%async_computation.1 | async-start | bytes 1048576 | tf_op jit(solution)/shard_map/all_to_all | solution.py:803
  74.8 9.1 %attend.3 = (f32[1024,256]{1,0:T(8,128)}, bf16[1024,256]{1,0:T(8,128)(2,1)}) custom-call(s32[16,4]{1,0:T(8,128)} %copy.7.refs_0_, bf16[2048,1024]{1,0:T(8,128)(2,1)} %copy-done, bf16[2,2048,128]{2,1,0:T(8,128)(2,1)} %copy-done.18, bf16[128,1280]{1,0:T(8,128)(2,1)} %copy-done.2, bf16[128,1280]{1,0:T(8,128)(2,1)} %copy-done.7, bf16[128,1280]{1,0:T(8,128)(2,1)} %copy-done.10, ...), custom_call_target="tpu_custom_call" | custom-call | flops 4831838208 | bytes 11534336 | tf_op jit(solution)/shard_map/attend/pallas_call | solution.py:566
  83.9 3.9 %all-to-all-done.1 = bf16[8,256,128]{2,1,0:T(8,128)(2,1)S(1)} async-done(((bf16[8,256,128]{2,1,0:T(8,128)(2,1)}), bf16[8,256,128]{2,1,0:T(8,128)(2,1)S(1)}, u32[]{:S(2)}, u32[]{:S(2)}) %all-to-all-start.1) | async-done | bytes 524320 | tf_op jit(solution)/shard_map/all_to_all | solution.py:803
  88.6 5.7 %mix.1 = (bf16[512,256]{1,0:T(8,128)(2,1)}, bf16[512,256]{1,0:T(8,128)(2,1)}, bf16[512,256]{1,0:T(8,128)(2,1)}, bf16[512,256]{1,0:T(8,128)(2,1)}) custom-call(f32[8,16]{1,0:T(8,128)} %bitcast.10, f32[8,16]{1,0:T(8,128)} %copy-done.17, f32[1024,256]{1,0:T(8,128)} %get-tuple-element.67.refs_2_, f32[1024,256]{1,0:T(8,128)} %get-tuple-element.70.refs_3_, ...), custom_call_target="tpu_custom_call" | custom-call | flops 1073741824 | bytes 6291456 | tf_op jit(solution)/shard_map/mix/pallas_call | solution.py:683
  94.4 1.6 %collective-permute-start.13 = (bf16[512,256]{1,0:T(8,128)(2,1)}, bf16[512,256]{1,0:T(8,128)(2,1)S(1)}, u32[]{:S(2)}, u32[]{:S(2)}) collective-permute-start(bf16[512,256]{1,0:T(8,128)(2,1)} %get-tuple-element.75), channel_id=1, source_target_pairs={{0,1},{1,0},{2,3},{3,2},{4,5},{5,4},{6,7},{7,6},{8,9},{9,8},{10,11... | collective-permute-start | bytes 786440 | tf_op jit(solution)/shard_map/ppermute | solution.py:95
  96.3 0.9 copy-done.13
  97.2 1.2 %project_out.2.refs_2_ = f32[512,1024]{1,0:T(8,128)S(1)} custom-call(bf16[1024,1024]{1,0:T(8,128)(2,1)S(1)} %copy-done.1, bf16[512,256]{1,0:T(8,128)(2,1)S(1)} %copy-done.13, bf16[512,256]{1,0:T(8,128)(2,1)S(1)} %collective-permute-done.15.refs_1_), custom_call_target="tpu_custom_call" | custom-call | bytes 2048 | tf_op jit(solution)/shard_map/project_out/pallas_call | solution.py:731
  98.4 5.4 %collective-permute-done.13.refs_0_ = bf16[512,256]{1,0:T(8,128)(2,1)S(1)} collective-permute-done((bf16[512,256]{1,0:T(8,128)(2,1)}, bf16[512,256]{1,0:T(8,128)(2,1)S(1)}, u32[]{:S(2)}, u32[]{:S(2)}) %collective-permute-start.13) | collective-permute-done | bytes 262176 | tf_op jit(solution)/shard_map/ppermute | solution.py:95
  103.8 4.7 %collective-permute-done.14.refs_1_ = bf16[512,256]{1,0:T(8,128)(2,1)S(1)} collective-permute-done((bf16[512,256]{1,0:T(8,128)(2,1)}, bf16[512,256]{1,0:T(8,128)(2,1)S(1)}, u32[]{:S(2)}, u32[]{:S(2)}) %collective-permute-start.14) | collective-permute-done | bytes 262176 | tf_op jit(solution)/shard_map/ppermute | solution.py:103
  108.5 1.9 %project_out.3 = bf16[512,1024]{1,0:T(8,128)(2,1)} custom-call(bf16[1024,1024]{1,0:T(8,128)(2,1)S(1)} %copy-done.1, bf16[512,256]{1,0:T(8,128)(2,1)S(1)} %collective-permute-done.13.refs_0_, bf16[512,256]{1,0:T(8,128)(2,1)S(1)} %collective-permute-done.14.refs_1_, f32[512,1024]{1,0:T(8,128)S(1)} %project_out.2.refs_2_), custom_call_target="tpu_custom_call" | custom-call | bytes 2048 | tf_op jit(solution)/shard_map/project_out/pallas_call | solution.py:731
  (64 shorter events, 4.9 us)
Async XLA Ops:
  0.0 19.1 %collective-permute-start.1 = (bf16[512,1024]{1,0:T(8,128)(2,1)}, bf16[512,1024]{1,0:T(8,128)(2,1)S(1)}, u32[]{:S(2)}, u32[]{:S(2)}) collective-permute-start(bf16[512,1024]{1,0:T(8,128)(2,1)} %bitcast.5), channel_id=1, source_target_pairs={{0,2},{2,0},{4,6},{6,4},{8,10},{10,8},{12,14},{14,12},{16,18},{18,... | collective-permute-start | bytes 3145736 | tf_op jit(solution)/shard_map/ppermute | solution.py:61
  0.5 4.1 %collective-permute-start.2 = (bf16[64,2560]{1,0:T(8,128)(2,1)}, bf16[64,2560]{1,0:T(8,128)(2,1)S(1)}, u32[]{:S(2)}, u32[]{:S(2)}) collective-permute-start(bf16[64,2560]{1,0:T(8,128)(2,1)} %refs_0_.3), channel_id=1, source_target_pairs={{0,2},{2,0},{4,6},{6,4},{8,10},{10,8},{12,14},{14,12},{16,18},{18,... | collective-permute-start | bytes 983048 | tf_op jit(solution)/shard_map/ppermute | solution.py:61
  0.5 28.5 %collective-permute-start.5 = (bf16[512,1024]{1,0:T(8,128)(2,1)}, bf16[512,1024]{1,0:T(8,128)(2,1)S(1)}, u32[]{:S(2)}, u32[]{:S(2)}) collective-permute-start(bf16[512,1024]{1,0:T(8,128)(2,1)} %bitcast.6), channel_id=1, source_target_pairs={{0,1},{1,0},{2,3},{3,2},{4,5},{5,4},{6,7},{7,6},{8,9},{9,8},{10,11... | collective-permute-start | bytes 3145736 | tf_op jit(solution)/shard_map/ppermute | solution.py:95
  4.7 38.9 %copy-start.2 = (bf16[128,1280]{1,0:T(8,128)(2,1)}, bf16[128,1280]{1,0:T(8,128)(2,1)S(1)}, u32[]{:S(2)}) copy-start(bf16[128,1280]{1,0:T(8,128)(2,1)S(1)} %reorder.3.refs_0_.refs_3_) | copy-start | bytes 983044
  4.7 11.9 %collective-permute-start.3 = (bf16[128,1280]{1,0:T(8,128)(2,1)S(1)}, bf16[128,1280]{1,0:T(8,128)(2,1)S(1)}, u32[]{:S(2)}, u32[]{:S(2)}) collective-permute-start(bf16[128,1280]{1,0:T(8,128)(2,1)S(1)} %reorder.3.refs_0_.refs_3_), channel_id=1, source_target_pairs={{0,8},{2,10},{4,12},{6,14},{8,16},{10,18},{12,20},{14,22},{16,24},... | collective-permute-start | bytes 983048 | tf_op jit(solution)/shard_map/ppermute | solution.py:66
  6.5 10.0 %collective-permute-start.4 = (bf16[128,1280]{1,0:T(8,128)(2,1)S(1)}, bf16[128,1280]{1,0:T(8,128)(2,1)S(1)}, u32[]{:S(2)}, u32[]{:S(2)}) collective-permute-start(bf16[128,1280]{1,0:T(8,128)(2,1)S(1)} %reorder.3.refs_0_.refs_3_), channel_id=1, source_target_pairs={{0,4},{2,6},{4,0},{6,2},{8,12},{10,14},{12,8},{14,10},{16,20},{18,... | collective-permute-start | bytes 983048 | tf_op jit(solution)/shard_map/ppermute | solution.py:71
  8.0 1.4 %collective-permute-start = (f32[8,16]{1,0:T(8,128)}, f32[8,16]{1,0:T(8,128)S(1)}, u32[]{:S(2)}, u32[]{:S(2)}) collective-permute-start(f32[8,16]{1,0:T(8,128)} %bitcast.9), channel_id=1, source_target_pairs={{0,2},{2,0},{4,6},{6,4},{8,10},{10,8},{12,14},{14,12},{16,18},{18,... | collective-permute-start | bytes 1544 | tf_op jit(solution)/shard_map/ppermute | solution.py:61
  9.4 37.7 %copy-start.17 = (f32[8,16]{1,0:T(8,128)}, f32[8,16]{1,0:T(8,128)S(1)}, u32[]{:S(2)}) copy-start(f32[8,16]{1,0:T(8,128)S(1)} %collective-permute-done.refs_1_) | copy-start | bytes 1540
  16.6 27.0 %copy-start.7 = (bf16[128,1280]{1,0:T(8,128)(2,1)}, bf16[128,1280]{1,0:T(8,128)(2,1)S(1)}, u32[]{:S(2)}) copy-start(bf16[128,1280]{1,0:T(8,128)(2,1)S(1)} %collective-permute-done.3.refs_1_.refs_4_) | copy-start | bytes 983044
  16.6 7.2 %copy-start.8 = (bf16[128,1280]{1,0:T(8,128)(2,1)}, bf16[128,1280]{1,0:T(8,128)(2,1)S(1)}, u32[]{:S(2)}) copy-start(bf16[128,1280]{1,0:T(8,128)(2,1)S(1)} %collective-permute-done.4.refs_4_.refs_7_) | copy-start | bytes 983044
  16.6 11.1 %collective-permute-start.6 = (bf16[128,1280]{1,0:T(8,128)(2,1)S(1)}, bf16[128,1280]{1,0:T(8,128)(2,1)S(1)}, u32[]{:S(2)}, u32[]{:S(2)}) collective-permute-start(bf16[128,1280]{1,0:T(8,128)(2,1)S(1)} %collective-permute-done.3.refs_1_.refs_4_), channel_id=1, source_target_pairs={{0,8},{2,10},{4,12},{6,14},{8,16},{10,18},{12,20},{14,22},{16,24},... | collective-permute-start | bytes 983048 | tf_op jit(solution)/shard_map/ppermute | solution.py:66
  17.6 10.1 %collective-permute-start.7 = (bf16[128,1280]{1,0:T(8,128)(2,1)S(1)}, bf16[128,1280]{1,0:T(8,128)(2,1)S(1)}, u32[]{:S(2)}, u32[]{:S(2)}) collective-permute-start(bf16[128,1280]{1,0:T(8,128)(2,1)S(1)} %collective-permute-done.3.refs_1_.refs_4_), channel_id=1, source_target_pairs={{0,4},{2,6},{4,0},{6,2},{8,12},{10,14},{12,8},{14,10},{16,20},{18,... | collective-permute-start | bytes 983048 | tf_op jit(solution)/shard_map/ppermute | solution.py:71
  27.7 15.9 %copy-start.10 = (bf16[128,1280]{1,0:T(8,128)(2,1)}, bf16[128,1280]{1,0:T(8,128)(2,1)S(1)}, u32[]{:S(2)}) copy-start(bf16[128,1280]{1,0:T(8,128)(2,1)S(1)} %collective-permute-done.6.refs_2_.refs_5_) | copy-start | bytes 983044
  27.7 15.9 %copy-start.11 = (bf16[128,1280]{1,0:T(8,128)(2,1)}, bf16[128,1280]{1,0:T(8,128)(2,1)S(1)}, u32[]{:S(2)}) copy-start(bf16[128,1280]{1,0:T(8,128)(2,1)S(1)} %collective-permute-done.7.refs_5_.refs_8_) | copy-start | bytes 983044
  27.7 8.4 %collective-permute-start.10 = (bf16[128,1280]{1,0:T(8,128)(2,1)S(1)}, bf16[128,1280]{1,0:T(8,128)(2,1)S(1)}, u32[]{:S(2)}, u32[]{:S(2)}) collective-permute-start(bf16[128,1280]{1,0:T(8,128)(2,1)S(1)} %collective-permute-done.6.refs_2_.refs_5_), channel_id=1, source_target_pairs={{0,4},{2,6},{4,0},{6,2},{8,12},{10,14},{12,8},{14,10},{16,20},{18,... | collective-permute-start | bytes 983048 | tf_op jit(solution)/shard_map/ppermute | solution.py:71
  29.0 9.6 %collective-permute-start.9 = (bf16[128,1280]{1,0:T(8,128)(2,1)S(1)}, bf16[128,1280]{1,0:T(8,128)(2,1)S(1)}, u32[]{:S(2)}, u32[]{:S(2)}) collective-permute-start(bf16[128,1280]{1,0:T(8,128)(2,1)S(1)} %collective-permute-done.6.refs_2_.refs_5_), channel_id=1, source_target_pairs={{0,8},{2,10},{4,12},{6,14},{8,16},{10,18},{12,20},{14,22},{16,24},... | collective-permute-start | bytes 983048 | tf_op jit(solution)/shard_map/ppermute | solution.py:66
  29.0 11.0 %collective-permute-start.8 = (bf16[512,1024]{1,0:T(8,128)(2,1)S(1)}, bf16[512,1024]{1,0:T(8,128)(2,1)S(1)}, u32[]{:S(2)}, u32[]{:S(2)}) collective-permute-start(bf16[512,1024]{1,0:T(8,128)(2,1)S(1)} %collective-permute-done.5.refs_0_), channel_id=1, source_target_pairs={{0,2},{2,0},{4,6},{6,4},{8,10},{10,8},{12,14},{14,12},{16,18},{18,... | collective-permute-start | bytes 3145736 | tf_op jit(solution)/shard_map/ppermute | solution.py:61
  36.0 7.6 %copy-start.4 = (bf16[128,1280]{1,0:T(8,128)(2,1)}, bf16[128,1280]{1,0:T(8,128)(2,1)S(1)}, u32[]{:S(2)}) copy-start(bf16[128,1280]{1,0:T(8,128)(2,1)S(1)} %collective-permute-done.10.refs_6_.refs_9_) | copy-start | bytes 983044
  38.6 5.0 %copy-start.5 = (bf16[128,1280]{1,0:T(8,128)(2,1)}, bf16[128,1280]{1,0:T(8,128)(2,1)S(1)}, u32[]{:S(2)}) copy-start(bf16[128,1280]{1,0:T(8,128)(2,1)S(1)} %collective-permute-done.9.refs_3_.refs_6_) | copy-start | bytes 983044
  38.8 8.0 %collective-permute-start.11 = (bf16[64,1280]{1,0:T(8,128)(2,1)S(1)}, bf16[64,1280]{1,0:T(8,128)(2,1)S(1)}, u32[]{:S(2)}, u32[]{:S(2)}) collective-permute-start(bf16[64,1280]{1,0:T(8,128)(2,1)S(1)} %slice.6), channel_id=1, source_target_pairs={{0,4},{2,6},{4,0},{6,2},{8,12},{10,14},{12,8},{14,10},{16,20},{18,... | collective-permute-start | bytes 491528 | tf_op jit(solution)/shard_map/ppermute | solution.py:71
  39.9 3.7 %copy-start.9 = (bf16[128,1280]{1,0:T(8,128)(2,1)S(1)}, bf16[128,1280]{1,0:T(8,128)(2,1)}, u32[]{:S(2)}) copy-start(bf16[128,1280]{1,0:T(8,128)(2,1)} %copy-done.8) | copy-start | bytes 983044
  39.9 7.2 %collective-permute-start.12 = (bf16[64,1280]{1,0:T(8,128)(2,1)S(1)}, bf16[64,1280]{1,0:T(8,128)(2,1)S(1)}, u32[]{:S(2)}, u32[]{:S(2)}) collective-permute-start(bf16[64,1280]{1,0:T(8,128)(2,1)S(1)} %slice.7), channel_id=1, source_target_pairs={{0,8},{2,10},{4,12},{6,14},{8,16},{10,18},{12,20},{14,22},{16,24},... | collective-permute-start | bytes 491528 | tf_op jit(solution)/shard_map/ppermute | solution.py:66
  43.6 3.4 %copy-start.16 = (f32[1,8,16]{2,1,0:T(8,128)S(1)}, f32[1,8,16]{2,1,0:T(8,128)}, u32[]{:S(2)}) copy-start(f32[1,8,16]{2,1,0:T(8,128)} %param.11) | copy-start | bytes 1540
  46.8 4.9 %copy-start.14 = (bf16[64,1280]{1,0:T(8,128)(2,1)}, bf16[64,1280]{1,0:T(8,128)(2,1)S(1)}, u32[]{:S(2)}) copy-start(bf16[64,1280]{1,0:T(8,128)(2,1)S(1)} %collective-permute-done.11.refs_5_.refs_10_) | copy-start | bytes 491524
  47.1 4.6 %copy-start.15 = (bf16[64,1280]{1,0:T(8,128)(2,1)}, bf16[64,1280]{1,0:T(8,128)(2,1)S(1)}, u32[]{:S(2)}) copy-start(bf16[64,1280]{1,0:T(8,128)(2,1)S(1)} %collective-permute-done.12.refs_6_.refs_11_) | copy-start | bytes 491524
  47.1 10.9 %copy-start.20 = (s32[16,4]{0,1:T(4,128)S(1)}, s32[16,4]{0,1:T(4,128)}, u32[]{:S(2)}) copy-start(s32[16,4]{0,1:T(4,128)} %param.10) | copy-start | bytes 772
  52.7 17.3 %all-to-all-start = ((bf16[8,272,128]{2,1,0:T(8,128)(2,1)}), bf16[8,272,128]{2,1,0:T(8,128)(2,1)S(1)}, u32[]{:S(2)}, u32[]{:S(2)}) async-start(bf16[8,272,128]{2,1,0:T(8,128)(2,1)} %get-tuple-element.63), calls=%async_computation | async-start | bytes 1114112 | tf_op jit(solution)/shard_map/all_to_all | solution.py:803
  71.0 16.8 %all-to-all-start.1 = ((bf16[8,256,128]{2,1,0:T(8,128)(2,1)}), bf16[8,256,128]{2,1,0:T(8,128)(2,1)S(1)}, u32[]{:S(2)}, u32[]{:S(2)}) async-start(bf16[8,256,128]{2,1,0:T(8,128)(2,1)} %scan_states.1), calls=%async_computation.1 | async-start | bytes 1048576 | tf_op jit(solution)/shard_map/all_to_all | solution.py:803
  88.6 7.7 %copy-start.1 = (bf16[1024,1024]{1,0:T(8,128)(2,1)S(1)}, bf16[1024,1024]{1,0:T(8,128)(2,1)}, u32[]{:S(2)}) copy-start(bf16[1024,1024]{1,0:T(8,128)(2,1)} %w_ref.3) | copy-start | bytes 6291460
  94.3 1.9 %collective-permute-start.15 = (bf16[512,256]{1,0:T(8,128)(2,1)}, bf16[512,256]{1,0:T(8,128)(2,1)S(1)}, u32[]{:S(2)}, u32[]{:S(2)}) collective-permute-start(bf16[512,256]{1,0:T(8,128)(2,1)} %get-tuple-element.78), channel_id=1, source_target_pairs={{0,2},{2,0},{4,6},{6,4},{8,10},{10,8},{12,14},{14,12},{16,18},{18,... | collective-permute-start | bytes 786440 | tf_op jit(solution)/shard_map/ppermute | solution.py:61
  94.4 9.4 %collective-permute-start.13 = (bf16[512,256]{1,0:T(8,128)(2,1)}, bf16[512,256]{1,0:T(8,128)(2,1)S(1)}, u32[]{:S(2)}, u32[]{:S(2)}) collective-permute-start(bf16[512,256]{1,0:T(8,128)(2,1)} %get-tuple-element.75), channel_id=1, source_target_pairs={{0,1},{1,0},{2,3},{3,2},{4,5},{5,4},{6,7},{7,6},{8,9},{9,8},{10,11... | collective-permute-start | bytes 786440 | tf_op jit(solution)/shard_map/ppermute | solution.py:95
  96.0 12.5 %collective-permute-start.14 = (bf16[512,256]{1,0:T(8,128)(2,1)}, bf16[512,256]{1,0:T(8,128)(2,1)S(1)}, u32[]{:S(2)}, u32[]{:S(2)}) collective-permute-start(bf16[512,256]{1,0:T(8,128)(2,1)} %get-tuple-element.76), channel_id=1, source_target_pairs={{0,3},{1,2},{2,1},{3,0},{4,7},{5,6},{6,5},{7,4},{8,11},{9,10},{10,... | collective-permute-start | bytes 786440 | tf_op jit(solution)/shard_map/ppermute | solution.py:103
  (7 other events, 9.3 us)

commit v14 on v13

--- a/solution.py
+++ b/solution.py
@@ -226,20 +226,24 @@
     )(ids.reshape(1, tokens))
 
 
-def turn_kernel(row_ref, col_ref):
-    for at in range(0, col_ref.shape[0], LANES):
-        col_ref[at : at + LANES, :] = jnp.broadcast_to(
-            row_ref[:, at : at + LANES], (LANES, LANES)
-        ).T
-
-
-def turn_places(rank):
-    return pl.pallas_call(
-        turn_kernel,
-        out_shape=jax.ShapeDtypeStruct((rank.shape[1], LANES), f32),
+def back_kernel(row_ref, back_ref):
+    tokens = back_ref.shape[0]
+    lane = lax.broadcasted_iota(jnp.int32, (LANES, LANES), 1)
+    for at in range(0, tokens, LANES):
+        place = jnp.broadcast_to(row_ref[:, at : at + LANES], (LANES, LANES)).T
+        for t in range(0, tokens, LANES):
+            back_ref[at : at + LANES, t : t + LANES] = jnp.where(
+                (lane + t).astype(f32) == place, 1.0, 0.0
+            ).astype(bf16)
+
+
+def back_tokens(rank):
+    return pl.pallas_call(
+        back_kernel,
+        out_shape=jax.ShapeDtypeStruct((rank.shape[1], rank.shape[1]), bf16),
         compiler_params=params(),
         cost_estimate=cost(2e10, 4 * LANES),
-        name="turn_places",
+        name="back_tokens",
     )(rank)
 
 
@@ -335,8 +339,8 @@
 
 def update_kernel(plan, groups, *refs):
     decay_refs, refs = refs[: plan.merge], refs[plan.merge :]
-    v_ref, b_ref, x_ref, last_refs, (left, total_out, total_ref, u, sems) = (
-        refs[0], refs[1], refs[2], refs[3:-5], refs[-5:]
+    v_ref, b_ref, x_ref, last_refs, (left_out, total_out, left, total_ref, u, sems) = (
+        refs[0], refs[1], refs[2], refs[3:-6], refs[-6:]
     )
     copies = Copies(sems)
     leaving = []
@@ -408,6 +412,9 @@
         if (d + 1) % (peers // 4) == 0:
             done = slice(d + 1 - peers // 4, d + 1)
             leaving.append(copies.start(total_ref.at[done], total_out.at[done]))
+            done = slice((d + 1 - peers // 4) * share, (d + 1) * share)
+            for s in range(plan.merge):
+                leaving.append(copies.start(left.at[s, done], left_out.at[s, done]))
     finish(leaving)
 
 
@@ -422,12 +429,13 @@
     return pl.pallas_call(
         functools.partial(update_kernel, plan, groups),
         in_specs=[smem] * plan.merge + [vmem] * (3 + len(last)),
-        out_specs=(vmem, hbm),
+        out_specs=(hbm, hbm),
         out_shape=(
             jax.ShapeDtypeStruct((plan.merge, rows, LANES), bf16),
             jax.ShapeDtypeStruct((plan.chips, share_rows(share), LANES), bf16),
         ),
         scratch_shapes=[
+            pltpu.VMEM((plan.merge, rows, LANES), bf16),
             pltpu.VMEM((plan.chips, share_rows(share), LANES), bf16),
             pltpu.VMEM((plan.merge, rows, LANES), f32),
             Copies.scratch(),
@@ -583,7 +591,7 @@
             jax.ShapeDtypeStruct((tokens, cols), f32),
             jax.ShapeDtypeStruct((tokens, cols), bf16),
         ),
-        compiler_params=params(60 + 3 * slot),
+        compiler_params=params(60),
         cost_estimate=cost(
             6 * tokens * width * 3 * cols,
             4 * (tokens * width + 5 * width * cols + local.size),
@@ -605,10 +613,10 @@
     decay_refs, refs = refs[: plan.merge], refs[plan.merge :]
     a_ins, refs = refs[: plan.merge], refs[plan.merge :]
     c_ins, refs = refs[: plan.merge], refs[plan.merge :]
-    s_in, rank_in, refs = refs[0], refs[1], refs[2:]
-    out_refs, (a, c, state, rank, mixed, out, sems) = refs[:-7], refs[-7:]
+    s_in, back_in, refs = refs[0], refs[1], refs[2:]
+    out_refs, (a, c, state, back, mixed, out, sems) = refs[:-7], refs[-7:]
     copies = Copies(sems)
-    tokens = rank.shape[0]
+    tokens = back.shape[0]
     block = tokens // groups
     width = a.shape[2]
     here = groups // 4
@@ -625,7 +633,12 @@
                 copies.start(c_ins[s].at[rows], c.at[s, rows, :]),
                 copies.start(a_ins[s].at[rows], a.at[s, rows, :]),
             ]
-    ranking = copies.start(rank_in, rank)
+    local = tokens // plan.peers
+    order = list(range(1, plan.peers)) + [0]
+    turning = []
+    for k in order:
+        rows = slice(k * local, (k + 1) * local)
+        turning.append(copies.start(back_in.at[rows], back.at[rows]))
 
     for g in range(groups):
         if g % here == 0:
@@ -646,11 +659,12 @@
                     a[s, rows, cols] + decays[s] * read[s * block : (s + 1) * block]
                 ).astype(bf16)
 
-    ranking.wait()
-    local = tokens // plan.peers
     leaving = []
-    for k in list(range(1, plan.peers)) + [0]:
-        placed = back_rows(rank, k * local, mixed, local)
+    for k, turned in zip(order, turning):
+        turned.wait()
+        placed = jnp.dot(
+            back[k * local : (k + 1) * local, :], mixed[...], preferred_element_type=f32
+        ).astype(bf16)
         for s in range(plan.merge):
             i = s * plan.peers + k
             out[i] = placed[:, s * width : (s + 1) * width]
@@ -658,26 +672,8 @@
     finish(leaving)
 
 
-def back_rows(rank, start, mixed, rows):
-    tokens = rank.shape[0]
-    step = min(256, rows)
-    placed = []
-    for at in range(start, start + rows, step):
-        place = rank[at : at + step, :]
-        lane = lax.broadcasted_iota(jnp.int32, place.shape, 1)
-        pick = jnp.concatenate(
-            [
-                jnp.where((lane + t).astype(f32) == place, 1.0, 0.0).astype(bf16)
-                for t in range(0, tokens, LANES)
-            ],
-            axis=1,
-        )
-        placed.append(jnp.dot(pick, mixed[...], preferred_element_type=f32).astype(bf16))
-    return jnp.concatenate(placed, axis=0)
-
-
-def mix(plan, decays, attended, readers, state, rank, groups):
-    tokens = rank.shape[0]
+def mix(plan, decays, attended, readers, state, back, groups):
+    tokens = back.shape[0]
     width = attended[0].shape[1]
     count = plan.merge * plan.peers
     return pl.pallas_call(
@@ -689,15 +685,15 @@
             pltpu.VMEM((plan.merge, tokens, width), f32),
             pltpu.VMEM((plan.merge, tokens, width), bf16),
             pltpu.VMEM(state.shape, bf16),
-            pltpu.VMEM(rank.shape, f32),
+            pltpu.VMEM(back.shape, bf16),
             pltpu.VMEM((tokens, plan.merge * width), bf16),
             pltpu.VMEM((count, tokens // plan.peers, width), bf16),
             Copies.scratch(),
         ],
-        compiler_params=params(60),
+        compiler_params=params(52),
         cost_estimate=cost(4 * tokens * tokens * width, 2 * tokens * tokens + 16 * tokens * width),
         name="mix",
-    )(*decays, *attended, *readers, state, rank)
+    )(*decays, *attended, *readers, state, back)
 
 
 def out_kernel(plan, sources, w_ref, *refs):
@@ -780,7 +776,7 @@
             if k == plan.along - 2:
                 rank, passed, across = lax.optimization_barrier((rank, passed, across))
                 places, passed, across = lax.optimization_barrier(
-                    (turn_places(rank), passed, across)
+                    (back_tokens(rank), passed, across)
                 )
             blocks.append(passed)
             crossed.append(across)
@@ -790,7 +786,7 @@
         weights = [
             lax.all_gather(block, "tm", axis=0, tiled=True, axis_index_groups=plan.groups())
         ]
-        places = turn_places(rank)
+        places = back_tokens(rank)
         x = fill(arriving, place_tokens(plan, rank, 0, owns, []))
     if plan.ringed:
         v, b, x_last = project(plan, x, weights[:-2])

time: 111 us -> 113 us (1.018)
  Pallas kernels: 43.4 us -> 44.8 us
    pallas_call x1, Pallas kernels: 4.61 us -> 6.07 us  [block_updates(): pl.pallas_call(functools.partial(update_kernel, plan, groups), in_specs=[...]
    unnamed x43 -> x39, local copies, waits for them, and re-layouts: 5.65 us -> 5.11 us
where the time goes in v14:
time: 113 us; the launch traced here: 112 us
  Pallas kernels  44.8 us (40%)
  waiting for transfers between devices  37.9 us (34%)
  starting transfers between devices  23 us (20%)
  local copies, waits for them, and re-layouts  5.13 us (5%)
    pallas_call x2, Pallas kernels, attend(): pl.pallas_call(functools.partial(attend_kernel, plan, slot), in_specs=[sm...  18.5 us
    ppermute x4, waiting for transfers between devices, round(): return lax.ppermute(block, 'tm', pairs)  13.5 us
    all_to_all x2, starting transfers between devices, exchange(): lax.all_to_all(blocks, 'tm', split_axis=0, concat_axis=0, tiled=True, axi...  9.08 us
    ppermute x4, waiting for transfers between devices, cross(): return lax.ppermute(block, 'tm', pairs)  7.05 us
    pallas_call x2, Pallas kernels, place_tokens(): pl.pallas_call(functools.partial(place_kernel, plan.merge, len(frames), s...  7.03 us
    ppermute x2, waiting for transfers between devices, to_peer(): return lax.ppermute(block, 'head', pairs)  6.14 us
    pallas_call x1, Pallas kernels, block_updates(): pl.pallas_call(functools.partial(update_kernel, plan, groups), in_specs=[...  6.07 us
    all_to_all x2, waiting for transfers between devices, exchange(): lax.all_to_all(blocks, 'tm', split_axis=0, concat_axis=0, tiled=True, axi...  5.91 us
  transfers between devices with their start and end apart: 18, of which 10 were waited for; matrix products, arithmetic and copies ran while one was open for 1% of the time, Pallas kernels for 27%

profile of v14, /device:TPU:0, one launch (start us, length us, event | category | flops | bytes accessed | tf_op | source)
XLA Modules:
  0.0 112.1 jit_solution(4871832343284023855)
XLA Ops:
  0.5 3.0 %collective-permute-start.5 = (bf16[512,1024]{1,0:T(8,128)(2,1)}, bf16[512,1024]{1,0:T(8,128)(2,1)S(1)}, u32[]{:S(2)}, u32[]{:S(2)}) collective-permute-start(bf16[512,1024]{1,0:T(8,128)(2,1)} %bitcast.6), channel_id=1, source_target_pairs={{0,1},{1,0},{2,3},{3,2},{4,5},{5,4},{6,7},{7,6},{8,9},{9,8},{10,11... | collective-permute-start | bytes 3145736 | tf_op jit(solution)/shard_map/ppermute | solution.py:95
  3.5 1.0 copy-done.12
  4.7 1.8 %collective-permute-start.3 = (bf16[128,1280]{1,0:T(8,128)(2,1)S(1)}, bf16[128,1280]{1,0:T(8,128)(2,1)S(1)}, u32[]{:S(2)}, u32[]{:S(2)}) collective-permute-start(bf16[128,1280]{1,0:T(8,128)(2,1)S(1)} %reorder.3.refs_0_.refs_3_), channel_id=1, source_target_pairs={{0,8},{2,10},{4,12},{6,14},{8,16},{10,18},{12,20},{14,22},{16,24},... | collective-permute-start | bytes 983048 | tf_op jit(solution)/shard_map/ppermute | solution.py:66
  6.5 1.5 %collective-permute-start.4 = (bf16[128,1280]{1,0:T(8,128)(2,1)S(1)}, bf16[128,1280]{1,0:T(8,128)(2,1)S(1)}, u32[]{:S(2)}, u32[]{:S(2)}) collective-permute-start(bf16[128,1280]{1,0:T(8,128)(2,1)S(1)} %reorder.3.refs_0_.refs_3_), channel_id=1, source_target_pairs={{0,4},{2,6},{4,0},{6,2},{8,12},{10,14},{12,8},{14,10},{16,20},{18,... | collective-permute-start | bytes 983048 | tf_op jit(solution)/shard_map/ppermute | solution.py:71
  9.7 6.8 %collective-permute-done.3.refs_1_.refs_4_ = bf16[128,1280]{1,0:T(8,128)(2,1)S(1)} collective-permute-done((bf16[128,1280]{1,0:T(8,128)(2,1)S(1)}, bf16[128,1280]{1,0:T(8,128)(2,1)S(1)}, u32[]{:S(2)}, u32[]{:S(2)}) %collective-permute-start.3) | collective-permute-done | bytes 327712 | tf_op jit(solution)/shard_map/ppermute | solution.py:66
  16.6 1.0 collective-permute-start.6
  17.6 1.5 %collective-permute-start.7 = (bf16[128,1280]{1,0:T(8,128)(2,1)S(1)}, bf16[128,1280]{1,0:T(8,128)(2,1)S(1)}, u32[]{:S(2)}, u32[]{:S(2)}) collective-permute-start(bf16[128,1280]{1,0:T(8,128)(2,1)S(1)} %collective-permute-done.3.refs_1_.refs_4_), channel_id=1, source_target_pairs={{0,4},{2,6},{4,0},{6,2},{8,12},{10,14},{12,8},{14,10},{16,20},{18,... | collective-permute-start | bytes 983048 | tf_op jit(solution)/shard_map/ppermute | solution.py:71
  19.1 1.2 %copy-done.4 = bf16[1,512,1024]{2,1,0:T(8,128)(2,1)S(1)} copy-done((bf16[1,512,1024]{2,1,0:T(8,128)(2,1)S(1)}, bf16[1,512,1024]{2,1,0:T(8,128)(2,1)}, u32[]{:S(2)}) %copy-start.4) | copy-done | bytes 1048600
  20.3 3.5 %place_tokens.2.refs_2_ = bf16[2048,1024]{1,0:T(8,128)(2,1)S(1)} custom-call(f32[1,1024]{1,0:T(1,128)S(1)} %rank_tokens.1.rank_ref.row_ref, bf16[512,1024]{1,0:T(8,128)(2,1)S(1)} %bitcast.7, bf16[512,1024]{1,0:T(8,128)(2,1)S(1)} %collective-permute-done.1.refs_1_), custom_call_target="tpu_custom_call" | custom-call | bytes 4096 | tf_op jit(solution)/shard_map/place_tokens/pallas_call | solution.py:279
  23.8 3.9 %collective-permute-done.6.refs_2_.refs_5_ = bf16[128,1280]{1,0:T(8,128)(2,1)S(1)} collective-permute-done((bf16[128,1280]{1,0:T(8,128)(2,1)S(1)}, bf16[128,1280]{1,0:T(8,128)(2,1)S(1)}, u32[]{:S(2)}, u32[]{:S(2)}) %collective-permute-start.6) | collective-permute-done | bytes 327712 | tf_op jit(solution)/shard_map/ppermute | solution.py:66
  27.7 1.3 %collective-permute-start.10 = (bf16[128,1280]{1,0:T(8,128)(2,1)S(1)}, bf16[128,1280]{1,0:T(8,128)(2,1)S(1)}, u32[]{:S(2)}, u32[]{:S(2)}) collective-permute-start(bf16[128,1280]{1,0:T(8,128)(2,1)S(1)} %collective-permute-done.6.refs_2_.refs_5_), channel_id=1, source_target_pairs={{0,4},{2,6},{4,0},{6,2},{8,12},{10,14},{12,8},{14,10},{16,20},{18,... | collective-permute-start | bytes 983048 | tf_op jit(solution)/shard_map/ppermute | solution.py:71
  29.0 7.0 %collective-permute-done.10.refs_6_.refs_9_ = bf16[128,1280]{1,0:T(8,128)(2,1)S(1)} collective-permute-done((bf16[128,1280]{1,0:T(8,128)(2,1)S(1)}, bf16[128,1280]{1,0:T(8,128)(2,1)S(1)}, u32[]{:S(2)}, u32[]{:S(2)}) %collective-permute-start.10) | collective-permute-done | bytes 327712 | tf_op jit(solution)/shard_map/ppermute | solution.py:71
  36.0 2.5 %collective-permute-done.9.refs_3_.refs_6_ = bf16[128,1280]{1,0:T(8,128)(2,1)S(1)} collective-permute-done((bf16[128,1280]{1,0:T(8,128)(2,1)S(1)}, bf16[128,1280]{1,0:T(8,128)(2,1)S(1)}, u32[]{:S(2)}, u32[]{:S(2)}) %collective-permute-start.9) | collective-permute-done | bytes 327712 | tf_op jit(solution)/shard_map/ppermute | solution.py:66
  39.1 1.4 %copy-done.2 = bf16[1024,1024]{1,0:T(8,128)(2,1)} copy-done((bf16[1024,1024]{1,0:T(8,128)(2,1)}, bf16[1024,1024]{1,0:T(8,128)(2,1)S(1)}, u32[]{:S(2)}) %copy-start.2) | copy-done | bytes 2097176
  40.5 1.1 collective-permute-start.11
  41.8 3.6 %place_tokens.3.x_ref.refs_1_ = bf16[2048,1024]{1,0:T(8,128)(2,1)S(1)} custom-call(f32[1,1024]{1,0:T(1,128)S(1)} %rank_tokens.1.rank_ref.row_ref, bf16[512,1024]{1,0:T(8,128)(2,1)S(1)} %collective-permute-done.5.refs_0_, bf16[512,1024]{1,0:T(8,128)(2,1)S(1)} %collective-permute-done.8.refs_1_, bf16[2048,1024]{1,0:T(8,128)(2,1)S(1)} %place_tokens.2.refs_2_), custom_call_target="tpu_custom_call" | custom-call | bytes 4096 | tf_op jit(solution)/shard_map/place_tokens/pallas_call | solution.py:279
  45.5 3.1 %project.1 = (f32[2048,256]{1,0:T(8,128)S(1)}, f32[256,2048]{1,0:T(8,128)S(1)}, bf16[2048,128]{1,0:T(8,128)(2,1)S(1)}) custom-call(bf16[2048,1024]{1,0:T(8,128)(2,1)S(1)} %place_tokens.3.x_ref.refs_1_, bf16[128,1280]{1,0:T(8,128)(2,1)S(1)} %reorder.3.refs_0_.refs_3_, bf16[128,1280]{1,0:T(8,128)(2,1)S(1)} %collective-permute-done.3.refs_1_.refs_4_, ...), custom_call_target="tpu_custom_call" | custom-call | bytes 4096 | tf_op jit(solution)/shard_map/project/pallas_call | solution.py:326
  48.9 6.1 %block_updates.1 = (bf16[2,2048,128]{2,1,0:T(8,128)(2,1)S(1)}, bf16[8,272,128]{2,1,0:T(8,128)(2,1)}) custom-call(f32[8,16]{1,0:T(8,128)S(1)} %bitcast.10, f32[8,16]{1,0:T(8,128)S(1)} %collective-permute-done.refs_1_, f32[2048,256]{1,0:T(8,128)S(1)} %get-tuple-element.60.refs_2_, f32[256,2048]{1,0:T(8,128)S(1)} %get-tuple-element.61.refs_3_, ...), custom_call_target="tpu_custom_call" | custom-call | flops 1073741824 | bytes 3145728 | tf_op jit(solution)/shard_map/block_updates/pallas_call | solution.py:429
  55.0 5.3 %all-to-all-start = ((bf16[8,272,128]{2,1,0:T(8,128)(2,1)}), bf16[8,272,128]{2,1,0:T(8,128)(2,1)S(1)}, u32[]{:S(2)}, u32[]{:S(2)}) async-start(bf16[8,272,128]{2,1,0:T(8,128)(2,1)} %get-tuple-element.63), calls=%async_computation | async-start | bytes 1114112 | tf_op jit(solution)/shard_map/all_to_all | solution.py:799
  61.0 9.1 %attend.2 = (f32[1024,256]{1,0:T(8,128)}, bf16[1024,256]{1,0:T(8,128)(2,1)}) custom-call(s32[16,4]{1,0:T(8,128)} %copy.7.refs_0_, bf16[2048,1024]{1,0:T(8,128)(2,1)} %copy-done, bf16[2,2048,128]{2,1,0:T(8,128)(2,1)} %copy-done.16, bf16[128,1280]{1,0:T(8,128)(2,1)} %copy-done.3, bf16[128,1280]{1,0:T(8,128)(2,1)} %copy-done.8, bf16[128,1280]{1,0:T(8,128)(2,1)} %copy-done.10, ...), custom_call_target="tpu_custom_call" | custom-call | flops 4831838208 | bytes 11534336 | tf_op jit(solution)/shard_map/attend/pallas_call | solution.py:574
  70.1 2.2 %all-to-all-done.u_ref = bf16[8,272,128]{2,1,0:T(8,128)(2,1)S(1)} async-done(((bf16[8,272,128]{2,1,0:T(8,128)(2,1)}), bf16[8,272,128]{2,1,0:T(8,128)(2,1)S(1)}, u32[]{:S(2)}, u32[]{:S(2)}) %all-to-all-start) | async-done | bytes 557088 | tf_op jit(solution)/shard_map/all_to_all | solution.py:799
  72.4 0.9 scan_states.1
  73.3 3.8 %all-to-all-start.1 = ((bf16[8,256,128]{2,1,0:T(8,128)(2,1)}), bf16[8,256,128]{2,1,0:T(8,128)(2,1)S(1)}, u32[]{:S(2)}, u32[]{:S(2)}) async-start(bf16[8,256,128]{2,1,0:T(8,128)(2,1)} %scan_states.1), calls=%async_computation.1 | async-start | bytes 1048576 | tf_op jit(solution)/shard_map/all_to_all | solution.py:799
  77.1 9.4 %attend.3 = (f32[1024,256]{1,0:T(8,128)}, bf16[1024,256]{1,0:T(8,128)(2,1)}) custom-call(s32[16,4]{1,0:T(8,128)} %copy.7.refs_0_, bf16[2048,1024]{1,0:T(8,128)(2,1)} %copy-done, bf16[2,2048,128]{2,1,0:T(8,128)(2,1)} %copy-done.16, bf16[128,1280]{1,0:T(8,128)(2,1)} %copy-done.3, bf16[128,1280]{1,0:T(8,128)(2,1)} %copy-done.8, bf16[128,1280]{1,0:T(8,128)(2,1)} %copy-done.10, ...), custom_call_target="tpu_custom_call" | custom-call | flops 4831838208 | bytes 11534336 | tf_op jit(solution)/shard_map/attend/pallas_call | solution.py:574
  86.4 3.7 %all-to-all-done.1 = bf16[8,256,128]{2,1,0:T(8,128)(2,1)S(1)} async-done(((bf16[8,256,128]{2,1,0:T(8,128)(2,1)}), bf16[8,256,128]{2,1,0:T(8,128)(2,1)S(1)}, u32[]{:S(2)}, u32[]{:S(2)}) %all-to-all-start.1) | async-done | bytes 524320 | tf_op jit(solution)/shard_map/all_to_all | solution.py:799
  90.1 0.8 copy-done.17
  90.9 5.1 %mix.1 = (bf16[512,256]{1,0:T(8,128)(2,1)S(1)}, bf16[512,256]{1,0:T(8,128)(2,1)S(1)}, bf16[512,256]{1,0:T(8,128)(2,1)S(1)}, bf16[512,256]{1,0:T(8,128)(2,1)S(1)}) custom-call(f32[8,16]{1,0:T(8,128)S(1)} %bitcast.11, f32[8,16]{1,0:T(8,128)S(1)} %collective-permute-done.refs_1_, f32[1024,256]{1,0:T(8,128)} %get-tuple-element.67.refs_2_, ...), custom_call_target="tpu_custom_call" | custom-call | flops 1073741824 | bytes 6291456 | tf_op jit(solution)/shard_map/mix/pallas_call | solution.py:679
  96.1 1.6 %collective-permute-start.13 = (bf16[512,256]{1,0:T(8,128)(2,1)S(1)}, bf16[512,256]{1,0:T(8,128)(2,1)S(1)}, u32[]{:S(2)}, u32[]{:S(2)}) collective-permute-start(bf16[512,256]{1,0:T(8,128)(2,1)S(1)} %get-tuple-element.75), channel_id=1, source_target_pairs={{0,1},{1,0},{2,3},{3,2},{4,5},{5,4},{6,7},{7,6},{8,9},{9,8},{10,11... | collective-permute-start | bytes 786440 | tf_op jit(solution)/shard_map/ppermute | solution.py:95
  98.0 1.2 %project_out.2.refs_2_ = f32[512,1024]{1,0:T(8,128)S(1)} custom-call(bf16[1024,1024]{1,0:T(8,128)(2,1)S(1)} %copy-done.1, bf16[512,256]{1,0:T(8,128)(2,1)S(1)} %get-tuple-element.77.refs_0_, bf16[512,256]{1,0:T(8,128)(2,1)S(1)} %collective-permute-done.15.refs_1_), custom_call_target="tpu_custom_call" | custom-call | bytes 2048 | tf_op jit(solution)/shard_map/project_out/pallas_call | solution.py:727
  99.1 6.1 %collective-permute-done.13.refs_0_ = bf16[512,256]{1,0:T(8,128)(2,1)S(1)} collective-permute-done((bf16[512,256]{1,0:T(8,128)(2,1)S(1)}, bf16[512,256]{1,0:T(8,128)(2,1)S(1)}, u32[]{:S(2)}, u32[]{:S(2)}) %collective-permute-start.13) | collective-permute-done | bytes 262176 | tf_op jit(solution)/shard_map/ppermute | solution.py:95
  105.3 4.7 %collective-permute-done.14.refs_1_ = bf16[512,256]{1,0:T(8,128)(2,1)S(1)} collective-permute-done((bf16[512,256]{1,0:T(8,128)(2,1)S(1)}, bf16[512,256]{1,0:T(8,128)(2,1)S(1)}, u32[]{:S(2)}, u32[]{:S(2)}) %collective-permute-start.14) | collective-permute-done | bytes 262176 | tf_op jit(solution)/shard_map/ppermute | solution.py:103
  110.0 1.9 %project_out.3 = bf16[512,1024]{1,0:T(8,128)(2,1)} custom-call(bf16[1024,1024]{1,0:T(8,128)(2,1)S(1)} %copy-done.1, bf16[512,256]{1,0:T(8,128)(2,1)S(1)} %collective-permute-done.13.refs_0_, bf16[512,256]{1,0:T(8,128)(2,1)S(1)} %collective-permute-done.14.refs_1_, f32[512,1024]{1,0:T(8,128)S(1)} %project_out.2.refs_2_), custom_call_target="tpu_custom_call" | custom-call | bytes 2048 | tf_op jit(solution)/shard_map/project_out/pallas_call | solution.py:727
  (60 shorter events, 4.6 us)
Async XLA Ops:
  0.0 19.1 %collective-permute-start.1 = (bf16[512,1024]{1,0:T(8,128)(2,1)}, bf16[512,1024]{1,0:T(8,128)(2,1)S(1)}, u32[]{:S(2)}, u32[]{:S(2)}) collective-permute-start(bf16[512,1024]{1,0:T(8,128)(2,1)} %bitcast.5), channel_id=1, source_target_pairs={{0,2},{2,0},{4,6},{6,4},{8,10},{10,8},{12,14},{14,12},{16,18},{18,... | collective-permute-start | bytes 3145736 | tf_op jit(solution)/shard_map/ppermute | solution.py:61
  0.5 4.1 %collective-permute-start.2 = (bf16[64,2560]{1,0:T(8,128)(2,1)}, bf16[64,2560]{1,0:T(8,128)(2,1)S(1)}, u32[]{:S(2)}, u32[]{:S(2)}) collective-permute-start(bf16[64,2560]{1,0:T(8,128)(2,1)} %refs_0_.3), channel_id=1, source_target_pairs={{0,2},{2,0},{4,6},{6,4},{8,10},{10,8},{12,14},{14,12},{16,18},{18,... | collective-permute-start | bytes 983048 | tf_op jit(solution)/shard_map/ppermute | solution.py:61
  0.5 28.5 %collective-permute-start.5 = (bf16[512,1024]{1,0:T(8,128)(2,1)}, bf16[512,1024]{1,0:T(8,128)(2,1)S(1)}, u32[]{:S(2)}, u32[]{:S(2)}) collective-permute-start(bf16[512,1024]{1,0:T(8,128)(2,1)} %bitcast.6), channel_id=1, source_target_pairs={{0,1},{1,0},{2,3},{3,2},{4,5},{5,4},{6,7},{7,6},{8,9},{9,8},{10,11... | collective-permute-start | bytes 3145736 | tf_op jit(solution)/shard_map/ppermute | solution.py:95
  4.7 40.7 %copy-start.3 = (bf16[128,1280]{1,0:T(8,128)(2,1)}, bf16[128,1280]{1,0:T(8,128)(2,1)S(1)}, u32[]{:S(2)}) copy-start(bf16[128,1280]{1,0:T(8,128)(2,1)S(1)} %reorder.3.refs_0_.refs_3_) | copy-start | bytes 983044
  4.7 11.9 %collective-permute-start.3 = (bf16[128,1280]{1,0:T(8,128)(2,1)S(1)}, bf16[128,1280]{1,0:T(8,128)(2,1)S(1)}, u32[]{:S(2)}, u32[]{:S(2)}) collective-permute-start(bf16[128,1280]{1,0:T(8,128)(2,1)S(1)} %reorder.3.refs_0_.refs_3_), channel_id=1, source_target_pairs={{0,8},{2,10},{4,12},{6,14},{8,16},{10,18},{12,20},{14,22},{16,24},... | collective-permute-start | bytes 983048 | tf_op jit(solution)/shard_map/ppermute | solution.py:66
  6.5 10.0 %collective-permute-start.4 = (bf16[128,1280]{1,0:T(8,128)(2,1)S(1)}, bf16[128,1280]{1,0:T(8,128)(2,1)S(1)}, u32[]{:S(2)}, u32[]{:S(2)}) collective-permute-start(bf16[128,1280]{1,0:T(8,128)(2,1)S(1)} %reorder.3.refs_0_.refs_3_), channel_id=1, source_target_pairs={{0,4},{2,6},{4,0},{6,2},{8,12},{10,14},{12,8},{14,10},{16,20},{18,... | collective-permute-start | bytes 983048 | tf_op jit(solution)/shard_map/ppermute | solution.py:71
  8.0 1.4 %collective-permute-start = (f32[8,16]{1,0:T(8,128)}, f32[8,16]{1,0:T(8,128)S(1)}, u32[]{:S(2)}, u32[]{:S(2)}) collective-permute-start(f32[8,16]{1,0:T(8,128)} %bitcast.9), channel_id=1, source_target_pairs={{0,2},{2,0},{4,6},{6,4},{8,10},{10,8},{12,14},{14,12},{16,18},{18,... | collective-permute-start | bytes 1544 | tf_op jit(solution)/shard_map/ppermute | solution.py:61
  16.6 28.8 %copy-start.8 = (bf16[128,1280]{1,0:T(8,128)(2,1)}, bf16[128,1280]{1,0:T(8,128)(2,1)S(1)}, u32[]{:S(2)}) copy-start(bf16[128,1280]{1,0:T(8,128)(2,1)S(1)} %collective-permute-done.3.refs_1_.refs_4_) | copy-start | bytes 983044
  16.6 28.8 %copy-start.9 = (bf16[128,1280]{1,0:T(8,128)(2,1)}, bf16[128,1280]{1,0:T(8,128)(2,1)S(1)}, u32[]{:S(2)}) copy-start(bf16[128,1280]{1,0:T(8,128)(2,1)S(1)} %collective-permute-done.4.refs_4_.refs_7_) | copy-start | bytes 983044
  16.6 11.1 %collective-permute-start.6 = (bf16[128,1280]{1,0:T(8,128)(2,1)S(1)}, bf16[128,1280]{1,0:T(8,128)(2,1)S(1)}, u32[]{:S(2)}, u32[]{:S(2)}) collective-permute-start(bf16[128,1280]{1,0:T(8,128)(2,1)S(1)} %collective-permute-done.3.refs_1_.refs_4_), channel_id=1, source_target_pairs={{0,8},{2,10},{4,12},{6,14},{8,16},{10,18},{12,20},{14,22},{16,24},... | collective-permute-start | bytes 983048 | tf_op jit(solution)/shard_map/ppermute | solution.py:66
  17.6 10.1 %collective-permute-start.7 = (bf16[128,1280]{1,0:T(8,128)(2,1)S(1)}, bf16[128,1280]{1,0:T(8,128)(2,1)S(1)}, u32[]{:S(2)}, u32[]{:S(2)}) collective-permute-start(bf16[128,1280]{1,0:T(8,128)(2,1)S(1)} %collective-permute-done.3.refs_1_.refs_4_), channel_id=1, source_target_pairs={{0,4},{2,6},{4,0},{6,2},{8,12},{10,14},{12,8},{14,10},{16,20},{18,... | collective-permute-start | bytes 983048 | tf_op jit(solution)/shard_map/ppermute | solution.py:71
  27.7 17.7 %copy-start.10 = (bf16[128,1280]{1,0:T(8,128)(2,1)}, bf16[128,1280]{1,0:T(8,128)(2,1)S(1)}, u32[]{:S(2)}) copy-start(bf16[128,1280]{1,0:T(8,128)(2,1)S(1)} %collective-permute-done.6.refs_2_.refs_5_) | copy-start | bytes 983044
  27.7 17.8 %copy-start.11 = (bf16[128,1280]{1,0:T(8,128)(2,1)}, bf16[128,1280]{1,0:T(8,128)(2,1)S(1)}, u32[]{:S(2)}) copy-start(bf16[128,1280]{1,0:T(8,128)(2,1)S(1)} %collective-permute-done.7.refs_5_.refs_8_) | copy-start | bytes 983044
  27.7 8.4 %collective-permute-start.10 = (bf16[128,1280]{1,0:T(8,128)(2,1)S(1)}, bf16[128,1280]{1,0:T(8,128)(2,1)S(1)}, u32[]{:S(2)}, u32[]{:S(2)}) collective-permute-start(bf16[128,1280]{1,0:T(8,128)(2,1)S(1)} %collective-permute-done.6.refs_2_.refs_5_), channel_id=1, source_target_pairs={{0,4},{2,6},{4,0},{6,2},{8,12},{10,14},{12,8},{14,10},{16,20},{18,... | collective-permute-start | bytes 983048 | tf_op jit(solution)/shard_map/ppermute | solution.py:71
  29.0 9.6 %collective-permute-start.9 = (bf16[128,1280]{1,0:T(8,128)(2,1)S(1)}, bf16[128,1280]{1,0:T(8,128)(2,1)S(1)}, u32[]{:S(2)}, u32[]{:S(2)}) collective-permute-start(bf16[128,1280]{1,0:T(8,128)(2,1)S(1)} %collective-permute-done.6.refs_2_.refs_5_), channel_id=1, source_target_pairs={{0,8},{2,10},{4,12},{6,14},{8,16},{10,18},{12,20},{14,22},{16,24},... | collective-permute-start | bytes 983048 | tf_op jit(solution)/shard_map/ppermute | solution.py:66
  29.0 12.8 %collective-permute-start.8 = (bf16[512,1024]{1,0:T(8,128)(2,1)S(1)}, bf16[512,1024]{1,0:T(8,128)(2,1)S(1)}, u32[]{:S(2)}, u32[]{:S(2)}) collective-permute-start(bf16[512,1024]{1,0:T(8,128)(2,1)S(1)} %collective-permute-done.5.refs_0_), channel_id=1, source_target_pairs={{0,2},{2,0},{4,6},{6,4},{8,10},{10,8},{12,14},{14,12},{16,18},{18,... | collective-permute-start | bytes 3145736 | tf_op jit(solution)/shard_map/ppermute | solution.py:61
  36.0 9.4 %copy-start.5 = (bf16[128,1280]{1,0:T(8,128)(2,1)}, bf16[128,1280]{1,0:T(8,128)(2,1)S(1)}, u32[]{:S(2)}) copy-start(bf16[128,1280]{1,0:T(8,128)(2,1)S(1)} %collective-permute-done.10.refs_6_.refs_9_) | copy-start | bytes 983044
  38.6 6.9 %copy-start.6 = (bf16[128,1280]{1,0:T(8,128)(2,1)}, bf16[128,1280]{1,0:T(8,128)(2,1)S(1)}, u32[]{:S(2)}) copy-start(bf16[128,1280]{1,0:T(8,128)(2,1)S(1)} %collective-permute-done.9.refs_3_.refs_6_) | copy-start | bytes 983044
  40.5 8.1 %collective-permute-start.11 = (bf16[64,1280]{1,0:T(8,128)(2,1)S(1)}, bf16[64,1280]{1,0:T(8,128)(2,1)S(1)}, u32[]{:S(2)}, u32[]{:S(2)}) collective-permute-start(bf16[64,1280]{1,0:T(8,128)(2,1)S(1)} %slice.6), channel_id=1, source_target_pairs={{0,4},{2,6},{4,0},{6,2},{8,12},{10,14},{12,8},{14,10},{16,20},{18,... | collective-permute-start | bytes 491528 | tf_op jit(solution)/shard_map/ppermute | solution.py:71
  41.6 7.3 %collective-permute-start.12 = (bf16[64,1280]{1,0:T(8,128)(2,1)S(1)}, bf16[64,1280]{1,0:T(8,128)(2,1)S(1)}, u32[]{:S(2)}, u32[]{:S(2)}) collective-permute-start(bf16[64,1280]{1,0:T(8,128)(2,1)S(1)} %slice.7), channel_id=1, source_target_pairs={{0,8},{2,10},{4,12},{6,14},{8,16},{10,18},{12,20},{14,22},{16,24},... | collective-permute-start | bytes 491528 | tf_op jit(solution)/shard_map/ppermute | solution.py:66
  45.5 3.5 %copy-start.15 = (f32[1,8,16]{2,1,0:T(8,128)S(1)}, f32[1,8,16]{2,1,0:T(8,128)}, u32[]{:S(2)}) copy-start(f32[1,8,16]{2,1,0:T(8,128)} %param.11) | copy-start | bytes 1540
  48.6 6.4 %copy-start.13 = (bf16[64,1280]{1,0:T(8,128)(2,1)}, bf16[64,1280]{1,0:T(8,128)(2,1)S(1)}, u32[]{:S(2)}) copy-start(bf16[64,1280]{1,0:T(8,128)(2,1)S(1)} %collective-permute-done.11.refs_5_.refs_10_) | copy-start | bytes 491524
  48.9 6.1 %copy-start.14 = (bf16[64,1280]{1,0:T(8,128)(2,1)}, bf16[64,1280]{1,0:T(8,128)(2,1)S(1)}, u32[]{:S(2)}) copy-start(bf16[64,1280]{1,0:T(8,128)(2,1)S(1)} %collective-permute-done.12.refs_6_.refs_11_) | copy-start | bytes 491524
  48.9 11.4 %copy-start.18 = (s32[16,4]{0,1:T(4,128)S(1)}, s32[16,4]{0,1:T(4,128)}, u32[]{:S(2)}) copy-start(s32[16,4]{0,1:T(4,128)} %param.10) | copy-start | bytes 772
  55.0 6.0 %copy-start.16 = (bf16[2,2048,128]{2,1,0:T(8,128)(2,1)}, bf16[2,2048,128]{2,1,0:T(8,128)(2,1)S(1)}, u32[]{:S(2)}) copy-start(bf16[2,2048,128]{2,1,0:T(8,128)(2,1)S(1)} %get-tuple-element.64.refs_2_) | copy-start | bytes 3145732
  55.0 17.3 %all-to-all-start = ((bf16[8,272,128]{2,1,0:T(8,128)(2,1)}), bf16[8,272,128]{2,1,0:T(8,128)(2,1)S(1)}, u32[]{:S(2)}, u32[]{:S(2)}) async-start(bf16[8,272,128]{2,1,0:T(8,128)(2,1)} %get-tuple-element.63), calls=%async_computation | async-start | bytes 1114112 | tf_op jit(solution)/shard_map/all_to_all | solution.py:799
  73.3 16.8 %all-to-all-start.1 = ((bf16[8,256,128]{2,1,0:T(8,128)(2,1)}), bf16[8,256,128]{2,1,0:T(8,128)(2,1)S(1)}, u32[]{:S(2)}, u32[]{:S(2)}) async-start(bf16[8,256,128]{2,1,0:T(8,128)(2,1)} %scan_states.1), calls=%async_computation.1 | async-start | bytes 1048576 | tf_op jit(solution)/shard_map/all_to_all | solution.py:799
  77.1 13.9 %copy-start.7 = (bf16[1024,256]{1,0:T(8,128)(2,1)S(1)}, bf16[1024,256]{1,0:T(8,128)(2,1)}, u32[]{:S(2)}) copy-start(bf16[1024,256]{1,0:T(8,128)(2,1)} %get-tuple-element.71.refs_4_) | copy-start | bytes 1572868
  90.9 7.0 %copy-start.1 = (bf16[1024,1024]{1,0:T(8,128)(2,1)S(1)}, bf16[1024,1024]{1,0:T(8,128)(2,1)}, u32[]{:S(2)}) copy-start(bf16[1024,1024]{1,0:T(8,128)(2,1)} %w_ref.3) | copy-start | bytes 6291460
  96.0 1.9 %collective-permute-start.15 = (bf16[512,256]{1,0:T(8,128)(2,1)S(1)}, bf16[512,256]{1,0:T(8,128)(2,1)S(1)}, u32[]{:S(2)}, u32[]{:S(2)}) collective-permute-start(bf16[512,256]{1,0:T(8,128)(2,1)S(1)} %get-tuple-element.78), channel_id=1, source_target_pairs={{0,2},{2,0},{4,6},{6,4},{8,10},{10,8},{12,14},{14,12},{16,18},{18,... | collective-permute-start | bytes 786440 | tf_op jit(solution)/shard_map/ppermute | solution.py:61
  96.1 9.2 %collective-permute-start.13 = (bf16[512,256]{1,0:T(8,128)(2,1)S(1)}, bf16[512,256]{1,0:T(8,128)(2,1)S(1)}, u32[]{:S(2)}, u32[]{:S(2)}) collective-permute-start(bf16[512,256]{1,0:T(8,128)(2,1)S(1)} %get-tuple-element.75), channel_id=1, source_target_pairs={{0,1},{1,0},{2,3},{3,2},{4,5},{5,4},{6,7},{7,6},{8,9},{9,8},{10,11... | collective-permute-start | bytes 786440 | tf_op jit(solution)/shard_map/ppermute | solution.py:95
  97.7 12.3 %collective-permute-start.14 = (bf16[512,256]{1,0:T(8,128)(2,1)S(1)}, bf16[512,256]{1,0:T(8,128)(2,1)S(1)}, u32[]{:S(2)}, u32[]{:S(2)}) collective-permute-start(bf16[512,256]{1,0:T(8,128)(2,1)S(1)} %get-tuple-element.76), channel_id=1, source_target_pairs={{0,3},{1,2},{2,1},{3,0},{4,7},{5,6},{6,5},{7,4},{8,11},{9,10},{10,... | collective-permute-start | bytes 786440 | tf_op jit(solution)/shard_map/ppermute | solution.py:103
  (5 other events, 7.5 us)

commit v15 on v14

--- a/solution.py
+++ b/solution.py
@@ -110,12 +110,6 @@
     def decay(self, refs, slot, pair, g):
         head = self.core() * self.heads + 2 * pair
         return halves((1, LANES), refs[slot][head, g], refs[slot][head + 1, g])
-
-    def last_decay(self, refs, pair, g):
-        if self.merge == 1:
-            return self.decay(refs, 0, pair, g)
-        one, two = (self.decay(refs, slot, pair, g) for slot in range(2))
-        return jnp.where(self.core() == 0, two, one)
 
 
 class Copies:
@@ -242,9 +236,22 @@
         back_kernel,
         out_shape=jax.ShapeDtypeStruct((rank.shape[1], rank.shape[1]), bf16),
         compiler_params=params(),
-        cost_estimate=cost(2e10, 4 * LANES),
+        cost_estimate=cost(0, 4 * LANES),
         name="back_tokens",
     )(rank)
+
+
+def hold(values):
+    def kernel(in_ref, out_ref):
+        out_ref[...] = in_ref[...]
+
+    return pl.pallas_call(
+        kernel,
+        out_shape=jax.ShapeDtypeStruct(values.shape, values.dtype),
+        compiler_params=params(),
+        cost_estimate=cost(2e10, 4 * LANES),
+        name="hold",
+    )(values)
 
 
 def picks(rank, at, rows):
@@ -337,10 +344,9 @@
     )(x, *weights)
 
 
-def update_kernel(plan, groups, *refs):
-    decay_refs, refs = refs[: plan.merge], refs[plan.merge :]
-    v_ref, b_ref, x_ref, last_refs, (left_out, total_out, left, total_ref, u, sems) = (
-        refs[0], refs[1], refs[2], refs[3:-6], refs[-6:]
+def update_kernel(plan, groups, decay_ref, *refs):
+    v_ref, b_ref, x_ref, last_refs, (left, total_out, total_ref, u, sems) = (
+        refs[0], refs[1], refs[2], refs[3:-5], refs[-5:]
     )
     copies = Copies(sems)
     leaving = []
@@ -388,8 +394,8 @@
         for i in range(items):
             row = d * share + i * N
             rows = slice(row, row + size)
-            p, g = row // N % plan.pairs, row // N // plan.pairs
-            product = last = plan.last_decay(decay_refs, p, g)
+            item = slice(row // N, row // N + 1)
+            last, product = decay_ref[0, item, :], decay_ref[1, item, :]
             if plan.merge == 2:
                 one, two = u[0, rows, :], u[1, rows, :]
                 one, two = (
@@ -399,7 +405,6 @@
                 left[0, rows, :] = one.astype(bf16)
                 left[1, rows, :] = two.astype(bf16)
                 total = jnp.where(first, two, one)
-                product = plan.decay(decay_refs, 0, p, g) * plan.decay(decay_refs, 1, p, g)
             else:
                 total = u[0, rows, :]
                 left[0, rows, :] = total.astype(bf16)
@@ -412,9 +417,6 @@
         if (d + 1) % (peers // 4) == 0:
             done = slice(d + 1 - peers // 4, d + 1)
             leaving.append(copies.start(total_ref.at[done], total_out.at[done]))
-            done = slice((d + 1 - peers // 4) * share, (d + 1) * share)
-            for s in range(plan.merge):
-                leaving.append(copies.start(left.at[s, done], left_out.at[s, done]))
     finish(leaving)
 
 
@@ -428,14 +430,13 @@
     share = rows // plan.chips
     return pl.pallas_call(
         functools.partial(update_kernel, plan, groups),
-        in_specs=[smem] * plan.merge + [vmem] * (3 + len(last)),
-        out_specs=(hbm, hbm),
+        in_specs=[vmem] * (4 + len(last)),
+        out_specs=(vmem, hbm),
         out_shape=(
             jax.ShapeDtypeStruct((plan.merge, rows, LANES), bf16),
             jax.ShapeDtypeStruct((plan.chips, share_rows(share), LANES), bf16),
         ),
         scratch_shapes=[
-            pltpu.VMEM((plan.merge, rows, LANES), bf16),
             pltpu.VMEM((plan.chips, share_rows(share), LANES), bf16),
             pltpu.VMEM((plan.merge, rows, LANES), f32),
             Copies.scratch(),
@@ -443,7 +444,37 @@
         compiler_params=params(),
         cost_estimate=cost(4 * every * 256 * 2 * cols, 6 * every * cols),
         name="block_updates",
-    )(*decays, v, b, x, *last)
+    )(decays, v, b, x, *last)
+
+
+def decay_kernel(plan, groups, *refs):
+    rate_refs, out_ref = refs[:-1], refs[-1]
+    first = plan.core() == 0
+    for g in range(groups):
+        for p in range(plan.pairs):
+            row = slice(g * plan.pairs + p, g * plan.pairs + p + 1)
+            slots = [plan.decay(rate_refs, s, p, g) for s in range(plan.merge)]
+            together, last = slots[0], slots[0]
+            if plan.merge == 2:
+                together = slots[0] * slots[1]
+                last = jnp.where(first, slots[1], slots[0])
+                slots = [
+                    jnp.where(first, slots[0], together),
+                    jnp.where(first, together, slots[1]),
+                ]
+            for i, value in enumerate([last, together] + slots):
+                out_ref[i, row, :] = value
+
+
+def decay_tables(plan, rates, groups):
+    return pl.pallas_call(
+        functools.partial(decay_kernel, plan, groups),
+        in_specs=[smem] * plan.merge,
+        out_shape=jax.ShapeDtypeStruct((2 + plan.merge, plan.pairs * groups, LANES), f32),
+        compiler_params=params(),
+        cost_estimate=cost(0, 4 * LANES),
+        name="decay_tables",
+    )(*rates)
 
 
 def scan_kernel(plan, u_ref, s_ref):
@@ -609,21 +640,20 @@
     )
 
 
-def mix_kernel(plan, groups, *refs):
-    decay_refs, refs = refs[: plan.merge], refs[plan.merge :]
+def mix_kernel(plan, groups, decay_in, *refs):
     a_ins, refs = refs[: plan.merge], refs[plan.merge :]
     c_ins, refs = refs[: plan.merge], refs[plan.merge :]
     s_in, back_in, refs = refs[0], refs[1], refs[2:]
-    out_refs, (a, c, state, back, mixed, out, sems) = refs[:-7], refs[-7:]
+    out_refs, (decay, a, c, state, back, mixed, out, sems) = refs[:-8], refs[-8:]
     copies = Copies(sems)
     tokens = back.shape[0]
     block = tokens // groups
     width = a.shape[2]
     here = groups // 4
     many = here * plan.pairs * N
-    first = plan.core() == 0
 
     arriving = []
+    decaying = copies.start(decay_in, decay)
     for i in range(4):
         rows = slice(i * here * block, (i + 1) * here * block)
         items = slice(i * many, (i + 1) * many)
@@ -640,6 +670,7 @@
         rows = slice(k * local, (k + 1) * local)
         turning.append(copies.start(back_in.at[rows], back.at[rows]))
 
+    decaying.wait()
     for g in range(groups):
         if g % here == 0:
             finish(arriving[g // here])
@@ -649,14 +680,12 @@
             at = (g * plan.pairs + p) * N
             readers = jnp.concatenate([c[s, rows, cols] for s in range(plan.merge)], axis=0)
             read = read_out(readers, state[at : at + N, :].astype(f32), block)
-            decays = [plan.decay(decay_refs, s, p, g) for s in range(plan.merge)]
-            if plan.merge == 2:
-                both = decays[0] * decays[1]
-                decays = [jnp.where(first, decays[0], both), jnp.where(first, both, decays[1])]
+            item = slice(g * plan.pairs + p, g * plan.pairs + p + 1)
             for s in range(plan.merge):
                 there = slice(s * width + p * LANES, s * width + (p + 1) * LANES)
                 mixed[rows, there] = (
-                    a[s, rows, cols] + decays[s] * read[s * block : (s + 1) * block]
+                    a[s, rows, cols]
+                    + decay[2 + s, item, :] * read[s * block : (s + 1) * block]
                 ).astype(bf16)
 
     leaving = []
@@ -678,10 +707,11 @@
     count = plan.merge * plan.peers
     return pl.pallas_call(
         functools.partial(mix_kernel, plan, groups),
-        in_specs=[smem] * plan.merge + [hbm] * (2 * plan.merge + 2),
+        in_specs=[hbm] * (2 * plan.merge + 3),
         out_specs=(hbm,) * count,
         out_shape=(jax.ShapeDtypeStruct((tokens // plan.peers, width), bf16),) * count,
         scratch_shapes=[
+            pltpu.VMEM(decays.shape, f32),
             pltpu.VMEM((plan.merge, tokens, width), f32),
             pltpu.VMEM((plan.merge, tokens, width), bf16),
             pltpu.VMEM(state.shape, bf16),
@@ -693,7 +723,7 @@
         compiler_params=params(52),
         cost_estimate=cost(4 * tokens * tokens * width, 2 * tokens * tokens + 16 * tokens * width),
         name="mix",
-    )(*decays, *attended, *readers, state, back)
+    )(decays, *attended, *readers, state, back)
 
 
 def out_kernel(plan, sources, w_ref, *refs):
@@ -752,6 +782,7 @@
         block = reorder(plan, plan.swap(in_weight), [block])
     ids = jnp.roll(block_ids, -me * local_tokens)
     ids, rates = lax.optimization_barrier((ids, rates))
+    tables = decay_tables(plan, rates, groups)
     rank = rank_tokens(ids, groups)
 
     def fill(arriving, part):
@@ -763,7 +794,10 @@
         blocks, crossed = [block], []
         half = block.shape[0] // 2
         for k in range(plan.along - 1):
-            with_ = rank if k == 0 else ()
+            with_ = ()
+            if k == 0:
+                places = back_tokens(rank)
+                with_ = (places, tables)
             if k == min(1, plan.along - 2):
                 rank, owns, _ = lax.optimization_barrier((rank, owns, blocks[-1]))
                 part = with_ = place_tokens(plan, rank, 0, owns, [])
@@ -774,9 +808,9 @@
                 (plan.round(blocks[-1]), plan.cross(blocks[-1]), with_)
             )
             if k == plan.along - 2:
-                rank, passed, across = lax.optimization_barrier((rank, passed, across))
-                places, passed, across = lax.optimization_barrier(
-                    (back_tokens(rank), passed, across)
+                tables, passed, across = lax.optimization_barrier((tables, passed, across))
+                tables, passed, across = lax.optimization_barrier(
+                    (hold(tables), passed, across)
                 )
             blocks.append(passed)
             crossed.append(across)
@@ -790,10 +824,10 @@
         x = fill(arriving, place_tokens(plan, rank, 0, owns, []))
     if plan.ringed:
         v, b, x_last = project(plan, x, weights[:-2])
-        local, total = block_updates(plan, rates, v, b, x_last, last, groups)
+        local, total = block_updates(plan, tables, v, b, x_last, last, groups)
     else:
         v, b, x_last = project(plan, x, weights)
-        local, total = block_updates(plan, rates, v, b, x_last, [], groups)
+        local, total = block_updates(plan, tables, v, b, x_last, [], groups)
 
     def exchange(blocks):
         return lax.all_to_all(
@@ -812,7 +846,7 @@
     state = exchange(states).reshape(-1, LANES)
 
     bases, readers = ([a[i] for a in attended] for i in range(2))
-    mixed = mix(plan, rates, bases, readers, state, places, groups)
+    mixed = mix(plan, tables, bases, readers, state, places, groups)
     moved = {
         (s, k): plan.to_peer(mixed[s * plan.peers + k], k, s == 1)
         for s in range(plan.merge)
@@ -822,7 +856,10 @@
     if plan.merge == 2:
         near[1, 0] = plan.swap(mixed[plan.peers])
     result = project_out(plan, out_weight, near, [], f32)
-    return project_out(plan, out_weight, moved, [result], bf16)[None]
+    last = {key: moved.pop(key) for key in list(moved)[-1:]}
+    if moved:
+        result = project_out(plan, out_weight, moved, [result], f32)
+    return project_out(plan, out_weight, last, [result], bf16)[None]
 
 
 def solution(mesh):

time: 113 us -> 107 us (0.947)
  waiting for transfers between devices: 37.9 us -> 33 us
  local copies, waits for them, and re-layouts: 5.13 us -> 3.91 us
    ppermute x4, waiting for transfers between devices: 7.05 us -> 0.01 us  [cross(): return lax.ppermute(block, 'tm', pairs)]
    ppermute x4, waiting for transfers between devices: 13.5 us -> 16.7 us  [round(): return lax.ppermute(block, 'tm', pairs)]
    pallas_call x1, Pallas kernels: 6.07 us -> 3.93 us  [block_updates(): pl.pallas_call(functools.partial(update_kernel, plan, groups), in_specs=[...]
    pallas_call x2 -> x3, Pallas kernels: 3.09 us -> 4.32 us  [project_out(): pl.pallas_call(functools.partial(out_kernel, plan, list(parts)), in_specs...]
    unnamed x39, local copies, waits for them, and re-layouts: 5.11 us -> 3.88 us
    pallas_call x2, Pallas kernels: 7.03 us -> 8.25 us  [place_tokens(): pl.pallas_call(functools.partial(place_kernel, plan.merge, len(frames), s...]
    ppermute x1, waiting for transfers between devices: 4.71 us -> 3.56 us  [to_peer(): return lax.ppermute(block, ('tm', 'head'), pairs)]
    pallas_call x1 -> x3, Pallas kernels: 5.09 us -> 5.27 us  [the longest x1 4.52 us: mix(): pl.pallas_call(functools.partial(mix_kernel, plan, groups), in_specs=[hbm...]
  transfers between devices with their start and end apart: 18 -> 18, of which waited for: 10 -> 9; matrix products, arithmetic and copies ran while one was open for 1% -> 1% of each run, Pallas kernels for 27% -> 32%
where the time goes in v15:
time: 107 us
  Pallas kernels  45.3 us (42%)
  waiting for transfers between devices  33 us (31%)
  starting transfers between devices  23.4 us (22%)
  local copies, waits for them, and re-layouts  3.91 us (4%)
    pallas_call x2, Pallas kernels, attend(): pl.pallas_call(functools.partial(attend_kernel, plan, slot), in_specs=[sm...  18.5 us
    ppermute x4, waiting for transfers between devices, round(): return lax.ppermute(block, 'tm', pairs)  16.7 us
    all_to_all x2, starting transfers between devices, exchange(): lax.all_to_all(blocks, 'tm', split_axis=0, concat_axis=0, tiled=True, axi...  8.57 us
    pallas_call x2, Pallas kernels, place_tokens(): pl.pallas_call(functools.partial(place_kernel, plan.merge, len(frames), s...  8.25 us
    all_to_all x2, waiting for transfers between devices, exchange(): lax.all_to_all(blocks, 'tm', split_axis=0, concat_axis=0, tiled=True, axi...  6.29 us
    ppermute x4, starting transfers between devices, cross(): return lax.ppermute(block, 'tm', pairs)  6.09 us
    ppermute x2, waiting for transfers between devices, to_peer(): return lax.ppermute(block, 'head', pairs)  5.91 us
    ppermute x2, starting transfers between devices, to_peer(): return lax.ppermute(block, 'head', pairs)  5.13 us
  transfers between devices with their start and end apart: 18, of which 9 were waited for; matrix products, arithmetic and copies ran while one was open for 1% of the time, Pallas kernels for 32%

profile of v15, /device:TPU:0, one launch (start us, length us, event | category | flops | bytes accessed | tf_op | source)
XLA Modules:
  0.0 106.9 jit_solution(919825082916606328)
XLA Ops:
  0.5 3.0 %collective-permute-start.9 = (bf16[512,1024]{1,0:T(8,128)(2,1)}, bf16[512,1024]{1,0:T(8,128)(2,1)S(1)}, u32[]{:S(2)}, u32[]{:S(2)}) collective-permute-start(bf16[512,1024]{1,0:T(8,128)(2,1)} %bitcast.6), channel_id=1, source_target_pairs={{0,1},{1,0},{2,3},{3,2},{4,5},{5,4},{6,7},{7,6},{8,9},{9,8},{10,11... | collective-permute-start | bytes 3145736 | tf_op jit(solution)/shard_map/ppermute | solution.py:95
  3.5 1.0 copy-done.12
  4.7 1.6 %collective-permute-start.2 = (bf16[128,1280]{1,0:T(8,128)(2,1)S(1)}, bf16[128,1280]{1,0:T(8,128)(2,1)S(1)}, u32[]{:S(2)}, u32[]{:S(2)}) collective-permute-start(bf16[128,1280]{1,0:T(8,128)(2,1)S(1)} %reorder.3.refs_0_.refs_3_), channel_id=1, source_target_pairs={{0,8},{2,10},{4,12},{6,14},{8,16},{10,18},{12,20},{14,22},{16,24},... | collective-permute-start | bytes 983048 | tf_op jit(solution)/shard_map/ppermute | solution.py:66
  6.3 1.5 %collective-permute-start.3 = (bf16[128,1280]{1,0:T(8,128)(2,1)S(1)}, bf16[128,1280]{1,0:T(8,128)(2,1)S(1)}, u32[]{:S(2)}, u32[]{:S(2)}) collective-permute-start(bf16[128,1280]{1,0:T(8,128)(2,1)S(1)} %reorder.3.refs_0_.refs_3_), channel_id=1, source_target_pairs={{0,4},{2,6},{4,0},{6,2},{8,12},{10,14},{12,8},{14,10},{16,20},{18,... | collective-permute-start | bytes 983048 | tf_op jit(solution)/shard_map/ppermute | solution.py:71
  7.8 0.8 fusion
  10.0 1.4 %copy-done.2 = bf16[1024,1024]{1,0:T(8,128)(2,1)} copy-done((bf16[1024,1024]{1,0:T(8,128)(2,1)}, bf16[1024,1024]{1,0:T(8,128)(2,1)S(1)}, u32[]{:S(2)}) %copy-start.2) | copy-done | bytes 2097176
  12.2 4.3 %collective-permute-done.2.refs_1_.refs_4_ = bf16[128,1280]{1,0:T(8,128)(2,1)S(1)} collective-permute-done((bf16[128,1280]{1,0:T(8,128)(2,1)S(1)}, bf16[128,1280]{1,0:T(8,128)(2,1)S(1)}, u32[]{:S(2)}, u32[]{:S(2)}) %collective-permute-start.2) | collective-permute-done | bytes 327712 | tf_op jit(solution)/shard_map/ppermute | solution.py:66
  16.5 1.0 collective-permute-start.4
  17.5 1.5 %collective-permute-start.5 = (bf16[128,1280]{1,0:T(8,128)(2,1)S(1)}, bf16[128,1280]{1,0:T(8,128)(2,1)S(1)}, u32[]{:S(2)}, u32[]{:S(2)}) collective-permute-start(bf16[128,1280]{1,0:T(8,128)(2,1)S(1)} %collective-permute-done.2.refs_1_.refs_4_), channel_id=1, source_target_pairs={{0,4},{2,6},{4,0},{6,2},{8,12},{10,14},{12,8},{14,10},{16,20},{18,... | collective-permute-start | bytes 983048 | tf_op jit(solution)/shard_map/ppermute | solution.py:71
  19.0 4.7 %place_tokens.2.refs_2_ = bf16[2048,1024]{1,0:T(8,128)(2,1)S(1)} custom-call(f32[1,1024]{1,0:T(1,128)S(1)} %rank_tokens.1.row_ref.rank_ref, bf16[512,1024]{1,0:T(8,128)(2,1)S(1)} %bitcast.7, bf16[512,1024]{1,0:T(8,128)(2,1)} %collective-permute-done.6.refs_1_), custom_call_target="tpu_custom_call" | custom-call | bytes 4096 | tf_op jit(solution)/shard_map/place_tokens/pallas_call | solution.py:286
  23.7 3.7 %collective-permute-done.4.refs_2_.refs_5_ = bf16[128,1280]{1,0:T(8,128)(2,1)S(1)} collective-permute-done((bf16[128,1280]{1,0:T(8,128)(2,1)S(1)}, bf16[128,1280]{1,0:T(8,128)(2,1)S(1)}, u32[]{:S(2)}, u32[]{:S(2)}) %collective-permute-start.4) | collective-permute-done | bytes 327712 | tf_op jit(solution)/shard_map/ppermute | solution.py:66
  27.4 1.6 %collective-permute-start.8 = (bf16[128,1280]{1,0:T(8,128)(2,1)S(1)}, bf16[128,1280]{1,0:T(8,128)(2,1)S(1)}, u32[]{:S(2)}, u32[]{:S(2)}) collective-permute-start(bf16[128,1280]{1,0:T(8,128)(2,1)S(1)} %collective-permute-done.4.refs_2_.refs_5_), channel_id=1, source_target_pairs={{0,4},{2,6},{4,0},{6,2},{8,12},{10,14},{12,8},{14,10},{16,20},{18,... | collective-permute-start | bytes 983048 | tf_op jit(solution)/shard_map/ppermute | solution.py:71
  29.0 8.4 %collective-permute-done.7.refs_3_.refs_6_ = bf16[128,1280]{1,0:T(8,128)(2,1)S(1)} collective-permute-done((bf16[128,1280]{1,0:T(8,128)(2,1)S(1)}, bf16[128,1280]{1,0:T(8,128)(2,1)S(1)}, u32[]{:S(2)}, u32[]{:S(2)}) %collective-permute-start.7) | collective-permute-done | bytes 327712 | tf_op jit(solution)/shard_map/ppermute | solution.py:66
  37.4 1.6 %collective-permute-start.11 = (bf16[64,1280]{1,0:T(8,128)(2,1)S(1)}, bf16[64,1280]{1,0:T(8,128)(2,1)S(1)}, u32[]{:S(2)}, u32[]{:S(2)}) collective-permute-start(bf16[64,1280]{1,0:T(8,128)(2,1)S(1)} %slice.6), channel_id=1, source_target_pairs={{0,4},{2,6},{4,0},{6,2},{8,12},{10,14},{12,8},{14,10},{16,20},{18,... | collective-permute-start | bytes 491528 | tf_op jit(solution)/shard_map/ppermute | solution.py:71
  39.2 3.6 %place_tokens.3.x_ref.refs_1_ = bf16[2048,1024]{1,0:T(8,128)(2,1)S(1)} custom-call(f32[1,1024]{1,0:T(1,128)S(1)} %rank_tokens.1.row_ref.rank_ref, bf16[512,1024]{1,0:T(8,128)(2,1)S(1)} %collective-permute-done.9.refs_0_, bf16[512,1024]{1,0:T(8,128)(2,1)S(1)} %collective-permute-done.10.refs_1_, bf16[2048,1024]{1,0:T(8,128)(2,1)S(1)} %place_tokens.2.refs_2_), custom_call_target="tpu_custom_call" | custom-call | bytes 4096 | tf_op jit(solution)/shard_map/place_tokens/pallas_call | solution.py:286
  42.9 3.1 %project.1 = (f32[2048,256]{1,0:T(8,128)S(1)}, f32[256,2048]{1,0:T(8,128)S(1)}, bf16[2048,128]{1,0:T(8,128)(2,1)S(1)}) custom-call(bf16[2048,1024]{1,0:T(8,128)(2,1)S(1)} %place_tokens.3.x_ref.refs_1_, bf16[128,1280]{1,0:T(8,128)(2,1)S(1)} %reorder.3.refs_0_.refs_3_, bf16[128,1280]{1,0:T(8,128)(2,1)S(1)} %collective-permute-done.2.refs_1_.refs_4_, ...), custom_call_target="tpu_custom_call" | custom-call | bytes 4096 | tf_op jit(solution)/shard_map/project/pallas_call | solution.py:333
  46.3 3.9 %block_updates.1 = (bf16[2,2048,128]{2,1,0:T(8,128)(2,1)S(1)}, bf16[8,272,128]{2,1,0:T(8,128)(2,1)}) custom-call(f32[4,32,128]{2,1,0:T(8,128)S(1)} %hold.1.decay_ref.decay_in, f32[2048,256]{1,0:T(8,128)S(1)} %get-tuple-element.61.refs_0_, f32[256,2048]{1,0:T(8,128)S(1)} %get-tuple-element.62.refs_1_, bf16[2048,128]{1,0:T(8,128)(2,1)S(1)} %get-tuple-element.63.refs_2_, ...), custom_call_target="tpu_custom_call" | custom-call | flops 1073741824 | bytes 3145728 | tf_op jit(solution)/shard_map/block_updates/pallas_call | solution.py:431
  50.3 4.8 %all-to-all-start = ((bf16[8,272,128]{2,1,0:T(8,128)(2,1)}), bf16[8,272,128]{2,1,0:T(8,128)(2,1)S(1)}, u32[]{:S(2)}, u32[]{:S(2)}) async-start(bf16[8,272,128]{2,1,0:T(8,128)(2,1)} %get-tuple-element.64), calls=%async_computation | async-start | bytes 1114112 | tf_op jit(solution)/shard_map/all_to_all | solution.py:833
  55.8 9.1 %attend.2 = (f32[1024,256]{1,0:T(8,128)}, bf16[1024,256]{1,0:T(8,128)(2,1)}) custom-call(s32[16,4]{1,0:T(8,128)} %copy.7.refs_0_, bf16[2048,1024]{1,0:T(8,128)(2,1)} %copy-done.1, bf16[2,2048,128]{2,1,0:T(8,128)(2,1)} %copy-done.16, bf16[128,1280]{1,0:T(8,128)(2,1)} %copy-done.3, bf16[128,1280]{1,0:T(8,128)(2,1)} %copy-done.8, bf16[128,1280]{1,0:T(8,128)(2,1)} %copy-done.10, ...), custom_call_target="tpu_custom_call" | custom-call | flops 4831838208 | bytes 11534336 | tf_op jit(solution)/shard_map/attend/pallas_call | solution.py:605
  64.9 2.6 %all-to-all-done.u_ref = bf16[8,272,128]{2,1,0:T(8,128)(2,1)S(1)} async-done(((bf16[8,272,128]{2,1,0:T(8,128)(2,1)}), bf16[8,272,128]{2,1,0:T(8,128)(2,1)S(1)}, u32[]{:S(2)}, u32[]{:S(2)}) %all-to-all-start) | async-done | bytes 557088 | tf_op jit(solution)/shard_map/all_to_all | solution.py:833
  67.5 0.9 scan_states.1
  68.4 3.8 %all-to-all-start.1 = ((bf16[8,256,128]{2,1,0:T(8,128)(2,1)}), bf16[8,256,128]{2,1,0:T(8,128)(2,1)S(1)}, u32[]{:S(2)}, u32[]{:S(2)}) async-start(bf16[8,256,128]{2,1,0:T(8,128)(2,1)} %scan_states.1), calls=%async_computation.1 | async-start | bytes 1048576 | tf_op jit(solution)/shard_map/all_to_all | solution.py:833
  72.2 9.4 %attend.3 = (f32[1024,256]{1,0:T(8,128)}, bf16[1024,256]{1,0:T(8,128)(2,1)}) custom-call(s32[16,4]{1,0:T(8,128)} %copy.7.refs_0_, bf16[2048,1024]{1,0:T(8,128)(2,1)} %copy-done.1, bf16[2,2048,128]{2,1,0:T(8,128)(2,1)} %copy-done.16, bf16[128,1280]{1,0:T(8,128)(2,1)} %copy-done.3, bf16[128,1280]{1,0:T(8,128)(2,1)} %copy-done.8, bf16[128,1280]{1,0:T(8,128)(2,1)} %copy-done.10, ...), custom_call_target="tpu_custom_call" | custom-call | flops 4831838208 | bytes 11534336 | tf_op jit(solution)/shard_map/attend/pallas_call | solution.py:605
  81.6 3.7 %all-to-all-done.1 = bf16[8,256,128]{2,1,0:T(8,128)(2,1)S(1)} async-done(((bf16[8,256,128]{2,1,0:T(8,128)(2,1)}), bf16[8,256,128]{2,1,0:T(8,128)(2,1)S(1)}, u32[]{:S(2)}, u32[]{:S(2)}) %all-to-all-start.1) | async-done | bytes 524320 | tf_op jit(solution)/shard_map/all_to_all | solution.py:833
  85.3 0.8 copy-done.17
  86.1 4.5 %mix.1 = (bf16[512,256]{1,0:T(8,128)(2,1)S(1)}, bf16[512,256]{1,0:T(8,128)(2,1)S(1)}, bf16[512,256]{1,0:T(8,128)(2,1)S(1)}, bf16[512,256]{1,0:T(8,128)(2,1)S(1)}) custom-call(f32[4,32,128]{2,1,0:T(8,128)S(1)} %hold.1.decay_ref.decay_in, f32[1024,256]{1,0:T(8,128)} %get-tuple-element.68.refs_0_, f32[1024,256]{1,0:T(8,128)} %get-tuple-element.71.refs_1_, ...), custom_call_target="tpu_custom_call" | custom-call | flops 1073741824 | bytes 6291456 | tf_op jit(solution)/shard_map/mix/pallas_call | solution.py:708
  90.7 2.2 %collective-permute-start.14 = (bf16[512,256]{1,0:T(8,128)(2,1)S(1)}, bf16[512,256]{1,0:T(8,128)(2,1)S(1)}, u32[]{:S(2)}, u32[]{:S(2)}) collective-permute-start(bf16[512,256]{1,0:T(8,128)(2,1)S(1)} %get-tuple-element.76), channel_id=1, source_target_pairs={{0,1},{1,0},{2,3},{3,2},{4,5},{5,4},{6,7},{7,6},{8,9},{9,8},{10,11... | collective-permute-start | bytes 786440 | tf_op jit(solution)/shard_map/ppermute | solution.py:95
  92.9 1.2 %project_out.3.refs_1_ = f32[512,1024]{1,0:T(8,128)S(1)} custom-call(bf16[1024,1024]{1,0:T(8,128)(2,1)S(1)} %copy-done, bf16[512,256]{1,0:T(8,128)(2,1)S(1)} %get-tuple-element.77.refs_0_, bf16[512,256]{1,0:T(8,128)(2,1)S(1)} %collective-permute-done.15.refs_1_), custom_call_target="tpu_custom_call" | custom-call | bytes 2048 | tf_op jit(solution)/shard_map/project_out/pallas_call | solution.py:757
  94.1 5.9 %collective-permute-done.14.refs_0_ = bf16[512,256]{1,0:T(8,128)(2,1)S(1)} collective-permute-done((bf16[512,256]{1,0:T(8,128)(2,1)S(1)}, bf16[512,256]{1,0:T(8,128)(2,1)S(1)}, u32[]{:S(2)}, u32[]{:S(2)}) %collective-permute-start.14) | collective-permute-done | bytes 262176 | tf_op jit(solution)/shard_map/ppermute | solution.py:95
  100.0 1.5 %project_out.4.refs_1_ = f32[512,1024]{1,0:T(8,128)S(1)} custom-call(bf16[1024,1024]{1,0:T(8,128)(2,1)S(1)} %copy-done, bf16[512,256]{1,0:T(8,128)(2,1)S(1)} %collective-permute-done.14.refs_0_, f32[512,1024]{1,0:T(8,128)S(1)} %project_out.3.refs_1_), custom_call_target="tpu_custom_call" | custom-call | bytes 2048 | tf_op jit(solution)/shard_map/project_out/pallas_call | solution.py:757
  101.5 3.6 %collective-permute-done.13.refs_0_ = bf16[512,256]{1,0:T(8,128)(2,1)S(1)} collective-permute-done((bf16[512,256]{1,0:T(8,128)(2,1)S(1)}, bf16[512,256]{1,0:T(8,128)(2,1)S(1)}, u32[]{:S(2)}, u32[]{:S(2)}) %collective-permute-start.13) | collective-permute-done | bytes 262176 | tf_op jit(solution)/shard_map/ppermute | solution.py:103
  105.1 1.6 %project_out.5 = bf16[512,1024]{1,0:T(8,128)(2,1)} custom-call(bf16[1024,1024]{1,0:T(8,128)(2,1)S(1)} %copy-done, bf16[512,256]{1,0:T(8,128)(2,1)S(1)} %collective-permute-done.13.refs_0_, f32[512,1024]{1,0:T(8,128)S(1)} %project_out.4.refs_1_), custom_call_target="tpu_custom_call" | custom-call | bytes 2048 | tf_op jit(solution)/shard_map/project_out/pallas_call | solution.py:757
  (63 shorter events, 4.4 us)
Async XLA Ops:
  0.0 19.0 %copy-start.4 = (bf16[1,512,1024]{2,1,0:T(8,128)(2,1)S(1)}, bf16[1,512,1024]{2,1,0:T(8,128)(2,1)}, u32[]{:S(2)}) copy-start(bf16[1,512,1024]{2,1,0:T(8,128)(2,1)} %param.6) | copy-start | bytes 3145732
  0.0 19.0 %collective-permute-start.6 = (bf16[512,1024]{1,0:T(8,128)(2,1)}, bf16[512,1024]{1,0:T(8,128)(2,1)}, u32[]{:S(2)}, u32[]{:S(2)}) collective-permute-start(bf16[512,1024]{1,0:T(8,128)(2,1)} %bitcast.5), channel_id=1, source_target_pairs={{0,2},{2,0},{4,6},{6,4},{8,10},{10,8},{12,14},{14,12},{16,18},{18,... | collective-permute-start | bytes 3145736 | tf_op jit(solution)/shard_map/ppermute | solution.py:61
  0.5 4.1 %collective-permute-start.1 = (bf16[64,2560]{1,0:T(8,128)(2,1)}, bf16[64,2560]{1,0:T(8,128)(2,1)S(1)}, u32[]{:S(2)}, u32[]{:S(2)}) collective-permute-start(bf16[64,2560]{1,0:T(8,128)(2,1)} %refs_0_.3), channel_id=1, source_target_pairs={{0,2},{2,0},{4,6},{6,4},{8,10},{10,8},{12,14},{14,12},{16,18},{18,... | collective-permute-start | bytes 983048 | tf_op jit(solution)/shard_map/ppermute | solution.py:61
  0.5 28.5 %collective-permute-start.9 = (bf16[512,1024]{1,0:T(8,128)(2,1)}, bf16[512,1024]{1,0:T(8,128)(2,1)S(1)}, u32[]{:S(2)}, u32[]{:S(2)}) collective-permute-start(bf16[512,1024]{1,0:T(8,128)(2,1)} %bitcast.6), channel_id=1, source_target_pairs={{0,1},{1,0},{2,3},{3,2},{4,5},{5,4},{6,7},{7,6},{8,9},{9,8},{10,11... | collective-permute-start | bytes 3145736 | tf_op jit(solution)/shard_map/ppermute | solution.py:95
  4.5 7.0 %copy-start.15 = (f32[1,8,16]{2,1,0:T(8,128)S(1)}, f32[1,8,16]{2,1,0:T(8,128)}, u32[]{:S(2)}) copy-start(f32[1,8,16]{2,1,0:T(8,128)} %param.11) | copy-start | bytes 1540
  4.7 38.1 %copy-start.3 = (bf16[128,1280]{1,0:T(8,128)(2,1)}, bf16[128,1280]{1,0:T(8,128)(2,1)S(1)}, u32[]{:S(2)}) copy-start(bf16[128,1280]{1,0:T(8,128)(2,1)S(1)} %reorder.3.refs_0_.refs_3_) | copy-start | bytes 983044
  4.7 11.7 %collective-permute-start.2 = (bf16[128,1280]{1,0:T(8,128)(2,1)S(1)}, bf16[128,1280]{1,0:T(8,128)(2,1)S(1)}, u32[]{:S(2)}, u32[]{:S(2)}) collective-permute-start(bf16[128,1280]{1,0:T(8,128)(2,1)S(1)} %reorder.3.refs_0_.refs_3_), channel_id=1, source_target_pairs={{0,8},{2,10},{4,12},{6,14},{8,16},{10,18},{12,20},{14,22},{16,24},... | collective-permute-start | bytes 983048 | tf_op jit(solution)/shard_map/ppermute | solution.py:66
  6.3 10.1 %collective-permute-start.3 = (bf16[128,1280]{1,0:T(8,128)(2,1)S(1)}, bf16[128,1280]{1,0:T(8,128)(2,1)S(1)}, u32[]{:S(2)}, u32[]{:S(2)}) collective-permute-start(bf16[128,1280]{1,0:T(8,128)(2,1)S(1)} %reorder.3.refs_0_.refs_3_), channel_id=1, source_target_pairs={{0,4},{2,6},{4,0},{6,2},{8,12},{10,14},{12,8},{14,10},{16,20},{18,... | collective-permute-start | bytes 983048 | tf_op jit(solution)/shard_map/ppermute | solution.py:71
  7.8 1.4 %collective-permute-start = (f32[8,16]{1,0:T(8,128)}, f32[8,16]{1,0:T(8,128)S(1)}, u32[]{:S(2)}, u32[]{:S(2)}) collective-permute-start(f32[8,16]{1,0:T(8,128)} %bitcast.9), channel_id=1, source_target_pairs={{0,2},{2,0},{4,6},{6,4},{8,10},{10,8},{12,14},{14,12},{16,18},{18,... | collective-permute-start | bytes 1544 | tf_op jit(solution)/shard_map/ppermute | solution.py:61
  16.5 26.4 %copy-start.8 = (bf16[128,1280]{1,0:T(8,128)(2,1)}, bf16[128,1280]{1,0:T(8,128)(2,1)S(1)}, u32[]{:S(2)}) copy-start(bf16[128,1280]{1,0:T(8,128)(2,1)S(1)} %collective-permute-done.2.refs_1_.refs_4_) | copy-start | bytes 983044
  16.5 26.4 %copy-start.9 = (bf16[128,1280]{1,0:T(8,128)(2,1)}, bf16[128,1280]{1,0:T(8,128)(2,1)S(1)}, u32[]{:S(2)}) copy-start(bf16[128,1280]{1,0:T(8,128)(2,1)S(1)} %collective-permute-done.3.refs_4_.refs_7_) | copy-start | bytes 983044
  16.5 10.9 %collective-permute-start.4 = (bf16[128,1280]{1,0:T(8,128)(2,1)S(1)}, bf16[128,1280]{1,0:T(8,128)(2,1)S(1)}, u32[]{:S(2)}, u32[]{:S(2)}) collective-permute-start(bf16[128,1280]{1,0:T(8,128)(2,1)S(1)} %collective-permute-done.2.refs_1_.refs_4_), channel_id=1, source_target_pairs={{0,8},{2,10},{4,12},{6,14},{8,16},{10,18},{12,20},{14,22},{16,24},... | collective-permute-start | bytes 983048 | tf_op jit(solution)/shard_map/ppermute | solution.py:66
  17.5 9.9 %collective-permute-start.5 = (bf16[128,1280]{1,0:T(8,128)(2,1)S(1)}, bf16[128,1280]{1,0:T(8,128)(2,1)S(1)}, u32[]{:S(2)}, u32[]{:S(2)}) collective-permute-start(bf16[128,1280]{1,0:T(8,128)(2,1)S(1)} %collective-permute-done.2.refs_1_.refs_4_), channel_id=1, source_target_pairs={{0,4},{2,6},{4,0},{6,2},{8,12},{10,14},{12,8},{14,10},{16,20},{18,... | collective-permute-start | bytes 983048 | tf_op jit(solution)/shard_map/ppermute | solution.py:71
  27.4 15.5 %copy-start.10 = (bf16[128,1280]{1,0:T(8,128)(2,1)}, bf16[128,1280]{1,0:T(8,128)(2,1)S(1)}, u32[]{:S(2)}) copy-start(bf16[128,1280]{1,0:T(8,128)(2,1)S(1)} %collective-permute-done.4.refs_2_.refs_5_) | copy-start | bytes 983044
  27.4 15.5 %copy-start.11 = (bf16[128,1280]{1,0:T(8,128)(2,1)}, bf16[128,1280]{1,0:T(8,128)(2,1)S(1)}, u32[]{:S(2)}) copy-start(bf16[128,1280]{1,0:T(8,128)(2,1)S(1)} %collective-permute-done.5.refs_5_.refs_8_) | copy-start | bytes 983044
  27.4 10.0 %collective-permute-start.7 = (bf16[128,1280]{1,0:T(8,128)(2,1)S(1)}, bf16[128,1280]{1,0:T(8,128)(2,1)S(1)}, u32[]{:S(2)}, u32[]{:S(2)}) collective-permute-start(bf16[128,1280]{1,0:T(8,128)(2,1)S(1)} %collective-permute-done.4.refs_2_.refs_5_), channel_id=1, source_target_pairs={{0,8},{2,10},{4,12},{6,14},{8,16},{10,18},{12,20},{14,22},{16,24},... | collective-permute-start | bytes 983048 | tf_op jit(solution)/shard_map/ppermute | solution.py:66
  27.4 9.9 %collective-permute-start.8 = (bf16[128,1280]{1,0:T(8,128)(2,1)S(1)}, bf16[128,1280]{1,0:T(8,128)(2,1)S(1)}, u32[]{:S(2)}, u32[]{:S(2)}) collective-permute-start(bf16[128,1280]{1,0:T(8,128)(2,1)S(1)} %collective-permute-done.4.refs_2_.refs_5_), channel_id=1, source_target_pairs={{0,4},{2,6},{4,0},{6,2},{8,12},{10,14},{12,8},{14,10},{16,20},{18,... | collective-permute-start | bytes 983048 | tf_op jit(solution)/shard_map/ppermute | solution.py:71
  29.0 10.2 %collective-permute-start.10 = (bf16[512,1024]{1,0:T(8,128)(2,1)S(1)}, bf16[512,1024]{1,0:T(8,128)(2,1)S(1)}, u32[]{:S(2)}, u32[]{:S(2)}) collective-permute-start(bf16[512,1024]{1,0:T(8,128)(2,1)S(1)} %collective-permute-done.9.refs_0_), channel_id=1, source_target_pairs={{0,2},{2,0},{4,6},{6,4},{8,10},{10,8},{12,14},{14,12},{16,18},{18,... | collective-permute-start | bytes 3145736 | tf_op jit(solution)/shard_map/ppermute | solution.py:61
  37.4 5.5 %copy-start.5 = (bf16[128,1280]{1,0:T(8,128)(2,1)}, bf16[128,1280]{1,0:T(8,128)(2,1)S(1)}, u32[]{:S(2)}) copy-start(bf16[128,1280]{1,0:T(8,128)(2,1)S(1)} %collective-permute-done.7.refs_3_.refs_6_) | copy-start | bytes 983044
  37.4 5.5 %copy-start.6 = (bf16[128,1280]{1,0:T(8,128)(2,1)}, bf16[128,1280]{1,0:T(8,128)(2,1)S(1)}, u32[]{:S(2)}) copy-start(bf16[128,1280]{1,0:T(8,128)(2,1)S(1)} %collective-permute-done.8.refs_6_.refs_9_) | copy-start | bytes 983044
  37.4 8.6 %collective-permute-start.11 = (bf16[64,1280]{1,0:T(8,128)(2,1)S(1)}, bf16[64,1280]{1,0:T(8,128)(2,1)S(1)}, u32[]{:S(2)}, u32[]{:S(2)}) collective-permute-start(bf16[64,1280]{1,0:T(8,128)(2,1)S(1)} %slice.6), channel_id=1, source_target_pairs={{0,4},{2,6},{4,0},{6,2},{8,12},{10,14},{12,8},{14,10},{16,20},{18,... | collective-permute-start | bytes 491528 | tf_op jit(solution)/shard_map/ppermute | solution.py:71
  39.0 7.3 %collective-permute-start.12 = (bf16[64,1280]{1,0:T(8,128)(2,1)S(1)}, bf16[64,1280]{1,0:T(8,128)(2,1)S(1)}, u32[]{:S(2)}, u32[]{:S(2)}) collective-permute-start(bf16[64,1280]{1,0:T(8,128)(2,1)S(1)} %slice.7), channel_id=1, source_target_pairs={{0,8},{2,10},{4,12},{6,14},{8,16},{10,18},{12,20},{14,22},{16,24},... | collective-permute-start | bytes 491528 | tf_op jit(solution)/shard_map/ppermute | solution.py:66
  46.0 4.2 %copy-start.13 = (bf16[64,1280]{1,0:T(8,128)(2,1)}, bf16[64,1280]{1,0:T(8,128)(2,1)S(1)}, u32[]{:S(2)}) copy-start(bf16[64,1280]{1,0:T(8,128)(2,1)S(1)} %collective-permute-done.11.refs_3_.refs_10_) | copy-start | bytes 491524
  46.3 8.8 %copy-start.18 = (s32[16,4]{0,1:T(4,128)S(1)}, s32[16,4]{0,1:T(4,128)}, u32[]{:S(2)}) copy-start(s32[16,4]{0,1:T(4,128)} %param.10) | copy-start | bytes 772
  50.3 5.5 %copy-start.16 = (bf16[2,2048,128]{2,1,0:T(8,128)(2,1)}, bf16[2,2048,128]{2,1,0:T(8,128)(2,1)S(1)}, u32[]{:S(2)}) copy-start(bf16[2,2048,128]{2,1,0:T(8,128)(2,1)S(1)} %get-tuple-element.65.refs_2_) | copy-start | bytes 3145732
  50.3 17.2 %all-to-all-start = ((bf16[8,272,128]{2,1,0:T(8,128)(2,1)}), bf16[8,272,128]{2,1,0:T(8,128)(2,1)S(1)}, u32[]{:S(2)}, u32[]{:S(2)}) async-start(bf16[8,272,128]{2,1,0:T(8,128)(2,1)} %get-tuple-element.64), calls=%async_computation | async-start | bytes 1114112 | tf_op jit(solution)/shard_map/all_to_all | solution.py:833
  68.4 16.8 %all-to-all-start.1 = ((bf16[8,256,128]{2,1,0:T(8,128)(2,1)}), bf16[8,256,128]{2,1,0:T(8,128)(2,1)S(1)}, u32[]{:S(2)}, u32[]{:S(2)}) async-start(bf16[8,256,128]{2,1,0:T(8,128)(2,1)} %scan_states.1), calls=%async_computation.1 | async-start | bytes 1048576 | tf_op jit(solution)/shard_map/all_to_all | solution.py:833
  72.2 13.9 %copy-start.7 = (bf16[1024,256]{1,0:T(8,128)(2,1)S(1)}, bf16[1024,256]{1,0:T(8,128)(2,1)}, u32[]{:S(2)}) copy-start(bf16[1024,256]{1,0:T(8,128)(2,1)} %get-tuple-element.72.refs_2_) | copy-start | bytes 1572868
  86.1 6.9 %copy-start = (bf16[1024,1024]{1,0:T(8,128)(2,1)S(1)}, bf16[1024,1024]{1,0:T(8,128)(2,1)}, u32[]{:S(2)}) copy-start(bf16[1024,1024]{1,0:T(8,128)(2,1)} %w_ref.5) | copy-start | bytes 6291460
  90.6 2.3 %collective-permute-start.15 = (bf16[512,256]{1,0:T(8,128)(2,1)S(1)}, bf16[512,256]{1,0:T(8,128)(2,1)S(1)}, u32[]{:S(2)}, u32[]{:S(2)}) collective-permute-start(bf16[512,256]{1,0:T(8,128)(2,1)S(1)} %get-tuple-element.78), channel_id=1, source_target_pairs={{0,2},{2,0},{4,6},{6,4},{8,10},{10,8},{12,14},{14,12},{16,18},{18,... | collective-permute-start | bytes 786440 | tf_op jit(solution)/shard_map/ppermute | solution.py:61
  90.7 9.3 %collective-permute-start.14 = (bf16[512,256]{1,0:T(8,128)(2,1)S(1)}, bf16[512,256]{1,0:T(8,128)(2,1)S(1)}, u32[]{:S(2)}, u32[]{:S(2)}) collective-permute-start(bf16[512,256]{1,0:T(8,128)(2,1)S(1)} %get-tuple-element.76), channel_id=1, source_target_pairs={{0,1},{1,0},{2,3},{3,2},{4,5},{5,4},{6,7},{7,6},{8,9},{9,8},{10,11... | collective-permute-start | bytes 786440 | tf_op jit(solution)/shard_map/ppermute | solution.py:95
  92.9 12.3 %collective-permute-start.13 = (bf16[512,256]{1,0:T(8,128)(2,1)S(1)}, bf16[512,256]{1,0:T(8,128)(2,1)S(1)}, u32[]{:S(2)}, u32[]{:S(2)}) collective-permute-start(bf16[512,256]{1,0:T(8,128)(2,1)S(1)} %get-tuple-element.75), channel_id=1, source_target_pairs={{0,3},{1,2},{2,1},{3,0},{4,7},{5,6},{6,5},{7,4},{8,11},{9,10},{10,... | collective-permute-start | bytes 786440 | tf_op jit(solution)/shard_map/ppermute | solution.py:103
  (5 other events, 10.2 us)

commit v16 on v15

--- a/solution.py
+++ b/solution.py
@@ -259,43 +259,46 @@
     return jnp.where(places.astype(f32) == rank, 1.0, 0.0).astype(bf16)
 
 
-def place_kernel(merge, parts, start, rank_ref, *refs):
-    frame_refs, refs = refs[:parts], refs[parts:]
+def place_kernel(slots, parts, start, rank_ref, *refs):
+    frame_refs, refs = refs[: len(slots) * parts], refs[len(slots) * parts :]
     base_refs, (x_ref, normed) = refs[:-2], refs[-2:]
     tokens = rank_ref.shape[1]
     count = normed.shape[1]
     step = 256
-    at = 0
-    for ref in frame_refs:
-        normalise(ref, normed.at[at // count], at % count)
-        at += ref.shape[0]
+    for i in range(len(slots)):
+        at = 0
+        for ref in frame_refs[i * parts : (i + 1) * parts]:
+            rows = ref.shape[0]
+            normalise(ref, normed.at[i], at)
+            at += rows
     for at in range(0, tokens, step):
         pick = picks(rank_ref[:, start : start + count], at, step)
-        for s in range(merge):
-            there = slice(s * tokens + at, s * tokens + at + step)
-            placed = jnp.dot(pick, normed[s], preferred_element_type=f32).astype(bf16)
+        for i, slot in enumerate(slots):
+            placed = jnp.dot(pick, normed[i], preferred_element_type=f32).astype(bf16)
             for base in base_refs:
-                placed = base[there, :] + placed
-            x_ref[there, :] = placed
-
-
-def place_tokens(plan, rank, start, frames, base):
+                placed = base[slot * tokens + at : slot * tokens + at + step, :] + placed
+            x_ref[i * tokens + at : i * tokens + at + step, :] = placed
+
+
+def place_tokens(slots, rank, start, frames, base):
     tokens = rank.shape[1]
     width = frames[0].shape[1]
-    count = sum(f.shape[0] for f in frames) // plan.merge
-    return pl.pallas_call(
-        functools.partial(place_kernel, plan.merge, len(frames), start),
-        out_shape=jax.ShapeDtypeStruct((plan.merge * tokens, width), bf16),
-        scratch_shapes=[pltpu.VMEM((plan.merge, count, width), bf16)],
+    parts = len(frames) // len(slots)
+    count = parts * frames[0].shape[0]
+    return pl.pallas_call(
+        functools.partial(place_kernel, slots, parts, start),
+        out_shape=jax.ShapeDtypeStruct((len(slots) * tokens, width), bf16),
+        scratch_shapes=[pltpu.VMEM((len(slots), count, width), bf16)],
         compiler_params=params(),
         cost_estimate=cost(0, 4 * tokens),
         name="place_tokens",
     )(rank, *frames, *base)
 
 
-def project_kernel(plan, x_ref, *refs):
+def project_kernel(plan, *refs):
+    x_refs, refs = refs[: plan.merge], refs[plan.merge :]
     w_refs, (v_ref, b_ref, rest_ref, w, turned) = refs[:-5], refs[-5:]
-    every = x_ref.shape[0]
+    tokens, width = x_refs[0].shape
     step = 256
     cols = plan.pairs * LANES
     if len(w_refs) > 1:
@@ -311,23 +314,24 @@
         ],
         axis=1,
     )
-    for at in range(0, every, step):
-        x = x_ref[at : at + step, :]
-        v_ref[at : at + step, :] = jnp.dot(x, w[...], preferred_element_type=f32)
-        b_ref[:, at : at + step] = lax.dot_general(
-            maps, x, (((1,), (1,)), ((), ())), preferred_element_type=f32
-        )
     count = rest_ref.shape[1]
     there = plan.last_chip() * count
-    for at in range(0, every, step):
-        rest = x_ref[at : at + step, :count]
-        for c in range(count, x_ref.shape[1], count):
-            rest = jnp.where(there == c, x_ref[at : at + step, c : c + count], rest)
-        rest_ref[at : at + step, :] = rest
+    for s, x_ref in enumerate(x_refs):
+        for at in range(0, tokens, step):
+            rows = slice(s * tokens + at, s * tokens + at + step)
+            x = x_ref[at : at + step, :]
+            v_ref[rows, :] = jnp.dot(x, w[...], preferred_element_type=f32)
+            b_ref[:, rows] = lax.dot_general(
+                maps, x, (((1,), (1,)), ((), ())), preferred_element_type=f32
+            )
+            rest = x[:, :count]
+            for c in range(count, width, count):
+                rest = jnp.where(there == c, x[:, c : c + count], rest)
+            rest_ref[rows, :] = rest
 
 
 def project(plan, x, weights):
-    every, width = x.shape
+    every, width = x[0].shape[0] * plan.merge, x[0].shape[1]
     cols = plan.pairs * LANES
     count = max(LANES, width // plan.chips)
     return pl.pallas_call(
@@ -341,7 +345,7 @@
         compiler_params=params(),
         cost_estimate=cost(0, 4 * width),
         name="project",
-    )(x, *weights)
+    )(*x, *weights)
 
 
 def update_kernel(plan, groups, decay_ref, *refs):
@@ -521,8 +525,7 @@
         weights.append(copies.start(ref.at[:, 2 * wide :], w.at[rows, wide:]))
     arriving = []
     for at in range(0, tokens, step):
-        from_ = slice(slot * tokens + at, slot * tokens + at + step)
-        arriving.append(copies.start(x_in.at[from_], x.at[at : at + step]))
+        arriving.append(copies.start(x_in.at[at : at + step], x.at[at : at + step]))
     later = copies.start(local_in.at[slot], local)
 
     same = lax.div(lax.broadcasted_iota(jnp.int32, (2 * LANES, 2 * LANES), 0), HD) == lax.div(
@@ -597,9 +600,9 @@
 
 
 def attend(plan, slot, lists, x, weights, local):
-    every, width = x.shape
+    tokens, width = x.shape
+    every = tokens * plan.merge
     groups, chosen = lists.shape
-    tokens = every // plan.merge
     block = tokens // groups
     cols = plan.pairs * LANES
     return pl.pallas_call(
@@ -643,21 +646,19 @@
 def mix_kernel(plan, groups, decay_in, *refs):
     a_ins, refs = refs[: plan.merge], refs[plan.merge :]
     c_ins, refs = refs[: plan.merge], refs[plan.merge :]
-    s_in, back_in, refs = refs[0], refs[1], refs[2:]
-    out_refs, (decay, a, c, state, back, mixed, out, sems) = refs[:-8], refs[-8:]
+    state, back_in, refs = refs[0], refs[1], refs[2:]
+    out_refs, (decay, a, c, back, mixed, out, sems) = refs[:-7], refs[-7:]
     copies = Copies(sems)
     tokens = back.shape[0]
     block = tokens // groups
     width = a.shape[2]
     here = groups // 4
-    many = here * plan.pairs * N
 
     arriving = []
     decaying = copies.start(decay_in, decay)
     for i in range(4):
         rows = slice(i * here * block, (i + 1) * here * block)
-        items = slice(i * many, (i + 1) * many)
-        arriving.append([copies.start(s_in.at[items], state.at[items])])
+        arriving.append([])
         for s in range(plan.merge):
             arriving[-1] += [
                 copies.start(c_ins[s].at[rows], c.at[s, rows, :]),
@@ -707,14 +708,13 @@
     count = plan.merge * plan.peers
     return pl.pallas_call(
         functools.partial(mix_kernel, plan, groups),
-        in_specs=[hbm] * (2 * plan.merge + 3),
+        in_specs=[hbm] * (2 * plan.merge + 1) + [vmem, hbm],
         out_specs=(hbm,) * count,
         out_shape=(jax.ShapeDtypeStruct((tokens // plan.peers, width), bf16),) * count,
         scratch_shapes=[
             pltpu.VMEM(decays.shape, f32),
             pltpu.VMEM((plan.merge, tokens, width), f32),
             pltpu.VMEM((plan.merge, tokens, width), bf16),
-            pltpu.VMEM(state.shape, bf16),
             pltpu.VMEM(back.shape, bf16),
             pltpu.VMEM((tokens, plan.merge * width), bf16),
             pltpu.VMEM((count, tokens // plan.peers, width), bf16),
@@ -785,10 +785,10 @@
     tables = decay_tables(plan, rates, groups)
     rank = rank_tokens(ids, groups)
 
-    def fill(arriving, part):
-        if plan.merge == 2:
-            arriving = arriving + [plan.swap(tokens) for tokens in arriving]
-        return place_tokens(plan, rank, local_tokens, arriving, [part])
+    def fill(slot, arriving, part):
+        if slot == 1:
+            arriving = [plan.swap(tokens) for tokens in arriving]
+        return place_tokens([slot], rank, local_tokens, arriving, [part])
 
     if plan.ringed:
         blocks, crossed = [block], []
@@ -800,15 +800,17 @@
                 with_ = (places, tables)
             if k == min(1, plan.along - 2):
                 rank, owns, _ = lax.optimization_barrier((rank, owns, blocks[-1]))
-                part = with_ = place_tokens(plan, rank, 0, owns, [])
+                part = with_ = place_tokens(list(range(plan.merge)), rank, 0, owns, [])
             if k == plan.along - 2:
                 arriving, _ = lax.optimization_barrier((arriving, blocks[-1]))
-                x = fill(arriving, part)
+                x = [fill(s, arriving, part) for s in range(plan.merge)]
             passed, across, with_ = lax.optimization_barrier(
                 (plan.round(blocks[-1]), plan.cross(blocks[-1]), with_)
             )
             if k == plan.along - 2:
-                tables, passed, across = lax.optimization_barrier((tables, passed, across))
+                tables, passed, across, x[0] = lax.optimization_barrier(
+                    (tables, passed, across, x[0])
+                )
                 tables, passed, across = lax.optimization_barrier(
                     (hold(tables), passed, across)
                 )
@@ -821,7 +823,8 @@
             lax.all_gather(block, "tm", axis=0, tiled=True, axis_index_groups=plan.groups())
         ]
         places = back_tokens(rank)
-        x = fill(arriving, place_tokens(plan, rank, 0, owns, []))
+        part = place_tokens(list(range(plan.merge)), rank, 0, owns, [])
+        x = [fill(s, arriving, part) for s in range(plan.merge)]
     if plan.ringed:
         v, b, x_last = project(plan, x, weights[:-2])
         local, total = block_updates(plan, tables, v, b, x_last, last, groups)
@@ -837,12 +840,12 @@
 
     share = local.shape[1] // plan.chips
     arrived = exchange(total)
-    attended = [attend(plan, 0, block_lists, x, weights, local)]
+    attended = [attend(plan, 0, block_lists, x[0], weights, local)]
     arrived, attended = lax.optimization_barrier((arrived, attended))
     states = scan_states(plan, arrived, share)
     x, states = lax.optimization_barrier((x, states))
     if plan.merge == 2:
-        attended.append(attend(plan, 1, block_lists, x, weights, local))
+        attended.append(attend(plan, 1, block_lists, x[1], weights, local))
     state = exchange(states).reshape(-1, LANES)
 
     bases, readers = ([a[i] for a in attended] for i in range(2))

time: 107 us -> 109 us (1.019)
  starting transfers between devices: 23.4 us -> 21.9 us
  waiting for transfers between devices: 33 us -> 34.1 us
    ppermute x2, starting transfers between devices: 5.13 us -> 3.85 us  [to_peer(): return lax.ppermute(block, 'head', pairs)]
    pallas_call x2 -> x3, Pallas kernels: 8.25 us -> 7.18 us  [place_tokens(): pl.pallas_call(functools.partial(place_kernel, slots, parts, start), out_...]
    unnamed x39 -> x37, local copies, waits for them, and re-layouts: 3.88 us -> 4.81 us
where the time goes in v16:
time: 109 us; the launch traced here: 108 us
  Pallas kernels  46.1 us (42%)
  waiting for transfers between devices  34.1 us (31%)
  starting transfers between devices  21.9 us (20%)
  local copies, waits for them, and re-layouts  4.83 us (4%)
    pallas_call x2, Pallas kernels, attend(): pl.pallas_call(functools.partial(attend_kernel, plan, slot), in_specs=[sm...  18.4 us
    ppermute x4, waiting for transfers between devices, round(): return lax.ppermute(block, 'tm', pairs)  17.6 us
    all_to_all x2, starting transfers between devices, exchange(): lax.all_to_all(blocks, 'tm', split_axis=0, concat_axis=0, tiled=True, axi...  8.13 us
    pallas_call x3, Pallas kernels, place_tokens(): pl.pallas_call(functools.partial(place_kernel, slots, parts, start), out_...  7.18 us
    all_to_all x2, waiting for transfers between devices, exchange(): lax.all_to_all(blocks, 'tm', split_axis=0, concat_axis=0, tiled=True, axi...  6.61 us
    ppermute x2, waiting for transfers between devices, to_peer(): return lax.ppermute(block, 'head', pairs)  6.14 us
    pallas_call x1, Pallas kernels, mix(): pl.pallas_call(functools.partial(mix_kernel, plan, groups), in_specs=[hbm...  5.52 us
    ppermute x4, starting transfers between devices, cross(): return lax.ppermute(block, 'tm', pairs)  5.39 us
  transfers between devices with their start and end apart: 18, of which 9 were waited for; matrix products, arithmetic and copies ran while one was open for 1% of the time, Pallas kernels for 32%

profile of v16, /device:TPU:0, one launch (start us, length us, event | category | flops | bytes accessed | tf_op | source)
XLA Modules:
  0.0 108.2 jit_solution(676508074875837663)
XLA Ops:
  0.5 3.0 %collective-permute-start.9 = (bf16[512,1024]{1,0:T(8,128)(2,1)}, bf16[512,1024]{1,0:T(8,128)(2,1)S(1)}, u32[]{:S(2)}, u32[]{:S(2)}) collective-permute-start(bf16[512,1024]{1,0:T(8,128)(2,1)} %bitcast.6), channel_id=1, source_target_pairs={{0,1},{1,0},{2,3},{3,2},{4,5},{5,4},{6,7},{7,6},{8,9},{9,8},{10,11... | collective-permute-start | bytes 3145736 | tf_op jit(solution)/shard_map/ppermute | solution.py:95
  3.5 1.0 copy-done.11
  4.7 1.8 %collective-permute-start.2 = (bf16[128,1280]{1,0:T(8,128)(2,1)S(1)}, bf16[128,1280]{1,0:T(8,128)(2,1)}, u32[]{:S(2)}, u32[]{:S(2)}) collective-permute-start(bf16[128,1280]{1,0:T(8,128)(2,1)S(1)} %reorder.3.refs_2_.refs_3_), channel_id=1, source_target_pairs={{0,8},{2,10},{4,12},{6,14},{8,16},{10,18},{12,20},{14,22},{16,24},... | collective-permute-start | bytes 983048 | tf_op jit(solution)/shard_map/ppermute | solution.py:66
  6.6 1.5 %collective-permute-start.3 = (bf16[128,1280]{1,0:T(8,128)(2,1)S(1)}, bf16[128,1280]{1,0:T(8,128)(2,1)}, u32[]{:S(2)}, u32[]{:S(2)}) collective-permute-start(bf16[128,1280]{1,0:T(8,128)(2,1)S(1)} %reorder.3.refs_2_.refs_3_), channel_id=1, source_target_pairs={{0,4},{2,6},{4,0},{6,2},{8,12},{10,14},{12,8},{14,10},{16,20},{18,... | collective-permute-start | bytes 983048 | tf_op jit(solution)/shard_map/ppermute | solution.py:71
  10.2 1.4 %copy-done.3 = bf16[1024,1024]{1,0:T(8,128)(2,1)} copy-done((bf16[1024,1024]{1,0:T(8,128)(2,1)}, bf16[1024,1024]{1,0:T(8,128)(2,1)S(1)}, u32[]{:S(2)}) %copy-start.3) | copy-done | bytes 2097176
  12.4 4.3 %collective-permute-done.2.refs_3_.refs_4_ = bf16[128,1280]{1,0:T(8,128)(2,1)} collective-permute-done((bf16[128,1280]{1,0:T(8,128)(2,1)S(1)}, bf16[128,1280]{1,0:T(8,128)(2,1)}, u32[]{:S(2)}, u32[]{:S(2)}) %collective-permute-start.2) | collective-permute-done | bytes 327712 | tf_op jit(solution)/shard_map/ppermute | solution.py:66
  16.7 1.0 collective-permute-start.4
  17.7 1.5 %collective-permute-start.5 = (bf16[128,1280]{1,0:T(8,128)(2,1)}, bf16[128,1280]{1,0:T(8,128)(2,1)S(1)}, u32[]{:S(2)}, u32[]{:S(2)}) collective-permute-start(bf16[128,1280]{1,0:T(8,128)(2,1)} %collective-permute-done.2.refs_3_.refs_4_), channel_id=1, source_target_pairs={{0,4},{2,6},{4,0},{6,2},{8,12},{10,14},{12,8},{14,10},{16,20},{18,... | collective-permute-start | bytes 983048 | tf_op jit(solution)/shard_map/ppermute | solution.py:71
  19.2 3.5 %place_tokens.3.refs_1_ = bf16[2048,1024]{1,0:T(8,128)(2,1)S(1)} custom-call(f32[1,1024]{1,0:T(1,128)S(1)} %rank_tokens.1.row_ref.rank_ref, bf16[512,1024]{1,0:T(8,128)(2,1)S(1)} %bitcast.7, bf16[512,1024]{1,0:T(8,128)(2,1)S(1)} %collective-permute-done.6.refs_1_), custom_call_target="tpu_custom_call" | custom-call | bytes 4096 | tf_op jit(solution)/shard_map/place_tokens/pallas_call | solution.py:288
  22.7 5.2 %collective-permute-done.4.refs_4_.refs_5_ = bf16[128,1280]{1,0:T(8,128)(2,1)S(1)} collective-permute-done((bf16[128,1280]{1,0:T(8,128)(2,1)}, bf16[128,1280]{1,0:T(8,128)(2,1)S(1)}, u32[]{:S(2)}, u32[]{:S(2)}) %collective-permute-start.4) | collective-permute-done | bytes 327712 | tf_op jit(solution)/shard_map/ppermute | solution.py:66
  28.0 1.3 %collective-permute-start.8 = (bf16[128,1280]{1,0:T(8,128)(2,1)S(1)}, bf16[128,1280]{1,0:T(8,128)(2,1)S(1)}, u32[]{:S(2)}, u32[]{:S(2)}) collective-permute-start(bf16[128,1280]{1,0:T(8,128)(2,1)S(1)} %collective-permute-done.4.refs_4_.refs_5_), channel_id=1, source_target_pairs={{0,4},{2,6},{4,0},{6,2},{8,12},{10,14},{12,8},{14,10},{16,20},{18,... | collective-permute-start | bytes 983048 | tf_op jit(solution)/shard_map/ppermute | solution.py:71
  29.3 1.9 %place_tokens.4.refs_0_.refs_1_ = bf16[1024,1024]{1,0:T(8,128)(2,1)S(1)} custom-call(f32[1,1024]{1,0:T(1,128)S(1)} %rank_tokens.1.row_ref.rank_ref, bf16[512,1024]{1,0:T(8,128)(2,1)S(1)} %collective-permute-done.9.refs_0_, bf16[2048,1024]{1,0:T(8,128)(2,1)S(1)} %place_tokens.3.refs_1_), custom_call_target="tpu_custom_call" | custom-call | bytes 4096 | tf_op jit(solution)/shard_map/place_tokens/pallas_call | solution.py:288
  31.2 6.9 %collective-permute-done.7.refs_5_.refs_6_ = bf16[128,1280]{1,0:T(8,128)(2,1)S(1)} collective-permute-done((bf16[128,1280]{1,0:T(8,128)(2,1)S(1)}, bf16[128,1280]{1,0:T(8,128)(2,1)S(1)}, u32[]{:S(2)}, u32[]{:S(2)}) %collective-permute-start.7) | collective-permute-done | bytes 327712 | tf_op jit(solution)/shard_map/ppermute | solution.py:66
  38.1 1.1 collective-permute-start.11
  39.3 1.9 %place_tokens.5.refs_1_ = bf16[1024,1024]{1,0:T(8,128)(2,1)S(1)} custom-call(f32[1,1024]{1,0:T(1,128)S(1)} %rank_tokens.1.row_ref.rank_ref, bf16[512,1024]{1,0:T(8,128)(2,1)S(1)} %collective-permute-done.10.refs_0_, bf16[2048,1024]{1,0:T(8,128)(2,1)S(1)} %place_tokens.3.refs_1_), custom_call_target="tpu_custom_call" | custom-call | bytes 4096 | tf_op jit(solution)/shard_map/place_tokens/pallas_call | solution.py:288
  41.2 4.0 %project.1 = (f32[2048,256]{1,0:T(8,128)S(1)}, f32[256,2048]{1,0:T(8,128)S(1)}, bf16[2048,128]{1,0:T(8,128)(2,1)S(1)}) custom-call(bf16[1024,1024]{1,0:T(8,128)(2,1)S(1)} %place_tokens.4.refs_0_.refs_1_, bf16[1024,1024]{1,0:T(8,128)(2,1)S(1)} %place_tokens.5.refs_1_, bf16[128,1280]{1,0:T(8,128)(2,1)S(1)} %reorder.3.refs_2_.refs_3_, ...), custom_call_target="tpu_custom_call" | custom-call | bytes 4096 | tf_op jit(solution)/shard_map/project/pallas_call | solution.py:337
  45.3 1.1 %collective-permute-done.12.refs_4_.refs_11_ = bf16[64,1280]{1,0:T(8,128)(2,1)S(1)} collective-permute-done((bf16[64,1280]{1,0:T(8,128)(2,1)S(1)}, bf16[64,1280]{1,0:T(8,128)(2,1)S(1)}, u32[]{:S(2)}, u32[]{:S(2)}) %collective-permute-start.12) | collective-permute-done | bytes 163872 | tf_op jit(solution)/shard_map/ppermute | solution.py:66
  46.4 3.9 %block_updates.1 = (bf16[2,2048,128]{2,1,0:T(8,128)(2,1)S(1)}, bf16[8,272,128]{2,1,0:T(8,128)(2,1)}) custom-call(f32[4,32,128]{2,1,0:T(8,128)S(1)} %hold.1.decay_ref.decay_in, f32[2048,256]{1,0:T(8,128)S(1)} %get-tuple-element.63.refs_0_, f32[256,2048]{1,0:T(8,128)S(1)} %get-tuple-element.64.refs_1_, bf16[2048,128]{1,0:T(8,128)(2,1)S(1)} %get-tuple-element.65.refs_2_, ...), custom_call_target="tpu_custom_call" | custom-call | flops 1073741824 | bytes 3145728 | tf_op jit(solution)/shard_map/block_updates/pallas_call | solution.py:435
  50.4 1.0 copy-done.15
  51.3 4.5 %all-to-all-start = ((bf16[8,272,128]{2,1,0:T(8,128)(2,1)}), bf16[8,272,128]{2,1,0:T(8,128)(2,1)S(1)}, u32[]{:S(2)}, u32[]{:S(2)}) async-start(bf16[8,272,128]{2,1,0:T(8,128)(2,1)} %get-tuple-element.66), calls=%async_computation | async-start | bytes 1114112 | tf_op jit(solution)/shard_map/all_to_all | solution.py:836
  56.5 9.1 %attend.2 = (f32[1024,256]{1,0:T(8,128)}, bf16[1024,256]{1,0:T(8,128)(2,1)}) custom-call(s32[16,4]{1,0:T(8,128)} %copy.7.refs_0_, bf16[1024,1024]{1,0:T(8,128)(2,1)} %copy-done.2, bf16[2,2048,128]{2,1,0:T(8,128)(2,1)} %copy-done.15, bf16[128,1280]{1,0:T(8,128)(2,1)} %copy-done.4, bf16[128,1280]{1,0:T(8,128)(2,1)} %collective-permute-done.2.refs_3_.refs_4_, ...), custom_call_target="tpu_custom_call" | custom-call | flops 4831838208 | bytes 11534336 | tf_op jit(solution)/shard_map/attend/pallas_call | solution.py:608
  65.6 2.8 %all-to-all-done.u_ref = bf16[8,272,128]{2,1,0:T(8,128)(2,1)S(1)} async-done(((bf16[8,272,128]{2,1,0:T(8,128)(2,1)}), bf16[8,272,128]{2,1,0:T(8,128)(2,1)S(1)}, u32[]{:S(2)}, u32[]{:S(2)}) %all-to-all-start) | async-done | bytes 557088 | tf_op jit(solution)/shard_map/all_to_all | solution.py:836
  69.3 3.7 %all-to-all-start.1 = ((bf16[8,256,128]{2,1,0:T(8,128)(2,1)}), bf16[8,256,128]{2,1,0:T(8,128)(2,1)S(1)}, u32[]{:S(2)}, u32[]{:S(2)}) async-start(bf16[8,256,128]{2,1,0:T(8,128)(2,1)} %scan_states.1), calls=%async_computation.1 | async-start | bytes 1048576 | tf_op jit(solution)/shard_map/all_to_all | solution.py:836
  73.0 9.3 %attend.3 = (f32[1024,256]{1,0:T(8,128)}, bf16[1024,256]{1,0:T(8,128)(2,1)}) custom-call(s32[16,4]{1,0:T(8,128)} %copy.7.refs_0_, bf16[1024,1024]{1,0:T(8,128)(2,1)} %copy-done.1, bf16[2,2048,128]{2,1,0:T(8,128)(2,1)} %copy-done.15, bf16[128,1280]{1,0:T(8,128)(2,1)} %copy-done.4, bf16[128,1280]{1,0:T(8,128)(2,1)} %collective-permute-done.2.refs_3_.refs_4_, ...), custom_call_target="tpu_custom_call" | custom-call | flops 4831838208 | bytes 11534336 | tf_op jit(solution)/shard_map/attend/pallas_call | solution.py:608
  82.3 3.8 %all-to-all-done.1 = bf16[8,256,128]{2,1,0:T(8,128)(2,1)S(1)} async-done(((bf16[8,256,128]{2,1,0:T(8,128)(2,1)}), bf16[8,256,128]{2,1,0:T(8,128)(2,1)S(1)}, u32[]{:S(2)}, u32[]{:S(2)}) %all-to-all-start.1) | async-done | bytes 524320 | tf_op jit(solution)/shard_map/all_to_all | solution.py:836
  86.9 5.5 %mix.1 = (bf16[512,256]{1,0:T(8,128)(2,1)S(1)}, bf16[512,256]{1,0:T(8,128)(2,1)S(1)}, bf16[512,256]{1,0:T(8,128)(2,1)S(1)}, bf16[512,256]{1,0:T(8,128)(2,1)S(1)}) custom-call(f32[4,32,128]{2,1,0:T(8,128)S(1)} %hold.1.decay_ref.decay_in, f32[1024,256]{1,0:T(8,128)} %get-tuple-element.70.refs_0_, f32[1024,256]{1,0:T(8,128)} %get-tuple-element.73.refs_1_, ...), custom_call_target="tpu_custom_call" | custom-call | flops 1073741824 | bytes 6291456 | tf_op jit(solution)/shard_map/mix/pallas_call | solution.py:709
  93.4 1.0 collective-permute-start.13
  94.4 1.2 %project_out.3.refs_1_ = f32[512,1024]{1,0:T(8,128)S(1)} custom-call(bf16[1024,1024]{1,0:T(8,128)(2,1)S(1)} %copy-done, bf16[512,256]{1,0:T(8,128)(2,1)S(1)} %get-tuple-element.79.refs_0_, bf16[512,256]{1,0:T(8,128)(2,1)S(1)} %collective-permute-done.15.refs_1_), custom_call_target="tpu_custom_call" | custom-call | bytes 2048 | tf_op jit(solution)/shard_map/project_out/pallas_call | solution.py:757
  95.6 6.1 %collective-permute-done.14.refs_0_ = bf16[512,256]{1,0:T(8,128)(2,1)S(1)} collective-permute-done((bf16[512,256]{1,0:T(8,128)(2,1)S(1)}, bf16[512,256]{1,0:T(8,128)(2,1)S(1)}, u32[]{:S(2)}, u32[]{:S(2)}) %collective-permute-start.14) | collective-permute-done | bytes 262176 | tf_op jit(solution)/shard_map/ppermute | solution.py:95
  101.7 1.5 %project_out.4.refs_1_ = f32[512,1024]{1,0:T(8,128)S(1)} custom-call(bf16[1024,1024]{1,0:T(8,128)(2,1)S(1)} %copy-done, bf16[512,256]{1,0:T(8,128)(2,1)S(1)} %collective-permute-done.14.refs_0_, f32[512,1024]{1,0:T(8,128)S(1)} %project_out.3.refs_1_), custom_call_target="tpu_custom_call" | custom-call | bytes 2048 | tf_op jit(solution)/shard_map/project_out/pallas_call | solution.py:757
  103.2 3.2 %collective-permute-done.13.refs_0_ = bf16[512,256]{1,0:T(8,128)(2,1)S(1)} collective-permute-done((bf16[512,256]{1,0:T(8,128)(2,1)S(1)}, bf16[512,256]{1,0:T(8,128)(2,1)S(1)}, u32[]{:S(2)}, u32[]{:S(2)}) %collective-permute-start.13) | collective-permute-done | bytes 262176 | tf_op jit(solution)/shard_map/ppermute | solution.py:103
  106.4 1.6 %project_out.5 = bf16[512,1024]{1,0:T(8,128)(2,1)} custom-call(bf16[1024,1024]{1,0:T(8,128)(2,1)S(1)} %copy-done, bf16[512,256]{1,0:T(8,128)(2,1)S(1)} %collective-permute-done.13.refs_0_, f32[512,1024]{1,0:T(8,128)S(1)} %project_out.4.refs_1_), custom_call_target="tpu_custom_call" | custom-call | bytes 2048 | tf_op jit(solution)/shard_map/project_out/pallas_call | solution.py:757
  (62 shorter events, 7.2 us)
Async XLA Ops:
  0.0 19.2 %copy-start.5 = (bf16[1,512,1024]{2,1,0:T(8,128)(2,1)S(1)}, bf16[1,512,1024]{2,1,0:T(8,128)(2,1)}, u32[]{:S(2)}) copy-start(bf16[1,512,1024]{2,1,0:T(8,128)(2,1)} %param.6) | copy-start | bytes 3145732
  0.0 19.2 %collective-permute-start.6 = (bf16[512,1024]{1,0:T(8,128)(2,1)}, bf16[512,1024]{1,0:T(8,128)(2,1)S(1)}, u32[]{:S(2)}, u32[]{:S(2)}) collective-permute-start(bf16[512,1024]{1,0:T(8,128)(2,1)} %bitcast.5), channel_id=1, source_target_pairs={{0,2},{2,0},{4,6},{6,4},{8,10},{10,8},{12,14},{14,12},{16,18},{18,... | collective-permute-start | bytes 3145736 | tf_op jit(solution)/shard_map/ppermute | solution.py:61
  0.5 4.1 %collective-permute-start.1 = (bf16[64,2560]{1,0:T(8,128)(2,1)}, bf16[64,2560]{1,0:T(8,128)(2,1)S(1)}, u32[]{:S(2)}, u32[]{:S(2)}) collective-permute-start(bf16[64,2560]{1,0:T(8,128)(2,1)} %refs_0_.3), channel_id=1, source_target_pairs={{0,2},{2,0},{4,6},{6,4},{8,10},{10,8},{12,14},{14,12},{16,18},{18,... | collective-permute-start | bytes 983048 | tf_op jit(solution)/shard_map/ppermute | solution.py:61
  0.5 28.8 %collective-permute-start.9 = (bf16[512,1024]{1,0:T(8,128)(2,1)}, bf16[512,1024]{1,0:T(8,128)(2,1)S(1)}, u32[]{:S(2)}, u32[]{:S(2)}) collective-permute-start(bf16[512,1024]{1,0:T(8,128)(2,1)} %bitcast.6), channel_id=1, source_target_pairs={{0,1},{1,0},{2,3},{3,2},{4,5},{5,4},{6,7},{7,6},{8,9},{9,8},{10,11... | collective-permute-start | bytes 3145736 | tf_op jit(solution)/shard_map/ppermute | solution.py:95
  4.5 7.1 %copy-start.14 = (f32[1,8,16]{2,1,0:T(8,128)S(1)}, f32[1,8,16]{2,1,0:T(8,128)}, u32[]{:S(2)}) copy-start(f32[1,8,16]{2,1,0:T(8,128)} %param.11) | copy-start | bytes 1540
  4.7 36.5 %copy-start.4 = (bf16[128,1280]{1,0:T(8,128)(2,1)}, bf16[128,1280]{1,0:T(8,128)(2,1)S(1)}, u32[]{:S(2)}) copy-start(bf16[128,1280]{1,0:T(8,128)(2,1)S(1)} %reorder.3.refs_2_.refs_3_) | copy-start | bytes 983044
  4.7 12.0 %collective-permute-start.2 = (bf16[128,1280]{1,0:T(8,128)(2,1)S(1)}, bf16[128,1280]{1,0:T(8,128)(2,1)}, u32[]{:S(2)}, u32[]{:S(2)}) collective-permute-start(bf16[128,1280]{1,0:T(8,128)(2,1)S(1)} %reorder.3.refs_2_.refs_3_), channel_id=1, source_target_pairs={{0,8},{2,10},{4,12},{6,14},{8,16},{10,18},{12,20},{14,22},{16,24},... | collective-permute-start | bytes 983048 | tf_op jit(solution)/shard_map/ppermute | solution.py:66
  6.6 10.1 %collective-permute-start.3 = (bf16[128,1280]{1,0:T(8,128)(2,1)S(1)}, bf16[128,1280]{1,0:T(8,128)(2,1)}, u32[]{:S(2)}, u32[]{:S(2)}) collective-permute-start(bf16[128,1280]{1,0:T(8,128)(2,1)S(1)} %reorder.3.refs_2_.refs_3_), channel_id=1, source_target_pairs={{0,4},{2,6},{4,0},{6,2},{8,12},{10,14},{12,8},{14,10},{16,20},{18,... | collective-permute-start | bytes 983048 | tf_op jit(solution)/shard_map/ppermute | solution.py:71
  8.0 1.4 %collective-permute-start = (f32[8,16]{1,0:T(8,128)}, f32[8,16]{1,0:T(8,128)S(1)}, u32[]{:S(2)}, u32[]{:S(2)}) collective-permute-start(f32[8,16]{1,0:T(8,128)} %bitcast.9), channel_id=1, source_target_pairs={{0,2},{2,0},{4,6},{6,4},{8,10},{10,8},{12,14},{14,12},{16,18},{18,... | collective-permute-start | bytes 1544 | tf_op jit(solution)/shard_map/ppermute | solution.py:61
  16.7 11.2 %collective-permute-start.4 = (bf16[128,1280]{1,0:T(8,128)(2,1)}, bf16[128,1280]{1,0:T(8,128)(2,1)S(1)}, u32[]{:S(2)}, u32[]{:S(2)}) collective-permute-start(bf16[128,1280]{1,0:T(8,128)(2,1)} %collective-permute-done.2.refs_3_.refs_4_), channel_id=1, source_target_pairs={{0,8},{2,10},{4,12},{6,14},{8,16},{10,18},{12,20},{14,22},{16,24},... | collective-permute-start | bytes 983048 | tf_op jit(solution)/shard_map/ppermute | solution.py:66
  17.7 10.2 %collective-permute-start.5 = (bf16[128,1280]{1,0:T(8,128)(2,1)}, bf16[128,1280]{1,0:T(8,128)(2,1)S(1)}, u32[]{:S(2)}, u32[]{:S(2)}) collective-permute-start(bf16[128,1280]{1,0:T(8,128)(2,1)} %collective-permute-done.2.refs_3_.refs_4_), channel_id=1, source_target_pairs={{0,4},{2,6},{4,0},{6,2},{8,12},{10,14},{12,8},{14,10},{16,20},{18,... | collective-permute-start | bytes 983048 | tf_op jit(solution)/shard_map/ppermute | solution.py:71
  27.9 13.3 %copy-start.9 = (bf16[128,1280]{1,0:T(8,128)(2,1)}, bf16[128,1280]{1,0:T(8,128)(2,1)S(1)}, u32[]{:S(2)}) copy-start(bf16[128,1280]{1,0:T(8,128)(2,1)S(1)} %collective-permute-done.4.refs_4_.refs_5_) | copy-start | bytes 983044
  27.9 13.3 %copy-start.10 = (bf16[128,1280]{1,0:T(8,128)(2,1)}, bf16[128,1280]{1,0:T(8,128)(2,1)S(1)}, u32[]{:S(2)}) copy-start(bf16[128,1280]{1,0:T(8,128)(2,1)S(1)} %collective-permute-done.5.refs_7_.refs_8_) | copy-start | bytes 983044
  27.9 10.2 %collective-permute-start.7 = (bf16[128,1280]{1,0:T(8,128)(2,1)S(1)}, bf16[128,1280]{1,0:T(8,128)(2,1)S(1)}, u32[]{:S(2)}, u32[]{:S(2)}) collective-permute-start(bf16[128,1280]{1,0:T(8,128)(2,1)S(1)} %collective-permute-done.4.refs_4_.refs_5_), channel_id=1, source_target_pairs={{0,8},{2,10},{4,12},{6,14},{8,16},{10,18},{12,20},{14,22},{16,24},... | collective-permute-start | bytes 983048 | tf_op jit(solution)/shard_map/ppermute | solution.py:66
  28.0 10.1 %collective-permute-start.8 = (bf16[128,1280]{1,0:T(8,128)(2,1)S(1)}, bf16[128,1280]{1,0:T(8,128)(2,1)S(1)}, u32[]{:S(2)}, u32[]{:S(2)}) collective-permute-start(bf16[128,1280]{1,0:T(8,128)(2,1)S(1)} %collective-permute-done.4.refs_4_.refs_5_), channel_id=1, source_target_pairs={{0,4},{2,6},{4,0},{6,2},{8,12},{10,14},{12,8},{14,10},{16,20},{18,... | collective-permute-start | bytes 983048 | tf_op jit(solution)/shard_map/ppermute | solution.py:71
  29.3 10.0 %collective-permute-start.10 = (bf16[512,1024]{1,0:T(8,128)(2,1)S(1)}, bf16[512,1024]{1,0:T(8,128)(2,1)S(1)}, u32[]{:S(2)}, u32[]{:S(2)}) collective-permute-start(bf16[512,1024]{1,0:T(8,128)(2,1)S(1)} %collective-permute-done.9.refs_0_), channel_id=1, source_target_pairs={{0,2},{2,0},{4,6},{6,4},{8,10},{10,8},{12,14},{14,12},{16,18},{18,... | collective-permute-start | bytes 3145736 | tf_op jit(solution)/shard_map/ppermute | solution.py:61
  31.2 10.0 %copy-start.2 = (bf16[1024,1024]{1,0:T(8,128)(2,1)}, bf16[1024,1024]{1,0:T(8,128)(2,1)S(1)}, u32[]{:S(2)}) copy-start(bf16[1024,1024]{1,0:T(8,128)(2,1)S(1)} %place_tokens.4.refs_0_.refs_1_) | copy-start | bytes 6291460
  38.1 3.1 %copy-start.6 = (bf16[128,1280]{1,0:T(8,128)(2,1)}, bf16[128,1280]{1,0:T(8,128)(2,1)S(1)}, u32[]{:S(2)}) copy-start(bf16[128,1280]{1,0:T(8,128)(2,1)S(1)} %collective-permute-done.7.refs_5_.refs_6_) | copy-start | bytes 983044
  38.1 3.1 %copy-start.7 = (bf16[128,1280]{1,0:T(8,128)(2,1)}, bf16[128,1280]{1,0:T(8,128)(2,1)S(1)}, u32[]{:S(2)}) copy-start(bf16[128,1280]{1,0:T(8,128)(2,1)S(1)} %collective-permute-done.8.refs_8_.refs_9_) | copy-start | bytes 983044
  38.1 7.1 %collective-permute-start.11 = (bf16[64,1280]{1,0:T(8,128)(2,1)S(1)}, bf16[64,1280]{1,0:T(8,128)(2,1)S(1)}, u32[]{:S(2)}, u32[]{:S(2)}) collective-permute-start(bf16[64,1280]{1,0:T(8,128)(2,1)S(1)} %slice.6), channel_id=1, source_target_pairs={{0,4},{2,6},{4,0},{6,2},{8,12},{10,14},{12,8},{14,10},{16,20},{18,... | collective-permute-start | bytes 491528 | tf_op jit(solution)/shard_map/ppermute | solution.py:71
  39.2 7.2 %collective-permute-start.12 = (bf16[64,1280]{1,0:T(8,128)(2,1)S(1)}, bf16[64,1280]{1,0:T(8,128)(2,1)S(1)}, u32[]{:S(2)}, u32[]{:S(2)}) collective-permute-start(bf16[64,1280]{1,0:T(8,128)(2,1)S(1)} %slice.7), channel_id=1, source_target_pairs={{0,8},{2,10},{4,12},{6,14},{8,16},{10,18},{12,20},{14,22},{16,24},... | collective-permute-start | bytes 491528 | tf_op jit(solution)/shard_map/ppermute | solution.py:66
  41.2 4.0 %copy-start.1 = (bf16[1024,1024]{1,0:T(8,128)(2,1)}, bf16[1024,1024]{1,0:T(8,128)(2,1)S(1)}, u32[]{:S(2)}) copy-start(bf16[1024,1024]{1,0:T(8,128)(2,1)S(1)} %place_tokens.5.refs_1_) | copy-start | bytes 6291460
  45.3 5.1 %copy-start.12 = (bf16[64,1280]{1,0:T(8,128)(2,1)}, bf16[64,1280]{1,0:T(8,128)(2,1)S(1)}, u32[]{:S(2)}) copy-start(bf16[64,1280]{1,0:T(8,128)(2,1)S(1)} %collective-permute-done.11.refs_3_.refs_10_) | copy-start | bytes 491524
  46.4 4.0 %copy-start.13 = (bf16[64,1280]{1,0:T(8,128)(2,1)}, bf16[64,1280]{1,0:T(8,128)(2,1)S(1)}, u32[]{:S(2)}) copy-start(bf16[64,1280]{1,0:T(8,128)(2,1)S(1)} %collective-permute-done.12.refs_4_.refs_11_) | copy-start | bytes 491524
  46.4 9.4 %copy-start.17 = (s32[16,4]{0,1:T(4,128)S(1)}, s32[16,4]{0,1:T(4,128)}, u32[]{:S(2)}) copy-start(s32[16,4]{0,1:T(4,128)} %param.10) | copy-start | bytes 772
  51.3 17.0 %all-to-all-start = ((bf16[8,272,128]{2,1,0:T(8,128)(2,1)}), bf16[8,272,128]{2,1,0:T(8,128)(2,1)S(1)}, u32[]{:S(2)}, u32[]{:S(2)}) async-start(bf16[8,272,128]{2,1,0:T(8,128)(2,1)} %get-tuple-element.66), calls=%async_computation | async-start | bytes 1114112 | tf_op jit(solution)/shard_map/all_to_all | solution.py:836
  69.3 16.8 %all-to-all-start.1 = ((bf16[8,256,128]{2,1,0:T(8,128)(2,1)}), bf16[8,256,128]{2,1,0:T(8,128)(2,1)S(1)}, u32[]{:S(2)}, u32[]{:S(2)}) async-start(bf16[8,256,128]{2,1,0:T(8,128)(2,1)} %scan_states.1), calls=%async_computation.1 | async-start | bytes 1048576 | tf_op jit(solution)/shard_map/all_to_all | solution.py:836
  73.0 13.9 %copy-start.8 = (bf16[1024,256]{1,0:T(8,128)(2,1)S(1)}, bf16[1024,256]{1,0:T(8,128)(2,1)}, u32[]{:S(2)}) copy-start(bf16[1024,256]{1,0:T(8,128)(2,1)} %get-tuple-element.74.refs_2_) | copy-start | bytes 1572868
  86.9 7.5 %copy-start = (bf16[1024,1024]{1,0:T(8,128)(2,1)S(1)}, bf16[1024,1024]{1,0:T(8,128)(2,1)}, u32[]{:S(2)}) copy-start(bf16[1024,1024]{1,0:T(8,128)(2,1)} %w_ref.5) | copy-start | bytes 6291460
  92.4 1.9 %collective-permute-start.15 = (bf16[512,256]{1,0:T(8,128)(2,1)S(1)}, bf16[512,256]{1,0:T(8,128)(2,1)S(1)}, u32[]{:S(2)}, u32[]{:S(2)}) collective-permute-start(bf16[512,256]{1,0:T(8,128)(2,1)S(1)} %get-tuple-element.80), channel_id=1, source_target_pairs={{0,2},{2,0},{4,6},{6,4},{8,10},{10,8},{12,14},{14,12},{16,18},{18,... | collective-permute-start | bytes 786440 | tf_op jit(solution)/shard_map/ppermute | solution.py:61
  92.5 9.2 %collective-permute-start.14 = (bf16[512,256]{1,0:T(8,128)(2,1)S(1)}, bf16[512,256]{1,0:T(8,128)(2,1)S(1)}, u32[]{:S(2)}, u32[]{:S(2)}) collective-permute-start(bf16[512,256]{1,0:T(8,128)(2,1)S(1)} %get-tuple-element.78), channel_id=1, source_target_pairs={{0,1},{1,0},{2,3},{3,2},{4,5},{5,4},{6,7},{7,6},{8,9},{9,8},{10,11... | collective-permute-start | bytes 786440 | tf_op jit(solution)/shard_map/ppermute | solution.py:95
  93.4 13.0 %collective-permute-start.13 = (bf16[512,256]{1,0:T(8,128)(2,1)S(1)}, bf16[512,256]{1,0:T(8,128)(2,1)S(1)}, u32[]{:S(2)}, u32[]{:S(2)}) collective-permute-start(bf16[512,256]{1,0:T(8,128)(2,1)S(1)} %get-tuple-element.77), channel_id=1, source_target_pairs={{0,3},{1,2},{2,1},{3,0},{4,7},{5,6},{6,5},{7,4},{8,11},{9,10},{10,... | collective-permute-start | bytes 786440 | tf_op jit(solution)/shard_map/ppermute | solution.py:103
  (4 other events, 4.1 us)

commit v17 on v16

--- a/solution.py
+++ b/solution.py
@@ -324,10 +324,13 @@
             b_ref[:, rows] = lax.dot_general(
                 maps, x, (((1,), (1,)), ((), ())), preferred_element_type=f32
             )
-            rest = x[:, :count]
+    for s, x_ref in enumerate(x_refs):
+        for at in range(0, tokens, step):
+            here = slice(at, at + step)
+            rest = x_ref[here, :count]
             for c in range(count, width, count):
-                rest = jnp.where(there == c, x[:, c : c + count], rest)
-            rest_ref[rows, :] = rest
+                rest = jnp.where(there == c, x_ref[here, c : c + count], rest)
+            rest_ref[s * tokens + at : s * tokens + at + step, :] = rest
 
 
 def project(plan, x, weights):
@@ -646,19 +649,21 @@
 def mix_kernel(plan, groups, decay_in, *refs):
     a_ins, refs = refs[: plan.merge], refs[plan.merge :]
     c_ins, refs = refs[: plan.merge], refs[plan.merge :]
-    state, back_in, refs = refs[0], refs[1], refs[2:]
-    out_refs, (decay, a, c, back, mixed, out, sems) = refs[:-7], refs[-7:]
+    s_in, back_in, refs = refs[0], refs[1], refs[2:]
+    out_refs, (decay, a, c, state, back, mixed, out, sems) = refs[:-8], refs[-8:]
     copies = Copies(sems)
     tokens = back.shape[0]
     block = tokens // groups
     width = a.shape[2]
     here = groups // 4
+    many = here * plan.pairs * N
 
     arriving = []
     decaying = copies.start(decay_in, decay)
     for i in range(4):
         rows = slice(i * here * block, (i + 1) * here * block)
-        arriving.append([])
+        items = slice(i * many, (i + 1) * many)
+        arriving.append([copies.start(s_in.at[items], state.at[items])])
         for s in range(plan.merge):
             arriving[-1] += [
                 copies.start(c_ins[s].at[rows], c.at[s, rows, :]),
@@ -708,13 +713,14 @@
     count = plan.merge * plan.peers
     return pl.pallas_call(
         functools.partial(mix_kernel, plan, groups),
-        in_specs=[hbm] * (2 * plan.merge + 1) + [vmem, hbm],
+        in_specs=[hbm] * (2 * plan.merge + 3),
         out_specs=(hbm,) * count,
         out_shape=(jax.ShapeDtypeStruct((tokens // plan.peers, width), bf16),) * count,
         scratch_shapes=[
             pltpu.VMEM(decays.shape, f32),
             pltpu.VMEM((plan.merge, tokens, width), f32),
             pltpu.VMEM((plan.merge, tokens, width), bf16),
+            pltpu.VMEM(state.shape, bf16),
             pltpu.VMEM(back.shape, bf16),
             pltpu.VMEM((tokens, plan.merge * width), bf16),
             pltpu.VMEM((count, tokens // plan.peers, width), bf16),

time: 109 us -> 109 us (level)
  no operation moved by 1% of the time
where the time goes in v17:
time: 109 us; the launch traced here: 108 us
  Pallas kernels  45.7 us (42%)
  waiting for transfers between devices  33.4 us (31%)
  starting transfers between devices  22.8 us (21%)
  local copies, waits for them, and re-layouts  4.83 us (4%)
    pallas_call x2, Pallas kernels, attend(): pl.pallas_call(functools.partial(attend_kernel, plan, slot), in_specs=[sm...  18.4 us
    ppermute x4, waiting for transfers between devices, round(): return lax.ppermute(block, 'tm', pairs)  16.9 us
    all_to_all x2, starting transfers between devices, exchange(): lax.all_to_all(blocks, 'tm', split_axis=0, concat_axis=0, tiled=True, axi...  8.82 us
    pallas_call x3, Pallas kernels, place_tokens(): pl.pallas_call(functools.partial(place_kernel, slots, parts, start), out_...  7.17 us
    all_to_all x2, waiting for transfers between devices, exchange(): lax.all_to_all(blocks, 'tm', split_axis=0, concat_axis=0, tiled=True, axi...  6.57 us
    ppermute x2, waiting for transfers between devices, to_peer(): return lax.ppermute(block, 'head', pairs)  6.14 us
    ppermute x4, starting transfers between devices, cross(): return lax.ppermute(block, 'tm', pairs)  5.39 us
    unnamed x37, local copies, waits for them, and re-layouts  4.81 us
  transfers between devices with their start and end apart: 18, of which 9 were waited for; matrix products, arithmetic and copies ran while one was open for 1% of the time, Pallas kernels for 32%

profile of v17, /device:TPU:0, one launch (start us, length us, event | category | flops | bytes accessed | tf_op | source)
XLA Modules:
  0.0 108.1 jit_solution(17913046884130964779)
XLA Ops:
  0.5 3.0 %collective-permute-start.9 = (bf16[512,1024]{1,0:T(8,128)(2,1)}, bf16[512,1024]{1,0:T(8,128)(2,1)S(1)}, u32[]{:S(2)}, u32[]{:S(2)}) collective-permute-start(bf16[512,1024]{1,0:T(8,128)(2,1)} %bitcast.6), channel_id=1, source_target_pairs={{0,1},{1,0},{2,3},{3,2},{4,5},{5,4},{6,7},{7,6},{8,9},{9,8},{10,11... | collective-permute-start | bytes 3145736 | tf_op jit(solution)/shard_map/ppermute | solution.py:95
  3.5 1.0 copy-done.11
  4.7 1.8 %collective-permute-start.2 = (bf16[128,1280]{1,0:T(8,128)(2,1)S(1)}, bf16[128,1280]{1,0:T(8,128)(2,1)}, u32[]{:S(2)}, u32[]{:S(2)}) collective-permute-start(bf16[128,1280]{1,0:T(8,128)(2,1)S(1)} %reorder.3.refs_2_.refs_3_), channel_id=1, source_target_pairs={{0,8},{2,10},{4,12},{6,14},{8,16},{10,18},{12,20},{14,22},{16,24},... | collective-permute-start | bytes 983048 | tf_op jit(solution)/shard_map/ppermute | solution.py:66
  6.6 1.5 %collective-permute-start.3 = (bf16[128,1280]{1,0:T(8,128)(2,1)S(1)}, bf16[128,1280]{1,0:T(8,128)(2,1)}, u32[]{:S(2)}, u32[]{:S(2)}) collective-permute-start(bf16[128,1280]{1,0:T(8,128)(2,1)S(1)} %reorder.3.refs_2_.refs_3_), channel_id=1, source_target_pairs={{0,4},{2,6},{4,0},{6,2},{8,12},{10,14},{12,8},{14,10},{16,20},{18,... | collective-permute-start | bytes 983048 | tf_op jit(solution)/shard_map/ppermute | solution.py:71
  10.2 1.4 %copy-done.3 = bf16[1024,1024]{1,0:T(8,128)(2,1)} copy-done((bf16[1024,1024]{1,0:T(8,128)(2,1)}, bf16[1024,1024]{1,0:T(8,128)(2,1)S(1)}, u32[]{:S(2)}) %copy-start.3) | copy-done | bytes 2097176
  12.4 4.3 %collective-permute-done.2.refs_3_.refs_4_ = bf16[128,1280]{1,0:T(8,128)(2,1)} collective-permute-done((bf16[128,1280]{1,0:T(8,128)(2,1)S(1)}, bf16[128,1280]{1,0:T(8,128)(2,1)}, u32[]{:S(2)}, u32[]{:S(2)}) %collective-permute-start.2) | collective-permute-done | bytes 327712 | tf_op jit(solution)/shard_map/ppermute | solution.py:66
  16.7 1.0 collective-permute-start.4
  17.7 1.5 %collective-permute-start.5 = (bf16[128,1280]{1,0:T(8,128)(2,1)}, bf16[128,1280]{1,0:T(8,128)(2,1)S(1)}, u32[]{:S(2)}, u32[]{:S(2)}) collective-permute-start(bf16[128,1280]{1,0:T(8,128)(2,1)} %collective-permute-done.2.refs_3_.refs_4_), channel_id=1, source_target_pairs={{0,4},{2,6},{4,0},{6,2},{8,12},{10,14},{12,8},{14,10},{16,20},{18,... | collective-permute-start | bytes 983048 | tf_op jit(solution)/shard_map/ppermute | solution.py:71
  19.2 3.5 %place_tokens.3.refs_1_ = bf16[2048,1024]{1,0:T(8,128)(2,1)S(1)} custom-call(f32[1,1024]{1,0:T(1,128)S(1)} %rank_tokens.1.row_ref.rank_ref, bf16[512,1024]{1,0:T(8,128)(2,1)S(1)} %bitcast.7, bf16[512,1024]{1,0:T(8,128)(2,1)S(1)} %collective-permute-done.6.refs_1_), custom_call_target="tpu_custom_call" | custom-call | bytes 4096 | tf_op jit(solution)/shard_map/place_tokens/pallas_call | solution.py:288
  22.7 5.2 %collective-permute-done.4.refs_4_.refs_5_ = bf16[128,1280]{1,0:T(8,128)(2,1)S(1)} collective-permute-done((bf16[128,1280]{1,0:T(8,128)(2,1)}, bf16[128,1280]{1,0:T(8,128)(2,1)S(1)}, u32[]{:S(2)}, u32[]{:S(2)}) %collective-permute-start.4) | collective-permute-done | bytes 327712 | tf_op jit(solution)/shard_map/ppermute | solution.py:66
  28.0 1.3 %collective-permute-start.8 = (bf16[128,1280]{1,0:T(8,128)(2,1)S(1)}, bf16[128,1280]{1,0:T(8,128)(2,1)S(1)}, u32[]{:S(2)}, u32[]{:S(2)}) collective-permute-start(bf16[128,1280]{1,0:T(8,128)(2,1)S(1)} %collective-permute-done.4.refs_4_.refs_5_), channel_id=1, source_target_pairs={{0,4},{2,6},{4,0},{6,2},{8,12},{10,14},{12,8},{14,10},{16,20},{18,... | collective-permute-start | bytes 983048 | tf_op jit(solution)/shard_map/ppermute | solution.py:71
  29.3 1.9 %place_tokens.4.refs_0_.refs_1_ = bf16[1024,1024]{1,0:T(8,128)(2,1)S(1)} custom-call(f32[1,1024]{1,0:T(1,128)S(1)} %rank_tokens.1.row_ref.rank_ref, bf16[512,1024]{1,0:T(8,128)(2,1)S(1)} %collective-permute-done.9.refs_0_, bf16[2048,1024]{1,0:T(8,128)(2,1)S(1)} %place_tokens.3.refs_1_), custom_call_target="tpu_custom_call" | custom-call | bytes 4096 | tf_op jit(solution)/shard_map/place_tokens/pallas_call | solution.py:288
  31.2 6.9 %collective-permute-done.7.refs_5_.refs_6_ = bf16[128,1280]{1,0:T(8,128)(2,1)S(1)} collective-permute-done((bf16[128,1280]{1,0:T(8,128)(2,1)S(1)}, bf16[128,1280]{1,0:T(8,128)(2,1)S(1)}, u32[]{:S(2)}, u32[]{:S(2)}) %collective-permute-start.7) | collective-permute-done | bytes 327712 | tf_op jit(solution)/shard_map/ppermute | solution.py:66
  38.1 1.1 collective-permute-start.11
  39.5 1.9 %place_tokens.5.refs_1_ = bf16[1024,1024]{1,0:T(8,128)(2,1)S(1)} custom-call(f32[1,1024]{1,0:T(1,128)S(1)} %rank_tokens.1.row_ref.rank_ref, bf16[512,1024]{1,0:T(8,128)(2,1)S(1)} %collective-permute-done.10.refs_0_, bf16[2048,1024]{1,0:T(8,128)(2,1)S(1)} %place_tokens.3.refs_1_), custom_call_target="tpu_custom_call" | custom-call | bytes 4096 | tf_op jit(solution)/shard_map/place_tokens/pallas_call | solution.py:288
  41.4 4.7 %project.1 = (f32[2048,256]{1,0:T(8,128)S(1)}, f32[256,2048]{1,0:T(8,128)S(1)}, bf16[2048,128]{1,0:T(8,128)(2,1)S(1)}) custom-call(bf16[1024,1024]{1,0:T(8,128)(2,1)S(1)} %place_tokens.4.refs_0_.refs_1_, bf16[1024,1024]{1,0:T(8,128)(2,1)S(1)} %place_tokens.5.refs_1_, bf16[128,1280]{1,0:T(8,128)(2,1)S(1)} %reorder.3.refs_2_.refs_3_, ...), custom_call_target="tpu_custom_call" | custom-call | bytes 4096 | tf_op jit(solution)/shard_map/project/pallas_call | solution.py:340
  46.6 3.9 %block_updates.1 = (bf16[2,2048,128]{2,1,0:T(8,128)(2,1)S(1)}, bf16[8,272,128]{2,1,0:T(8,128)(2,1)}) custom-call(f32[4,32,128]{2,1,0:T(8,128)S(1)} %hold.1.decay_ref.decay_in, f32[2048,256]{1,0:T(8,128)S(1)} %get-tuple-element.63.refs_0_, f32[256,2048]{1,0:T(8,128)S(1)} %get-tuple-element.64.refs_1_, bf16[2048,128]{1,0:T(8,128)(2,1)S(1)} %get-tuple-element.65.refs_2_, ...), custom_call_target="tpu_custom_call" | custom-call | flops 1073741824 | bytes 3145728 | tf_op jit(solution)/shard_map/block_updates/pallas_call | solution.py:438
  50.6 1.0 copy-done.15
  51.5 5.1 %all-to-all-start = ((bf16[8,272,128]{2,1,0:T(8,128)(2,1)}), bf16[8,272,128]{2,1,0:T(8,128)(2,1)S(1)}, u32[]{:S(2)}, u32[]{:S(2)}) async-start(bf16[8,272,128]{2,1,0:T(8,128)(2,1)} %get-tuple-element.66), calls=%async_computation | async-start | bytes 1114112 | tf_op jit(solution)/shard_map/all_to_all | solution.py:842
  57.3 9.1 %attend.2 = (f32[1024,256]{1,0:T(8,128)}, bf16[1024,256]{1,0:T(8,128)(2,1)}) custom-call(s32[16,4]{1,0:T(8,128)} %copy.7.refs_0_, bf16[1024,1024]{1,0:T(8,128)(2,1)} %copy-done.2, bf16[2,2048,128]{2,1,0:T(8,128)(2,1)} %copy-done.15, bf16[128,1280]{1,0:T(8,128)(2,1)} %copy-done.4, bf16[128,1280]{1,0:T(8,128)(2,1)} %collective-permute-done.2.refs_3_.refs_4_, ...), custom_call_target="tpu_custom_call" | custom-call | flops 4831838208 | bytes 11534336 | tf_op jit(solution)/shard_map/attend/pallas_call | solution.py:611
  66.4 2.8 %all-to-all-done.u_ref = bf16[8,272,128]{2,1,0:T(8,128)(2,1)S(1)} async-done(((bf16[8,272,128]{2,1,0:T(8,128)(2,1)}), bf16[8,272,128]{2,1,0:T(8,128)(2,1)S(1)}, u32[]{:S(2)}, u32[]{:S(2)}) %all-to-all-start) | async-done | bytes 557088 | tf_op jit(solution)/shard_map/all_to_all | solution.py:842
  69.2 0.9 scan_states.1
  70.1 3.7 %all-to-all-start.1 = ((bf16[8,256,128]{2,1,0:T(8,128)(2,1)}), bf16[8,256,128]{2,1,0:T(8,128)(2,1)S(1)}, u32[]{:S(2)}, u32[]{:S(2)}) async-start(bf16[8,256,128]{2,1,0:T(8,128)(2,1)} %scan_states.1), calls=%async_computation.1 | async-start | bytes 1048576 | tf_op jit(solution)/shard_map/all_to_all | solution.py:842
  73.8 9.3 %attend.3 = (f32[1024,256]{1,0:T(8,128)}, bf16[1024,256]{1,0:T(8,128)(2,1)}) custom-call(s32[16,4]{1,0:T(8,128)} %copy.7.refs_0_, bf16[1024,1024]{1,0:T(8,128)(2,1)} %copy-done.1, bf16[2,2048,128]{2,1,0:T(8,128)(2,1)} %copy-done.15, bf16[128,1280]{1,0:T(8,128)(2,1)} %copy-done.4, bf16[128,1280]{1,0:T(8,128)(2,1)} %collective-permute-done.2.refs_3_.refs_4_, ...), custom_call_target="tpu_custom_call" | custom-call | flops 4831838208 | bytes 11534336 | tf_op jit(solution)/shard_map/attend/pallas_call | solution.py:611
  83.2 3.8 %all-to-all-done.1 = bf16[8,256,128]{2,1,0:T(8,128)(2,1)S(1)} async-done(((bf16[8,256,128]{2,1,0:T(8,128)(2,1)}), bf16[8,256,128]{2,1,0:T(8,128)(2,1)S(1)}, u32[]{:S(2)}, u32[]{:S(2)}) %all-to-all-start.1) | async-done | bytes 524320 | tf_op jit(solution)/shard_map/all_to_all | solution.py:842
  87.7 4.5 %mix.1 = (bf16[512,256]{1,0:T(8,128)(2,1)S(1)}, bf16[512,256]{1,0:T(8,128)(2,1)S(1)}, bf16[512,256]{1,0:T(8,128)(2,1)S(1)}, bf16[512,256]{1,0:T(8,128)(2,1)S(1)}) custom-call(f32[4,32,128]{2,1,0:T(8,128)S(1)} %hold.1.decay_ref.decay_in, f32[1024,256]{1,0:T(8,128)} %get-tuple-element.70.refs_0_, f32[1024,256]{1,0:T(8,128)} %get-tuple-element.73.refs_1_, ...), custom_call_target="tpu_custom_call" | custom-call | flops 1073741824 | bytes 6291456 | tf_op jit(solution)/shard_map/mix/pallas_call | solution.py:714
  93.2 1.0 collective-permute-start.13
  94.2 1.2 %project_out.3.refs_1_ = f32[512,1024]{1,0:T(8,128)S(1)} custom-call(bf16[1024,1024]{1,0:T(8,128)(2,1)S(1)} %copy-done, bf16[512,256]{1,0:T(8,128)(2,1)S(1)} %get-tuple-element.79.refs_0_, bf16[512,256]{1,0:T(8,128)(2,1)S(1)} %collective-permute-done.15.refs_1_), custom_call_target="tpu_custom_call" | custom-call | bytes 2048 | tf_op jit(solution)/shard_map/project_out/pallas_call | solution.py:763
  95.4 6.1 %collective-permute-done.14.refs_0_ = bf16[512,256]{1,0:T(8,128)(2,1)S(1)} collective-permute-done((bf16[512,256]{1,0:T(8,128)(2,1)S(1)}, bf16[512,256]{1,0:T(8,128)(2,1)S(1)}, u32[]{:S(2)}, u32[]{:S(2)}) %collective-permute-start.14) | collective-permute-done | bytes 262176 | tf_op jit(solution)/shard_map/ppermute | solution.py:95
  101.5 1.5 %project_out.4.refs_1_ = f32[512,1024]{1,0:T(8,128)S(1)} custom-call(bf16[1024,1024]{1,0:T(8,128)(2,1)S(1)} %copy-done, bf16[512,256]{1,0:T(8,128)(2,1)S(1)} %collective-permute-done.14.refs_0_, f32[512,1024]{1,0:T(8,128)S(1)} %project_out.3.refs_1_), custom_call_target="tpu_custom_call" | custom-call | bytes 2048 | tf_op jit(solution)/shard_map/project_out/pallas_call | solution.py:763
  103.1 3.2 %collective-permute-done.13.refs_0_ = bf16[512,256]{1,0:T(8,128)(2,1)S(1)} collective-permute-done((bf16[512,256]{1,0:T(8,128)(2,1)S(1)}, bf16[512,256]{1,0:T(8,128)(2,1)S(1)}, u32[]{:S(2)}, u32[]{:S(2)}) %collective-permute-start.13) | collective-permute-done | bytes 262176 | tf_op jit(solution)/shard_map/ppermute | solution.py:103
  106.2 1.6 %project_out.5 = bf16[512,1024]{1,0:T(8,128)(2,1)} custom-call(bf16[1024,1024]{1,0:T(8,128)(2,1)S(1)} %copy-done, bf16[512,256]{1,0:T(8,128)(2,1)S(1)} %collective-permute-done.13.refs_0_, f32[512,1024]{1,0:T(8,128)S(1)} %project_out.4.refs_1_), custom_call_target="tpu_custom_call" | custom-call | bytes 2048 | tf_op jit(solution)/shard_map/project_out/pallas_call | solution.py:763
  (62 shorter events, 6.9 us)
Async XLA Ops:
  0.0 19.2 %copy-start.5 = (bf16[1,512,1024]{2,1,0:T(8,128)(2,1)S(1)}, bf16[1,512,1024]{2,1,0:T(8,128)(2,1)}, u32[]{:S(2)}) copy-start(bf16[1,512,1024]{2,1,0:T(8,128)(2,1)} %param.6) | copy-start | bytes 3145732
  0.0 19.2 %collective-permute-start.6 = (bf16[512,1024]{1,0:T(8,128)(2,1)}, bf16[512,1024]{1,0:T(8,128)(2,1)S(1)}, u32[]{:S(2)}, u32[]{:S(2)}) collective-permute-start(bf16[512,1024]{1,0:T(8,128)(2,1)} %bitcast.5), channel_id=1, source_target_pairs={{0,2},{2,0},{4,6},{6,4},{8,10},{10,8},{12,14},{14,12},{16,18},{18,... | collective-permute-start | bytes 3145736 | tf_op jit(solution)/shard_map/ppermute | solution.py:61
  0.5 4.1 %collective-permute-start.1 = (bf16[64,2560]{1,0:T(8,128)(2,1)}, bf16[64,2560]{1,0:T(8,128)(2,1)S(1)}, u32[]{:S(2)}, u32[]{:S(2)}) collective-permute-start(bf16[64,2560]{1,0:T(8,128)(2,1)} %refs_0_.3), channel_id=1, source_target_pairs={{0,2},{2,0},{4,6},{6,4},{8,10},{10,8},{12,14},{14,12},{16,18},{18,... | collective-permute-start | bytes 983048 | tf_op jit(solution)/shard_map/ppermute | solution.py:61
  0.5 28.8 %collective-permute-start.9 = (bf16[512,1024]{1,0:T(8,128)(2,1)}, bf16[512,1024]{1,0:T(8,128)(2,1)S(1)}, u32[]{:S(2)}, u32[]{:S(2)}) collective-permute-start(bf16[512,1024]{1,0:T(8,128)(2,1)} %bitcast.6), channel_id=1, source_target_pairs={{0,1},{1,0},{2,3},{3,2},{4,5},{5,4},{6,7},{7,6},{8,9},{9,8},{10,11... | collective-permute-start | bytes 3145736 | tf_op jit(solution)/shard_map/ppermute | solution.py:95
  4.5 7.1 %copy-start.14 = (f32[1,8,16]{2,1,0:T(8,128)S(1)}, f32[1,8,16]{2,1,0:T(8,128)}, u32[]{:S(2)}) copy-start(f32[1,8,16]{2,1,0:T(8,128)} %param.11) | copy-start | bytes 1540
  4.7 36.6 %copy-start.4 = (bf16[128,1280]{1,0:T(8,128)(2,1)}, bf16[128,1280]{1,0:T(8,128)(2,1)S(1)}, u32[]{:S(2)}) copy-start(bf16[128,1280]{1,0:T(8,128)(2,1)S(1)} %reorder.3.refs_2_.refs_3_) | copy-start | bytes 983044
  4.7 12.0 %collective-permute-start.2 = (bf16[128,1280]{1,0:T(8,128)(2,1)S(1)}, bf16[128,1280]{1,0:T(8,128)(2,1)}, u32[]{:S(2)}, u32[]{:S(2)}) collective-permute-start(bf16[128,1280]{1,0:T(8,128)(2,1)S(1)} %reorder.3.refs_2_.refs_3_), channel_id=1, source_target_pairs={{0,8},{2,10},{4,12},{6,14},{8,16},{10,18},{12,20},{14,22},{16,24},... | collective-permute-start | bytes 983048 | tf_op jit(solution)/shard_map/ppermute | solution.py:66
  6.6 10.1 %collective-permute-start.3 = (bf16[128,1280]{1,0:T(8,128)(2,1)S(1)}, bf16[128,1280]{1,0:T(8,128)(2,1)}, u32[]{:S(2)}, u32[]{:S(2)}) collective-permute-start(bf16[128,1280]{1,0:T(8,128)(2,1)S(1)} %reorder.3.refs_2_.refs_3_), channel_id=1, source_target_pairs={{0,4},{2,6},{4,0},{6,2},{8,12},{10,14},{12,8},{14,10},{16,20},{18,... | collective-permute-start | bytes 983048 | tf_op jit(solution)/shard_map/ppermute | solution.py:71
  8.0 1.4 %collective-permute-start = (f32[8,16]{1,0:T(8,128)}, f32[8,16]{1,0:T(8,128)S(1)}, u32[]{:S(2)}, u32[]{:S(2)}) collective-permute-start(f32[8,16]{1,0:T(8,128)} %bitcast.9), channel_id=1, source_target_pairs={{0,2},{2,0},{4,6},{6,4},{8,10},{10,8},{12,14},{14,12},{16,18},{18,... | collective-permute-start | bytes 1544 | tf_op jit(solution)/shard_map/ppermute | solution.py:61
  16.7 11.2 %collective-permute-start.4 = (bf16[128,1280]{1,0:T(8,128)(2,1)}, bf16[128,1280]{1,0:T(8,128)(2,1)S(1)}, u32[]{:S(2)}, u32[]{:S(2)}) collective-permute-start(bf16[128,1280]{1,0:T(8,128)(2,1)} %collective-permute-done.2.refs_3_.refs_4_), channel_id=1, source_target_pairs={{0,8},{2,10},{4,12},{6,14},{8,16},{10,18},{12,20},{14,22},{16,24},... | collective-permute-start | bytes 983048 | tf_op jit(solution)/shard_map/ppermute | solution.py:66
  17.7 10.2 %collective-permute-start.5 = (bf16[128,1280]{1,0:T(8,128)(2,1)}, bf16[128,1280]{1,0:T(8,128)(2,1)S(1)}, u32[]{:S(2)}, u32[]{:S(2)}) collective-permute-start(bf16[128,1280]{1,0:T(8,128)(2,1)} %collective-permute-done.2.refs_3_.refs_4_), channel_id=1, source_target_pairs={{0,4},{2,6},{4,0},{6,2},{8,12},{10,14},{12,8},{14,10},{16,20},{18,... | collective-permute-start | bytes 983048 | tf_op jit(solution)/shard_map/ppermute | solution.py:71
  27.9 13.4 %copy-start.9 = (bf16[128,1280]{1,0:T(8,128)(2,1)}, bf16[128,1280]{1,0:T(8,128)(2,1)S(1)}, u32[]{:S(2)}) copy-start(bf16[128,1280]{1,0:T(8,128)(2,1)S(1)} %collective-permute-done.4.refs_4_.refs_5_) | copy-start | bytes 983044
  27.9 13.4 %copy-start.10 = (bf16[128,1280]{1,0:T(8,128)(2,1)}, bf16[128,1280]{1,0:T(8,128)(2,1)S(1)}, u32[]{:S(2)}) copy-start(bf16[128,1280]{1,0:T(8,128)(2,1)S(1)} %collective-permute-done.5.refs_7_.refs_8_) | copy-start | bytes 983044
  27.9 10.2 %collective-permute-start.7 = (bf16[128,1280]{1,0:T(8,128)(2,1)S(1)}, bf16[128,1280]{1,0:T(8,128)(2,1)S(1)}, u32[]{:S(2)}, u32[]{:S(2)}) collective-permute-start(bf16[128,1280]{1,0:T(8,128)(2,1)S(1)} %collective-permute-done.4.refs_4_.refs_5_), channel_id=1, source_target_pairs={{0,8},{2,10},{4,12},{6,14},{8,16},{10,18},{12,20},{14,22},{16,24},... | collective-permute-start | bytes 983048 | tf_op jit(solution)/shard_map/ppermute | solution.py:66
  28.0 10.1 %collective-permute-start.8 = (bf16[128,1280]{1,0:T(8,128)(2,1)S(1)}, bf16[128,1280]{1,0:T(8,128)(2,1)S(1)}, u32[]{:S(2)}, u32[]{:S(2)}) collective-permute-start(bf16[128,1280]{1,0:T(8,128)(2,1)S(1)} %collective-permute-done.4.refs_4_.refs_5_), channel_id=1, source_target_pairs={{0,4},{2,6},{4,0},{6,2},{8,12},{10,14},{12,8},{14,10},{16,20},{18,... | collective-permute-start | bytes 983048 | tf_op jit(solution)/shard_map/ppermute | solution.py:71
  29.3 10.2 %collective-permute-start.10 = (bf16[512,1024]{1,0:T(8,128)(2,1)S(1)}, bf16[512,1024]{1,0:T(8,128)(2,1)S(1)}, u32[]{:S(2)}, u32[]{:S(2)}) collective-permute-start(bf16[512,1024]{1,0:T(8,128)(2,1)S(1)} %collective-permute-done.9.refs_0_), channel_id=1, source_target_pairs={{0,2},{2,0},{4,6},{6,4},{8,10},{10,8},{12,14},{14,12},{16,18},{18,... | collective-permute-start | bytes 3145736 | tf_op jit(solution)/shard_map/ppermute | solution.py:61
  31.2 10.2 %copy-start.2 = (bf16[1024,1024]{1,0:T(8,128)(2,1)}, bf16[1024,1024]{1,0:T(8,128)(2,1)S(1)}, u32[]{:S(2)}) copy-start(bf16[1024,1024]{1,0:T(8,128)(2,1)S(1)} %place_tokens.4.refs_0_.refs_1_) | copy-start | bytes 6291460
  38.1 3.3 %copy-start.6 = (bf16[128,1280]{1,0:T(8,128)(2,1)}, bf16[128,1280]{1,0:T(8,128)(2,1)S(1)}, u32[]{:S(2)}) copy-start(bf16[128,1280]{1,0:T(8,128)(2,1)S(1)} %collective-permute-done.7.refs_5_.refs_6_) | copy-start | bytes 983044
  38.1 3.3 %copy-start.7 = (bf16[128,1280]{1,0:T(8,128)(2,1)}, bf16[128,1280]{1,0:T(8,128)(2,1)S(1)}, u32[]{:S(2)}) copy-start(bf16[128,1280]{1,0:T(8,128)(2,1)S(1)} %collective-permute-done.8.refs_8_.refs_9_) | copy-start | bytes 983044
  38.1 8.0 %collective-permute-start.11 = (bf16[64,1280]{1,0:T(8,128)(2,1)S(1)}, bf16[64,1280]{1,0:T(8,128)(2,1)S(1)}, u32[]{:S(2)}, u32[]{:S(2)}) collective-permute-start(bf16[64,1280]{1,0:T(8,128)(2,1)S(1)} %slice.6), channel_id=1, source_target_pairs={{0,4},{2,6},{4,0},{6,2},{8,12},{10,14},{12,8},{14,10},{16,20},{18,... | collective-permute-start | bytes 491528 | tf_op jit(solution)/shard_map/ppermute | solution.py:71
  39.2 7.3 %collective-permute-start.12 = (bf16[64,1280]{1,0:T(8,128)(2,1)S(1)}, bf16[64,1280]{1,0:T(8,128)(2,1)S(1)}, u32[]{:S(2)}, u32[]{:S(2)}) collective-permute-start(bf16[64,1280]{1,0:T(8,128)(2,1)S(1)} %slice.7), channel_id=1, source_target_pairs={{0,8},{2,10},{4,12},{6,14},{8,16},{10,18},{12,20},{14,22},{16,24},... | collective-permute-start | bytes 491528 | tf_op jit(solution)/shard_map/ppermute | solution.py:66
  41.4 4.7 %copy-start.1 = (bf16[1024,1024]{1,0:T(8,128)(2,1)}, bf16[1024,1024]{1,0:T(8,128)(2,1)S(1)}, u32[]{:S(2)}) copy-start(bf16[1024,1024]{1,0:T(8,128)(2,1)S(1)} %place_tokens.5.refs_1_) | copy-start | bytes 6291460
  46.1 4.4 %copy-start.12 = (bf16[64,1280]{1,0:T(8,128)(2,1)}, bf16[64,1280]{1,0:T(8,128)(2,1)S(1)}, u32[]{:S(2)}) copy-start(bf16[64,1280]{1,0:T(8,128)(2,1)S(1)} %collective-permute-done.11.refs_3_.refs_10_) | copy-start | bytes 491524
  46.6 4.0 %copy-start.13 = (bf16[64,1280]{1,0:T(8,128)(2,1)}, bf16[64,1280]{1,0:T(8,128)(2,1)S(1)}, u32[]{:S(2)}) copy-start(bf16[64,1280]{1,0:T(8,128)(2,1)S(1)} %collective-permute-done.12.refs_4_.refs_11_) | copy-start | bytes 491524
  46.6 10.0 %copy-start.17 = (s32[16,4]{0,1:T(4,128)S(1)}, s32[16,4]{0,1:T(4,128)}, u32[]{:S(2)}) copy-start(s32[16,4]{0,1:T(4,128)} %param.10) | copy-start | bytes 772
  51.5 17.7 %all-to-all-start = ((bf16[8,272,128]{2,1,0:T(8,128)(2,1)}), bf16[8,272,128]{2,1,0:T(8,128)(2,1)S(1)}, u32[]{:S(2)}, u32[]{:S(2)}) async-start(bf16[8,272,128]{2,1,0:T(8,128)(2,1)} %get-tuple-element.66), calls=%async_computation | async-start | bytes 1114112 | tf_op jit(solution)/shard_map/all_to_all | solution.py:842
  70.1 16.8 %all-to-all-start.1 = ((bf16[8,256,128]{2,1,0:T(8,128)(2,1)}), bf16[8,256,128]{2,1,0:T(8,128)(2,1)S(1)}, u32[]{:S(2)}, u32[]{:S(2)}) async-start(bf16[8,256,128]{2,1,0:T(8,128)(2,1)} %scan_states.1), calls=%async_computation.1 | async-start | bytes 1048576 | tf_op jit(solution)/shard_map/all_to_all | solution.py:842
  73.8 13.9 %copy-start.8 = (bf16[1024,256]{1,0:T(8,128)(2,1)S(1)}, bf16[1024,256]{1,0:T(8,128)(2,1)}, u32[]{:S(2)}) copy-start(bf16[1024,256]{1,0:T(8,128)(2,1)} %get-tuple-element.74.refs_2_) | copy-start | bytes 1572868
  87.7 6.5 %copy-start = (bf16[1024,1024]{1,0:T(8,128)(2,1)S(1)}, bf16[1024,1024]{1,0:T(8,128)(2,1)}, u32[]{:S(2)}) copy-start(bf16[1024,1024]{1,0:T(8,128)(2,1)} %w_ref.5) | copy-start | bytes 6291460
  92.3 1.9 %collective-permute-start.15 = (bf16[512,256]{1,0:T(8,128)(2,1)S(1)}, bf16[512,256]{1,0:T(8,128)(2,1)S(1)}, u32[]{:S(2)}, u32[]{:S(2)}) collective-permute-start(bf16[512,256]{1,0:T(8,128)(2,1)S(1)} %get-tuple-element.80), channel_id=1, source_target_pairs={{0,2},{2,0},{4,6},{6,4},{8,10},{10,8},{12,14},{14,12},{16,18},{18,... | collective-permute-start | bytes 786440 | tf_op jit(solution)/shard_map/ppermute | solution.py:61
  92.4 9.2 %collective-permute-start.14 = (bf16[512,256]{1,0:T(8,128)(2,1)S(1)}, bf16[512,256]{1,0:T(8,128)(2,1)S(1)}, u32[]{:S(2)}, u32[]{:S(2)}) collective-permute-start(bf16[512,256]{1,0:T(8,128)(2,1)S(1)} %get-tuple-element.78), channel_id=1, source_target_pairs={{0,1},{1,0},{2,3},{3,2},{4,5},{5,4},{6,7},{7,6},{8,9},{9,8},{10,11... | collective-permute-start | bytes 786440 | tf_op jit(solution)/shard_map/ppermute | solution.py:95
  93.2 13.0 %collective-permute-start.13 = (bf16[512,256]{1,0:T(8,128)(2,1)S(1)}, bf16[512,256]{1,0:T(8,128)(2,1)S(1)}, u32[]{:S(2)}, u32[]{:S(2)}) collective-permute-start(bf16[512,256]{1,0:T(8,128)(2,1)S(1)} %get-tuple-element.77), channel_id=1, source_target_pairs={{0,3},{1,2},{2,1},{3,0},{4,7},{5,6},{6,5},{7,4},{8,11},{9,10},{10,... | collective-permute-start | bytes 786440 | tf_op jit(solution)/shard_map/ppermute | solution.py:103
  (4 other events, 4.1 us)

commit v18 on v17

--- a/solution.py
+++ b/solution.py
@@ -26,7 +26,7 @@
 bf16 = jnp.bfloat16
 
 
-def params(mib=16):
+def params(mib=12):
     return pltpu.CompilerParams(vmem_limit_bytes=mib << 20)
 
 

time: 109 us -> 109 us (level)
  no operation moved by 1% of the time
where the time goes in v18:
time: 109 us; the launch traced here: 108 us
  Pallas kernels  45.7 us (42%)
  waiting for transfers between devices  33.4 us (31%)
  starting transfers between devices  22.8 us (21%)
  local copies, waits for them, and re-layouts  4.83 us (4%)
    pallas_call x2, Pallas kernels, attend(): pl.pallas_call(functools.partial(attend_kernel, plan, slot), in_specs=[sm...  18.4 us
    ppermute x4, waiting for transfers between devices, round(): return lax.ppermute(block, 'tm', pairs)  16.9 us
    all_to_all x2, starting transfers between devices, exchange(): lax.all_to_all(blocks, 'tm', split_axis=0, concat_axis=0, tiled=True, axi...  8.82 us
    pallas_call x3, Pallas kernels, place_tokens(): pl.pallas_call(functools.partial(place_kernel, slots, parts, start), out_...  7.17 us
    all_to_all x2, waiting for transfers between devices, exchange(): lax.all_to_all(blocks, 'tm', split_axis=0, concat_axis=0, tiled=True, axi...  6.57 us
    ppermute x2, waiting for transfers between devices, to_peer(): return lax.ppermute(block, 'head', pairs)  6.14 us
    ppermute x4, starting transfers between devices, cross(): return lax.ppermute(block, 'tm', pairs)  5.39 us
    unnamed x37, local copies, waits for them, and re-layouts  4.81 us
  transfers between devices with their start and end apart: 18, of which 9 were waited for; matrix products, arithmetic and copies ran while one was open for 1% of the time, Pallas kernels for 32%

profile of v18, /device:TPU:0, one launch (start us, length us, event | category | flops | bytes accessed | tf_op | source)
XLA Modules:
  0.0 108.1 jit_solution(2612693470668617321)
XLA Ops:
  0.5 3.0 %collective-permute-start.9 = (bf16[512,1024]{1,0:T(8,128)(2,1)}, bf16[512,1024]{1,0:T(8,128)(2,1)S(1)}, u32[]{:S(2)}, u32[]{:S(2)}) collective-permute-start(bf16[512,1024]{1,0:T(8,128)(2,1)} %bitcast.6), channel_id=1, source_target_pairs={{0,1},{1,0},{2,3},{3,2},{4,5},{5,4},{6,7},{7,6},{8,9},{9,8},{10,11... | collective-permute-start | bytes 3145736 | tf_op jit(solution)/shard_map/ppermute | solution.py:95
  3.5 1.0 copy-done.11
  4.7 1.8 %collective-permute-start.2 = (bf16[128,1280]{1,0:T(8,128)(2,1)S(1)}, bf16[128,1280]{1,0:T(8,128)(2,1)}, u32[]{:S(2)}, u32[]{:S(2)}) collective-permute-start(bf16[128,1280]{1,0:T(8,128)(2,1)S(1)} %reorder.3.refs_2_.refs_3_), channel_id=1, source_target_pairs={{0,8},{2,10},{4,12},{6,14},{8,16},{10,18},{12,20},{14,22},{16,24},... | collective-permute-start | bytes 983048 | tf_op jit(solution)/shard_map/ppermute | solution.py:66
  6.6 1.5 %collective-permute-start.3 = (bf16[128,1280]{1,0:T(8,128)(2,1)S(1)}, bf16[128,1280]{1,0:T(8,128)(2,1)}, u32[]{:S(2)}, u32[]{:S(2)}) collective-permute-start(bf16[128,1280]{1,0:T(8,128)(2,1)S(1)} %reorder.3.refs_2_.refs_3_), channel_id=1, source_target_pairs={{0,4},{2,6},{4,0},{6,2},{8,12},{10,14},{12,8},{14,10},{16,20},{18,... | collective-permute-start | bytes 983048 | tf_op jit(solution)/shard_map/ppermute | solution.py:71
  10.2 1.4 %copy-done.3 = bf16[1024,1024]{1,0:T(8,128)(2,1)} copy-done((bf16[1024,1024]{1,0:T(8,128)(2,1)}, bf16[1024,1024]{1,0:T(8,128)(2,1)S(1)}, u32[]{:S(2)}) %copy-start.3) | copy-done | bytes 2097176
  12.4 4.3 %collective-permute-done.2.refs_3_.refs_4_ = bf16[128,1280]{1,0:T(8,128)(2,1)} collective-permute-done((bf16[128,1280]{1,0:T(8,128)(2,1)S(1)}, bf16[128,1280]{1,0:T(8,128)(2,1)}, u32[]{:S(2)}, u32[]{:S(2)}) %collective-permute-start.2) | collective-permute-done | bytes 327712 | tf_op jit(solution)/shard_map/ppermute | solution.py:66
  16.7 1.0 collective-permute-start.4
  17.7 1.5 %collective-permute-start.5 = (bf16[128,1280]{1,0:T(8,128)(2,1)}, bf16[128,1280]{1,0:T(8,128)(2,1)S(1)}, u32[]{:S(2)}, u32[]{:S(2)}) collective-permute-start(bf16[128,1280]{1,0:T(8,128)(2,1)} %collective-permute-done.2.refs_3_.refs_4_), channel_id=1, source_target_pairs={{0,4},{2,6},{4,0},{6,2},{8,12},{10,14},{12,8},{14,10},{16,20},{18,... | collective-permute-start | bytes 983048 | tf_op jit(solution)/shard_map/ppermute | solution.py:71
  19.2 3.5 %place_tokens.3.refs_1_ = bf16[2048,1024]{1,0:T(8,128)(2,1)S(1)} custom-call(f32[1,1024]{1,0:T(1,128)S(1)} %rank_tokens.1.row_ref.rank_ref, bf16[512,1024]{1,0:T(8,128)(2,1)S(1)} %bitcast.7, bf16[512,1024]{1,0:T(8,128)(2,1)S(1)} %collective-permute-done.6.refs_1_), custom_call_target="tpu_custom_call" | custom-call | bytes 4096 | tf_op jit(solution)/shard_map/place_tokens/pallas_call | solution.py:288
  22.7 5.2 %collective-permute-done.4.refs_4_.refs_5_ = bf16[128,1280]{1,0:T(8,128)(2,1)S(1)} collective-permute-done((bf16[128,1280]{1,0:T(8,128)(2,1)}, bf16[128,1280]{1,0:T(8,128)(2,1)S(1)}, u32[]{:S(2)}, u32[]{:S(2)}) %collective-permute-start.4) | collective-permute-done | bytes 327712 | tf_op jit(solution)/shard_map/ppermute | solution.py:66
  28.0 1.3 %collective-permute-start.8 = (bf16[128,1280]{1,0:T(8,128)(2,1)S(1)}, bf16[128,1280]{1,0:T(8,128)(2,1)S(1)}, u32[]{:S(2)}, u32[]{:S(2)}) collective-permute-start(bf16[128,1280]{1,0:T(8,128)(2,1)S(1)} %collective-permute-done.4.refs_4_.refs_5_), channel_id=1, source_target_pairs={{0,4},{2,6},{4,0},{6,2},{8,12},{10,14},{12,8},{14,10},{16,20},{18,... | collective-permute-start | bytes 983048 | tf_op jit(solution)/shard_map/ppermute | solution.py:71
  29.3 1.9 %place_tokens.4.refs_0_.refs_1_ = bf16[1024,1024]{1,0:T(8,128)(2,1)S(1)} custom-call(f32[1,1024]{1,0:T(1,128)S(1)} %rank_tokens.1.row_ref.rank_ref, bf16[512,1024]{1,0:T(8,128)(2,1)S(1)} %collective-permute-done.9.refs_0_, bf16[2048,1024]{1,0:T(8,128)(2,1)S(1)} %place_tokens.3.refs_1_), custom_call_target="tpu_custom_call" | custom-call | bytes 4096 | tf_op jit(solution)/shard_map/place_tokens/pallas_call | solution.py:288
  31.2 6.9 %collective-permute-done.7.refs_5_.refs_6_ = bf16[128,1280]{1,0:T(8,128)(2,1)S(1)} collective-permute-done((bf16[128,1280]{1,0:T(8,128)(2,1)S(1)}, bf16[128,1280]{1,0:T(8,128)(2,1)S(1)}, u32[]{:S(2)}, u32[]{:S(2)}) %collective-permute-start.7) | collective-permute-done | bytes 327712 | tf_op jit(solution)/shard_map/ppermute | solution.py:66
  38.1 1.1 collective-permute-start.11
  39.5 1.9 %place_tokens.5.refs_1_ = bf16[1024,1024]{1,0:T(8,128)(2,1)S(1)} custom-call(f32[1,1024]{1,0:T(1,128)S(1)} %rank_tokens.1.row_ref.rank_ref, bf16[512,1024]{1,0:T(8,128)(2,1)S(1)} %collective-permute-done.10.refs_0_, bf16[2048,1024]{1,0:T(8,128)(2,1)S(1)} %place_tokens.3.refs_1_), custom_call_target="tpu_custom_call" | custom-call | bytes 4096 | tf_op jit(solution)/shard_map/place_tokens/pallas_call | solution.py:288
  41.4 4.7 %project.1 = (f32[2048,256]{1,0:T(8,128)S(1)}, f32[256,2048]{1,0:T(8,128)S(1)}, bf16[2048,128]{1,0:T(8,128)(2,1)S(1)}) custom-call(bf16[1024,1024]{1,0:T(8,128)(2,1)S(1)} %place_tokens.4.refs_0_.refs_1_, bf16[1024,1024]{1,0:T(8,128)(2,1)S(1)} %place_tokens.5.refs_1_, bf16[128,1280]{1,0:T(8,128)(2,1)S(1)} %reorder.3.refs_2_.refs_3_, ...), custom_call_target="tpu_custom_call" | custom-call | bytes 4096 | tf_op jit(solution)/shard_map/project/pallas_call | solution.py:340
  46.6 3.9 %block_updates.1 = (bf16[2,2048,128]{2,1,0:T(8,128)(2,1)S(1)}, bf16[8,272,128]{2,1,0:T(8,128)(2,1)}) custom-call(f32[4,32,128]{2,1,0:T(8,128)S(1)} %hold.1.decay_ref.decay_in, f32[2048,256]{1,0:T(8,128)S(1)} %get-tuple-element.63.refs_0_, f32[256,2048]{1,0:T(8,128)S(1)} %get-tuple-element.64.refs_1_, bf16[2048,128]{1,0:T(8,128)(2,1)S(1)} %get-tuple-element.65.refs_2_, ...), custom_call_target="tpu_custom_call" | custom-call | flops 1073741824 | bytes 3145728 | tf_op jit(solution)/shard_map/block_updates/pallas_call | solution.py:438
  50.6 1.0 copy-done.15
  51.5 5.1 %all-to-all-start = ((bf16[8,272,128]{2,1,0:T(8,128)(2,1)}), bf16[8,272,128]{2,1,0:T(8,128)(2,1)S(1)}, u32[]{:S(2)}, u32[]{:S(2)}) async-start(bf16[8,272,128]{2,1,0:T(8,128)(2,1)} %get-tuple-element.66), calls=%async_computation | async-start | bytes 1114112 | tf_op jit(solution)/shard_map/all_to_all | solution.py:842
  57.3 9.1 %attend.2 = (f32[1024,256]{1,0:T(8,128)}, bf16[1024,256]{1,0:T(8,128)(2,1)}) custom-call(s32[16,4]{1,0:T(8,128)} %copy.7.refs_0_, bf16[1024,1024]{1,0:T(8,128)(2,1)} %copy-done.2, bf16[2,2048,128]{2,1,0:T(8,128)(2,1)} %copy-done.15, bf16[128,1280]{1,0:T(8,128)(2,1)} %copy-done.4, bf16[128,1280]{1,0:T(8,128)(2,1)} %collective-permute-done.2.refs_3_.refs_4_, ...), custom_call_target="tpu_custom_call" | custom-call | flops 4831838208 | bytes 11534336 | tf_op jit(solution)/shard_map/attend/pallas_call | solution.py:611
  66.4 2.8 %all-to-all-done.u_ref = bf16[8,272,128]{2,1,0:T(8,128)(2,1)S(1)} async-done(((bf16[8,272,128]{2,1,0:T(8,128)(2,1)}), bf16[8,272,128]{2,1,0:T(8,128)(2,1)S(1)}, u32[]{:S(2)}, u32[]{:S(2)}) %all-to-all-start) | async-done | bytes 557088 | tf_op jit(solution)/shard_map/all_to_all | solution.py:842
  69.2 0.9 scan_states.1
  70.1 3.7 %all-to-all-start.1 = ((bf16[8,256,128]{2,1,0:T(8,128)(2,1)}), bf16[8,256,128]{2,1,0:T(8,128)(2,1)S(1)}, u32[]{:S(2)}, u32[]{:S(2)}) async-start(bf16[8,256,128]{2,1,0:T(8,128)(2,1)} %scan_states.1), calls=%async_computation.1 | async-start | bytes 1048576 | tf_op jit(solution)/shard_map/all_to_all | solution.py:842
  73.8 9.3 %attend.3 = (f32[1024,256]{1,0:T(8,128)}, bf16[1024,256]{1,0:T(8,128)(2,1)}) custom-call(s32[16,4]{1,0:T(8,128)} %copy.7.refs_0_, bf16[1024,1024]{1,0:T(8,128)(2,1)} %copy-done.1, bf16[2,2048,128]{2,1,0:T(8,128)(2,1)} %copy-done.15, bf16[128,1280]{1,0:T(8,128)(2,1)} %copy-done.4, bf16[128,1280]{1,0:T(8,128)(2,1)} %collective-permute-done.2.refs_3_.refs_4_, ...), custom_call_target="tpu_custom_call" | custom-call | flops 4831838208 | bytes 11534336 | tf_op jit(solution)/shard_map/attend/pallas_call | solution.py:611
  83.2 3.8 %all-to-all-done.1 = bf16[8,256,128]{2,1,0:T(8,128)(2,1)S(1)} async-done(((bf16[8,256,128]{2,1,0:T(8,128)(2,1)}), bf16[8,256,128]{2,1,0:T(8,128)(2,1)S(1)}, u32[]{:S(2)}, u32[]{:S(2)}) %all-to-all-start.1) | async-done | bytes 524320 | tf_op jit(solution)/shard_map/all_to_all | solution.py:842
  87.7 4.5 %mix.1 = (bf16[512,256]{1,0:T(8,128)(2,1)S(1)}, bf16[512,256]{1,0:T(8,128)(2,1)S(1)}, bf16[512,256]{1,0:T(8,128)(2,1)S(1)}, bf16[512,256]{1,0:T(8,128)(2,1)S(1)}) custom-call(f32[4,32,128]{2,1,0:T(8,128)S(1)} %hold.1.decay_ref.decay_in, f32[1024,256]{1,0:T(8,128)} %get-tuple-element.70.refs_0_, f32[1024,256]{1,0:T(8,128)} %get-tuple-element.73.refs_1_, ...), custom_call_target="tpu_custom_call" | custom-call | flops 1073741824 | bytes 6291456 | tf_op jit(solution)/shard_map/mix/pallas_call | solution.py:714
  93.2 1.0 collective-permute-start.13
  94.2 1.2 %project_out.3.refs_1_ = f32[512,1024]{1,0:T(8,128)S(1)} custom-call(bf16[1024,1024]{1,0:T(8,128)(2,1)S(1)} %copy-done, bf16[512,256]{1,0:T(8,128)(2,1)S(1)} %get-tuple-element.79.refs_0_, bf16[512,256]{1,0:T(8,128)(2,1)S(1)} %collective-permute-done.15.refs_1_), custom_call_target="tpu_custom_call" | custom-call | bytes 2048 | tf_op jit(solution)/shard_map/project_out/pallas_call | solution.py:763
  95.4 6.1 %collective-permute-done.14.refs_0_ = bf16[512,256]{1,0:T(8,128)(2,1)S(1)} collective-permute-done((bf16[512,256]{1,0:T(8,128)(2,1)S(1)}, bf16[512,256]{1,0:T(8,128)(2,1)S(1)}, u32[]{:S(2)}, u32[]{:S(2)}) %collective-permute-start.14) | collective-permute-done | bytes 262176 | tf_op jit(solution)/shard_map/ppermute | solution.py:95
  101.5 1.5 %project_out.4.refs_1_ = f32[512,1024]{1,0:T(8,128)S(1)} custom-call(bf16[1024,1024]{1,0:T(8,128)(2,1)S(1)} %copy-done, bf16[512,256]{1,0:T(8,128)(2,1)S(1)} %collective-permute-done.14.refs_0_, f32[512,1024]{1,0:T(8,128)S(1)} %project_out.3.refs_1_), custom_call_target="tpu_custom_call" | custom-call | bytes 2048 | tf_op jit(solution)/shard_map/project_out/pallas_call | solution.py:763
  103.1 3.2 %collective-permute-done.13.refs_0_ = bf16[512,256]{1,0:T(8,128)(2,1)S(1)} collective-permute-done((bf16[512,256]{1,0:T(8,128)(2,1)S(1)}, bf16[512,256]{1,0:T(8,128)(2,1)S(1)}, u32[]{:S(2)}, u32[]{:S(2)}) %collective-permute-start.13) | collective-permute-done | bytes 262176 | tf_op jit(solution)/shard_map/ppermute | solution.py:103
  106.2 1.6 %project_out.5 = bf16[512,1024]{1,0:T(8,128)(2,1)} custom-call(bf16[1024,1024]{1,0:T(8,128)(2,1)S(1)} %copy-done, bf16[512,256]{1,0:T(8,128)(2,1)S(1)} %collective-permute-done.13.refs_0_, f32[512,1024]{1,0:T(8,128)S(1)} %project_out.4.refs_1_), custom_call_target="tpu_custom_call" | custom-call | bytes 2048 | tf_op jit(solution)/shard_map/project_out/pallas_call | solution.py:763
  (62 shorter events, 6.9 us)
Async XLA Ops:
  0.0 19.2 %copy-start.5 = (bf16[1,512,1024]{2,1,0:T(8,128)(2,1)S(1)}, bf16[1,512,1024]{2,1,0:T(8,128)(2,1)}, u32[]{:S(2)}) copy-start(bf16[1,512,1024]{2,1,0:T(8,128)(2,1)} %param.6) | copy-start | bytes 3145732
  0.0 19.2 %collective-permute-start.6 = (bf16[512,1024]{1,0:T(8,128)(2,1)}, bf16[512,1024]{1,0:T(8,128)(2,1)S(1)}, u32[]{:S(2)}, u32[]{:S(2)}) collective-permute-start(bf16[512,1024]{1,0:T(8,128)(2,1)} %bitcast.5), channel_id=1, source_target_pairs={{0,2},{2,0},{4,6},{6,4},{8,10},{10,8},{12,14},{14,12},{16,18},{18,... | collective-permute-start | bytes 3145736 | tf_op jit(solution)/shard_map/ppermute | solution.py:61
  0.5 4.1 %collective-permute-start.1 = (bf16[64,2560]{1,0:T(8,128)(2,1)}, bf16[64,2560]{1,0:T(8,128)(2,1)S(1)}, u32[]{:S(2)}, u32[]{:S(2)}) collective-permute-start(bf16[64,2560]{1,0:T(8,128)(2,1)} %refs_0_.3), channel_id=1, source_target_pairs={{0,2},{2,0},{4,6},{6,4},{8,10},{10,8},{12,14},{14,12},{16,18},{18,... | collective-permute-start | bytes 983048 | tf_op jit(solution)/shard_map/ppermute | solution.py:61
  0.5 28.8 %collective-permute-start.9 = (bf16[512,1024]{1,0:T(8,128)(2,1)}, bf16[512,1024]{1,0:T(8,128)(2,1)S(1)}, u32[]{:S(2)}, u32[]{:S(2)}) collective-permute-start(bf16[512,1024]{1,0:T(8,128)(2,1)} %bitcast.6), channel_id=1, source_target_pairs={{0,1},{1,0},{2,3},{3,2},{4,5},{5,4},{6,7},{7,6},{8,9},{9,8},{10,11... | collective-permute-start | bytes 3145736 | tf_op jit(solution)/shard_map/ppermute | solution.py:95
  4.5 7.1 %copy-start.14 = (f32[1,8,16]{2,1,0:T(8,128)S(1)}, f32[1,8,16]{2,1,0:T(8,128)}, u32[]{:S(2)}) copy-start(f32[1,8,16]{2,1,0:T(8,128)} %param.11) | copy-start | bytes 1540
  4.7 36.6 %copy-start.4 = (bf16[128,1280]{1,0:T(8,128)(2,1)}, bf16[128,1280]{1,0:T(8,128)(2,1)S(1)}, u32[]{:S(2)}) copy-start(bf16[128,1280]{1,0:T(8,128)(2,1)S(1)} %reorder.3.refs_2_.refs_3_) | copy-start | bytes 983044
  4.7 12.0 %collective-permute-start.2 = (bf16[128,1280]{1,0:T(8,128)(2,1)S(1)}, bf16[128,1280]{1,0:T(8,128)(2,1)}, u32[]{:S(2)}, u32[]{:S(2)}) collective-permute-start(bf16[128,1280]{1,0:T(8,128)(2,1)S(1)} %reorder.3.refs_2_.refs_3_), channel_id=1, source_target_pairs={{0,8},{2,10},{4,12},{6,14},{8,16},{10,18},{12,20},{14,22},{16,24},... | collective-permute-start | bytes 983048 | tf_op jit(solution)/shard_map/ppermute | solution.py:66
  6.6 10.1 %collective-permute-start.3 = (bf16[128,1280]{1,0:T(8,128)(2,1)S(1)}, bf16[128,1280]{1,0:T(8,128)(2,1)}, u32[]{:S(2)}, u32[]{:S(2)}) collective-permute-start(bf16[128,1280]{1,0:T(8,128)(2,1)S(1)} %reorder.3.refs_2_.refs_3_), channel_id=1, source_target_pairs={{0,4},{2,6},{4,0},{6,2},{8,12},{10,14},{12,8},{14,10},{16,20},{18,... | collective-permute-start | bytes 983048 | tf_op jit(solution)/shard_map/ppermute | solution.py:71
  8.0 1.4 %collective-permute-start = (f32[8,16]{1,0:T(8,128)}, f32[8,16]{1,0:T(8,128)S(1)}, u32[]{:S(2)}, u32[]{:S(2)}) collective-permute-start(f32[8,16]{1,0:T(8,128)} %bitcast.9), channel_id=1, source_target_pairs={{0,2},{2,0},{4,6},{6,4},{8,10},{10,8},{12,14},{14,12},{16,18},{18,... | collective-permute-start | bytes 1544 | tf_op jit(solution)/shard_map/ppermute | solution.py:61
  16.7 11.2 %collective-permute-start.4 = (bf16[128,1280]{1,0:T(8,128)(2,1)}, bf16[128,1280]{1,0:T(8,128)(2,1)S(1)}, u32[]{:S(2)}, u32[]{:S(2)}) collective-permute-start(bf16[128,1280]{1,0:T(8,128)(2,1)} %collective-permute-done.2.refs_3_.refs_4_), channel_id=1, source_target_pairs={{0,8},{2,10},{4,12},{6,14},{8,16},{10,18},{12,20},{14,22},{16,24},... | collective-permute-start | bytes 983048 | tf_op jit(solution)/shard_map/ppermute | solution.py:66
  17.7 10.2 %collective-permute-start.5 = (bf16[128,1280]{1,0:T(8,128)(2,1)}, bf16[128,1280]{1,0:T(8,128)(2,1)S(1)}, u32[]{:S(2)}, u32[]{:S(2)}) collective-permute-start(bf16[128,1280]{1,0:T(8,128)(2,1)} %collective-permute-done.2.refs_3_.refs_4_), channel_id=1, source_target_pairs={{0,4},{2,6},{4,0},{6,2},{8,12},{10,14},{12,8},{14,10},{16,20},{18,... | collective-permute-start | bytes 983048 | tf_op jit(solution)/shard_map/ppermute | solution.py:71
  27.9 13.4 %copy-start.9 = (bf16[128,1280]{1,0:T(8,128)(2,1)}, bf16[128,1280]{1,0:T(8,128)(2,1)S(1)}, u32[]{:S(2)}) copy-start(bf16[128,1280]{1,0:T(8,128)(2,1)S(1)} %collective-permute-done.4.refs_4_.refs_5_) | copy-start | bytes 983044
  27.9 13.4 %copy-start.10 = (bf16[128,1280]{1,0:T(8,128)(2,1)}, bf16[128,1280]{1,0:T(8,128)(2,1)S(1)}, u32[]{:S(2)}) copy-start(bf16[128,1280]{1,0:T(8,128)(2,1)S(1)} %collective-permute-done.5.refs_7_.refs_8_) | copy-start | bytes 983044
  27.9 10.2 %collective-permute-start.7 = (bf16[128,1280]{1,0:T(8,128)(2,1)S(1)}, bf16[128,1280]{1,0:T(8,128)(2,1)S(1)}, u32[]{:S(2)}, u32[]{:S(2)}) collective-permute-start(bf16[128,1280]{1,0:T(8,128)(2,1)S(1)} %collective-permute-done.4.refs_4_.refs_5_), channel_id=1, source_target_pairs={{0,8},{2,10},{4,12},{6,14},{8,16},{10,18},{12,20},{14,22},{16,24},... | collective-permute-start | bytes 983048 | tf_op jit(solution)/shard_map/ppermute | solution.py:66
  28.0 10.1 %collective-permute-start.8 = (bf16[128,1280]{1,0:T(8,128)(2,1)S(1)}, bf16[128,1280]{1,0:T(8,128)(2,1)S(1)}, u32[]{:S(2)}, u32[]{:S(2)}) collective-permute-start(bf16[128,1280]{1,0:T(8,128)(2,1)S(1)} %collective-permute-done.4.refs_4_.refs_5_), channel_id=1, source_target_pairs={{0,4},{2,6},{4,0},{6,2},{8,12},{10,14},{12,8},{14,10},{16,20},{18,... | collective-permute-start | bytes 983048 | tf_op jit(solution)/shard_map/ppermute | solution.py:71
  29.3 10.2 %collective-permute-start.10 = (bf16[512,1024]{1,0:T(8,128)(2,1)S(1)}, bf16[512,1024]{1,0:T(8,128)(2,1)S(1)}, u32[]{:S(2)}, u32[]{:S(2)}) collective-permute-start(bf16[512,1024]{1,0:T(8,128)(2,1)S(1)} %collective-permute-done.9.refs_0_), channel_id=1, source_target_pairs={{0,2},{2,0},{4,6},{6,4},{8,10},{10,8},{12,14},{14,12},{16,18},{18,... | collective-permute-start | bytes 3145736 | tf_op jit(solution)/shard_map/ppermute | solution.py:61
  31.2 10.2 %copy-start.2 = (bf16[1024,1024]{1,0:T(8,128)(2,1)}, bf16[1024,1024]{1,0:T(8,128)(2,1)S(1)}, u32[]{:S(2)}) copy-start(bf16[1024,1024]{1,0:T(8,128)(2,1)S(1)} %place_tokens.4.refs_0_.refs_1_) | copy-start | bytes 6291460
  38.1 3.3 %copy-start.6 = (bf16[128,1280]{1,0:T(8,128)(2,1)}, bf16[128,1280]{1,0:T(8,128)(2,1)S(1)}, u32[]{:S(2)}) copy-start(bf16[128,1280]{1,0:T(8,128)(2,1)S(1)} %collective-permute-done.7.refs_5_.refs_6_) | copy-start | bytes 983044
  38.1 3.3 %copy-start.7 = (bf16[128,1280]{1,0:T(8,128)(2,1)}, bf16[128,1280]{1,0:T(8,128)(2,1)S(1)}, u32[]{:S(2)}) copy-start(bf16[128,1280]{1,0:T(8,128)(2,1)S(1)} %collective-permute-done.8.refs_8_.refs_9_) | copy-start | bytes 983044
  38.1 8.0 %collective-permute-start.11 = (bf16[64,1280]{1,0:T(8,128)(2,1)S(1)}, bf16[64,1280]{1,0:T(8,128)(2,1)S(1)}, u32[]{:S(2)}, u32[]{:S(2)}) collective-permute-start(bf16[64,1280]{1,0:T(8,128)(2,1)S(1)} %slice.6), channel_id=1, source_target_pairs={{0,4},{2,6},{4,0},{6,2},{8,12},{10,14},{12,8},{14,10},{16,20},{18,... | collective-permute-start | bytes 491528 | tf_op jit(solution)/shard_map/ppermute | solution.py:71
  39.2 7.3 %collective-permute-start.12 = (bf16[64,1280]{1,0:T(8,128)(2,1)S(1)}, bf16[64,1280]{1,0:T(8,128)(2,1)S(1)}, u32[]{:S(2)}, u32[]{:S(2)}) collective-permute-start(bf16[64,1280]{1,0:T(8,128)(2,1)S(1)} %slice.7), channel_id=1, source_target_pairs={{0,8},{2,10},{4,12},{6,14},{8,16},{10,18},{12,20},{14,22},{16,24},... | collective-permute-start | bytes 491528 | tf_op jit(solution)/shard_map/ppermute | solution.py:66
  41.4 4.7 %copy-start.1 = (bf16[1024,1024]{1,0:T(8,128)(2,1)}, bf16[1024,1024]{1,0:T(8,128)(2,1)S(1)}, u32[]{:S(2)}) copy-start(bf16[1024,1024]{1,0:T(8,128)(2,1)S(1)} %place_tokens.5.refs_1_) | copy-start | bytes 6291460
  46.1 4.4 %copy-start.12 = (bf16[64,1280]{1,0:T(8,128)(2,1)}, bf16[64,1280]{1,0:T(8,128)(2,1)S(1)}, u32[]{:S(2)}) copy-start(bf16[64,1280]{1,0:T(8,128)(2,1)S(1)} %collective-permute-done.11.refs_3_.refs_10_) | copy-start | bytes 491524
  46.6 4.0 %copy-start.13 = (bf16[64,1280]{1,0:T(8,128)(2,1)}, bf16[64,1280]{1,0:T(8,128)(2,1)S(1)}, u32[]{:S(2)}) copy-start(bf16[64,1280]{1,0:T(8,128)(2,1)S(1)} %collective-permute-done.12.refs_4_.refs_11_) | copy-start | bytes 491524
  46.6 10.0 %copy-start.17 = (s32[16,4]{0,1:T(4,128)S(1)}, s32[16,4]{0,1:T(4,128)}, u32[]{:S(2)}) copy-start(s32[16,4]{0,1:T(4,128)} %param.10) | copy-start | bytes 772
  51.5 17.7 %all-to-all-start = ((bf16[8,272,128]{2,1,0:T(8,128)(2,1)}), bf16[8,272,128]{2,1,0:T(8,128)(2,1)S(1)}, u32[]{:S(2)}, u32[]{:S(2)}) async-start(bf16[8,272,128]{2,1,0:T(8,128)(2,1)} %get-tuple-element.66), calls=%async_computation | async-start | bytes 1114112 | tf_op jit(solution)/shard_map/all_to_all | solution.py:842
  70.1 16.8 %all-to-all-start.1 = ((bf16[8,256,128]{2,1,0:T(8,128)(2,1)}), bf16[8,256,128]{2,1,0:T(8,128)(2,1)S(1)}, u32[]{:S(2)}, u32[]{:S(2)}) async-start(bf16[8,256,128]{2,1,0:T(8,128)(2,1)} %scan_states.1), calls=%async_computation.1 | async-start | bytes 1048576 | tf_op jit(solution)/shard_map/all_to_all | solution.py:842
  73.8 13.9 %copy-start.8 = (bf16[1024,256]{1,0:T(8,128)(2,1)S(1)}, bf16[1024,256]{1,0:T(8,128)(2,1)}, u32[]{:S(2)}) copy-start(bf16[1024,256]{1,0:T(8,128)(2,1)} %get-tuple-element.74.refs_2_) | copy-start | bytes 1572868
  87.7 6.5 %copy-start = (bf16[1024,1024]{1,0:T(8,128)(2,1)S(1)}, bf16[1024,1024]{1,0:T(8,128)(2,1)}, u32[]{:S(2)}) copy-start(bf16[1024,1024]{1,0:T(8,128)(2,1)} %w_ref.5) | copy-start | bytes 6291460
  92.3 1.9 %collective-permute-start.15 = (bf16[512,256]{1,0:T(8,128)(2,1)S(1)}, bf16[512,256]{1,0:T(8,128)(2,1)S(1)}, u32[]{:S(2)}, u32[]{:S(2)}) collective-permute-start(bf16[512,256]{1,0:T(8,128)(2,1)S(1)} %get-tuple-element.80), channel_id=1, source_target_pairs={{0,2},{2,0},{4,6},{6,4},{8,10},{10,8},{12,14},{14,12},{16,18},{18,... | collective-permute-start | bytes 786440 | tf_op jit(solution)/shard_map/ppermute | solution.py:61
  92.4 9.2 %collective-permute-start.14 = (bf16[512,256]{1,0:T(8,128)(2,1)S(1)}, bf16[512,256]{1,0:T(8,128)(2,1)S(1)}, u32[]{:S(2)}, u32[]{:S(2)}) collective-permute-start(bf16[512,256]{1,0:T(8,128)(2,1)S(1)} %get-tuple-element.78), channel_id=1, source_target_pairs={{0,1},{1,0},{2,3},{3,2},{4,5},{5,4},{6,7},{7,6},{8,9},{9,8},{10,11... | collective-permute-start | bytes 786440 | tf_op jit(solution)/shard_map/ppermute | solution.py:95
  93.2 13.0 %collective-permute-start.13 = (bf16[512,256]{1,0:T(8,128)(2,1)S(1)}, bf16[512,256]{1,0:T(8,128)(2,1)S(1)}, u32[]{:S(2)}, u32[]{:S(2)}) collective-permute-start(bf16[512,256]{1,0:T(8,128)(2,1)S(1)} %get-tuple-element.77), channel_id=1, source_target_pairs={{0,3},{1,2},{2,1},{3,0},{4,7},{5,6},{6,5},{7,4},{8,11},{9,10},{10,... | collective-permute-start | bytes 786440 | tf_op jit(solution)/shard_map/ppermute | solution.py:103
  (4 other events, 4.1 us)

commit v19 on v15

--- a/solution.py
+++ b/solution.py
@@ -259,38 +259,44 @@
     return jnp.where(places.astype(f32) == rank, 1.0, 0.0).astype(bf16)
 
 
-def place_kernel(merge, parts, start, rank_ref, *refs):
-    frame_refs, refs = refs[:parts], refs[parts:]
-    base_refs, (x_ref, normed) = refs[:-2], refs[-2:]
+def place_kernel(slots, parts, start, bases, rank_ref, *refs):
+    frame_refs, refs = refs[: len(slots) * parts], refs[len(slots) * parts :]
+    base_refs, before_refs, (x_ref, normed) = refs[:bases], refs[bases:-2], refs[-2:]
     tokens = rank_ref.shape[1]
     count = normed.shape[1]
     step = 256
-    at = 0
-    for ref in frame_refs:
-        normalise(ref, normed.at[at // count], at % count)
-        at += ref.shape[0]
+    done = 0
+    for ref in before_refs:
+        x_ref[done : done + ref.shape[0], :] = ref[...]
+        done += ref.shape[0]
+    for i in range(len(slots)):
+        at = 0
+        for ref in frame_refs[i * parts : (i + 1) * parts]:
+            normalise(ref, normed.at[i], at)
+            at += ref.shape[0]
     for at in range(0, tokens, step):
         pick = picks(rank_ref[:, start : start + count], at, step)
-        for s in range(merge):
-            there = slice(s * tokens + at, s * tokens + at + step)
-            placed = jnp.dot(pick, normed[s], preferred_element_type=f32).astype(bf16)
+        for i, slot in enumerate(slots):
+            placed = jnp.dot(pick, normed[i], preferred_element_type=f32).astype(bf16)
             for base in base_refs:
-                placed = base[there, :] + placed
-            x_ref[there, :] = placed
-
-
-def place_tokens(plan, rank, start, frames, base):
+                placed = base[slot * tokens + at : slot * tokens + at + step, :] + placed
+            x_ref[done + i * tokens + at : done + i * tokens + at + step, :] = placed
+
+
+def place_tokens(slots, rank, start, frames, base, before=()):
     tokens = rank.shape[1]
     width = frames[0].shape[1]
-    count = sum(f.shape[0] for f in frames) // plan.merge
-    return pl.pallas_call(
-        functools.partial(place_kernel, plan.merge, len(frames), start),
-        out_shape=jax.ShapeDtypeStruct((plan.merge * tokens, width), bf16),
-        scratch_shapes=[pltpu.VMEM((plan.merge, count, width), bf16)],
+    parts = len(frames) // len(slots)
+    count = parts * frames[0].shape[0]
+    rows = len(slots) * tokens + sum(b.shape[0] for b in before)
+    return pl.pallas_call(
+        functools.partial(place_kernel, slots, parts, start, len(base)),
+        out_shape=jax.ShapeDtypeStruct((rows, width), bf16),
+        scratch_shapes=[pltpu.VMEM((len(slots), count, width), bf16)],
         compiler_params=params(),
         cost_estimate=cost(0, 4 * tokens),
         name="place_tokens",
-    )(rank, *frames, *base)
+    )(rank, *frames, *base, *before)
 
 
 def project_kernel(plan, x_ref, *refs):
@@ -785,10 +791,10 @@
     tables = decay_tables(plan, rates, groups)
     rank = rank_tokens(ids, groups)
 
-    def fill(arriving, part):
-        if plan.merge == 2:
-            arriving = arriving + [plan.swap(tokens) for tokens in arriving]
-        return place_tokens(plan, rank, local_tokens, arriving, [part])
+    def fill(slot, arriving, part, before):
+        if slot == 1:
+            arriving = [plan.swap(tokens) for tokens in arriving]
+        return place_tokens([slot], rank, local_tokens, arriving, [part], before)
 
     if plan.ringed:
         blocks, crossed = [block], []
@@ -800,15 +806,19 @@
                 with_ = (places, tables)
             if k == min(1, plan.along - 2):
                 rank, owns, _ = lax.optimization_barrier((rank, owns, blocks[-1]))
-                part = with_ = place_tokens(plan, rank, 0, owns, [])
+                part = with_ = place_tokens(list(range(plan.merge)), rank, 0, owns, [])
             if k == plan.along - 2:
                 arriving, _ = lax.optimization_barrier((arriving, blocks[-1]))
-                x = fill(arriving, part)
+                x = fill(0, arriving, part, [])
             passed, across, with_ = lax.optimization_barrier(
                 (plan.round(blocks[-1]), plan.cross(blocks[-1]), with_)
             )
             if k == plan.along - 2:
-                tables, passed, across = lax.optimization_barrier((tables, passed, across))
+                tables, passed, across, x = lax.optimization_barrier(
+                    (tables, passed, across, x)
+                )
+                if plan.merge == 2:
+                    x = fill(1, arriving, part, [x])
                 tables, passed, across = lax.optimization_barrier(
                     (hold(tables), passed, across)
                 )
@@ -821,7 +831,10 @@
             lax.all_gather(block, "tm", axis=0, tiled=True, axis_index_groups=plan.groups())
         ]
         places = back_tokens(rank)
-        x = fill(arriving, place_tokens(plan, rank, 0, owns, []))
+        part = place_tokens(list(range(plan.merge)), rank, 0, owns, [])
+        x = fill(0, arriving, part, [])
+        if plan.merge == 2:
+            x = fill(1, arriving, part, [x])
     if plan.ringed:
         v, b, x_last = project(plan, x, weights[:-2])
         local, total = block_updates(plan, tables, v, b, x_last, last, groups)

time: 107 us -> 106 us (level)
  starting transfers between devices: 23.4 us -> 22.2 us
    all_to_all x2, starting transfers between devices: 8.57 us -> 7.26 us  [exchange(): lax.all_to_all(blocks, 'tm', split_axis=0, concat_axis=0, tiled=True, axi...]
    pallas_call x2 -> x3, Pallas kernels: 8.25 us -> 8.53 us  [place_tokens(): pl.pallas_call(functools.partial(place_kernel, slots, parts, start, len(b...]
  transfers between devices with their start and end apart: 18 -> 18, of which waited for: 9 -> 9; matrix products, arithmetic and copies ran while one was open for 1% -> 1% of each run, Pallas kernels for 32% -> 33%
where the time goes in v19:
time: 106 us; the launch traced here: 105 us
  Pallas kernels  45.7 us (43%)
  waiting for transfers between devices  32.4 us (31%)
  starting transfers between devices  22.2 us (21%)
  local copies, waits for them, and re-layouts  3.91 us (4%)
    pallas_call x2, Pallas kernels, attend(): pl.pallas_call(functools.partial(attend_kernel, plan, slot), in_specs=[sm...  18.5 us
    ppermute x4, waiting for transfers between devices, round(): return lax.ppermute(block, 'tm', pairs)  16.2 us
    pallas_call x3, Pallas kernels, place_tokens(): pl.pallas_call(functools.partial(place_kernel, slots, parts, start, len(b...  8.53 us
    all_to_all x2, starting transfers between devices, exchange(): lax.all_to_all(blocks, 'tm', split_axis=0, concat_axis=0, tiled=True, axi...  7.26 us
    all_to_all x2, waiting for transfers between devices, exchange(): lax.all_to_all(blocks, 'tm', split_axis=0, concat_axis=0, tiled=True, axi...  6.11 us
    ppermute x4, starting transfers between devices, cross(): return lax.ppermute(block, 'tm', pairs)  6.09 us
    ppermute x2, waiting for transfers between devices, to_peer(): return lax.ppermute(block, 'head', pairs)  5.92 us
    ppermute x2, starting transfers between devices, to_peer(): return lax.ppermute(block, 'head', pairs)  5.13 us
  transfers between devices with their start and end apart: 18, of which 9 were waited for; matrix products, arithmetic and copies ran while one was open for 1% of the time, Pallas kernels for 33%

profile of v19, /device:TPU:0, one launch (start us, length us, event | category | flops | bytes accessed | tf_op | source)
XLA Modules:
  0.0 105.4 jit_solution(13518556767292825726)
XLA Ops:
  0.5 3.0 %collective-permute-start.9 = (bf16[512,1024]{1,0:T(8,128)(2,1)}, bf16[512,1024]{1,0:T(8,128)(2,1)S(1)}, u32[]{:S(2)}, u32[]{:S(2)}) collective-permute-start(bf16[512,1024]{1,0:T(8,128)(2,1)} %bitcast.6), channel_id=1, source_target_pairs={{0,1},{1,0},{2,3},{3,2},{4,5},{5,4},{6,7},{7,6},{8,9},{9,8},{10,11... | collective-permute-start | bytes 3145736 | tf_op jit(solution)/shard_map/ppermute | solution.py:95
  3.5 1.0 copy-done.12
  4.7 1.6 %collective-permute-start.2 = (bf16[128,1280]{1,0:T(8,128)(2,1)S(1)}, bf16[128,1280]{1,0:T(8,128)(2,1)S(1)}, u32[]{:S(2)}, u32[]{:S(2)}) collective-permute-start(bf16[128,1280]{1,0:T(8,128)(2,1)S(1)} %reorder.3.refs_0_.refs_3_), channel_id=1, source_target_pairs={{0,8},{2,10},{4,12},{6,14},{8,16},{10,18},{12,20},{14,22},{16,24},... | collective-permute-start | bytes 983048 | tf_op jit(solution)/shard_map/ppermute | solution.py:66
  6.3 1.5 %collective-permute-start.3 = (bf16[128,1280]{1,0:T(8,128)(2,1)S(1)}, bf16[128,1280]{1,0:T(8,128)(2,1)S(1)}, u32[]{:S(2)}, u32[]{:S(2)}) collective-permute-start(bf16[128,1280]{1,0:T(8,128)(2,1)S(1)} %reorder.3.refs_0_.refs_3_), channel_id=1, source_target_pairs={{0,4},{2,6},{4,0},{6,2},{8,12},{10,14},{12,8},{14,10},{16,20},{18,... | collective-permute-start | bytes 983048 | tf_op jit(solution)/shard_map/ppermute | solution.py:71
  10.0 1.4 %copy-done.2 = bf16[1024,1024]{1,0:T(8,128)(2,1)} copy-done((bf16[1024,1024]{1,0:T(8,128)(2,1)}, bf16[1024,1024]{1,0:T(8,128)(2,1)S(1)}, u32[]{:S(2)}) %copy-start.2) | copy-done | bytes 2097176
  12.2 4.3 %collective-permute-done.2.refs_1_.refs_4_ = bf16[128,1280]{1,0:T(8,128)(2,1)S(1)} collective-permute-done((bf16[128,1280]{1,0:T(8,128)(2,1)S(1)}, bf16[128,1280]{1,0:T(8,128)(2,1)S(1)}, u32[]{:S(2)}, u32[]{:S(2)}) %collective-permute-start.2) | collective-permute-done | bytes 327712 | tf_op jit(solution)/shard_map/ppermute | solution.py:66
  16.5 1.0 collective-permute-start.4
  17.5 1.5 %collective-permute-start.5 = (bf16[128,1280]{1,0:T(8,128)(2,1)S(1)}, bf16[128,1280]{1,0:T(8,128)(2,1)S(1)}, u32[]{:S(2)}, u32[]{:S(2)}) collective-permute-start(bf16[128,1280]{1,0:T(8,128)(2,1)S(1)} %collective-permute-done.2.refs_1_.refs_4_), channel_id=1, source_target_pairs={{0,4},{2,6},{4,0},{6,2},{8,12},{10,14},{12,8},{14,10},{16,20},{18,... | collective-permute-start | bytes 983048 | tf_op jit(solution)/shard_map/ppermute | solution.py:71
  19.0 4.7 %place_tokens.3.refs_1_ = bf16[2048,1024]{1,0:T(8,128)(2,1)S(1)} custom-call(f32[1,1024]{1,0:T(1,128)S(1)} %rank_tokens.1.row_ref.rank_ref, bf16[512,1024]{1,0:T(8,128)(2,1)S(1)} %bitcast.7, bf16[512,1024]{1,0:T(8,128)(2,1)} %collective-permute-done.6.refs_1_), custom_call_target="tpu_custom_call" | custom-call | bytes 4096 | tf_op jit(solution)/shard_map/place_tokens/pallas_call | solution.py:292
  23.7 3.7 %collective-permute-done.4.refs_2_.refs_5_ = bf16[128,1280]{1,0:T(8,128)(2,1)S(1)} collective-permute-done((bf16[128,1280]{1,0:T(8,128)(2,1)S(1)}, bf16[128,1280]{1,0:T(8,128)(2,1)S(1)}, u32[]{:S(2)}, u32[]{:S(2)}) %collective-permute-start.4) | collective-permute-done | bytes 327712 | tf_op jit(solution)/shard_map/ppermute | solution.py:66
  27.4 1.6 %collective-permute-start.8 = (bf16[128,1280]{1,0:T(8,128)(2,1)S(1)}, bf16[128,1280]{1,0:T(8,128)(2,1)S(1)}, u32[]{:S(2)}, u32[]{:S(2)}) collective-permute-start(bf16[128,1280]{1,0:T(8,128)(2,1)S(1)} %collective-permute-done.4.refs_2_.refs_5_), channel_id=1, source_target_pairs={{0,4},{2,6},{4,0},{6,2},{8,12},{10,14},{12,8},{14,10},{16,20},{18,... | collective-permute-start | bytes 983048 | tf_op jit(solution)/shard_map/ppermute | solution.py:71
  29.0 1.8 %place_tokens.4.refs_2_ = bf16[1024,1024]{1,0:T(8,128)(2,1)S(1)} custom-call(f32[1,1024]{1,0:T(1,128)S(1)} %rank_tokens.1.row_ref.rank_ref, bf16[512,1024]{1,0:T(8,128)(2,1)S(1)} %collective-permute-done.9.refs_0_, bf16[2048,1024]{1,0:T(8,128)(2,1)S(1)} %place_tokens.3.refs_1_), custom_call_target="tpu_custom_call" | custom-call | bytes 4096 | tf_op jit(solution)/shard_map/place_tokens/pallas_call | solution.py:292
  30.9 6.4 %collective-permute-done.7.refs_3_.refs_6_ = bf16[128,1280]{1,0:T(8,128)(2,1)S(1)} collective-permute-done((bf16[128,1280]{1,0:T(8,128)(2,1)S(1)}, bf16[128,1280]{1,0:T(8,128)(2,1)S(1)}, u32[]{:S(2)}, u32[]{:S(2)}) %collective-permute-start.7) | collective-permute-done | bytes 327712 | tf_op jit(solution)/shard_map/ppermute | solution.py:66
  37.4 1.6 %collective-permute-start.11 = (bf16[64,1280]{1,0:T(8,128)(2,1)S(1)}, bf16[64,1280]{1,0:T(8,128)(2,1)S(1)}, u32[]{:S(2)}, u32[]{:S(2)}) collective-permute-start(bf16[64,1280]{1,0:T(8,128)(2,1)S(1)} %slice.6), channel_id=1, source_target_pairs={{0,4},{2,6},{4,0},{6,2},{8,12},{10,14},{12,8},{14,10},{16,20},{18,... | collective-permute-start | bytes 491528 | tf_op jit(solution)/shard_map/ppermute | solution.py:71
  39.2 2.0 %place_tokens.5.x_ref.refs_1_ = bf16[2048,1024]{1,0:T(8,128)(2,1)S(1)} custom-call(f32[1,1024]{1,0:T(1,128)S(1)} %rank_tokens.1.row_ref.rank_ref, bf16[512,1024]{1,0:T(8,128)(2,1)S(1)} %collective-permute-done.10.refs_0_, bf16[2048,1024]{1,0:T(8,128)(2,1)S(1)} %place_tokens.3.refs_1_, bf16[1024,1024]{1,0:T(8,128)(2,1)S(1)} %place_tokens.4.refs_2_), custom_call_target="tpu_custom_call" | custom-call | bytes 4096 | tf_op jit(solution)/shard_map/place_tokens/pallas_call | solution.py:292
  41.3 3.2 %project.1 = (f32[2048,256]{1,0:T(8,128)S(1)}, f32[256,2048]{1,0:T(8,128)S(1)}, bf16[2048,128]{1,0:T(8,128)(2,1)S(1)}) custom-call(bf16[2048,1024]{1,0:T(8,128)(2,1)S(1)} %place_tokens.5.x_ref.refs_1_, bf16[128,1280]{1,0:T(8,128)(2,1)S(1)} %reorder.3.refs_0_.refs_3_, bf16[128,1280]{1,0:T(8,128)(2,1)S(1)} %collective-permute-done.2.refs_1_.refs_4_, ...), custom_call_target="tpu_custom_call" | custom-call | bytes 4096 | tf_op jit(solution)/shard_map/project/pallas_call | solution.py:339
  44.6 1.8 %collective-permute-done.12.refs_4_.refs_11_ = bf16[64,1280]{1,0:T(8,128)(2,1)S(1)} collective-permute-done((bf16[64,1280]{1,0:T(8,128)(2,1)S(1)}, bf16[64,1280]{1,0:T(8,128)(2,1)S(1)}, u32[]{:S(2)}, u32[]{:S(2)}) %collective-permute-start.12) | collective-permute-done | bytes 163872 | tf_op jit(solution)/shard_map/ppermute | solution.py:66
  46.3 3.9 %block_updates.1 = (bf16[2,2048,128]{2,1,0:T(8,128)(2,1)S(1)}, bf16[8,272,128]{2,1,0:T(8,128)(2,1)}) custom-call(f32[4,32,128]{2,1,0:T(8,128)S(1)} %hold.1.decay_ref.decay_in, f32[2048,256]{1,0:T(8,128)S(1)} %get-tuple-element.63.refs_0_, f32[256,2048]{1,0:T(8,128)S(1)} %get-tuple-element.64.refs_1_, bf16[2048,128]{1,0:T(8,128)(2,1)S(1)} %get-tuple-element.65.refs_2_, ...), custom_call_target="tpu_custom_call" | custom-call | flops 1073741824 | bytes 3145728 | tf_op jit(solution)/shard_map/block_updates/pallas_call | solution.py:437
  50.3 3.5 %all-to-all-start = ((bf16[8,272,128]{2,1,0:T(8,128)(2,1)}), bf16[8,272,128]{2,1,0:T(8,128)(2,1)S(1)}, u32[]{:S(2)}, u32[]{:S(2)}) async-start(bf16[8,272,128]{2,1,0:T(8,128)(2,1)} %get-tuple-element.66), calls=%async_computation | async-start | bytes 1114112 | tf_op jit(solution)/shard_map/all_to_all | solution.py:846
  54.5 9.1 %attend.2 = (f32[1024,256]{1,0:T(8,128)}, bf16[1024,256]{1,0:T(8,128)(2,1)}) custom-call(s32[16,4]{1,0:T(8,128)} %copy.7.refs_0_, bf16[2048,1024]{1,0:T(8,128)(2,1)} %copy-done.1, bf16[2,2048,128]{2,1,0:T(8,128)(2,1)} %copy-done.16, bf16[128,1280]{1,0:T(8,128)(2,1)} %copy-done.3, bf16[128,1280]{1,0:T(8,128)(2,1)} %copy-done.8, bf16[128,1280]{1,0:T(8,128)(2,1)} %copy-done.10, ...), custom_call_target="tpu_custom_call" | custom-call | flops 4831838208 | bytes 11534336 | tf_op jit(solution)/shard_map/attend/pallas_call | solution.py:611
  63.7 2.4 %all-to-all-done.u_ref = bf16[8,272,128]{2,1,0:T(8,128)(2,1)S(1)} async-done(((bf16[8,272,128]{2,1,0:T(8,128)(2,1)}), bf16[8,272,128]{2,1,0:T(8,128)(2,1)S(1)}, u32[]{:S(2)}, u32[]{:S(2)}) %all-to-all-start) | async-done | bytes 557088 | tf_op jit(solution)/shard_map/all_to_all | solution.py:846
  66.1 0.9 scan_states.1
  67.0 3.7 %all-to-all-start.1 = ((bf16[8,256,128]{2,1,0:T(8,128)(2,1)}), bf16[8,256,128]{2,1,0:T(8,128)(2,1)S(1)}, u32[]{:S(2)}, u32[]{:S(2)}) async-start(bf16[8,256,128]{2,1,0:T(8,128)(2,1)} %scan_states.1), calls=%async_computation.1 | async-start | bytes 1048576 | tf_op jit(solution)/shard_map/all_to_all | solution.py:846
  70.7 9.4 %attend.3 = (f32[1024,256]{1,0:T(8,128)}, bf16[1024,256]{1,0:T(8,128)(2,1)}) custom-call(s32[16,4]{1,0:T(8,128)} %copy.7.refs_0_, bf16[2048,1024]{1,0:T(8,128)(2,1)} %copy-done.1, bf16[2,2048,128]{2,1,0:T(8,128)(2,1)} %copy-done.16, bf16[128,1280]{1,0:T(8,128)(2,1)} %copy-done.3, bf16[128,1280]{1,0:T(8,128)(2,1)} %copy-done.8, bf16[128,1280]{1,0:T(8,128)(2,1)} %copy-done.10, ...), custom_call_target="tpu_custom_call" | custom-call | flops 4831838208 | bytes 11534336 | tf_op jit(solution)/shard_map/attend/pallas_call | solution.py:611
  80.1 3.7 %all-to-all-done.1 = bf16[8,256,128]{2,1,0:T(8,128)(2,1)S(1)} async-done(((bf16[8,256,128]{2,1,0:T(8,128)(2,1)}), bf16[8,256,128]{2,1,0:T(8,128)(2,1)S(1)}, u32[]{:S(2)}, u32[]{:S(2)}) %all-to-all-start.1) | async-done | bytes 524320 | tf_op jit(solution)/shard_map/all_to_all | solution.py:846
  84.6 4.5 %mix.1 = (bf16[512,256]{1,0:T(8,128)(2,1)S(1)}, bf16[512,256]{1,0:T(8,128)(2,1)S(1)}, bf16[512,256]{1,0:T(8,128)(2,1)S(1)}, bf16[512,256]{1,0:T(8,128)(2,1)S(1)}) custom-call(f32[4,32,128]{2,1,0:T(8,128)S(1)} %hold.1.decay_ref.decay_in, f32[1024,256]{1,0:T(8,128)} %get-tuple-element.70.refs_0_, f32[1024,256]{1,0:T(8,128)} %get-tuple-element.73.refs_1_, ...), custom_call_target="tpu_custom_call" | custom-call | flops 1073741824 | bytes 6291456 | tf_op jit(solution)/shard_map/mix/pallas_call | solution.py:714
  89.2 2.2 %collective-permute-start.14 = (bf16[512,256]{1,0:T(8,128)(2,1)S(1)}, bf16[512,256]{1,0:T(8,128)(2,1)S(1)}, u32[]{:S(2)}, u32[]{:S(2)}) collective-permute-start(bf16[512,256]{1,0:T(8,128)(2,1)S(1)} %get-tuple-element.78), channel_id=1, source_target_pairs={{0,1},{1,0},{2,3},{3,2},{4,5},{5,4},{6,7},{7,6},{8,9},{9,8},{10,11... | collective-permute-start | bytes 786440 | tf_op jit(solution)/shard_map/ppermute | solution.py:95
  91.5 1.2 %project_out.3.refs_1_ = f32[512,1024]{1,0:T(8,128)S(1)} custom-call(bf16[1024,1024]{1,0:T(8,128)(2,1)S(1)} %copy-done, bf16[512,256]{1,0:T(8,128)(2,1)S(1)} %get-tuple-element.79.refs_0_, bf16[512,256]{1,0:T(8,128)(2,1)S(1)} %collective-permute-done.15.refs_1_), custom_call_target="tpu_custom_call" | custom-call | bytes 2048 | tf_op jit(solution)/shard_map/project_out/pallas_call | solution.py:763
  92.6 5.9 %collective-permute-done.14.refs_0_ = bf16[512,256]{1,0:T(8,128)(2,1)S(1)} collective-permute-done((bf16[512,256]{1,0:T(8,128)(2,1)S(1)}, bf16[512,256]{1,0:T(8,128)(2,1)S(1)}, u32[]{:S(2)}, u32[]{:S(2)}) %collective-permute-start.14) | collective-permute-done | bytes 262176 | tf_op jit(solution)/shard_map/ppermute | solution.py:95
  98.5 1.5 %project_out.4.refs_1_ = f32[512,1024]{1,0:T(8,128)S(1)} custom-call(bf16[1024,1024]{1,0:T(8,128)(2,1)S(1)} %copy-done, bf16[512,256]{1,0:T(8,128)(2,1)S(1)} %collective-permute-done.14.refs_0_, f32[512,1024]{1,0:T(8,128)S(1)} %project_out.3.refs_1_), custom_call_target="tpu_custom_call" | custom-call | bytes 2048 | tf_op jit(solution)/shard_map/project_out/pallas_call | solution.py:763
  100.1 3.6 %collective-permute-done.13.refs_0_ = bf16[512,256]{1,0:T(8,128)(2,1)S(1)} collective-permute-done((bf16[512,256]{1,0:T(8,128)(2,1)S(1)}, bf16[512,256]{1,0:T(8,128)(2,1)S(1)}, u32[]{:S(2)}, u32[]{:S(2)}) %collective-permute-start.13) | collective-permute-done | bytes 262176 | tf_op jit(solution)/shard_map/ppermute | solution.py:103
  103.6 1.6 %project_out.5 = bf16[512,1024]{1,0:T(8,128)(2,1)} custom-call(bf16[1024,1024]{1,0:T(8,128)(2,1)S(1)} %copy-done, bf16[512,256]{1,0:T(8,128)(2,1)S(1)} %collective-permute-done.13.refs_0_, f32[512,1024]{1,0:T(8,128)S(1)} %project_out.4.refs_1_), custom_call_target="tpu_custom_call" | custom-call | bytes 2048 | tf_op jit(solution)/shard_map/project_out/pallas_call | solution.py:763
  (64 shorter events, 5.8 us)
Async XLA Ops:
  0.0 19.0 %copy-start.4 = (bf16[1,512,1024]{2,1,0:T(8,128)(2,1)S(1)}, bf16[1,512,1024]{2,1,0:T(8,128)(2,1)}, u32[]{:S(2)}) copy-start(bf16[1,512,1024]{2,1,0:T(8,128)(2,1)} %param.6) | copy-start | bytes 3145732
  0.0 19.0 %collective-permute-start.6 = (bf16[512,1024]{1,0:T(8,128)(2,1)}, bf16[512,1024]{1,0:T(8,128)(2,1)}, u32[]{:S(2)}, u32[]{:S(2)}) collective-permute-start(bf16[512,1024]{1,0:T(8,128)(2,1)} %bitcast.5), channel_id=1, source_target_pairs={{0,2},{2,0},{4,6},{6,4},{8,10},{10,8},{12,14},{14,12},{16,18},{18,... | collective-permute-start | bytes 3145736 | tf_op jit(solution)/shard_map/ppermute | solution.py:61
  0.5 4.1 %collective-permute-start.1 = (bf16[64,2560]{1,0:T(8,128)(2,1)}, bf16[64,2560]{1,0:T(8,128)(2,1)S(1)}, u32[]{:S(2)}, u32[]{:S(2)}) collective-permute-start(bf16[64,2560]{1,0:T(8,128)(2,1)} %refs_0_.3), channel_id=1, source_target_pairs={{0,2},{2,0},{4,6},{6,4},{8,10},{10,8},{12,14},{14,12},{16,18},{18,... | collective-permute-start | bytes 983048 | tf_op jit(solution)/shard_map/ppermute | solution.py:61
  0.5 28.5 %collective-permute-start.9 = (bf16[512,1024]{1,0:T(8,128)(2,1)}, bf16[512,1024]{1,0:T(8,128)(2,1)S(1)}, u32[]{:S(2)}, u32[]{:S(2)}) collective-permute-start(bf16[512,1024]{1,0:T(8,128)(2,1)} %bitcast.6), channel_id=1, source_target_pairs={{0,1},{1,0},{2,3},{3,2},{4,5},{5,4},{6,7},{7,6},{8,9},{9,8},{10,11... | collective-permute-start | bytes 3145736 | tf_op jit(solution)/shard_map/ppermute | solution.py:95
  4.5 7.0 %copy-start.15 = (f32[1,8,16]{2,1,0:T(8,128)S(1)}, f32[1,8,16]{2,1,0:T(8,128)}, u32[]{:S(2)}) copy-start(f32[1,8,16]{2,1,0:T(8,128)} %param.11) | copy-start | bytes 1540
  4.7 36.5 %copy-start.3 = (bf16[128,1280]{1,0:T(8,128)(2,1)}, bf16[128,1280]{1,0:T(8,128)(2,1)S(1)}, u32[]{:S(2)}) copy-start(bf16[128,1280]{1,0:T(8,128)(2,1)S(1)} %reorder.3.refs_0_.refs_3_) | copy-start | bytes 983044
  4.7 11.7 %collective-permute-start.2 = (bf16[128,1280]{1,0:T(8,128)(2,1)S(1)}, bf16[128,1280]{1,0:T(8,128)(2,1)S(1)}, u32[]{:S(2)}, u32[]{:S(2)}) collective-permute-start(bf16[128,1280]{1,0:T(8,128)(2,1)S(1)} %reorder.3.refs_0_.refs_3_), channel_id=1, source_target_pairs={{0,8},{2,10},{4,12},{6,14},{8,16},{10,18},{12,20},{14,22},{16,24},... | collective-permute-start | bytes 983048 | tf_op jit(solution)/shard_map/ppermute | solution.py:66
  6.3 10.1 %collective-permute-start.3 = (bf16[128,1280]{1,0:T(8,128)(2,1)S(1)}, bf16[128,1280]{1,0:T(8,128)(2,1)S(1)}, u32[]{:S(2)}, u32[]{:S(2)}) collective-permute-start(bf16[128,1280]{1,0:T(8,128)(2,1)S(1)} %reorder.3.refs_0_.refs_3_), channel_id=1, source_target_pairs={{0,4},{2,6},{4,0},{6,2},{8,12},{10,14},{12,8},{14,10},{16,20},{18,... | collective-permute-start | bytes 983048 | tf_op jit(solution)/shard_map/ppermute | solution.py:71
  7.8 1.4 %collective-permute-start = (f32[8,16]{1,0:T(8,128)}, f32[8,16]{1,0:T(8,128)S(1)}, u32[]{:S(2)}, u32[]{:S(2)}) collective-permute-start(f32[8,16]{1,0:T(8,128)} %bitcast.9), channel_id=1, source_target_pairs={{0,2},{2,0},{4,6},{6,4},{8,10},{10,8},{12,14},{14,12},{16,18},{18,... | collective-permute-start | bytes 1544 | tf_op jit(solution)/shard_map/ppermute | solution.py:61
  16.5 24.8 %copy-start.8 = (bf16[128,1280]{1,0:T(8,128)(2,1)}, bf16[128,1280]{1,0:T(8,128)(2,1)S(1)}, u32[]{:S(2)}) copy-start(bf16[128,1280]{1,0:T(8,128)(2,1)S(1)} %collective-permute-done.2.refs_1_.refs_4_) | copy-start | bytes 983044
  16.5 24.8 %copy-start.9 = (bf16[128,1280]{1,0:T(8,128)(2,1)}, bf16[128,1280]{1,0:T(8,128)(2,1)S(1)}, u32[]{:S(2)}) copy-start(bf16[128,1280]{1,0:T(8,128)(2,1)S(1)} %collective-permute-done.3.refs_4_.refs_7_) | copy-start | bytes 983044
  16.5 10.9 %collective-permute-start.4 = (bf16[128,1280]{1,0:T(8,128)(2,1)S(1)}, bf16[128,1280]{1,0:T(8,128)(2,1)S(1)}, u32[]{:S(2)}, u32[]{:S(2)}) collective-permute-start(bf16[128,1280]{1,0:T(8,128)(2,1)S(1)} %collective-permute-done.2.refs_1_.refs_4_), channel_id=1, source_target_pairs={{0,8},{2,10},{4,12},{6,14},{8,16},{10,18},{12,20},{14,22},{16,24},... | collective-permute-start | bytes 983048 | tf_op jit(solution)/shard_map/ppermute | solution.py:66
  17.5 9.9 %collective-permute-start.5 = (bf16[128,1280]{1,0:T(8,128)(2,1)S(1)}, bf16[128,1280]{1,0:T(8,128)(2,1)S(1)}, u32[]{:S(2)}, u32[]{:S(2)}) collective-permute-start(bf16[128,1280]{1,0:T(8,128)(2,1)S(1)} %collective-permute-done.2.refs_1_.refs_4_), channel_id=1, source_target_pairs={{0,4},{2,6},{4,0},{6,2},{8,12},{10,14},{12,8},{14,10},{16,20},{18,... | collective-permute-start | bytes 983048 | tf_op jit(solution)/shard_map/ppermute | solution.py:71
  27.4 13.9 %copy-start.10 = (bf16[128,1280]{1,0:T(8,128)(2,1)}, bf16[128,1280]{1,0:T(8,128)(2,1)S(1)}, u32[]{:S(2)}) copy-start(bf16[128,1280]{1,0:T(8,128)(2,1)S(1)} %collective-permute-done.4.refs_2_.refs_5_) | copy-start | bytes 983044
  27.4 13.9 %copy-start.11 = (bf16[128,1280]{1,0:T(8,128)(2,1)}, bf16[128,1280]{1,0:T(8,128)(2,1)S(1)}, u32[]{:S(2)}) copy-start(bf16[128,1280]{1,0:T(8,128)(2,1)S(1)} %collective-permute-done.5.refs_5_.refs_8_) | copy-start | bytes 983044
  27.4 10.0 %collective-permute-start.7 = (bf16[128,1280]{1,0:T(8,128)(2,1)S(1)}, bf16[128,1280]{1,0:T(8,128)(2,1)S(1)}, u32[]{:S(2)}, u32[]{:S(2)}) collective-permute-start(bf16[128,1280]{1,0:T(8,128)(2,1)S(1)} %collective-permute-done.4.refs_2_.refs_5_), channel_id=1, source_target_pairs={{0,8},{2,10},{4,12},{6,14},{8,16},{10,18},{12,20},{14,22},{16,24},... | collective-permute-start | bytes 983048 | tf_op jit(solution)/shard_map/ppermute | solution.py:66
  27.4 9.9 %collective-permute-start.8 = (bf16[128,1280]{1,0:T(8,128)(2,1)S(1)}, bf16[128,1280]{1,0:T(8,128)(2,1)S(1)}, u32[]{:S(2)}, u32[]{:S(2)}) collective-permute-start(bf16[128,1280]{1,0:T(8,128)(2,1)S(1)} %collective-permute-done.4.refs_2_.refs_5_), channel_id=1, source_target_pairs={{0,4},{2,6},{4,0},{6,2},{8,12},{10,14},{12,8},{14,10},{16,20},{18,... | collective-permute-start | bytes 983048 | tf_op jit(solution)/shard_map/ppermute | solution.py:71
  30.9 8.4 %collective-permute-start.10 = (bf16[512,1024]{1,0:T(8,128)(2,1)S(1)}, bf16[512,1024]{1,0:T(8,128)(2,1)S(1)}, u32[]{:S(2)}, u32[]{:S(2)}) collective-permute-start(bf16[512,1024]{1,0:T(8,128)(2,1)S(1)} %collective-permute-done.9.refs_0_), channel_id=1, source_target_pairs={{0,2},{2,0},{4,6},{6,4},{8,10},{10,8},{12,14},{14,12},{16,18},{18,... | collective-permute-start | bytes 3145736 | tf_op jit(solution)/shard_map/ppermute | solution.py:61
  37.4 3.9 %copy-start.6 = (bf16[128,1280]{1,0:T(8,128)(2,1)}, bf16[128,1280]{1,0:T(8,128)(2,1)S(1)}, u32[]{:S(2)}) copy-start(bf16[128,1280]{1,0:T(8,128)(2,1)S(1)} %collective-permute-done.8.refs_6_.refs_9_) | copy-start | bytes 983044
  37.4 7.1 %collective-permute-start.11 = (bf16[64,1280]{1,0:T(8,128)(2,1)S(1)}, bf16[64,1280]{1,0:T(8,128)(2,1)S(1)}, u32[]{:S(2)}, u32[]{:S(2)}) collective-permute-start(bf16[64,1280]{1,0:T(8,128)(2,1)S(1)} %slice.6), channel_id=1, source_target_pairs={{0,4},{2,6},{4,0},{6,2},{8,12},{10,14},{12,8},{14,10},{16,20},{18,... | collective-permute-start | bytes 491528 | tf_op jit(solution)/shard_map/ppermute | solution.py:71
  39.0 7.3 %collective-permute-start.12 = (bf16[64,1280]{1,0:T(8,128)(2,1)S(1)}, bf16[64,1280]{1,0:T(8,128)(2,1)S(1)}, u32[]{:S(2)}, u32[]{:S(2)}) collective-permute-start(bf16[64,1280]{1,0:T(8,128)(2,1)S(1)} %slice.7), channel_id=1, source_target_pairs={{0,8},{2,10},{4,12},{6,14},{8,16},{10,18},{12,20},{14,22},{16,24},... | collective-permute-start | bytes 491528 | tf_op jit(solution)/shard_map/ppermute | solution.py:66
  44.5 5.7 %copy-start.13 = (bf16[64,1280]{1,0:T(8,128)(2,1)}, bf16[64,1280]{1,0:T(8,128)(2,1)S(1)}, u32[]{:S(2)}) copy-start(bf16[64,1280]{1,0:T(8,128)(2,1)S(1)} %collective-permute-done.11.refs_3_.refs_10_) | copy-start | bytes 491524
  46.3 3.9 %copy-start.14 = (bf16[64,1280]{1,0:T(8,128)(2,1)}, bf16[64,1280]{1,0:T(8,128)(2,1)S(1)}, u32[]{:S(2)}) copy-start(bf16[64,1280]{1,0:T(8,128)(2,1)S(1)} %collective-permute-done.12.refs_4_.refs_11_) | copy-start | bytes 491524
  46.3 7.5 %copy-start.18 = (s32[16,4]{0,1:T(4,128)S(1)}, s32[16,4]{0,1:T(4,128)}, u32[]{:S(2)}) copy-start(s32[16,4]{0,1:T(4,128)} %param.10) | copy-start | bytes 772
  50.3 4.3 %copy-start.16 = (bf16[2,2048,128]{2,1,0:T(8,128)(2,1)}, bf16[2,2048,128]{2,1,0:T(8,128)(2,1)S(1)}, u32[]{:S(2)}) copy-start(bf16[2,2048,128]{2,1,0:T(8,128)(2,1)S(1)} %get-tuple-element.67.refs_2_) | copy-start | bytes 3145732
  50.3 15.7 %all-to-all-start = ((bf16[8,272,128]{2,1,0:T(8,128)(2,1)}), bf16[8,272,128]{2,1,0:T(8,128)(2,1)S(1)}, u32[]{:S(2)}, u32[]{:S(2)}) async-start(bf16[8,272,128]{2,1,0:T(8,128)(2,1)} %get-tuple-element.66), calls=%async_computation | async-start | bytes 1114112 | tf_op jit(solution)/shard_map/all_to_all | solution.py:846
  67.0 16.8 %all-to-all-start.1 = ((bf16[8,256,128]{2,1,0:T(8,128)(2,1)}), bf16[8,256,128]{2,1,0:T(8,128)(2,1)S(1)}, u32[]{:S(2)}, u32[]{:S(2)}) async-start(bf16[8,256,128]{2,1,0:T(8,128)(2,1)} %scan_states.1), calls=%async_computation.1 | async-start | bytes 1048576 | tf_op jit(solution)/shard_map/all_to_all | solution.py:846
  70.7 13.9 %copy-start.7 = (bf16[1024,256]{1,0:T(8,128)(2,1)S(1)}, bf16[1024,256]{1,0:T(8,128)(2,1)}, u32[]{:S(2)}) copy-start(bf16[1024,256]{1,0:T(8,128)(2,1)} %get-tuple-element.74.refs_2_) | copy-start | bytes 1572868
  84.6 6.9 %copy-start = (bf16[1024,1024]{1,0:T(8,128)(2,1)S(1)}, bf16[1024,1024]{1,0:T(8,128)(2,1)}, u32[]{:S(2)}) copy-start(bf16[1024,1024]{1,0:T(8,128)(2,1)} %w_ref.5) | copy-start | bytes 6291460
  89.1 2.3 %collective-permute-start.15 = (bf16[512,256]{1,0:T(8,128)(2,1)S(1)}, bf16[512,256]{1,0:T(8,128)(2,1)S(1)}, u32[]{:S(2)}, u32[]{:S(2)}) collective-permute-start(bf16[512,256]{1,0:T(8,128)(2,1)S(1)} %get-tuple-element.80), channel_id=1, source_target_pairs={{0,2},{2,0},{4,6},{6,4},{8,10},{10,8},{12,14},{14,12},{16,18},{18,... | collective-permute-start | bytes 786440 | tf_op jit(solution)/shard_map/ppermute | solution.py:61
  89.2 9.3 %collective-permute-start.14 = (bf16[512,256]{1,0:T(8,128)(2,1)S(1)}, bf16[512,256]{1,0:T(8,128)(2,1)S(1)}, u32[]{:S(2)}, u32[]{:S(2)}) collective-permute-start(bf16[512,256]{1,0:T(8,128)(2,1)S(1)} %get-tuple-element.78), channel_id=1, source_target_pairs={{0,1},{1,0},{2,3},{3,2},{4,5},{5,4},{6,7},{7,6},{8,9},{9,8},{10,11... | collective-permute-start | bytes 786440 | tf_op jit(solution)/shard_map/ppermute | solution.py:95
  91.4 12.3 %collective-permute-start.13 = (bf16[512,256]{1,0:T(8,128)(2,1)S(1)}, bf16[512,256]{1,0:T(8,128)(2,1)S(1)}, u32[]{:S(2)}, u32[]{:S(2)}) collective-permute-start(bf16[512,256]{1,0:T(8,128)(2,1)S(1)} %get-tuple-element.77), channel_id=1, source_target_pairs={{0,3},{1,2},{2,1},{3,0},{4,7},{5,6},{6,5},{7,4},{8,11},{9,10},{10,... | collective-permute-start | bytes 786440 | tf_op jit(solution)/shard_map/ppermute | solution.py:103
  (5 other events, 10.3 us)
